TPU v7x, 32 devices: a whole 2x2x4 slice. The times are simulated.
32 devices in a mesh: modes: 16 (over z, y, x), rows: 2 (over core).
Axes of the slice: x: 2, y: 2, z: 4, core: 2. Of those that a mesh axis runs over, the one named last changes fastest.
Arguments:
- forward: bfloat16 [16, 768, 1536], P('modes', 'rows'), may hold values from -6 to 6
- backward: bfloat16 [16, 768, 1536], P('modes', 'rows'), may hold values from -6 to 6
- targets: bfloat16 [2, 16, 768, 768], P(None, None, ('rows', 'modes')), may hold values from -0.0078125 to 0.0078125
Outputs:
- phase_plane: bfloat16 [768, 1536], P('rows')
- output_fields: bfloat16 [16, 768, 1536], P('modes', 'rows')
- coupling: float32 [32, 16], P(('modes', 'rows'))
All inputs are finite; a program needn't handle non-finite values.
Results may differ from a plain program's by a relative error of at most 0.012.
Values may be sent and summed in bfloat16 or wider, within the bound.
No kernel may reach another device: no remote copies, remote signals or barrier semaphores. Data moves between devices by JAX's collectives and lax.ppermute only.
A program may use at most 64 MiB of HBM per device.

v0:
```python
import math

import jax
import jax.numpy as jnp
from jax import lax
from jax.sharding import PartitionSpec as P

two_pi = 2.0 * math.pi


def fourier_pair(row_index, col_index, grid_size):
    product = row_index[:, None] * col_index[None, :] % grid_size
    angles = product.astype(jnp.float32) * (two_pi / grid_size)
    factor = 1.0 / math.sqrt(grid_size)
    return (jnp.cos(angles) * factor, jnp.sin(angles) * factor)


def column_matrices(grid_size):
    index_all = jnp.arange(grid_size, dtype=jnp.int32)
    cosine, sine_part = fourier_pair(index_all, index_all, grid_size)
    forward_cols = jnp.concatenate(
        [jnp.concatenate([cosine, -sine_part], 1), jnp.concatenate([sine_part, cosine], 1)], 0
    )
    inverse_cols = jnp.concatenate(
        [jnp.concatenate([cosine, sine_part], 1), jnp.concatenate([-sine_part, cosine], 1)], 0
    )
    return (forward_cols.astype(jnp.bfloat16), inverse_cols.astype(jnp.bfloat16))


def spectral_phase(row_freq, col_freq, grid_size):

    def squared(freq):
        centred = (freq + grid_size // 2) % grid_size - grid_size // 2
        return centred * centred % (4 * grid_size)

    summed = (squared(row_freq)[:, None] + squared(col_freq)[None, :]) % (4 * grid_size)
    theta = summed.astype(jnp.float32) * (-two_pi / (4 * grid_size))
    return (jnp.cos(theta), jnp.sin(theta))


def swap_parts(values):
    half_width = values.shape[-1] // 2
    return jnp.concatenate([values[..., half_width:], -values[..., :half_width]], -1)


def apply_phase(values, phase_re, phase_im):
    half_width = values.shape[-1] // 2
    real_part = values[..., :half_width]
    imag_part = values[..., half_width:]
    return jnp.concatenate(
        [real_part * phase_re - imag_part * phase_im, real_part * phase_im + imag_part * phase_re],
        -1,
    )


def transmission(intersection, mode_total):
    magnitude = (
        intersection[:, 0, :] * intersection[:, 0, :]
        + intersection[:, 1, :] * intersection[:, 1, :]
    )
    scale = lax.rsqrt(magnitude + mode_total)
    return (intersection * scale[:, None, :]).astype(jnp.bfloat16)


def local(forward, backward, targets):
    modes_here, local_rows, double_width = forward.shape
    grid_size = double_width // 2
    row_index = lax.axis_index("rows")
    mode_total = modes_here * lax.axis_size("modes")
    forward32 = forward.astype(jnp.float32)
    backward32 = backward.astype(jnp.float32)
    fore_re = forward32[..., :grid_size]
    fore_im = forward32[..., grid_size:]
    back_re = backward32[..., :grid_size]
    back_im = backward32[..., grid_size:]
    partial_re = jnp.sum(back_re * fore_re + back_im * fore_im, 0)
    partial_im = jnp.sum(back_re * fore_im - back_im * fore_re, 0)
    partial_value = jnp.stack([partial_re, partial_im], 1)
    summed = lax.psum(partial_value, "modes")
    plane_parts = transmission(summed, mode_total)
    phase_plane = plane_parts.reshape(local_rows, double_width)
    plane32 = phase_plane.astype(jnp.float32)
    shaped = apply_phase(forward32, plane32[:, :grid_size], plane32[:, grid_size:]).astype(
        jnp.bfloat16
    )
    forward_cols, inverse_cols = column_matrices(grid_size)
    across = jnp.dot(
        shaped.reshape(-1, double_width), forward_cols, preferred_element_type=jnp.float32
    )
    across = across.astype(jnp.bfloat16).reshape(modes_here, local_rows, double_width)
    index_all = jnp.arange(grid_size, dtype=jnp.int32)
    own_rows = row_index * local_rows + jnp.arange(local_rows, dtype=jnp.int32)
    cosine, sine_part = fourier_pair(own_rows, index_all, grid_size)
    cos_rows = cosine.astype(jnp.bfloat16)
    sin_rows = sine_part.astype(jnp.bfloat16)
    neg_rows = (-sine_part).astype(jnp.bfloat16)
    phase_re, phase_im = spectral_phase(own_rows, index_all, grid_size)

    def row_step(table_sin, running, shard_piece):
        running = jnp.einsum(
            "kj,mjx->mkx", cos_rows, shard_piece, preferred_element_type=jnp.float32
        )
        return running + jnp.einsum(
            "kj,mjx->mkx", table_sin, swap_parts(shard_piece), preferred_element_type=jnp.float32
        )

    zero_carry = jnp.zeros((modes_here, local_rows, double_width), jnp.float32)
    transformed = row_step(sin_rows, zero_carry, lax.all_gather(across, "rows", axis=1, tiled=True))
    spectrum = apply_phase(transformed, phase_re, phase_im).astype(jnp.bfloat16)
    returned = row_step(
        neg_rows, zero_carry, lax.all_gather(spectrum, "rows", axis=1, tiled=True)
    ).astype(jnp.bfloat16)
    output_fields = jnp.dot(
        returned.reshape(-1, double_width), inverse_cols, preferred_element_type=jnp.float32
    )
    output_fields = output_fields.astype(jnp.bfloat16).reshape(modes_here, local_rows, double_width)
    pixels = lax.all_to_all(output_fields, "modes", split_axis=1, concat_axis=0, tiled=True)
    pixel_rows = pixels.shape[1]
    pixel_parts = pixels.reshape(mode_total, pixel_rows, 2, grid_size)
    conj_pairs = jnp.stack(
        [jnp.stack([targets[0], targets[1]]), jnp.stack([-targets[1], targets[0]])]
    )
    term_all = jnp.einsum(
        "mpcx,kcnpx->kmn", pixel_parts, conj_pairs, preferred_element_type=jnp.float32
    )
    term_all = term_all.reshape(2 * mode_total, mode_total)
    coupling = lax.psum_scatter(term_all, ("modes", "rows"), scatter_dimension=0, tiled=True)
    return (phase_plane, output_fields, coupling)


def solution(mesh):
    return jax.shard_map(
        local,
        mesh=mesh,
        in_specs=(
            P("modes", "rows", None),
            P("modes", "rows", None),
            P(None, None, ("rows", "modes"), None),
        ),
        out_specs=(P("rows", None), P("modes", "rows", None), P(("modes", "rows"), None)),
        check_vma=False,
    )
```

profile of v0, /device:TPU:0, one launch (start us, length us, event | category | flops | bytes accessed | tf_op | source)
XLA Modules:
  0.0 339.2 jit_solution(12769903161601096874)
XLA Ops:
  7.2 1.6 convert_element_type.86
  8.9 0.3 convert_element_type.85
  9.2 0.3 add_bitcast_fusion
  9.5 1.6 pad_maximum_fusion.6
  11.1 10.0 %fusion.37 = bf16[768,768]{1,0:T(8,128)(2,1)} fusion(), kind=kLoop, calls=%fused_computation.44 | loop fusion | flops 6488064 | bytes 1179648 | tf_op jit(solution)/shard_map/convert.10
  21.1 10.7 %negate_convert_fusion = (bf16[768,768]{1,0:T(8,128)(2,1)}, bf16[768,768]{1,0:T(8,128)(2,1)}) fusion(), kind=kLoop, calls=%fused_computation.36 | loop fusion | flops 8257536 | bytes 2359296 | tf_op jit(solution)/shard_map/convert.13
  31.9 115.4 %all-reduce.3.cloned.1.call-done = f32[384,2,768]{2,0,1:T(8,128)} async-done(((f32[384,2,768]{2,0,1:T(8,128)}), f32[384,2,768]{2,0,1:T(8,128)}) %all-reduce.3.cloned.1.call-update) | async-done | bytes 2359312 | tf_op jit(solution)/shard_map/psum | solution.py:79
  147.3 2.0 fusion.46
  149.3 0.4 copy-done
  149.7 0.3 fusion.42
  150.1 0.3 convert_element_type.88
  150.4 0.7 copy-done.1
  151.1 0.4 fusion.82
  151.5 0.9 copy-done.9
  152.4 0.4 copy-done.11
  152.7 0.4 copy-done.13
  153.1 3.0 fusion.14
  156.1 0.2 all-gather.4.cloned.1.call-start
  156.4 10.3 %all-gather.6.cloned.1.call-done = bf16[768,1536]{1,0:T(8,128)(2,1)} async-done(((bf16[384,1536]{1,0:T(8,128)(2,1)}), bf16[768,1536]{1,0:T(8,128)(2,1)}) %all-gather.6.cloned.1.call-update) | async-done | bytes 2359312 | tf_op jit(solution)/shard_map/all_gather | solution.py:108
  166.8 1.9 fusion.119
  168.7 0.4 copy-done.4
  169.1 5.3 %fusion.81 = f32[1536,384]{1,0:T(8,128)S(1)} fusion(bf16[768,1536]{1,0:T(8,128)(2,1)S(1)} %copy-done.4, s32[384]{0:T(512)S(1)} %iota_add_fusion), kind=kOutput, calls=%fused_computation.98 | convolution fusion | flops 909213696 | bytes 4720128 | tf_op jit(solution)/shard_map/kj,mjx->mkx/dot_general | solution.py:100
  174.5 5.4 %fusion.10 = f32[1,384,1536]{1,2,0:T(8,128)S(1)} fusion(f32[1536,384]{1,0:T(8,128)S(1)} %fusion.81, bf16[1,768,768]{2,1,0:T(8,128)(2,1)S(1)} %get-tuple-element.21, bf16[1,768,768]{2,1,0:T(8,128)(2,1)S(1)} %get-tuple-element.20, s32[384]{0:T(512)S(1)} %iota_add_fusion), kind=kOutput, calls=%fused_computation.15 | convolution fusion | flops 914522112 | bytes 7079424 | tf_op jit(solution)/shard_map/kj,mjx->mkx/dot_general | solution.py:103
  179.9 5.9 %subtract_convert_fusion = (bf16[1,384,768]{1,2,0:T(8,128)(2,1)S(1)}, bf16[1,384,768]{1,2,0:T(8,128)(2,1)S(1)}) fusion(f32[1,384,1536]{1,2,0:T(8,128)S(1)} %fusion.10, s32[768]{0:T(1024)S(1)} %add_select_fusion.3, s32[384]{0:T(512)S(1)} %add_select_fusion.5), kind=kLoop, calls=%fused_computation.70 | loop fusion | flops 5013504 | bytes 3543552 | tf_op jit(solution)/shard_map/convert.6
  185.8 1.2 pad_maximum_fusion.7
  187.0 12.2 %all-gather.4.cloned.1.call-done = bf16[1,768,1536]{1,2,0:T(8,128)(2,1)} async-done(((bf16[1,384,1536]{1,2,0:T(8,128)(2,1)}), bf16[1,768,1536]{1,2,0:T(8,128)(2,1)}) %all-gather.4.cloned.1.call-update) | async-done | bytes 2359312 | tf_op jit(solution)/shard_map/all_gather | solution.py:111
  199.2 1.9 fusion.118
  201.2 0.4 copy-done.5
  201.6 5.4 %fusion.32 = f32[1536,384]{1,0:T(8,128)S(1)} fusion(bf16[1,768,1536]{1,2,0:T(8,128)(2,1)S(1)} %copy-done.5, s32[384]{0:T(512)S(1)} %iota_add_fusion), kind=kOutput, calls=%fused_computation.34 | convolution fusion | flops 909213696 | bytes 4720128 | tf_op jit(solution)/shard_map/kj,mjx->mkx/dot_general | solution.py:100
  207.0 5.5 %fusion.18.clone.5 = bf16[384,1536]{0,1:T(8,128)(2,1)S(1)} fusion(f32[1536,384]{1,0:T(8,128)S(1)} %fusion.32, bf16[1,768,768]{1,2,0:T(8,128)(2,1)S(1)} %get-tuple-element.19, bf16[1,768,768]{1,2,0:T(8,128)(2,1)S(1)} %get-tuple-element.18, s32[384]{0:T(512)S(1)} %iota_add_fusion), kind=kOutput, calls=%fused_computation.19.clone.clone.clone.2 | convolution fusion | flops 915406848 | bytes 5899776 | tf_op jit(solution)/shard_map/kj,mjx->mkx/dot_general | solution.py:103
  212.6 19.6 %fusion.19 = bf16[1,384,1536]{2,1,0:T(8,128)(2,1)S(1)} fusion(bf16[768,768]{1,0:T(8,128)(2,1)S(1)} %copy-done.14, bf16[768,768]{1,0:T(8,128)(2,1)S(1)} %copy-done.12, bf16[768,768]{1,0:T(8,128)(2,1)S(1)} %copy-done.10, bf16[384,1536]{0,1:T(8,128)(2,1)S(1)} %fusion.18.clone.5), kind=kOutput, calls=%fused_computation.20 | convolution fusion | flops 1831403520 | bytes 5898240 | tf_op jit(solution)/shard_map/dot_general | solution.py:113
  232.2 1.8 copy.48
  234.1 0.5 broadcast.270
  234.6 7.8 %reduce.2 = bf16[384,1536]{1,0:T(8,128)(2,1)S(1)} reduce(bf16[384,1,1536]{2,1,0:T(2,128)(2,1)S(1)} %bitcast.92, bf16[]{:T(256)} %broadcast.270), dimensions={1}, to_apply=%bitcast.91.reduce_sub_computation | reduce | bytes 2359298
  242.4 1.3 reshape.262
  243.7 7.1 %all-to-all-start = ((bf16[16,2,18432]{2,1,0:T(2,128)(2,1)}), bf16[16,2,18432]{2,1,0:T(2,128)(2,1)S(1)}, u32[]{:S(2)}, u32[]{:S(2)}) async-start(bf16[16,2,18432]{2,1,0:T(2,128)(2,1)} %reshape.262), calls=%async_computation | async-start | bytes 2359296 | tf_op jit(solution)/shard_map/all_to_all | solution.py:117
  250.8 0.2 copy.47
  251.2 0.9 copy-done.2
  252.1 1.1 maximum_bitcast_fusion.4
  253.2 24.8 %all-to-all-done = bf16[16,2,18432]{2,1,0:T(2,128)(2,1)S(1)} async-done(((bf16[16,2,18432]{2,1,0:T(2,128)(2,1)}), bf16[16,2,18432]{2,1,0:T(2,128)(2,1)S(1)}, u32[]{:S(2)}, u32[]{:S(2)}) %all-to-all-start) | async-done | bytes 1179680 | tf_op jit(solution)/shard_map/all_to_all | solution.py:117
  278.0 1.2 reshape.263
  279.1 7.0 %bitcast_reduce_fusion = bf16[384,1536]{1,0:T(8,128)(2,1)S(1)} fusion(bf16[384,1,1536]{2,1,0:T(2,128)(2,1)S(1)} %reshape.263), kind=kLoop, calls=%fused_computation.141 | loop fusion | bytes 2359296 | tf_op jit(solution)/shard_map/all_to_all | solution.py:117
  286.1 1.2 reshape.253
  287.3 0.5 copy-done.3
  287.8 0.4 copy-done.15
  288.2 2.0 fusion.60
  290.3 41.4 %all-reduce = f32[32,16]{0,1:T(8,128)S(1)} all-reduce(f32[32,16]{0,1:T(8,128)S(1)} %reshape.254), channel_id=3, replica_groups=mesh['modes'=16,'rows'=2] {'modes','rows'}, use_global_device_ids=true, to_apply=%region_1.0.clone | all-reduce | flops 512 | bytes 4096
  331.8 0.6 copy.32
  (35 shorter events, 0.6 us)
Async XLA Ops:
  7.2 1.7 copy-start.6
  7.2 140.1 %all-reduce.3.cloned.1.call-start = ((), (), s32[]{:S(2)}) async-start(), calls=%async_computation.1 | async-start | bytes 4718592 | tf_op jit(solution)/shard_map/psum | solution.py:79
  11.1 155.7 %all-gather.6.cloned.1.call-start = ((), (), s32[]{:S(2)}) async-start(), calls=%async_computation.3 | async-start | bytes 3538944 | tf_op jit(solution)/shard_map/all_gather | solution.py:108
  147.3 2.4 copy-start
  150.1 1.0 copy-start.1
  151.1 1.3 copy-start.9
  151.1 1.6 copy-start.11
  151.1 2.0 copy-start.13
  156.1 43.1 %all-gather.4.cloned.1.call-start = ((), (), s32[]{:S(2)}) async-start(), calls=%async_computation.2 | async-start | bytes 3538944 | tf_op jit(solution)/shard_map/all_gather | solution.py:111
  166.8 2.4 copy-start.4
  199.2 2.4 copy-start.5
  207.0 5.6 %copy-start.10 = (bf16[768,768]{1,0:T(8,128)(2,1)S(1)}, bf16[768,768]{1,0:T(8,128)(2,1)}, u32[]{:S(2)}) copy-start(bf16[768,768]{1,0:T(8,128)(2,1)} %fusion.37) | copy-start | bytes 3538948
  207.0 5.6 %copy-start.12 = (bf16[768,768]{1,0:T(8,128)(2,1)S(1)}, bf16[768,768]{1,0:T(8,128)(2,1)}, u32[]{:S(2)}) copy-start(bf16[768,768]{1,0:T(8,128)(2,1)} %get-tuple-element.26) | copy-start | bytes 3538948
  207.0 5.6 %copy-start.14 = (bf16[768,768]{1,0:T(8,128)(2,1)S(1)}, bf16[768,768]{1,0:T(8,128)(2,1)}, u32[]{:S(2)}) copy-start(bf16[768,768]{1,0:T(8,128)(2,1)} %get-tuple-element.27) | copy-start | bytes 3538948
  232.2 1.8 copy-start.7
  243.7 7.1 %copy-start.8 = (bf16[2,16,24,768]{3,2,1,0:T(8,128)(2,1)S(1)}, bf16[2,16,24,768]{3,2,1,0:T(8,128)(2,1)}, u32[]{:S(2)}) copy-start(bf16[2,16,24,768]{3,2,1,0:T(8,128)(2,1)} %param.5) | copy-start | bytes 3538948
  243.7 34.3 %all-to-all-start = ((bf16[16,2,18432]{2,1,0:T(2,128)(2,1)}), bf16[16,2,18432]{2,1,0:T(2,128)(2,1)S(1)}, u32[]{:S(2)}, u32[]{:S(2)}) async-start(bf16[16,2,18432]{2,1,0:T(2,128)(2,1)} %reshape.262), calls=%async_computation | async-start | bytes 2359296 | tf_op jit(solution)/shard_map/all_to_all | solution.py:117
  251.1 1.0 copy-start.2
  286.1 1.7 copy-start.3
  286.1 2.0 copy-start.15
Sparse Core Ops, SparseCore 0:
  13.6 133.6 all-reduce.2
  156.3 10.4 all-gather.5
  187.1 12.0 all-gather.3
where the time goes:
time: 344 us; the launch traced here: 339 us
  waiting for transfers between devices  163 us (47%)
  other arithmetic  47.5 us (14%)
  matrix products  46.3 us (13%)
  blocking collectives  41.4 us (12%)
  local copies, waits for them, and re-layouts  19.4 us (6%)
  between operations  14.3 us (4%)
  starting transfers between devices  7.41 us (2%)
    psum x1, waiting for transfers between devices, local(): summed = lax.psum(partial_value, 'modes')  115 us
    unnamed x1, blocking collectives  41.4 us
    another operation x3, other arithmetic  26.6 us
    all_to_all x1, waiting for transfers between devices, local(): lax.all_to_all(output_fields, 'modes', split_axis=1, concat_axis=0, tiled...  24.8 us
    dot_general x1, matrix products, local(): jnp.dot(returned.reshape(-1, double_width), inverse_cols, preferred_eleme...  19.6 us
    all_gather x1, waiting for transfers between devices, local(): lax.all_gather(spectrum, 'rows', axis=1, tiled=True)  12.2 us
    dot_general x2, matrix products, row_step(): jnp.einsum('kj,mjx->mkx', table_sin, swap_parts(shard_piece), preferred_e...  11 us
    dot_general x2, matrix products, row_step(): jnp.einsum('kj,mjx->mkx', cos_rows, shard_piece, preferred_element_type=j...  10.8 us
  transfers between devices with their start and end apart: 4, of which 4 were waited for; matrix products, arithmetic and copies ran while one was open for 7% of the time, Pallas kernels for 0%

commit v1 on v0

v1 whole, which is shorter than its diff:
```python
import numpy as np

import jax
import jax.numpy as jnp
from jax import lax
from jax.experimental import pallas as pl
from jax.experimental.pallas import tpu as pltpu
from jax.sharding import PartitionSpec as P

bf16 = jnp.bfloat16
f32 = jnp.float32


def propagator(grid_size):
    index = np.arange(grid_size)
    centred = (index + grid_size // 2) % grid_size - grid_size // 2
    squared = centred * centred % (4 * grid_size)
    column = np.fft.ifft(np.exp(-2j * np.pi * squared / (4 * grid_size)))
    matrix = column[(index[:, None] - index[None, :]) % grid_size]
    return matrix.real, matrix.imag


def stages(count):
    digits, stride = [], 1
    while count // stride > 4:
        digits.append((stride, 2))
        stride *= 2
    digits.append((stride, count // stride))
    return digits


def exchange(values, offset, count):
    return lax.ppermute(values, "modes", [(i, i ^ offset) for i in range(count)])


def pick(values, index, axis):
    return lax.dynamic_index_in_dim(values, index, axis, keepdims=False)


def reduce_part(partial, digits, order, count):
    me = lax.axis_index("modes")
    axes = [len(digits) - 1 - d for d in range(len(digits))]
    for d in order:
        stride, size = digits[d]
        own = me // stride % size
        axis = axes[d]
        got = [
            exchange(pick(partial, own ^ e, axis).astype(bf16), e * stride, count)
            for e in range(1, size)
        ]
        partial = pick(partial, own, axis)
        for g in got:
            partial = partial + g.astype(f32)
        axes = [a - (a > axis) for a in axes]
    return partial


def gather_part(block, digits, order, count):
    me = lax.axis_index("modes")
    done = []
    for d in reversed(order):
        stride, size = digits[d]
        own = me // stride % size
        got = [block] + [exchange(block, e * stride, count) for e in range(1, size)]
        axis = sum(1 for other in done if other > d)
        stacked = jnp.stack(got, axis)
        if size == 2:
            block = jnp.where(own == 0, stacked, jnp.flip(stacked, axis))
        else:
            block = jnp.stack([pick(stacked, own ^ at, axis) for at in range(size)], axis)
        done.append(d)
    return block


def columns_kernel(own_ref, other_ref, re_ref, im_ref, out_ref):
    half = own_ref.shape[1] // 2
    rows = own_ref.shape[0]

    def times(table, values):
        return jnp.dot(table, values, preferred_element_type=f32)

    def both(table, part):
        cols = pl.ds(part * half, half)
        return times(table[:, :rows], own_ref[:, cols]) + times(table[:, rows:], other_ref[:, cols])

    c_re, c_im = re_ref[...], im_ref[...]
    out_ref[:, :half] = (both(c_re, 0) - both(c_im, 1)).astype(bf16)
    out_ref[:, half:] = (both(c_im, 0) + both(c_re, 1)).astype(bf16)


def coupling_kernel(mode_rows, fields_ref, targets_ref, out_ref):
    product = lax.dot_general(
        fields_ref[...], targets_ref[...], (((1,), (1,)), ((), ())), preferred_element_type=f32
    )
    left, right = product.shape
    row = lax.broadcasted_iota(jnp.int32, (left, right), 0) % mode_rows
    col = lax.broadcasted_iota(jnp.int32, (left, right), 1) % mode_rows
    product = jnp.where(row == col, product, 0.0)

    def groups(size):
        member = lax.broadcasted_iota(jnp.int32, (size // mode_rows, size), 1) // mode_rows
        group = lax.broadcasted_iota(jnp.int32, (size // mode_rows, size), 0)
        return jnp.where(member == group, 1.0, 0.0).astype(f32)

    narrow = lax.dot_general(
        groups(left),
        product,
        (((1,), (0,)), ((), ())),
        precision=lax.Precision.HIGHEST,
        preferred_element_type=f32,
    )
    out_ref[...] = lax.dot_general(
        narrow,
        groups(right),
        (((1,), (1,)), ((), ())),
        precision=lax.Precision.HIGHEST,
        preferred_element_type=f32,
    )


def kernel_call(kernel, shape, dtype, flops, operands):
    return pl.pallas_call(
        kernel,
        out_shape=jax.ShapeDtypeStruct(shape, dtype),
        in_specs=[pl.BlockSpec(memory_space=pltpu.VMEM)] * len(operands),
        out_specs=pl.BlockSpec(memory_space=pltpu.VMEM),
        compiler_params=pltpu.CompilerParams(vmem_limit_bytes=32 * 1024 * 1024),
        cost_estimate=pl.CostEstimate(flops=flops, bytes_accessed=4 << 20, transcendentals=0),
    )(*operands)


def local(forward, backward, targets):
    modes_here, local_rows, double_width = forward.shape
    grid_size = double_width // 2
    count = lax.axis_size("modes")
    mode_total = modes_here * count
    block_rows = local_rows // count
    digits = stages(count)
    sizes = [size for _, size in reversed(digits)]
    half = grid_size // 2

    fore = forward[0].astype(f32)
    back = backward[0].astype(f32)
    fore_re, fore_im = fore[:, :grid_size], fore[:, grid_size:]
    back_re, back_im = back[:, :grid_size], back[:, grid_size:]
    partial_re = back_re * fore_re + back_im * fore_im
    partial_im = back_re * fore_im - back_im * fore_re
    first = list(range(len(digits)))
    orders = [first, [1, 0] + first[2:]]
    planes = []
    for part, order in enumerate(orders):
        cols = slice(part * half, (part + 1) * half)
        partial = jnp.concatenate([partial_re[:, cols], partial_im[:, cols]], -1)
        summed = reduce_part(partial.reshape(*sizes, block_rows, grid_size), digits, order, count)
        over_re, over_im = summed[:, :half], summed[:, half:]
        scale = lax.rsqrt(over_re * over_re + over_im * over_im + mode_total)
        block = jnp.concatenate([over_re * scale, over_im * scale], -1).astype(bf16)
        planes.append(gather_part(block, digits, order, count).reshape(local_rows, grid_size))
    plane_re = jnp.concatenate([p[:, :half] for p in planes], -1)
    plane_im = jnp.concatenate([p[:, half:] for p in planes], -1)
    phase_plane = jnp.concatenate([plane_re, plane_im], -1)

    plane_re, plane_im = plane_re.astype(f32), plane_im.astype(f32)
    shaped = jnp.concatenate(
        [fore_re * plane_re - fore_im * plane_im, fore_re * plane_im + fore_im * plane_re], -1
    ).astype(bf16)
    other = lax.ppermute(shaped, "rows", [(0, 1), (1, 0)])

    c_re, c_im = propagator(grid_size)
    own_re = jnp.asarray(c_re[:local_rows], bf16)
    own_im = jnp.asarray(c_im[:local_rows], bf16)
    columns = kernel_call(
        columns_kernel,
        (local_rows, double_width),
        bf16,
        2 * local_rows * double_width * double_width,
        (shaped, other, own_re, own_im),
    )

    back_table = jnp.asarray(np.block([[c_re, -c_im], [c_im, c_re]]), bf16)
    rows_table = jnp.asarray(np.block([[c_re, c_im], [-c_im, c_re]]), bf16)
    flat = jnp.concatenate([targets[0], targets[1]], -1).reshape(-1, double_width)
    seen = jnp.dot(flat, back_table, preferred_element_type=f32).astype(bf16)
    turned = jnp.concatenate([-seen[:, grid_size:], seen[:, :grid_size]], -1)
    target_pair = jnp.concatenate([seen, turned], 0)

    pixels = lax.all_to_all(
        columns.reshape(count, block_rows, double_width), "modes", 0, 0, tiled=True
    )
    output_fields = jnp.dot(columns, rows_table, preferred_element_type=f32).astype(bf16)

    term = kernel_call(
        lambda *refs: coupling_kernel(block_rows, *refs),
        (mode_total, 2 * mode_total),
        f32,
        4 * local_rows * local_rows * double_width,
        (pixels.reshape(local_rows, double_width), target_pair),
    )
    term = jnp.concatenate([term[:, :mode_total], term[:, mode_total:]], 0)
    pieces = lax.all_to_all(term, ("modes", "rows"), 0, 0, tiled=True)
    coupling = jnp.sum(pieces, 0, keepdims=True)
    return (phase_plane, output_fields[None], coupling)


def solution(mesh):
    return jax.shard_map(
        local,
        mesh=mesh,
        in_specs=(
            P("modes", "rows", None),
            P("modes", "rows", None),
            P(None, None, ("rows", "modes"), None),
        ),
        out_specs=(P("rows", None), P("modes", "rows", None), P(("modes", "rows"), None)),
        check_vma=False,
    )
```

time: 344 us -> 118 us (0.34); the launches traced: 339 us -> 118 us
  waiting for transfers between devices: 163 us -> 41.5 us
  blocking collectives: 41.4 us -> 0 us
  matrix products: 46.3 us -> 7.88 us
  other arithmetic: 47.5 us -> 12.6 us
  starting transfers between devices: 7.41 us -> 41.3 us
  between operations: 14.3 us -> 1.12 us
  local copies, waits for them, and re-layouts: 19.4 us -> 7.74 us
  Pallas kernels: 0 us -> 5.65 us
    psum x1 -> x0, waiting for transfers between devices: 115 us -> none  [local(): summed = lax.psum(partial_value, 'modes')]
    unnamed x1 -> x0, blocking collectives: 41.4 us -> none
    dot_general x7 -> x3, matrix products: 46.3 us -> 7.88 us  [the longest x1 5.71 us: local(): jnp.dot(columns, rows_table, preferred_element_type=f32).astype(bf16)]
    ppermute x0 -> x21, starting transfers between devices: none -> 30.6 us  [the longest x20 30.6 us: exchange(): lax.ppermute(values, 'modes', [(i, i ^ offset) for i in range(count)])]
    another operation x6 -> x13, other arithmetic: 29.7 us -> 0.84 us
    all_gather x2 -> x0, waiting for transfers between devices: 22.6 us -> none  [the longest x1 12.2 us: local(): lax.all_gather(spectrum, 'rows', axis=1, tiled=True)]
    ppermute x0 -> x21, waiting for transfers between devices: none -> 19.8 us  [the longest x20 17 us: exchange(): lax.ppermute(values, 'modes', [(i, i ^ offset) for i in range(count)])]
    unnamed x2 -> x0, other arithmetic: 8.13 us -> none
  transfers between devices with their start and end apart: 4 -> 23, of which waited for: 4 -> 13; matrix products, arithmetic and copies ran while one was open for 7% -> 12% of each run, Pallas kernels for 0% -> 0%
where the time goes in v1:
time: 118 us
  waiting for transfers between devices  41.5 us (35%)
  starting transfers between devices  41.3 us (35%)
  other arithmetic  12.6 us (11%)
  matrix products  7.88 us (7%)
  local copies, waits for them, and re-layouts  7.74 us (7%)
  Pallas kernels  5.65 us (5%)
    ppermute x20, starting transfers between devices, exchange(): lax.ppermute(values, 'modes', [(i, i ^ offset) for i in range(count)])  30.6 us
    all_to_all x1, waiting for transfers between devices, local(): lax.all_to_all(columns.reshape(count, block_rows, double_width), 'modes',...  20.2 us
    ppermute x20, waiting for transfers between devices, exchange(): lax.ppermute(values, 'modes', [(i, i ^ offset) for i in range(count)])  17 us
    all_to_all x1, starting transfers between devices, local(): pieces = lax.all_to_all(term, ('modes', 'rows'), 0, 0, tiled=True)  5.75 us
    dot_general x1, matrix products, local(): jnp.dot(columns, rows_table, preferred_element_type=f32).astype(bf16)  5.71 us
    pallas_call x2, Pallas kernels, kernel_call(): pl.pallas_call(kernel, out_shape=jax.ShapeDtypeStruct(shape, dtype), in_s...  5.65 us
    all_to_all x1, starting transfers between devices, local(): lax.all_to_all(columns.reshape(count, block_rows, double_width), 'modes',...  4.92 us
    unnamed x32, local copies, waits for them, and re-layouts  4.56 us
  transfers between devices with their start and end apart: 23, of which 13 were waited for; matrix products, arithmetic and copies ran while one was open for 12% of the time, Pallas kernels for 0%

profile of v1, /device:TPU:0, one launch (start us, length us, event | category | flops | bytes accessed | tf_op | source)
XLA Modules:
  0.0 117.8 jit_solution(4262653911414952506)
XLA Ops:
  0.7 1.6 %bitcast_convert_fusion = f32[384,1536]{1,0:T(8,128)S(1)} fusion(bf16[1,384,1536]{2,1,0:T(8,128)(2,1)} %param.7), kind=kLoop, calls=%fused_computation.18 | loop fusion | flops 589824 | bytes 3538944 | tf_op jit(solution)/shard_map/convert_element_type | solution.py:142
  2.3 1.7 %bitcast_convert_fusion.1 = f32[384,1536]{1,0:T(8,128)} fusion(bf16[1,384,1536]{2,1,0:T(8,128)(2,1)S(1)} %copy-done.12), kind=kLoop, calls=%fused_computation.19 | loop fusion | flops 589824 | bytes 3538944 | tf_op jit(solution)/shard_map/convert_element_type | solution.py:143
  4.0 1.9 %multiply_add_fusion = (f32[384,768]{1,0:T(8,128)S(1)}, f32[384,768]{1,0:T(8,128)S(1)}) fusion(f32[384,1536]{1,0:T(8,128)} %bitcast_convert_fusion.1, f32[384,1536]{1,0:T(8,128)S(1)} %bitcast_convert_fusion), kind=kLoop, calls=%fused_computation.21 | loop fusion | flops 1769472 | bytes 7077888 | tf_op jit(solution)/shard_map/add | solution.py:146
  5.9 1.2 fusion.24
  7.2 0.8 fusion.8
  8.0 2.9 %collective-permute-start = (bf16[4,2,24,768]{3,2,0,1:T(8,128)(2,1)}, bf16[4,2,24,768]{3,2,0,1:T(8,128)(2,1)}, u32[]{:S(2)}, u32[]{:S(2)}) collective-permute-start(bf16[4,2,24,768]{3,2,0,1:T(8,128)(2,1)} %fusion.8), channel_id=1, source_target_pairs={{0,2},{2,0},{4,6},{6,4},{8,10},{10,8},{12,14},{14,12},{16,18},{18,... | collective-permute-start | bytes 884744 | tf_op jit(solution)/shard_map/ppermute | solution.py:33
  10.9 1.3 %pad_maximum_fusion.1 = f32[384,768]{1,0:T(8,128)S(1)} fusion(f32[384,384]{1,0:T(8,128)} %get-tuple-element.43, f32[384,384]{1,0:T(8,128)} %get-tuple-element.12), kind=kLoop, calls=%fused_computation.15 | loop fusion | flops 294912 | bytes 2359296 | tf_op jit(solution)/shard_map/concatenate | solution.py:153
  12.2 1.0 copy-done.2
  13.2 0.7 fusion.7
  14.0 1.5 %collective-permute-start.10 = (bf16[4,2,24,768]{3,2,1,0:T(8,128)(2,1)}, bf16[4,2,24,768]{3,2,1,0:T(8,128)(2,1)}, u32[]{:S(2)}, u32[]{:S(2)}) collective-permute-start(bf16[4,2,24,768]{3,2,1,0:T(8,128)(2,1)} %fusion.7), channel_id=1, source_target_pairs={{0,4},{2,6},{4,0},{6,2},{8,12},{10,14},{12,8},{14,10},{16,20},{18,... | collective-permute-start | bytes 884744 | tf_op jit(solution)/shard_map/ppermute | solution.py:33
  15.5 2.7 %collective-permute-done = bf16[4,2,24,768]{3,2,0,1:T(8,128)(2,1)} collective-permute-done((bf16[4,2,24,768]{3,2,0,1:T(8,128)(2,1)}, bf16[4,2,24,768]{3,2,0,1:T(8,128)(2,1)}, u32[]{:S(2)}, u32[]{:S(2)}) %collective-permute-start) | collective-permute-done | bytes 294944 | tf_op jit(solution)/shard_map/ppermute | solution.py:33
  18.2 1.0 bitcast_add_fusion.1
  19.3 1.8 %collective-permute-start.1 = (bf16[4,24,768]{2,1,0:T(8,128)(2,1)S(1)}, bf16[4,24,768]{2,1,0:T(8,128)(2,1)S(1)}, u32[]{:S(2)}, u32[]{:S(2)}) collective-permute-start(bf16[4,24,768]{2,1,0:T(8,128)(2,1)S(1)} %fusion.9), channel_id=1, source_target_pairs={{0,4},{2,6},{4,0},{6,2},{8,12},{10,14},{12,8},{14,10},{16,20},{18,... | collective-permute-start | bytes 442376 | tf_op jit(solution)/shard_map/ppermute | solution.py:33
  21.1 3.0 %collective-permute-done.10 = bf16[4,2,24,768]{3,2,1,0:T(8,128)(2,1)} collective-permute-done((bf16[4,2,24,768]{3,2,1,0:T(8,128)(2,1)}, bf16[4,2,24,768]{3,2,1,0:T(8,128)(2,1)}, u32[]{:S(2)}, u32[]{:S(2)}) %collective-permute-start.10) | collective-permute-done | bytes 294944 | tf_op jit(solution)/shard_map/ppermute | solution.py:33
  24.1 1.0 bitcast_add_fusion
  25.9 1.6 %collective-permute-start.2 = (bf16[24,768]{1,0:T(8,128)(2,1)S(1)}, bf16[24,768]{1,0:T(8,128)(2,1)S(1)}, u32[]{:S(2)}, u32[]{:S(2)}) collective-permute-start(bf16[24,768]{1,0:T(8,128)(2,1)S(1)} %get-tuple-element.19), channel_id=1, source_target_pairs={{0,8},{2,10},{4,12},{6,14},{8,0},{10,2},{12,4},{14,6},{16,24},{18,... | collective-permute-start | bytes 110600 | tf_op jit(solution)/shard_map/ppermute | solution.py:33
  27.5 2.6 %collective-permute-start.3 = (bf16[24,768]{1,0:T(8,128)(2,1)S(1)}, bf16[24,768]{1,0:T(8,128)(2,1)S(1)}, u32[]{:S(2)}, u32[]{:S(2)}) collective-permute-start(bf16[24,768]{1,0:T(8,128)(2,1)S(1)} %get-tuple-element.21), channel_id=1, source_target_pairs={{0,16},{2,18},{4,20},{6,22},{8,24},{10,26},{12,28},{14,30},{16,0},... | collective-permute-start | bytes 110600 | tf_op jit(solution)/shard_map/ppermute | solution.py:33
  30.5 1.7 %collective-permute-start.12 = (bf16[24,768]{1,0:T(8,128)(2,1)S(1)}, bf16[24,768]{1,0:T(8,128)(2,1)S(1)}, u32[]{:S(2)}, u32[]{:S(2)}) collective-permute-start(bf16[24,768]{1,0:T(8,128)(2,1)S(1)} %get-tuple-element.22), channel_id=1, source_target_pairs={{0,8},{2,10},{4,12},{6,14},{8,0},{10,2},{12,4},{14,6},{16,24},{18,... | collective-permute-start | bytes 110600 | tf_op jit(solution)/shard_map/ppermute | solution.py:33
  32.2 2.6 %collective-permute-start.13 = (bf16[24,768]{1,0:T(8,128)(2,1)S(1)}, bf16[24,768]{1,0:T(8,128)(2,1)S(1)}, u32[]{:S(2)}, u32[]{:S(2)}) collective-permute-start(bf16[24,768]{1,0:T(8,128)(2,1)S(1)} %get-tuple-element.24), channel_id=1, source_target_pairs={{0,16},{2,18},{4,20},{6,22},{8,24},{10,26},{12,28},{14,30},{16,0},... | collective-permute-start | bytes 110600 | tf_op jit(solution)/shard_map/ppermute | solution.py:33
  34.9 1.0 collective-permute-done.4
  36.0 3.3 %collective-permute-start.6 = (bf16[24,768]{1,0:T(8,128)(2,1)S(1)}, bf16[24,768]{1,0:T(8,128)(2,1)S(1)}, u32[]{:S(2)}, u32[]{:S(2)}) collective-permute-start(bf16[24,768]{1,0:T(8,128)(2,1)S(1)} %pad_maximum_fusion.14), channel_id=1, source_target_pairs={{0,16},{2,18},{4,20},{6,22},{8,24},{10,26},{12,28},{14,30},{16,0},... | collective-permute-start | bytes 110600 | tf_op jit(solution)/shard_map/ppermute | solution.py:33
  39.3 1.1 collective-permute-start.7
  40.4 0.6 collective-permute-done.14
  41.1 2.7 %collective-permute-start.16 = (bf16[24,768]{1,0:T(8,128)(2,1)S(1)}, bf16[24,768]{1,0:T(8,128)(2,1)S(1)}, u32[]{:S(2)}, u32[]{:S(2)}) collective-permute-start(bf16[24,768]{1,0:T(8,128)(2,1)S(1)} %pad_maximum_fusion.15), channel_id=1, source_target_pairs={{0,16},{2,18},{4,20},{6,22},{8,24},{10,26},{12,28},{14,30},{16,0},... | collective-permute-start | bytes 110600 | tf_op jit(solution)/shard_map/ppermute | solution.py:33
  43.9 1.7 %collective-permute-start.17 = (bf16[24,768]{1,0:T(8,128)(2,1)S(1)}, bf16[24,768]{1,0:T(8,128)(2,1)S(1)}, u32[]{:S(2)}, u32[]{:S(2)}) collective-permute-start(bf16[24,768]{1,0:T(8,128)(2,1)S(1)} %pad_maximum_fusion.15), channel_id=1, source_target_pairs={{0,24},{2,26},{4,28},{6,30},{8,16},{10,18},{12,20},{14,22},{16,8},... | collective-permute-start | bytes 110600 | tf_op jit(solution)/shard_map/ppermute | solution.py:33
  45.6 1.6 %collective-permute-start.8 = (bf16[4,24,768]{2,1,0:T(8,128)(2,1)S(1)}, bf16[4,24,768]{2,1,0:T(8,128)(2,1)S(1)}, u32[]{:S(2)}, u32[]{:S(2)}) collective-permute-start(bf16[4,24,768]{2,1,0:T(8,128)(2,1)S(1)} %get-tuple-element.26), channel_id=1, source_target_pairs={{0,4},{2,6},{4,0},{6,2},{8,12},{10,14},{12,8},{14,10},{16,20},{18,... | collective-permute-start | bytes 442376 | tf_op jit(solution)/shard_map/ppermute | solution.py:33
  47.2 2.4 %collective-permute-done.17 = bf16[24,768]{1,0:T(8,128)(2,1)S(1)} collective-permute-done((bf16[24,768]{1,0:T(8,128)(2,1)S(1)}, bf16[24,768]{1,0:T(8,128)(2,1)S(1)}, u32[]{:S(2)}, u32[]{:S(2)}) %collective-permute-start.17) | collective-permute-done | bytes 36896 | tf_op jit(solution)/shard_map/ppermute | solution.py:33
  49.7 1.5 %collective-permute-start.18 = (bf16[4,24,768]{2,1,0:T(8,128)(2,1)S(1)}, bf16[4,24,768]{2,1,0:T(8,128)(2,1)S(1)}, u32[]{:S(2)}, u32[]{:S(2)}) collective-permute-start(bf16[4,24,768]{2,1,0:T(8,128)(2,1)S(1)} %get-tuple-element.32), channel_id=1, source_target_pairs={{0,2},{2,0},{4,6},{6,4},{8,10},{10,8},{12,14},{14,12},{16,18},{18,... | collective-permute-start | bytes 442376 | tf_op jit(solution)/shard_map/ppermute | solution.py:33
  51.3 1.8 %collective-permute-start.9 = (bf16[4,2,24,768]{3,2,0,1:T(8,128)(2,1)S(1)}, bf16[4,2,24,768]{3,2,0,1:T(8,128)(2,1)S(1)}, u32[]{:S(2)}, u32[]{:S(2)}) collective-permute-start(bf16[4,2,24,768]{3,2,0,1:T(8,128)(2,1)S(1)} %reverse_select_fusion.3), channel_id=1, source_target_pairs={{0,2},{2,0},{4,6},{6,4},{8,10},{10,8},{12,14},{14,12},{16,18},{18,... | collective-permute-start | bytes 884744 | tf_op jit(solution)/shard_map/ppermute | solution.py:33
  53.1 1.8 %collective-permute-done.18 = bf16[4,24,768]{2,1,0:T(8,128)(2,1)S(1)} collective-permute-done((bf16[4,24,768]{2,1,0:T(8,128)(2,1)S(1)}, bf16[4,24,768]{2,1,0:T(8,128)(2,1)S(1)}, u32[]{:S(2)}, u32[]{:S(2)}) %collective-permute-start.18) | collective-permute-done | bytes 147488 | tf_op jit(solution)/shard_map/ppermute | solution.py:33
  55.0 1.6 %collective-permute-start.19 = (bf16[4,2,24,768]{3,2,0,1:T(8,128)(2,1)S(1)}, bf16[4,2,24,768]{3,2,0,1:T(8,128)(2,1)S(1)}, u32[]{:S(2)}, u32[]{:S(2)}) collective-permute-start(bf16[4,2,24,768]{3,2,0,1:T(8,128)(2,1)S(1)} %reverse_select_fusion.2), channel_id=1, source_target_pairs={{0,4},{2,6},{4,0},{6,2},{8,12},{10,14},{12,8},{14,10},{16,20},{18,... | collective-permute-start | bytes 884744 | tf_op jit(solution)/shard_map/ppermute | solution.py:33
  56.6 1.4 %collective-permute-done.9 = bf16[4,2,24,768]{3,2,0,1:T(8,128)(2,1)S(1)} collective-permute-done((bf16[4,2,24,768]{3,2,0,1:T(8,128)(2,1)S(1)}, bf16[4,2,24,768]{3,2,0,1:T(8,128)(2,1)S(1)}, u32[]{:S(2)}, u32[]{:S(2)}) %collective-permute-start.9) | collective-permute-done | bytes 294944 | tf_op jit(solution)/shard_map/ppermute | solution.py:33
  58.4 3.4 %collective-permute-done.19 = bf16[4,2,24,768]{3,2,0,1:T(8,128)(2,1)S(1)} collective-permute-done((bf16[4,2,24,768]{3,2,0,1:T(8,128)(2,1)S(1)}, bf16[4,2,24,768]{3,2,0,1:T(8,128)(2,1)S(1)}, u32[]{:S(2)}, u32[]{:S(2)}) %collective-permute-start.19) | collective-permute-done | bytes 294944 | tf_op jit(solution)/shard_map/ppermute | solution.py:33
  63.1 2.8 %collective-permute-done.20.other_ref = bf16[384,1536]{1,0:T(8,128)(2,1)S(1)} collective-permute-done((bf16[384,1536]{1,0:T(8,128)(2,1)S(1)}, bf16[384,1536]{1,0:T(8,128)(2,1)S(1)}, u32[]{:S(2)}, u32[]{:S(2)}) %collective-permute-start.20) | collective-permute-done | bytes 1179680 | tf_op jit(solution)/shard_map/ppermute | solution.py:167
  65.9 3.7 %shard_map.94 = bf16[384,1536]{1,0:T(8,128)(2,1)} custom-call(bf16[384,1536]{1,0:T(8,128)(2,1)S(1)} %pad_maximum_fusion.3.own_ref, bf16[384,1536]{1,0:T(8,128)(2,1)S(1)} %collective-permute-done.20.other_ref, bf16[384,768]{1,0:T(8,128)(2,1)S(1)} %copy-done, bf16[384,768]{1,0:T(8,128)(2,1)S(1)} %copy-done.1), custom_call_target="tpu_custom_call" | custom-call | flops 1811939328 | bytes 4194304 | tf_op jit(solution)/shard_map/pallas_call | solution.py:122
  69.6 4.9 %all-to-all-start = ((bf16[16,24,1536]{2,1,0:T(8,128)(2,1)}), bf16[16,24,1536]{2,1,0:T(8,128)(2,1)S(1)}, u32[]{:S(2)}, u32[]{:S(2)}) async-start(bf16[16,24,1536]{2,1,0:T(8,128)(2,1)} %bitcast.43), calls=%async_computation | async-start | bytes 2359296 | tf_op jit(solution)/shard_map/all_to_all | solution.py:187
  74.6 1.6 %copy-done.15 = bf16[768,1536]{1,0:T(8,128)(2,1)S(1)} copy-done((bf16[768,1536]{1,0:T(8,128)(2,1)S(1)}, bf16[768,1536]{1,0:T(8,128)(2,1)}, u32[]{:S(2)}) %copy-start.15) | copy-done | bytes 2359320
  76.2 1.1 fusion.29
  77.3 0.6 copy-done.14
  77.8 1.1 fusion.1
  79.3 0.7 copy-done.5
  80.3 1.1 pad_maximum_fusion.2
  81.4 20.2 %all-to-all-done = bf16[16,24,1536]{2,1,0:T(8,128)(2,1)S(1)} async-done(((bf16[16,24,1536]{2,1,0:T(8,128)(2,1)}), bf16[16,24,1536]{2,1,0:T(8,128)(2,1)S(1)}, u32[]{:S(2)}, u32[]{:S(2)}) %all-to-all-start) | async-done | bytes 1179680 | tf_op jit(solution)/shard_map/all_to_all | solution.py:187
  101.6 2.0 %shard_map.95 = f32[16,32]{1,0:T(8,128)S(1)} custom-call(bf16[384,1536]{1,0:T(8,128)(2,1)S(1)} %bitcast.90, bf16[768,1536]{1,0:T(8,128)(2,1)S(1)} %maximum_maximum_fusion.refs_1_), custom_call_target="tpu_custom_call" | custom-call | flops 905969664 | bytes 4194304 | tf_op jit(solution)/shard_map/pallas_call | solution.py:122
  103.7 0.6 pad_maximum_fusion.16
  104.3 5.8 %all-to-all-start.1 = ((f32[32,1,16]{2,1,0:T(1,128)}), f32[32,1,16]{2,1,0:T(1,128)S(1)}, u32[]{:S(2)}, u32[]{:S(2)}) async-start(f32[32,1,16]{2,1,0:T(1,128)} %bitcast.49), calls=%async_computation.1 | async-start | bytes 32768 | tf_op jit(solution)/shard_map/all_to_all | solution.py:200
  110.1 5.7 %fusion.2 = bf16[1,384,1536]{2,1,0:T(8,128)(2,1)} fusion(bf16[384,1536]{1,0:T(8,128)(2,1)} %shard_map.94, bf16[1536,1536]{1,0:T(8,128)(2,1)} %constant.172.clone), kind=kOutput, calls=%fused_computation.4 | convolution fusion | flops 1812529152 | bytes 7077888 | tf_op jit(solution)/shard_map/dot_general | solution.py:190
  115.8 1.4 %all-to-all-done.1 = f32[32,1,16]{2,1,0:T(1,128)S(1)} async-done(((f32[32,1,16]{2,1,0:T(1,128)}), f32[32,1,16]{2,1,0:T(1,128)S(1)}, u32[]{:S(2)}, u32[]{:S(2)}) %all-to-all-start.1) | async-done | bytes 2080 | tf_op jit(solution)/shard_map/all_to_all | solution.py:200
  (86 shorter events, 4.7 us)
Async XLA Ops:
  0.6 1.7 %copy-start.12 = (bf16[1,384,1536]{2,1,0:T(8,128)(2,1)S(1)}, bf16[1,384,1536]{2,1,0:T(8,128)(2,1)}, u32[]{:S(2)}) copy-start(bf16[1,384,1536]{2,1,0:T(8,128)(2,1)} %param.8) | copy-start | bytes 3538948
  8.0 10.3 %collective-permute-start = (bf16[4,2,24,768]{3,2,0,1:T(8,128)(2,1)}, bf16[4,2,24,768]{3,2,0,1:T(8,128)(2,1)}, u32[]{:S(2)}, u32[]{:S(2)}) collective-permute-start(bf16[4,2,24,768]{3,2,0,1:T(8,128)(2,1)} %fusion.8), channel_id=1, source_target_pairs={{0,2},{2,0},{4,6},{6,4},{8,10},{10,8},{12,14},{14,12},{16,18},{18,... | collective-permute-start | bytes 884744 | tf_op jit(solution)/shard_map/ppermute | solution.py:33
  12.2 1.0 copy-start.2
  14.0 10.2 %collective-permute-start.10 = (bf16[4,2,24,768]{3,2,1,0:T(8,128)(2,1)}, bf16[4,2,24,768]{3,2,1,0:T(8,128)(2,1)}, u32[]{:S(2)}, u32[]{:S(2)}) collective-permute-start(bf16[4,2,24,768]{3,2,1,0:T(8,128)(2,1)} %fusion.7), channel_id=1, source_target_pairs={{0,4},{2,6},{4,0},{6,2},{8,12},{10,14},{12,8},{14,10},{16,20},{18,... | collective-permute-start | bytes 884744 | tf_op jit(solution)/shard_map/ppermute | solution.py:33
  15.5 8.6 %copy-start.3 = (f32[384,768]{1,0:T(8,128)S(1)}, f32[384,768]{1,0:T(8,128)}, u32[]{:S(2)}) copy-start(f32[384,768]{1,0:T(8,128)} %copy-done.2) | copy-start | bytes 3538948
  19.3 6.6 %collective-permute-start.1 = (bf16[4,24,768]{2,1,0:T(8,128)(2,1)S(1)}, bf16[4,24,768]{2,1,0:T(8,128)(2,1)S(1)}, u32[]{:S(2)}, u32[]{:S(2)}) collective-permute-start(bf16[4,24,768]{2,1,0:T(8,128)(2,1)S(1)} %fusion.9), channel_id=1, source_target_pairs={{0,4},{2,6},{4,0},{6,2},{8,12},{10,14},{12,8},{14,10},{16,20},{18,... | collective-permute-start | bytes 442376 | tf_op jit(solution)/shard_map/ppermute | solution.py:33
  25.2 5.2 %collective-permute-start.11 = (bf16[4,24,768]{2,1,0:T(8,128)(2,1)S(1)}, bf16[4,24,768]{2,1,0:T(8,128)(2,1)S(1)}, u32[]{:S(2)}, u32[]{:S(2)}) collective-permute-start(bf16[4,24,768]{2,1,0:T(8,128)(2,1)S(1)} %fusion.10), channel_id=1, source_target_pairs={{0,2},{2,0},{4,6},{6,4},{8,10},{10,8},{12,14},{14,12},{16,18},{18,... | collective-permute-start | bytes 442376 | tf_op jit(solution)/shard_map/ppermute | solution.py:33
  25.9 8.9 %collective-permute-start.2 = (bf16[24,768]{1,0:T(8,128)(2,1)S(1)}, bf16[24,768]{1,0:T(8,128)(2,1)S(1)}, u32[]{:S(2)}, u32[]{:S(2)}) collective-permute-start(bf16[24,768]{1,0:T(8,128)(2,1)S(1)} %get-tuple-element.19), channel_id=1, source_target_pairs={{0,8},{2,10},{4,12},{6,14},{8,0},{10,2},{12,4},{14,6},{16,24},{18,... | collective-permute-start | bytes 110600 | tf_op jit(solution)/shard_map/ppermute | solution.py:33
  27.5 7.4 %collective-permute-start.3 = (bf16[24,768]{1,0:T(8,128)(2,1)S(1)}, bf16[24,768]{1,0:T(8,128)(2,1)S(1)}, u32[]{:S(2)}, u32[]{:S(2)}) collective-permute-start(bf16[24,768]{1,0:T(8,128)(2,1)S(1)} %get-tuple-element.21), channel_id=1, source_target_pairs={{0,16},{2,18},{4,20},{6,22},{8,24},{10,26},{12,28},{14,30},{16,0},... | collective-permute-start | bytes 110600 | tf_op jit(solution)/shard_map/ppermute | solution.py:33
  30.1 5.8 %collective-permute-start.4 = (bf16[24,768]{1,0:T(8,128)(2,1)S(1)}, bf16[24,768]{1,0:T(8,128)(2,1)S(1)}, u32[]{:S(2)}, u32[]{:S(2)}) collective-permute-start(bf16[24,768]{1,0:T(8,128)(2,1)S(1)} %get-tuple-element.20), channel_id=1, source_target_pairs={{0,24},{2,26},{4,28},{6,30},{8,16},{10,18},{12,20},{14,22},{16,8},... | collective-permute-start | bytes 110600 | tf_op jit(solution)/shard_map/ppermute | solution.py:33
  30.5 8.8 %collective-permute-start.12 = (bf16[24,768]{1,0:T(8,128)(2,1)S(1)}, bf16[24,768]{1,0:T(8,128)(2,1)S(1)}, u32[]{:S(2)}, u32[]{:S(2)}) collective-permute-start(bf16[24,768]{1,0:T(8,128)(2,1)S(1)} %get-tuple-element.22), channel_id=1, source_target_pairs={{0,8},{2,10},{4,12},{6,14},{8,0},{10,2},{12,4},{14,6},{16,24},{18,... | collective-permute-start | bytes 110600 | tf_op jit(solution)/shard_map/ppermute | solution.py:33
  32.2 8.2 %collective-permute-start.13 = (bf16[24,768]{1,0:T(8,128)(2,1)S(1)}, bf16[24,768]{1,0:T(8,128)(2,1)S(1)}, u32[]{:S(2)}, u32[]{:S(2)}) collective-permute-start(bf16[24,768]{1,0:T(8,128)(2,1)S(1)} %get-tuple-element.24), channel_id=1, source_target_pairs={{0,16},{2,18},{4,20},{6,22},{8,24},{10,26},{12,28},{14,30},{16,0},... | collective-permute-start | bytes 110600 | tf_op jit(solution)/shard_map/ppermute | solution.py:33
  34.8 6.2 %collective-permute-start.14 = (bf16[24,768]{1,0:T(8,128)(2,1)S(1)}, bf16[24,768]{1,0:T(8,128)(2,1)S(1)}, u32[]{:S(2)}, u32[]{:S(2)}) collective-permute-start(bf16[24,768]{1,0:T(8,128)(2,1)S(1)} %get-tuple-element.23), channel_id=1, source_target_pairs={{0,24},{2,26},{4,28},{6,30},{8,16},{10,18},{12,20},{14,22},{16,8},... | collective-permute-start | bytes 110600 | tf_op jit(solution)/shard_map/ppermute | solution.py:33
  36.0 7.9 %collective-permute-start.5 = (bf16[24,768]{1,0:T(8,128)(2,1)S(1)}, bf16[24,768]{1,0:T(8,128)(2,1)S(1)}, u32[]{:S(2)}, u32[]{:S(2)}) collective-permute-start(bf16[24,768]{1,0:T(8,128)(2,1)S(1)} %pad_maximum_fusion.14), channel_id=1, source_target_pairs={{0,8},{2,10},{4,12},{6,14},{8,0},{10,2},{12,4},{14,6},{16,24},{18,... | collective-permute-start | bytes 110600 | tf_op jit(solution)/shard_map/ppermute | solution.py:33
  36.0 9.5 %collective-permute-start.6 = (bf16[24,768]{1,0:T(8,128)(2,1)S(1)}, bf16[24,768]{1,0:T(8,128)(2,1)S(1)}, u32[]{:S(2)}, u32[]{:S(2)}) collective-permute-start(bf16[24,768]{1,0:T(8,128)(2,1)S(1)} %pad_maximum_fusion.14), channel_id=1, source_target_pairs={{0,16},{2,18},{4,20},{6,22},{8,24},{10,26},{12,28},{14,30},{16,0},... | collective-permute-start | bytes 110600 | tf_op jit(solution)/shard_map/ppermute | solution.py:33
  39.3 6.2 %collective-permute-start.7 = (bf16[24,768]{1,0:T(8,128)(2,1)S(1)}, bf16[24,768]{1,0:T(8,128)(2,1)S(1)}, u32[]{:S(2)}, u32[]{:S(2)}) collective-permute-start(bf16[24,768]{1,0:T(8,128)(2,1)S(1)} %pad_maximum_fusion.14), channel_id=1, source_target_pairs={{0,24},{2,26},{4,28},{6,30},{8,16},{10,18},{12,20},{14,22},{16,8},... | collective-permute-start | bytes 110600 | tf_op jit(solution)/shard_map/ppermute | solution.py:33
  41.1 6.1 %collective-permute-start.15 = (bf16[24,768]{1,0:T(8,128)(2,1)S(1)}, bf16[24,768]{1,0:T(8,128)(2,1)S(1)}, u32[]{:S(2)}, u32[]{:S(2)}) collective-permute-start(bf16[24,768]{1,0:T(8,128)(2,1)S(1)} %pad_maximum_fusion.15), channel_id=1, source_target_pairs={{0,8},{2,10},{4,12},{6,14},{8,0},{10,2},{12,4},{14,6},{16,24},{18,... | collective-permute-start | bytes 110600 | tf_op jit(solution)/shard_map/ppermute | solution.py:33
  41.1 6.1 %collective-permute-start.16 = (bf16[24,768]{1,0:T(8,128)(2,1)S(1)}, bf16[24,768]{1,0:T(8,128)(2,1)S(1)}, u32[]{:S(2)}, u32[]{:S(2)}) collective-permute-start(bf16[24,768]{1,0:T(8,128)(2,1)S(1)} %pad_maximum_fusion.15), channel_id=1, source_target_pairs={{0,16},{2,18},{4,20},{6,22},{8,24},{10,26},{12,28},{14,30},{16,0},... | collective-permute-start | bytes 110600 | tf_op jit(solution)/shard_map/ppermute | solution.py:33
  43.9 5.8 %collective-permute-start.17 = (bf16[24,768]{1,0:T(8,128)(2,1)S(1)}, bf16[24,768]{1,0:T(8,128)(2,1)S(1)}, u32[]{:S(2)}, u32[]{:S(2)}) collective-permute-start(bf16[24,768]{1,0:T(8,128)(2,1)S(1)} %pad_maximum_fusion.15), channel_id=1, source_target_pairs={{0,24},{2,26},{4,28},{6,30},{8,16},{10,18},{12,20},{14,22},{16,8},... | collective-permute-start | bytes 110600 | tf_op jit(solution)/shard_map/ppermute | solution.py:33
  45.6 5.6 %collective-permute-start.8 = (bf16[4,24,768]{2,1,0:T(8,128)(2,1)S(1)}, bf16[4,24,768]{2,1,0:T(8,128)(2,1)S(1)}, u32[]{:S(2)}, u32[]{:S(2)}) collective-permute-start(bf16[4,24,768]{2,1,0:T(8,128)(2,1)S(1)} %get-tuple-element.26), channel_id=1, source_target_pairs={{0,4},{2,6},{4,0},{6,2},{8,12},{10,14},{12,8},{14,10},{16,20},{18,... | collective-permute-start | bytes 442376 | tf_op jit(solution)/shard_map/ppermute | solution.py:33
  49.7 5.2 %collective-permute-start.18 = (bf16[4,24,768]{2,1,0:T(8,128)(2,1)S(1)}, bf16[4,24,768]{2,1,0:T(8,128)(2,1)S(1)}, u32[]{:S(2)}, u32[]{:S(2)}) collective-permute-start(bf16[4,24,768]{2,1,0:T(8,128)(2,1)S(1)} %get-tuple-element.32), channel_id=1, source_target_pairs={{0,2},{2,0},{4,6},{6,4},{8,10},{10,8},{12,14},{14,12},{16,18},{18,... | collective-permute-start | bytes 442376 | tf_op jit(solution)/shard_map/ppermute | solution.py:33
  51.3 6.8 %collective-permute-start.9 = (bf16[4,2,24,768]{3,2,0,1:T(8,128)(2,1)S(1)}, bf16[4,2,24,768]{3,2,0,1:T(8,128)(2,1)S(1)}, u32[]{:S(2)}, u32[]{:S(2)}) collective-permute-start(bf16[4,2,24,768]{3,2,0,1:T(8,128)(2,1)S(1)} %reverse_select_fusion.3), channel_id=1, source_target_pairs={{0,2},{2,0},{4,6},{6,4},{8,10},{10,8},{12,14},{14,12},{16,18},{18,... | collective-permute-start | bytes 884744 | tf_op jit(solution)/shard_map/ppermute | solution.py:33
  55.0 6.8 %collective-permute-start.19 = (bf16[4,2,24,768]{3,2,0,1:T(8,128)(2,1)S(1)}, bf16[4,2,24,768]{3,2,0,1:T(8,128)(2,1)S(1)}, u32[]{:S(2)}, u32[]{:S(2)}) collective-permute-start(bf16[4,2,24,768]{3,2,0,1:T(8,128)(2,1)S(1)} %reverse_select_fusion.2), channel_id=1, source_target_pairs={{0,4},{2,6},{4,0},{6,2},{8,12},{10,14},{12,8},{14,10},{16,20},{18,... | collective-permute-start | bytes 884744 | tf_op jit(solution)/shard_map/ppermute | solution.py:33
  58.4 3.7 %copy-start.4 = (bf16[384,384]{1,0:T(8,128)(2,1)}, bf16[384,384]{1,0:T(8,128)(2,1)S(1)}, u32[]{:S(2)}) copy-start(bf16[384,384]{1,0:T(8,128)(2,1)S(1)} %get-tuple-element.15) | copy-start | bytes 884740
  58.4 3.7 %copy-start.6 = (bf16[384,384]{1,0:T(8,128)(2,1)}, bf16[384,384]{1,0:T(8,128)(2,1)S(1)}, u32[]{:S(2)}) copy-start(bf16[384,384]{1,0:T(8,128)(2,1)S(1)} %get-tuple-element.16) | copy-start | bytes 884740
  62.1 0.8 copy-start.8
  62.1 0.8 copy-start.10
  62.9 3.0 %copy-start = (bf16[384,768]{1,0:T(8,128)(2,1)S(1)}, bf16[384,768]{1,0:T(8,128)(2,1)}, u32[]{:S(2)}) copy-start(bf16[384,768]{1,0:T(8,128)(2,1)} %constant.169.clone.re_ref) | copy-start | bytes 1769476
  62.9 3.0 %copy-start.1 = (bf16[384,768]{1,0:T(8,128)(2,1)S(1)}, bf16[384,768]{1,0:T(8,128)(2,1)}, u32[]{:S(2)}) copy-start(bf16[384,768]{1,0:T(8,128)(2,1)} %constant.170.clone.im_ref) | copy-start | bytes 1769476
  63.0 2.9 %collective-permute-start.20 = (bf16[384,1536]{1,0:T(8,128)(2,1)S(1)}, bf16[384,1536]{1,0:T(8,128)(2,1)S(1)}, u32[]{:S(2)}, u32[]{:S(2)}) collective-permute-start(bf16[384,1536]{1,0:T(8,128)(2,1)S(1)} %pad_maximum_fusion.3.own_ref), channel_id=1, source_target_pairs={{0,1},{1,0},{2,3},{3,2},{4,5},{5,4},{6,7},{7,6},{8,9},{9,8},{10,11... | collective-permute-start | bytes 3538952 | tf_op jit(solution)/shard_map/ppermute | solution.py:167
  69.6 4.9 %copy-start.13 = (bf16[2,16,24,768]{3,2,1,0:T(8,128)(2,1)S(1)}, bf16[2,16,24,768]{3,2,1,0:T(8,128)(2,1)}, u32[]{:S(2)}) copy-start(bf16[2,16,24,768]{3,2,1,0:T(8,128)(2,1)} %param.9) | copy-start | bytes 3538948
  69.6 32.0 %all-to-all-start = ((bf16[16,24,1536]{2,1,0:T(8,128)(2,1)}), bf16[16,24,1536]{2,1,0:T(8,128)(2,1)S(1)}, u32[]{:S(2)}, u32[]{:S(2)}) async-start(bf16[16,24,1536]{2,1,0:T(8,128)(2,1)} %bitcast.43), calls=%async_computation | async-start | bytes 2359296 | tf_op jit(solution)/shard_map/all_to_all | solution.py:187
  74.5 1.7 %copy-start.15 = (bf16[768,1536]{1,0:T(8,128)(2,1)S(1)}, bf16[768,1536]{1,0:T(8,128)(2,1)}, u32[]{:S(2)}) copy-start(bf16[768,1536]{1,0:T(8,128)(2,1)} %constant.176) | copy-start | bytes 7077892
  76.2 1.7 %copy-start.14 = (bf16[768,1536]{1,0:T(8,128)(2,1)S(1)}, bf16[768,1536]{1,0:T(8,128)(2,1)}, u32[]{:S(2)}) copy-start(bf16[768,1536]{1,0:T(8,128)(2,1)} %constant.177) | copy-start | bytes 7077892
  79.0 1.0 copy-start.5
  79.0 1.0 copy-start.7
  79.1 1.1 copy-start.9
  79.1 1.2 %copy-start.11 = (bf16[384,384]{1,0:T(8,128)(2,1)S(1)}, bf16[384,384]{1,0:T(8,128)(2,1)}, u32[]{:S(2)}) copy-start(bf16[384,384]{1,0:T(8,128)(2,1)} %copy-done.10) | copy-start | bytes 884740
  104.3 12.9 %all-to-all-start.1 = ((f32[32,1,16]{2,1,0:T(1,128)}), f32[32,1,16]{2,1,0:T(1,128)S(1)}, u32[]{:S(2)}, u32[]{:S(2)}) async-start(f32[32,1,16]{2,1,0:T(1,128)} %bitcast.49), calls=%async_computation.1 | async-start | bytes 32768 | tf_op jit(solution)/shard_map/all_to_all | solution.py:200

commit v2 on v1

--- a/solution.py
+++ b/solution.py
@@ -37,39 +37,58 @@
     return lax.dynamic_index_in_dim(values, index, axis, keepdims=False)
 
 
-def reduce_part(partial, digits, order, count):
+def reduce_digit(keep, got):
+    for g in got:
+        keep = keep + g.astype(f32)
+    return keep
+
+
+def gather_digit(block, own, stride, size, axis, count):
+    got = [block] + [exchange(block, e * stride, count) for e in range(1, size)]
+    stacked = jnp.stack(got, axis)
+    if size == 2:
+        return jnp.where(own == 0, stacked, jnp.flip(stacked, axis))
+    return jnp.stack([pick(stacked, own ^ at, axis) for at in range(size)], axis)
+
+
+def split_digit(partial, own, size, axis):
+    send = [pick(partial, own ^ e, axis).astype(bf16) for e in range(1, size)]
+    return send, pick(partial, own, axis)
+
+
+def product_of(fore, back):
+    half = fore.shape[-1] // 2
+    fore, back = fore.astype(f32), back.astype(f32)
+    fore_re, fore_im = fore[..., :half], fore[..., half:]
+    back_re, back_im = back[..., :half], back[..., half:]
+    return back_re * fore_re + back_im * fore_im, back_re * fore_im - back_im * fore_re
+
+
+def products_kernel(rows, fore_ref, back_ref, send_a, keep_a, send_b, keep_b):
     me = lax.axis_index("modes")
-    axes = [len(digits) - 1 - d for d in range(len(digits))]
-    for d in order:
-        stride, size = digits[d]
-        own = me // stride % size
-        axis = axes[d]
-        got = [
-            exchange(pick(partial, own ^ e, axis).astype(bf16), e * stride, count)
-            for e in range(1, size)
-        ]
-        partial = pick(partial, own, axis)
-        for g in got:
-            partial = partial + g.astype(f32)
-        axes = [a - (a > axis) for a in axes]
-    return partial
-
-
-def gather_part(block, digits, order, count):
-    me = lax.axis_index("modes")
-    done = []
-    for d in reversed(order):
-        stride, size = digits[d]
-        own = me // stride % size
-        got = [block] + [exchange(block, e * stride, count) for e in range(1, size)]
-        axis = sum(1 for other in done if other > d)
-        stacked = jnp.stack(got, axis)
-        if size == 2:
-            block = jnp.where(own == 0, stacked, jnp.flip(stacked, axis))
-        else:
-            block = jnp.stack([pick(stacked, own ^ at, axis) for at in range(size)], axis)
-        done.append(d)
-    return block
+    low, high = me % 2 == 1, me // 2 % 2 == 1
+    grid_size = fore_ref.shape[1] // 2
+    half = grid_size // 2
+    pair = 2 * rows
+    for group in range(fore_ref.shape[0] // (4 * rows)):
+        at = pl.ds(group * 4 * rows, 4 * rows)
+        out = pl.ds(group * pair, pair)
+        for part in range(2):
+            cols = [pl.ds(part * half, half), pl.ds(grid_size + part * half, half)]
+            fore_re, fore_im = [fore_ref[at, c].astype(f32) for c in cols]
+            back_re, back_im = [back_ref[at, c].astype(f32) for c in cols]
+            values = (back_re * fore_re + back_im * fore_im, back_re * fore_im - back_im * fore_re)
+            for k, v in enumerate(values):
+                into = pl.ds(k * half, half)
+                if part == 0:
+                    first = jnp.concatenate([v[:rows], v[pair : pair + rows]], 0)
+                    second = jnp.concatenate([v[rows:pair], v[pair + rows :]], 0)
+                    send_a[out, into] = jnp.where(low, first, second).astype(bf16)
+                    keep_a[out, into] = jnp.where(low, second, first)
+                else:
+                    first, second = v[:pair], v[pair:]
+                    send_b[out, into] = jnp.where(high, first, second).astype(bf16)
+                    keep_b[out, into] = jnp.where(high, second, first)
 
 
 def columns_kernel(own_ref, other_ref, re_ref, im_ref, out_ref):
@@ -119,11 +138,17 @@
 
 
 def kernel_call(kernel, shape, dtype, flops, operands):
+    place = pl.BlockSpec(memory_space=pltpu.VMEM)
+    several = isinstance(dtype, list)
+    if several:
+        out_shape = [jax.ShapeDtypeStruct(s, d) for s, d in zip(shape, dtype)]
+    else:
+        out_shape = jax.ShapeDtypeStruct(shape, dtype)
     return pl.pallas_call(
         kernel,
-        out_shape=jax.ShapeDtypeStruct(shape, dtype),
-        in_specs=[pl.BlockSpec(memory_space=pltpu.VMEM)] * len(operands),
-        out_specs=pl.BlockSpec(memory_space=pltpu.VMEM),
+        out_shape=out_shape,
+        in_specs=[place] * len(operands),
+        out_specs=[place] * len(shape) if several else place,
         compiler_params=pltpu.CompilerParams(vmem_limit_bytes=32 * 1024 * 1024),
         cost_estimate=pl.CostEstimate(flops=flops, bytes_accessed=4 << 20, transcendentals=0),
     )(*operands)
@@ -139,27 +164,66 @@
     sizes = [size for _, size in reversed(digits)]
     half = grid_size // 2
 
-    fore = forward[0].astype(f32)
-    back = backward[0].astype(f32)
-    fore_re, fore_im = fore[:, :grid_size], fore[:, grid_size:]
-    back_re, back_im = back[:, :grid_size], back[:, grid_size:]
-    partial_re = back_re * fore_re + back_im * fore_im
-    partial_im = back_re * fore_im - back_im * fore_re
-    first = list(range(len(digits)))
+    me = lax.axis_index("modes")
+    owns = [me // stride % size for stride, size in digits]
+    last = len(digits) - 1
+    first = list(range(last))
     orders = [first, [1, 0] + first[2:]]
+    kernel_first = block_rows % 8 == 0 and local_rows % (4 * block_rows) == 0
+    if kernel_first:
+        halves = kernel_call(
+            lambda *refs: products_kernel(block_rows, *refs),
+            [(local_rows // 2, grid_size)] * 4,
+            [bf16, f32, bf16, f32],
+            8 * local_rows * double_width,
+            (forward[0], backward[0]),
+        )
+    else:
+        product = product_of(forward[0], backward[0])
+    kept = []
+    for part, order in enumerate(orders):
+        cols = slice(part * half, (part + 1) * half)
+        axes = [last - d for d in range(len(digits))]
+        if not kernel_first:
+            partial = jnp.concatenate([p[:, cols] for p in product], -1)
+            partial = partial.reshape(*sizes, block_rows, grid_size)
+        for at, d in enumerate(order):
+            stride, size = digits[d]
+            left = sizes[: axes[d]] + sizes[axes[d] + 1 :] if at == 0 else None
+            if at == 0 and kernel_first:
+                send = [halves[2 * part].reshape(*left, block_rows, grid_size)]
+                keep = halves[2 * part + 1].reshape(*left, block_rows, grid_size)
+            else:
+                send, keep = split_digit(partial, owns[d], size, axes[d])
+            got = [exchange(v, (e + 1) * stride, count) for e, v in enumerate(send)]
+            partial = reduce_digit(keep, got)
+            axes = [a - (a > axes[d]) for a in axes]
+        kept.append(partial)
+    stride, size = digits[last]
+    send, keep = split_digit(jnp.concatenate(kept, -1), owns[last], size, 0)
+    got = [exchange(v, (e + 1) * stride, count) for e, v in enumerate(send)]
+    summed = reduce_digit(keep, got).reshape(block_rows, 2, 2, half)
+    over_re, over_im = summed[:, :, 0], summed[:, :, 1]
+    scale = lax.rsqrt(over_re * over_re + over_im * over_im + mode_total)
+    block = jnp.stack([over_re * scale, over_im * scale], 2).astype(bf16)
+    block = block.reshape(block_rows, double_width)
+
+    block = gather_digit(block, owns[last], stride, size, 0, count)
     planes = []
     for part, order in enumerate(orders):
-        cols = slice(part * half, (part + 1) * half)
-        partial = jnp.concatenate([partial_re[:, cols], partial_im[:, cols]], -1)
-        summed = reduce_part(partial.reshape(*sizes, block_rows, grid_size), digits, order, count)
-        over_re, over_im = summed[:, :half], summed[:, half:]
-        scale = lax.rsqrt(over_re * over_re + over_im * over_im + mode_total)
-        block = jnp.concatenate([over_re * scale, over_im * scale], -1).astype(bf16)
-        planes.append(gather_part(block, digits, order, count).reshape(local_rows, grid_size))
+        piece = block[..., part * grid_size : (part + 1) * grid_size]
+        done = [last]
+        for d in reversed(order):
+            axis = sum(1 for other in done if other > d)
+            piece = gather_digit(piece, owns[d], *digits[d], axis, count)
+            done.append(d)
+        planes.append(piece.reshape(local_rows, grid_size))
     plane_re = jnp.concatenate([p[:, :half] for p in planes], -1)
     plane_im = jnp.concatenate([p[:, half:] for p in planes], -1)
     phase_plane = jnp.concatenate([plane_re, plane_im], -1)
 
+    fore = forward[0].astype(f32)
+    fore_re, fore_im = fore[:, :grid_size], fore[:, grid_size:]
     plane_re, plane_im = plane_re.astype(f32), plane_im.astype(f32)
     shaped = jnp.concatenate(
         [fore_re * plane_re - fore_im * plane_im, fore_re * plane_im + fore_im * plane_re], -1
@@ -188,6 +252,7 @@
         columns.reshape(count, block_rows, double_width), "modes", 0, 0, tiled=True
     )
     output_fields = jnp.dot(columns, rows_table, preferred_element_type=f32).astype(bf16)
+    pixels, output_fields = lax.optimization_barrier((pixels, output_fields))
 
     term = kernel_call(
         lambda *refs: coupling_kernel(block_rows, *refs),

time: 118 us -> 110 us (0.932)
  waiting for transfers between devices: 41.5 us -> 52.2 us
  starting transfers between devices: 41.3 us -> 32.2 us
  other arithmetic: 12.6 us -> 5.51 us
  local copies, waits for them, and re-layouts: 7.74 us -> 4.05 us
    ppermute x20 -> x14, waiting for transfers between devices: 17 us -> 26.2 us  [exchange(): lax.ppermute(values, 'modes', [(i, i ^ offset) for i in range(count)])]
    ppermute x20 -> x14, starting transfers between devices: 30.6 us -> 21.7 us  [exchange(): lax.ppermute(values, 'modes', [(i, i ^ offset) for i in range(count)])]
    add x7 -> x5, other arithmetic: 4.05 us -> 0.19 us  [reduce_digit(): keep = keep + g.astype(f32)]
    all_to_all x1, waiting for transfers between devices: 1.44 us -> 4.81 us  [local(): pieces = lax.all_to_all(term, ('modes', 'rows'), 0, 0, tiled=True)]
    all_to_all x1, waiting for transfers between devices: 20.2 us -> 18.4 us  [local(): lax.all_to_all(columns.reshape(count, block_rows, double_width), 'modes',...]
    dot_general x2, matrix products: 2.17 us -> 3.97 us  [local(): seen = jnp.dot(flat, back_table, preferred_element_type=f32).astype(bf16)]
    convert_element_type x1 -> x2, other arithmetic: 1.7 us -> 0.06 us  [the longest x1 0.04 us: split_digit(): send = [pick(partial, own ^ e, axis).astype(bf16) for e in range(1, size)]]
    dot_general x1, matrix products: 5.71 us -> 4.28 us  [local(): jnp.dot(columns, rows_table, preferred_element_type=f32).astype(bf16)]
  transfers between devices with their start and end apart: 23 -> 17, of which waited for: 13 -> 13; matrix products, arithmetic and copies ran while one was open for 12% -> 11% of each run, Pallas kernels for 0% -> 0%
where the time goes in v2:
time: 110 us
  waiting for transfers between devices  52.2 us (47%)
  starting transfers between devices  32.2 us (29%)
  matrix products  8.24 us (7%)
  Pallas kernels  6.23 us (6%)
  other arithmetic  5.51 us (5%)
  local copies, waits for them, and re-layouts  4.05 us (4%)
    ppermute x14, waiting for transfers between devices, exchange(): lax.ppermute(values, 'modes', [(i, i ^ offset) for i in range(count)])  26.2 us
    ppermute x14, starting transfers between devices, exchange(): lax.ppermute(values, 'modes', [(i, i ^ offset) for i in range(count)])  21.7 us
    all_to_all x1, waiting for transfers between devices, local(): lax.all_to_all(columns.reshape(count, block_rows, double_width), 'modes',...  18.4 us
    pallas_call x3, Pallas kernels, kernel_call(): pl.pallas_call(kernel, out_shape=out_shape, in_specs=[place] * len(operan...  6.23 us
    all_to_all x1, starting transfers between devices, local(): pieces = lax.all_to_all(term, ('modes', 'rows'), 0, 0, tiled=True)  5.74 us
    all_to_all x1, waiting for transfers between devices, local(): pieces = lax.all_to_all(term, ('modes', 'rows'), 0, 0, tiled=True)  4.81 us
    all_to_all x1, starting transfers between devices, local(): lax.all_to_all(columns.reshape(count, block_rows, double_width), 'modes',...  4.68 us
    dot_general x1, matrix products, local(): jnp.dot(columns, rows_table, preferred_element_type=f32).astype(bf16)  4.28 us
  transfers between devices with their start and end apart: 17, of which 13 were waited for; matrix products, arithmetic and copies ran while one was open for 11% of the time, Pallas kernels for 0%

profile of v2, /device:TPU:0, one launch (start us, length us, event | category | flops | bytes accessed | tf_op | source)
XLA Modules:
  0.0 109.5 jit_solution(13332516795498970084)
XLA Ops:
  0.6 1.3 %copy-done = bf16[1,384,1536]{2,1,0:T(8,128)(2,1)S(1)} copy-done((bf16[1,384,1536]{2,1,0:T(8,128)(2,1)S(1)}, bf16[1,384,1536]{2,1,0:T(8,128)(2,1)}, u32[]{:S(2)}) %copy-start) | copy-done | bytes 1179672
  1.9 1.3 %copy-done.2 = bf16[1,384,1536]{2,1,0:T(8,128)(2,1)S(1)} copy-done((bf16[1,384,1536]{2,1,0:T(8,128)(2,1)S(1)}, bf16[1,384,1536]{2,1,0:T(8,128)(2,1)}, u32[]{:S(2)}) %copy-start.2) | copy-done | bytes 1179672
  3.2 0.6 shard_map.94
  3.9 3.0 %collective-permute-start = (bf16[4,2,24,768]{3,2,0,1:T(8,128)(2,1)S(1)}, bf16[4,2,24,768]{3,2,0,1:T(8,128)(2,1)S(1)}, u32[]{:S(2)}, u32[]{:S(2)}) collective-permute-start(bf16[4,2,24,768]{3,2,0,1:T(8,128)(2,1)S(1)} %copy.33), channel_id=1, source_target_pairs={{0,2},{2,0},{4,6},{6,4},{8,10},{10,8},{12,14},{14,12},{16,18},{18,... | collective-permute-start | bytes 884744 | tf_op jit(solution)/shard_map/ppermute | solution.py:33
  6.9 1.6 %collective-permute-start.2 = (bf16[4,2,24,768]{3,2,0,1:T(8,128)(2,1)S(1)}, bf16[4,2,24,768]{3,2,0,1:T(8,128)(2,1)S(1)}, u32[]{:S(2)}, u32[]{:S(2)}) collective-permute-start(bf16[4,2,24,768]{3,2,0,1:T(8,128)(2,1)S(1)} %copy.35), channel_id=1, source_target_pairs={{0,4},{2,6},{4,0},{6,2},{8,12},{10,14},{12,8},{14,10},{16,20},{18,... | collective-permute-start | bytes 884744 | tf_op jit(solution)/shard_map/ppermute | solution.py:33
  8.5 5.4 %collective-permute-done = bf16[4,2,24,768]{3,2,0,1:T(8,128)(2,1)S(1)} collective-permute-done((bf16[4,2,24,768]{3,2,0,1:T(8,128)(2,1)S(1)}, bf16[4,2,24,768]{3,2,0,1:T(8,128)(2,1)S(1)}, u32[]{:S(2)}, u32[]{:S(2)}) %collective-permute-start) | collective-permute-done | bytes 294944 | tf_op jit(solution)/shard_map/ppermute | solution.py:33
  14.0 1.8 %collective-permute-start.1 = (bf16[4,24,768]{2,1,0:T(8,128)(2,1)S(1)}, bf16[4,24,768]{2,1,0:T(8,128)(2,1)S(1)}, u32[]{:S(2)}, u32[]{:S(2)}) collective-permute-start(bf16[4,24,768]{2,1,0:T(8,128)(2,1)S(1)} %fusion.6), channel_id=1, source_target_pairs={{0,4},{2,6},{4,0},{6,2},{8,12},{10,14},{12,8},{14,10},{16,20},{18,... | collective-permute-start | bytes 442376 | tf_op jit(solution)/shard_map/ppermute | solution.py:33
  15.9 1.6 %collective-permute-start.3 = (bf16[4,24,768]{2,1,0:T(8,128)(2,1)S(1)}, bf16[4,24,768]{2,1,0:T(8,128)(2,1)S(1)}, u32[]{:S(2)}, u32[]{:S(2)}) collective-permute-start(bf16[4,24,768]{2,1,0:T(8,128)(2,1)S(1)} %fusion.7), channel_id=1, source_target_pairs={{0,2},{2,0},{4,6},{6,4},{8,10},{10,8},{12,14},{14,12},{16,18},{18,... | collective-permute-start | bytes 442376 | tf_op jit(solution)/shard_map/ppermute | solution.py:33
  17.4 1.7 %collective-permute-done.1 = bf16[4,24,768]{2,1,0:T(8,128)(2,1)S(1)} collective-permute-done((bf16[4,24,768]{2,1,0:T(8,128)(2,1)S(1)}, bf16[4,24,768]{2,1,0:T(8,128)(2,1)S(1)}, u32[]{:S(2)}, u32[]{:S(2)}) %collective-permute-start.1) | collective-permute-done | bytes 147488 | tf_op jit(solution)/shard_map/ppermute | solution.py:33
  19.2 1.9 %collective-permute-done.3 = bf16[4,24,768]{2,1,0:T(8,128)(2,1)S(1)} collective-permute-done((bf16[4,24,768]{2,1,0:T(8,128)(2,1)S(1)}, bf16[4,24,768]{2,1,0:T(8,128)(2,1)S(1)}, u32[]{:S(2)}, u32[]{:S(2)}) %collective-permute-start.3) | collective-permute-done | bytes 147488 | tf_op jit(solution)/shard_map/ppermute | solution.py:33
  21.2 3.7 %collective-permute-start.6 = (bf16[24,1536]{1,0:T(8,128)(2,1)S(1)}, bf16[24,1536]{1,0:T(8,128)(2,1)S(1)}, u32[]{:S(2)}, u32[]{:S(2)}) collective-permute-start(bf16[24,1536]{1,0:T(8,128)(2,1)S(1)} %get-tuple-element.27), channel_id=1, source_target_pairs={{0,24},{2,26},{4,28},{6,30},{8,16},{10,18},{12,20},{14,22},{16,8},... | collective-permute-start | bytes 221192 | tf_op jit(solution)/shard_map/ppermute | solution.py:33
  24.8 0.8 collective-permute-start.4
  25.6 2.2 %collective-permute-done.6 = bf16[24,1536]{1,0:T(8,128)(2,1)S(1)} collective-permute-done((bf16[24,1536]{1,0:T(8,128)(2,1)S(1)}, bf16[24,1536]{1,0:T(8,128)(2,1)S(1)}, u32[]{:S(2)}, u32[]{:S(2)}) %collective-permute-start.6) | collective-permute-done | bytes 73760 | tf_op jit(solution)/shard_map/ppermute | solution.py:33
  27.8 2.3 %collective-permute-done.5 = bf16[24,1536]{1,0:T(8,128)(2,1)S(1)} collective-permute-done((bf16[24,1536]{1,0:T(8,128)(2,1)S(1)}, bf16[24,1536]{1,0:T(8,128)(2,1)S(1)}, u32[]{:S(2)}, u32[]{:S(2)}) %collective-permute-start.5) | collective-permute-done | bytes 73760 | tf_op jit(solution)/shard_map/ppermute | solution.py:33
  30.2 0.1 fusion.27
  30.5 1.9 %collective-permute-start.9 = (bf16[24,1536]{1,0:T(8,128)(2,1)S(1)}, bf16[24,1536]{1,0:T(8,128)(2,1)S(1)}, u32[]{:S(2)}, u32[]{:S(2)}) collective-permute-start(bf16[24,1536]{1,0:T(8,128)(2,1)S(1)} %convert_element_type.103), channel_id=1, source_target_pairs={{0,24},{2,26},{4,28},{6,30},{8,16},{10,18},{12,20},{14,22},{16,8},... | collective-permute-start | bytes 221192 | tf_op jit(solution)/shard_map/ppermute | solution.py:33
  32.4 0.4 collective-permute-start.8
  32.8 2.2 %collective-permute-start.7 = (bf16[24,1536]{1,0:T(8,128)(2,1)S(1)}, bf16[24,1536]{1,0:T(8,128)(2,1)S(1)}, u32[]{:S(2)}, u32[]{:S(2)}) collective-permute-start(bf16[24,1536]{1,0:T(8,128)(2,1)S(1)} %convert_element_type.103), channel_id=1, source_target_pairs={{0,8},{2,10},{4,12},{6,14},{8,0},{10,2},{12,4},{14,6},{16,24},{18,... | collective-permute-start | bytes 221192 | tf_op jit(solution)/shard_map/ppermute | solution.py:33
  35.0 1.7 %collective-permute-done.9 = bf16[24,1536]{1,0:T(8,128)(2,1)S(1)} collective-permute-done((bf16[24,1536]{1,0:T(8,128)(2,1)S(1)}, bf16[24,1536]{1,0:T(8,128)(2,1)S(1)}, u32[]{:S(2)}, u32[]{:S(2)}) %collective-permute-start.9) | collective-permute-done | bytes 73760 | tf_op jit(solution)/shard_map/ppermute | solution.py:33
  36.8 1.7 %collective-permute-done.8 = bf16[24,1536]{1,0:T(8,128)(2,1)S(1)} collective-permute-done((bf16[24,1536]{1,0:T(8,128)(2,1)S(1)}, bf16[24,1536]{1,0:T(8,128)(2,1)S(1)}, u32[]{:S(2)}, u32[]{:S(2)}) %collective-permute-start.8) | collective-permute-done | bytes 73760 | tf_op jit(solution)/shard_map/ppermute | solution.py:33
  38.6 1.2 %collective-permute-start.10 = (bf16[4,24,768]{2,1,0:T(8,128)(2,1)S(1)}, bf16[4,24,768]{2,1,0:T(8,128)(2,1)S(1)}, u32[]{:S(2)}, u32[]{:S(2)}) collective-permute-start(bf16[4,24,768]{2,1,0:T(8,128)(2,1)S(1)} %get-tuple-element.31), channel_id=1, source_target_pairs={{0,4},{2,6},{4,0},{6,2},{8,12},{10,14},{12,8},{14,10},{16,20},{18,... | collective-permute-start | bytes 442376 | tf_op jit(solution)/shard_map/ppermute | solution.py:33
  39.9 0.3 bitcast_convert_fusion
  40.2 1.5 %collective-permute-start.12 = (bf16[4,24,768]{2,1,0:T(8,128)(2,1)S(1)}, bf16[4,24,768]{2,1,0:T(8,128)(2,1)S(1)}, u32[]{:S(2)}, u32[]{:S(2)}) collective-permute-start(bf16[4,24,768]{2,1,0:T(8,128)(2,1)S(1)} %get-tuple-element.30), channel_id=1, source_target_pairs={{0,2},{2,0},{4,6},{6,4},{8,10},{10,8},{12,14},{14,12},{16,18},{18,... | collective-permute-start | bytes 442376 | tf_op jit(solution)/shard_map/ppermute | solution.py:33
  41.6 3.3 %collective-permute-done.10 = bf16[4,24,768]{2,1,0:T(8,128)(2,1)S(1)} collective-permute-done((bf16[4,24,768]{2,1,0:T(8,128)(2,1)S(1)}, bf16[4,24,768]{2,1,0:T(8,128)(2,1)S(1)}, u32[]{:S(2)}, u32[]{:S(2)}) %collective-permute-start.10) | collective-permute-done | bytes 147488 | tf_op jit(solution)/shard_map/ppermute | solution.py:33
  45.1 1.6 %collective-permute-start.11 = (bf16[4,2,24,768]{3,2,0,1:T(8,128)(2,1)S(1)}, bf16[4,2,24,768]{3,2,0,1:T(8,128)(2,1)S(1)}, u32[]{:S(2)}, u32[]{:S(2)}) collective-permute-start(bf16[4,2,24,768]{3,2,0,1:T(8,128)(2,1)S(1)} %reverse_select_fusion.3), channel_id=1, source_target_pairs={{0,2},{2,0},{4,6},{6,4},{8,10},{10,8},{12,14},{14,12},{16,18},{18,... | collective-permute-start | bytes 884744 | tf_op jit(solution)/shard_map/ppermute | solution.py:33
  46.8 0.6 collective-permute-start.13
  47.4 4.4 %collective-permute-done.11 = bf16[4,2,24,768]{3,2,0,1:T(8,128)(2,1)S(1)} collective-permute-done((bf16[4,2,24,768]{3,2,0,1:T(8,128)(2,1)S(1)}, bf16[4,2,24,768]{3,2,0,1:T(8,128)(2,1)S(1)}, u32[]{:S(2)}, u32[]{:S(2)}) %collective-permute-start.11) | collective-permute-done | bytes 294944 | tf_op jit(solution)/shard_map/ppermute | solution.py:33
  52.1 1.5 %collective-permute-done.13 = bf16[4,2,24,768]{3,2,0,1:T(8,128)(2,1)S(1)} collective-permute-done((bf16[4,2,24,768]{3,2,0,1:T(8,128)(2,1)S(1)}, bf16[4,2,24,768]{3,2,0,1:T(8,128)(2,1)S(1)}, u32[]{:S(2)}, u32[]{:S(2)}) %collective-permute-start.13) | collective-permute-done | bytes 294944 | tf_op jit(solution)/shard_map/ppermute | solution.py:33
  53.8 0.1 fusion.25
  54.0 0.4 fusion.3
  54.4 0.2 copy-done.5
  54.6 0.1 copy-done.6
  54.8 0.1 copy-done.7
  54.9 0.1 copy-done.8
  55.2 2.8 %collective-permute-done.14.other_ref = bf16[384,1536]{1,0:T(8,128)(2,1)S(1)} collective-permute-done((bf16[384,1536]{1,0:T(8,128)(2,1)S(1)}, bf16[384,1536]{1,0:T(8,128)(2,1)S(1)}, u32[]{:S(2)}, u32[]{:S(2)}) %collective-permute-start.14) | collective-permute-done | bytes 1179680 | tf_op jit(solution)/shard_map/ppermute | solution.py:231
  58.0 3.6 %shard_map.95 = bf16[384,1536]{1,0:T(8,128)(2,1)} custom-call(bf16[384,1536]{1,0:T(8,128)(2,1)S(1)} %pad_maximum_fusion.1.own_ref, bf16[384,1536]{1,0:T(8,128)(2,1)S(1)} %collective-permute-done.14.other_ref, bf16[384,768]{1,0:T(8,128)(2,1)S(1)} %copy-done.3, bf16[384,768]{1,0:T(8,128)(2,1)S(1)} %copy-done.4), custom_call_target="tpu_custom_call" | custom-call | flops 1811939328 | bytes 4194304 | tf_op jit(solution)/shard_map/pallas_call | solution.py:147
  61.6 4.7 %all-to-all-start = ((bf16[16,24,1536]{2,1,0:T(8,128)(2,1)}), bf16[16,24,1536]{2,1,0:T(8,128)(2,1)S(1)}, u32[]{:S(2)}, u32[]{:S(2)}) async-start(bf16[16,24,1536]{2,1,0:T(8,128)(2,1)} %bitcast.27), calls=%async_computation | async-start | bytes 2359296 | tf_op jit(solution)/shard_map/all_to_all | solution.py:251
  66.4 2.9 %fusion.29 = f32[1536,384]{0,1:T(8,128)S(1)} fusion(bf16[384,768]{1,0:T(8,128)(2,1)S(1)} %bitcast.73, bf16[768,1536]{1,0:T(8,128)(2,1)} %constant.112), kind=kOutput, calls=%fused_computation.75 | convolution fusion | flops 905969664 | bytes 5308416 | tf_op jit(solution)/shard_map/dot_general | solution.py:247
  69.3 1.1 fusion.1
  70.5 0.2 maximum_maximum_fusion.refs_1_
  70.7 4.3 %convolution_convert_fusion = bf16[384,1536]{1,0:T(8,128)(2,1)} fusion(bf16[384,1536]{1,0:T(8,128)(2,1)} %shard_map.95, bf16[1536,1536]{1,0:T(8,128)(2,1)S(1)} %bitcast.83), kind=kOutput, calls=%fused_computation.1 | convolution fusion | flops 1812529152 | bytes 7077888 | tf_op jit(solution)/shard_map/dot_general | solution.py:254
  75.0 18.4 %all-to-all-done = bf16[16,24,1536]{2,1,0:T(8,128)(2,1)S(1)} async-done(((bf16[16,24,1536]{2,1,0:T(8,128)(2,1)}), bf16[16,24,1536]{2,1,0:T(8,128)(2,1)S(1)}, u32[]{:S(2)}, u32[]{:S(2)}) %all-to-all-start) | async-done | bytes 1179680 | tf_op jit(solution)/shard_map/all_to_all | solution.py:251
  93.4 2.0 %shard_map.96 = f32[16,32]{1,0:T(8,128)S(1)} custom-call(bf16[384,1536]{1,0:T(8,128)(2,1)S(1)} %bitcast.64, bf16[768,1536]{1,0:T(8,128)(2,1)S(1)} %maximum_maximum_fusion.refs_1_), custom_call_target="tpu_custom_call" | custom-call | flops 905969664 | bytes 4194304 | tf_op jit(solution)/shard_map/pallas_call | solution.py:147
  95.4 0.6 pad_maximum_fusion.10
  96.1 5.7 %all-to-all-start.1 = ((f32[32,1,16]{2,1,0:T(1,128)}), f32[32,1,16]{2,1,0:T(1,128)S(1)}, u32[]{:S(2)}, u32[]{:S(2)}) async-start(f32[32,1,16]{2,1,0:T(1,128)} %bitcast.34), calls=%async_computation.1 | async-start | bytes 32768 | tf_op jit(solution)/shard_map/all_to_all | solution.py:265
  101.8 2.3 %pad_maximum_fusion = bf16[384,1536]{1,0:T(8,128)(2,1)} fusion(bf16[384,384]{1,0:T(8,128)(2,1)} %copy-done.7, bf16[384,384]{1,0:T(8,128)(2,1)} %copy-done.6, bf16[384,384]{1,0:T(8,128)(2,1)} %copy-done.8, bf16[384,384]{1,0:T(8,128)(2,1)} %copy-done.5), kind=kLoop, calls=%fused_computation.13 | loop fusion | flops 4718592 | bytes 2359296 | tf_op jit(solution)/shard_map/concatenate | solution.py:223
  104.2 4.8 %all-to-all-done.1 = f32[32,1,16]{2,1,0:T(1,128)S(1)} async-done(((f32[32,1,16]{2,1,0:T(1,128)}), f32[32,1,16]{2,1,0:T(1,128)S(1)}, u32[]{:S(2)}, u32[]{:S(2)}) %all-to-all-start.1) | async-done | bytes 2080 | tf_op jit(solution)/shard_map/all_to_all | solution.py:265
  109.0 0.6 reduce_sum.9
  (63 shorter events, 1.9 us)
Async XLA Ops:
  0.6 1.3 %copy-start = (bf16[1,384,1536]{2,1,0:T(8,128)(2,1)S(1)}, bf16[1,384,1536]{2,1,0:T(8,128)(2,1)}, u32[]{:S(2)}) copy-start(bf16[1,384,1536]{2,1,0:T(8,128)(2,1)} %param.7) | copy-start | bytes 3538948
  1.9 1.3 %copy-start.2 = (bf16[1,384,1536]{2,1,0:T(8,128)(2,1)S(1)}, bf16[1,384,1536]{2,1,0:T(8,128)(2,1)}, u32[]{:S(2)}) copy-start(bf16[1,384,1536]{2,1,0:T(8,128)(2,1)} %param.8) | copy-start | bytes 3538948
  3.9 10.0 %collective-permute-start = (bf16[4,2,24,768]{3,2,0,1:T(8,128)(2,1)S(1)}, bf16[4,2,24,768]{3,2,0,1:T(8,128)(2,1)S(1)}, u32[]{:S(2)}, u32[]{:S(2)}) collective-permute-start(bf16[4,2,24,768]{3,2,0,1:T(8,128)(2,1)S(1)} %copy.33), channel_id=1, source_target_pairs={{0,2},{2,0},{4,6},{6,4},{8,10},{10,8},{12,14},{14,12},{16,18},{18,... | collective-permute-start | bytes 884744 | tf_op jit(solution)/shard_map/ppermute | solution.py:33
  6.9 8.9 %collective-permute-start.2 = (bf16[4,2,24,768]{3,2,0,1:T(8,128)(2,1)S(1)}, bf16[4,2,24,768]{3,2,0,1:T(8,128)(2,1)S(1)}, u32[]{:S(2)}, u32[]{:S(2)}) collective-permute-start(bf16[4,2,24,768]{3,2,0,1:T(8,128)(2,1)S(1)} %copy.35), channel_id=1, source_target_pairs={{0,4},{2,6},{4,0},{6,2},{8,12},{10,14},{12,8},{14,10},{16,20},{18,... | collective-permute-start | bytes 884744 | tf_op jit(solution)/shard_map/ppermute | solution.py:33
  14.0 5.2 %collective-permute-start.1 = (bf16[4,24,768]{2,1,0:T(8,128)(2,1)S(1)}, bf16[4,24,768]{2,1,0:T(8,128)(2,1)S(1)}, u32[]{:S(2)}, u32[]{:S(2)}) collective-permute-start(bf16[4,24,768]{2,1,0:T(8,128)(2,1)S(1)} %fusion.6), channel_id=1, source_target_pairs={{0,4},{2,6},{4,0},{6,2},{8,12},{10,14},{12,8},{14,10},{16,20},{18,... | collective-permute-start | bytes 442376 | tf_op jit(solution)/shard_map/ppermute | solution.py:33
  15.9 5.2 %collective-permute-start.3 = (bf16[4,24,768]{2,1,0:T(8,128)(2,1)S(1)}, bf16[4,24,768]{2,1,0:T(8,128)(2,1)S(1)}, u32[]{:S(2)}, u32[]{:S(2)}) collective-permute-start(bf16[4,24,768]{2,1,0:T(8,128)(2,1)S(1)} %fusion.7), channel_id=1, source_target_pairs={{0,2},{2,0},{4,6},{6,4},{8,10},{10,8},{12,14},{14,12},{16,18},{18,... | collective-permute-start | bytes 442376 | tf_op jit(solution)/shard_map/ppermute | solution.py:33
  21.2 6.6 %collective-permute-start.6 = (bf16[24,1536]{1,0:T(8,128)(2,1)S(1)}, bf16[24,1536]{1,0:T(8,128)(2,1)S(1)}, u32[]{:S(2)}, u32[]{:S(2)}) collective-permute-start(bf16[24,1536]{1,0:T(8,128)(2,1)S(1)} %get-tuple-element.27), channel_id=1, source_target_pairs={{0,24},{2,26},{4,28},{6,30},{8,16},{10,18},{12,20},{14,22},{16,8},... | collective-permute-start | bytes 221192 | tf_op jit(solution)/shard_map/ppermute | solution.py:33
  24.8 5.3 %collective-permute-start.5 = (bf16[24,1536]{1,0:T(8,128)(2,1)S(1)}, bf16[24,1536]{1,0:T(8,128)(2,1)S(1)}, u32[]{:S(2)}, u32[]{:S(2)}) collective-permute-start(bf16[24,1536]{1,0:T(8,128)(2,1)S(1)} %get-tuple-element.26), channel_id=1, source_target_pairs={{0,16},{2,18},{4,20},{6,22},{8,24},{10,26},{12,28},{14,30},{16,0},... | collective-permute-start | bytes 221192 | tf_op jit(solution)/shard_map/ppermute | solution.py:33
  24.8 5.3 %collective-permute-start.4 = (bf16[24,1536]{1,0:T(8,128)(2,1)S(1)}, bf16[24,1536]{1,0:T(8,128)(2,1)S(1)}, u32[]{:S(2)}, u32[]{:S(2)}) collective-permute-start(bf16[24,1536]{1,0:T(8,128)(2,1)S(1)} %get-tuple-element.25), channel_id=1, source_target_pairs={{0,8},{2,10},{4,12},{6,14},{8,0},{10,2},{12,4},{14,6},{16,24},{18,... | collective-permute-start | bytes 221192 | tf_op jit(solution)/shard_map/ppermute | solution.py:33
  30.5 6.2 %collective-permute-start.9 = (bf16[24,1536]{1,0:T(8,128)(2,1)S(1)}, bf16[24,1536]{1,0:T(8,128)(2,1)S(1)}, u32[]{:S(2)}, u32[]{:S(2)}) collective-permute-start(bf16[24,1536]{1,0:T(8,128)(2,1)S(1)} %convert_element_type.103), channel_id=1, source_target_pairs={{0,24},{2,26},{4,28},{6,30},{8,16},{10,18},{12,20},{14,22},{16,8},... | collective-permute-start | bytes 221192 | tf_op jit(solution)/shard_map/ppermute | solution.py:33
  32.4 6.0 %collective-permute-start.8 = (bf16[24,1536]{1,0:T(8,128)(2,1)S(1)}, bf16[24,1536]{1,0:T(8,128)(2,1)S(1)}, u32[]{:S(2)}, u32[]{:S(2)}) collective-permute-start(bf16[24,1536]{1,0:T(8,128)(2,1)S(1)} %convert_element_type.103), channel_id=1, source_target_pairs={{0,16},{2,18},{4,20},{6,22},{8,24},{10,26},{12,28},{14,30},{16,0},... | collective-permute-start | bytes 221192 | tf_op jit(solution)/shard_map/ppermute | solution.py:33
  32.8 5.7 %collective-permute-start.7 = (bf16[24,1536]{1,0:T(8,128)(2,1)S(1)}, bf16[24,1536]{1,0:T(8,128)(2,1)S(1)}, u32[]{:S(2)}, u32[]{:S(2)}) collective-permute-start(bf16[24,1536]{1,0:T(8,128)(2,1)S(1)} %convert_element_type.103), channel_id=1, source_target_pairs={{0,8},{2,10},{4,12},{6,14},{8,0},{10,2},{12,4},{14,6},{16,24},{18,... | collective-permute-start | bytes 221192 | tf_op jit(solution)/shard_map/ppermute | solution.py:33
  38.5 1.4 %copy-start.1 = (bf16[1,384,1536]{2,1,0:T(8,128)(2,1)S(1)}, bf16[1,384,1536]{2,1,0:T(8,128)(2,1)}, u32[]{:S(2)}) copy-start(bf16[1,384,1536]{2,1,0:T(8,128)(2,1)} %param.7) | copy-start | bytes 3538948
  38.6 6.3 %collective-permute-start.10 = (bf16[4,24,768]{2,1,0:T(8,128)(2,1)S(1)}, bf16[4,24,768]{2,1,0:T(8,128)(2,1)S(1)}, u32[]{:S(2)}, u32[]{:S(2)}) collective-permute-start(bf16[4,24,768]{2,1,0:T(8,128)(2,1)S(1)} %get-tuple-element.31), channel_id=1, source_target_pairs={{0,4},{2,6},{4,0},{6,2},{8,12},{10,14},{12,8},{14,10},{16,20},{18,... | collective-permute-start | bytes 442376 | tf_op jit(solution)/shard_map/ppermute | solution.py:33
  40.2 6.5 %collective-permute-start.12 = (bf16[4,24,768]{2,1,0:T(8,128)(2,1)S(1)}, bf16[4,24,768]{2,1,0:T(8,128)(2,1)S(1)}, u32[]{:S(2)}, u32[]{:S(2)}) collective-permute-start(bf16[4,24,768]{2,1,0:T(8,128)(2,1)S(1)} %get-tuple-element.30), channel_id=1, source_target_pairs={{0,2},{2,0},{4,6},{6,4},{8,10},{10,8},{12,14},{14,12},{16,18},{18,... | collective-permute-start | bytes 442376 | tf_op jit(solution)/shard_map/ppermute | solution.py:33
  45.1 6.8 %collective-permute-start.11 = (bf16[4,2,24,768]{3,2,0,1:T(8,128)(2,1)S(1)}, bf16[4,2,24,768]{3,2,0,1:T(8,128)(2,1)S(1)}, u32[]{:S(2)}, u32[]{:S(2)}) collective-permute-start(bf16[4,2,24,768]{3,2,0,1:T(8,128)(2,1)S(1)} %reverse_select_fusion.3), channel_id=1, source_target_pairs={{0,2},{2,0},{4,6},{6,4},{8,10},{10,8},{12,14},{14,12},{16,18},{18,... | collective-permute-start | bytes 884744 | tf_op jit(solution)/shard_map/ppermute | solution.py:33
  46.8 6.8 %collective-permute-start.13 = (bf16[4,2,24,768]{3,2,0,1:T(8,128)(2,1)S(1)}, bf16[4,2,24,768]{3,2,0,1:T(8,128)(2,1)S(1)}, u32[]{:S(2)}, u32[]{:S(2)}) collective-permute-start(bf16[4,2,24,768]{3,2,0,1:T(8,128)(2,1)S(1)} %reverse_select_fusion.2), channel_id=1, source_target_pairs={{0,4},{2,6},{4,0},{6,2},{8,12},{10,14},{12,8},{14,10},{16,20},{18,... | collective-permute-start | bytes 884744 | tf_op jit(solution)/shard_map/ppermute | solution.py:33
  53.9 0.7 copy-start.5
  53.9 0.8 copy-start.6
  54.0 0.9 copy-start.7
  54.0 1.0 copy-start.8
  55.0 3.0 %copy-start.3 = (bf16[384,768]{1,0:T(8,128)(2,1)S(1)}, bf16[384,768]{1,0:T(8,128)(2,1)}, u32[]{:S(2)}) copy-start(bf16[384,768]{1,0:T(8,128)(2,1)} %constant.105.clone.re_ref) | copy-start | bytes 1769476
  55.0 3.0 %copy-start.4 = (bf16[384,768]{1,0:T(8,128)(2,1)S(1)}, bf16[384,768]{1,0:T(8,128)(2,1)}, u32[]{:S(2)}) copy-start(bf16[384,768]{1,0:T(8,128)(2,1)} %constant.106.clone.im_ref) | copy-start | bytes 1769476
  55.1 2.9 %collective-permute-start.14 = (bf16[384,1536]{1,0:T(8,128)(2,1)S(1)}, bf16[384,1536]{1,0:T(8,128)(2,1)S(1)}, u32[]{:S(2)}, u32[]{:S(2)}) collective-permute-start(bf16[384,1536]{1,0:T(8,128)(2,1)S(1)} %pad_maximum_fusion.1.own_ref), channel_id=1, source_target_pairs={{0,1},{1,0},{2,3},{3,2},{4,5},{5,4},{6,7},{7,6},{8,9},{9,8},{10,11... | collective-permute-start | bytes 3538952 | tf_op jit(solution)/shard_map/ppermute | solution.py:231
  61.6 4.7 %copy-start.9 = (bf16[2,16,24,768]{3,2,1,0:T(8,128)(2,1)S(1)}, bf16[2,16,24,768]{3,2,1,0:T(8,128)(2,1)}, u32[]{:S(2)}) copy-start(bf16[2,16,24,768]{3,2,1,0:T(8,128)(2,1)} %param.9) | copy-start | bytes 3538948
  61.6 31.8 %all-to-all-start = ((bf16[16,24,1536]{2,1,0:T(8,128)(2,1)}), bf16[16,24,1536]{2,1,0:T(8,128)(2,1)S(1)}, u32[]{:S(2)}, u32[]{:S(2)}) async-start(bf16[16,24,1536]{2,1,0:T(8,128)(2,1)} %bitcast.27), calls=%async_computation | async-start | bytes 2359296 | tf_op jit(solution)/shard_map/all_to_all | solution.py:251
  66.3 3.0 %copy-start.10 = (bf16[768,1536]{1,0:T(8,128)(2,1)S(1)}, bf16[768,1536]{1,0:T(8,128)(2,1)}, u32[]{:S(2)}) copy-start(bf16[768,1536]{1,0:T(8,128)(2,1)} %constant.113) | copy-start | bytes 7077892
  66.4 4.3 %slice-start = ((s8[4718592]{0:T(1024)(128)(4,1)}), s8[4194304]{0:T(1024)(128)(4,1)S(1)}, s32[]{:S(2)}) async-start(s8[4718592]{0:T(1024)(128)(4,1)} %bitcast.82), calls=%async_computation.2 | async-start | bytes 8388608
  69.3 1.4 %slice-start.1 = ((s8[4718592]{0:T(1024)(128)(4,1)}), s8[524288]{0:T(1024)(128)(4,1)S(1)}, s32[]{:S(2)}) async-start(s8[4718592]{0:T(1024)(128)(4,1)} %bitcast.82), calls=%async_computation.3 | async-start | bytes 1048576
  96.1 12.9 %all-to-all-start.1 = ((f32[32,1,16]{2,1,0:T(1,128)}), f32[32,1,16]{2,1,0:T(1,128)S(1)}, u32[]{:S(2)}, u32[]{:S(2)}) async-start(f32[32,1,16]{2,1,0:T(1,128)} %bitcast.34), calls=%async_computation.1 | async-start | bytes 32768 | tf_op jit(solution)/shard_map/all_to_all | solution.py:265

commit v3 on v2

--- a/solution.py
+++ b/solution.py
@@ -91,50 +91,44 @@
                     keep_b[out, into] = jnp.where(high, second, first)
 
 
-def columns_kernel(own_ref, other_ref, re_ref, im_ref, out_ref):
-    half = own_ref.shape[1] // 2
-    rows = own_ref.shape[0]
-
-    def times(table, values):
-        return jnp.dot(table, values, preferred_element_type=f32)
-
-    def both(table, part):
-        cols = pl.ds(part * half, half)
-        return times(table[:, :rows], own_ref[:, cols]) + times(table[:, rows:], other_ref[:, cols])
-
-    c_re, c_im = re_ref[...], im_ref[...]
-    out_ref[:, :half] = (both(c_re, 0) - both(c_im, 1)).astype(bf16)
-    out_ref[:, half:] = (both(c_im, 0) + both(c_re, 1)).astype(bf16)
-
-
-def coupling_kernel(mode_rows, fields_ref, targets_ref, out_ref):
-    product = lax.dot_general(
-        fields_ref[...], targets_ref[...], (((1,), (1,)), ((), ())), preferred_element_type=f32
-    )
-    left, right = product.shape
-    row = lax.broadcasted_iota(jnp.int32, (left, right), 0) % mode_rows
-    col = lax.broadcasted_iota(jnp.int32, (left, right), 1) % mode_rows
-    product = jnp.where(row == col, product, 0.0)
-
-    def groups(size):
-        member = lax.broadcasted_iota(jnp.int32, (size // mode_rows, size), 1) // mode_rows
-        group = lax.broadcasted_iota(jnp.int32, (size // mode_rows, size), 0)
+def coupling_kernel(mode_rows, starts, fields_ref, *rest):
+    targets, out_ref = rest[:-1], rest[-1]
+    sources, _, pixel_rows, grid_size = fields_ref.shape
+    count = lax.axis_size("modes")
+    half = lax.axis_index("modes") // (count // 2)
+    left = sources * pixel_rows
+    field_re = fields_ref[:, 0].reshape(left, grid_size)
+    field_im = fields_ref[:, 1].reshape(left, grid_size)
+    contract = (((1,), (1,)), ((), ()))
+
+    def groups(size, each):
+        member = lax.broadcasted_iota(jnp.int32, (size // each, size), 1) // each
+        group = lax.broadcasted_iota(jnp.int32, (size // each, size), 0)
         return jnp.where(member == group, 1.0, 0.0).astype(f32)
 
-    narrow = lax.dot_general(
-        groups(left),
-        product,
-        (((1,), (0,)), ((), ())),
-        precision=lax.Precision.HIGHEST,
-        preferred_element_type=f32,
-    )
-    out_ref[...] = lax.dot_general(
-        narrow,
-        groups(right),
-        (((1,), (1,)), ((), ())),
-        precision=lax.Precision.HIGHEST,
-        preferred_element_type=f32,
-    )
+    def times(one, two):
+        return lax.dot_general(one, two, contract, preferred_element_type=f32)
+
+    def exactly(one, two, dims):
+        return lax.dot_general(one, two, (dims, ((), ())), precision=lax.Precision.HIGHEST, preferred_element_type=f32)
+
+    modes = out_ref.shape[1] // 2
+    total_re = total_im = jnp.zeros((sources, modes), f32)
+    for which, (start, target) in enumerate(zip(starts, targets)):
+        right = target.shape[0]
+        each = right // modes
+        in_half = half if which == 0 else 1 - half
+        target_re, target_im = target[:, :grid_size], target[:, grid_size:]
+        row = lax.broadcasted_iota(jnp.int32, (left, right), 0) % pixel_rows
+        col = lax.broadcasted_iota(jnp.int32, (left, right), 1) % each
+        same = row == col + (in_half * mode_rows + start)
+        real = jnp.where(same, times(field_re, target_re) + times(field_im, target_im), 0.0)
+        imag = jnp.where(same, times(field_im, target_re) - times(field_re, target_im), 0.0)
+        rows_of, cols_of = groups(left, pixel_rows), groups(right, each)
+        total_re += exactly(exactly(rows_of, real, ((1,), (0,))), cols_of, ((1,), (1,)))
+        total_im += exactly(exactly(rows_of, imag, ((1,), (0,))), cols_of, ((1,), (1,)))
+    out_ref[:, :modes] = total_re
+    out_ref[:, modes:] = total_im
 
 
 def kernel_call(kernel, shape, dtype, flops, operands):
@@ -163,6 +157,17 @@
     digits = stages(count)
     sizes = [size for _, size in reversed(digits)]
     half = grid_size // 2
+
+    c_re, c_im = propagator(grid_size)
+    back_table = jnp.asarray(np.block([[c_re, -c_im], [c_im, c_re]]), bf16)
+
+    def back(part):
+        flat = jnp.concatenate([part[0], part[1]], -1).reshape(-1, double_width)
+        return jnp.dot(flat, back_table, preferred_element_type=f32).astype(bf16)
+
+    cut = block_rows // 3
+    early = exchange(targets[:, :, :cut], count // 2, count)
+    seen = back(targets)
 
     me = lax.axis_index("modes")
     owns = [me // stride % size for stride, size in digits]
@@ -196,6 +201,8 @@
             else:
                 send, keep = split_digit(partial, owns[d], size, axes[d])
             got = [exchange(v, (e + 1) * stride, count) for e, v in enumerate(send)]
+            if at == 0 and part == 0:
+                got, seen = lax.optimization_barrier((got, seen))
             partial = reduce_digit(keep, got)
             axes = [a - (a > axes[d]) for a in axes]
         kept.append(partial)
@@ -209,6 +216,8 @@
     block = block.reshape(block_rows, double_width)
 
     block = gather_digit(block, owns[last], stride, size, 0, count)
+    block, later = lax.optimization_barrier((block, targets[:, :, cut:]))
+    later = exchange(later, count // 2, count)
     planes = []
     for part, order in enumerate(orders):
         piece = block[..., part * grid_size : (part + 1) * grid_size]
@@ -226,42 +235,41 @@
     fore_re, fore_im = fore[:, :grid_size], fore[:, grid_size:]
     plane_re, plane_im = plane_re.astype(f32), plane_im.astype(f32)
     shaped = jnp.concatenate(
-        [fore_re * plane_re - fore_im * plane_im, fore_re * plane_im + fore_im * plane_re], -1
+        [fore_re * plane_re - fore_im * plane_im, fore_re * plane_im + fore_im * plane_re], 0
     ).astype(bf16)
     other = lax.ppermute(shaped, "rows", [(0, 1), (1, 0)])
 
-    c_re, c_im = propagator(grid_size)
-    own_re = jnp.asarray(c_re[:local_rows], bf16)
-    own_im = jnp.asarray(c_im[:local_rows], bf16)
-    columns = kernel_call(
-        columns_kernel,
-        (local_rows, double_width),
-        bf16,
-        2 * local_rows * double_width * double_width,
-        (shaped, other, own_re, own_im),
-    )
-
-    back_table = jnp.asarray(np.block([[c_re, -c_im], [c_im, c_re]]), bf16)
+    order = np.arange(local_rows).reshape(2, count // 2, block_rows).transpose(1, 0, 2).reshape(count // 2, -1)
+
+    def table(cols):
+        real, imag = c_re[:local_rows, cols], c_im[:local_rows, cols]
+        rows = np.stack([np.concatenate([real, -imag], 1)[order], np.concatenate([imag, real], 1)[order]], 1)
+        return jnp.asarray(rows.reshape(2 * local_rows, -1), bf16)
+
+    columns = jnp.dot(table(slice(0, local_rows)), shaped, preferred_element_type=f32)
+    columns, other = lax.optimization_barrier((columns, other))
+    columns = columns + jnp.dot(table(slice(local_rows, None)), other, preferred_element_type=f32)
+    columns = columns.astype(bf16).reshape(count // 2, 2, 2 * block_rows, grid_size)
+
+    together = [list(range(count // 2)), list(range(count // 2, count))]
+    pixels = lax.all_to_all(columns, "modes", 0, 0, tiled=True, axis_index_groups=together)
+
+    columns = columns.reshape(count // 2, 2, 2, block_rows, grid_size)
+    columns = columns.transpose(2, 0, 3, 1, 4).reshape(local_rows, double_width)
     rows_table = jnp.asarray(np.block([[c_re, c_im], [-c_im, c_re]]), bf16)
-    flat = jnp.concatenate([targets[0], targets[1]], -1).reshape(-1, double_width)
-    seen = jnp.dot(flat, back_table, preferred_element_type=f32).astype(bf16)
-    turned = jnp.concatenate([-seen[:, grid_size:], seen[:, :grid_size]], -1)
-    target_pair = jnp.concatenate([seen, turned], 0)
-
-    pixels = lax.all_to_all(
-        columns.reshape(count, block_rows, double_width), "modes", 0, 0, tiled=True
-    )
     output_fields = jnp.dot(columns, rows_table, preferred_element_type=f32).astype(bf16)
     pixels, output_fields = lax.optimization_barrier((pixels, output_fields))
 
     term = kernel_call(
-        lambda *refs: coupling_kernel(block_rows, *refs),
-        (mode_total, 2 * mode_total),
+        lambda *refs: coupling_kernel(block_rows, (0, 0, cut), *refs),
+        (mode_total // 2, 2 * mode_total),
         f32,
-        4 * local_rows * local_rows * double_width,
-        (pixels.reshape(local_rows, double_width), target_pair),
+        8 * local_rows * local_rows * double_width,
+        (pixels, seen, back(early), back(later)),
     )
-    term = jnp.concatenate([term[:, :mode_total], term[:, mode_total:]], 0)
+    term = term.reshape(mode_total // 2, 2, 1, mode_total).transpose(1, 2, 0, 3)
+    in_half = (jnp.arange(2) == me // (count // 2)).reshape(1, 2, 1, 1)
+    term = jnp.where(in_half, term, 0.0).reshape(2 * mode_total, mode_total)
     pieces = lax.all_to_all(term, ("modes", "rows"), 0, 0, tiled=True)
     coupling = jnp.sum(pieces, 0, keepdims=True)
     return (phase_plane, output_fields[None], coupling)

time: 110 us -> 147 us (1.34)
  local copies, waits for them, and re-layouts: 4.05 us -> 19.9 us
  matrix products: 8.24 us -> 19.5 us
  waiting for transfers between devices: 52.2 us -> 60.7 us
  other arithmetic: 5.51 us -> 12 us
  starting transfers between devices: 32.2 us -> 27.6 us
    ppermute x14 -> x16, waiting for transfers between devices: 26.2 us -> 55.8 us  [exchange(): lax.ppermute(values, 'modes', [(i, i ^ offset) for i in range(count)])]
    all_to_all x1, waiting for transfers between devices: 18.4 us -> 0.01 us  [local(): lax.all_to_all(columns, 'modes', 0, 0, tiled=True, axis_index_groups=toge...]
    dot_general x2 -> x9, matrix products: 3.97 us -> 16.5 us  [the longest x6 11.4 us: back(): return jnp.dot(flat, back_table, preferred_element_type=f32).astype(bf16)]
    slice x2 -> x4, local copies, waits for them, and re-layouts: 0.15 us -> 5.02 us  [the longest x2 3.3 us: back(): flat = jnp.concatenate([part[0], part[1]], -1).reshape(-1, double_width)]
    ppermute x1, waiting for transfers between devices: 2.83 us -> 0.01 us  [local(): other = lax.ppermute(shaped, 'rows', [(0, 1), (1, 0)])]
    unnamed x26 -> x39, local copies, waits for them, and re-layouts: 3.15 us -> 5.81 us
    all_to_all x1, starting transfers between devices: 5.74 us -> 3.26 us  [local(): pieces = lax.all_to_all(term, ('modes', 'rows'), 0, 0, tiled=True)]
    convert_element_type x3, local copies, waits for them, and re-layouts: 0.16 us -> 2.4 us  [local(): block = jnp.stack([over_re * scale, over_im * scale], 2).astype(bf16)]
  transfers between devices with their start and end apart: 17 -> 19, of which waited for: 13 -> 12; matrix products, arithmetic and copies ran while one was open for 11% -> 27% of each run, Pallas kernels for 0% -> 0%
where the time goes in v3:
time: 147 us
  waiting for transfers between devices  60.7 us (41%)
  starting transfers between devices  27.6 us (19%)
  local copies, waits for them, and re-layouts  19.9 us (14%)
  matrix products  19.5 us (13%)
  other arithmetic  12 us (8%)
  Pallas kernels  5.73 us (4%)
    ppermute x16, waiting for transfers between devices, exchange(): lax.ppermute(values, 'modes', [(i, i ^ offset) for i in range(count)])  55.8 us
    ppermute x16, starting transfers between devices, exchange(): lax.ppermute(values, 'modes', [(i, i ^ offset) for i in range(count)])  20.6 us
    dot_general x6, matrix products, back(): return jnp.dot(flat, back_table, preferred_element_type=f32).astype(bf16)  11.4 us
    unnamed x39, local copies, waits for them, and re-layouts  5.81 us
    pallas_call x2, Pallas kernels, kernel_call(): pl.pallas_call(kernel, out_shape=out_shape, in_specs=[place] * len(operan...  5.73 us
    all_to_all x1, waiting for transfers between devices, local(): pieces = lax.all_to_all(term, ('modes', 'rows'), 0, 0, tiled=True)  4.81 us
    all_to_all x1, starting transfers between devices, local(): lax.all_to_all(columns, 'modes', 0, 0, tiled=True, axis_index_groups=toge...  3.75 us
    slice x2, local copies, waits for them, and re-layouts, back(): flat = jnp.concatenate([part[0], part[1]], -1).reshape(-1, double_width)  3.3 us
  transfers between devices with their start and end apart: 19, of which 12 were waited for; matrix products, arithmetic and copies ran while one was open for 27% of the time, Pallas kernels for 0%

profile of v3, /device:TPU:0, one launch (start us, length us, event | category | flops | bytes accessed | tf_op | source)
XLA Modules:
  0.0 146.5 jit_solution(990117119153873245)
XLA Ops:
  0.6 1.3 copy-done
  1.9 1.3 copy-done.2
  4.6 2.9 %collective-permute-start = (bf16[4,2,24,768]{3,2,0,1:T(8,128)(2,1)}, bf16[4,2,24,768]{3,2,0,1:T(8,128)(2,1)}, u32[]{:S(2)}, u32[]{:S(2)}) collective-permute-start(bf16[4,2,24,768]{3,2,0,1:T(8,128)(2,1)} %copy.97), channel_id=1, source_target_pairs={{0,2},{2,0},{4,6},{6,4},{8,10},{10,8},{12,14},{14,12},{16,18},{18,... | collective-permute-start | bytes 884744 | tf_op jit(solution)/shard_map/ppermute | solution.py:33
  8.2 1.5 %collective-permute-start.2 = (bf16[4,2,24,768]{3,2,0,1:T(8,128)(2,1)}, bf16[4,2,24,768]{3,2,0,1:T(8,128)(2,1)}, u32[]{:S(2)}, u32[]{:S(2)}) collective-permute-start(bf16[4,2,24,768]{3,2,0,1:T(8,128)(2,1)} %copy.101), channel_id=1, source_target_pairs={{0,4},{2,6},{4,0},{6,2},{8,12},{10,14},{12,8},{14,10},{16,20},{18,... | collective-permute-start | bytes 884744 | tf_op jit(solution)/shard_map/ppermute | solution.py:33
  9.7 2.1 %fusion.28 = (bf16[1,16,24,768]{3,2,1,0:T(8,128)(2,1)}, bf16[1,16,24,768]{3,2,1,0:T(8,128)(2,1)S(1)}) fusion(bf16[2,16,24,768]{3,2,1,0:T(8,128)(2,1)} %param.9), kind=kLoop, calls=%fused_computation.79 | loop fusion | bytes 2359296 | tf_op jit(solution)/shard_map/slice | solution.py:165
  11.9 2.5 %fusion.36 = f32[1536,384]{0,1:T(8,128)} fusion(bf16[384,768]{1,0:T(8,128)(2,1)S(1)} %bitcast.107, bf16[768,1536]{1,0:T(8,128)(2,1)S(1)} %copy-done.3), kind=kOutput, calls=%fused_computation.87 | convolution fusion | flops 905969664 | bytes 5308416 | tf_op jit(solution)/shard_map/dot_general | solution.py:166
  14.4 3.6 %fusion.1.refs_1_ = bf16[384,1536]{1,0:T(8,128)(2,1)S(1)} fusion(f32[1536,384]{0,1:T(8,128)} %fusion.36, bf16[384,768]{1,0:T(8,128)(2,1)} %bitcast.106, bf16[768,1536]{1,0:T(8,128)(2,1)} %constant.123), kind=kOutput, calls=%fused_computation.4 | convolution fusion | flops 907149312 | bytes 6488064 | tf_op jit(solution)/shard_map/dot_general | solution.py:166
  18.0 1.0 copy_add_fusion.1
  19.7 1.0 copy_add_fusion
  20.8 3.5 %collective-permute-done.1 = bf16[4,24,768]{2,1,0:T(8,128)(2,1)S(1)} collective-permute-done((bf16[4,24,768]{2,1,0:T(8,128)(2,1)S(1)}, bf16[4,24,768]{2,1,0:T(8,128)(2,1)S(1)}, u32[]{:S(2)}, u32[]{:S(2)}) %collective-permute-start.1) | collective-permute-done | bytes 147488 | tf_op jit(solution)/shard_map/ppermute | solution.py:33
  24.3 1.6 %collective-permute-done.3 = bf16[4,24,768]{2,1,0:T(8,128)(2,1)S(1)} collective-permute-done((bf16[4,24,768]{2,1,0:T(8,128)(2,1)S(1)}, bf16[4,24,768]{2,1,0:T(8,128)(2,1)S(1)}, u32[]{:S(2)}, u32[]{:S(2)}) %collective-permute-start.3) | collective-permute-done | bytes 147488 | tf_op jit(solution)/shard_map/ppermute | solution.py:33
  26.0 3.7 %collective-permute-start.6 = (bf16[24,1536]{1,0:T(8,128)(2,1)S(1)}, bf16[24,1536]{1,0:T(8,128)(2,1)S(1)}, u32[]{:S(2)}, u32[]{:S(2)}) collective-permute-start(bf16[24,1536]{1,0:T(8,128)(2,1)S(1)} %get-tuple-element.39), channel_id=1, source_target_pairs={{0,24},{2,26},{4,28},{6,30},{8,16},{10,18},{12,20},{14,22},{16,8},... | collective-permute-start | bytes 221192 | tf_op jit(solution)/shard_map/ppermute | solution.py:33
  30.5 1.9 %collective-permute-done.6 = bf16[24,1536]{1,0:T(8,128)(2,1)S(1)} collective-permute-done((bf16[24,1536]{1,0:T(8,128)(2,1)S(1)}, bf16[24,1536]{1,0:T(8,128)(2,1)S(1)}, u32[]{:S(2)}, u32[]{:S(2)}) %collective-permute-start.6) | collective-permute-done | bytes 73760 | tf_op jit(solution)/shard_map/ppermute | solution.py:33
  32.3 2.6 %collective-permute-done.5 = bf16[24,1536]{1,0:T(8,128)(2,1)S(1)} collective-permute-done((bf16[24,1536]{1,0:T(8,128)(2,1)S(1)}, bf16[24,1536]{1,0:T(8,128)(2,1)S(1)}, u32[]{:S(2)}, u32[]{:S(2)}) %collective-permute-start.5) | collective-permute-done | bytes 73760 | tf_op jit(solution)/shard_map/ppermute | solution.py:33
  36.0 2.0 %collective-permute-start.9 = (bf16[24,1536]{1,0:T(8,128)(2,1)}, bf16[24,1536]{1,0:T(8,128)(2,1)}, u32[]{:S(2)}, u32[]{:S(2)}) collective-permute-start(bf16[24,1536]{1,0:T(8,128)(2,1)} %convert_element_type.113), channel_id=1, source_target_pairs={{0,24},{2,26},{4,28},{6,30},{8,16},{10,18},{12,20},{14,22},{16,8},... | collective-permute-start | bytes 221192 | tf_op jit(solution)/shard_map/ppermute | solution.py:33
  38.2 2.2 %collective-permute-start.7 = (bf16[24,1536]{1,0:T(8,128)(2,1)}, bf16[24,1536]{1,0:T(8,128)(2,1)}, u32[]{:S(2)}, u32[]{:S(2)}) collective-permute-start(bf16[24,1536]{1,0:T(8,128)(2,1)} %convert_element_type.113), channel_id=1, source_target_pairs={{0,8},{2,10},{4,12},{6,14},{8,0},{10,2},{12,4},{14,6},{16,24},{18,... | collective-permute-start | bytes 221192 | tf_op jit(solution)/shard_map/ppermute | solution.py:33
  40.4 0.9 slice.58
  41.3 1.7 %convert_element_type.112 = bf16[1,24,1536]{2,1,0:T(8,128)(2,1)} reshape(bf16[24,2,2,384]{3,2,1,0:T(2,128)(2,1)} %copy-done.12) | data formatting | bytes 147456 | tf_op jit(solution)/shard_map/convert_element_type | solution.py:215
  43.0 1.4 collective-permute-done.8
  44.4 1.0 pad_maximum_fusion.6
  45.5 0.8 slice_bitcast_fusion.5
  46.4 1.3 collective-permute-start.10
  47.7 1.7 %bitcast_convert_fusion = f32[384,1536]{1,0:T(8,128)} fusion(bf16[1,384,1536]{2,1,0:T(8,128)(2,1)S(1)} %copy-done.1), kind=kLoop, calls=%fused_computation.76 | loop fusion | flops 589824 | bytes 3538944 | tf_op jit(solution)/shard_map/convert_element_type | solution.py:234
  49.9 1.9 %collective-permute-done.10 = bf16[4,24,768]{2,1,0:T(8,128)(2,1)} collective-permute-done((bf16[4,24,768]{2,1,0:T(8,128)(2,1)}, bf16[4,24,768]{2,1,0:T(8,128)(2,1)}, u32[]{:S(2)}, u32[]{:S(2)}) %collective-permute-start.10) | collective-permute-done | bytes 147488 | tf_op jit(solution)/shard_map/ppermute | solution.py:33
  51.8 1.0 pad_maximum_fusion.8
  53.5 1.6 %collective-permute-done.12 = bf16[4,24,768]{2,1,0:T(8,128)(2,1)S(1)} collective-permute-done((bf16[4,24,768]{2,1,0:T(8,128)(2,1)}, bf16[4,24,768]{2,1,0:T(8,128)(2,1)S(1)}, u32[]{:S(2)}, u32[]{:S(2)}) %collective-permute-start.12) | collective-permute-done | bytes 147488 | tf_op jit(solution)/shard_map/ppermute | solution.py:33
  55.3 1.2 collective-permute-start.13
  56.6 3.1 %collective-permute-done.11 = bf16[4,2,24,768]{3,2,0,1:T(8,128)(2,1)S(1)} collective-permute-done((bf16[4,2,24,768]{3,2,0,1:T(8,128)(2,1)S(1)}, bf16[4,2,24,768]{3,2,0,1:T(8,128)(2,1)S(1)}, u32[]{:S(2)}, u32[]{:S(2)}) %collective-permute-start.11) | collective-permute-done | bytes 294944 | tf_op jit(solution)/shard_map/ppermute | solution.py:33
  59.9 2.2 %collective-permute-done.13 = bf16[4,2,24,768]{3,2,0,1:T(8,128)(2,1)S(1)} collective-permute-done((bf16[4,2,24,768]{3,2,0,1:T(8,128)(2,1)S(1)}, bf16[4,2,24,768]{3,2,0,1:T(8,128)(2,1)S(1)}, u32[]{:S(2)}, u32[]{:S(2)}) %collective-permute-start.13) | collective-permute-done | bytes 294944 | tf_op jit(solution)/shard_map/ppermute | solution.py:33
  62.5 1.9 %copy-done.6 = f32[384,1536]{1,0:T(8,128)S(1)} copy-done((f32[384,1536]{1,0:T(8,128)S(1)}, f32[384,1536]{1,0:T(8,128)}, u32[]{:S(2)}) %copy-start.6) | copy-done | bytes 2359320
  64.8 1.1 pad_maximum_fusion.1
  66.7 1.2 collective-permute-start.15
  68.0 1.8 %collective-permute-start.16 = (bf16[2,16,16,768]{3,2,1,0:T(8,128)(2,1)}, bf16[2,16,16,768]{3,2,1,0:T(8,128)(2,1)}, u32[]{:S(2)}, u32[]{:S(2)}) collective-permute-start(bf16[2,16,16,768]{3,2,1,0:T(8,128)(2,1)} %slice.58), channel_id=1, source_target_pairs={{0,16},{2,18},{4,20},{6,22},{8,24},{10,26},{12,28},{14,30},{16,0},... | collective-permute-start | bytes 2359304 | tf_op jit(solution)/shard_map/ppermute | solution.py:33
  69.8 1.9 %fusion.33 = f32[768,768]{1,0:T(8,128)S(1)} fusion(bf16[384,768]{1,0:T(8,128)(2,1)S(1)} %get-tuple-element.28, bf16[768,384]{1,0:T(8,128)(2,1)} %constant.124), kind=kOutput, calls=%fused_computation.84 | convolution fusion | flops 452984832 | bytes 3538944 | tf_op jit(solution)/shard_map/dot_general | solution.py:249
  72.9 2.4 %fusion.34 = f32[768,768]{0,1:T(8,128)S(1)} fusion(bf16[768,768]{1,0:T(8,128)(2,1)S(1)} %copy-done.16, bf16[768,768]{1,0:T(8,128)(2,1)} %collective-permute-done.14), kind=kOutput, calls=%fused_computation.85 | convolution fusion | flops 905969664 | bytes 4718592 | tf_op jit(solution)/shard_map/dot_general | solution.py:251
  75.7 1.5 copy.110
  77.2 3.7 %all-to-all-start = ((bf16[8,2,48,768]{3,2,1,0:T(8,128)(2,1)}), bf16[8,2,48,768]{3,2,1,0:T(8,128)(2,1)S(1)}, u32[]{:S(2)}, u32[]{:S(2)}) async-start(bf16[8,2,48,768]{3,2,1,0:T(8,128)(2,1)} %bitcast.31), calls=%async_computation | async-start | bytes 2359296 | tf_op jit(solution)/shard_map/all_to_all | solution.py:255
  81.0 24.0 %collective-permute-done.15 = bf16[2,16,8,768]{3,2,1,0:T(8,128)(2,1)S(1)} collective-permute-done((bf16[2,16,8,768]{3,2,1,0:T(8,128)(2,1)}, bf16[2,16,8,768]{3,2,1,0:T(8,128)(2,1)S(1)}, u32[]{:S(2)}, u32[]{:S(2)}) %collective-permute-start.15) | collective-permute-done | bytes 393248 | tf_op jit(solution)/shard_map/ppermute | solution.py:33
  105.7 2.1 %fusion.9 = f32[1536,128]{0,1:T(8,128)S(1)} fusion(bf16[768,1536]{1,0:T(8,128)(2,1)} %constant.123, bf16[2,16,8,768]{3,2,1,0:T(8,128)(2,1)S(1)} %collective-permute-done.15), kind=kOutput, calls=%fused_computation.49 | convolution fusion | flops 301989888 | bytes 3342336 | tf_op jit(solution)/shard_map/dot_general | solution.py:166
  107.9 1.6 %fusion.4.refs_2_ = bf16[128,1536]{1,0:T(8,128)(2,1)S(1)} fusion(f32[1536,128]{0,1:T(8,128)S(1)} %fusion.9, bf16[768,1536]{1,0:T(8,128)(2,1)S(1)} %copy-done.4, bf16[2,16,8,768]{3,2,1,0:T(8,128)(2,1)} %copy-done.15), kind=kOutput, calls=%fused_computation.10 | convolution fusion | flops 302383104 | bytes 3735552 | tf_op jit(solution)/shard_map/dot_general | solution.py:166
  109.5 12.1 %collective-permute-done.16 = bf16[2,16,16,768]{3,2,1,0:T(8,128)(2,1)} collective-permute-done((bf16[2,16,16,768]{3,2,1,0:T(8,128)(2,1)}, bf16[2,16,16,768]{3,2,1,0:T(8,128)(2,1)}, u32[]{:S(2)}, u32[]{:S(2)}) %collective-permute-start.16) | collective-permute-done | bytes 786464 | tf_op jit(solution)/shard_map/ppermute | solution.py:33
  121.5 1.2 fusion.29
  124.3 2.2 %copy.112 = bf16[2,8,24,2,768]{4,3,2,1,0:T(2,128)(2,1)S(1)} copy(bf16[2,8,24,2,768]{4,2,0,3,1:T(8,128)(2,1)} %bitcast.33) | data formatting | bytes 2359296 | tf_op jit(solution)/shard_map/transpose | solution.py:258
  126.7 3.0 %convolution_convert_fusion = bf16[384,1536]{1,0:T(8,128)(2,1)} fusion(bf16[384,1536]{1,0:T(8,128)(2,1)S(1)} %bitcast.105, bf16[1536,1536]{1,0:T(8,128)(2,1)S(1)} %bitcast.115), kind=kOutput, calls=%fused_computation.1 | convolution fusion | flops 1812529152 | bytes 7077888 | tf_op jit(solution)/shard_map/dot_general | solution.py:260
  129.7 5.1 %shard_map.95 = f32[8,32]{1,0:T(8,128)S(1)} custom-call(bf16[8,2,48,768]{3,2,1,0:T(8,128)(2,1)S(1)} %all-to-all-done.refs_0_, bf16[384,1536]{1,0:T(8,128)(2,1)S(1)} %fusion.1.refs_1_, bf16[128,1536]{1,0:T(8,128)(2,1)S(1)} %fusion.4.refs_2_, bf16[256,1536]{1,0:T(8,128)(2,1)S(1)} %fusion.2.refs_3_), custom_call_target="tpu_custom_call" | custom-call | flops 1811939328 | bytes 4194304 | tf_op jit(solution)/shard_map/pallas_call | solution.py:141
  135.6 3.3 %all-to-all-start.1 = ((f32[32,1,16]{2,1,0:T(1,128)}), f32[32,1,16]{2,1,0:T(1,128)S(1)}, u32[]{:S(2)}, u32[]{:S(2)}) async-start(f32[32,1,16]{2,1,0:T(1,128)} %bitcast.43), calls=%async_computation.1 | async-start | bytes 32768 | tf_op jit(solution)/shard_map/all_to_all | solution.py:273
  138.8 2.3 %pad_maximum_fusion = bf16[384,1536]{1,0:T(8,128)(2,1)} fusion(bf16[384,384]{1,0:T(8,128)(2,1)} %copy-done.10, bf16[384,384]{1,0:T(8,128)(2,1)} %copy-done.9, bf16[384,384]{1,0:T(8,128)(2,1)} %copy-done.11, bf16[384,384]{1,0:T(8,128)(2,1)} %copy-done.8), kind=kLoop, calls=%fused_computation.19 | loop fusion | flops 4718592 | bytes 2359296 | tf_op jit(solution)/shard_map/concatenate | solution.py:232
  141.2 4.8 %all-to-all-done.1 = f32[32,1,16]{2,1,0:T(1,128)S(1)} async-done(((f32[32,1,16]{2,1,0:T(1,128)}), f32[32,1,16]{2,1,0:T(1,128)S(1)}, u32[]{:S(2)}, u32[]{:S(2)}) %all-to-all-start.1) | async-done | bytes 2080 | tf_op jit(solution)/shard_map/all_to_all | solution.py:273
  (95 shorter events, 13.8 us)
Async XLA Ops:
  0.6 1.3 copy-start
  1.9 1.3 copy-start.2
  4.6 7.3 %copy-start.3 = (bf16[768,1536]{1,0:T(8,128)(2,1)S(1)}, bf16[768,1536]{1,0:T(8,128)(2,1)}, u32[]{:S(2)}) copy-start(bf16[768,1536]{1,0:T(8,128)(2,1)} %constant.122) | copy-start | bytes 7077892
  4.6 13.5 %collective-permute-start = (bf16[4,2,24,768]{3,2,0,1:T(8,128)(2,1)}, bf16[4,2,24,768]{3,2,0,1:T(8,128)(2,1)}, u32[]{:S(2)}, u32[]{:S(2)}) collective-permute-start(bf16[4,2,24,768]{3,2,0,1:T(8,128)(2,1)} %copy.97), channel_id=1, source_target_pairs={{0,2},{2,0},{4,6},{6,4},{8,10},{10,8},{12,14},{14,12},{16,18},{18,... | collective-permute-start | bytes 884744 | tf_op jit(solution)/shard_map/ppermute | solution.py:33
  8.2 11.4 %collective-permute-start.2 = (bf16[4,2,24,768]{3,2,0,1:T(8,128)(2,1)}, bf16[4,2,24,768]{3,2,0,1:T(8,128)(2,1)}, u32[]{:S(2)}, u32[]{:S(2)}) collective-permute-start(bf16[4,2,24,768]{3,2,0,1:T(8,128)(2,1)} %copy.101), channel_id=1, source_target_pairs={{0,4},{2,6},{4,0},{6,2},{8,12},{10,14},{12,8},{14,10},{16,20},{18,... | collective-permute-start | bytes 884744 | tf_op jit(solution)/shard_map/ppermute | solution.py:33
  19.1 5.2 %collective-permute-start.1 = (bf16[4,24,768]{2,1,0:T(8,128)(2,1)S(1)}, bf16[4,24,768]{2,1,0:T(8,128)(2,1)S(1)}, u32[]{:S(2)}, u32[]{:S(2)}) collective-permute-start(bf16[4,24,768]{2,1,0:T(8,128)(2,1)S(1)} %fusion.10), channel_id=1, source_target_pairs={{0,4},{2,6},{4,0},{6,2},{8,12},{10,14},{12,8},{14,10},{16,20},{18,... | collective-permute-start | bytes 442376 | tf_op jit(solution)/shard_map/ppermute | solution.py:33
  20.7 5.2 %collective-permute-start.3 = (bf16[4,24,768]{2,1,0:T(8,128)(2,1)S(1)}, bf16[4,24,768]{2,1,0:T(8,128)(2,1)S(1)}, u32[]{:S(2)}, u32[]{:S(2)}) collective-permute-start(bf16[4,24,768]{2,1,0:T(8,128)(2,1)S(1)} %fusion.11), channel_id=1, source_target_pairs={{0,2},{2,0},{4,6},{6,4},{8,10},{10,8},{12,14},{14,12},{16,18},{18,... | collective-permute-start | bytes 442376 | tf_op jit(solution)/shard_map/ppermute | solution.py:33
  26.0 14.5 %copy-start.7 = (bf16[2,16,24,768]{3,2,1,0:T(8,128)(2,1)S(1)}, bf16[2,16,24,768]{3,2,1,0:T(8,128)(2,1)}, u32[]{:S(2)}) copy-start(bf16[2,16,24,768]{3,2,1,0:T(8,128)(2,1)} %param.9) | copy-start | bytes 3538948
  26.0 6.3 %collective-permute-start.6 = (bf16[24,1536]{1,0:T(8,128)(2,1)S(1)}, bf16[24,1536]{1,0:T(8,128)(2,1)S(1)}, u32[]{:S(2)}, u32[]{:S(2)}) collective-permute-start(bf16[24,1536]{1,0:T(8,128)(2,1)S(1)} %get-tuple-element.39), channel_id=1, source_target_pairs={{0,24},{2,26},{4,28},{6,30},{8,16},{10,18},{12,20},{14,22},{16,8},... | collective-permute-start | bytes 221192 | tf_op jit(solution)/shard_map/ppermute | solution.py:33
  29.7 5.3 %collective-permute-start.5 = (bf16[24,1536]{1,0:T(8,128)(2,1)S(1)}, bf16[24,1536]{1,0:T(8,128)(2,1)S(1)}, u32[]{:S(2)}, u32[]{:S(2)}) collective-permute-start(bf16[24,1536]{1,0:T(8,128)(2,1)S(1)} %get-tuple-element.38), channel_id=1, source_target_pairs={{0,16},{2,18},{4,20},{6,22},{8,24},{10,26},{12,28},{14,30},{16,0},... | collective-permute-start | bytes 221192 | tf_op jit(solution)/shard_map/ppermute | solution.py:33
  29.7 5.3 %collective-permute-start.4 = (bf16[24,1536]{1,0:T(8,128)(2,1)S(1)}, bf16[24,1536]{1,0:T(8,128)(2,1)S(1)}, u32[]{:S(2)}, u32[]{:S(2)}) collective-permute-start(bf16[24,1536]{1,0:T(8,128)(2,1)S(1)} %get-tuple-element.37), channel_id=1, source_target_pairs={{0,8},{2,10},{4,12},{6,14},{8,0},{10,2},{12,4},{14,6},{16,24},{18,... | collective-permute-start | bytes 221192 | tf_op jit(solution)/shard_map/ppermute | solution.py:33
  35.3 5.1 %copy-start.12 = (bf16[24,2,2,384]{3,2,1,0:T(2,128)(2,1)}, bf16[24,2,2,384]{3,2,1,0:T(2,128)(2,1)S(1)}, u32[]{:S(2)}) copy-start(bf16[24,2,2,384]{3,2,1,0:T(2,128)(2,1)S(1)} %copy.105) | copy-start | bytes 221188
  36.0 7.0 %collective-permute-start.9 = (bf16[24,1536]{1,0:T(8,128)(2,1)}, bf16[24,1536]{1,0:T(8,128)(2,1)}, u32[]{:S(2)}, u32[]{:S(2)}) collective-permute-start(bf16[24,1536]{1,0:T(8,128)(2,1)} %convert_element_type.113), channel_id=1, source_target_pairs={{0,24},{2,26},{4,28},{6,30},{8,16},{10,18},{12,20},{14,22},{16,8},... | collective-permute-start | bytes 221192 | tf_op jit(solution)/shard_map/ppermute | solution.py:33
  38.0 6.4 %collective-permute-start.8 = (bf16[24,1536]{1,0:T(8,128)(2,1)}, bf16[24,1536]{1,0:T(8,128)(2,1)}, u32[]{:S(2)}, u32[]{:S(2)}) collective-permute-start(bf16[24,1536]{1,0:T(8,128)(2,1)} %convert_element_type.113), channel_id=1, source_target_pairs={{0,16},{2,18},{4,20},{6,22},{8,24},{10,26},{12,28},{14,30},{16,0},... | collective-permute-start | bytes 221192 | tf_op jit(solution)/shard_map/ppermute | solution.py:33
  38.2 6.2 %collective-permute-start.7 = (bf16[24,1536]{1,0:T(8,128)(2,1)}, bf16[24,1536]{1,0:T(8,128)(2,1)}, u32[]{:S(2)}, u32[]{:S(2)}) collective-permute-start(bf16[24,1536]{1,0:T(8,128)(2,1)} %convert_element_type.113), channel_id=1, source_target_pairs={{0,8},{2,10},{4,12},{6,14},{8,0},{10,2},{12,4},{14,6},{16,24},{18,... | collective-permute-start | bytes 221192 | tf_op jit(solution)/shard_map/ppermute | solution.py:33
  41.3 6.3 %copy-start.1 = (bf16[1,384,1536]{2,1,0:T(8,128)(2,1)S(1)}, bf16[1,384,1536]{2,1,0:T(8,128)(2,1)}, u32[]{:S(2)}) copy-start(bf16[1,384,1536]{2,1,0:T(8,128)(2,1)} %param.7) | copy-start | bytes 3538948
  46.4 5.5 %collective-permute-start.10 = (bf16[4,24,768]{2,1,0:T(8,128)(2,1)}, bf16[4,24,768]{2,1,0:T(8,128)(2,1)}, u32[]{:S(2)}, u32[]{:S(2)}) collective-permute-start(bf16[4,24,768]{2,1,0:T(8,128)(2,1)} %get-tuple-element.43), channel_id=1, source_target_pairs={{0,4},{2,6},{4,0},{6,2},{8,12},{10,14},{12,8},{14,10},{16,20},{18,... | collective-permute-start | bytes 442376 | tf_op jit(solution)/shard_map/ppermute | solution.py:33
  49.4 5.8 %copy-start.14 = (bf16[4,1,24,768]{3,2,0,1:T(8,128)(2,1)S(1)}, bf16[4,1,24,768]{3,2,0,1:T(8,128)(2,1)}, u32[]{:S(2)}) copy-start(bf16[4,1,24,768]{3,2,0,1:T(8,128)(2,1)} %get-tuple-element.41) | copy-start | bytes 442372
  49.4 5.8 %collective-permute-start.12 = (bf16[4,24,768]{2,1,0:T(8,128)(2,1)}, bf16[4,24,768]{2,1,0:T(8,128)(2,1)S(1)}, u32[]{:S(2)}, u32[]{:S(2)}) collective-permute-start(bf16[4,24,768]{2,1,0:T(8,128)(2,1)} %get-tuple-element.42), channel_id=1, source_target_pairs={{0,2},{2,0},{4,6},{6,4},{8,10},{10,8},{12,14},{14,12},{16,18},{18,... | collective-permute-start | bytes 442376 | tf_op jit(solution)/shard_map/ppermute | solution.py:33
  52.9 6.8 %collective-permute-start.11 = (bf16[4,2,24,768]{3,2,0,1:T(8,128)(2,1)S(1)}, bf16[4,2,24,768]{3,2,0,1:T(8,128)(2,1)S(1)}, u32[]{:S(2)}, u32[]{:S(2)}) collective-permute-start(bf16[4,2,24,768]{3,2,0,1:T(8,128)(2,1)S(1)} %reverse_select_fusion.3), channel_id=1, source_target_pairs={{0,2},{2,0},{4,6},{6,4},{8,10},{10,8},{12,14},{14,12},{16,18},{18,... | collective-permute-start | bytes 884744 | tf_op jit(solution)/shard_map/ppermute | solution.py:33
  55.3 6.8 %collective-permute-start.13 = (bf16[4,2,24,768]{3,2,0,1:T(8,128)(2,1)S(1)}, bf16[4,2,24,768]{3,2,0,1:T(8,128)(2,1)S(1)}, u32[]{:S(2)}, u32[]{:S(2)}) collective-permute-start(bf16[4,2,24,768]{3,2,0,1:T(8,128)(2,1)S(1)} %reverse_select_fusion.2), channel_id=1, source_target_pairs={{0,4},{2,6},{4,0},{6,2},{8,12},{10,14},{12,8},{14,10},{16,20},{18,... | collective-permute-start | bytes 884744 | tf_op jit(solution)/shard_map/ppermute | solution.py:33
  62.2 2.1 %copy-start.6 = (f32[384,1536]{1,0:T(8,128)S(1)}, f32[384,1536]{1,0:T(8,128)}, u32[]{:S(2)}) copy-start(f32[384,1536]{1,0:T(8,128)} %bitcast_convert_fusion) | copy-start | bytes 7077892
  62.4 2.3 %copy-start.10 = (bf16[384,384]{1,0:T(8,128)(2,1)}, bf16[384,384]{1,0:T(8,128)(2,1)S(1)}, u32[]{:S(2)}) copy-start(bf16[384,384]{1,0:T(8,128)(2,1)S(1)} %get-tuple-element.52) | copy-start | bytes 884740
  62.4 2.3 %copy-start.11 = (bf16[384,384]{1,0:T(8,128)(2,1)}, bf16[384,384]{1,0:T(8,128)(2,1)S(1)}, u32[]{:S(2)}) copy-start(bf16[384,384]{1,0:T(8,128)(2,1)S(1)} %get-tuple-element.53) | copy-start | bytes 884740
  62.4 4.2 %copy-start.8 = (bf16[384,384]{1,0:T(8,128)(2,1)}, bf16[384,384]{1,0:T(8,128)(2,1)S(1)}, u32[]{:S(2)}) copy-start(bf16[384,384]{1,0:T(8,128)(2,1)S(1)} %get-tuple-element.33) | copy-start | bytes 884740
  62.5 4.2 %copy-start.9 = (bf16[384,384]{1,0:T(8,128)(2,1)}, bf16[384,384]{1,0:T(8,128)(2,1)S(1)}, u32[]{:S(2)}) copy-start(bf16[384,384]{1,0:T(8,128)(2,1)S(1)} %get-tuple-element.34) | copy-start | bytes 884740
  65.9 6.6 %collective-permute-start.14 = (bf16[768,768]{1,0:T(8,128)(2,1)}, bf16[768,768]{1,0:T(8,128)(2,1)}, u32[]{:S(2)}, u32[]{:S(2)}) collective-permute-start(bf16[768,768]{1,0:T(8,128)(2,1)} %pad_maximum_fusion.1), channel_id=1, source_target_pairs={{0,1},{1,0},{2,3},{3,2},{4,5},{5,4},{6,7},{7,6},{8,9},{9,8},{10,11... | collective-permute-start | bytes 3538952 | tf_op jit(solution)/shard_map/ppermute | solution.py:240
  66.7 38.3 %collective-permute-start.15 = (bf16[2,16,8,768]{3,2,1,0:T(8,128)(2,1)}, bf16[2,16,8,768]{3,2,1,0:T(8,128)(2,1)S(1)}, u32[]{:S(2)}, u32[]{:S(2)}) collective-permute-start(bf16[2,16,8,768]{3,2,1,0:T(8,128)(2,1)} %slice.67), channel_id=1, source_target_pairs={{0,16},{2,18},{4,20},{6,22},{8,24},{10,26},{12,28},{14,30},{16,0},... | collective-permute-start | bytes 1179656 | tf_op jit(solution)/shard_map/ppermute | solution.py:33
  68.0 3.7 %copy-start.13 = (bf16[768,384]{1,0:T(8,128)(2,1)S(1)}, bf16[768,384]{1,0:T(8,128)(2,1)}, u32[]{:S(2)}) copy-start(bf16[768,384]{1,0:T(8,128)(2,1)} %constant.125) | copy-start | bytes 1769476
  68.0 53.5 %collective-permute-start.16 = (bf16[2,16,16,768]{3,2,1,0:T(8,128)(2,1)}, bf16[2,16,16,768]{3,2,1,0:T(8,128)(2,1)}, u32[]{:S(2)}, u32[]{:S(2)}) collective-permute-start(bf16[2,16,16,768]{3,2,1,0:T(8,128)(2,1)} %slice.58), channel_id=1, source_target_pairs={{0,16},{2,18},{4,20},{6,22},{8,24},{10,26},{12,28},{14,30},{16,0},... | collective-permute-start | bytes 2359304 | tf_op jit(solution)/shard_map/ppermute | solution.py:33
  71.6 1.3 copy-start.16
  77.2 52.5 %all-to-all-start = ((bf16[8,2,48,768]{3,2,1,0:T(8,128)(2,1)}), bf16[8,2,48,768]{3,2,1,0:T(8,128)(2,1)S(1)}, u32[]{:S(2)}, u32[]{:S(2)}) async-start(bf16[8,2,48,768]{3,2,1,0:T(8,128)(2,1)} %bitcast.31), calls=%async_computation | async-start | bytes 2359296 | tf_op jit(solution)/shard_map/all_to_all | solution.py:255
  80.9 26.9 %copy-start.4 = (bf16[768,1536]{1,0:T(8,128)(2,1)S(1)}, bf16[768,1536]{1,0:T(8,128)(2,1)}, u32[]{:S(2)}) copy-start(bf16[768,1536]{1,0:T(8,128)(2,1)} %constant.122) | copy-start | bytes 7077892
  105.0 0.7 copy-start.15
  107.9 14.8 %copy-start.5 = (bf16[768,1536]{1,0:T(8,128)(2,1)S(1)}, bf16[768,1536]{1,0:T(8,128)(2,1)}, u32[]{:S(2)}) copy-start(bf16[768,1536]{1,0:T(8,128)(2,1)} %constant.123) | copy-start | bytes 7077892
  122.7 3.9 %slice-start = ((s8[4718592]{0:T(1024)(128)(4,1)}), s8[4194304]{0:T(1024)(128)(4,1)S(1)}, s32[]{:S(2)}) async-start(s8[4718592]{0:T(1024)(128)(4,1)} %bitcast.114), calls=%async_computation.2 | async-start | bytes 8388608
  123.5 3.2 %slice-start.1 = ((s8[4718592]{0:T(1024)(128)(4,1)}), s8[524288]{0:T(1024)(128)(4,1)S(1)}, s32[]{:S(2)}) async-start(s8[4718592]{0:T(1024)(128)(4,1)} %bitcast.114), calls=%async_computation.3 | async-start | bytes 1048576
  135.6 10.4 %all-to-all-start.1 = ((f32[32,1,16]{2,1,0:T(1,128)}), f32[32,1,16]{2,1,0:T(1,128)S(1)}, u32[]{:S(2)}, u32[]{:S(2)}) async-start(f32[32,1,16]{2,1,0:T(1,128)} %bitcast.43), calls=%async_computation.1 | async-start | bytes 32768 | tf_op jit(solution)/shard_map/all_to_all | solution.py:273

commit v4 on v3

v4 whole, which is shorter than its diff:
```python
import numpy as np

import jax
import jax.numpy as jnp
from jax import lax
from jax.experimental import pallas as pl
from jax.experimental.pallas import tpu as pltpu
from jax.sharding import PartitionSpec as P

bf16 = jnp.bfloat16
f32 = jnp.float32


def propagator(grid_size):
    index = np.arange(grid_size)
    centred = (index + grid_size // 2) % grid_size - grid_size // 2
    squared = centred * centred % (4 * grid_size)
    column = np.fft.ifft(np.exp(-2j * np.pi * squared / (4 * grid_size)))
    matrix = column[(index[:, None] - index[None, :]) % grid_size]
    return matrix.real, matrix.imag


def stages(count):
    digits, stride = [], 1
    while count // stride > 4:
        digits.append((stride, 2))
        stride *= 2
    digits.append((stride, count // stride))
    return digits


def exchange(values, offset, count):
    return lax.ppermute(values, "modes", [(i, i ^ offset) for i in range(count)])


def pick(values, index, axis):
    return lax.dynamic_index_in_dim(values, index, axis, keepdims=False)


def reduce_digit(keep, got):
    for g in got:
        keep = keep + g.astype(f32)
    return keep


def gather_digit(block, own, stride, size, axis, count):
    got = [block] + [exchange(block, e * stride, count) for e in range(1, size)]
    stacked = jnp.stack(got, axis)
    if size == 2:
        return jnp.where(own == 0, stacked, jnp.flip(stacked, axis))
    return jnp.stack([pick(stacked, own ^ at, axis) for at in range(size)], axis)


def split_digit(partial, own, size, axis):
    send = [pick(partial, own ^ e, axis).astype(bf16) for e in range(1, size)]
    return send, pick(partial, own, axis)


def product_of(fore, back):
    half = fore.shape[-1] // 2
    fore, back = fore.astype(f32), back.astype(f32)
    fore_re, fore_im = fore[..., :half], fore[..., half:]
    back_re, back_im = back[..., :half], back[..., half:]
    return back_re * fore_re + back_im * fore_im, back_re * fore_im - back_im * fore_re


def products_kernel(rows, fore_ref, back_ref, send_a, keep_a, send_b, keep_b):
    me = lax.axis_index("modes")
    low, high = me % 2 == 1, me // 2 % 2 == 1
    grid_size = fore_ref.shape[1] // 2
    half = grid_size // 2
    pair = 2 * rows
    for part in range(2):
        cols = [pl.ds(part * half, half), pl.ds(grid_size + part * half, half)]
        fore_re, fore_im = [fore_ref[:, c].astype(f32) for c in cols]
        back_re, back_im = [back_ref[:, c].astype(f32) for c in cols]
        values = (back_re * fore_re + back_im * fore_im, back_re * fore_im - back_im * fore_re)
        for k, v in enumerate(values):
            into = pl.ds(k * half, half)
            if part == 0:
                first = jnp.concatenate([v[:rows], v[pair : pair + rows]], 0)
                second = jnp.concatenate([v[rows:pair], v[pair + rows :]], 0)
                send_a[:, into] = jnp.where(low, first, second).astype(bf16)
                keep_a[:, into] = jnp.where(low, second, first)
            else:
                first, second = v[:pair], v[pair:]
                send_b[:, into] = jnp.where(high, first, second).astype(bf16)
                keep_b[:, into] = jnp.where(high, second, first)


def halve_kernel(rows, stride, keep_ref, got_ref, send_ref, left_ref):
    upper = lax.axis_index("modes") // stride % 2 == 1
    pair = 2 * rows
    for group in range(keep_ref.shape[0] // (2 * pair)):
        at = pl.ds(group * 2 * pair, 2 * pair)
        v = keep_ref[at] + got_ref[at].astype(f32)
        first = jnp.concatenate([v[:rows], v[pair : pair + rows]], 0)
        second = jnp.concatenate([v[rows:pair], v[pair + rows :]], 0)
        into = pl.ds(group * pair, pair)
        send_ref[into] = jnp.where(upper, first, second).astype(bf16)
        left_ref[into] = jnp.where(upper, second, first)


def shape_kernel(plane_a, plane_b, fore_ref, plane_ref, shaped_ref):
    rows, grid_size = plane_a.shape
    half = grid_size // 2
    step = 48
    for at in range(0, rows, step):
        here = pl.ds(at, step)
        for part, ref in enumerate((plane_a, plane_b)):
            real, imag = ref[here, :half], ref[here, half:]
            left, right = pl.ds(part * half, half), pl.ds(grid_size + part * half, half)
            plane_ref[here, left] = real
            plane_ref[here, right] = imag
            real, imag = real.astype(f32), imag.astype(f32)
            fore_re, fore_im = fore_ref[here, left].astype(f32), fore_ref[here, right].astype(f32)
            shaped_ref[here, left] = (fore_re * real - fore_im * imag).astype(bf16)
            shaped_ref[pl.ds(rows + at, step), left] = (fore_re * imag + fore_im * real).astype(bf16)


def times(one, two):
    return jnp.dot(one, two, preferred_element_type=f32)


def own_kernel(table_ref, shaped_ref, out_ref):
    out_ref[...] = times(table_ref[...], shaped_ref[...])


def other_kernel(table_ref, shaped_ref, own_ref, out_ref):
    out_ref[...] = (own_ref[...] + times(table_ref[...], shaped_ref[...])).astype(bf16)


def fields_kernel(mode_rows, columns_ref, re_ref, im_ref, out_ref):
    owners, _, pixel_rows, grid_size = columns_ref.shape
    rows = owners * pixel_rows
    real = columns_ref[:, 0].reshape(rows, grid_size)
    imag = columns_ref[:, 1].reshape(rows, grid_size)
    c_re, c_im = re_ref[...], im_ref[...]
    for k, v in enumerate(
        (times(real, c_re) - times(imag, c_im), times(real, c_im) + times(imag, c_re))
    ):
        into = pl.ds(k * grid_size, grid_size)
        if mode_rows % 8 == 0:
            for half in range(2):
                for owner in range(0, owners, 2):
                    at = [o * pixel_rows + half * mode_rows for o in (owner, owner + 1)]
                    both = jnp.concatenate([v[a : a + mode_rows] for a in at], 0)
                    start = half * owners * mode_rows + owner * mode_rows
                    out_ref[pl.ds(start, 2 * mode_rows), into] = both.astype(bf16)
        else:
            out_ref[:, into] = v.astype(bf16)


def targets_kernel(re_ref, im_ref, *refs):
    grid_size = re_ref.shape[0]
    c_re, c_im = re_ref[...], im_ref[...]
    start = 0
    for ref in refs[:-1]:
        real, imag = ref[0], ref[1]
        rows = pl.ds(start, real.shape[0])
        refs[-1][rows, :grid_size] = (times(real, c_re) + times(imag, c_im)).astype(bf16)
        refs[-1][rows, grid_size:] = (times(imag, c_re) - times(real, c_im)).astype(bf16)
        start += real.shape[0]


def coupling_kernel(mode_rows, fields_ref, *rest):
    targets, out_ref = rest[:-1], rest[-1]
    sources, _, pixel_rows, grid_size = fields_ref.shape
    count = lax.axis_size("modes")
    half = lax.axis_index("modes") // (count // 2)
    left = sources * pixel_rows
    field_re = fields_ref[:, 0].reshape(left, grid_size)
    field_im = fields_ref[:, 1].reshape(left, grid_size)

    def against(one, two):
        return lax.dot_general(one, two, (((1,), (1,)), ((), ())), preferred_element_type=f32)

    modes = out_ref.shape[1] // 2
    totals = [jnp.zeros((sources, modes), f32)] * 2
    first = 0
    for which, target in enumerate(targets):
        right = target.shape[0]
        if which == 1:
            first = 0
        in_half = half if which == 0 else 1 - half
        target_re, target_im = target[:, :grid_size], target[:, grid_size:]
        row = lax.broadcasted_iota(jnp.int32, (left, right), 0) % pixel_rows
        col = lax.broadcasted_iota(jnp.int32, (left, right), 1) % mode_rows
        same = row == col + in_half * mode_rows
        member = lax.broadcasted_iota(jnp.int32, (modes, right), 1) // mode_rows + first
        group = lax.broadcasted_iota(jnp.int32, (modes, right), 0)
        groups = jnp.where(member == group, 1.0, 0.0).astype(f32)
        parts = (
            against(field_re, target_re) + against(field_im, target_im),
            against(field_im, target_re) - against(field_re, target_im),
        )
        for k, v in enumerate(parts):
            v = jnp.where(same, v, 0.0).reshape(sources, pixel_rows, right)
            totals[k] = totals[k] + lax.dot_general(
                jnp.sum(v, 1),
                groups,
                (((1,), (1,)), ((), ())),
                precision=lax.Precision.HIGHEST,
                preferred_element_type=f32,
            )
        first += right // mode_rows
    out_ref[:, :modes] = totals[0]
    out_ref[:, modes:] = totals[1]


def kernel_call(kernel, shape, dtype, flops, operands, grant=8, **more):
    place = pl.BlockSpec(memory_space=pltpu.VMEM)
    several = isinstance(dtype, list)
    if several:
        out_shape = [jax.ShapeDtypeStruct(s, d) for s, d in zip(shape, dtype)]
    else:
        out_shape = jax.ShapeDtypeStruct(shape, dtype)
    specs = dict(in_specs=[place] * len(operands), out_specs=[place] * len(shape) if several else place)
    return pl.pallas_call(
        kernel,
        out_shape=out_shape,
        compiler_params=pltpu.CompilerParams(vmem_limit_bytes=grant << 20),
        cost_estimate=pl.CostEstimate(flops=flops, bytes_accessed=1 << 20, transcendentals=0),
        **(specs | more),
    )(*operands)


def local(forward, backward, targets):
    modes_here, local_rows, double_width = forward.shape
    grid_size = double_width // 2
    count = lax.axis_size("modes")
    mode_total = modes_here * count
    block_rows = local_rows // count
    digits = stages(count)
    sizes = [size for _, size in reversed(digits)]
    half = grid_size // 2
    matmul = 2 * local_rows * double_width * double_width
    me = lax.axis_index("modes")
    owns = [me // stride % size for stride, size in digits]
    last = len(digits) - 1

    c_re, c_im = propagator(grid_size)
    full_re, full_im = jnp.asarray(c_re, bf16), jnp.asarray(c_im, bf16)

    def across(*parts):
        flat = [part.reshape(2, -1, grid_size) for part in parts]
        rows = sum(f.shape[1] for f in flat)
        flops = 4 * rows * grid_size * double_width
        return kernel_call(targets_kernel, (rows, double_width), bf16, flops, (full_re, full_im, *flat))

    unit = mode_total // 8
    cuts = [unit * at for at in range(6)] + [mode_total]
    chunks = [targets[:, a:b] for a, b in zip(cuts, cuts[1:])]
    partner = [exchange(chunk, count // 2, count) for chunk in chunks]
    seen = across(targets)

    first = list(range(last))
    orders = [first, [1, 0] + first[2:]]
    in_kernels = last == 2 and block_rows % 8 == 0
    kept = []
    if in_kernels:
        lanes, wide = 4 * block_rows, pl.BlockSpec((4 * block_rows, double_width), lambda i: (i, 0))
        narrow = pl.BlockSpec((2 * block_rows, grid_size), lambda i: (i, 0))
        halves = kernel_call(
            lambda *refs: products_kernel(block_rows, *refs),
            [(local_rows // 2, grid_size)] * 4,
            [bf16, f32, bf16, f32],
            8 * local_rows * double_width,
            (forward[0], backward[0]),
            grid=(local_rows // lanes,),
            grant=56,
            in_specs=[wide] * 2,
            out_specs=[narrow] * 4,
        )
        got = [exchange(halves[2 * part], digits[part][0], count) for part in range(2)]
        got[0], seen = lax.optimization_barrier((got[0], seen))
        got[1], partner[0] = lax.optimization_barrier((got[1], partner[0]))
        for part in range(2):
            stride = digits[1 - part][0]
            send, keep = kernel_call(
                lambda *refs: halve_kernel(block_rows, stride, *refs),
                [(local_rows // 4, grid_size)] * 2,
                [bf16, f32],
                4 * local_rows * grid_size,
                (halves[2 * part + 1], got[part]),
            )
            came = exchange(send, stride, count)
            if part == 1:
                came, partner[1] = lax.optimization_barrier((came, partner[1]))
            keep = reduce_digit(keep, [came])
            kept.append(keep.reshape(-1, block_rows, grid_size))
    else:
        product = product_of(forward[0], backward[0])
        for part, order in enumerate(orders):
            cols = slice(part * half, (part + 1) * half)
            axes = [last - d for d in range(len(digits))]
            partial = jnp.concatenate([p[:, cols] for p in product], -1)
            partial = partial.reshape(*sizes, block_rows, grid_size)
            for d in order:
                stride, size = digits[d]
                send, keep = split_digit(partial, owns[d], size, axes[d])
                got = [exchange(v, (e + 1) * stride, count) for e, v in enumerate(send)]
                partial = reduce_digit(keep, got)
                axes = [a - (a > axes[d]) for a in axes]
            kept.append(partial)
    stride, size = digits[last]
    send, keep = split_digit(jnp.concatenate(kept, -1), owns[last], size, 0)
    got = [exchange(v, (e + 1) * stride, count) for e, v in enumerate(send)]
    summed = reduce_digit(keep, got)
    parts = []
    for part in range(2):
        over_re = summed[:, part * grid_size : part * grid_size + half]
        over_im = summed[:, part * grid_size + half : (part + 1) * grid_size]
        scale = lax.rsqrt(over_re * over_re + over_im * over_im + mode_total)
        parts += [over_re * scale, over_im * scale]
    block = jnp.concatenate(parts, -1).astype(bf16)

    block = gather_digit(block, owns[last], stride, size, 0, count)
    planes = []
    for part, order in enumerate(orders):
        piece = block[..., part * grid_size : (part + 1) * grid_size]
        done = [last]
        for at, d in enumerate(reversed(order)):
            axis = sum(1 for other in done if other > d)
            piece = gather_digit(piece, owns[d], *digits[d], axis, count)
            if part == 1 and at < 2:
                piece, partner[2 + at] = lax.optimization_barrier((piece, partner[2 + at]))
            done.append(d)
        planes.append(piece.reshape(local_rows, grid_size))

    phase_plane, shaped = kernel_call(
        shape_kernel,
        [(local_rows, double_width), (2 * local_rows, grid_size)],
        [bf16, bf16],
        8 * local_rows * double_width,
        (*planes, forward[0]),
    )
    other = lax.ppermute(shaped, "rows", [(0, 1), (1, 0)])

    order = np.arange(local_rows).reshape(2, count // 2, block_rows).transpose(1, 0, 2).reshape(count // 2, -1)

    def table(cols):
        real, imag = c_re[:local_rows, cols], c_im[:local_rows, cols]
        rows = np.stack([np.concatenate([real, -imag], 1)[order], np.concatenate([imag, real], 1)[order]], 1)
        return jnp.asarray(rows.reshape(2 * local_rows, -1), bf16)

    column_shape = (2 * local_rows, grid_size)
    columns = kernel_call(
        own_kernel, column_shape, f32, matmul // 2, (table(slice(0, local_rows)), shaped)
    )
    columns, other, partner[4] = lax.optimization_barrier((columns, other, partner[4]))
    columns = kernel_call(
        other_kernel, column_shape, bf16, matmul // 2, (table(slice(local_rows, None)), other, columns)
    ).reshape(count // 2, 2, 2 * block_rows, grid_size)

    together = [list(range(count // 2)), list(range(count // 2, count))]
    pixels = lax.all_to_all(columns, "modes", 0, 0, tiled=True, axis_index_groups=together)

    output_fields = kernel_call(
        lambda *refs: fields_kernel(block_rows, *refs),
        (local_rows, double_width),
        bf16,
        matmul,
        (columns, full_re, full_im),
    )
    if block_rows % 8 != 0:
        output_fields = output_fields.reshape(count // 2, 2, block_rows, double_width)
        output_fields = output_fields.transpose(1, 0, 2, 3).reshape(local_rows, double_width)
    pixels, output_fields = lax.optimization_barrier((pixels, output_fields))

    term = kernel_call(
        lambda *refs: coupling_kernel(block_rows, *refs),
        (mode_total // 2, 2 * mode_total),
        f32,
        2 * matmul,
        (pixels, seen, across(*partner[:5]), across(partner[5])),
        grant=16,
    )
    term = term.reshape(mode_total // 2, 2, 1, mode_total).transpose(1, 2, 0, 3)
    in_half = (jnp.arange(2) == me // (count // 2)).reshape(1, 2, 1, 1)
    term = jnp.where(in_half, term, 0.0).reshape(2 * mode_total, mode_total)
    pieces = lax.all_to_all(term, ("modes", "rows"), 0, 0, tiled=True)
    coupling = jnp.sum(pieces, 0, keepdims=True)
    return (phase_plane, output_fields[None], coupling)


def solution(mesh):
    return jax.shard_map(
        local,
        mesh=mesh,
        in_specs=(
            P("modes", "rows", None),
            P("modes", "rows", None),
            P(None, None, ("rows", "modes"), None),
        ),
        out_specs=(P("rows", None), P("modes", "rows", None), P(("modes", "rows"), None)),
        check_vma=False,
    )
```

time: 147 us -> 148 us (level)
  Pallas kernels: 5.73 us -> 27.3 us
  matrix products: 19.5 us -> 0 us
  blocking collectives: 0 us -> 13.5 us
  local copies, waits for them, and re-layouts: 19.9 us -> 10.5 us
  other arithmetic: 12 us -> 4.12 us
  starting transfers between devices: 27.6 us -> 29.3 us
    pallas_call x2 -> x11, Pallas kernels: 5.73 us -> 27.3 us  [kernel_call(): pl.pallas_call(kernel, out_shape=out_shape, compiler_params=pltpu.Compile...]
    dot_general x10 -> x0, matrix products: 19.5 us -> none  [the longest x6 11.4 us: back(): return jnp.dot(flat, back_table, preferred_element_type=f32).astype(bf16)]
    all_to_all x0 -> x1, blocking collectives: none -> 13.5 us  [local(): pieces = lax.all_to_all(term, ('modes', 'rows'), 0, 0, tiled=True)]
    ppermute x16 -> x20, waiting for transfers between devices: 55.8 us -> 61.6 us  [exchange(): lax.ppermute(values, 'modes', [(i, i ^ offset) for i in range(count)])]
    all_to_all x1 -> x0, waiting for transfers between devices: 4.81 us -> none  [local(): pieces = lax.all_to_all(term, ('modes', 'rows'), 0, 0, tiled=True)]
    ppermute x16 -> x20, starting transfers between devices: 20.6 us -> 24.9 us  [exchange(): lax.ppermute(values, 'modes', [(i, i ^ offset) for i in range(count)])]
    convert_element_type x6 -> x0, local copies, waits for them, and re-layouts: 3.91 us -> none  [the longest x3 2.4 us: local(): block = jnp.stack([over_re * scale, over_im * scale], 2).astype(bf16)]
    slice x6 -> x2, local copies, waits for them, and re-layouts: 5.25 us -> 1.69 us  [local(): chunks = [targets[:, a:b] for a, b in zip(cuts, cuts[1:])]]
  transfers between devices with their start and end apart: 19 -> 22, of which waited for: 12 -> 13; matrix products, arithmetic and copies ran while one was open for 27% -> 2% of each run, Pallas kernels for 0% -> 11%
where the time goes in v4:
time: 148 us; the launch traced here: 147 us
  waiting for transfers between devices  61.6 us (42%)
  starting transfers between devices  29.3 us (20%)
  Pallas kernels  27.3 us (18%)
  blocking collectives  13.5 us (9%)
  local copies, waits for them, and re-layouts  10.5 us (7%)
  other arithmetic  4.12 us (3%)
    ppermute x20, waiting for transfers between devices, exchange(): lax.ppermute(values, 'modes', [(i, i ^ offset) for i in range(count)])  61.6 us
    pallas_call x11, Pallas kernels, kernel_call(): pl.pallas_call(kernel, out_shape=out_shape, compiler_params=pltpu.Compile...  27.3 us
    ppermute x20, starting transfers between devices, exchange(): lax.ppermute(values, 'modes', [(i, i ^ offset) for i in range(count)])  24.9 us
    all_to_all x1, blocking collectives, local(): pieces = lax.all_to_all(term, ('modes', 'rows'), 0, 0, tiled=True)  13.5 us
    unnamed x36, local copies, waits for them, and re-layouts  7.69 us
    all_to_all x1, starting transfers between devices, local(): lax.all_to_all(columns, 'modes', 0, 0, tiled=True, axis_index_groups=toge...  4.43 us
  transfers between devices with their start and end apart: 22, of which 13 were waited for; matrix products, arithmetic and copies ran while one was open for 2% of the time, Pallas kernels for 11%

profile of v4, /device:TPU:0, one launch (start us, length us, event | category | flops | bytes accessed | tf_op | source)
XLA Modules:
  0.0 147.3 jit_solution(6499547490525212904)
XLA Ops:
  0.6 4.0 %shard_map.94 = (bf16[192,768]{1,0:T(8,128)(2,1)}, f32[192,768]{1,0:T(8,128)}, bf16[192,768]{1,0:T(8,128)(2,1)}, f32[192,768]{1,0:T(8,128)}) custom-call(bf16[384,1536]{1,0:T(8,128)(2,1)} %bitcast.57, bf16[384,1536]{1,0:T(8,128)(2,1)} %bitcast.68), custom_call_target="tpu_custom_call" | custom-call | flops 4718592 | bytes 1048576 | tf_op jit(solution)/shard_map/pallas_call | solution.py:219
  4.6 3.0 %collective-permute-start.2 = (bf16[192,768]{1,0:T(8,128)(2,1)}, bf16[192,768]{1,0:T(8,128)(2,1)}, u32[]{:S(2)}, u32[]{:S(2)}) collective-permute-start(bf16[192,768]{1,0:T(8,128)(2,1)} %get-tuple-element.34), channel_id=1, source_target_pairs={{0,4},{2,6},{4,0},{6,2},{8,12},{10,14},{12,8},{14,10},{16,20},{18,... | collective-permute-start | bytes 884744 | tf_op jit(solution)/shard_map/ppermute | solution.py:33
  7.6 0.9 fusion.14
  8.5 2.6 %collective-permute-start.3 = (bf16[2,2,24,768]{3,2,1,0:T(8,128)(2,1)}, bf16[2,2,24,768]{3,2,1,0:T(8,128)(2,1)}, u32[]{:S(2)}, u32[]{:S(2)}) collective-permute-start(bf16[2,2,24,768]{3,2,1,0:T(8,128)(2,1)} %get-tuple-element.57), channel_id=1, source_target_pairs={{0,16},{2,18},{4,20},{6,22},{8,24},{10,26},{12,28},{14,30},{16,0},... | collective-permute-start | bytes 442376 | tf_op jit(solution)/shard_map/ppermute | solution.py:33
  11.1 1.5 %collective-permute-start = (bf16[192,768]{1,0:T(8,128)(2,1)}, bf16[192,768]{1,0:T(8,128)(2,1)}, u32[]{:S(2)}, u32[]{:S(2)}) collective-permute-start(bf16[192,768]{1,0:T(8,128)(2,1)} %get-tuple-element.29), channel_id=1, source_target_pairs={{0,2},{2,0},{4,6},{6,4},{8,10},{10,8},{12,14},{14,12},{16,18},{18,... | collective-permute-start | bytes 884744 | tf_op jit(solution)/shard_map/ppermute | solution.py:33
  13.0 9.6 %collective-permute-done.3 = bf16[2,2,24,768]{3,2,1,0:T(8,128)(2,1)} collective-permute-done((bf16[2,2,24,768]{3,2,1,0:T(8,128)(2,1)}, bf16[2,2,24,768]{3,2,1,0:T(8,128)(2,1)}, u32[]{:S(2)}, u32[]{:S(2)}) %collective-permute-start.3) | collective-permute-done | bytes 147488 | tf_op jit(solution)/shard_map/ppermute | solution.py:33
  22.6 1.1 copy-done.7
  23.6 1.0 shard_map.97
  24.7 1.6 %collective-permute-start.4 = (bf16[96,768]{1,0:T(8,128)(2,1)S(1)}, bf16[96,768]{1,0:T(8,128)(2,1)S(1)}, u32[]{:S(2)}, u32[]{:S(2)}) collective-permute-start(bf16[96,768]{1,0:T(8,128)(2,1)S(1)} %get-tuple-element.37), channel_id=1, source_target_pairs={{0,2},{2,0},{4,6},{6,4},{8,10},{10,8},{12,14},{14,12},{16,18},{18,... | collective-permute-start | bytes 442376 | tf_op jit(solution)/shard_map/ppermute | solution.py:33
  26.2 2.0 %shard_map.95.refs_1_ = bf16[384,1536]{1,0:T(8,128)(2,1)S(1)} custom-call(bf16[768,768]{1,0:T(8,128)(2,1)S(1)} %copy-done.1, bf16[768,768]{1,0:T(8,128)(2,1)S(1)} %copy-done.2, bf16[2,384,768]{2,1,0:T(8,128)(2,1)S(1)} %bitcast.61), custom_call_target="tpu_custom_call" | custom-call | flops 1811939328 | bytes 1048576 | tf_op jit(solution)/shard_map/pallas_call | solution.py:219
  28.2 1.0 copy-done.12
  29.3 1.0 shard_map.96
  30.9 4.6 %collective-permute-done.1 = bf16[96,768]{1,0:T(8,128)(2,1)S(1)} collective-permute-done((bf16[96,768]{1,0:T(8,128)(2,1)S(1)}, bf16[96,768]{1,0:T(8,128)(2,1)S(1)}, u32[]{:S(2)}, u32[]{:S(2)}) %collective-permute-start.1) | collective-permute-done | bytes 147488 | tf_op jit(solution)/shard_map/ppermute | solution.py:33
  35.6 0.7 fusion.12
  36.3 2.7 %collective-permute-start.8 = (bf16[24,1536]{1,0:T(8,128)(2,1)}, bf16[24,1536]{1,0:T(8,128)(2,1)}, u32[]{:S(2)}, u32[]{:S(2)}) collective-permute-start(bf16[24,1536]{1,0:T(8,128)(2,1)} %get-tuple-element.60), channel_id=1, source_target_pairs={{0,24},{2,26},{4,28},{6,30},{8,16},{10,18},{12,20},{14,22},{16,8},... | collective-permute-start | bytes 221192 | tf_op jit(solution)/shard_map/ppermute | solution.py:33
  39.0 1.7 %collective-permute-start.6 = (bf16[24,1536]{1,0:T(8,128)(2,1)}, bf16[24,1536]{1,0:T(8,128)(2,1)}, u32[]{:S(2)}, u32[]{:S(2)}) collective-permute-start(bf16[24,1536]{1,0:T(8,128)(2,1)} %get-tuple-element.58), channel_id=1, source_target_pairs={{0,8},{2,10},{4,12},{6,14},{8,0},{10,2},{12,4},{14,6},{16,24},{18,... | collective-permute-start | bytes 221192 | tf_op jit(solution)/shard_map/ppermute | solution.py:33
  40.7 2.5 %collective-permute-done.8 = bf16[24,1536]{1,0:T(8,128)(2,1)} collective-permute-done((bf16[24,1536]{1,0:T(8,128)(2,1)}, bf16[24,1536]{1,0:T(8,128)(2,1)}, u32[]{:S(2)}, u32[]{:S(2)}) %collective-permute-start.8) | collective-permute-done | bytes 73760 | tf_op jit(solution)/shard_map/ppermute | solution.py:33
  43.2 1.9 %collective-permute-done.7 = bf16[24,1536]{1,0:T(8,128)(2,1)} collective-permute-done((bf16[24,1536]{1,0:T(8,128)(2,1)}, bf16[24,1536]{1,0:T(8,128)(2,1)}, u32[]{:S(2)}, u32[]{:S(2)}) %collective-permute-start.7) | collective-permute-done | bytes 73760 | tf_op jit(solution)/shard_map/ppermute | solution.py:33
  45.1 1.1 fusion.6
  46.2 2.2 %collective-permute-start.11 = (bf16[24,1536]{1,0:T(8,128)(2,1)S(1)}, bf16[24,1536]{1,0:T(8,128)(2,1)S(1)}, u32[]{:S(2)}, u32[]{:S(2)}) collective-permute-start(bf16[24,1536]{1,0:T(8,128)(2,1)S(1)} %pad_maximum_fusion.6), channel_id=1, source_target_pairs={{0,24},{2,26},{4,28},{6,30},{8,16},{10,18},{12,20},{14,22},{16,8},... | collective-permute-start | bytes 221192 | tf_op jit(solution)/shard_map/ppermute | solution.py:33
  48.4 2.3 %collective-permute-start.9 = (bf16[24,1536]{1,0:T(8,128)(2,1)S(1)}, bf16[24,1536]{1,0:T(8,128)(2,1)S(1)}, u32[]{:S(2)}, u32[]{:S(2)}) collective-permute-start(bf16[24,1536]{1,0:T(8,128)(2,1)S(1)} %pad_maximum_fusion.6), channel_id=1, source_target_pairs={{0,8},{2,10},{4,12},{6,14},{8,0},{10,2},{12,4},{14,6},{16,24},{18,... | collective-permute-start | bytes 221192 | tf_op jit(solution)/shard_map/ppermute | solution.py:33
  50.7 1.8 %collective-permute-done.11 = bf16[24,1536]{1,0:T(8,128)(2,1)S(1)} collective-permute-done((bf16[24,1536]{1,0:T(8,128)(2,1)S(1)}, bf16[24,1536]{1,0:T(8,128)(2,1)S(1)}, u32[]{:S(2)}, u32[]{:S(2)}) %collective-permute-start.11) | collective-permute-done | bytes 73760 | tf_op jit(solution)/shard_map/ppermute | solution.py:33
  52.5 1.6 %collective-permute-done.10 = bf16[24,1536]{1,0:T(8,128)(2,1)S(1)} collective-permute-done((bf16[24,1536]{1,0:T(8,128)(2,1)S(1)}, bf16[24,1536]{1,0:T(8,128)(2,1)S(1)}, u32[]{:S(2)}, u32[]{:S(2)}) %collective-permute-start.10) | collective-permute-done | bytes 73760 | tf_op jit(solution)/shard_map/ppermute | solution.py:33
  54.1 0.8 slice_bitcast_fusion
  55.5 1.7 %collective-permute-start.15 = (bf16[2,2,24,768]{3,2,1,0:T(8,128)(2,1)}, bf16[2,2,24,768]{3,2,1,0:T(8,128)(2,1)}, u32[]{:S(2)}, u32[]{:S(2)}) collective-permute-start(bf16[2,2,24,768]{3,2,1,0:T(8,128)(2,1)} %get-tuple-element.55), channel_id=1, source_target_pairs={{0,16},{2,18},{4,20},{6,22},{8,24},{10,26},{12,28},{14,30},{16,0},... | collective-permute-start | bytes 442376 | tf_op jit(solution)/shard_map/ppermute | solution.py:33
  57.1 1.3 collective-permute-start.17
  58.8 1.6 %collective-permute-done.12 = bf16[4,24,768]{2,1,0:T(8,128)(2,1)} collective-permute-done((bf16[4,24,768]{2,1,0:T(8,128)(2,1)}, bf16[4,24,768]{2,1,0:T(8,128)(2,1)}, u32[]{:S(2)}, u32[]{:S(2)}) %collective-permute-start.12) | collective-permute-done | bytes 147488 | tf_op jit(solution)/shard_map/ppermute | solution.py:33
  60.4 1.0 pad_maximum_fusion.4
  62.1 2.2 %collective-permute-done.14 = bf16[4,24,768]{2,1,0:T(8,128)(2,1)S(1)} collective-permute-done((bf16[4,24,768]{2,1,0:T(8,128)(2,1)}, bf16[4,24,768]{2,1,0:T(8,128)(2,1)S(1)}, u32[]{:S(2)}, u32[]{:S(2)}) %collective-permute-start.14) | collective-permute-done | bytes 147488 | tf_op jit(solution)/shard_map/ppermute | solution.py:33
  64.4 1.9 %collective-permute-done.15 = bf16[2,2,24,768]{3,2,1,0:T(8,128)(2,1)} collective-permute-done((bf16[2,2,24,768]{3,2,1,0:T(8,128)(2,1)}, bf16[2,2,24,768]{3,2,1,0:T(8,128)(2,1)}, u32[]{:S(2)}, u32[]{:S(2)}) %collective-permute-start.15) | collective-permute-done | bytes 147488 | tf_op jit(solution)/shard_map/ppermute | solution.py:33
  66.3 1.4 collective-permute-start.16
  68.5 4.5 %collective-permute-done.16 = bf16[4,2,24,768]{3,2,1,0:T(8,128)(2,1)S(1)} collective-permute-done((bf16[4,2,24,768]{3,2,1,0:T(8,128)(2,1)S(1)}, bf16[4,2,24,768]{3,2,1,0:T(8,128)(2,1)S(1)}, u32[]{:S(2)}, u32[]{:S(2)}) %collective-permute-start.16) | collective-permute-done | bytes 294944 | tf_op jit(solution)/shard_map/ppermute | solution.py:33
  73.2 1.1 copy-done
  74.3 1.2 shard_map.98
  76.1 1.1 shard_map.99.own_ref
  77.1 7.7 %collective-permute-done.19 = bf16[2,2,24,768]{3,2,1,0:T(8,128)(2,1)S(1)} collective-permute-done((bf16[2,2,24,768]{3,2,1,0:T(8,128)(2,1)S(1)}, bf16[2,2,24,768]{3,2,1,0:T(8,128)(2,1)S(1)}, u32[]{:S(2)}, u32[]{:S(2)}) %collective-permute-start.19) | collective-permute-done | bytes 147488 | tf_op jit(solution)/shard_map/ppermute | solution.py:33
  85.5 2.1 %shard_map.100 = bf16[768,768]{1,0:T(8,128)(2,1)} custom-call(bf16[768,768]{1,0:T(8,128)(2,1)S(1)} %copy-done.4, bf16[768,768]{1,0:T(8,128)(2,1)S(1)} %collective-permute-done.18.shaped_ref, f32[768,768]{1,0:T(8,128)S(1)} %shard_map.99.own_ref), custom_call_target="tpu_custom_call" | custom-call | flops 905969664 | bytes 1048576 | tf_op jit(solution)/shard_map/pallas_call | solution.py:219
  87.6 4.4 %all-to-all-start = ((bf16[8,2,48,768]{3,2,1,0:T(8,128)(2,1)}), bf16[8,2,48,768]{3,2,1,0:T(8,128)(2,1)}, u32[]{:S(2)}, u32[]{:S(2)}) async-start(bf16[8,2,48,768]{3,2,1,0:T(8,128)(2,1)} %bitcast.28.refs_0_), calls=%async_computation | async-start | bytes 2359296 | tf_op jit(solution)/shard_map/all_to_all | solution.py:357
  92.0 0.8 slice.47
  93.5 21.4 %collective-permute-done.20 = bf16[2,6,24,768]{3,2,1,0:T(8,128)(2,1)S(1)} collective-permute-done((bf16[2,6,24,768]{3,2,1,0:T(8,128)(2,1)}, bf16[2,6,24,768]{3,2,1,0:T(8,128)(2,1)S(1)}, u32[]{:S(2)}, u32[]{:S(2)}) %collective-permute-start.20) | collective-permute-done | bytes 442400 | tf_op jit(solution)/shard_map/ppermute | solution.py:33
  114.9 0.9 shard_map.103.refs_3_
  115.8 5.3 %shard_map.102.refs_2_ = bf16[240,1536]{1,0:T(8,128)(2,1)S(1)} custom-call(bf16[768,768]{1,0:T(8,128)(2,1)S(1)} %copy-done.1, bf16[768,768]{1,0:T(8,128)(2,1)S(1)} %copy-done.2, bf16[2,48,768]{2,1,0:T(8,128)(2,1)} %bitcast.30.refs_0_, bf16[2,48,768]{2,1,0:T(8,128)(2,1)} %bitcast.31.refs_1_, bf16[2,48,768]{2,1,0:T(8,128)(2,1)} %bitcast.32.refs_2_, ...), custom_call_target="tpu_custom_call" | custom-call | flops 1132462080 | bytes 1048576 | tf_op jit(solution)/shard_map/pallas_call | solution.py:219
  121.1 0.9 copy-done.10
  122.0 4.3 %shard_map.101 = bf16[384,1536]{1,0:T(8,128)(2,1)} custom-call(bf16[8,2,48,768]{3,2,1,0:T(8,128)(2,1)} %bitcast.28.refs_0_, bf16[768,768]{1,0:T(8,128)(2,1)S(1)} %copy-done.1, bf16[768,768]{1,0:T(8,128)(2,1)S(1)} %copy-done.2), custom_call_target="tpu_custom_call" | custom-call | flops 1811939328 | bytes 1048576 | tf_op jit(solution)/shard_map/pallas_call | solution.py:219
  126.3 1.1 copy-done.11
  127.4 1.3 copy-done.13
  128.7 4.4 %shard_map.104 = f32[8,32]{1,0:T(8,128)S(1)} custom-call(bf16[8,2,48,768]{3,2,1,0:T(8,128)(2,1)} %all-to-all-done.refs_0_, bf16[384,1536]{1,0:T(8,128)(2,1)S(1)} %copy-done.13, bf16[240,1536]{1,0:T(8,128)(2,1)S(1)} %copy-done.11, bf16[144,1536]{1,0:T(8,128)(2,1)S(1)} %shard_map.103.refs_3_), custom_call_target="tpu_custom_call" | custom-call | flops 3623878656 | bytes 1048576 | tf_op jit(solution)/shard_map/pallas_call | solution.py:219
  133.2 13.5 %all_to_all.11 = f32[32,1,16]{2,1,0:T(1,128)S(1)} all-to-all(f32[32,1,16]{2,1,0:T(1,128)S(1)} %bitcast.81), channel_id=1, replica_groups=mesh['modes'=16,'rows'=2] {'modes','rows'}, dimensions={0} | all-to-all | bytes 4096 | tf_op jit(solution)/shard_map/all_to_all | solution.py:382
  (74 shorter events, 6.4 us)
Async XLA Ops:
  0.6 7.0 %copy-start.3 = (bf16[2,16,24,768]{3,2,1,0:T(8,128)(2,1)S(1)}, bf16[2,16,24,768]{3,2,1,0:T(8,128)(2,1)}, u32[]{:S(2)}) copy-start(bf16[2,16,24,768]{3,2,1,0:T(8,128)(2,1)} %param.9) | copy-start | bytes 3538948
  4.6 21.6 %copy-start.1 = (bf16[768,768]{1,0:T(8,128)(2,1)S(1)}, bf16[768,768]{1,0:T(8,128)(2,1)}, u32[]{:S(2)}) copy-start(bf16[768,768]{1,0:T(8,128)(2,1)} %constant.105.clone.re_ref.refs_1_) | copy-start | bytes 3538948
  4.6 21.6 %copy-start.2 = (bf16[768,768]{1,0:T(8,128)(2,1)S(1)}, bf16[768,768]{1,0:T(8,128)(2,1)}, u32[]{:S(2)}) copy-start(bf16[768,768]{1,0:T(8,128)(2,1)} %constant.106.clone.im_ref.refs_2_) | copy-start | bytes 3538948
  4.6 17.9 %collective-permute-start.2 = (bf16[192,768]{1,0:T(8,128)(2,1)}, bf16[192,768]{1,0:T(8,128)(2,1)}, u32[]{:S(2)}, u32[]{:S(2)}) collective-permute-start(bf16[192,768]{1,0:T(8,128)(2,1)} %get-tuple-element.34), channel_id=1, source_target_pairs={{0,4},{2,6},{4,0},{6,2},{8,12},{10,14},{12,8},{14,10},{16,20},{18,... | collective-permute-start | bytes 884744 | tf_op jit(solution)/shard_map/ppermute | solution.py:33
  8.5 14.0 %collective-permute-start.3 = (bf16[2,2,24,768]{3,2,1,0:T(8,128)(2,1)}, bf16[2,2,24,768]{3,2,1,0:T(8,128)(2,1)}, u32[]{:S(2)}, u32[]{:S(2)}) collective-permute-start(bf16[2,2,24,768]{3,2,1,0:T(8,128)(2,1)} %get-tuple-element.57), channel_id=1, source_target_pairs={{0,16},{2,18},{4,20},{6,22},{8,24},{10,26},{12,28},{14,30},{16,0},... | collective-permute-start | bytes 442376 | tf_op jit(solution)/shard_map/ppermute | solution.py:33
  11.1 18.1 %collective-permute-start = (bf16[192,768]{1,0:T(8,128)(2,1)}, bf16[192,768]{1,0:T(8,128)(2,1)}, u32[]{:S(2)}, u32[]{:S(2)}) collective-permute-start(bf16[192,768]{1,0:T(8,128)(2,1)} %get-tuple-element.29), channel_id=1, source_target_pairs={{0,2},{2,0},{4,6},{6,4},{8,10},{10,8},{12,14},{14,12},{16,18},{18,... | collective-permute-start | bytes 884744 | tf_op jit(solution)/shard_map/ppermute | solution.py:33
  12.6 18.3 %collective-permute-start.5 = (bf16[2,2,24,768]{3,2,1,0:T(8,128)(2,1)}, bf16[2,2,24,768]{3,2,1,0:T(8,128)(2,1)}, u32[]{:S(2)}, u32[]{:S(2)}) collective-permute-start(bf16[2,2,24,768]{3,2,1,0:T(8,128)(2,1)} %get-tuple-element.56), channel_id=1, source_target_pairs={{0,16},{2,18},{4,20},{6,22},{8,24},{10,26},{12,28},{14,30},{16,0},... | collective-permute-start | bytes 442376 | tf_op jit(solution)/shard_map/ppermute | solution.py:33
  22.6 1.1 copy-start.7
  24.7 6.2 %collective-permute-start.4 = (bf16[96,768]{1,0:T(8,128)(2,1)S(1)}, bf16[96,768]{1,0:T(8,128)(2,1)S(1)}, u32[]{:S(2)}, u32[]{:S(2)}) collective-permute-start(bf16[96,768]{1,0:T(8,128)(2,1)S(1)} %get-tuple-element.37), channel_id=1, source_target_pairs={{0,2},{2,0},{4,6},{6,4},{8,10},{10,8},{12,14},{14,12},{16,18},{18,... | collective-permute-start | bytes 442376 | tf_op jit(solution)/shard_map/ppermute | solution.py:33
  26.2 3.0 %copy-start.6 = (f32[192,768]{1,0:T(8,128)S(1)}, f32[192,768]{1,0:T(8,128)}, u32[]{:S(2)}) copy-start(f32[192,768]{1,0:T(8,128)} %get-tuple-element.28.refs_0_) | copy-start | bytes 1769476
  28.2 1.0 copy-start.12
  30.3 5.2 %collective-permute-start.1 = (bf16[96,768]{1,0:T(8,128)(2,1)S(1)}, bf16[96,768]{1,0:T(8,128)(2,1)S(1)}, u32[]{:S(2)}, u32[]{:S(2)}) collective-permute-start(bf16[96,768]{1,0:T(8,128)(2,1)S(1)} %get-tuple-element.32), channel_id=1, source_target_pairs={{0,4},{2,6},{4,0},{6,2},{8,12},{10,14},{12,8},{14,10},{16,20},{18,... | collective-permute-start | bytes 442376 | tf_op jit(solution)/shard_map/ppermute | solution.py:33
  30.9 4.6 %copy-start.14 = (f32[96,768]{1,0:T(8,128)}, f32[96,768]{1,0:T(8,128)S(1)}, u32[]{:S(2)}) copy-start(f32[96,768]{1,0:T(8,128)S(1)} %convert_add_fusion) | copy-start | bytes 884740
  35.6 0.8 copy-start.15
  36.3 6.9 %collective-permute-start.8 = (bf16[24,1536]{1,0:T(8,128)(2,1)}, bf16[24,1536]{1,0:T(8,128)(2,1)}, u32[]{:S(2)}, u32[]{:S(2)}) collective-permute-start(bf16[24,1536]{1,0:T(8,128)(2,1)} %get-tuple-element.60), channel_id=1, source_target_pairs={{0,24},{2,26},{4,28},{6,30},{8,16},{10,18},{12,20},{14,22},{16,8},... | collective-permute-start | bytes 221192 | tf_op jit(solution)/shard_map/ppermute | solution.py:33
  39.0 6.1 %collective-permute-start.7 = (bf16[24,1536]{1,0:T(8,128)(2,1)}, bf16[24,1536]{1,0:T(8,128)(2,1)}, u32[]{:S(2)}, u32[]{:S(2)}) collective-permute-start(bf16[24,1536]{1,0:T(8,128)(2,1)} %get-tuple-element.59), channel_id=1, source_target_pairs={{0,16},{2,18},{4,20},{6,22},{8,24},{10,26},{12,28},{14,30},{16,0},... | collective-permute-start | bytes 221192 | tf_op jit(solution)/shard_map/ppermute | solution.py:33
  39.0 6.1 %collective-permute-start.6 = (bf16[24,1536]{1,0:T(8,128)(2,1)}, bf16[24,1536]{1,0:T(8,128)(2,1)}, u32[]{:S(2)}, u32[]{:S(2)}) collective-permute-start(bf16[24,1536]{1,0:T(8,128)(2,1)} %get-tuple-element.58), channel_id=1, source_target_pairs={{0,8},{2,10},{4,12},{6,14},{8,0},{10,2},{12,4},{14,6},{16,24},{18,... | collective-permute-start | bytes 221192 | tf_op jit(solution)/shard_map/ppermute | solution.py:33
  46.2 6.2 %collective-permute-start.11 = (bf16[24,1536]{1,0:T(8,128)(2,1)S(1)}, bf16[24,1536]{1,0:T(8,128)(2,1)S(1)}, u32[]{:S(2)}, u32[]{:S(2)}) collective-permute-start(bf16[24,1536]{1,0:T(8,128)(2,1)S(1)} %pad_maximum_fusion.6), channel_id=1, source_target_pairs={{0,24},{2,26},{4,28},{6,30},{8,16},{10,18},{12,20},{14,22},{16,8},... | collective-permute-start | bytes 221192 | tf_op jit(solution)/shard_map/ppermute | solution.py:33
  48.4 5.6 %collective-permute-start.10 = (bf16[24,1536]{1,0:T(8,128)(2,1)S(1)}, bf16[24,1536]{1,0:T(8,128)(2,1)S(1)}, u32[]{:S(2)}, u32[]{:S(2)}) collective-permute-start(bf16[24,1536]{1,0:T(8,128)(2,1)S(1)} %pad_maximum_fusion.6), channel_id=1, source_target_pairs={{0,16},{2,18},{4,20},{6,22},{8,24},{10,26},{12,28},{14,30},{16,0},... | collective-permute-start | bytes 221192 | tf_op jit(solution)/shard_map/ppermute | solution.py:33
  48.4 5.6 %collective-permute-start.9 = (bf16[24,1536]{1,0:T(8,128)(2,1)S(1)}, bf16[24,1536]{1,0:T(8,128)(2,1)S(1)}, u32[]{:S(2)}, u32[]{:S(2)}) collective-permute-start(bf16[24,1536]{1,0:T(8,128)(2,1)S(1)} %pad_maximum_fusion.6), channel_id=1, source_target_pairs={{0,8},{2,10},{4,12},{6,14},{8,0},{10,2},{12,4},{14,6},{16,24},{18,... | collective-permute-start | bytes 221192 | tf_op jit(solution)/shard_map/ppermute | solution.py:33
  55.0 5.5 %collective-permute-start.12 = (bf16[4,24,768]{2,1,0:T(8,128)(2,1)}, bf16[4,24,768]{2,1,0:T(8,128)(2,1)}, u32[]{:S(2)}, u32[]{:S(2)}) collective-permute-start(bf16[4,24,768]{2,1,0:T(8,128)(2,1)} %get-tuple-element.64), channel_id=1, source_target_pairs={{0,4},{2,6},{4,0},{6,2},{8,12},{10,14},{12,8},{14,10},{16,20},{18,... | collective-permute-start | bytes 442376 | tf_op jit(solution)/shard_map/ppermute | solution.py:33
  55.5 10.8 %collective-permute-start.15 = (bf16[2,2,24,768]{3,2,1,0:T(8,128)(2,1)}, bf16[2,2,24,768]{3,2,1,0:T(8,128)(2,1)}, u32[]{:S(2)}, u32[]{:S(2)}) collective-permute-start(bf16[2,2,24,768]{3,2,1,0:T(8,128)(2,1)} %get-tuple-element.55), channel_id=1, source_target_pairs={{0,16},{2,18},{4,20},{6,22},{8,24},{10,26},{12,28},{14,30},{16,0},... | collective-permute-start | bytes 442376 | tf_op jit(solution)/shard_map/ppermute | solution.py:33
  57.1 16.0 %collective-permute-start.17 = (bf16[2,2,24,768]{3,2,1,0:T(8,128)(2,1)}, bf16[2,2,24,768]{3,2,1,0:T(8,128)(2,1)}, u32[]{:S(2)}, u32[]{:S(2)}) collective-permute-start(bf16[2,2,24,768]{3,2,1,0:T(8,128)(2,1)} %get-tuple-element.54), channel_id=1, source_target_pairs={{0,16},{2,18},{4,20},{6,22},{8,24},{10,26},{12,28},{14,30},{16,0},... | collective-permute-start | bytes 442376 | tf_op jit(solution)/shard_map/ppermute | solution.py:33
  58.4 5.9 %copy-start.16 = (bf16[4,1,24,768]{3,2,1,0:T(8,128)(2,1)S(1)}, bf16[4,1,24,768]{3,2,1,0:T(8,128)(2,1)}, u32[]{:S(2)}) copy-start(bf16[4,1,24,768]{3,2,1,0:T(8,128)(2,1)} %get-tuple-element.61) | copy-start | bytes 442372
  58.4 5.9 %collective-permute-start.14 = (bf16[4,24,768]{2,1,0:T(8,128)(2,1)}, bf16[4,24,768]{2,1,0:T(8,128)(2,1)S(1)}, u32[]{:S(2)}, u32[]{:S(2)}) collective-permute-start(bf16[4,24,768]{2,1,0:T(8,128)(2,1)} %get-tuple-element.63), channel_id=1, source_target_pairs={{0,2},{2,0},{4,6},{6,4},{8,10},{10,8},{12,14},{14,12},{16,18},{18,... | collective-permute-start | bytes 442376 | tf_op jit(solution)/shard_map/ppermute | solution.py:33
  61.5 6.8 %collective-permute-start.13 = (bf16[4,2,24,768]{3,2,0,1:T(8,128)(2,1)S(1)}, bf16[4,2,24,768]{3,2,0,1:T(8,128)(2,1)S(1)}, u32[]{:S(2)}, u32[]{:S(2)}) collective-permute-start(bf16[4,2,24,768]{3,2,0,1:T(8,128)(2,1)S(1)} %reverse_select_fusion.3), channel_id=1, source_target_pairs={{0,2},{2,0},{4,6},{6,4},{8,10},{10,8},{12,14},{14,12},{16,18},{18,... | collective-permute-start | bytes 884744 | tf_op jit(solution)/shard_map/ppermute | solution.py:33
  66.3 6.7 %collective-permute-start.16 = (bf16[4,2,24,768]{3,2,1,0:T(8,128)(2,1)S(1)}, bf16[4,2,24,768]{3,2,1,0:T(8,128)(2,1)S(1)}, u32[]{:S(2)}, u32[]{:S(2)}) collective-permute-start(bf16[4,2,24,768]{3,2,1,0:T(8,128)(2,1)S(1)} %reverse_select_fusion.2), channel_id=1, source_target_pairs={{0,4},{2,6},{4,0},{6,2},{8,12},{10,14},{12,8},{14,10},{16,20},{18,... | collective-permute-start | bytes 884744 | tf_op jit(solution)/shard_map/ppermute | solution.py:33
  73.0 1.3 copy-start
  74.3 1.2 copy-start.17
  74.3 1.8 %copy-start.5 = (bf16[768,768]{1,0:T(8,128)(2,1)S(1)}, bf16[768,768]{1,0:T(8,128)(2,1)}, u32[]{:S(2)}) copy-start(bf16[768,768]{1,0:T(8,128)(2,1)} %constant.107.clone.table_ref) | copy-start | bytes 3538948
  75.5 10.0 %collective-permute-start.18 = (bf16[768,768]{1,0:T(8,128)(2,1)S(1)}, bf16[768,768]{1,0:T(8,128)(2,1)S(1)}, u32[]{:S(2)}, u32[]{:S(2)}) collective-permute-start(bf16[768,768]{1,0:T(8,128)(2,1)S(1)} %get-tuple-element.42.shaped_ref), channel_id=1, source_target_pairs={{0,1},{1,0},{2,3},{3,2},{4,5},{5,4},{6,7},{7,6},{8,9},{9,8},{10,11... | collective-permute-start | bytes 3538952 | tf_op jit(solution)/shard_map/ppermute | solution.py:338
  75.5 10.0 %copy-start.4 = (bf16[768,768]{1,0:T(8,128)(2,1)S(1)}, bf16[768,768]{1,0:T(8,128)(2,1)}, u32[]{:S(2)}) copy-start(bf16[768,768]{1,0:T(8,128)(2,1)} %constant.108.clone.table_ref) | copy-start | bytes 3538948
  75.5 9.3 %collective-permute-start.19 = (bf16[2,2,24,768]{3,2,1,0:T(8,128)(2,1)S(1)}, bf16[2,2,24,768]{3,2,1,0:T(8,128)(2,1)S(1)}, u32[]{:S(2)}, u32[]{:S(2)}) collective-permute-start(bf16[2,2,24,768]{3,2,1,0:T(8,128)(2,1)S(1)} %copy-done.17), channel_id=1, source_target_pairs={{0,16},{2,18},{4,20},{6,22},{8,24},{10,26},{12,28},{14,30},{16,0},... | collective-permute-start | bytes 442376 | tf_op jit(solution)/shard_map/ppermute | solution.py:33
  84.8 0.7 copy-start.8
  87.6 38.7 %all-to-all-start = ((bf16[8,2,48,768]{3,2,1,0:T(8,128)(2,1)}), bf16[8,2,48,768]{3,2,1,0:T(8,128)(2,1)}, u32[]{:S(2)}, u32[]{:S(2)}) async-start(bf16[8,2,48,768]{3,2,1,0:T(8,128)(2,1)} %bitcast.28.refs_0_), calls=%async_computation | async-start | bytes 2359296 | tf_op jit(solution)/shard_map/all_to_all | solution.py:357
  92.8 22.1 %collective-permute-start.20 = (bf16[2,6,24,768]{3,2,1,0:T(8,128)(2,1)}, bf16[2,6,24,768]{3,2,1,0:T(8,128)(2,1)S(1)}, u32[]{:S(2)}, u32[]{:S(2)}) collective-permute-start(bf16[2,6,24,768]{3,2,1,0:T(8,128)(2,1)} %slice.47), channel_id=1, source_target_pairs={{0,16},{2,18},{4,20},{6,22},{8,24},{10,26},{12,28},{14,30},{16,0},... | collective-permute-start | bytes 1327112 | tf_op jit(solution)/shard_map/ppermute | solution.py:33
  114.9 0.9 copy-start.9
  121.1 0.9 copy-start.10
  126.3 1.1 copy-start.11
  127.4 1.3 copy-start.13

commit v5 on v2

--- a/solution.py
+++ b/solution.py
@@ -64,13 +64,23 @@
     return back_re * fore_re + back_im * fore_im, back_re * fore_im - back_im * fore_re
 
 
-def products_kernel(rows, fore_ref, back_ref, send_a, keep_a, send_b, keep_b):
+def products_kernel(rows, fore_hbm, back_hbm, send_a, keep_a, send_b, keep_b, fore_ref, back_ref, sems):
     me = lax.axis_index("modes")
     low, high = me % 2 == 1, me // 2 % 2 == 1
     grid_size = fore_ref.shape[1] // 2
     half = grid_size // 2
     pair = 2 * rows
-    for group in range(fore_ref.shape[0] // (4 * rows)):
+    groups = fore_ref.shape[0] // (4 * rows)
+    copies = []
+    for group in range(groups):
+        at = pl.ds(group * 4 * rows, 4 * rows)
+        for k, (hbm, ref) in enumerate(((fore_hbm, fore_ref), (back_hbm, back_ref))):
+            copies.append(pltpu.make_async_copy(hbm.at[at], ref.at[at], sems.at[2 * group + k]))
+    for copy in copies:
+        copy.start()
+    for group in range(groups):
+        copies[2 * group].wait()
+        copies[2 * group + 1].wait()
         at = pl.ds(group * 4 * rows, 4 * rows)
         out = pl.ds(group * pair, pair)
         for part in range(2):
@@ -91,66 +101,94 @@
                     keep_b[out, into] = jnp.where(high, second, first)
 
 
-def columns_kernel(own_ref, other_ref, re_ref, im_ref, out_ref):
-    half = own_ref.shape[1] // 2
-    rows = own_ref.shape[0]
-
-    def times(table, values):
-        return jnp.dot(table, values, preferred_element_type=f32)
-
-    def both(table, part):
-        cols = pl.ds(part * half, half)
-        return times(table[:, :rows], own_ref[:, cols]) + times(table[:, rows:], other_ref[:, cols])
-
+def times(one, two):
+    return jnp.dot(one, two, preferred_element_type=f32)
+
+
+def own_kernel(table_ref, shaped_ref, out_ref):
+    out_ref[...] = times(table_ref[...], shaped_ref[...])
+
+
+def other_kernel(table_ref, shaped_ref, own_ref, out_ref):
+    out_ref[...] = (own_ref[...] + times(table_ref[...], shaped_ref[...])).astype(bf16)
+
+
+def fields_kernel(block_rows, columns_ref, re_ref, im_ref, out_ref):
+    rows, grid_size = out_ref.shape[0], columns_ref.shape[1]
+    by_re, by_im = times(columns_ref[...], re_ref[...]), times(columns_ref[...], im_ref[...])
+    if block_rows % 8 == 0:
+        step, block = 2 * block_rows, block_rows
+    else:
+        step, block = rows, rows
+    for at in range(0, rows, step):
+        pieces = [[], []]
+        for start in range(2 * at, 2 * (at + step), 2 * block):
+            real, imag = slice(start, start + block), slice(start + block, start + 2 * block)
+            pieces[0].append(by_re[real] - by_im[imag])
+            pieces[1].append(by_im[real] + by_re[imag])
+        for k, piece in enumerate(pieces):
+            out = jnp.concatenate(piece, 0).astype(bf16)
+            out_ref[pl.ds(at, step), pl.ds(k * grid_size, grid_size)] = out
+
+
+def targets_kernel(targets_ref, re_ref, im_ref, out_ref):
+    rows = targets_ref.shape[0] // 2
+    real, imag = targets_ref[:rows], targets_ref[rows:]
     c_re, c_im = re_ref[...], im_ref[...]
-    out_ref[:, :half] = (both(c_re, 0) - both(c_im, 1)).astype(bf16)
-    out_ref[:, half:] = (both(c_im, 0) + both(c_re, 1)).astype(bf16)
-
-
-def coupling_kernel(mode_rows, fields_ref, targets_ref, out_ref):
+    out_ref[:rows] = (times(real, c_re) + times(imag, c_im)).astype(bf16)
+    out_ref[rows:] = (times(imag, c_re) - times(real, c_im)).astype(bf16)
+
+
+def exactly(one, two, dims):
+    return lax.dot_general(
+        one, two, (dims, ((), ())), precision=lax.Precision.HIGHEST, preferred_element_type=f32
+    )
+
+
+def coupling_kernel(block_rows, fields_ref, targets_ref, out_ref):
+    modes = out_ref.shape[1]
     product = lax.dot_general(
         fields_ref[...], targets_ref[...], (((1,), (1,)), ((), ())), preferred_element_type=f32
     )
     left, right = product.shape
-    row = lax.broadcasted_iota(jnp.int32, (left, right), 0) % mode_rows
-    col = lax.broadcasted_iota(jnp.int32, (left, right), 1) % mode_rows
+    row = lax.broadcasted_iota(jnp.int32, (left, right), 0) % block_rows
+    col = lax.broadcasted_iota(jnp.int32, (left, right), 1) % block_rows
     product = jnp.where(row == col, product, 0.0)
 
     def groups(size):
-        member = lax.broadcasted_iota(jnp.int32, (size // mode_rows, size), 1) // mode_rows
-        group = lax.broadcasted_iota(jnp.int32, (size // mode_rows, size), 0)
+        member = lax.broadcasted_iota(jnp.int32, (size // block_rows, size), 1) // block_rows
+        group = lax.broadcasted_iota(jnp.int32, (size // block_rows, size), 0)
         return jnp.where(member == group, 1.0, 0.0).astype(f32)
 
-    narrow = lax.dot_general(
-        groups(left),
-        product,
-        (((1,), (0,)), ((), ())),
-        precision=lax.Precision.HIGHEST,
-        preferred_element_type=f32,
-    )
-    out_ref[...] = lax.dot_general(
-        narrow,
-        groups(right),
-        (((1,), (1,)), ((), ())),
-        precision=lax.Precision.HIGHEST,
-        preferred_element_type=f32,
-    )
-
-
-def kernel_call(kernel, shape, dtype, flops, operands):
+    if block_rows % 8 == 0:
+        product = jnp.sum(product.reshape(left // block_rows, block_rows, right), 1)
+    else:
+        product = exactly(groups(left), product, ((1,), (0,)))
+    product = exactly(product, groups(right), ((1,), (1,)))
+    by_re, by_im = product[:, :modes], product[:, modes:]
+    mode = lax.broadcasted_iota(jnp.int32, (modes, 2 * modes), 0)
+    from_row = lax.broadcasted_iota(jnp.int32, (modes, 2 * modes), 1)
+    real = jnp.where(from_row == 2 * mode, 1.0, 0.0).astype(f32)
+    imag = jnp.where(from_row == 2 * mode + 1, 1.0, 0.0).astype(f32)
+    inner = ((1,), (0,))
+    out_ref[:modes] = exactly(real, by_re, inner) + exactly(imag, by_im, inner)
+    out_ref[modes:] = exactly(imag, by_re, inner) - exactly(real, by_im, inner)
+
+
+def kernel_call(kernel, shape, dtype, flops, operands, grant=12, **more):
     place = pl.BlockSpec(memory_space=pltpu.VMEM)
     several = isinstance(dtype, list)
     if several:
         out_shape = [jax.ShapeDtypeStruct(s, d) for s, d in zip(shape, dtype)]
     else:
         out_shape = jax.ShapeDtypeStruct(shape, dtype)
+    specs = dict(in_specs=[place] * len(operands), out_specs=[place] * len(shape) if several else place)
     return pl.pallas_call(
         kernel,
         out_shape=out_shape,
-        in_specs=[place] * len(operands),
-        out_specs=[place] * len(shape) if several else place,
-        compiler_params=pltpu.CompilerParams(vmem_limit_bytes=32 * 1024 * 1024),
+        compiler_params=pltpu.CompilerParams(vmem_limit_bytes=grant << 20),
         cost_estimate=pl.CostEstimate(flops=flops, bytes_accessed=4 << 20, transcendentals=0),
+        **(specs | more),
     )(*operands)
 
 
@@ -163,6 +201,7 @@
     digits = stages(count)
     sizes = [size for _, size in reversed(digits)]
     half = grid_size // 2
+    matmul = 2 * local_rows * double_width * double_width
 
     me = lax.axis_index("modes")
     owns = [me // stride % size for stride, size in digits]
@@ -177,6 +216,9 @@
             [bf16, f32, bf16, f32],
             8 * local_rows * double_width,
             (forward[0], backward[0]),
+            in_specs=[pl.BlockSpec(memory_space=pltpu.HBM)] * 2,
+            scratch_shapes=[pltpu.VMEM((local_rows, double_width), bf16)] * 2
+            + [pltpu.SemaphoreType.DMA((2 * local_rows // (4 * block_rows),))],
         )
     else:
         product = product_of(forward[0], backward[0])
@@ -202,11 +244,14 @@
     stride, size = digits[last]
     send, keep = split_digit(jnp.concatenate(kept, -1), owns[last], size, 0)
     got = [exchange(v, (e + 1) * stride, count) for e, v in enumerate(send)]
-    summed = reduce_digit(keep, got).reshape(block_rows, 2, 2, half)
-    over_re, over_im = summed[:, :, 0], summed[:, :, 1]
-    scale = lax.rsqrt(over_re * over_re + over_im * over_im + mode_total)
-    block = jnp.stack([over_re * scale, over_im * scale], 2).astype(bf16)
-    block = block.reshape(block_rows, double_width)
+    summed = reduce_digit(keep, got)
+    parts = []
+    for part in range(2):
+        over_re = summed[:, part * grid_size : part * grid_size + half]
+        over_im = summed[:, part * grid_size + half : (part + 1) * grid_size]
+        scale = lax.rsqrt(over_re * over_re + over_im * over_im + mode_total)
+        parts += [over_re * scale, over_im * scale]
+    block = jnp.concatenate(parts, -1).astype(bf16)
 
     block = gather_digit(block, owns[last], stride, size, 0, count)
     planes = []
@@ -226,42 +271,51 @@
     fore_re, fore_im = fore[:, :grid_size], fore[:, grid_size:]
     plane_re, plane_im = plane_re.astype(f32), plane_im.astype(f32)
     shaped = jnp.concatenate(
-        [fore_re * plane_re - fore_im * plane_im, fore_re * plane_im + fore_im * plane_re], -1
+        [fore_re * plane_re - fore_im * plane_im, fore_re * plane_im + fore_im * plane_re], 0
     ).astype(bf16)
     other = lax.ppermute(shaped, "rows", [(0, 1), (1, 0)])
 
     c_re, c_im = propagator(grid_size)
-    own_re = jnp.asarray(c_re[:local_rows], bf16)
-    own_im = jnp.asarray(c_im[:local_rows], bf16)
+    full_re, full_im = jnp.asarray(c_re, bf16), jnp.asarray(c_im, bf16)
+    owners = count if block_rows % 8 == 0 else 1
+    order = np.arange(local_rows).reshape(owners, -1)
+
+    def table(cols):
+        real, imag = c_re[:local_rows, cols], c_im[:local_rows, cols]
+        rows = np.stack([np.concatenate([real, -imag], 1)[order], np.concatenate([imag, real], 1)[order]], 1)
+        return jnp.asarray(rows.reshape(2 * local_rows, -1), bf16)
+
+    column_shape = (2 * local_rows, grid_size)
     columns = kernel_call(
-        columns_kernel,
+        own_kernel, column_shape, f32, matmul // 2, (table(slice(0, local_rows)), shaped)
+    )
+    columns, other = lax.optimization_barrier((columns, other))
+    columns = kernel_call(
+        other_kernel, column_shape, bf16, matmul // 2, (table(slice(local_rows, None)), other, columns)
+    )
+    blocks = columns.reshape(owners, 2, -1, block_rows, grid_size).transpose(0, 2, 1, 3, 4)
+    blocks = blocks.reshape(count, 2 * block_rows, grid_size)
+    pixels = lax.all_to_all(blocks, "modes", 0, 0, tiled=True).reshape(column_shape)
+
+    seen = kernel_call(
+        targets_kernel, column_shape, bf16, matmul, (targets.reshape(column_shape), full_re, full_im)
+    )
+    output_fields = kernel_call(
+        lambda *refs: fields_kernel(block_rows, *refs),
         (local_rows, double_width),
         bf16,
-        2 * local_rows * double_width * double_width,
-        (shaped, other, own_re, own_im),
-    )
-
-    back_table = jnp.asarray(np.block([[c_re, -c_im], [c_im, c_re]]), bf16)
-    rows_table = jnp.asarray(np.block([[c_re, c_im], [-c_im, c_re]]), bf16)
-    flat = jnp.concatenate([targets[0], targets[1]], -1).reshape(-1, double_width)
-    seen = jnp.dot(flat, back_table, preferred_element_type=f32).astype(bf16)
-    turned = jnp.concatenate([-seen[:, grid_size:], seen[:, :grid_size]], -1)
-    target_pair = jnp.concatenate([seen, turned], 0)
-
-    pixels = lax.all_to_all(
-        columns.reshape(count, block_rows, double_width), "modes", 0, 0, tiled=True
-    )
-    output_fields = jnp.dot(columns, rows_table, preferred_element_type=f32).astype(bf16)
-    pixels, output_fields = lax.optimization_barrier((pixels, output_fields))
+        matmul,
+        (columns, full_re, full_im),
+    )
+    pixels, output_fields, seen = lax.optimization_barrier((pixels, output_fields, seen))
 
     term = kernel_call(
         lambda *refs: coupling_kernel(block_rows, *refs),
-        (mode_total, 2 * mode_total),
+        (2 * mode_total, mode_total),
         f32,
-        4 * local_rows * local_rows * double_width,
-        (pixels.reshape(local_rows, double_width), target_pair),
-    )
-    term = jnp.concatenate([term[:, :mode_total], term[:, mode_total:]], 0)
+        matmul,
+        (pixels, seen),
+    )
     pieces = lax.all_to_all(term, ("modes", "rows"), 0, 0, tiled=True)
     coupling = jnp.sum(pieces, 0, keepdims=True)
     return (phase_plane, output_fields[None], coupling)

time: 110 us -> 112 us (1.018)
  matrix products: 8.24 us -> 0 us
  Pallas kernels: 6.23 us -> 13 us
  local copies, waits for them, and re-layouts: 4.05 us -> 8.13 us
  other arithmetic: 5.51 us -> 3.38 us
  waiting for transfers between devices: 52.2 us -> 53.8 us
    dot_general x3 -> x0, matrix products: 8.24 us -> none  [the longest x1 4.28 us: local(): jnp.dot(columns, rows_table, preferred_element_type=f32).astype(bf16)]
    pallas_call x3 -> x6, Pallas kernels: 6.23 us -> 13 us  [kernel_call(): pl.pallas_call(kernel, out_shape=out_shape, compiler_params=pltpu.Compile...]
    unnamed x26 -> x38, local copies, waits for them, and re-layouts: 3.15 us -> 7.8 us
    ppermute x14, waiting for transfers between devices: 26.2 us -> 28.7 us  [exchange(): lax.ppermute(values, 'modes', [(i, i ^ offset) for i in range(count)])]
    ppermute x1, waiting for transfers between devices: 2.83 us -> 0.65 us  [local(): other = lax.ppermute(shaped, 'rows', [(0, 1), (1, 0)])]
    concatenate x1, other arithmetic: 2.34 us -> 1.11 us  [local(): phase_plane = jnp.concatenate([plane_re, plane_im], -1)]
    all_to_all x1, waiting for transfers between devices: 4.81 us -> 6 us  [local(): pieces = lax.all_to_all(term, ('modes', 'rows'), 0, 0, tiled=True)]
  transfers between devices with their start and end apart: 17 -> 17, of which waited for: 13 -> 13; matrix products, arithmetic and copies ran while one was open for 11% -> 2% of each run, Pallas kernels for 0% -> 7%
where the time goes in v5:
time: 112 us
  waiting for transfers between devices  53.8 us (48%)
  starting transfers between devices  32.5 us (29%)
  Pallas kernels  13 us (12%)
  local copies, waits for them, and re-layouts  8.13 us (7%)
  other arithmetic  3.38 us (3%)
    ppermute x14, waiting for transfers between devices, exchange(): lax.ppermute(values, 'modes', [(i, i ^ offset) for i in range(count)])  28.7 us
    ppermute x14, starting transfers between devices, exchange(): lax.ppermute(values, 'modes', [(i, i ^ offset) for i in range(count)])  21.7 us
    all_to_all x1, waiting for transfers between devices, local(): lax.all_to_all(blocks, 'modes', 0, 0, tiled=True).reshape(column_shape)  18.5 us
    pallas_call x6, Pallas kernels, kernel_call(): pl.pallas_call(kernel, out_shape=out_shape, compiler_params=pltpu.Compile...  13 us
    unnamed x38, local copies, waits for them, and re-layouts  7.8 us
    all_to_all x1, waiting for transfers between devices, local(): pieces = lax.all_to_all(term, ('modes', 'rows'), 0, 0, tiled=True)  6 us
    all_to_all x1, starting transfers between devices, local(): pieces = lax.all_to_all(term, ('modes', 'rows'), 0, 0, tiled=True)  5.76 us
    all_to_all x1, starting transfers between devices, local(): lax.all_to_all(blocks, 'modes', 0, 0, tiled=True).reshape(column_shape)  5.03 us
  transfers between devices with their start and end apart: 17, of which 13 were waited for; matrix products, arithmetic and copies ran while one was open for 2% of the time, Pallas kernels for 7%

profile of v5, /device:TPU:0, one launch (start us, length us, event | category | flops | bytes accessed | tf_op | source)
XLA Modules:
  0.0 111.9 jit_solution(776552379814439162)
XLA Ops:
  0.6 1.3 %copy-done = bf16[1,384,1536]{2,1,0:T(8,128)(2,1)S(1)} copy-done((bf16[1,384,1536]{2,1,0:T(8,128)(2,1)S(1)}, bf16[1,384,1536]{2,1,0:T(8,128)(2,1)}, u32[]{:S(2)}) %copy-start) | copy-done | bytes 1179672
  1.9 1.3 %copy-done.2 = bf16[1,384,1536]{2,1,0:T(8,128)(2,1)S(1)} copy-done((bf16[1,384,1536]{2,1,0:T(8,128)(2,1)S(1)}, bf16[1,384,1536]{2,1,0:T(8,128)(2,1)}, u32[]{:S(2)}) %copy-start.2) | copy-done | bytes 1179672
  3.2 1.2 %shard_map.94 = (bf16[192,768]{1,0:T(8,128)(2,1)S(1)}, f32[192,768]{1,0:T(8,128)S(1)}, bf16[192,768]{1,0:T(8,128)(2,1)S(1)}, f32[192,768]{1,0:T(8,128)S(1)}) custom-call(bf16[384,1536]{1,0:T(8,128)(2,1)S(1)} %bitcast.62, bf16[384,1536]{1,0:T(8,128)(2,1)S(1)} %bitcast.63), custom_call_target="tpu_custom_call" | custom-call | flops 4718592 | bytes 4194304 | tf_op jit(solution)/shard_map/pallas_call | solution.py:186
  4.4 3.0 %collective-permute-start.2 = (bf16[4,2,24,768]{3,2,0,1:T(8,128)(2,1)S(1)}, bf16[4,2,24,768]{3,2,0,1:T(8,128)(2,1)S(1)}, u32[]{:S(2)}, u32[]{:S(2)}) collective-permute-start(bf16[4,2,24,768]{3,2,0,1:T(8,128)(2,1)S(1)} %copy.19), channel_id=1, source_target_pairs={{0,4},{2,6},{4,0},{6,2},{8,12},{10,14},{12,8},{14,10},{16,20},{18,... | collective-permute-start | bytes 884744 | tf_op jit(solution)/shard_map/ppermute | solution.py:33
  7.4 1.6 %collective-permute-start = (bf16[4,2,24,768]{3,2,0,1:T(8,128)(2,1)S(1)}, bf16[4,2,24,768]{3,2,0,1:T(8,128)(2,1)S(1)}, u32[]{:S(2)}, u32[]{:S(2)}) collective-permute-start(bf16[4,2,24,768]{3,2,0,1:T(8,128)(2,1)S(1)} %copy.17), channel_id=1, source_target_pairs={{0,2},{2,0},{4,6},{6,4},{8,10},{10,8},{12,14},{14,12},{16,18},{18,... | collective-permute-start | bytes 884744 | tf_op jit(solution)/shard_map/ppermute | solution.py:33
  9.0 5.4 %collective-permute-done.2 = bf16[4,2,24,768]{3,2,0,1:T(8,128)(2,1)S(1)} collective-permute-done((bf16[4,2,24,768]{3,2,0,1:T(8,128)(2,1)S(1)}, bf16[4,2,24,768]{3,2,0,1:T(8,128)(2,1)S(1)}, u32[]{:S(2)}, u32[]{:S(2)}) %collective-permute-start.2) | collective-permute-done | bytes 294944 | tf_op jit(solution)/shard_map/ppermute | solution.py:33
  14.5 1.8 %collective-permute-start.3 = (bf16[4,24,768]{2,1,0:T(8,128)(2,1)S(1)}, bf16[4,24,768]{2,1,0:T(8,128)(2,1)S(1)}, u32[]{:S(2)}, u32[]{:S(2)}) collective-permute-start(bf16[4,24,768]{2,1,0:T(8,128)(2,1)S(1)} %fusion.5), channel_id=1, source_target_pairs={{0,2},{2,0},{4,6},{6,4},{8,10},{10,8},{12,14},{14,12},{16,18},{18,... | collective-permute-start | bytes 442376 | tf_op jit(solution)/shard_map/ppermute | solution.py:33
  16.4 1.6 %collective-permute-start.1 = (bf16[4,24,768]{2,1,0:T(8,128)(2,1)S(1)}, bf16[4,24,768]{2,1,0:T(8,128)(2,1)S(1)}, u32[]{:S(2)}, u32[]{:S(2)}) collective-permute-start(bf16[4,24,768]{2,1,0:T(8,128)(2,1)S(1)} %fusion.4), channel_id=1, source_target_pairs={{0,4},{2,6},{4,0},{6,2},{8,12},{10,14},{12,8},{14,10},{16,20},{18,... | collective-permute-start | bytes 442376 | tf_op jit(solution)/shard_map/ppermute | solution.py:33
  18.0 1.8 %collective-permute-done.3 = bf16[4,24,768]{2,1,0:T(8,128)(2,1)S(1)} collective-permute-done((bf16[4,24,768]{2,1,0:T(8,128)(2,1)S(1)}, bf16[4,24,768]{2,1,0:T(8,128)(2,1)S(1)}, u32[]{:S(2)}, u32[]{:S(2)}) %collective-permute-start.3) | collective-permute-done | bytes 147488 | tf_op jit(solution)/shard_map/ppermute | solution.py:33
  19.7 1.8 %collective-permute-done.1 = bf16[4,24,768]{2,1,0:T(8,128)(2,1)S(1)} collective-permute-done((bf16[4,24,768]{2,1,0:T(8,128)(2,1)S(1)}, bf16[4,24,768]{2,1,0:T(8,128)(2,1)S(1)}, u32[]{:S(2)}, u32[]{:S(2)}) %collective-permute-start.1) | collective-permute-done | bytes 147488 | tf_op jit(solution)/shard_map/ppermute | solution.py:33
  21.7 1.6 %collective-permute-start.4 = (bf16[24,1536]{1,0:T(8,128)(2,1)S(1)}, bf16[24,1536]{1,0:T(8,128)(2,1)S(1)}, u32[]{:S(2)}, u32[]{:S(2)}) collective-permute-start(bf16[24,1536]{1,0:T(8,128)(2,1)S(1)} %get-tuple-element.27), channel_id=1, source_target_pairs={{0,8},{2,10},{4,12},{6,14},{8,0},{10,2},{12,4},{14,6},{16,24},{18,... | collective-permute-start | bytes 221192 | tf_op jit(solution)/shard_map/ppermute | solution.py:33
  23.3 2.6 %collective-permute-start.5 = (bf16[24,1536]{1,0:T(8,128)(2,1)S(1)}, bf16[24,1536]{1,0:T(8,128)(2,1)S(1)}, u32[]{:S(2)}, u32[]{:S(2)}) collective-permute-start(bf16[24,1536]{1,0:T(8,128)(2,1)S(1)} %get-tuple-element.28), channel_id=1, source_target_pairs={{0,16},{2,18},{4,20},{6,22},{8,24},{10,26},{12,28},{14,30},{16,0},... | collective-permute-start | bytes 221192 | tf_op jit(solution)/shard_map/ppermute | solution.py:33
  25.9 0.2 collective-permute-start.6
  26.1 3.9 %collective-permute-done.5 = bf16[24,1536]{1,0:T(8,128)(2,1)S(1)} collective-permute-done((bf16[24,1536]{1,0:T(8,128)(2,1)S(1)}, bf16[24,1536]{1,0:T(8,128)(2,1)S(1)}, u32[]{:S(2)}, u32[]{:S(2)}) %collective-permute-start.5) | collective-permute-done | bytes 73760 | tf_op jit(solution)/shard_map/ppermute | solution.py:33
  30.0 2.8 %collective-permute-done.6 = bf16[24,1536]{1,0:T(8,128)(2,1)S(1)} collective-permute-done((bf16[24,1536]{1,0:T(8,128)(2,1)S(1)}, bf16[24,1536]{1,0:T(8,128)(2,1)S(1)}, u32[]{:S(2)}, u32[]{:S(2)}) %collective-permute-start.6) | collective-permute-done | bytes 73760 | tf_op jit(solution)/shard_map/ppermute | solution.py:33
  33.0 0.7 collective-permute-start.8
  33.7 3.7 %collective-permute-start.9 = (bf16[24,1536]{1,0:T(8,128)(2,1)S(1)}, bf16[24,1536]{1,0:T(8,128)(2,1)S(1)}, u32[]{:S(2)}, u32[]{:S(2)}) collective-permute-start(bf16[24,1536]{1,0:T(8,128)(2,1)S(1)} %pad_maximum_fusion.10), channel_id=1, source_target_pairs={{0,24},{2,26},{4,28},{6,30},{8,16},{10,18},{12,20},{14,22},{16,8},... | collective-permute-start | bytes 221192 | tf_op jit(solution)/shard_map/ppermute | solution.py:33
  37.4 0.9 collective-permute-done.8
  38.3 2.3 %collective-permute-done.9 = bf16[24,1536]{1,0:T(8,128)(2,1)S(1)} collective-permute-done((bf16[24,1536]{1,0:T(8,128)(2,1)S(1)}, bf16[24,1536]{1,0:T(8,128)(2,1)S(1)}, u32[]{:S(2)}, u32[]{:S(2)}) %collective-permute-start.9) | collective-permute-done | bytes 73760 | tf_op jit(solution)/shard_map/ppermute | solution.py:33
  40.8 1.2 %collective-permute-start.12 = (bf16[4,24,768]{2,1,0:T(8,128)(2,1)S(1)}, bf16[4,24,768]{2,1,0:T(8,128)(2,1)S(1)}, u32[]{:S(2)}, u32[]{:S(2)}) collective-permute-start(bf16[4,24,768]{2,1,0:T(8,128)(2,1)S(1)} %get-tuple-element.32), channel_id=1, source_target_pairs={{0,2},{2,0},{4,6},{6,4},{8,10},{10,8},{12,14},{14,12},{16,18},{18,... | collective-permute-start | bytes 442376 | tf_op jit(solution)/shard_map/ppermute | solution.py:33
  42.0 0.3 bitcast_convert_fusion
  42.3 1.5 %collective-permute-start.10 = (bf16[4,24,768]{2,1,0:T(8,128)(2,1)S(1)}, bf16[4,24,768]{2,1,0:T(8,128)(2,1)S(1)}, u32[]{:S(2)}, u32[]{:S(2)}) collective-permute-start(bf16[4,24,768]{2,1,0:T(8,128)(2,1)S(1)} %get-tuple-element.33), channel_id=1, source_target_pairs={{0,4},{2,6},{4,0},{6,2},{8,12},{10,14},{12,8},{14,10},{16,20},{18,... | collective-permute-start | bytes 442376 | tf_op jit(solution)/shard_map/ppermute | solution.py:33
  43.8 3.8 %collective-permute-done.12 = bf16[4,24,768]{2,1,0:T(8,128)(2,1)S(1)} collective-permute-done((bf16[4,24,768]{2,1,0:T(8,128)(2,1)S(1)}, bf16[4,24,768]{2,1,0:T(8,128)(2,1)S(1)}, u32[]{:S(2)}, u32[]{:S(2)}) %collective-permute-start.12) | collective-permute-done | bytes 147488 | tf_op jit(solution)/shard_map/ppermute | solution.py:33
  47.7 1.5 %collective-permute-start.13 = (bf16[4,2,24,768]{3,2,0,1:T(8,128)(2,1)S(1)}, bf16[4,2,24,768]{3,2,0,1:T(8,128)(2,1)S(1)}, u32[]{:S(2)}, u32[]{:S(2)}) collective-permute-start(bf16[4,2,24,768]{3,2,0,1:T(8,128)(2,1)S(1)} %reverse_select_fusion.2), channel_id=1, source_target_pairs={{0,4},{2,6},{4,0},{6,2},{8,12},{10,14},{12,8},{14,10},{16,20},{18,... | collective-permute-start | bytes 884744 | tf_op jit(solution)/shard_map/ppermute | solution.py:33
  49.4 0.6 collective-permute-start.11
  50.0 4.4 %collective-permute-done.13 = bf16[4,2,24,768]{3,2,0,1:T(8,128)(2,1)S(1)} collective-permute-done((bf16[4,2,24,768]{3,2,0,1:T(8,128)(2,1)S(1)}, bf16[4,2,24,768]{3,2,0,1:T(8,128)(2,1)S(1)}, u32[]{:S(2)}, u32[]{:S(2)}) %collective-permute-start.13) | collective-permute-done | bytes 294944 | tf_op jit(solution)/shard_map/ppermute | solution.py:33
  54.7 1.5 %collective-permute-done.11 = bf16[4,2,24,768]{3,2,1,0:T(8,128)(2,1)S(1)} collective-permute-done((bf16[4,2,24,768]{3,2,1,0:T(8,128)(2,1)S(1)}, bf16[4,2,24,768]{3,2,1,0:T(8,128)(2,1)S(1)}, u32[]{:S(2)}, u32[]{:S(2)}) %collective-permute-start.11) | collective-permute-done | bytes 294944 | tf_op jit(solution)/shard_map/ppermute | solution.py:33
  56.3 0.1 fusion.20
  56.5 0.4 fusion.1
  56.9 0.2 copy-done.11
  57.3 0.1 copy-done.15
  57.4 0.1 copy-done.17
  57.6 1.1 copy-done.4
  58.7 1.1 shard_map.95.own_ref
  59.8 0.7 collective-permute-done.14.shaped_ref
  60.5 2.1 %shard_map.96.refs_0_ = bf16[768,768]{1,0:T(8,128)(2,1)} custom-call(bf16[768,768]{1,0:T(8,128)(2,1)S(1)} %copy-done.3, bf16[768,768]{1,0:T(8,128)(2,1)S(1)} %collective-permute-done.14.shaped_ref, f32[768,768]{1,0:T(8,128)S(1)} %shard_map.95.own_ref), custom_call_target="tpu_custom_call" | custom-call | flops 905969664 | bytes 4194304 | tf_op jit(solution)/shard_map/pallas_call | solution.py:186
  62.6 5.0 %all-to-all-start = ((bf16[16,48,768]{2,1,0:T(8,128)(2,1)}), bf16[16,48,768]{2,1,0:T(8,128)(2,1)S(1)}, u32[]{:S(2)}, u32[]{:S(2)}) async-start(bf16[16,48,768]{2,1,0:T(8,128)(2,1)} %bitcast.33), calls=%async_computation | async-start | bytes 2359296 | tf_op jit(solution)/shard_map/all_to_all | solution.py:298
  67.7 1.3 %copy-done.7 = bf16[768,768]{1,0:T(8,128)(2,1)S(1)} copy-done((bf16[768,768]{1,0:T(8,128)(2,1)S(1)}, bf16[768,768]{1,0:T(8,128)(2,1)}, u32[]{:S(2)}) %copy-start.7) | copy-done | bytes 1179672
  68.9 2.0 %shard_map.98.refs_1_ = bf16[768,768]{1,0:T(8,128)(2,1)S(1)} custom-call(bf16[768,768]{1,0:T(8,128)(2,1)S(1)} %bitcast.69, bf16[768,768]{1,0:T(8,128)(2,1)S(1)} %copy-done.6, bf16[768,768]{1,0:T(8,128)(2,1)S(1)} %copy-done.7), custom_call_target="tpu_custom_call" | custom-call | flops 1811939328 | bytes 4194304 | tf_op jit(solution)/shard_map/pallas_call | solution.py:186
  70.9 1.0 copy-done.9
  72.0 4.3 %shard_map.97 = bf16[384,1536]{1,0:T(8,128)(2,1)} custom-call(bf16[768,768]{1,0:T(8,128)(2,1)} %shard_map.96.refs_0_, bf16[768,768]{1,0:T(8,128)(2,1)S(1)} %copy-done.6, bf16[768,768]{1,0:T(8,128)(2,1)S(1)} %copy-done.8), custom_call_target="tpu_custom_call" | custom-call | flops 1811939328 | bytes 4194304 | tf_op jit(solution)/shard_map/pallas_call | solution.py:186
  76.2 18.5 %all-to-all-done = bf16[16,48,768]{2,1,0:T(8,128)(2,1)S(1)} async-done(((bf16[16,48,768]{2,1,0:T(8,128)(2,1)}), bf16[16,48,768]{2,1,0:T(8,128)(2,1)S(1)}, u32[]{:S(2)}, u32[]{:S(2)}) %all-to-all-start) | async-done | bytes 1179680 | tf_op jit(solution)/shard_map/all_to_all | solution.py:298
  94.7 1.3 %copy-done.10 = bf16[768,768]{1,0:T(8,128)(2,1)S(1)} copy-done((bf16[768,768]{1,0:T(8,128)(2,1)S(1)}, bf16[768,768]{1,0:T(8,128)(2,1)}, u32[]{:S(2)}) %copy-start.10) | copy-done | bytes 1179672
  96.0 2.4 %shard_map.99 = f32[32,16]{1,0:T(8,128)} custom-call(bf16[768,768]{1,0:T(8,128)(2,1)S(1)} %bitcast.64, bf16[768,768]{1,0:T(8,128)(2,1)S(1)} %copy-done.10), custom_call_target="tpu_custom_call" | custom-call | flops 1811939328 | bytes 4194304 | tf_op jit(solution)/shard_map/pallas_call | solution.py:186
  98.4 5.8 %all-to-all-start.1 = ((f32[32,1,16]{2,1,0:T(1,128)}), f32[32,1,16]{2,1,0:T(1,128)S(1)}, u32[]{:S(2)}, u32[]{:S(2)}) async-start(f32[32,1,16]{2,1,0:T(1,128)} %bitcast.38), calls=%async_computation.1 | async-start | bytes 32768 | tf_op jit(solution)/shard_map/all_to_all | solution.py:319
  104.2 1.1 pad_maximum_fusion
  105.3 6.0 %all-to-all-done.1 = f32[32,1,16]{2,1,0:T(1,128)S(1)} async-done(((f32[32,1,16]{2,1,0:T(1,128)}), f32[32,1,16]{2,1,0:T(1,128)S(1)}, u32[]{:S(2)}, u32[]{:S(2)}) %all-to-all-start.1) | async-done | bytes 2080 | tf_op jit(solution)/shard_map/all_to_all | solution.py:319
  111.3 0.6 reduce_sum.9
  (63 shorter events, 1.5 us)
Async XLA Ops:
  0.6 1.3 %copy-start = (bf16[1,384,1536]{2,1,0:T(8,128)(2,1)S(1)}, bf16[1,384,1536]{2,1,0:T(8,128)(2,1)}, u32[]{:S(2)}) copy-start(bf16[1,384,1536]{2,1,0:T(8,128)(2,1)} %param.7) | copy-start | bytes 3538948
  1.9 1.3 %copy-start.2 = (bf16[1,384,1536]{2,1,0:T(8,128)(2,1)S(1)}, bf16[1,384,1536]{2,1,0:T(8,128)(2,1)}, u32[]{:S(2)}) copy-start(bf16[1,384,1536]{2,1,0:T(8,128)(2,1)} %param.8) | copy-start | bytes 3538948
  4.4 10.0 %collective-permute-start.2 = (bf16[4,2,24,768]{3,2,0,1:T(8,128)(2,1)S(1)}, bf16[4,2,24,768]{3,2,0,1:T(8,128)(2,1)S(1)}, u32[]{:S(2)}, u32[]{:S(2)}) collective-permute-start(bf16[4,2,24,768]{3,2,0,1:T(8,128)(2,1)S(1)} %copy.19), channel_id=1, source_target_pairs={{0,4},{2,6},{4,0},{6,2},{8,12},{10,14},{12,8},{14,10},{16,20},{18,... | collective-permute-start | bytes 884744 | tf_op jit(solution)/shard_map/ppermute | solution.py:33
  7.4 8.9 %collective-permute-start = (bf16[4,2,24,768]{3,2,0,1:T(8,128)(2,1)S(1)}, bf16[4,2,24,768]{3,2,0,1:T(8,128)(2,1)S(1)}, u32[]{:S(2)}, u32[]{:S(2)}) collective-permute-start(bf16[4,2,24,768]{3,2,0,1:T(8,128)(2,1)S(1)} %copy.17), channel_id=1, source_target_pairs={{0,2},{2,0},{4,6},{6,4},{8,10},{10,8},{12,14},{14,12},{16,18},{18,... | collective-permute-start | bytes 884744 | tf_op jit(solution)/shard_map/ppermute | solution.py:33
  14.5 5.2 %collective-permute-start.3 = (bf16[4,24,768]{2,1,0:T(8,128)(2,1)S(1)}, bf16[4,24,768]{2,1,0:T(8,128)(2,1)S(1)}, u32[]{:S(2)}, u32[]{:S(2)}) collective-permute-start(bf16[4,24,768]{2,1,0:T(8,128)(2,1)S(1)} %fusion.5), channel_id=1, source_target_pairs={{0,2},{2,0},{4,6},{6,4},{8,10},{10,8},{12,14},{14,12},{16,18},{18,... | collective-permute-start | bytes 442376 | tf_op jit(solution)/shard_map/ppermute | solution.py:33
  16.4 5.2 %collective-permute-start.1 = (bf16[4,24,768]{2,1,0:T(8,128)(2,1)S(1)}, bf16[4,24,768]{2,1,0:T(8,128)(2,1)S(1)}, u32[]{:S(2)}, u32[]{:S(2)}) collective-permute-start(bf16[4,24,768]{2,1,0:T(8,128)(2,1)S(1)} %fusion.4), channel_id=1, source_target_pairs={{0,4},{2,6},{4,0},{6,2},{8,12},{10,14},{12,8},{14,10},{16,20},{18,... | collective-permute-start | bytes 442376 | tf_op jit(solution)/shard_map/ppermute | solution.py:33
  21.7 4.5 %collective-permute-start.4 = (bf16[24,1536]{1,0:T(8,128)(2,1)S(1)}, bf16[24,1536]{1,0:T(8,128)(2,1)S(1)}, u32[]{:S(2)}, u32[]{:S(2)}) collective-permute-start(bf16[24,1536]{1,0:T(8,128)(2,1)S(1)} %get-tuple-element.27), channel_id=1, source_target_pairs={{0,8},{2,10},{4,12},{6,14},{8,0},{10,2},{12,4},{14,6},{16,24},{18,... | collective-permute-start | bytes 221192 | tf_op jit(solution)/shard_map/ppermute | solution.py:33
  23.3 6.7 %collective-permute-start.5 = (bf16[24,1536]{1,0:T(8,128)(2,1)S(1)}, bf16[24,1536]{1,0:T(8,128)(2,1)S(1)}, u32[]{:S(2)}, u32[]{:S(2)}) collective-permute-start(bf16[24,1536]{1,0:T(8,128)(2,1)S(1)} %get-tuple-element.28), channel_id=1, source_target_pairs={{0,16},{2,18},{4,20},{6,22},{8,24},{10,26},{12,28},{14,30},{16,0},... | collective-permute-start | bytes 221192 | tf_op jit(solution)/shard_map/ppermute | solution.py:33
  25.9 7.0 %collective-permute-start.6 = (bf16[24,1536]{1,0:T(8,128)(2,1)S(1)}, bf16[24,1536]{1,0:T(8,128)(2,1)S(1)}, u32[]{:S(2)}, u32[]{:S(2)}) collective-permute-start(bf16[24,1536]{1,0:T(8,128)(2,1)S(1)} %get-tuple-element.29), channel_id=1, source_target_pairs={{0,24},{2,26},{4,28},{6,30},{8,16},{10,18},{12,20},{14,22},{16,8},... | collective-permute-start | bytes 221192 | tf_op jit(solution)/shard_map/ppermute | solution.py:33
  32.9 4.5 %collective-permute-start.7 = (bf16[24,1536]{1,0:T(8,128)(2,1)S(1)}, bf16[24,1536]{1,0:T(8,128)(2,1)S(1)}, u32[]{:S(2)}, u32[]{:S(2)}) collective-permute-start(bf16[24,1536]{1,0:T(8,128)(2,1)S(1)} %pad_maximum_fusion.10), channel_id=1, source_target_pairs={{0,8},{2,10},{4,12},{6,14},{8,0},{10,2},{12,4},{14,6},{16,24},{18,... | collective-permute-start | bytes 221192 | tf_op jit(solution)/shard_map/ppermute | solution.py:33
  33.0 5.3 %collective-permute-start.8 = (bf16[24,1536]{1,0:T(8,128)(2,1)S(1)}, bf16[24,1536]{1,0:T(8,128)(2,1)S(1)}, u32[]{:S(2)}, u32[]{:S(2)}) collective-permute-start(bf16[24,1536]{1,0:T(8,128)(2,1)S(1)} %pad_maximum_fusion.10), channel_id=1, source_target_pairs={{0,16},{2,18},{4,20},{6,22},{8,24},{10,26},{12,28},{14,30},{16,0},... | collective-permute-start | bytes 221192 | tf_op jit(solution)/shard_map/ppermute | solution.py:33
  33.7 6.9 %collective-permute-start.9 = (bf16[24,1536]{1,0:T(8,128)(2,1)S(1)}, bf16[24,1536]{1,0:T(8,128)(2,1)S(1)}, u32[]{:S(2)}, u32[]{:S(2)}) collective-permute-start(bf16[24,1536]{1,0:T(8,128)(2,1)S(1)} %pad_maximum_fusion.10), channel_id=1, source_target_pairs={{0,24},{2,26},{4,28},{6,30},{8,16},{10,18},{12,20},{14,22},{16,8},... | collective-permute-start | bytes 221192 | tf_op jit(solution)/shard_map/ppermute | solution.py:33
  40.6 1.4 %copy-start.1 = (bf16[1,384,1536]{2,1,0:T(8,128)(2,1)S(1)}, bf16[1,384,1536]{2,1,0:T(8,128)(2,1)}, u32[]{:S(2)}) copy-start(bf16[1,384,1536]{2,1,0:T(8,128)(2,1)} %param.7) | copy-start | bytes 3538948
  40.8 6.8 %collective-permute-start.12 = (bf16[4,24,768]{2,1,0:T(8,128)(2,1)S(1)}, bf16[4,24,768]{2,1,0:T(8,128)(2,1)S(1)}, u32[]{:S(2)}, u32[]{:S(2)}) collective-permute-start(bf16[4,24,768]{2,1,0:T(8,128)(2,1)S(1)} %get-tuple-element.32), channel_id=1, source_target_pairs={{0,2},{2,0},{4,6},{6,4},{8,10},{10,8},{12,14},{14,12},{16,18},{18,... | collective-permute-start | bytes 442376 | tf_op jit(solution)/shard_map/ppermute | solution.py:33
  42.3 6.9 %collective-permute-start.10 = (bf16[4,24,768]{2,1,0:T(8,128)(2,1)S(1)}, bf16[4,24,768]{2,1,0:T(8,128)(2,1)S(1)}, u32[]{:S(2)}, u32[]{:S(2)}) collective-permute-start(bf16[4,24,768]{2,1,0:T(8,128)(2,1)S(1)} %get-tuple-element.33), channel_id=1, source_target_pairs={{0,4},{2,6},{4,0},{6,2},{8,12},{10,14},{12,8},{14,10},{16,20},{18,... | collective-permute-start | bytes 442376 | tf_op jit(solution)/shard_map/ppermute | solution.py:33
  47.7 6.8 %collective-permute-start.13 = (bf16[4,2,24,768]{3,2,0,1:T(8,128)(2,1)S(1)}, bf16[4,2,24,768]{3,2,0,1:T(8,128)(2,1)S(1)}, u32[]{:S(2)}, u32[]{:S(2)}) collective-permute-start(bf16[4,2,24,768]{3,2,0,1:T(8,128)(2,1)S(1)} %reverse_select_fusion.2), channel_id=1, source_target_pairs={{0,4},{2,6},{4,0},{6,2},{8,12},{10,14},{12,8},{14,10},{16,20},{18,... | collective-permute-start | bytes 884744 | tf_op jit(solution)/shard_map/ppermute | solution.py:33
  49.4 6.8 %collective-permute-start.11 = (bf16[4,2,24,768]{3,2,1,0:T(8,128)(2,1)S(1)}, bf16[4,2,24,768]{3,2,1,0:T(8,128)(2,1)S(1)}, u32[]{:S(2)}, u32[]{:S(2)}) collective-permute-start(bf16[4,2,24,768]{3,2,1,0:T(8,128)(2,1)S(1)} %reverse_select_fusion.3), channel_id=1, source_target_pairs={{0,2},{2,0},{4,6},{6,4},{8,10},{10,8},{12,14},{14,12},{16,18},{18,... | collective-permute-start | bytes 884744 | tf_op jit(solution)/shard_map/ppermute | solution.py:33
  56.4 0.7 copy-start.11
  56.5 0.8 copy-start.13
  56.5 0.9 copy-start.15
  56.5 1.0 copy-start.17
  57.5 1.3 %copy-start.4 = (bf16[768,768]{1,0:T(8,128)(2,1)S(1)}, bf16[768,768]{1,0:T(8,128)(2,1)}, u32[]{:S(2)}) copy-start(bf16[768,768]{1,0:T(8,128)(2,1)} %constant.107.clone.table_ref) | copy-start | bytes 3538948
  57.6 2.9 %copy-start.3 = (bf16[768,768]{1,0:T(8,128)(2,1)S(1)}, bf16[768,768]{1,0:T(8,128)(2,1)}, u32[]{:S(2)}) copy-start(bf16[768,768]{1,0:T(8,128)(2,1)} %constant.108.clone.table_ref) | copy-start | bytes 3538948
  57.6 2.9 %collective-permute-start.14 = (bf16[768,768]{1,0:T(8,128)(2,1)S(1)}, bf16[768,768]{1,0:T(8,128)(2,1)S(1)}, u32[]{:S(2)}, u32[]{:S(2)}) collective-permute-start(bf16[768,768]{1,0:T(8,128)(2,1)S(1)} %pad_maximum_fusion.1.shaped_ref), channel_id=1, source_target_pairs={{0,1},{1,0},{2,3},{3,2},{4,5},{5,4},{6,7},{7,6},{8,9},{9,8},{10,11... | collective-permute-start | bytes 3538952 | tf_op jit(solution)/shard_map/ppermute | solution.py:276
  62.6 5.0 %copy-start.5 = (bf16[2,16,24,768]{3,2,1,0:T(8,128)(2,1)S(1)}, bf16[2,16,24,768]{3,2,1,0:T(8,128)(2,1)}, u32[]{:S(2)}) copy-start(bf16[2,16,24,768]{3,2,1,0:T(8,128)(2,1)} %param.9) | copy-start | bytes 3538948
  62.6 5.0 %copy-start.6 = (bf16[768,768]{1,0:T(8,128)(2,1)S(1)}, bf16[768,768]{1,0:T(8,128)(2,1)}, u32[]{:S(2)}) copy-start(bf16[768,768]{1,0:T(8,128)(2,1)} %constant.105.clone.refs_1_.re_ref) | copy-start | bytes 3538948
  62.6 32.1 %all-to-all-start = ((bf16[16,48,768]{2,1,0:T(8,128)(2,1)}), bf16[16,48,768]{2,1,0:T(8,128)(2,1)S(1)}, u32[]{:S(2)}, u32[]{:S(2)}) async-start(bf16[16,48,768]{2,1,0:T(8,128)(2,1)} %bitcast.33), calls=%async_computation | async-start | bytes 2359296 | tf_op jit(solution)/shard_map/all_to_all | solution.py:298
  67.6 1.3 %copy-start.7 = (bf16[768,768]{1,0:T(8,128)(2,1)S(1)}, bf16[768,768]{1,0:T(8,128)(2,1)}, u32[]{:S(2)}) copy-start(bf16[768,768]{1,0:T(8,128)(2,1)} %constant.106.clone.refs_2_.im_ref) | copy-start | bytes 3538948
  68.9 3.0 %copy-start.8 = (bf16[768,768]{1,0:T(8,128)(2,1)S(1)}, bf16[768,768]{1,0:T(8,128)(2,1)}, u32[]{:S(2)}) copy-start(bf16[768,768]{1,0:T(8,128)(2,1)} %constant.106.clone.refs_2_.im_ref) | copy-start | bytes 3538948
  70.9 1.0 copy-start.9
  94.7 1.3 %copy-start.10 = (bf16[768,768]{1,0:T(8,128)(2,1)S(1)}, bf16[768,768]{1,0:T(8,128)(2,1)}, u32[]{:S(2)}) copy-start(bf16[768,768]{1,0:T(8,128)(2,1)} %copy-done.9) | copy-start | bytes 3538948
  96.0 8.2 %copy-start.12 = (bf16[384,384]{1,0:T(8,128)(2,1)S(1)}, bf16[384,384]{1,0:T(8,128)(2,1)}, u32[]{:S(2)}) copy-start(bf16[384,384]{1,0:T(8,128)(2,1)} %copy-done.11) | copy-start | bytes 884740
  96.0 8.2 %copy-start.14 = (bf16[384,384]{1,0:T(8,128)(2,1)S(1)}, bf16[384,384]{1,0:T(8,128)(2,1)}, u32[]{:S(2)}) copy-start(bf16[384,384]{1,0:T(8,128)(2,1)} %copy-done.13) | copy-start | bytes 884740
  96.0 8.2 %copy-start.16 = (bf16[384,384]{1,0:T(8,128)(2,1)S(1)}, bf16[384,384]{1,0:T(8,128)(2,1)}, u32[]{:S(2)}) copy-start(bf16[384,384]{1,0:T(8,128)(2,1)} %copy-done.15) | copy-start | bytes 884740
  96.0 8.2 %copy-start.18 = (bf16[384,384]{1,0:T(8,128)(2,1)S(1)}, bf16[384,384]{1,0:T(8,128)(2,1)}, u32[]{:S(2)}) copy-start(bf16[384,384]{1,0:T(8,128)(2,1)} %copy-done.17) | copy-start | bytes 884740
  98.4 12.9 %all-to-all-start.1 = ((f32[32,1,16]{2,1,0:T(1,128)}), f32[32,1,16]{2,1,0:T(1,128)S(1)}, u32[]{:S(2)}, u32[]{:S(2)}) async-start(f32[32,1,16]{2,1,0:T(1,128)} %bitcast.38), calls=%async_computation.1 | async-start | bytes 32768 | tf_op jit(solution)/shard_map/all_to_all | solution.py:319

commit v6 on v5

--- a/solution.py
+++ b/solution.py
@@ -145,7 +145,7 @@
     )
 
 
-def coupling_kernel(block_rows, fields_ref, targets_ref, out_ref):
+def coupling_kernel(block_rows, by_xor, fields_ref, targets_ref, out_ref):
     modes = out_ref.shape[1]
     product = lax.dot_general(
         fields_ref[...], targets_ref[...], (((1,), (1,)), ((), ())), preferred_element_type=f32
@@ -167,6 +167,9 @@
     product = exactly(product, groups(right), ((1,), (1,)))
     by_re, by_im = product[:, :modes], product[:, modes:]
     mode = lax.broadcasted_iota(jnp.int32, (modes, 2 * modes), 0)
+    if by_xor:
+        mode = mode ^ lax.axis_index("modes")
+        mode = mode % (modes // 2) * 2 + mode // (modes // 2)
     from_row = lax.broadcasted_iota(jnp.int32, (modes, 2 * modes), 1)
     real = jnp.where(from_row == 2 * mode, 1.0, 0.0).astype(f32)
     imag = jnp.where(from_row == 2 * mode + 1, 1.0, 0.0).astype(f32)
@@ -295,11 +298,12 @@
     )
     blocks = columns.reshape(owners, 2, -1, block_rows, grid_size).transpose(0, 2, 1, 3, 4)
     blocks = blocks.reshape(count, 2 * block_rows, grid_size)
-    pixels = lax.all_to_all(blocks, "modes", 0, 0, tiled=True).reshape(column_shape)
-
-    seen = kernel_call(
-        targets_kernel, column_shape, bf16, matmul, (targets.reshape(column_shape), full_re, full_im)
-    )
+    if count <= 16:
+        turns = [at // 2 + count // 2 * (at % 2) for at in range(count)]
+        pixels = tuple(exchange(pick(blocks, me ^ e, 0), e, count) if e else pick(blocks, me, 0) for e in turns)
+    else:
+        pixels = (lax.all_to_all(blocks, "modes", 0, 0, tiled=True),)
+
     output_fields = kernel_call(
         lambda *refs: fields_kernel(block_rows, *refs),
         (local_rows, double_width),
@@ -307,14 +311,18 @@
         matmul,
         (columns, full_re, full_im),
     )
+    targets, output_fields = lax.optimization_barrier((targets, output_fields))
+    seen = kernel_call(
+        targets_kernel, column_shape, bf16, matmul, (targets.reshape(column_shape), full_re, full_im)
+    )
     pixels, output_fields, seen = lax.optimization_barrier((pixels, output_fields, seen))
 
     term = kernel_call(
-        lambda *refs: coupling_kernel(block_rows, *refs),
+        lambda *refs: coupling_kernel(block_rows, len(pixels) > 1, *refs),
         (2 * mode_total, mode_total),
         f32,
         matmul,
-        (pixels, seen),
+        (jnp.concatenate(pixels, 0).reshape(column_shape), seen),
     )
     pieces = lax.all_to_all(term, ("modes", "rows"), 0, 0, tiled=True)
     coupling = jnp.sum(pieces, 0, keepdims=True)

time: 112 us -> 108 us (0.964)
  starting transfers between devices: 32.5 us -> 47.8 us
  waiting for transfers between devices: 53.8 us -> 39.4 us
  local copies, waits for them, and re-layouts: 8.13 us -> 4.73 us
  Pallas kernels: 13 us -> 10.7 us
    ppermute x14 -> x29, starting transfers between devices: 21.7 us -> 44.9 us  [exchange(): lax.ppermute(values, 'modes', [(i, i ^ offset) for i in range(count)])]
    all_to_all x1 -> x0, waiting for transfers between devices: 18.5 us -> none  [local(): lax.all_to_all(blocks, 'modes', 0, 0, tiled=True).reshape(column_shape)]
    all_to_all x1 -> x0, starting transfers between devices: 5.03 us -> none  [local(): lax.all_to_all(blocks, 'modes', 0, 0, tiled=True).reshape(column_shape)]
    ppermute x14 -> x29, waiting for transfers between devices: 28.7 us -> 32.7 us  [exchange(): lax.ppermute(values, 'modes', [(i, i ^ offset) for i in range(count)])]
    unnamed x38 -> x47, local copies, waits for them, and re-layouts: 7.8 us -> 4.24 us
    all_to_all x1, starting transfers between devices: 5.76 us -> 2.88 us  [local(): pieces = lax.all_to_all(term, ('modes', 'rows'), 0, 0, tiled=True)]
    pallas_call x6, Pallas kernels: 13 us -> 10.7 us  [kernel_call(): pl.pallas_call(kernel, out_shape=out_shape, compiler_params=pltpu.Compile...]
  transfers between devices with their start and end apart: 17 -> 31, of which waited for: 13 -> 16; matrix products, arithmetic and copies ran while one was open for 2% -> 2% of each run, Pallas kernels for 7% -> 6%
where the time goes in v6:
time: 108 us; the launch traced here: 107 us
  starting transfers between devices  47.8 us (44%)
  waiting for transfers between devices  39.4 us (36%)
  Pallas kernels  10.7 us (10%)
  local copies, waits for them, and re-layouts  4.73 us (4%)
  other arithmetic  3.38 us (3%)
  between operations  1.25 us (1%)
    ppermute x29, starting transfers between devices, exchange(): lax.ppermute(values, 'modes', [(i, i ^ offset) for i in range(count)])  44.9 us
    ppermute x29, waiting for transfers between devices, exchange(): lax.ppermute(values, 'modes', [(i, i ^ offset) for i in range(count)])  32.7 us
    pallas_call x6, Pallas kernels, kernel_call(): pl.pallas_call(kernel, out_shape=out_shape, compiler_params=pltpu.Compile...  10.7 us
    all_to_all x1, waiting for transfers between devices, local(): pieces = lax.all_to_all(term, ('modes', 'rows'), 0, 0, tiled=True)  6 us
    unnamed x47, local copies, waits for them, and re-layouts  4.24 us
    all_to_all x1, starting transfers between devices, local(): pieces = lax.all_to_all(term, ('modes', 'rows'), 0, 0, tiled=True)  2.88 us
  transfers between devices with their start and end apart: 31, of which 16 were waited for; matrix products, arithmetic and copies ran while one was open for 2% of the time, Pallas kernels for 6%

profile of v6, /device:TPU:0, one launch (start us, length us, event | category | flops | bytes accessed | tf_op | source)
XLA Modules:
  0.0 107.2 jit_solution(17493205699738393606)
XLA Ops:
  0.6 1.3 %copy-done = bf16[1,384,1536]{2,1,0:T(8,128)(2,1)S(1)} copy-done((bf16[1,384,1536]{2,1,0:T(8,128)(2,1)S(1)}, bf16[1,384,1536]{2,1,0:T(8,128)(2,1)}, u32[]{:S(2)}) %copy-start) | copy-done | bytes 1179672
  1.9 1.3 %copy-done.2 = bf16[1,384,1536]{2,1,0:T(8,128)(2,1)S(1)} copy-done((bf16[1,384,1536]{2,1,0:T(8,128)(2,1)S(1)}, bf16[1,384,1536]{2,1,0:T(8,128)(2,1)}, u32[]{:S(2)}) %copy-start.2) | copy-done | bytes 1179672
  3.2 1.2 %shard_map.94 = (bf16[192,768]{1,0:T(8,128)(2,1)S(1)}, f32[192,768]{1,0:T(8,128)S(1)}, bf16[192,768]{1,0:T(8,128)(2,1)S(1)}, f32[192,768]{1,0:T(8,128)S(1)}) custom-call(bf16[384,1536]{1,0:T(8,128)(2,1)S(1)} %bitcast.93, bf16[384,1536]{1,0:T(8,128)(2,1)S(1)} %bitcast.95), custom_call_target="tpu_custom_call" | custom-call | flops 4718592 | bytes 4194304 | tf_op jit(solution)/shard_map/pallas_call | solution.py:189
  4.4 3.0 %collective-permute-start.2 = (bf16[4,2,24,768]{3,2,0,1:T(8,128)(2,1)S(1)}, bf16[4,2,24,768]{3,2,0,1:T(8,128)(2,1)S(1)}, u32[]{:S(2)}, u32[]{:S(2)}) collective-permute-start(bf16[4,2,24,768]{3,2,0,1:T(8,128)(2,1)S(1)} %copy.19), channel_id=1, source_target_pairs={{0,4},{2,6},{4,0},{6,2},{8,12},{10,14},{12,8},{14,10},{16,20},{18,... | collective-permute-start | bytes 884744 | tf_op jit(solution)/shard_map/ppermute | solution.py:33
  7.4 1.6 %collective-permute-start = (bf16[4,2,24,768]{3,2,0,1:T(8,128)(2,1)S(1)}, bf16[4,2,24,768]{3,2,0,1:T(8,128)(2,1)S(1)}, u32[]{:S(2)}, u32[]{:S(2)}) collective-permute-start(bf16[4,2,24,768]{3,2,0,1:T(8,128)(2,1)S(1)} %copy.17), channel_id=1, source_target_pairs={{0,2},{2,0},{4,6},{6,4},{8,10},{10,8},{12,14},{14,12},{16,18},{18,... | collective-permute-start | bytes 884744 | tf_op jit(solution)/shard_map/ppermute | solution.py:33
  9.0 5.4 %collective-permute-done.2 = bf16[4,2,24,768]{3,2,0,1:T(8,128)(2,1)S(1)} collective-permute-done((bf16[4,2,24,768]{3,2,0,1:T(8,128)(2,1)S(1)}, bf16[4,2,24,768]{3,2,0,1:T(8,128)(2,1)S(1)}, u32[]{:S(2)}, u32[]{:S(2)}) %collective-permute-start.2) | collective-permute-done | bytes 294944 | tf_op jit(solution)/shard_map/ppermute | solution.py:33
  14.5 1.8 %collective-permute-start.3 = (bf16[4,24,768]{2,1,0:T(8,128)(2,1)S(1)}, bf16[4,24,768]{2,1,0:T(8,128)(2,1)S(1)}, u32[]{:S(2)}, u32[]{:S(2)}) collective-permute-start(bf16[4,24,768]{2,1,0:T(8,128)(2,1)S(1)} %fusion.5), channel_id=1, source_target_pairs={{0,2},{2,0},{4,6},{6,4},{8,10},{10,8},{12,14},{14,12},{16,18},{18,... | collective-permute-start | bytes 442376 | tf_op jit(solution)/shard_map/ppermute | solution.py:33
  16.4 1.6 %collective-permute-start.1 = (bf16[4,24,768]{2,1,0:T(8,128)(2,1)S(1)}, bf16[4,24,768]{2,1,0:T(8,128)(2,1)S(1)}, u32[]{:S(2)}, u32[]{:S(2)}) collective-permute-start(bf16[4,24,768]{2,1,0:T(8,128)(2,1)S(1)} %fusion.4), channel_id=1, source_target_pairs={{0,4},{2,6},{4,0},{6,2},{8,12},{10,14},{12,8},{14,10},{16,20},{18,... | collective-permute-start | bytes 442376 | tf_op jit(solution)/shard_map/ppermute | solution.py:33
  18.0 1.8 %collective-permute-done.3 = bf16[4,24,768]{2,1,0:T(8,128)(2,1)S(1)} collective-permute-done((bf16[4,24,768]{2,1,0:T(8,128)(2,1)S(1)}, bf16[4,24,768]{2,1,0:T(8,128)(2,1)S(1)}, u32[]{:S(2)}, u32[]{:S(2)}) %collective-permute-start.3) | collective-permute-done | bytes 147488 | tf_op jit(solution)/shard_map/ppermute | solution.py:33
  19.7 1.8 %collective-permute-done.1 = bf16[4,24,768]{2,1,0:T(8,128)(2,1)S(1)} collective-permute-done((bf16[4,24,768]{2,1,0:T(8,128)(2,1)S(1)}, bf16[4,24,768]{2,1,0:T(8,128)(2,1)S(1)}, u32[]{:S(2)}, u32[]{:S(2)}) %collective-permute-start.1) | collective-permute-done | bytes 147488 | tf_op jit(solution)/shard_map/ppermute | solution.py:33
  21.7 1.6 %collective-permute-start.4 = (bf16[24,1536]{1,0:T(8,128)(2,1)S(1)}, bf16[24,1536]{1,0:T(8,128)(2,1)S(1)}, u32[]{:S(2)}, u32[]{:S(2)}) collective-permute-start(bf16[24,1536]{1,0:T(8,128)(2,1)S(1)} %get-tuple-element.77), channel_id=1, source_target_pairs={{0,8},{2,10},{4,12},{6,14},{8,0},{10,2},{12,4},{14,6},{16,24},{18,... | collective-permute-start | bytes 221192 | tf_op jit(solution)/shard_map/ppermute | solution.py:33
  23.3 2.6 %collective-permute-start.5 = (bf16[24,1536]{1,0:T(8,128)(2,1)S(1)}, bf16[24,1536]{1,0:T(8,128)(2,1)S(1)}, u32[]{:S(2)}, u32[]{:S(2)}) collective-permute-start(bf16[24,1536]{1,0:T(8,128)(2,1)S(1)} %get-tuple-element.78), channel_id=1, source_target_pairs={{0,16},{2,18},{4,20},{6,22},{8,24},{10,26},{12,28},{14,30},{16,0},... | collective-permute-start | bytes 221192 | tf_op jit(solution)/shard_map/ppermute | solution.py:33
  26.1 3.9 %collective-permute-done.5 = bf16[24,1536]{1,0:T(8,128)(2,1)S(1)} collective-permute-done((bf16[24,1536]{1,0:T(8,128)(2,1)S(1)}, bf16[24,1536]{1,0:T(8,128)(2,1)S(1)}, u32[]{:S(2)}, u32[]{:S(2)}) %collective-permute-start.5) | collective-permute-done | bytes 73760 | tf_op jit(solution)/shard_map/ppermute | solution.py:33
  30.0 2.1 %collective-permute-done.6 = bf16[24,1536]{1,0:T(8,128)(2,1)S(1)} collective-permute-done((bf16[24,1536]{1,0:T(8,128)(2,1)S(1)}, bf16[24,1536]{1,0:T(8,128)(2,1)S(1)}, u32[]{:S(2)}, u32[]{:S(2)}) %collective-permute-start.6) | collective-permute-done | bytes 73760 | tf_op jit(solution)/shard_map/ppermute | solution.py:33
  32.2 0.9 collective-permute-start.9
  33.1 1.5 %collective-permute-start.8 = (bf16[24,1536]{1,0:T(8,128)(2,1)S(1)}, bf16[24,1536]{1,0:T(8,128)(2,1)S(1)}, u32[]{:S(2)}, u32[]{:S(2)}) collective-permute-start(bf16[24,1536]{1,0:T(8,128)(2,1)S(1)} %pad_maximum_fusion.10), channel_id=1, source_target_pairs={{0,16},{2,18},{4,20},{6,22},{8,24},{10,26},{12,28},{14,30},{16,0},... | collective-permute-start | bytes 221192 | tf_op jit(solution)/shard_map/ppermute | solution.py:33
  34.6 2.1 %collective-permute-start.7 = (bf16[24,1536]{1,0:T(8,128)(2,1)S(1)}, bf16[24,1536]{1,0:T(8,128)(2,1)S(1)}, u32[]{:S(2)}, u32[]{:S(2)}) collective-permute-start(bf16[24,1536]{1,0:T(8,128)(2,1)S(1)} %pad_maximum_fusion.10), channel_id=1, source_target_pairs={{0,8},{2,10},{4,12},{6,14},{8,0},{10,2},{12,4},{14,6},{16,24},{18,... | collective-permute-start | bytes 221192 | tf_op jit(solution)/shard_map/ppermute | solution.py:33
  36.7 1.9 %collective-permute-done.9 = bf16[24,1536]{1,0:T(8,128)(2,1)S(1)} collective-permute-done((bf16[24,1536]{1,0:T(8,128)(2,1)S(1)}, bf16[24,1536]{1,0:T(8,128)(2,1)S(1)}, u32[]{:S(2)}, u32[]{:S(2)}) %collective-permute-start.9) | collective-permute-done | bytes 73760 | tf_op jit(solution)/shard_map/ppermute | solution.py:33
  38.6 1.3 %collective-permute-done.8 = bf16[24,1536]{1,0:T(8,128)(2,1)S(1)} collective-permute-done((bf16[24,1536]{1,0:T(8,128)(2,1)S(1)}, bf16[24,1536]{1,0:T(8,128)(2,1)S(1)}, u32[]{:S(2)}, u32[]{:S(2)}) %collective-permute-start.8) | collective-permute-done | bytes 73760 | tf_op jit(solution)/shard_map/ppermute | solution.py:33
  40.1 1.2 %collective-permute-start.12 = (bf16[4,24,768]{2,1,0:T(8,128)(2,1)S(1)}, bf16[4,24,768]{2,1,0:T(8,128)(2,1)S(1)}, u32[]{:S(2)}, u32[]{:S(2)}) collective-permute-start(bf16[4,24,768]{2,1,0:T(8,128)(2,1)S(1)} %get-tuple-element.82), channel_id=1, source_target_pairs={{0,2},{2,0},{4,6},{6,4},{8,10},{10,8},{12,14},{14,12},{16,18},{18,... | collective-permute-start | bytes 442376 | tf_op jit(solution)/shard_map/ppermute | solution.py:33
  41.6 1.5 %collective-permute-start.10 = (bf16[4,24,768]{2,1,0:T(8,128)(2,1)S(1)}, bf16[4,24,768]{2,1,0:T(8,128)(2,1)S(1)}, u32[]{:S(2)}, u32[]{:S(2)}) collective-permute-start(bf16[4,24,768]{2,1,0:T(8,128)(2,1)S(1)} %get-tuple-element.83), channel_id=1, source_target_pairs={{0,4},{2,6},{4,0},{6,2},{8,12},{10,14},{12,8},{14,10},{16,20},{18,... | collective-permute-start | bytes 442376 | tf_op jit(solution)/shard_map/ppermute | solution.py:33
  43.1 3.3 %collective-permute-done.12 = bf16[4,24,768]{2,1,0:T(8,128)(2,1)S(1)} collective-permute-done((bf16[4,24,768]{2,1,0:T(8,128)(2,1)S(1)}, bf16[4,24,768]{2,1,0:T(8,128)(2,1)S(1)}, u32[]{:S(2)}, u32[]{:S(2)}) %collective-permute-start.12) | collective-permute-done | bytes 147488 | tf_op jit(solution)/shard_map/ppermute | solution.py:33
  46.5 1.7 %collective-permute-start.13 = (bf16[4,2,24,768]{3,2,0,1:T(8,128)(2,1)S(1)}, bf16[4,2,24,768]{3,2,0,1:T(8,128)(2,1)S(1)}, u32[]{:S(2)}, u32[]{:S(2)}) collective-permute-start(bf16[4,2,24,768]{3,2,0,1:T(8,128)(2,1)S(1)} %reverse_select_fusion.2), channel_id=1, source_target_pairs={{0,4},{2,6},{4,0},{6,2},{8,12},{10,14},{12,8},{14,10},{16,20},{18,... | collective-permute-start | bytes 884744 | tf_op jit(solution)/shard_map/ppermute | solution.py:33
  49.0 4.3 %collective-permute-done.13 = bf16[4,2,24,768]{3,2,0,1:T(8,128)(2,1)S(1)} collective-permute-done((bf16[4,2,24,768]{3,2,0,1:T(8,128)(2,1)S(1)}, bf16[4,2,24,768]{3,2,0,1:T(8,128)(2,1)S(1)}, u32[]{:S(2)}, u32[]{:S(2)}) %collective-permute-start.13) | collective-permute-done | bytes 294944 | tf_op jit(solution)/shard_map/ppermute | solution.py:33
  53.5 1.7 %collective-permute-done.11 = bf16[4,2,24,768]{3,2,1,0:T(8,128)(2,1)S(1)} collective-permute-done((bf16[4,2,24,768]{3,2,1,0:T(8,128)(2,1)S(1)}, bf16[4,2,24,768]{3,2,1,0:T(8,128)(2,1)S(1)}, u32[]{:S(2)}, u32[]{:S(2)}) %collective-permute-start.11) | collective-permute-done | bytes 294944 | tf_op jit(solution)/shard_map/ppermute | solution.py:33
  56.8 1.0 copy-done.4
  57.8 1.1 %shard_map.95.own_ref = f32[768,768]{1,0:T(8,128)S(1)} custom-call(bf16[768,768]{1,0:T(8,128)(2,1)S(1)} %copy-done.4, bf16[768,768]{1,0:T(8,128)(2,1)S(1)} %pad_maximum_fusion.1.shaped_ref), custom_call_target="tpu_custom_call" | custom-call | flops 905969664 | bytes 4194304 | tf_op jit(solution)/shard_map/pallas_call | solution.py:189
  59.5 1.1 %shard_map.96.refs_0_ = bf16[768,768]{1,0:T(8,128)(2,1)S(1)} custom-call(bf16[768,768]{1,0:T(8,128)(2,1)S(1)} %copy-done.3, bf16[768,768]{1,0:T(8,128)(2,1)S(1)} %collective-permute-done.14.shaped_ref, f32[768,768]{1,0:T(8,128)S(1)} %shard_map.95.own_ref), custom_call_target="tpu_custom_call" | custom-call | flops 905969664 | bytes 4194304 | tf_op jit(solution)/shard_map/pallas_call | solution.py:189
  60.8 2.4 %collective-permute-start.29 = (bf16[48,768]{1,0:T(8,128)(2,1)S(1)}, bf16[48,768]{1,0:T(8,128)(2,1)S(1)}, u32[]{:S(2)}, u32[]{:S(2)}) collective-permute-start(bf16[48,768]{1,0:T(8,128)(2,1)S(1)} %get-tuple-element.57), channel_id=1, source_target_pairs={{0,30},{2,28},{4,26},{6,24},{8,22},{10,20},{12,18},{14,16},{16,14}... | collective-permute-start | bytes 221192 | tf_op jit(solution)/shard_map/ppermute | solution.py:33
  63.9 2.9 %collective-permute-start.27 = (bf16[48,768]{1,0:T(8,128)(2,1)S(1)}, bf16[48,768]{1,0:T(8,128)(2,1)S(1)}, u32[]{:S(2)}, u32[]{:S(2)}) collective-permute-start(bf16[48,768]{1,0:T(8,128)(2,1)S(1)} %get-tuple-element.59), channel_id=1, source_target_pairs={{0,28},{2,30},{4,24},{6,26},{8,20},{10,22},{12,16},{14,18},{16,12}... | collective-permute-start | bytes 221192 | tf_op jit(solution)/shard_map/ppermute | solution.py:33
  66.8 1.7 %collective-permute-start.26 = (bf16[48,768]{1,0:T(8,128)(2,1)S(1)}, bf16[48,768]{1,0:T(8,128)(2,1)S(1)}, u32[]{:S(2)}, u32[]{:S(2)}) collective-permute-start(bf16[48,768]{1,0:T(8,128)(2,1)S(1)} %get-tuple-element.60), channel_id=1, source_target_pairs={{0,12},{2,14},{4,8},{6,10},{8,4},{10,6},{12,0},{14,2},{16,28},{18,... | collective-permute-start | bytes 221192 | tf_op jit(solution)/shard_map/ppermute | solution.py:33
  68.5 1.4 %collective-permute-start.25 = (bf16[48,768]{1,0:T(8,128)(2,1)S(1)}, bf16[48,768]{1,0:T(8,128)(2,1)S(1)}, u32[]{:S(2)}, u32[]{:S(2)}) collective-permute-start(bf16[48,768]{1,0:T(8,128)(2,1)S(1)} %get-tuple-element.61), channel_id=1, source_target_pairs={{0,26},{2,24},{4,30},{6,28},{8,18},{10,16},{12,22},{14,20},{16,10}... | collective-permute-start | bytes 221192 | tf_op jit(solution)/shard_map/ppermute | solution.py:33
  70.6 1.7 %collective-permute-done.28 = bf16[48,768]{1,0:T(8,128)(2,1)S(1)} collective-permute-done((bf16[48,768]{1,0:T(8,128)(2,1)S(1)}, bf16[48,768]{1,0:T(8,128)(2,1)S(1)}, u32[]{:S(2)}, u32[]{:S(2)}) %collective-permute-start.28) | collective-permute-done | bytes 73760 | tf_op jit(solution)/shard_map/ppermute | solution.py:33
  72.3 1.7 %collective-permute-start.23 = (bf16[48,768]{1,0:T(8,128)(2,1)S(1)}, bf16[48,768]{1,0:T(8,128)(2,1)S(1)}, u32[]{:S(2)}, u32[]{:S(2)}) collective-permute-start(bf16[48,768]{1,0:T(8,128)(2,1)S(1)} %get-tuple-element.63), channel_id=1, source_target_pairs={{0,24},{2,26},{4,28},{6,30},{8,16},{10,18},{12,20},{14,22},{16,8},... | collective-permute-start | bytes 221192 | tf_op jit(solution)/shard_map/ppermute | solution.py:33
  74.5 2.8 %collective-permute-start.21 = (bf16[48,768]{1,0:T(8,128)(2,1)S(1)}, bf16[48,768]{1,0:T(8,128)(2,1)S(1)}, u32[]{:S(2)}, u32[]{:S(2)}) collective-permute-start(bf16[48,768]{1,0:T(8,128)(2,1)S(1)} %get-tuple-element.65), channel_id=1, source_target_pairs={{0,22},{2,20},{4,18},{6,16},{8,30},{10,28},{12,26},{14,24},{16,6},... | collective-permute-start | bytes 221192 | tf_op jit(solution)/shard_map/ppermute | solution.py:33
  77.3 1.8 %collective-permute-start.20 = (bf16[48,768]{1,0:T(8,128)(2,1)S(1)}, bf16[48,768]{1,0:T(8,128)(2,1)S(1)}, u32[]{:S(2)}, u32[]{:S(2)}) collective-permute-start(bf16[48,768]{1,0:T(8,128)(2,1)S(1)} %get-tuple-element.66), channel_id=1, source_target_pairs={{0,6},{2,4},{4,2},{6,0},{8,14},{10,12},{12,10},{14,8},{16,22},{18,... | collective-permute-start | bytes 221192 | tf_op jit(solution)/shard_map/ppermute | solution.py:33
  79.1 3.0 %shard_map.97 = bf16[384,1536]{1,0:T(8,128)(2,1)} custom-call(bf16[768,768]{1,0:T(8,128)(2,1)S(1)} %shard_map.96.refs_0_, bf16[768,768]{1,0:T(8,128)(2,1)S(1)} %copy-done.7, bf16[768,768]{1,0:T(8,128)(2,1)S(1)} %copy-done.6), custom_call_target="tpu_custom_call" | custom-call | flops 1811939328 | bytes 4194304 | tf_op jit(solution)/shard_map/pallas_call | solution.py:189
  82.1 1.2 %collective-permute-start.19 = (bf16[48,768]{1,0:T(8,128)(2,1)S(1)}, bf16[48,768]{1,0:T(8,128)(2,1)S(1)}, u32[]{:S(2)}, u32[]{:S(2)}) collective-permute-start(bf16[48,768]{1,0:T(8,128)(2,1)S(1)} %get-tuple-element.67), channel_id=1, source_target_pairs={{0,20},{2,22},{4,16},{6,18},{8,28},{10,30},{12,24},{14,26},{16,4},... | collective-permute-start | bytes 221192 | tf_op jit(solution)/shard_map/ppermute | solution.py:33
  83.3 1.0 collective-permute-start.18
  84.3 1.7 %collective-permute-start.17 = (bf16[48,768]{1,0:T(8,128)(2,1)S(1)}, bf16[48,768]{1,0:T(8,128)(2,1)S(1)}, u32[]{:S(2)}, u32[]{:S(2)}) collective-permute-start(bf16[48,768]{1,0:T(8,128)(2,1)S(1)} %get-tuple-element.69), channel_id=1, source_target_pairs={{0,18},{2,16},{4,22},{6,20},{8,26},{10,24},{12,30},{14,28},{16,2},... | collective-permute-start | bytes 221192 | tf_op jit(solution)/shard_map/ppermute | solution.py:33
  86.0 2.0 %collective-permute-start.16 = (bf16[48,768]{1,0:T(8,128)(2,1)S(1)}, bf16[48,768]{1,0:T(8,128)(2,1)S(1)}, u32[]{:S(2)}, u32[]{:S(2)}) collective-permute-start(bf16[48,768]{1,0:T(8,128)(2,1)S(1)} %get-tuple-element.70), channel_id=1, source_target_pairs={{0,2},{2,0},{4,6},{6,4},{8,10},{10,8},{12,14},{14,12},{16,18},{18,... | collective-permute-start | bytes 221192 | tf_op jit(solution)/shard_map/ppermute | solution.py:33
  88.7 2.0 %shard_map.98.refs_1_ = bf16[768,768]{1,0:T(8,128)(2,1)S(1)} custom-call(bf16[768,768]{1,0:T(8,128)(2,1)S(1)} %bitcast.100, bf16[768,768]{1,0:T(8,128)(2,1)S(1)} %copy-done.7, bf16[768,768]{1,0:T(8,128)(2,1)S(1)} %copy-done.6), custom_call_target="tpu_custom_call" | custom-call | flops 1811939328 | bytes 4194304 | tf_op jit(solution)/shard_map/pallas_call | solution.py:189
  90.7 1.8 %collective-permute-done.17 = bf16[48,768]{1,0:T(8,128)(2,1)S(1)} collective-permute-done((bf16[48,768]{1,0:T(8,128)(2,1)S(1)}, bf16[48,768]{1,0:T(8,128)(2,1)S(1)}, u32[]{:S(2)}, u32[]{:S(2)}) %collective-permute-start.17) | collective-permute-done | bytes 73760 | tf_op jit(solution)/shard_map/ppermute | solution.py:33
  92.5 1.5 %collective-permute-done.15 = bf16[48,768]{1,0:T(8,128)(2,1)S(1)} collective-permute-done((bf16[48,768]{1,0:T(8,128)(2,1)S(1)}, bf16[48,768]{1,0:T(8,128)(2,1)S(1)}, u32[]{:S(2)}, u32[]{:S(2)}) %collective-permute-start.15) | collective-permute-done | bytes 73760 | tf_op jit(solution)/shard_map/ppermute | solution.py:33
  94.3 2.4 %shard_map.99 = f32[32,16]{1,0:T(8,128)} custom-call(bf16[768,768]{1,0:T(8,128)(2,1)S(1)} %constant_dynamic-update-slice_fusion.refs_0_, bf16[768,768]{1,0:T(8,128)(2,1)S(1)} %shard_map.98.refs_1_), custom_call_target="tpu_custom_call" | custom-call | flops 1811939328 | bytes 4194304 | tf_op jit(solution)/shard_map/pallas_call | solution.py:189
  96.6 2.9 %all-to-all-start = ((f32[32,1,16]{2,1,0:T(1,128)}), f32[32,1,16]{2,1,0:T(1,128)S(1)}, u32[]{:S(2)}, u32[]{:S(2)}) async-start(f32[32,1,16]{2,1,0:T(1,128)} %bitcast.53), calls=%async_computation | async-start | bytes 32768 | tf_op jit(solution)/shard_map/all_to_all | solution.py:327
  99.6 1.1 %pad_maximum_fusion = bf16[384,1536]{1,0:T(8,128)(2,1)} fusion(bf16[384,384]{1,0:T(8,128)(2,1)S(1)} %copy-done.13, bf16[384,384]{1,0:T(8,128)(2,1)S(1)} %copy-done.11, bf16[384,384]{1,0:T(8,128)(2,1)S(1)} %copy-done.15, bf16[384,384]{1,0:T(8,128)(2,1)S(1)} %copy-done.9), kind=kLoop, calls=%fused_computation.8 | loop fusion | flops 4718592 | bytes 2359296 | tf_op jit(solution)/shard_map/concatenate | solution.py:271
  100.7 6.0 %all-to-all-done = f32[32,1,16]{2,1,0:T(1,128)S(1)} async-done(((f32[32,1,16]{2,1,0:T(1,128)}), f32[32,1,16]{2,1,0:T(1,128)S(1)}, u32[]{:S(2)}, u32[]{:S(2)}) %all-to-all-start) | async-done | bytes 2080 | tf_op jit(solution)/shard_map/all_to_all | solution.py:327
  (102 shorter events, 7.7 us)
Async XLA Ops:
  0.6 1.3 %copy-start = (bf16[1,384,1536]{2,1,0:T(8,128)(2,1)S(1)}, bf16[1,384,1536]{2,1,0:T(8,128)(2,1)}, u32[]{:S(2)}) copy-start(bf16[1,384,1536]{2,1,0:T(8,128)(2,1)} %param.7) | copy-start | bytes 3538948
  1.9 1.3 %copy-start.2 = (bf16[1,384,1536]{2,1,0:T(8,128)(2,1)S(1)}, bf16[1,384,1536]{2,1,0:T(8,128)(2,1)}, u32[]{:S(2)}) copy-start(bf16[1,384,1536]{2,1,0:T(8,128)(2,1)} %param.8) | copy-start | bytes 3538948
  4.4 10.0 %collective-permute-start.2 = (bf16[4,2,24,768]{3,2,0,1:T(8,128)(2,1)S(1)}, bf16[4,2,24,768]{3,2,0,1:T(8,128)(2,1)S(1)}, u32[]{:S(2)}, u32[]{:S(2)}) collective-permute-start(bf16[4,2,24,768]{3,2,0,1:T(8,128)(2,1)S(1)} %copy.19), channel_id=1, source_target_pairs={{0,4},{2,6},{4,0},{6,2},{8,12},{10,14},{12,8},{14,10},{16,20},{18,... | collective-permute-start | bytes 884744 | tf_op jit(solution)/shard_map/ppermute | solution.py:33
  7.4 8.9 %collective-permute-start = (bf16[4,2,24,768]{3,2,0,1:T(8,128)(2,1)S(1)}, bf16[4,2,24,768]{3,2,0,1:T(8,128)(2,1)S(1)}, u32[]{:S(2)}, u32[]{:S(2)}) collective-permute-start(bf16[4,2,24,768]{3,2,0,1:T(8,128)(2,1)S(1)} %copy.17), channel_id=1, source_target_pairs={{0,2},{2,0},{4,6},{6,4},{8,10},{10,8},{12,14},{14,12},{16,18},{18,... | collective-permute-start | bytes 884744 | tf_op jit(solution)/shard_map/ppermute | solution.py:33
  14.5 5.2 %collective-permute-start.3 = (bf16[4,24,768]{2,1,0:T(8,128)(2,1)S(1)}, bf16[4,24,768]{2,1,0:T(8,128)(2,1)S(1)}, u32[]{:S(2)}, u32[]{:S(2)}) collective-permute-start(bf16[4,24,768]{2,1,0:T(8,128)(2,1)S(1)} %fusion.5), channel_id=1, source_target_pairs={{0,2},{2,0},{4,6},{6,4},{8,10},{10,8},{12,14},{14,12},{16,18},{18,... | collective-permute-start | bytes 442376 | tf_op jit(solution)/shard_map/ppermute | solution.py:33
  16.4 5.2 %collective-permute-start.1 = (bf16[4,24,768]{2,1,0:T(8,128)(2,1)S(1)}, bf16[4,24,768]{2,1,0:T(8,128)(2,1)S(1)}, u32[]{:S(2)}, u32[]{:S(2)}) collective-permute-start(bf16[4,24,768]{2,1,0:T(8,128)(2,1)S(1)} %fusion.4), channel_id=1, source_target_pairs={{0,4},{2,6},{4,0},{6,2},{8,12},{10,14},{12,8},{14,10},{16,20},{18,... | collective-permute-start | bytes 442376 | tf_op jit(solution)/shard_map/ppermute | solution.py:33
  21.7 4.5 %collective-permute-start.4 = (bf16[24,1536]{1,0:T(8,128)(2,1)S(1)}, bf16[24,1536]{1,0:T(8,128)(2,1)S(1)}, u32[]{:S(2)}, u32[]{:S(2)}) collective-permute-start(bf16[24,1536]{1,0:T(8,128)(2,1)S(1)} %get-tuple-element.77), channel_id=1, source_target_pairs={{0,8},{2,10},{4,12},{6,14},{8,0},{10,2},{12,4},{14,6},{16,24},{18,... | collective-permute-start | bytes 221192 | tf_op jit(solution)/shard_map/ppermute | solution.py:33
  23.3 6.7 %collective-permute-start.5 = (bf16[24,1536]{1,0:T(8,128)(2,1)S(1)}, bf16[24,1536]{1,0:T(8,128)(2,1)S(1)}, u32[]{:S(2)}, u32[]{:S(2)}) collective-permute-start(bf16[24,1536]{1,0:T(8,128)(2,1)S(1)} %get-tuple-element.78), channel_id=1, source_target_pairs={{0,16},{2,18},{4,20},{6,22},{8,24},{10,26},{12,28},{14,30},{16,0},... | collective-permute-start | bytes 221192 | tf_op jit(solution)/shard_map/ppermute | solution.py:33
  25.9 6.3 %collective-permute-start.6 = (bf16[24,1536]{1,0:T(8,128)(2,1)S(1)}, bf16[24,1536]{1,0:T(8,128)(2,1)S(1)}, u32[]{:S(2)}, u32[]{:S(2)}) collective-permute-start(bf16[24,1536]{1,0:T(8,128)(2,1)S(1)} %get-tuple-element.79), channel_id=1, source_target_pairs={{0,24},{2,26},{4,28},{6,30},{8,16},{10,18},{12,20},{14,22},{16,8},... | collective-permute-start | bytes 221192 | tf_op jit(solution)/shard_map/ppermute | solution.py:33
  32.2 6.4 %collective-permute-start.9 = (bf16[24,1536]{1,0:T(8,128)(2,1)S(1)}, bf16[24,1536]{1,0:T(8,128)(2,1)S(1)}, u32[]{:S(2)}, u32[]{:S(2)}) collective-permute-start(bf16[24,1536]{1,0:T(8,128)(2,1)S(1)} %pad_maximum_fusion.10), channel_id=1, source_target_pairs={{0,24},{2,26},{4,28},{6,30},{8,16},{10,18},{12,20},{14,22},{16,8},... | collective-permute-start | bytes 221192 | tf_op jit(solution)/shard_map/ppermute | solution.py:33
  33.1 6.8 %collective-permute-start.8 = (bf16[24,1536]{1,0:T(8,128)(2,1)S(1)}, bf16[24,1536]{1,0:T(8,128)(2,1)S(1)}, u32[]{:S(2)}, u32[]{:S(2)}) collective-permute-start(bf16[24,1536]{1,0:T(8,128)(2,1)S(1)} %pad_maximum_fusion.10), channel_id=1, source_target_pairs={{0,16},{2,18},{4,20},{6,22},{8,24},{10,26},{12,28},{14,30},{16,0},... | collective-permute-start | bytes 221192 | tf_op jit(solution)/shard_map/ppermute | solution.py:33
  34.6 5.4 %collective-permute-start.7 = (bf16[24,1536]{1,0:T(8,128)(2,1)S(1)}, bf16[24,1536]{1,0:T(8,128)(2,1)S(1)}, u32[]{:S(2)}, u32[]{:S(2)}) collective-permute-start(bf16[24,1536]{1,0:T(8,128)(2,1)S(1)} %pad_maximum_fusion.10), channel_id=1, source_target_pairs={{0,8},{2,10},{4,12},{6,14},{8,0},{10,2},{12,4},{14,6},{16,24},{18,... | collective-permute-start | bytes 221192 | tf_op jit(solution)/shard_map/ppermute | solution.py:33
  40.0 1.4 %copy-start.1 = (bf16[1,384,1536]{2,1,0:T(8,128)(2,1)S(1)}, bf16[1,384,1536]{2,1,0:T(8,128)(2,1)}, u32[]{:S(2)}) copy-start(bf16[1,384,1536]{2,1,0:T(8,128)(2,1)} %param.7) | copy-start | bytes 3538948
  40.1 6.3 %collective-permute-start.12 = (bf16[4,24,768]{2,1,0:T(8,128)(2,1)S(1)}, bf16[4,24,768]{2,1,0:T(8,128)(2,1)S(1)}, u32[]{:S(2)}, u32[]{:S(2)}) collective-permute-start(bf16[4,24,768]{2,1,0:T(8,128)(2,1)S(1)} %get-tuple-element.82), channel_id=1, source_target_pairs={{0,2},{2,0},{4,6},{6,4},{8,10},{10,8},{12,14},{14,12},{16,18},{18,... | collective-permute-start | bytes 442376 | tf_op jit(solution)/shard_map/ppermute | solution.py:33
  41.6 6.6 %collective-permute-start.10 = (bf16[4,24,768]{2,1,0:T(8,128)(2,1)S(1)}, bf16[4,24,768]{2,1,0:T(8,128)(2,1)S(1)}, u32[]{:S(2)}, u32[]{:S(2)}) collective-permute-start(bf16[4,24,768]{2,1,0:T(8,128)(2,1)S(1)} %get-tuple-element.83), channel_id=1, source_target_pairs={{0,4},{2,6},{4,0},{6,2},{8,12},{10,14},{12,8},{14,10},{16,20},{18,... | collective-permute-start | bytes 442376 | tf_op jit(solution)/shard_map/ppermute | solution.py:33
  46.5 6.8 %collective-permute-start.13 = (bf16[4,2,24,768]{3,2,0,1:T(8,128)(2,1)S(1)}, bf16[4,2,24,768]{3,2,0,1:T(8,128)(2,1)S(1)}, u32[]{:S(2)}, u32[]{:S(2)}) collective-permute-start(bf16[4,2,24,768]{3,2,0,1:T(8,128)(2,1)S(1)} %reverse_select_fusion.2), channel_id=1, source_target_pairs={{0,4},{2,6},{4,0},{6,2},{8,12},{10,14},{12,8},{14,10},{16,20},{18,... | collective-permute-start | bytes 884744 | tf_op jit(solution)/shard_map/ppermute | solution.py:33
  48.4 6.8 %collective-permute-start.11 = (bf16[4,2,24,768]{3,2,1,0:T(8,128)(2,1)S(1)}, bf16[4,2,24,768]{3,2,1,0:T(8,128)(2,1)S(1)}, u32[]{:S(2)}, u32[]{:S(2)}) collective-permute-start(bf16[4,2,24,768]{3,2,1,0:T(8,128)(2,1)S(1)} %reverse_select_fusion.3), channel_id=1, source_target_pairs={{0,2},{2,0},{4,6},{6,4},{8,10},{10,8},{12,14},{14,12},{16,18},{18,... | collective-permute-start | bytes 884744 | tf_op jit(solution)/shard_map/ppermute | solution.py:33
  55.5 0.7 copy-start.8
  55.5 0.8 copy-start.10
  55.5 0.9 copy-start.12
  55.5 1.0 copy-start.14
  56.5 1.3 %copy-start.4 = (bf16[768,768]{1,0:T(8,128)(2,1)S(1)}, bf16[768,768]{1,0:T(8,128)(2,1)}, u32[]{:S(2)}) copy-start(bf16[768,768]{1,0:T(8,128)(2,1)} %constant.164.clone.table_ref) | copy-start | bytes 3538948
  56.6 2.9 %collective-permute-start.14 = (bf16[768,768]{1,0:T(8,128)(2,1)S(1)}, bf16[768,768]{1,0:T(8,128)(2,1)S(1)}, u32[]{:S(2)}, u32[]{:S(2)}) collective-permute-start(bf16[768,768]{1,0:T(8,128)(2,1)S(1)} %pad_maximum_fusion.1.shaped_ref), channel_id=1, source_target_pairs={{0,1},{1,0},{2,3},{3,2},{4,5},{5,4},{6,7},{7,6},{8,9},{9,8},{10,11... | collective-permute-start | bytes 3538952 | tf_op jit(solution)/shard_map/ppermute | solution.py:279
  57.8 1.7 %copy-start.3 = (bf16[768,768]{1,0:T(8,128)(2,1)S(1)}, bf16[768,768]{1,0:T(8,128)(2,1)}, u32[]{:S(2)}) copy-start(bf16[768,768]{1,0:T(8,128)(2,1)} %constant.165.clone.table_ref) | copy-start | bytes 3538948
  60.6 18.5 %copy-start.6 = (bf16[768,768]{1,0:T(8,128)(2,1)S(1)}, bf16[768,768]{1,0:T(8,128)(2,1)}, u32[]{:S(2)}) copy-start(bf16[768,768]{1,0:T(8,128)(2,1)} %constant.163.clone.refs_2_.im_ref) | copy-start | bytes 3538948
  60.6 18.5 %copy-start.7 = (bf16[768,768]{1,0:T(8,128)(2,1)S(1)}, bf16[768,768]{1,0:T(8,128)(2,1)}, u32[]{:S(2)}) copy-start(bf16[768,768]{1,0:T(8,128)(2,1)} %constant.162.clone.refs_1_.re_ref) | copy-start | bytes 3538948
  60.8 9.2 %collective-permute-start.29 = (bf16[48,768]{1,0:T(8,128)(2,1)S(1)}, bf16[48,768]{1,0:T(8,128)(2,1)S(1)}, u32[]{:S(2)}, u32[]{:S(2)}) collective-permute-start(bf16[48,768]{1,0:T(8,128)(2,1)S(1)} %get-tuple-element.57), channel_id=1, source_target_pairs={{0,30},{2,28},{4,26},{6,24},{8,22},{10,20},{12,18},{14,16},{16,14}... | collective-permute-start | bytes 221192 | tf_op jit(solution)/shard_map/ppermute | solution.py:33
  63.2 9.1 %collective-permute-start.28 = (bf16[48,768]{1,0:T(8,128)(2,1)S(1)}, bf16[48,768]{1,0:T(8,128)(2,1)S(1)}, u32[]{:S(2)}, u32[]{:S(2)}) collective-permute-start(bf16[48,768]{1,0:T(8,128)(2,1)S(1)} %get-tuple-element.58), channel_id=1, source_target_pairs={{0,14},{2,12},{4,10},{6,8},{8,6},{10,4},{12,2},{14,0},{16,30},{18,... | collective-permute-start | bytes 221192 | tf_op jit(solution)/shard_map/ppermute | solution.py:33
  63.9 10.1 %collective-permute-start.27 = (bf16[48,768]{1,0:T(8,128)(2,1)S(1)}, bf16[48,768]{1,0:T(8,128)(2,1)S(1)}, u32[]{:S(2)}, u32[]{:S(2)}) collective-permute-start(bf16[48,768]{1,0:T(8,128)(2,1)S(1)} %get-tuple-element.59), channel_id=1, source_target_pairs={{0,28},{2,30},{4,24},{6,26},{8,20},{10,22},{12,16},{14,18},{16,12}... | collective-permute-start | bytes 221192 | tf_op jit(solution)/shard_map/ppermute | solution.py:33
  66.8 7.7 %collective-permute-start.26 = (bf16[48,768]{1,0:T(8,128)(2,1)S(1)}, bf16[48,768]{1,0:T(8,128)(2,1)S(1)}, u32[]{:S(2)}, u32[]{:S(2)}) collective-permute-start(bf16[48,768]{1,0:T(8,128)(2,1)S(1)} %get-tuple-element.60), channel_id=1, source_target_pairs={{0,12},{2,14},{4,8},{6,10},{8,4},{10,6},{12,0},{14,2},{16,28},{18,... | collective-permute-start | bytes 221192 | tf_op jit(solution)/shard_map/ppermute | solution.py:33
  68.5 8.8 %collective-permute-start.25 = (bf16[48,768]{1,0:T(8,128)(2,1)S(1)}, bf16[48,768]{1,0:T(8,128)(2,1)S(1)}, u32[]{:S(2)}, u32[]{:S(2)}) collective-permute-start(bf16[48,768]{1,0:T(8,128)(2,1)S(1)} %get-tuple-element.61), channel_id=1, source_target_pairs={{0,26},{2,24},{4,30},{6,28},{8,18},{10,16},{12,22},{14,20},{16,10}... | collective-permute-start | bytes 221192 | tf_op jit(solution)/shard_map/ppermute | solution.py:33
  69.9 12.1 %collective-permute-start.24 = (bf16[48,768]{1,0:T(8,128)(2,1)S(1)}, bf16[48,768]{1,0:T(8,128)(2,1)S(1)}, u32[]{:S(2)}, u32[]{:S(2)}) collective-permute-start(bf16[48,768]{1,0:T(8,128)(2,1)S(1)} %get-tuple-element.62), channel_id=1, source_target_pairs={{0,10},{2,8},{4,14},{6,12},{8,2},{10,0},{12,6},{14,4},{16,26},{18,... | collective-permute-start | bytes 221192 | tf_op jit(solution)/shard_map/ppermute | solution.py:33
  72.3 11.0 %collective-permute-start.23 = (bf16[48,768]{1,0:T(8,128)(2,1)S(1)}, bf16[48,768]{1,0:T(8,128)(2,1)S(1)}, u32[]{:S(2)}, u32[]{:S(2)}) collective-permute-start(bf16[48,768]{1,0:T(8,128)(2,1)S(1)} %get-tuple-element.63), channel_id=1, source_target_pairs={{0,24},{2,26},{4,28},{6,30},{8,16},{10,18},{12,20},{14,22},{16,8},... | collective-permute-start | bytes 221192 | tf_op jit(solution)/shard_map/ppermute | solution.py:33
  74.0 10.3 %collective-permute-start.22 = (bf16[48,768]{1,0:T(8,128)(2,1)S(1)}, bf16[48,768]{1,0:T(8,128)(2,1)S(1)}, u32[]{:S(2)}, u32[]{:S(2)}) collective-permute-start(bf16[48,768]{1,0:T(8,128)(2,1)S(1)} %get-tuple-element.64), channel_id=1, source_target_pairs={{0,8},{2,10},{4,12},{6,14},{8,0},{10,2},{12,4},{14,6},{16,24},{18,... | collective-permute-start | bytes 221192 | tf_op jit(solution)/shard_map/ppermute | solution.py:33
  74.5 11.5 %collective-permute-start.21 = (bf16[48,768]{1,0:T(8,128)(2,1)S(1)}, bf16[48,768]{1,0:T(8,128)(2,1)S(1)}, u32[]{:S(2)}, u32[]{:S(2)}) collective-permute-start(bf16[48,768]{1,0:T(8,128)(2,1)S(1)} %get-tuple-element.65), channel_id=1, source_target_pairs={{0,22},{2,20},{4,18},{6,16},{8,30},{10,28},{12,26},{14,24},{16,6},... | collective-permute-start | bytes 221192 | tf_op jit(solution)/shard_map/ppermute | solution.py:33
  77.3 11.4 %copy-start.5 = (bf16[2,16,24,768]{3,2,1,0:T(8,128)(2,1)S(1)}, bf16[2,16,24,768]{3,2,1,0:T(8,128)(2,1)}, u32[]{:S(2)}) copy-start(bf16[2,16,24,768]{3,2,1,0:T(8,128)(2,1)} %param.9) | copy-start | bytes 3538948
  77.3 10.7 %collective-permute-start.20 = (bf16[48,768]{1,0:T(8,128)(2,1)S(1)}, bf16[48,768]{1,0:T(8,128)(2,1)S(1)}, u32[]{:S(2)}, u32[]{:S(2)}) collective-permute-start(bf16[48,768]{1,0:T(8,128)(2,1)S(1)} %get-tuple-element.66), channel_id=1, source_target_pairs={{0,6},{2,4},{4,2},{6,0},{8,14},{10,12},{12,10},{14,8},{16,22},{18,... | collective-permute-start | bytes 221192 | tf_op jit(solution)/shard_map/ppermute | solution.py:33
  82.1 8.6 %collective-permute-start.19 = (bf16[48,768]{1,0:T(8,128)(2,1)S(1)}, bf16[48,768]{1,0:T(8,128)(2,1)S(1)}, u32[]{:S(2)}, u32[]{:S(2)}) collective-permute-start(bf16[48,768]{1,0:T(8,128)(2,1)S(1)} %get-tuple-element.67), channel_id=1, source_target_pairs={{0,20},{2,22},{4,16},{6,18},{8,28},{10,30},{12,24},{14,26},{16,4},... | collective-permute-start | bytes 221192 | tf_op jit(solution)/shard_map/ppermute | solution.py:33
  83.3 7.4 %collective-permute-start.18 = (bf16[48,768]{1,0:T(8,128)(2,1)S(1)}, bf16[48,768]{1,0:T(8,128)(2,1)S(1)}, u32[]{:S(2)}, u32[]{:S(2)}) collective-permute-start(bf16[48,768]{1,0:T(8,128)(2,1)S(1)} %get-tuple-element.68), channel_id=1, source_target_pairs={{0,4},{2,6},{4,0},{6,2},{8,12},{10,14},{12,8},{14,10},{16,20},{18,... | collective-permute-start | bytes 221192 | tf_op jit(solution)/shard_map/ppermute | solution.py:33
  84.3 8.2 %collective-permute-start.17 = (bf16[48,768]{1,0:T(8,128)(2,1)S(1)}, bf16[48,768]{1,0:T(8,128)(2,1)S(1)}, u32[]{:S(2)}, u32[]{:S(2)}) collective-permute-start(bf16[48,768]{1,0:T(8,128)(2,1)S(1)} %get-tuple-element.69), channel_id=1, source_target_pairs={{0,18},{2,16},{4,22},{6,20},{8,26},{10,24},{12,30},{14,28},{16,2},... | collective-permute-start | bytes 221192 | tf_op jit(solution)/shard_map/ppermute | solution.py:33
  86.0 6.6 %collective-permute-start.16 = (bf16[48,768]{1,0:T(8,128)(2,1)S(1)}, bf16[48,768]{1,0:T(8,128)(2,1)S(1)}, u32[]{:S(2)}, u32[]{:S(2)}) collective-permute-start(bf16[48,768]{1,0:T(8,128)(2,1)S(1)} %get-tuple-element.70), channel_id=1, source_target_pairs={{0,2},{2,0},{4,6},{6,4},{8,10},{10,8},{12,14},{14,12},{16,18},{18,... | collective-permute-start | bytes 221192 | tf_op jit(solution)/shard_map/ppermute | solution.py:33
  88.0 6.0 %collective-permute-start.15 = (bf16[48,768]{1,0:T(8,128)(2,1)S(1)}, bf16[48,768]{1,0:T(8,128)(2,1)S(1)}, u32[]{:S(2)}, u32[]{:S(2)}) collective-permute-start(bf16[48,768]{1,0:T(8,128)(2,1)S(1)} %get-tuple-element.71), channel_id=1, source_target_pairs={{0,16},{2,18},{4,20},{6,22},{8,24},{10,26},{12,28},{14,30},{16,0},... | collective-permute-start | bytes 221192 | tf_op jit(solution)/shard_map/ppermute | solution.py:33
  94.2 5.3 %copy-start.9 = (bf16[384,384]{1,0:T(8,128)(2,1)S(1)}, bf16[384,384]{1,0:T(8,128)(2,1)}, u32[]{:S(2)}) copy-start(bf16[384,384]{1,0:T(8,128)(2,1)} %copy-done.8) | copy-start | bytes 884740
  94.2 5.3 %copy-start.11 = (bf16[384,384]{1,0:T(8,128)(2,1)S(1)}, bf16[384,384]{1,0:T(8,128)(2,1)}, u32[]{:S(2)}) copy-start(bf16[384,384]{1,0:T(8,128)(2,1)} %copy-done.10) | copy-start | bytes 884740
  94.2 5.3 %copy-start.13 = (bf16[384,384]{1,0:T(8,128)(2,1)S(1)}, bf16[384,384]{1,0:T(8,128)(2,1)}, u32[]{:S(2)}) copy-start(bf16[384,384]{1,0:T(8,128)(2,1)} %copy-done.12) | copy-start | bytes 884740
  94.3 5.3 %copy-start.15 = (bf16[384,384]{1,0:T(8,128)(2,1)S(1)}, bf16[384,384]{1,0:T(8,128)(2,1)}, u32[]{:S(2)}) copy-start(bf16[384,384]{1,0:T(8,128)(2,1)} %copy-done.14) | copy-start | bytes 884740
  96.6 10.0 %all-to-all-start = ((f32[32,1,16]{2,1,0:T(1,128)}), f32[32,1,16]{2,1,0:T(1,128)S(1)}, u32[]{:S(2)}, u32[]{:S(2)}) async-start(f32[32,1,16]{2,1,0:T(1,128)} %bitcast.53), calls=%async_computation | async-start | bytes 32768 | tf_op jit(solution)/shard_map/all_to_all | solution.py:327

commit v7 on v6

--- a/solution.py
+++ b/solution.py
@@ -206,6 +206,13 @@
     half = grid_size // 2
     matmul = 2 * local_rows * double_width * double_width
 
+    c_re, c_im = propagator(grid_size)
+    full_re, full_im = jnp.asarray(c_re, bf16), jnp.asarray(c_im, bf16)
+    column_shape = (2 * local_rows, grid_size)
+    seen = kernel_call(
+        targets_kernel, column_shape, bf16, matmul, (targets.reshape(column_shape), full_re, full_im)
+    )
+
     me = lax.axis_index("modes")
     owns = [me // stride % size for stride, size in digits]
     last = len(digits) - 1
@@ -219,6 +226,7 @@
             [bf16, f32, bf16, f32],
             8 * local_rows * double_width,
             (forward[0], backward[0]),
+            grant=52,
             in_specs=[pl.BlockSpec(memory_space=pltpu.HBM)] * 2,
             scratch_shapes=[pltpu.VMEM((local_rows, double_width), bf16)] * 2
             + [pltpu.SemaphoreType.DMA((2 * local_rows // (4 * block_rows),))],
@@ -241,6 +249,8 @@
             else:
                 send, keep = split_digit(partial, owns[d], size, axes[d])
             got = [exchange(v, (e + 1) * stride, count) for e, v in enumerate(send)]
+            if at == 0 and part == 0:
+                got, seen = lax.optimization_barrier((got, seen))
             partial = reduce_digit(keep, got)
             axes = [a - (a > axes[d]) for a in axes]
         kept.append(partial)
@@ -278,8 +288,6 @@
     ).astype(bf16)
     other = lax.ppermute(shaped, "rows", [(0, 1), (1, 0)])
 
-    c_re, c_im = propagator(grid_size)
-    full_re, full_im = jnp.asarray(c_re, bf16), jnp.asarray(c_im, bf16)
     owners = count if block_rows % 8 == 0 else 1
     order = np.arange(local_rows).reshape(owners, -1)
 
@@ -288,11 +296,10 @@
         rows = np.stack([np.concatenate([real, -imag], 1)[order], np.concatenate([imag, real], 1)[order]], 1)
         return jnp.asarray(rows.reshape(2 * local_rows, -1), bf16)
 
-    column_shape = (2 * local_rows, grid_size)
     columns = kernel_call(
         own_kernel, column_shape, f32, matmul // 2, (table(slice(0, local_rows)), shaped)
     )
-    columns, other = lax.optimization_barrier((columns, other))
+    columns, other, phase_plane = lax.optimization_barrier((columns, other, phase_plane))
     columns = kernel_call(
         other_kernel, column_shape, bf16, matmul // 2, (table(slice(local_rows, None)), other, columns)
     )
@@ -304,25 +311,20 @@
     else:
         pixels = (lax.all_to_all(blocks, "modes", 0, 0, tiled=True),)
 
+    term = kernel_call(
+        lambda *refs: coupling_kernel(block_rows, len(pixels) > 1, *refs),
+        (2 * mode_total, mode_total),
+        f32,
+        matmul,
+        (jnp.concatenate(pixels, 0).reshape(column_shape), seen),
+    )
+    columns, term = lax.optimization_barrier((columns, term))
     output_fields = kernel_call(
         lambda *refs: fields_kernel(block_rows, *refs),
         (local_rows, double_width),
         bf16,
         matmul,
         (columns, full_re, full_im),
-    )
-    targets, output_fields = lax.optimization_barrier((targets, output_fields))
-    seen = kernel_call(
-        targets_kernel, column_shape, bf16, matmul, (targets.reshape(column_shape), full_re, full_im)
-    )
-    pixels, output_fields, seen = lax.optimization_barrier((pixels, output_fields, seen))
-
-    term = kernel_call(
-        lambda *refs: coupling_kernel(block_rows, len(pixels) > 1, *refs),
-        (2 * mode_total, mode_total),
-        f32,
-        matmul,
-        (jnp.concatenate(pixels, 0).reshape(column_shape), seen),
     )
     pieces = lax.all_to_all(term, ("modes", "rows"), 0, 0, tiled=True)
     coupling = jnp.sum(pieces, 0, keepdims=True)

time: 108 us -> 148 us (1.37)
  waiting for transfers between devices: 39.4 us -> 87.5 us
  starting transfers between devices: 47.8 us -> 36.8 us
  other arithmetic: 3.38 us -> 5.3 us
    ppermute x29, waiting for transfers between devices: 32.7 us -> 83.4 us  [exchange(): lax.ppermute(values, 'modes', [(i, i ^ offset) for i in range(count)])]
    ppermute x29, starting transfers between devices: 44.9 us -> 34.2 us  [exchange(): lax.ppermute(values, 'modes', [(i, i ^ offset) for i in range(count)])]
    add x5, other arithmetic: 0.19 us -> 2.12 us  [reduce_digit(): keep = keep + g.astype(f32)]
    all_to_all x1, waiting for transfers between devices: 6 us -> 4.12 us  [local(): pieces = lax.all_to_all(term, ('modes', 'rows'), 0, 0, tiled=True)]
    unnamed x47 -> x51, local copies, waits for them, and re-layouts: 4.24 us -> 3.88 us
  transfers between devices with their start and end apart: 31 -> 31, of which waited for: 16 -> 22; matrix products, arithmetic and copies ran while one was open for 2% -> 3% of each run, Pallas kernels for 6% -> 4%
where the time goes in v7:
time: 148 us
  waiting for transfers between devices  87.5 us (59%)
  starting transfers between devices  36.8 us (25%)
  Pallas kernels  11.5 us (8%)
  local copies, waits for them, and re-layouts  5.79 us (4%)
  other arithmetic  5.3 us (4%)
    ppermute x29, waiting for transfers between devices, exchange(): lax.ppermute(values, 'modes', [(i, i ^ offset) for i in range(count)])  83.4 us
    ppermute x29, starting transfers between devices, exchange(): lax.ppermute(values, 'modes', [(i, i ^ offset) for i in range(count)])  34.2 us
    pallas_call x6, Pallas kernels, kernel_call(): pl.pallas_call(kernel, out_shape=out_shape, compiler_params=pltpu.Compile...  11.5 us
    all_to_all x1, waiting for transfers between devices, local(): pieces = lax.all_to_all(term, ('modes', 'rows'), 0, 0, tiled=True)  4.12 us
    unnamed x51, local copies, waits for them, and re-layouts  3.88 us
  transfers between devices with their start and end apart: 31, of which 22 were waited for; matrix products, arithmetic and copies ran while one was open for 3% of the time, Pallas kernels for 4%

profile of v7, /device:TPU:0, one launch (start us, length us, event | category | flops | bytes accessed | tf_op | source)
XLA Modules:
  0.0 148.0 jit_solution(5841530060409398225)
XLA Ops:
  0.6 1.9 %shard_map.94 = (bf16[192,768]{1,0:T(8,128)(2,1)S(1)}, f32[192,768]{1,0:T(8,128)S(1)}, bf16[192,768]{1,0:T(8,128)(2,1)S(1)}, f32[192,768]{1,0:T(8,128)S(1)}) custom-call(bf16[384,1536]{1,0:T(8,128)(2,1)} %bitcast.100, bf16[384,1536]{1,0:T(8,128)(2,1)} %bitcast.103), custom_call_target="tpu_custom_call" | custom-call | flops 4718592 | bytes 4194304 | tf_op jit(solution)/shard_map/pallas_call | solution.py:189
  3.3 3.0 %collective-permute-start.2 = (bf16[4,2,24,768]{3,2,0,1:T(8,128)(2,1)}, bf16[4,2,24,768]{3,2,0,1:T(8,128)(2,1)}, u32[]{:S(2)}, u32[]{:S(2)}) collective-permute-start(bf16[4,2,24,768]{3,2,0,1:T(8,128)(2,1)} %copy.19), channel_id=1, source_target_pairs={{0,4},{2,6},{4,0},{6,2},{8,12},{10,14},{12,8},{14,10},{16,20},{18,... | collective-permute-start | bytes 884744 | tf_op jit(solution)/shard_map/ppermute | solution.py:33
  7.0 1.5 %collective-permute-start = (bf16[4,2,24,768]{3,2,0,1:T(8,128)(2,1)}, bf16[4,2,24,768]{3,2,0,1:T(8,128)(2,1)}, u32[]{:S(2)}, u32[]{:S(2)}) collective-permute-start(bf16[4,2,24,768]{3,2,0,1:T(8,128)(2,1)} %copy.17), channel_id=1, source_target_pairs={{0,2},{2,0},{4,6},{6,4},{8,10},{10,8},{12,14},{14,12},{16,18},{18,... | collective-permute-start | bytes 884744 | tf_op jit(solution)/shard_map/ppermute | solution.py:33
  8.5 1.3 copy-done.5
  9.8 2.0 %shard_map.95.refs_1_ = bf16[768,768]{1,0:T(8,128)(2,1)S(1)} custom-call(bf16[768,768]{1,0:T(8,128)(2,1)S(1)} %bitcast.99, bf16[768,768]{1,0:T(8,128)(2,1)S(1)} %copy-done.5, bf16[768,768]{1,0:T(8,128)(2,1)S(1)} %copy-done.3), custom_call_target="tpu_custom_call" | custom-call | flops 1811939328 | bytes 4194304 | tf_op jit(solution)/shard_map/pallas_call | solution.py:189
  11.8 1.8 %collective-permute-done.2 = bf16[4,2,24,768]{3,2,0,1:T(8,128)(2,1)} collective-permute-done((bf16[4,2,24,768]{3,2,0,1:T(8,128)(2,1)}, bf16[4,2,24,768]{3,2,0,1:T(8,128)(2,1)}, u32[]{:S(2)}, u32[]{:S(2)}) %collective-permute-start.2) | collective-permute-done | bytes 294944 | tf_op jit(solution)/shard_map/ppermute | solution.py:33
  13.6 1.0 copy_add_fusion
  14.6 1.8 %collective-permute-start.3 = (bf16[4,24,768]{2,1,0:T(8,128)(2,1)S(1)}, bf16[4,24,768]{2,1,0:T(8,128)(2,1)S(1)}, u32[]{:S(2)}, u32[]{:S(2)}) collective-permute-start(bf16[4,24,768]{2,1,0:T(8,128)(2,1)S(1)} %fusion.5), channel_id=1, source_target_pairs={{0,2},{2,0},{4,6},{6,4},{8,10},{10,8},{12,14},{14,12},{16,18},{18,... | collective-permute-start | bytes 442376 | tf_op jit(solution)/shard_map/ppermute | solution.py:33
  16.4 1.0 copy_add_fusion.1
  17.5 1.6 %collective-permute-start.1 = (bf16[4,24,768]{2,1,0:T(8,128)(2,1)S(1)}, bf16[4,24,768]{2,1,0:T(8,128)(2,1)S(1)}, u32[]{:S(2)}, u32[]{:S(2)}) collective-permute-start(bf16[4,24,768]{2,1,0:T(8,128)(2,1)S(1)} %fusion.4), channel_id=1, source_target_pairs={{0,4},{2,6},{4,0},{6,2},{8,12},{10,14},{12,8},{14,10},{16,20},{18,... | collective-permute-start | bytes 442376 | tf_op jit(solution)/shard_map/ppermute | solution.py:33
  19.9 2.8 %collective-permute-done.1 = bf16[4,24,768]{2,1,0:T(8,128)(2,1)S(1)} collective-permute-done((bf16[4,24,768]{2,1,0:T(8,128)(2,1)S(1)}, bf16[4,24,768]{2,1,0:T(8,128)(2,1)S(1)}, u32[]{:S(2)}, u32[]{:S(2)}) %collective-permute-start.1) | collective-permute-done | bytes 147488 | tf_op jit(solution)/shard_map/ppermute | solution.py:33
  22.8 1.6 %collective-permute-start.4 = (bf16[24,1536]{1,0:T(8,128)(2,1)S(1)}, bf16[24,1536]{1,0:T(8,128)(2,1)S(1)}, u32[]{:S(2)}, u32[]{:S(2)}) collective-permute-start(bf16[24,1536]{1,0:T(8,128)(2,1)S(1)} %get-tuple-element.46), channel_id=1, source_target_pairs={{0,8},{2,10},{4,12},{6,14},{8,0},{10,2},{12,4},{14,6},{16,24},{18,... | collective-permute-start | bytes 221192 | tf_op jit(solution)/shard_map/ppermute | solution.py:33
  24.4 2.6 %collective-permute-start.5 = (bf16[24,1536]{1,0:T(8,128)(2,1)S(1)}, bf16[24,1536]{1,0:T(8,128)(2,1)S(1)}, u32[]{:S(2)}, u32[]{:S(2)}) collective-permute-start(bf16[24,1536]{1,0:T(8,128)(2,1)S(1)} %get-tuple-element.47), channel_id=1, source_target_pairs={{0,16},{2,18},{4,20},{6,22},{8,24},{10,26},{12,28},{14,30},{16,0},... | collective-permute-start | bytes 221192 | tf_op jit(solution)/shard_map/ppermute | solution.py:33
  27.3 3.7 %collective-permute-done.5 = bf16[24,1536]{1,0:T(8,128)(2,1)S(1)} collective-permute-done((bf16[24,1536]{1,0:T(8,128)(2,1)S(1)}, bf16[24,1536]{1,0:T(8,128)(2,1)S(1)}, u32[]{:S(2)}, u32[]{:S(2)}) %collective-permute-start.5) | collective-permute-done | bytes 73760 | tf_op jit(solution)/shard_map/ppermute | solution.py:33
  31.0 2.3 %collective-permute-done.6 = bf16[24,1536]{1,0:T(8,128)(2,1)S(1)} collective-permute-done((bf16[24,1536]{1,0:T(8,128)(2,1)S(1)}, bf16[24,1536]{1,0:T(8,128)(2,1)S(1)}, u32[]{:S(2)}, u32[]{:S(2)}) %collective-permute-start.6) | collective-permute-done | bytes 73760 | tf_op jit(solution)/shard_map/ppermute | solution.py:33
  34.6 3.2 %collective-permute-start.7 = (bf16[24,1536]{1,0:T(8,128)(2,1)S(1)}, bf16[24,1536]{1,0:T(8,128)(2,1)S(1)}, u32[]{:S(2)}, u32[]{:S(2)}) collective-permute-start(bf16[24,1536]{1,0:T(8,128)(2,1)S(1)} %pad_maximum_fusion.10), channel_id=1, source_target_pairs={{0,8},{2,10},{4,12},{6,14},{8,0},{10,2},{12,4},{14,6},{16,24},{18,... | collective-permute-start | bytes 221192 | tf_op jit(solution)/shard_map/ppermute | solution.py:33
  37.8 1.9 %collective-permute-done.9 = bf16[24,1536]{1,0:T(8,128)(2,1)S(1)} collective-permute-done((bf16[24,1536]{1,0:T(8,128)(2,1)S(1)}, bf16[24,1536]{1,0:T(8,128)(2,1)S(1)}, u32[]{:S(2)}, u32[]{:S(2)}) %collective-permute-start.9) | collective-permute-done | bytes 73760 | tf_op jit(solution)/shard_map/ppermute | solution.py:33
  39.7 1.3 collective-permute-done.8
  42.6 1.6 %collective-permute-start.10 = (bf16[4,24,768]{2,1,0:T(8,128)(2,1)S(1)}, bf16[4,24,768]{2,1,0:T(8,128)(2,1)S(1)}, u32[]{:S(2)}, u32[]{:S(2)}) collective-permute-start(bf16[4,24,768]{2,1,0:T(8,128)(2,1)S(1)} %get-tuple-element.52), channel_id=1, source_target_pairs={{0,4},{2,6},{4,0},{6,2},{8,12},{10,14},{12,8},{14,10},{16,20},{18,... | collective-permute-start | bytes 442376 | tf_op jit(solution)/shard_map/ppermute | solution.py:33
  44.2 3.7 %collective-permute-done.12 = bf16[4,24,768]{2,1,0:T(8,128)(2,1)S(1)} collective-permute-done((bf16[4,24,768]{2,1,0:T(8,128)(2,1)S(1)}, bf16[4,24,768]{2,1,0:T(8,128)(2,1)S(1)}, u32[]{:S(2)}, u32[]{:S(2)}) %collective-permute-start.12) | collective-permute-done | bytes 147488 | tf_op jit(solution)/shard_map/ppermute | solution.py:33
  48.0 1.7 %collective-permute-start.13 = (bf16[4,2,24,768]{3,2,0,1:T(8,128)(2,1)S(1)}, bf16[4,2,24,768]{3,2,0,1:T(8,128)(2,1)S(1)}, u32[]{:S(2)}, u32[]{:S(2)}) collective-permute-start(bf16[4,2,24,768]{3,2,0,1:T(8,128)(2,1)S(1)} %reverse_select_fusion.2), channel_id=1, source_target_pairs={{0,4},{2,6},{4,0},{6,2},{8,12},{10,14},{12,8},{14,10},{16,20},{18,... | collective-permute-start | bytes 884744 | tf_op jit(solution)/shard_map/ppermute | solution.py:33
  50.2 4.6 %collective-permute-done.13 = bf16[4,2,24,768]{3,2,0,1:T(8,128)(2,1)S(1)} collective-permute-done((bf16[4,2,24,768]{3,2,0,1:T(8,128)(2,1)S(1)}, bf16[4,2,24,768]{3,2,0,1:T(8,128)(2,1)S(1)}, u32[]{:S(2)}, u32[]{:S(2)}) %collective-permute-start.13) | collective-permute-done | bytes 294944 | tf_op jit(solution)/shard_map/ppermute | solution.py:33
  55.0 1.6 %collective-permute-done.11 = bf16[4,2,24,768]{3,2,1,0:T(8,128)(2,1)S(1)} collective-permute-done((bf16[4,2,24,768]{3,2,1,0:T(8,128)(2,1)S(1)}, bf16[4,2,24,768]{3,2,1,0:T(8,128)(2,1)S(1)}, u32[]{:S(2)}, u32[]{:S(2)}) %collective-permute-start.11) | collective-permute-done | bytes 294944 | tf_op jit(solution)/shard_map/ppermute | solution.py:33
  58.2 1.0 copy-done.1
  59.2 1.1 shard_map.96.own_ref
  60.4 1.1 pad_maximum_fusion.1
  62.1 1.1 shard_map.97.refs_0_
  63.4 1.8 %collective-permute-start.29 = (bf16[48,768]{1,0:T(8,128)(2,1)S(1)}, bf16[48,768]{1,0:T(8,128)(2,1)S(1)}, u32[]{:S(2)}, u32[]{:S(2)}) collective-permute-start(bf16[48,768]{1,0:T(8,128)(2,1)S(1)} %get-tuple-element.27), channel_id=1, source_target_pairs={{0,30},{2,28},{4,26},{6,24},{8,22},{10,20},{12,18},{14,16},{16,14}... | collective-permute-start | bytes 221192 | tf_op jit(solution)/shard_map/ppermute | solution.py:33
  65.2 1.4 collective-permute-start.28
  66.5 2.7 %collective-permute-start.27 = (bf16[48,768]{1,0:T(8,128)(2,1)S(1)}, bf16[48,768]{1,0:T(8,128)(2,1)S(1)}, u32[]{:S(2)}, u32[]{:S(2)}) collective-permute-start(bf16[48,768]{1,0:T(8,128)(2,1)S(1)} %get-tuple-element.29), channel_id=1, source_target_pairs={{0,28},{2,30},{4,24},{6,26},{8,20},{10,22},{12,16},{14,18},{16,12}... | collective-permute-start | bytes 221192 | tf_op jit(solution)/shard_map/ppermute | solution.py:33
  69.2 1.9 %collective-permute-start.26 = (bf16[48,768]{1,0:T(8,128)(2,1)S(1)}, bf16[48,768]{1,0:T(8,128)(2,1)S(1)}, u32[]{:S(2)}, u32[]{:S(2)}) collective-permute-start(bf16[48,768]{1,0:T(8,128)(2,1)S(1)} %get-tuple-element.30), channel_id=1, source_target_pairs={{0,12},{2,14},{4,8},{6,10},{8,4},{10,6},{12,0},{14,2},{16,28},{18,... | collective-permute-start | bytes 221192 | tf_op jit(solution)/shard_map/ppermute | solution.py:33
  71.8 5.3 %collective-permute-done.15 = bf16[48,768]{1,0:T(8,128)(2,1)S(1)} collective-permute-done((bf16[48,768]{1,0:T(8,128)(2,1)S(1)}, bf16[48,768]{1,0:T(8,128)(2,1)S(1)}, u32[]{:S(2)}, u32[]{:S(2)}) %collective-permute-start.15) | collective-permute-done | bytes 73760 | tf_op jit(solution)/shard_map/ppermute | solution.py:33
  77.2 4.3 %collective-permute-done.16 = bf16[48,768]{1,0:T(8,128)(2,1)S(1)} collective-permute-done((bf16[48,768]{1,0:T(8,128)(2,1)S(1)}, bf16[48,768]{1,0:T(8,128)(2,1)S(1)}, u32[]{:S(2)}, u32[]{:S(2)}) %collective-permute-start.16) | collective-permute-done | bytes 73760 | tf_op jit(solution)/shard_map/ppermute | solution.py:33
  81.5 6.8 %collective-permute-done.17 = bf16[48,768]{1,0:T(8,128)(2,1)S(1)} collective-permute-done((bf16[48,768]{1,0:T(8,128)(2,1)S(1)}, bf16[48,768]{1,0:T(8,128)(2,1)S(1)}, u32[]{:S(2)}, u32[]{:S(2)}) %collective-permute-start.17) | collective-permute-done | bytes 73760 | tf_op jit(solution)/shard_map/ppermute | solution.py:33
  88.8 4.5 %collective-permute-done.18 = bf16[48,768]{1,0:T(8,128)(2,1)S(1)} collective-permute-done((bf16[48,768]{1,0:T(8,128)(2,1)S(1)}, bf16[48,768]{1,0:T(8,128)(2,1)S(1)}, u32[]{:S(2)}, u32[]{:S(2)}) %collective-permute-start.18) | collective-permute-done | bytes 73760 | tf_op jit(solution)/shard_map/ppermute | solution.py:33
  93.3 6.1 %collective-permute-done.19 = bf16[48,768]{1,0:T(8,128)(2,1)S(1)} collective-permute-done((bf16[48,768]{1,0:T(8,128)(2,1)S(1)}, bf16[48,768]{1,0:T(8,128)(2,1)S(1)}, u32[]{:S(2)}, u32[]{:S(2)}) %collective-permute-start.19) | collective-permute-done | bytes 73760 | tf_op jit(solution)/shard_map/ppermute | solution.py:33
  100.4 4.3 %collective-permute-done.20 = bf16[48,768]{1,0:T(8,128)(2,1)S(1)} collective-permute-done((bf16[48,768]{1,0:T(8,128)(2,1)S(1)}, bf16[48,768]{1,0:T(8,128)(2,1)S(1)}, u32[]{:S(2)}, u32[]{:S(2)}) %collective-permute-start.20) | collective-permute-done | bytes 73760 | tf_op jit(solution)/shard_map/ppermute | solution.py:33
  104.8 7.7 %collective-permute-done.21 = bf16[48,768]{1,0:T(8,128)(2,1)S(1)} collective-permute-done((bf16[48,768]{1,0:T(8,128)(2,1)S(1)}, bf16[48,768]{1,0:T(8,128)(2,1)S(1)}, u32[]{:S(2)}, u32[]{:S(2)}) %collective-permute-start.21) | collective-permute-done | bytes 73760 | tf_op jit(solution)/shard_map/ppermute | solution.py:33
  112.5 4.3 %collective-permute-done.22 = bf16[48,768]{1,0:T(8,128)(2,1)S(1)} collective-permute-done((bf16[48,768]{1,0:T(8,128)(2,1)S(1)}, bf16[48,768]{1,0:T(8,128)(2,1)S(1)}, u32[]{:S(2)}, u32[]{:S(2)}) %collective-permute-start.22) | collective-permute-done | bytes 73760 | tf_op jit(solution)/shard_map/ppermute | solution.py:33
  116.8 1.4 collective-permute-start.23
  118.2 4.8 %collective-permute-done.23 = bf16[48,768]{1,0:T(8,128)(2,1)S(1)} collective-permute-done((bf16[48,768]{1,0:T(8,128)(2,1)S(1)}, bf16[48,768]{1,0:T(8,128)(2,1)S(1)}, u32[]{:S(2)}, u32[]{:S(2)}) %collective-permute-start.23) | collective-permute-done | bytes 73760 | tf_op jit(solution)/shard_map/ppermute | solution.py:33
  123.0 5.2 %collective-permute-done.24 = bf16[48,768]{1,0:T(8,128)(2,1)S(1)} collective-permute-done((bf16[48,768]{1,0:T(8,128)(2,1)S(1)}, bf16[48,768]{1,0:T(8,128)(2,1)S(1)}, u32[]{:S(2)}, u32[]{:S(2)}) %collective-permute-start.24) | collective-permute-done | bytes 73760 | tf_op jit(solution)/shard_map/ppermute | solution.py:33
  128.2 1.6 %collective-permute-start.25 = (bf16[48,768]{1,0:T(8,128)(2,1)S(1)}, bf16[48,768]{1,0:T(8,128)(2,1)S(1)}, u32[]{:S(2)}, u32[]{:S(2)}) collective-permute-start(bf16[48,768]{1,0:T(8,128)(2,1)S(1)} %get-tuple-element.31), channel_id=1, source_target_pairs={{0,26},{2,24},{4,30},{6,28},{8,18},{10,16},{12,22},{14,20},{16,10}... | collective-permute-start | bytes 221192 | tf_op jit(solution)/shard_map/ppermute | solution.py:33
  129.8 5.5 %collective-permute-done.25 = bf16[48,768]{1,0:T(8,128)(2,1)S(1)} collective-permute-done((bf16[48,768]{1,0:T(8,128)(2,1)S(1)}, bf16[48,768]{1,0:T(8,128)(2,1)S(1)}, u32[]{:S(2)}, u32[]{:S(2)}) %collective-permute-start.25) | collective-permute-done | bytes 73760 | tf_op jit(solution)/shard_map/ppermute | solution.py:33
  135.4 2.4 %shard_map.98 = f32[32,16]{1,0:T(8,128)} custom-call(bf16[768,768]{1,0:T(8,128)(2,1)S(1)} %constant_dynamic-update-slice_fusion.refs_0_, bf16[768,768]{1,0:T(8,128)(2,1)S(1)} %copy-done.8), custom_call_target="tpu_custom_call" | custom-call | flops 1811939328 | bytes 4194304 | tf_op jit(solution)/shard_map/pallas_call | solution.py:189
  137.8 2.5 %all-to-all-start = ((f32[32,1,16]{2,1,0:T(1,128)}), f32[32,1,16]{2,1,0:T(1,128)S(1)}, u32[]{:S(2)}, u32[]{:S(2)}) async-start(f32[32,1,16]{2,1,0:T(1,128)} %bitcast.53), calls=%async_computation | async-start | bytes 32768 | tf_op jit(solution)/shard_map/all_to_all | solution.py:329
  140.4 3.0 %shard_map.99 = bf16[384,1536]{1,0:T(8,128)(2,1)} custom-call(bf16[768,768]{1,0:T(8,128)(2,1)S(1)} %shard_map.97.refs_0_, bf16[768,768]{1,0:T(8,128)(2,1)S(1)} %copy-done.6, bf16[768,768]{1,0:T(8,128)(2,1)S(1)} %copy-done.4), custom_call_target="tpu_custom_call" | custom-call | flops 1811939328 | bytes 4194304 | tf_op jit(solution)/shard_map/pallas_call | solution.py:189
  143.4 4.1 %all-to-all-done = f32[32,1,16]{2,1,0:T(1,128)S(1)} async-done(((f32[32,1,16]{2,1,0:T(1,128)}), f32[32,1,16]{2,1,0:T(1,128)S(1)}, u32[]{:S(2)}, u32[]{:S(2)}) %all-to-all-start) | async-done | bytes 2080 | tf_op jit(solution)/shard_map/all_to_all | solution.py:329
  (106 shorter events, 11.6 us)
Async XLA Ops:
  0.6 7.9 %copy-start.3 = (bf16[768,768]{1,0:T(8,128)(2,1)S(1)}, bf16[768,768]{1,0:T(8,128)(2,1)}, u32[]{:S(2)}) copy-start(bf16[768,768]{1,0:T(8,128)(2,1)} %constant.163.clone.im_ref.refs_2_) | copy-start | bytes 3538948
  2.5 6.0 %copy-start.2 = (bf16[2,16,24,768]{3,2,1,0:T(8,128)(2,1)S(1)}, bf16[2,16,24,768]{3,2,1,0:T(8,128)(2,1)}, u32[]{:S(2)}) copy-start(bf16[2,16,24,768]{3,2,1,0:T(8,128)(2,1)} %param.9) | copy-start | bytes 3538948
  3.3 10.3 %collective-permute-start.2 = (bf16[4,2,24,768]{3,2,0,1:T(8,128)(2,1)}, bf16[4,2,24,768]{3,2,0,1:T(8,128)(2,1)}, u32[]{:S(2)}, u32[]{:S(2)}) collective-permute-start(bf16[4,2,24,768]{3,2,0,1:T(8,128)(2,1)} %copy.19), channel_id=1, source_target_pairs={{0,4},{2,6},{4,0},{6,2},{8,12},{10,14},{12,8},{14,10},{16,20},{18,... | collective-permute-start | bytes 884744 | tf_op jit(solution)/shard_map/ppermute | solution.py:33
  7.0 9.4 %collective-permute-start = (bf16[4,2,24,768]{3,2,0,1:T(8,128)(2,1)}, bf16[4,2,24,768]{3,2,0,1:T(8,128)(2,1)}, u32[]{:S(2)}, u32[]{:S(2)}) collective-permute-start(bf16[4,2,24,768]{3,2,0,1:T(8,128)(2,1)} %copy.17), channel_id=1, source_target_pairs={{0,2},{2,0},{4,6},{6,4},{8,10},{10,8},{12,14},{14,12},{16,18},{18,... | collective-permute-start | bytes 884744 | tf_op jit(solution)/shard_map/ppermute | solution.py:33
  8.5 1.3 copy-start.5
  11.8 5.7 %copy-start.7 = (bf16[768,768]{1,0:T(8,128)(2,1)}, bf16[768,768]{1,0:T(8,128)(2,1)S(1)}, u32[]{:S(2)}) copy-start(bf16[768,768]{1,0:T(8,128)(2,1)S(1)} %shard_map.95.refs_1_) | copy-start | bytes 3538948
  14.6 5.2 %collective-permute-start.3 = (bf16[4,24,768]{2,1,0:T(8,128)(2,1)S(1)}, bf16[4,24,768]{2,1,0:T(8,128)(2,1)S(1)}, u32[]{:S(2)}, u32[]{:S(2)}) collective-permute-start(bf16[4,24,768]{2,1,0:T(8,128)(2,1)S(1)} %fusion.5), channel_id=1, source_target_pairs={{0,2},{2,0},{4,6},{6,4},{8,10},{10,8},{12,14},{14,12},{16,18},{18,... | collective-permute-start | bytes 442376 | tf_op jit(solution)/shard_map/ppermute | solution.py:33
  17.5 5.2 %collective-permute-start.1 = (bf16[4,24,768]{2,1,0:T(8,128)(2,1)S(1)}, bf16[4,24,768]{2,1,0:T(8,128)(2,1)S(1)}, u32[]{:S(2)}, u32[]{:S(2)}) collective-permute-start(bf16[4,24,768]{2,1,0:T(8,128)(2,1)S(1)} %fusion.4), channel_id=1, source_target_pairs={{0,4},{2,6},{4,0},{6,2},{8,12},{10,14},{12,8},{14,10},{16,20},{18,... | collective-permute-start | bytes 442376 | tf_op jit(solution)/shard_map/ppermute | solution.py:33
  22.8 4.5 %collective-permute-start.4 = (bf16[24,1536]{1,0:T(8,128)(2,1)S(1)}, bf16[24,1536]{1,0:T(8,128)(2,1)S(1)}, u32[]{:S(2)}, u32[]{:S(2)}) collective-permute-start(bf16[24,1536]{1,0:T(8,128)(2,1)S(1)} %get-tuple-element.46), channel_id=1, source_target_pairs={{0,8},{2,10},{4,12},{6,14},{8,0},{10,2},{12,4},{14,6},{16,24},{18,... | collective-permute-start | bytes 221192 | tf_op jit(solution)/shard_map/ppermute | solution.py:33
  24.4 6.5 %collective-permute-start.5 = (bf16[24,1536]{1,0:T(8,128)(2,1)S(1)}, bf16[24,1536]{1,0:T(8,128)(2,1)S(1)}, u32[]{:S(2)}, u32[]{:S(2)}) collective-permute-start(bf16[24,1536]{1,0:T(8,128)(2,1)S(1)} %get-tuple-element.47), channel_id=1, source_target_pairs={{0,16},{2,18},{4,20},{6,22},{8,24},{10,26},{12,28},{14,30},{16,0},... | collective-permute-start | bytes 221192 | tf_op jit(solution)/shard_map/ppermute | solution.py:33
  27.0 6.3 %collective-permute-start.6 = (bf16[24,1536]{1,0:T(8,128)(2,1)S(1)}, bf16[24,1536]{1,0:T(8,128)(2,1)S(1)}, u32[]{:S(2)}, u32[]{:S(2)}) collective-permute-start(bf16[24,1536]{1,0:T(8,128)(2,1)S(1)} %get-tuple-element.48), channel_id=1, source_target_pairs={{0,24},{2,26},{4,28},{6,30},{8,16},{10,18},{12,20},{14,22},{16,8},... | collective-permute-start | bytes 221192 | tf_op jit(solution)/shard_map/ppermute | solution.py:33
  33.4 6.4 %collective-permute-start.9 = (bf16[24,1536]{1,0:T(8,128)(2,1)S(1)}, bf16[24,1536]{1,0:T(8,128)(2,1)S(1)}, u32[]{:S(2)}, u32[]{:S(2)}) collective-permute-start(bf16[24,1536]{1,0:T(8,128)(2,1)S(1)} %pad_maximum_fusion.10), channel_id=1, source_target_pairs={{0,24},{2,26},{4,28},{6,30},{8,16},{10,18},{12,20},{14,22},{16,8},... | collective-permute-start | bytes 221192 | tf_op jit(solution)/shard_map/ppermute | solution.py:33
  34.2 6.8 %collective-permute-start.8 = (bf16[24,1536]{1,0:T(8,128)(2,1)S(1)}, bf16[24,1536]{1,0:T(8,128)(2,1)S(1)}, u32[]{:S(2)}, u32[]{:S(2)}) collective-permute-start(bf16[24,1536]{1,0:T(8,128)(2,1)S(1)} %pad_maximum_fusion.10), channel_id=1, source_target_pairs={{0,16},{2,18},{4,20},{6,22},{8,24},{10,26},{12,28},{14,30},{16,0},... | collective-permute-start | bytes 221192 | tf_op jit(solution)/shard_map/ppermute | solution.py:33
  34.6 6.4 %collective-permute-start.7 = (bf16[24,1536]{1,0:T(8,128)(2,1)S(1)}, bf16[24,1536]{1,0:T(8,128)(2,1)S(1)}, u32[]{:S(2)}, u32[]{:S(2)}) collective-permute-start(bf16[24,1536]{1,0:T(8,128)(2,1)S(1)} %pad_maximum_fusion.10), channel_id=1, source_target_pairs={{0,8},{2,10},{4,12},{6,14},{8,0},{10,2},{12,4},{14,6},{16,24},{18,... | collective-permute-start | bytes 221192 | tf_op jit(solution)/shard_map/ppermute | solution.py:33
  41.1 1.3 copy-start.9
  41.2 6.7 %collective-permute-start.12 = (bf16[4,24,768]{2,1,0:T(8,128)(2,1)S(1)}, bf16[4,24,768]{2,1,0:T(8,128)(2,1)S(1)}, u32[]{:S(2)}, u32[]{:S(2)}) collective-permute-start(bf16[4,24,768]{2,1,0:T(8,128)(2,1)S(1)} %get-tuple-element.51), channel_id=1, source_target_pairs={{0,2},{2,0},{4,6},{6,4},{8,10},{10,8},{12,14},{14,12},{16,18},{18,... | collective-permute-start | bytes 442376 | tf_op jit(solution)/shard_map/ppermute | solution.py:33
  42.6 7.0 %collective-permute-start.10 = (bf16[4,24,768]{2,1,0:T(8,128)(2,1)S(1)}, bf16[4,24,768]{2,1,0:T(8,128)(2,1)S(1)}, u32[]{:S(2)}, u32[]{:S(2)}) collective-permute-start(bf16[4,24,768]{2,1,0:T(8,128)(2,1)S(1)} %get-tuple-element.52), channel_id=1, source_target_pairs={{0,4},{2,6},{4,0},{6,2},{8,12},{10,14},{12,8},{14,10},{16,20},{18,... | collective-permute-start | bytes 442376 | tf_op jit(solution)/shard_map/ppermute | solution.py:33
  48.0 6.8 %collective-permute-start.13 = (bf16[4,2,24,768]{3,2,0,1:T(8,128)(2,1)S(1)}, bf16[4,2,24,768]{3,2,0,1:T(8,128)(2,1)S(1)}, u32[]{:S(2)}, u32[]{:S(2)}) collective-permute-start(bf16[4,2,24,768]{3,2,0,1:T(8,128)(2,1)S(1)} %reverse_select_fusion.2), channel_id=1, source_target_pairs={{0,4},{2,6},{4,0},{6,2},{8,12},{10,14},{12,8},{14,10},{16,20},{18,... | collective-permute-start | bytes 884744 | tf_op jit(solution)/shard_map/ppermute | solution.py:33
  49.8 6.8 %collective-permute-start.11 = (bf16[4,2,24,768]{3,2,1,0:T(8,128)(2,1)S(1)}, bf16[4,2,24,768]{3,2,1,0:T(8,128)(2,1)S(1)}, u32[]{:S(2)}, u32[]{:S(2)}) collective-permute-start(bf16[4,2,24,768]{3,2,1,0:T(8,128)(2,1)S(1)} %reverse_select_fusion.3), channel_id=1, source_target_pairs={{0,2},{2,0},{4,6},{6,4},{8,10},{10,8},{12,14},{14,12},{16,18},{18,... | collective-permute-start | bytes 884744 | tf_op jit(solution)/shard_map/ppermute | solution.py:33
  56.9 0.8 copy-start.12
  56.9 0.9 copy-start.14
  57.0 1.0 copy-start.16
  57.9 1.3 copy-start.1
  58.0 3.5 %collective-permute-start.14 = (bf16[768,768]{1,0:T(8,128)(2,1)S(1)}, bf16[768,768]{1,0:T(8,128)(2,1)S(1)}, u32[]{:S(2)}, u32[]{:S(2)}) collective-permute-start(bf16[768,768]{1,0:T(8,128)(2,1)S(1)} %pad_maximum_fusion.shaped_ref), channel_id=1, source_target_pairs={{0,1},{1,0},{2,3},{3,2},{4,5},{5,4},{6,7},{7,6},{8,9},{9,8},{10,11... | collective-permute-start | bytes 3538952 | tf_op jit(solution)/shard_map/ppermute | solution.py:289
  59.2 1.1 copy-start.11
  59.2 1.1 copy-start.13
  59.2 1.1 copy-start.15
  59.2 1.2 copy-start.17
  60.4 1.7 %copy-start = (bf16[768,768]{1,0:T(8,128)(2,1)S(1)}, bf16[768,768]{1,0:T(8,128)(2,1)}, u32[]{:S(2)}) copy-start(bf16[768,768]{1,0:T(8,128)(2,1)} %constant.165.clone.table_ref) | copy-start | bytes 3538948
  63.4 72.0 %collective-permute-start.29 = (bf16[48,768]{1,0:T(8,128)(2,1)S(1)}, bf16[48,768]{1,0:T(8,128)(2,1)S(1)}, u32[]{:S(2)}, u32[]{:S(2)}) collective-permute-start(bf16[48,768]{1,0:T(8,128)(2,1)S(1)} %get-tuple-element.27), channel_id=1, source_target_pairs={{0,30},{2,28},{4,26},{6,24},{8,22},{10,20},{12,18},{14,16},{16,14}... | collective-permute-start | bytes 221192 | tf_op jit(solution)/shard_map/ppermute | solution.py:33
  65.2 70.1 %collective-permute-start.28 = (bf16[48,768]{1,0:T(8,128)(2,1)S(1)}, bf16[48,768]{1,0:T(8,128)(2,1)S(1)}, u32[]{:S(2)}, u32[]{:S(2)}) collective-permute-start(bf16[48,768]{1,0:T(8,128)(2,1)S(1)} %get-tuple-element.28), channel_id=1, source_target_pairs={{0,14},{2,12},{4,10},{6,8},{8,6},{10,4},{12,2},{14,0},{16,30},{18,... | collective-permute-start | bytes 221192 | tf_op jit(solution)/shard_map/ppermute | solution.py:33
  66.5 68.8 %collective-permute-start.27 = (bf16[48,768]{1,0:T(8,128)(2,1)S(1)}, bf16[48,768]{1,0:T(8,128)(2,1)S(1)}, u32[]{:S(2)}, u32[]{:S(2)}) collective-permute-start(bf16[48,768]{1,0:T(8,128)(2,1)S(1)} %get-tuple-element.29), channel_id=1, source_target_pairs={{0,28},{2,30},{4,24},{6,26},{8,20},{10,22},{12,16},{14,18},{16,12}... | collective-permute-start | bytes 221192 | tf_op jit(solution)/shard_map/ppermute | solution.py:33
  69.2 66.0 %collective-permute-start.26 = (bf16[48,768]{1,0:T(8,128)(2,1)S(1)}, bf16[48,768]{1,0:T(8,128)(2,1)S(1)}, u32[]{:S(2)}, u32[]{:S(2)}) collective-permute-start(bf16[48,768]{1,0:T(8,128)(2,1)S(1)} %get-tuple-element.30), channel_id=1, source_target_pairs={{0,12},{2,14},{4,8},{6,10},{8,4},{10,6},{12,0},{14,2},{16,28},{18,... | collective-permute-start | bytes 221192 | tf_op jit(solution)/shard_map/ppermute | solution.py:33
  71.1 64.3 %copy-start.8 = (bf16[768,768]{1,0:T(8,128)(2,1)S(1)}, bf16[768,768]{1,0:T(8,128)(2,1)}, u32[]{:S(2)}) copy-start(bf16[768,768]{1,0:T(8,128)(2,1)} %copy-done.7) | copy-start | bytes 3538948
  71.1 6.0 %collective-permute-start.15 = (bf16[48,768]{1,0:T(8,128)(2,1)S(1)}, bf16[48,768]{1,0:T(8,128)(2,1)S(1)}, u32[]{:S(2)}, u32[]{:S(2)}) collective-permute-start(bf16[48,768]{1,0:T(8,128)(2,1)S(1)} %get-tuple-element.41), channel_id=1, source_target_pairs={{0,16},{2,18},{4,20},{6,22},{8,24},{10,26},{12,28},{14,30},{16,0},... | collective-permute-start | bytes 221192 | tf_op jit(solution)/shard_map/ppermute | solution.py:33
  77.2 4.4 %collective-permute-start.16 = (bf16[48,768]{1,0:T(8,128)(2,1)S(1)}, bf16[48,768]{1,0:T(8,128)(2,1)S(1)}, u32[]{:S(2)}, u32[]{:S(2)}) collective-permute-start(bf16[48,768]{1,0:T(8,128)(2,1)S(1)} %get-tuple-element.40), channel_id=1, source_target_pairs={{0,2},{2,0},{4,6},{6,4},{8,10},{10,8},{12,14},{14,12},{16,18},{18,... | collective-permute-start | bytes 221192 | tf_op jit(solution)/shard_map/ppermute | solution.py:33
  81.5 6.8 %collective-permute-start.17 = (bf16[48,768]{1,0:T(8,128)(2,1)S(1)}, bf16[48,768]{1,0:T(8,128)(2,1)S(1)}, u32[]{:S(2)}, u32[]{:S(2)}) collective-permute-start(bf16[48,768]{1,0:T(8,128)(2,1)S(1)} %get-tuple-element.39), channel_id=1, source_target_pairs={{0,18},{2,16},{4,22},{6,20},{8,26},{10,24},{12,30},{14,28},{16,2},... | collective-permute-start | bytes 221192 | tf_op jit(solution)/shard_map/ppermute | solution.py:33
  88.3 5.0 %collective-permute-start.18 = (bf16[48,768]{1,0:T(8,128)(2,1)S(1)}, bf16[48,768]{1,0:T(8,128)(2,1)S(1)}, u32[]{:S(2)}, u32[]{:S(2)}) collective-permute-start(bf16[48,768]{1,0:T(8,128)(2,1)S(1)} %get-tuple-element.38), channel_id=1, source_target_pairs={{0,4},{2,6},{4,0},{6,2},{8,12},{10,14},{12,8},{14,10},{16,20},{18,... | collective-permute-start | bytes 221192 | tf_op jit(solution)/shard_map/ppermute | solution.py:33
  93.3 6.2 %collective-permute-start.19 = (bf16[48,768]{1,0:T(8,128)(2,1)S(1)}, bf16[48,768]{1,0:T(8,128)(2,1)S(1)}, u32[]{:S(2)}, u32[]{:S(2)}) collective-permute-start(bf16[48,768]{1,0:T(8,128)(2,1)S(1)} %get-tuple-element.37), channel_id=1, source_target_pairs={{0,20},{2,22},{4,16},{6,18},{8,28},{10,30},{12,24},{14,26},{16,4},... | collective-permute-start | bytes 221192 | tf_op jit(solution)/shard_map/ppermute | solution.py:33
  99.5 5.3 %collective-permute-start.20 = (bf16[48,768]{1,0:T(8,128)(2,1)S(1)}, bf16[48,768]{1,0:T(8,128)(2,1)S(1)}, u32[]{:S(2)}, u32[]{:S(2)}) collective-permute-start(bf16[48,768]{1,0:T(8,128)(2,1)S(1)} %get-tuple-element.36), channel_id=1, source_target_pairs={{0,6},{2,4},{4,2},{6,0},{8,14},{10,12},{12,10},{14,8},{16,22},{18,... | collective-permute-start | bytes 221192 | tf_op jit(solution)/shard_map/ppermute | solution.py:33
  104.7 7.8 %collective-permute-start.21 = (bf16[48,768]{1,0:T(8,128)(2,1)S(1)}, bf16[48,768]{1,0:T(8,128)(2,1)S(1)}, u32[]{:S(2)}, u32[]{:S(2)}) collective-permute-start(bf16[48,768]{1,0:T(8,128)(2,1)S(1)} %get-tuple-element.35), channel_id=1, source_target_pairs={{0,22},{2,20},{4,18},{6,16},{8,30},{10,28},{12,26},{14,24},{16,6},... | collective-permute-start | bytes 221192 | tf_op jit(solution)/shard_map/ppermute | solution.py:33
  112.5 4.4 %collective-permute-start.22 = (bf16[48,768]{1,0:T(8,128)(2,1)S(1)}, bf16[48,768]{1,0:T(8,128)(2,1)S(1)}, u32[]{:S(2)}, u32[]{:S(2)}) collective-permute-start(bf16[48,768]{1,0:T(8,128)(2,1)S(1)} %get-tuple-element.34), channel_id=1, source_target_pairs={{0,8},{2,10},{4,12},{6,14},{8,0},{10,2},{12,4},{14,6},{16,24},{18,... | collective-permute-start | bytes 221192 | tf_op jit(solution)/shard_map/ppermute | solution.py:33
  116.8 6.2 %collective-permute-start.23 = (bf16[48,768]{1,0:T(8,128)(2,1)S(1)}, bf16[48,768]{1,0:T(8,128)(2,1)S(1)}, u32[]{:S(2)}, u32[]{:S(2)}) collective-permute-start(bf16[48,768]{1,0:T(8,128)(2,1)S(1)} %get-tuple-element.33), channel_id=1, source_target_pairs={{0,24},{2,26},{4,28},{6,30},{8,16},{10,18},{12,20},{14,22},{16,8},... | collective-permute-start | bytes 221192 | tf_op jit(solution)/shard_map/ppermute | solution.py:33
  123.0 5.3 %collective-permute-start.24 = (bf16[48,768]{1,0:T(8,128)(2,1)S(1)}, bf16[48,768]{1,0:T(8,128)(2,1)S(1)}, u32[]{:S(2)}, u32[]{:S(2)}) collective-permute-start(bf16[48,768]{1,0:T(8,128)(2,1)S(1)} %get-tuple-element.32), channel_id=1, source_target_pairs={{0,10},{2,8},{4,14},{6,12},{8,2},{10,0},{12,6},{14,4},{16,26},{18,... | collective-permute-start | bytes 221192 | tf_op jit(solution)/shard_map/ppermute | solution.py:33
  128.2 7.0 %collective-permute-start.25 = (bf16[48,768]{1,0:T(8,128)(2,1)S(1)}, bf16[48,768]{1,0:T(8,128)(2,1)S(1)}, u32[]{:S(2)}, u32[]{:S(2)}) collective-permute-start(bf16[48,768]{1,0:T(8,128)(2,1)S(1)} %get-tuple-element.31), channel_id=1, source_target_pairs={{0,26},{2,24},{4,30},{6,28},{8,18},{10,16},{12,22},{14,20},{16,10}... | collective-permute-start | bytes 221192 | tf_op jit(solution)/shard_map/ppermute | solution.py:33
  135.4 4.9 %copy-start.4 = (bf16[768,768]{1,0:T(8,128)(2,1)S(1)}, bf16[768,768]{1,0:T(8,128)(2,1)}, u32[]{:S(2)}) copy-start(bf16[768,768]{1,0:T(8,128)(2,1)} %constant.163.clone.im_ref.refs_2_) | copy-start | bytes 3538948
  135.4 4.9 %copy-start.6 = (bf16[768,768]{1,0:T(8,128)(2,1)S(1)}, bf16[768,768]{1,0:T(8,128)(2,1)}, u32[]{:S(2)}) copy-start(bf16[768,768]{1,0:T(8,128)(2,1)} %constant.162.clone.re_ref.refs_1_) | copy-start | bytes 3538948
  137.8 9.7 %all-to-all-start = ((f32[32,1,16]{2,1,0:T(1,128)}), f32[32,1,16]{2,1,0:T(1,128)S(1)}, u32[]{:S(2)}, u32[]{:S(2)}) async-start(f32[32,1,16]{2,1,0:T(1,128)} %bitcast.53), calls=%async_computation | async-start | bytes 32768 | tf_op jit(solution)/shard_map/all_to_all | solution.py:329
  (1 other events, 0.7 us)

commit v8 on v7

--- a/solution.py
+++ b/solution.py
@@ -9,6 +9,7 @@
 
 bf16 = jnp.bfloat16
 f32 = jnp.float32
+LANES = 5
 
 
 def propagator(grid_size):
@@ -226,7 +227,7 @@
             [bf16, f32, bf16, f32],
             8 * local_rows * double_width,
             (forward[0], backward[0]),
-            grant=52,
+            grant=12,
             in_specs=[pl.BlockSpec(memory_space=pltpu.HBM)] * 2,
             scratch_shapes=[pltpu.VMEM((local_rows, double_width), bf16)] * 2
             + [pltpu.SemaphoreType.DMA((2 * local_rows // (4 * block_rows),))],
@@ -307,7 +308,12 @@
     blocks = blocks.reshape(count, 2 * block_rows, grid_size)
     if count <= 16:
         turns = [at // 2 + count // 2 * (at % 2) for at in range(count)]
-        pixels = tuple(exchange(pick(blocks, me ^ e, 0), e, count) if e else pick(blocks, me, 0) for e in turns)
+        pixels = [pick(blocks, me, 0)]
+        for at, e in enumerate(turns[1:], 1):
+            block = pick(blocks, me ^ e, 0)
+            if at > LANES:
+                block, pixels[at - LANES] = lax.optimization_barrier((block, pixels[at - LANES]))
+            pixels.append(exchange(block, e, count))
     else:
         pixels = (lax.all_to_all(blocks, "modes", 0, 0, tiled=True),)
 

time: 148 us -> 112 us (0.76)
  waiting for transfers between devices: 87.5 us -> 37 us
  starting transfers between devices: 36.8 us -> 49.1 us
  local copies, waits for them, and re-layouts: 5.79 us -> 8.33 us
    ppermute x29, waiting for transfers between devices: 83.4 us -> 32.8 us  [exchange(): lax.ppermute(values, 'modes', [(i, i ^ offset) for i in range(count)])]
    ppermute x29, starting transfers between devices: 34.2 us -> 45.1 us  [exchange(): lax.ppermute(values, 'modes', [(i, i ^ offset) for i in range(count)])]
    unnamed x51 -> x55, local copies, waits for them, and re-layouts: 3.88 us -> 6.42 us
  transfers between devices with their start and end apart: 31 -> 31, of which waited for: 22 -> 13; matrix products, arithmetic and copies ran while one was open for 3% -> 4% of each run, Pallas kernels for 4% -> 5%
where the time goes in v8:
time: 112 us
  starting transfers between devices  49.1 us (44%)
  waiting for transfers between devices  37 us (33%)
  Pallas kernels  10.7 us (10%)
  local copies, waits for them, and re-layouts  8.33 us (7%)
  other arithmetic  5.3 us (5%)
  between operations  1.23 us (1%)
    ppermute x29, starting transfers between devices, exchange(): lax.ppermute(values, 'modes', [(i, i ^ offset) for i in range(count)])  45.1 us
    ppermute x29, waiting for transfers between devices, exchange(): lax.ppermute(values, 'modes', [(i, i ^ offset) for i in range(count)])  32.8 us
    pallas_call x6, Pallas kernels, kernel_call(): pl.pallas_call(kernel, out_shape=out_shape, compiler_params=pltpu.Compile...  10.7 us
    unnamed x55, local copies, waits for them, and re-layouts  6.42 us
    all_to_all x1, waiting for transfers between devices, local(): pieces = lax.all_to_all(term, ('modes', 'rows'), 0, 0, tiled=True)  4.12 us
    all_to_all x1, starting transfers between devices, local(): pieces = lax.all_to_all(term, ('modes', 'rows'), 0, 0, tiled=True)  4 us
  transfers between devices with their start and end apart: 31, of which 13 were waited for; matrix products, arithmetic and copies ran while one was open for 4% of the time, Pallas kernels for 5%

profile of v8, /device:TPU:0, one launch (start us, length us, event | category | flops | bytes accessed | tf_op | source)
XLA Modules:
  0.0 111.7 jit_solution(4151063007849948064)
XLA Ops:
  0.6 1.3 %copy-done = bf16[1,384,1536]{2,1,0:T(8,128)(2,1)S(1)} copy-done((bf16[1,384,1536]{2,1,0:T(8,128)(2,1)S(1)}, bf16[1,384,1536]{2,1,0:T(8,128)(2,1)}, u32[]{:S(2)}) %copy-start) | copy-done | bytes 1179672
  1.9 1.3 %copy-done.2 = bf16[1,384,1536]{2,1,0:T(8,128)(2,1)S(1)} copy-done((bf16[1,384,1536]{2,1,0:T(8,128)(2,1)S(1)}, bf16[1,384,1536]{2,1,0:T(8,128)(2,1)}, u32[]{:S(2)}) %copy-start.2) | copy-done | bytes 1179672
  3.2 1.2 %shard_map.94 = (bf16[192,768]{1,0:T(8,128)(2,1)S(1)}, f32[192,768]{1,0:T(8,128)S(1)}, bf16[192,768]{1,0:T(8,128)(2,1)S(1)}, f32[192,768]{1,0:T(8,128)S(1)}) custom-call(bf16[384,1536]{1,0:T(8,128)(2,1)S(1)} %bitcast.93, bf16[384,1536]{1,0:T(8,128)(2,1)S(1)} %bitcast.96), custom_call_target="tpu_custom_call" | custom-call | flops 4718592 | bytes 4194304 | tf_op jit(solution)/shard_map/pallas_call | solution.py:190
  5.1 3.0 %collective-permute-start.2 = (bf16[4,2,24,768]{3,2,0,1:T(8,128)(2,1)}, bf16[4,2,24,768]{3,2,0,1:T(8,128)(2,1)}, u32[]{:S(2)}, u32[]{:S(2)}) collective-permute-start(bf16[4,2,24,768]{3,2,0,1:T(8,128)(2,1)} %copy.19), channel_id=1, source_target_pairs={{0,4},{2,6},{4,0},{6,2},{8,12},{10,14},{12,8},{14,10},{16,20},{18,... | collective-permute-start | bytes 884744 | tf_op jit(solution)/shard_map/ppermute | solution.py:34
  8.8 1.5 %collective-permute-start = (bf16[4,2,24,768]{3,2,0,1:T(8,128)(2,1)}, bf16[4,2,24,768]{3,2,0,1:T(8,128)(2,1)}, u32[]{:S(2)}, u32[]{:S(2)}) collective-permute-start(bf16[4,2,24,768]{3,2,0,1:T(8,128)(2,1)} %copy.17), channel_id=1, source_target_pairs={{0,2},{2,0},{4,6},{6,4},{8,10},{10,8},{12,14},{14,12},{16,18},{18,... | collective-permute-start | bytes 884744 | tf_op jit(solution)/shard_map/ppermute | solution.py:34
  10.3 1.3 %copy-done.8 = bf16[768,768]{1,0:T(8,128)(2,1)S(1)} copy-done((bf16[768,768]{1,0:T(8,128)(2,1)S(1)}, bf16[768,768]{1,0:T(8,128)(2,1)}, u32[]{:S(2)}) %copy-start.8) | copy-done | bytes 1179672
  11.6 2.0 %shard_map.95.refs_1_ = bf16[768,768]{1,0:T(8,128)(2,1)S(1)} custom-call(bf16[768,768]{1,0:T(8,128)(2,1)S(1)} %bitcast.101, bf16[768,768]{1,0:T(8,128)(2,1)S(1)} %copy-done.8, bf16[768,768]{1,0:T(8,128)(2,1)S(1)} %copy-done.6), custom_call_target="tpu_custom_call" | custom-call | flops 1811939328 | bytes 4194304 | tf_op jit(solution)/shard_map/pallas_call | solution.py:190
  13.6 1.8 %collective-permute-done.2 = bf16[4,2,24,768]{3,2,0,1:T(8,128)(2,1)} collective-permute-done((bf16[4,2,24,768]{3,2,0,1:T(8,128)(2,1)}, bf16[4,2,24,768]{3,2,0,1:T(8,128)(2,1)}, u32[]{:S(2)}, u32[]{:S(2)}) %collective-permute-start.2) | collective-permute-done | bytes 294944 | tf_op jit(solution)/shard_map/ppermute | solution.py:34
  15.4 1.0 copy_add_fusion
  16.4 1.8 %collective-permute-start.3 = (bf16[4,24,768]{2,1,0:T(8,128)(2,1)S(1)}, bf16[4,24,768]{2,1,0:T(8,128)(2,1)S(1)}, u32[]{:S(2)}, u32[]{:S(2)}) collective-permute-start(bf16[4,24,768]{2,1,0:T(8,128)(2,1)S(1)} %fusion.5), channel_id=1, source_target_pairs={{0,2},{2,0},{4,6},{6,4},{8,10},{10,8},{12,14},{14,12},{16,18},{18,... | collective-permute-start | bytes 442376 | tf_op jit(solution)/shard_map/ppermute | solution.py:34
  18.2 1.0 copy_add_fusion.1
  19.3 1.6 %collective-permute-start.1 = (bf16[4,24,768]{2,1,0:T(8,128)(2,1)S(1)}, bf16[4,24,768]{2,1,0:T(8,128)(2,1)S(1)}, u32[]{:S(2)}, u32[]{:S(2)}) collective-permute-start(bf16[4,24,768]{2,1,0:T(8,128)(2,1)S(1)} %fusion.4), channel_id=1, source_target_pairs={{0,4},{2,6},{4,0},{6,2},{8,12},{10,14},{12,8},{14,10},{16,20},{18,... | collective-permute-start | bytes 442376 | tf_op jit(solution)/shard_map/ppermute | solution.py:34
  20.9 0.8 collective-permute-done.3
  21.7 2.8 %collective-permute-done.1 = bf16[4,24,768]{2,1,0:T(8,128)(2,1)S(1)} collective-permute-done((bf16[4,24,768]{2,1,0:T(8,128)(2,1)S(1)}, bf16[4,24,768]{2,1,0:T(8,128)(2,1)S(1)}, u32[]{:S(2)}, u32[]{:S(2)}) %collective-permute-start.1) | collective-permute-done | bytes 147488 | tf_op jit(solution)/shard_map/ppermute | solution.py:34
  24.6 1.6 %collective-permute-start.4 = (bf16[24,1536]{1,0:T(8,128)(2,1)S(1)}, bf16[24,1536]{1,0:T(8,128)(2,1)S(1)}, u32[]{:S(2)}, u32[]{:S(2)}) collective-permute-start(bf16[24,1536]{1,0:T(8,128)(2,1)S(1)} %get-tuple-element.86), channel_id=1, source_target_pairs={{0,8},{2,10},{4,12},{6,14},{8,0},{10,2},{12,4},{14,6},{16,24},{18,... | collective-permute-start | bytes 221192 | tf_op jit(solution)/shard_map/ppermute | solution.py:34
  26.2 2.6 %collective-permute-start.5 = (bf16[24,1536]{1,0:T(8,128)(2,1)S(1)}, bf16[24,1536]{1,0:T(8,128)(2,1)S(1)}, u32[]{:S(2)}, u32[]{:S(2)}) collective-permute-start(bf16[24,1536]{1,0:T(8,128)(2,1)S(1)} %get-tuple-element.87), channel_id=1, source_target_pairs={{0,16},{2,18},{4,20},{6,22},{8,24},{10,26},{12,28},{14,30},{16,0},... | collective-permute-start | bytes 221192 | tf_op jit(solution)/shard_map/ppermute | solution.py:34
  29.1 3.7 %collective-permute-done.5 = bf16[24,1536]{1,0:T(8,128)(2,1)S(1)} collective-permute-done((bf16[24,1536]{1,0:T(8,128)(2,1)S(1)}, bf16[24,1536]{1,0:T(8,128)(2,1)S(1)}, u32[]{:S(2)}, u32[]{:S(2)}) %collective-permute-start.5) | collective-permute-done | bytes 73760 | tf_op jit(solution)/shard_map/ppermute | solution.py:34
  32.8 2.3 %collective-permute-done.6 = bf16[24,1536]{1,0:T(8,128)(2,1)S(1)} collective-permute-done((bf16[24,1536]{1,0:T(8,128)(2,1)S(1)}, bf16[24,1536]{1,0:T(8,128)(2,1)S(1)}, u32[]{:S(2)}, u32[]{:S(2)}) %collective-permute-start.6) | collective-permute-done | bytes 73760 | tf_op jit(solution)/shard_map/ppermute | solution.py:34
  35.1 0.9 collective-permute-start.9
  36.4 3.2 %collective-permute-start.7 = (bf16[24,1536]{1,0:T(8,128)(2,1)S(1)}, bf16[24,1536]{1,0:T(8,128)(2,1)S(1)}, u32[]{:S(2)}, u32[]{:S(2)}) collective-permute-start(bf16[24,1536]{1,0:T(8,128)(2,1)S(1)} %pad_maximum_fusion.10), channel_id=1, source_target_pairs={{0,8},{2,10},{4,12},{6,14},{8,0},{10,2},{12,4},{14,6},{16,24},{18,... | collective-permute-start | bytes 221192 | tf_op jit(solution)/shard_map/ppermute | solution.py:34
  39.6 1.9 %collective-permute-done.9 = bf16[24,1536]{1,0:T(8,128)(2,1)S(1)} collective-permute-done((bf16[24,1536]{1,0:T(8,128)(2,1)S(1)}, bf16[24,1536]{1,0:T(8,128)(2,1)S(1)}, u32[]{:S(2)}, u32[]{:S(2)}) %collective-permute-start.9) | collective-permute-done | bytes 73760 | tf_op jit(solution)/shard_map/ppermute | solution.py:34
  41.5 1.3 %collective-permute-done.8 = bf16[24,1536]{1,0:T(8,128)(2,1)S(1)} collective-permute-done((bf16[24,1536]{1,0:T(8,128)(2,1)S(1)}, bf16[24,1536]{1,0:T(8,128)(2,1)S(1)}, u32[]{:S(2)}, u32[]{:S(2)}) %collective-permute-start.8) | collective-permute-done | bytes 73760 | tf_op jit(solution)/shard_map/ppermute | solution.py:34
  43.0 0.9 collective-permute-start.12
  44.4 1.6 %collective-permute-start.10 = (bf16[4,24,768]{2,1,0:T(8,128)(2,1)S(1)}, bf16[4,24,768]{2,1,0:T(8,128)(2,1)S(1)}, u32[]{:S(2)}, u32[]{:S(2)}) collective-permute-start(bf16[4,24,768]{2,1,0:T(8,128)(2,1)S(1)} %get-tuple-element.92), channel_id=1, source_target_pairs={{0,4},{2,6},{4,0},{6,2},{8,12},{10,14},{12,8},{14,10},{16,20},{18,... | collective-permute-start | bytes 442376 | tf_op jit(solution)/shard_map/ppermute | solution.py:34
  46.0 3.7 %collective-permute-done.12 = bf16[4,24,768]{2,1,0:T(8,128)(2,1)S(1)} collective-permute-done((bf16[4,24,768]{2,1,0:T(8,128)(2,1)S(1)}, bf16[4,24,768]{2,1,0:T(8,128)(2,1)S(1)}, u32[]{:S(2)}, u32[]{:S(2)}) %collective-permute-start.12) | collective-permute-done | bytes 147488 | tf_op jit(solution)/shard_map/ppermute | solution.py:34
  49.8 1.7 %collective-permute-start.13 = (bf16[4,2,24,768]{3,2,0,1:T(8,128)(2,1)S(1)}, bf16[4,2,24,768]{3,2,0,1:T(8,128)(2,1)S(1)}, u32[]{:S(2)}, u32[]{:S(2)}) collective-permute-start(bf16[4,2,24,768]{3,2,0,1:T(8,128)(2,1)S(1)} %reverse_select_fusion.2), channel_id=1, source_target_pairs={{0,4},{2,6},{4,0},{6,2},{8,12},{10,14},{12,8},{14,10},{16,20},{18,... | collective-permute-start | bytes 884744 | tf_op jit(solution)/shard_map/ppermute | solution.py:34
  52.0 4.6 %collective-permute-done.13 = bf16[4,2,24,768]{3,2,0,1:T(8,128)(2,1)S(1)} collective-permute-done((bf16[4,2,24,768]{3,2,0,1:T(8,128)(2,1)S(1)}, bf16[4,2,24,768]{3,2,0,1:T(8,128)(2,1)S(1)}, u32[]{:S(2)}, u32[]{:S(2)}) %collective-permute-start.13) | collective-permute-done | bytes 294944 | tf_op jit(solution)/shard_map/ppermute | solution.py:34
  56.8 1.6 %collective-permute-done.11 = bf16[4,2,24,768]{3,2,1,0:T(8,128)(2,1)S(1)} collective-permute-done((bf16[4,2,24,768]{3,2,1,0:T(8,128)(2,1)S(1)}, bf16[4,2,24,768]{3,2,1,0:T(8,128)(2,1)S(1)}, u32[]{:S(2)}, u32[]{:S(2)}) %collective-permute-start.11) | collective-permute-done | bytes 294944 | tf_op jit(solution)/shard_map/ppermute | solution.py:34
  60.0 1.0 copy-done.4
  61.0 1.1 shard_map.96.own_ref
  62.2 1.1 pad_maximum_fusion.1
  63.9 1.1 shard_map.97.refs_0_
  65.7 1.8 %collective-permute-start.18 = (bf16[48,768]{1,0:T(8,128)(2,1)S(1)}, bf16[48,768]{1,0:T(8,128)(2,1)S(1)}, u32[]{:S(2)}, u32[]{:S(2)}) collective-permute-start(bf16[48,768]{1,0:T(8,128)(2,1)S(1)} %get-tuple-element.74), channel_id=1, source_target_pairs={{0,4},{2,6},{4,0},{6,2},{8,12},{10,14},{12,8},{14,10},{16,20},{18,... | collective-permute-start | bytes 221192 | tf_op jit(solution)/shard_map/ppermute | solution.py:34
  67.4 1.9 %collective-permute-start.17 = (bf16[48,768]{1,0:T(8,128)(2,1)S(1)}, bf16[48,768]{1,0:T(8,128)(2,1)S(1)}, u32[]{:S(2)}, u32[]{:S(2)}) collective-permute-start(bf16[48,768]{1,0:T(8,128)(2,1)S(1)} %get-tuple-element.76), channel_id=1, source_target_pairs={{0,18},{2,16},{4,22},{6,20},{8,26},{10,24},{12,30},{14,28},{16,2},... | collective-permute-start | bytes 221192 | tf_op jit(solution)/shard_map/ppermute | solution.py:34
  69.3 1.8 %collective-permute-start.16 = (bf16[48,768]{1,0:T(8,128)(2,1)S(1)}, bf16[48,768]{1,0:T(8,128)(2,1)S(1)}, u32[]{:S(2)}, u32[]{:S(2)}) collective-permute-start(bf16[48,768]{1,0:T(8,128)(2,1)S(1)} %get-tuple-element.78), channel_id=1, source_target_pairs={{0,2},{2,0},{4,6},{6,4},{8,10},{10,8},{12,14},{14,12},{16,18},{18,... | collective-permute-start | bytes 221192 | tf_op jit(solution)/shard_map/ppermute | solution.py:34
  71.8 3.6 %collective-permute-done.19 = bf16[48,768]{1,0:T(8,128)(2,1)S(1)} collective-permute-done((bf16[48,768]{1,0:T(8,128)(2,1)S(1)}, bf16[48,768]{1,0:T(8,128)(2,1)S(1)}, u32[]{:S(2)}, u32[]{:S(2)}) %collective-permute-start.19) | collective-permute-done | bytes 73760 | tf_op jit(solution)/shard_map/ppermute | solution.py:34
  75.4 1.2 %collective-permute-start.23 = (bf16[48,768]{1,0:T(8,128)(2,1)S(1)}, bf16[48,768]{1,0:T(8,128)(2,1)S(1)}, u32[]{:S(2)}, u32[]{:S(2)}) collective-permute-start(bf16[48,768]{1,0:T(8,128)(2,1)S(1)} %get-tuple-element.53), channel_id=1, source_target_pairs={{0,24},{2,26},{4,28},{6,30},{8,16},{10,18},{12,20},{14,22},{16,8},... | collective-permute-start | bytes 221192 | tf_op jit(solution)/shard_map/ppermute | solution.py:34
  76.7 4.6 %collective-permute-start.21 = (bf16[48,768]{1,0:T(8,128)(2,1)S(1)}, bf16[48,768]{1,0:T(8,128)(2,1)S(1)}, u32[]{:S(2)}, u32[]{:S(2)}) collective-permute-start(bf16[48,768]{1,0:T(8,128)(2,1)S(1)} %get-tuple-element.49), channel_id=1, source_target_pairs={{0,22},{2,20},{4,18},{6,16},{8,30},{10,28},{12,26},{14,24},{16,6},... | collective-permute-start | bytes 221192 | tf_op jit(solution)/shard_map/ppermute | solution.py:34
  81.3 1.3 %collective-permute-start.20 = (bf16[48,768]{1,0:T(8,128)(2,1)S(1)}, bf16[48,768]{1,0:T(8,128)(2,1)S(1)}, u32[]{:S(2)}, u32[]{:S(2)}) collective-permute-start(bf16[48,768]{1,0:T(8,128)(2,1)S(1)} %get-tuple-element.47), channel_id=1, source_target_pairs={{0,6},{2,4},{4,2},{6,0},{8,14},{10,12},{12,10},{14,8},{16,22},{18,... | collective-permute-start | bytes 221192 | tf_op jit(solution)/shard_map/ppermute | solution.py:34
  82.7 3.7 %collective-permute-start.29 = (bf16[48,768]{1,0:T(8,128)(2,1)S(1)}, bf16[48,768]{1,0:T(8,128)(2,1)S(1)}, u32[]{:S(2)}, u32[]{:S(2)}) collective-permute-start(bf16[48,768]{1,0:T(8,128)(2,1)S(1)} %get-tuple-element.61), channel_id=1, source_target_pairs={{0,30},{2,28},{4,26},{6,24},{8,22},{10,20},{12,18},{14,16},{16,14}... | collective-permute-start | bytes 221192 | tf_op jit(solution)/shard_map/ppermute | solution.py:34
  86.4 1.8 %collective-permute-start.27 = (bf16[48,768]{1,0:T(8,128)(2,1)S(1)}, bf16[48,768]{1,0:T(8,128)(2,1)S(1)}, u32[]{:S(2)}, u32[]{:S(2)}) collective-permute-start(bf16[48,768]{1,0:T(8,128)(2,1)S(1)} %get-tuple-element.59), channel_id=1, source_target_pairs={{0,28},{2,30},{4,24},{6,26},{8,20},{10,22},{12,16},{14,18},{16,12}... | collective-permute-start | bytes 221192 | tf_op jit(solution)/shard_map/ppermute | solution.py:34
  88.1 2.3 %collective-permute-start.26 = (bf16[48,768]{1,0:T(8,128)(2,1)S(1)}, bf16[48,768]{1,0:T(8,128)(2,1)S(1)}, u32[]{:S(2)}, u32[]{:S(2)}) collective-permute-start(bf16[48,768]{1,0:T(8,128)(2,1)S(1)} %get-tuple-element.58), channel_id=1, source_target_pairs={{0,12},{2,14},{4,8},{6,10},{8,4},{10,6},{12,0},{14,2},{16,28},{18,... | collective-permute-start | bytes 221192 | tf_op jit(solution)/shard_map/ppermute | solution.py:34
  90.4 2.3 %collective-permute-start.25 = (bf16[48,768]{1,0:T(8,128)(2,1)S(1)}, bf16[48,768]{1,0:T(8,128)(2,1)S(1)}, u32[]{:S(2)}, u32[]{:S(2)}) collective-permute-start(bf16[48,768]{1,0:T(8,128)(2,1)S(1)} %get-tuple-element.57), channel_id=1, source_target_pairs={{0,26},{2,24},{4,30},{6,28},{8,18},{10,16},{12,22},{14,20},{16,10}... | collective-permute-start | bytes 221192 | tf_op jit(solution)/shard_map/ppermute | solution.py:34
  92.8 4.7 %collective-permute-done.25 = bf16[48,768]{1,0:T(8,128)(2,1)S(1)} collective-permute-done((bf16[48,768]{1,0:T(8,128)(2,1)S(1)}, bf16[48,768]{1,0:T(8,128)(2,1)S(1)}, u32[]{:S(2)}, u32[]{:S(2)}) %collective-permute-start.25) | collective-permute-done | bytes 73760 | tf_op jit(solution)/shard_map/ppermute | solution.py:34
  97.6 2.4 %shard_map.98 = f32[32,16]{1,0:T(8,128)} custom-call(bf16[768,768]{1,0:T(8,128)(2,1)S(1)} %constant_dynamic-update-slice_fusion.refs_0_, bf16[768,768]{1,0:T(8,128)(2,1)S(1)} %copy-done.11), custom_call_target="tpu_custom_call" | custom-call | flops 1811939328 | bytes 4194304 | tf_op jit(solution)/shard_map/pallas_call | solution.py:190
  100.0 4.0 %all-to-all-start = ((f32[32,1,16]{2,1,0:T(1,128)}), f32[32,1,16]{2,1,0:T(1,128)S(1)}, u32[]{:S(2)}, u32[]{:S(2)}) async-start(f32[32,1,16]{2,1,0:T(1,128)} %bitcast.53), calls=%async_computation | async-start | bytes 32768 | tf_op jit(solution)/shard_map/all_to_all | solution.py:335
  104.0 3.0 %shard_map.99 = bf16[384,1536]{1,0:T(8,128)(2,1)} custom-call(bf16[768,768]{1,0:T(8,128)(2,1)S(1)} %shard_map.97.refs_0_, bf16[768,768]{1,0:T(8,128)(2,1)S(1)} %copy-done.9, bf16[768,768]{1,0:T(8,128)(2,1)S(1)} %copy-done.7), custom_call_target="tpu_custom_call" | custom-call | flops 1811939328 | bytes 4194304 | tf_op jit(solution)/shard_map/pallas_call | solution.py:190
  107.0 4.1 %all-to-all-done = f32[32,1,16]{2,1,0:T(1,128)S(1)} async-done(((f32[32,1,16]{2,1,0:T(1,128)}), f32[32,1,16]{2,1,0:T(1,128)S(1)}, u32[]{:S(2)}, u32[]{:S(2)}) %all-to-all-start) | async-done | bytes 2080 | tf_op jit(solution)/shard_map/all_to_all | solution.py:335
  (110 shorter events, 8.0 us)
Async XLA Ops:
  0.6 1.3 %copy-start = (bf16[1,384,1536]{2,1,0:T(8,128)(2,1)S(1)}, bf16[1,384,1536]{2,1,0:T(8,128)(2,1)}, u32[]{:S(2)}) copy-start(bf16[1,384,1536]{2,1,0:T(8,128)(2,1)} %param.7) | copy-start | bytes 3538948
  1.9 1.3 %copy-start.2 = (bf16[1,384,1536]{2,1,0:T(8,128)(2,1)S(1)}, bf16[1,384,1536]{2,1,0:T(8,128)(2,1)}, u32[]{:S(2)}) copy-start(bf16[1,384,1536]{2,1,0:T(8,128)(2,1)} %param.8) | copy-start | bytes 3538948
  3.2 7.1 %copy-start.6 = (bf16[768,768]{1,0:T(8,128)(2,1)S(1)}, bf16[768,768]{1,0:T(8,128)(2,1)}, u32[]{:S(2)}) copy-start(bf16[768,768]{1,0:T(8,128)(2,1)} %constant.163.clone.im_ref.refs_2_) | copy-start | bytes 3538948
  4.3 6.0 %copy-start.5 = (bf16[2,16,24,768]{3,2,1,0:T(8,128)(2,1)S(1)}, bf16[2,16,24,768]{3,2,1,0:T(8,128)(2,1)}, u32[]{:S(2)}) copy-start(bf16[2,16,24,768]{3,2,1,0:T(8,128)(2,1)} %param.9) | copy-start | bytes 3538948
  5.1 10.3 %collective-permute-start.2 = (bf16[4,2,24,768]{3,2,0,1:T(8,128)(2,1)}, bf16[4,2,24,768]{3,2,0,1:T(8,128)(2,1)}, u32[]{:S(2)}, u32[]{:S(2)}) collective-permute-start(bf16[4,2,24,768]{3,2,0,1:T(8,128)(2,1)} %copy.19), channel_id=1, source_target_pairs={{0,4},{2,6},{4,0},{6,2},{8,12},{10,14},{12,8},{14,10},{16,20},{18,... | collective-permute-start | bytes 884744 | tf_op jit(solution)/shard_map/ppermute | solution.py:34
  8.8 9.4 %collective-permute-start = (bf16[4,2,24,768]{3,2,0,1:T(8,128)(2,1)}, bf16[4,2,24,768]{3,2,0,1:T(8,128)(2,1)}, u32[]{:S(2)}, u32[]{:S(2)}) collective-permute-start(bf16[4,2,24,768]{3,2,0,1:T(8,128)(2,1)} %copy.17), channel_id=1, source_target_pairs={{0,2},{2,0},{4,6},{6,4},{8,10},{10,8},{12,14},{14,12},{16,18},{18,... | collective-permute-start | bytes 884744 | tf_op jit(solution)/shard_map/ppermute | solution.py:34
  10.3 1.3 %copy-start.8 = (bf16[768,768]{1,0:T(8,128)(2,1)S(1)}, bf16[768,768]{1,0:T(8,128)(2,1)}, u32[]{:S(2)}) copy-start(bf16[768,768]{1,0:T(8,128)(2,1)} %constant.162.clone.re_ref.refs_1_) | copy-start | bytes 3538948
  13.6 5.7 %copy-start.10 = (bf16[768,768]{1,0:T(8,128)(2,1)}, bf16[768,768]{1,0:T(8,128)(2,1)S(1)}, u32[]{:S(2)}) copy-start(bf16[768,768]{1,0:T(8,128)(2,1)S(1)} %shard_map.95.refs_1_) | copy-start | bytes 3538948
  16.4 5.2 %collective-permute-start.3 = (bf16[4,24,768]{2,1,0:T(8,128)(2,1)S(1)}, bf16[4,24,768]{2,1,0:T(8,128)(2,1)S(1)}, u32[]{:S(2)}, u32[]{:S(2)}) collective-permute-start(bf16[4,24,768]{2,1,0:T(8,128)(2,1)S(1)} %fusion.5), channel_id=1, source_target_pairs={{0,2},{2,0},{4,6},{6,4},{8,10},{10,8},{12,14},{14,12},{16,18},{18,... | collective-permute-start | bytes 442376 | tf_op jit(solution)/shard_map/ppermute | solution.py:34
  19.3 5.2 %collective-permute-start.1 = (bf16[4,24,768]{2,1,0:T(8,128)(2,1)S(1)}, bf16[4,24,768]{2,1,0:T(8,128)(2,1)S(1)}, u32[]{:S(2)}, u32[]{:S(2)}) collective-permute-start(bf16[4,24,768]{2,1,0:T(8,128)(2,1)S(1)} %fusion.4), channel_id=1, source_target_pairs={{0,4},{2,6},{4,0},{6,2},{8,12},{10,14},{12,8},{14,10},{16,20},{18,... | collective-permute-start | bytes 442376 | tf_op jit(solution)/shard_map/ppermute | solution.py:34
  24.6 4.5 %collective-permute-start.4 = (bf16[24,1536]{1,0:T(8,128)(2,1)S(1)}, bf16[24,1536]{1,0:T(8,128)(2,1)S(1)}, u32[]{:S(2)}, u32[]{:S(2)}) collective-permute-start(bf16[24,1536]{1,0:T(8,128)(2,1)S(1)} %get-tuple-element.86), channel_id=1, source_target_pairs={{0,8},{2,10},{4,12},{6,14},{8,0},{10,2},{12,4},{14,6},{16,24},{18,... | collective-permute-start | bytes 221192 | tf_op jit(solution)/shard_map/ppermute | solution.py:34
  26.2 6.5 %collective-permute-start.5 = (bf16[24,1536]{1,0:T(8,128)(2,1)S(1)}, bf16[24,1536]{1,0:T(8,128)(2,1)S(1)}, u32[]{:S(2)}, u32[]{:S(2)}) collective-permute-start(bf16[24,1536]{1,0:T(8,128)(2,1)S(1)} %get-tuple-element.87), channel_id=1, source_target_pairs={{0,16},{2,18},{4,20},{6,22},{8,24},{10,26},{12,28},{14,30},{16,0},... | collective-permute-start | bytes 221192 | tf_op jit(solution)/shard_map/ppermute | solution.py:34
  28.8 6.3 %collective-permute-start.6 = (bf16[24,1536]{1,0:T(8,128)(2,1)S(1)}, bf16[24,1536]{1,0:T(8,128)(2,1)S(1)}, u32[]{:S(2)}, u32[]{:S(2)}) collective-permute-start(bf16[24,1536]{1,0:T(8,128)(2,1)S(1)} %get-tuple-element.88), channel_id=1, source_target_pairs={{0,24},{2,26},{4,28},{6,30},{8,16},{10,18},{12,20},{14,22},{16,8},... | collective-permute-start | bytes 221192 | tf_op jit(solution)/shard_map/ppermute | solution.py:34
  35.1 6.4 %collective-permute-start.9 = (bf16[24,1536]{1,0:T(8,128)(2,1)S(1)}, bf16[24,1536]{1,0:T(8,128)(2,1)S(1)}, u32[]{:S(2)}, u32[]{:S(2)}) collective-permute-start(bf16[24,1536]{1,0:T(8,128)(2,1)S(1)} %pad_maximum_fusion.10), channel_id=1, source_target_pairs={{0,24},{2,26},{4,28},{6,30},{8,16},{10,18},{12,20},{14,22},{16,8},... | collective-permute-start | bytes 221192 | tf_op jit(solution)/shard_map/ppermute | solution.py:34
  36.0 6.8 %collective-permute-start.8 = (bf16[24,1536]{1,0:T(8,128)(2,1)S(1)}, bf16[24,1536]{1,0:T(8,128)(2,1)S(1)}, u32[]{:S(2)}, u32[]{:S(2)}) collective-permute-start(bf16[24,1536]{1,0:T(8,128)(2,1)S(1)} %pad_maximum_fusion.10), channel_id=1, source_target_pairs={{0,16},{2,18},{4,20},{6,22},{8,24},{10,26},{12,28},{14,30},{16,0},... | collective-permute-start | bytes 221192 | tf_op jit(solution)/shard_map/ppermute | solution.py:34
  36.4 6.4 %collective-permute-start.7 = (bf16[24,1536]{1,0:T(8,128)(2,1)S(1)}, bf16[24,1536]{1,0:T(8,128)(2,1)S(1)}, u32[]{:S(2)}, u32[]{:S(2)}) collective-permute-start(bf16[24,1536]{1,0:T(8,128)(2,1)S(1)} %pad_maximum_fusion.10), channel_id=1, source_target_pairs={{0,8},{2,10},{4,12},{6,14},{8,0},{10,2},{12,4},{14,6},{16,24},{18,... | collective-permute-start | bytes 221192 | tf_op jit(solution)/shard_map/ppermute | solution.py:34
  42.9 1.3 %copy-start.1 = (bf16[1,384,1536]{2,1,0:T(8,128)(2,1)S(1)}, bf16[1,384,1536]{2,1,0:T(8,128)(2,1)}, u32[]{:S(2)}) copy-start(bf16[1,384,1536]{2,1,0:T(8,128)(2,1)} %param.7) | copy-start | bytes 3538948
  43.0 6.7 %collective-permute-start.12 = (bf16[4,24,768]{2,1,0:T(8,128)(2,1)S(1)}, bf16[4,24,768]{2,1,0:T(8,128)(2,1)S(1)}, u32[]{:S(2)}, u32[]{:S(2)}) collective-permute-start(bf16[4,24,768]{2,1,0:T(8,128)(2,1)S(1)} %get-tuple-element.91), channel_id=1, source_target_pairs={{0,2},{2,0},{4,6},{6,4},{8,10},{10,8},{12,14},{14,12},{16,18},{18,... | collective-permute-start | bytes 442376 | tf_op jit(solution)/shard_map/ppermute | solution.py:34
  44.4 7.0 %collective-permute-start.10 = (bf16[4,24,768]{2,1,0:T(8,128)(2,1)S(1)}, bf16[4,24,768]{2,1,0:T(8,128)(2,1)S(1)}, u32[]{:S(2)}, u32[]{:S(2)}) collective-permute-start(bf16[4,24,768]{2,1,0:T(8,128)(2,1)S(1)} %get-tuple-element.92), channel_id=1, source_target_pairs={{0,4},{2,6},{4,0},{6,2},{8,12},{10,14},{12,8},{14,10},{16,20},{18,... | collective-permute-start | bytes 442376 | tf_op jit(solution)/shard_map/ppermute | solution.py:34
  49.8 6.8 %collective-permute-start.13 = (bf16[4,2,24,768]{3,2,0,1:T(8,128)(2,1)S(1)}, bf16[4,2,24,768]{3,2,0,1:T(8,128)(2,1)S(1)}, u32[]{:S(2)}, u32[]{:S(2)}) collective-permute-start(bf16[4,2,24,768]{3,2,0,1:T(8,128)(2,1)S(1)} %reverse_select_fusion.2), channel_id=1, source_target_pairs={{0,4},{2,6},{4,0},{6,2},{8,12},{10,14},{12,8},{14,10},{16,20},{18,... | collective-permute-start | bytes 884744 | tf_op jit(solution)/shard_map/ppermute | solution.py:34
  51.6 6.8 %collective-permute-start.11 = (bf16[4,2,24,768]{3,2,1,0:T(8,128)(2,1)S(1)}, bf16[4,2,24,768]{3,2,1,0:T(8,128)(2,1)S(1)}, u32[]{:S(2)}, u32[]{:S(2)}) collective-permute-start(bf16[4,2,24,768]{3,2,1,0:T(8,128)(2,1)S(1)} %reverse_select_fusion.3), channel_id=1, source_target_pairs={{0,2},{2,0},{4,6},{6,4},{8,10},{10,8},{12,14},{14,12},{16,18},{18,... | collective-permute-start | bytes 884744 | tf_op jit(solution)/shard_map/ppermute | solution.py:34
  58.7 1.0 copy-start.18
  59.7 1.3 %copy-start.4 = (bf16[768,768]{1,0:T(8,128)(2,1)S(1)}, bf16[768,768]{1,0:T(8,128)(2,1)}, u32[]{:S(2)}) copy-start(bf16[768,768]{1,0:T(8,128)(2,1)} %constant.164.clone.table_ref) | copy-start | bytes 3538948
  59.8 3.5 %collective-permute-start.14 = (bf16[768,768]{1,0:T(8,128)(2,1)S(1)}, bf16[768,768]{1,0:T(8,128)(2,1)S(1)}, u32[]{:S(2)}, u32[]{:S(2)}) collective-permute-start(bf16[768,768]{1,0:T(8,128)(2,1)S(1)} %pad_maximum_fusion.shaped_ref), channel_id=1, source_target_pairs={{0,1},{1,0},{2,3},{3,2},{4,5},{5,4},{6,7},{7,6},{8,9},{9,8},{10,11... | collective-permute-start | bytes 3538952 | tf_op jit(solution)/shard_map/ppermute | solution.py:290
  61.0 1.1 copy-start.13
  61.0 1.1 copy-start.15
  61.0 1.1 %copy-start.17 = (bf16[384,384]{1,0:T(8,128)(2,1)S(1)}, bf16[384,384]{1,0:T(8,128)(2,1)}, u32[]{:S(2)}) copy-start(bf16[384,384]{1,0:T(8,128)(2,1)} %copy-done.16) | copy-start | bytes 884740
  61.0 1.2 %copy-start.19 = (bf16[384,384]{1,0:T(8,128)(2,1)S(1)}, bf16[384,384]{1,0:T(8,128)(2,1)}, u32[]{:S(2)}) copy-start(bf16[384,384]{1,0:T(8,128)(2,1)} %copy-done.18) | copy-start | bytes 884740
  62.2 1.7 %copy-start.3 = (bf16[768,768]{1,0:T(8,128)(2,1)S(1)}, bf16[768,768]{1,0:T(8,128)(2,1)}, u32[]{:S(2)}) copy-start(bf16[768,768]{1,0:T(8,128)(2,1)} %constant.165.clone.table_ref) | copy-start | bytes 3538948
  65.2 10.2 %collective-permute-start.19 = (bf16[48,768]{1,0:T(8,128)(2,1)S(1)}, bf16[48,768]{1,0:T(8,128)(2,1)S(1)}, u32[]{:S(2)}, u32[]{:S(2)}) collective-permute-start(bf16[48,768]{1,0:T(8,128)(2,1)S(1)} %get-tuple-element.72), channel_id=1, source_target_pairs={{0,20},{2,22},{4,16},{6,18},{8,28},{10,30},{12,24},{14,26},{16,4},... | collective-permute-start | bytes 221192 | tf_op jit(solution)/shard_map/ppermute | solution.py:34
  65.7 9.7 %collective-permute-start.18 = (bf16[48,768]{1,0:T(8,128)(2,1)S(1)}, bf16[48,768]{1,0:T(8,128)(2,1)S(1)}, u32[]{:S(2)}, u32[]{:S(2)}) collective-permute-start(bf16[48,768]{1,0:T(8,128)(2,1)S(1)} %get-tuple-element.74), channel_id=1, source_target_pairs={{0,4},{2,6},{4,0},{6,2},{8,12},{10,14},{12,8},{14,10},{16,20},{18,... | collective-permute-start | bytes 221192 | tf_op jit(solution)/shard_map/ppermute | solution.py:34
  67.4 9.2 %collective-permute-start.17 = (bf16[48,768]{1,0:T(8,128)(2,1)S(1)}, bf16[48,768]{1,0:T(8,128)(2,1)S(1)}, u32[]{:S(2)}, u32[]{:S(2)}) collective-permute-start(bf16[48,768]{1,0:T(8,128)(2,1)S(1)} %get-tuple-element.76), channel_id=1, source_target_pairs={{0,18},{2,16},{4,22},{6,20},{8,26},{10,24},{12,30},{14,28},{16,2},... | collective-permute-start | bytes 221192 | tf_op jit(solution)/shard_map/ppermute | solution.py:34
  69.3 7.4 %collective-permute-start.16 = (bf16[48,768]{1,0:T(8,128)(2,1)S(1)}, bf16[48,768]{1,0:T(8,128)(2,1)S(1)}, u32[]{:S(2)}, u32[]{:S(2)}) collective-permute-start(bf16[48,768]{1,0:T(8,128)(2,1)S(1)} %get-tuple-element.78), channel_id=1, source_target_pairs={{0,2},{2,0},{4,6},{6,4},{8,10},{10,8},{12,14},{14,12},{16,18},{18,... | collective-permute-start | bytes 221192 | tf_op jit(solution)/shard_map/ppermute | solution.py:34
  71.1 26.5 %copy-start.11 = (bf16[768,768]{1,0:T(8,128)(2,1)S(1)}, bf16[768,768]{1,0:T(8,128)(2,1)}, u32[]{:S(2)}) copy-start(bf16[768,768]{1,0:T(8,128)(2,1)} %copy-done.10) | copy-start | bytes 3538948
  71.1 10.2 %collective-permute-start.15 = (bf16[48,768]{1,0:T(8,128)(2,1)S(1)}, bf16[48,768]{1,0:T(8,128)(2,1)S(1)}, u32[]{:S(2)}, u32[]{:S(2)}) collective-permute-start(bf16[48,768]{1,0:T(8,128)(2,1)S(1)} %get-tuple-element.80), channel_id=1, source_target_pairs={{0,16},{2,18},{4,20},{6,22},{8,24},{10,26},{12,28},{14,30},{16,0},... | collective-permute-start | bytes 221192 | tf_op jit(solution)/shard_map/ppermute | solution.py:34
  75.4 7.2 %collective-permute-start.24 = (bf16[48,768]{1,0:T(8,128)(2,1)S(1)}, bf16[48,768]{1,0:T(8,128)(2,1)S(1)}, u32[]{:S(2)}, u32[]{:S(2)}) collective-permute-start(bf16[48,768]{1,0:T(8,128)(2,1)S(1)} %get-tuple-element.55), channel_id=1, source_target_pairs={{0,10},{2,8},{4,14},{6,12},{8,2},{10,0},{12,6},{14,4},{16,26},{18,... | collective-permute-start | bytes 221192 | tf_op jit(solution)/shard_map/ppermute | solution.py:34
  75.4 10.9 %collective-permute-start.23 = (bf16[48,768]{1,0:T(8,128)(2,1)S(1)}, bf16[48,768]{1,0:T(8,128)(2,1)S(1)}, u32[]{:S(2)}, u32[]{:S(2)}) collective-permute-start(bf16[48,768]{1,0:T(8,128)(2,1)S(1)} %get-tuple-element.53), channel_id=1, source_target_pairs={{0,24},{2,26},{4,28},{6,30},{8,16},{10,18},{12,20},{14,22},{16,8},... | collective-permute-start | bytes 221192 | tf_op jit(solution)/shard_map/ppermute | solution.py:34
  76.7 9.7 %collective-permute-start.22 = (bf16[48,768]{1,0:T(8,128)(2,1)S(1)}, bf16[48,768]{1,0:T(8,128)(2,1)S(1)}, u32[]{:S(2)}, u32[]{:S(2)}) collective-permute-start(bf16[48,768]{1,0:T(8,128)(2,1)S(1)} %get-tuple-element.51), channel_id=1, source_target_pairs={{0,8},{2,10},{4,12},{6,14},{8,0},{10,2},{12,4},{14,6},{16,24},{18,... | collective-permute-start | bytes 221192 | tf_op jit(solution)/shard_map/ppermute | solution.py:34
  76.7 11.5 %collective-permute-start.21 = (bf16[48,768]{1,0:T(8,128)(2,1)S(1)}, bf16[48,768]{1,0:T(8,128)(2,1)S(1)}, u32[]{:S(2)}, u32[]{:S(2)}) collective-permute-start(bf16[48,768]{1,0:T(8,128)(2,1)S(1)} %get-tuple-element.49), channel_id=1, source_target_pairs={{0,22},{2,20},{4,18},{6,16},{8,30},{10,28},{12,26},{14,24},{16,6},... | collective-permute-start | bytes 221192 | tf_op jit(solution)/shard_map/ppermute | solution.py:34
  81.3 9.1 %collective-permute-start.20 = (bf16[48,768]{1,0:T(8,128)(2,1)S(1)}, bf16[48,768]{1,0:T(8,128)(2,1)S(1)}, u32[]{:S(2)}, u32[]{:S(2)}) collective-permute-start(bf16[48,768]{1,0:T(8,128)(2,1)S(1)} %get-tuple-element.47), channel_id=1, source_target_pairs={{0,6},{2,4},{4,2},{6,0},{8,14},{10,12},{12,10},{14,8},{16,22},{18,... | collective-permute-start | bytes 221192 | tf_op jit(solution)/shard_map/ppermute | solution.py:34
  82.7 14.9 %collective-permute-start.29 = (bf16[48,768]{1,0:T(8,128)(2,1)S(1)}, bf16[48,768]{1,0:T(8,128)(2,1)S(1)}, u32[]{:S(2)}, u32[]{:S(2)}) collective-permute-start(bf16[48,768]{1,0:T(8,128)(2,1)S(1)} %get-tuple-element.61), channel_id=1, source_target_pairs={{0,30},{2,28},{4,26},{6,24},{8,22},{10,20},{12,18},{14,16},{16,14}... | collective-permute-start | bytes 221192 | tf_op jit(solution)/shard_map/ppermute | solution.py:34
  86.4 11.1 %collective-permute-start.28 = (bf16[48,768]{1,0:T(8,128)(2,1)S(1)}, bf16[48,768]{1,0:T(8,128)(2,1)S(1)}, u32[]{:S(2)}, u32[]{:S(2)}) collective-permute-start(bf16[48,768]{1,0:T(8,128)(2,1)S(1)} %get-tuple-element.60), channel_id=1, source_target_pairs={{0,14},{2,12},{4,10},{6,8},{8,6},{10,4},{12,2},{14,0},{16,30},{18,... | collective-permute-start | bytes 221192 | tf_op jit(solution)/shard_map/ppermute | solution.py:34
  86.4 11.1 %collective-permute-start.27 = (bf16[48,768]{1,0:T(8,128)(2,1)S(1)}, bf16[48,768]{1,0:T(8,128)(2,1)S(1)}, u32[]{:S(2)}, u32[]{:S(2)}) collective-permute-start(bf16[48,768]{1,0:T(8,128)(2,1)S(1)} %get-tuple-element.59), channel_id=1, source_target_pairs={{0,28},{2,30},{4,24},{6,26},{8,20},{10,22},{12,16},{14,18},{16,12}... | collective-permute-start | bytes 221192 | tf_op jit(solution)/shard_map/ppermute | solution.py:34
  88.1 9.3 %collective-permute-start.26 = (bf16[48,768]{1,0:T(8,128)(2,1)S(1)}, bf16[48,768]{1,0:T(8,128)(2,1)S(1)}, u32[]{:S(2)}, u32[]{:S(2)}) collective-permute-start(bf16[48,768]{1,0:T(8,128)(2,1)S(1)} %get-tuple-element.58), channel_id=1, source_target_pairs={{0,12},{2,14},{4,8},{6,10},{8,4},{10,6},{12,0},{14,2},{16,28},{18,... | collective-permute-start | bytes 221192 | tf_op jit(solution)/shard_map/ppermute | solution.py:34
  90.4 7.1 %collective-permute-start.25 = (bf16[48,768]{1,0:T(8,128)(2,1)S(1)}, bf16[48,768]{1,0:T(8,128)(2,1)S(1)}, u32[]{:S(2)}, u32[]{:S(2)}) collective-permute-start(bf16[48,768]{1,0:T(8,128)(2,1)S(1)} %get-tuple-element.57), channel_id=1, source_target_pairs={{0,26},{2,24},{4,30},{6,28},{8,18},{10,16},{12,22},{14,20},{16,10}... | collective-permute-start | bytes 221192 | tf_op jit(solution)/shard_map/ppermute | solution.py:34
  97.6 6.4 %copy-start.7 = (bf16[768,768]{1,0:T(8,128)(2,1)S(1)}, bf16[768,768]{1,0:T(8,128)(2,1)}, u32[]{:S(2)}) copy-start(bf16[768,768]{1,0:T(8,128)(2,1)} %constant.163.clone.im_ref.refs_2_) | copy-start | bytes 3538948
  97.6 6.4 %copy-start.9 = (bf16[768,768]{1,0:T(8,128)(2,1)S(1)}, bf16[768,768]{1,0:T(8,128)(2,1)}, u32[]{:S(2)}) copy-start(bf16[768,768]{1,0:T(8,128)(2,1)} %constant.162.clone.re_ref.refs_1_) | copy-start | bytes 3538948
  100.0 11.1 %all-to-all-start = ((f32[32,1,16]{2,1,0:T(1,128)}), f32[32,1,16]{2,1,0:T(1,128)S(1)}, u32[]{:S(2)}, u32[]{:S(2)}) async-start(f32[32,1,16]{2,1,0:T(1,128)} %bitcast.53), calls=%async_computation | async-start | bytes 32768 | tf_op jit(solution)/shard_map/all_to_all | solution.py:335
  (3 other events, 2.4 us)

commit v9 on v6

--- a/solution.py
+++ b/solution.py
@@ -9,6 +9,8 @@
 
 bf16 = jnp.bfloat16
 f32 = jnp.float32
+LANES = 5
+LATE = 4
 
 
 def propagator(grid_size):
@@ -145,7 +147,8 @@
     )
 
 
-def coupling_kernel(block_rows, by_xor, fields_ref, targets_ref, out_ref):
+def coupling_kernel(block_rows, by_xor, first, fields_ref, targets_ref, *rest):
+    out_ref = rest[-1]
     modes = out_ref.shape[1]
     product = lax.dot_general(
         fields_ref[...], targets_ref[...], (((1,), (1,)), ((), ())), preferred_element_type=f32
@@ -166,16 +169,21 @@
         product = exactly(groups(left), product, ((1,), (0,)))
     product = exactly(product, groups(right), ((1,), (1,)))
     by_re, by_im = product[:, :modes], product[:, modes:]
-    mode = lax.broadcasted_iota(jnp.int32, (modes, 2 * modes), 0)
+    sources = left // block_rows
+    mode = lax.broadcasted_iota(jnp.int32, (modes, sources), 0)
     if by_xor:
         mode = mode ^ lax.axis_index("modes")
         mode = mode % (modes // 2) * 2 + mode // (modes // 2)
-    from_row = lax.broadcasted_iota(jnp.int32, (modes, 2 * modes), 1)
+    from_row = lax.broadcasted_iota(jnp.int32, (modes, sources), 1) + 2 * first
     real = jnp.where(from_row == 2 * mode, 1.0, 0.0).astype(f32)
     imag = jnp.where(from_row == 2 * mode + 1, 1.0, 0.0).astype(f32)
     inner = ((1,), (0,))
-    out_ref[:modes] = exactly(real, by_re, inner) + exactly(imag, by_im, inner)
-    out_ref[modes:] = exactly(imag, by_re, inner) - exactly(real, by_im, inner)
+    total_re = exactly(real, by_re, inner) + exactly(imag, by_im, inner)
+    total_im = exactly(imag, by_re, inner) - exactly(real, by_im, inner)
+    if len(rest) > 1:
+        total_re, total_im = total_re + rest[0][:modes], total_im + rest[0][modes:]
+    out_ref[:modes] = total_re
+    out_ref[modes:] = total_im
 
 
 def kernel_call(kernel, shape, dtype, flops, operands, grant=12, **more):
@@ -219,6 +227,7 @@
             [bf16, f32, bf16, f32],
             8 * local_rows * double_width,
             (forward[0], backward[0]),
+            grant=52,
             in_specs=[pl.BlockSpec(memory_space=pltpu.HBM)] * 2,
             scratch_shapes=[pltpu.VMEM((local_rows, double_width), bf16)] * 2
             + [pltpu.SemaphoreType.DMA((2 * local_rows // (4 * block_rows),))],
@@ -300,9 +309,14 @@
     blocks = blocks.reshape(count, 2 * block_rows, grid_size)
     if count <= 16:
         turns = [at // 2 + count // 2 * (at % 2) for at in range(count)]
-        pixels = tuple(exchange(pick(blocks, me ^ e, 0), e, count) if e else pick(blocks, me, 0) for e in turns)
-    else:
-        pixels = (lax.all_to_all(blocks, "modes", 0, 0, tiled=True),)
+        pixels = [pick(blocks, me, 0)]
+        for at, e in enumerate(turns[1:], 1):
+            block = pick(blocks, me ^ e, 0)
+            if at > LANES:
+                block, pixels[at - LANES] = lax.optimization_barrier((block, pixels[at - LANES]))
+            pixels.append(exchange(block, e, count))
+    else:
+        pixels = [lax.all_to_all(blocks, "modes", 0, 0, tiled=True)]
 
     output_fields = kernel_call(
         lambda *refs: fields_kernel(block_rows, *refs),
@@ -315,15 +329,20 @@
     seen = kernel_call(
         targets_kernel, column_shape, bf16, matmul, (targets.reshape(column_shape), full_re, full_im)
     )
-    pixels, output_fields, seen = lax.optimization_barrier((pixels, output_fields, seen))
-
-    term = kernel_call(
-        lambda *refs: coupling_kernel(block_rows, len(pixels) > 1, *refs),
-        (2 * mode_total, mode_total),
-        f32,
-        matmul,
-        (jnp.concatenate(pixels, 0).reshape(column_shape), seen),
-    )
+    cut = len(pixels) - LATE if len(pixels) > LATE else len(pixels)
+    seen, output_fields = lax.optimization_barrier((seen, output_fields))
+    term, at = None, 0
+    for group in (pixels[:cut], pixels[cut:]):
+        if group:
+            rows = jnp.concatenate(group, 0).reshape(-1, grid_size)
+            term = kernel_call(
+                lambda *refs: coupling_kernel(block_rows, len(pixels) > 1, at, *refs),
+                (2 * mode_total, mode_total),
+                f32,
+                2 * rows.shape[0] * 2 * local_rows * grid_size,
+                (rows, seen) if term is None else (rows, seen, term),
+            )
+            at += len(group)
     pieces = lax.all_to_all(term, ("modes", "rows"), 0, 0, tiled=True)
     coupling = jnp.sum(pieces, 0, keepdims=True)
     return (phase_plane, output_fields[None], coupling)

time: 108 us -> 106 us (0.981)
  waiting for transfers between devices: 39.4 us -> 35.5 us
  starting transfers between devices: 47.8 us -> 51.1 us
  local copies, waits for them, and re-layouts: 4.73 us -> 2.18 us
  Pallas kernels: 10.7 us -> 12.1 us
    ppermute x29, waiting for transfers between devices: 32.7 us -> 28.9 us  [exchange(): lax.ppermute(values, 'modes', [(i, i ^ offset) for i in range(count)])]
    ppermute x29, starting transfers between devices: 44.9 us -> 47.5 us  [exchange(): lax.ppermute(values, 'modes', [(i, i ^ offset) for i in range(count)])]
    unnamed x47 -> x39, local copies, waits for them, and re-layouts: 4.24 us -> 1.7 us
    pallas_call x6 -> x7, Pallas kernels: 10.7 us -> 12.1 us  [kernel_call(): pl.pallas_call(kernel, out_shape=out_shape, compiler_params=pltpu.Compile...]
  transfers between devices with their start and end apart: 31 -> 31, of which waited for: 16 -> 14; matrix products, arithmetic and copies ran while one was open for 2% -> 2% of each run, Pallas kernels for 6% -> 7%
where the time goes in v9:
time: 106 us; the launch traced here: 105 us
  starting transfers between devices  51.1 us (48%)
  waiting for transfers between devices  35.5 us (33%)
  Pallas kernels  12.1 us (11%)
  other arithmetic  3.4 us (3%)
  local copies, waits for them, and re-layouts  2.18 us (2%)
  between operations  1.19 us (1%)
    ppermute x29, starting transfers between devices, exchange(): lax.ppermute(values, 'modes', [(i, i ^ offset) for i in range(count)])  47.5 us
    ppermute x29, waiting for transfers between devices, exchange(): lax.ppermute(values, 'modes', [(i, i ^ offset) for i in range(count)])  28.9 us
    pallas_call x7, Pallas kernels, kernel_call(): pl.pallas_call(kernel, out_shape=out_shape, compiler_params=pltpu.Compile...  12.1 us
    all_to_all x1, waiting for transfers between devices, local(): pieces = lax.all_to_all(term, ('modes', 'rows'), 0, 0, tiled=True)  5.99 us
    all_to_all x1, starting transfers between devices, local(): pieces = lax.all_to_all(term, ('modes', 'rows'), 0, 0, tiled=True)  3.45 us
  transfers between devices with their start and end apart: 31, of which 14 were waited for; matrix products, arithmetic and copies ran while one was open for 2% of the time, Pallas kernels for 7%

profile of v9, /device:TPU:0, one launch (start us, length us, event | category | flops | bytes accessed | tf_op | source)
XLA Modules:
  0.0 105.5 jit_solution(12733767687031746977)
XLA Ops:
  0.6 1.8 %shard_map.94 = (bf16[192,768]{1,0:T(8,128)(2,1)S(1)}, f32[192,768]{1,0:T(8,128)S(1)}, bf16[192,768]{1,0:T(8,128)(2,1)S(1)}, f32[192,768]{1,0:T(8,128)S(1)}) custom-call(bf16[384,1536]{1,0:T(8,128)(2,1)} %bitcast.100, bf16[384,1536]{1,0:T(8,128)(2,1)} %bitcast.103), custom_call_target="tpu_custom_call" | custom-call | flops 4718592 | bytes 4194304 | tf_op jit(solution)/shard_map/pallas_call | solution.py:197
  2.5 3.0 %collective-permute-start.2 = (bf16[4,2,24,768]{3,2,0,1:T(8,128)(2,1)S(1)}, bf16[4,2,24,768]{3,2,0,1:T(8,128)(2,1)S(1)}, u32[]{:S(2)}, u32[]{:S(2)}) collective-permute-start(bf16[4,2,24,768]{3,2,0,1:T(8,128)(2,1)S(1)} %copy.19), channel_id=1, source_target_pairs={{0,4},{2,6},{4,0},{6,2},{8,12},{10,14},{12,8},{14,10},{16,20},{18,... | collective-permute-start | bytes 884744 | tf_op jit(solution)/shard_map/ppermute | solution.py:35
  5.5 1.6 %collective-permute-start = (bf16[4,2,24,768]{3,2,0,1:T(8,128)(2,1)S(1)}, bf16[4,2,24,768]{3,2,0,1:T(8,128)(2,1)S(1)}, u32[]{:S(2)}, u32[]{:S(2)}) collective-permute-start(bf16[4,2,24,768]{3,2,0,1:T(8,128)(2,1)S(1)} %copy.17), channel_id=1, source_target_pairs={{0,2},{2,0},{4,6},{6,4},{8,10},{10,8},{12,14},{14,12},{16,18},{18,... | collective-permute-start | bytes 884744 | tf_op jit(solution)/shard_map/ppermute | solution.py:35
  7.1 5.4 %collective-permute-done.2 = bf16[4,2,24,768]{3,2,0,1:T(8,128)(2,1)S(1)} collective-permute-done((bf16[4,2,24,768]{3,2,0,1:T(8,128)(2,1)S(1)}, bf16[4,2,24,768]{3,2,0,1:T(8,128)(2,1)S(1)}, u32[]{:S(2)}, u32[]{:S(2)}) %collective-permute-start.2) | collective-permute-done | bytes 294944 | tf_op jit(solution)/shard_map/ppermute | solution.py:35
  12.6 1.8 %collective-permute-start.3 = (bf16[4,24,768]{2,1,0:T(8,128)(2,1)S(1)}, bf16[4,24,768]{2,1,0:T(8,128)(2,1)S(1)}, u32[]{:S(2)}, u32[]{:S(2)}) collective-permute-start(bf16[4,24,768]{2,1,0:T(8,128)(2,1)S(1)} %fusion.5), channel_id=1, source_target_pairs={{0,2},{2,0},{4,6},{6,4},{8,10},{10,8},{12,14},{14,12},{16,18},{18,... | collective-permute-start | bytes 442376 | tf_op jit(solution)/shard_map/ppermute | solution.py:35
  14.5 1.6 %collective-permute-start.1 = (bf16[4,24,768]{2,1,0:T(8,128)(2,1)S(1)}, bf16[4,24,768]{2,1,0:T(8,128)(2,1)S(1)}, u32[]{:S(2)}, u32[]{:S(2)}) collective-permute-start(bf16[4,24,768]{2,1,0:T(8,128)(2,1)S(1)} %fusion.4), channel_id=1, source_target_pairs={{0,4},{2,6},{4,0},{6,2},{8,12},{10,14},{12,8},{14,10},{16,20},{18,... | collective-permute-start | bytes 442376 | tf_op jit(solution)/shard_map/ppermute | solution.py:35
  16.1 1.8 %collective-permute-done.3 = bf16[4,24,768]{2,1,0:T(8,128)(2,1)S(1)} collective-permute-done((bf16[4,24,768]{2,1,0:T(8,128)(2,1)S(1)}, bf16[4,24,768]{2,1,0:T(8,128)(2,1)S(1)}, u32[]{:S(2)}, u32[]{:S(2)}) %collective-permute-start.3) | collective-permute-done | bytes 147488 | tf_op jit(solution)/shard_map/ppermute | solution.py:35
  17.8 1.8 %collective-permute-done.1 = bf16[4,24,768]{2,1,0:T(8,128)(2,1)S(1)} collective-permute-done((bf16[4,24,768]{2,1,0:T(8,128)(2,1)S(1)}, bf16[4,24,768]{2,1,0:T(8,128)(2,1)S(1)}, u32[]{:S(2)}, u32[]{:S(2)}) %collective-permute-start.1) | collective-permute-done | bytes 147488 | tf_op jit(solution)/shard_map/ppermute | solution.py:35
  19.8 1.6 %collective-permute-start.4 = (bf16[24,1536]{1,0:T(8,128)(2,1)S(1)}, bf16[24,1536]{1,0:T(8,128)(2,1)S(1)}, u32[]{:S(2)}, u32[]{:S(2)}) collective-permute-start(bf16[24,1536]{1,0:T(8,128)(2,1)S(1)} %get-tuple-element.84), channel_id=1, source_target_pairs={{0,8},{2,10},{4,12},{6,14},{8,0},{10,2},{12,4},{14,6},{16,24},{18,... | collective-permute-start | bytes 221192 | tf_op jit(solution)/shard_map/ppermute | solution.py:35
  21.4 2.6 %collective-permute-start.5 = (bf16[24,1536]{1,0:T(8,128)(2,1)S(1)}, bf16[24,1536]{1,0:T(8,128)(2,1)S(1)}, u32[]{:S(2)}, u32[]{:S(2)}) collective-permute-start(bf16[24,1536]{1,0:T(8,128)(2,1)S(1)} %get-tuple-element.85), channel_id=1, source_target_pairs={{0,16},{2,18},{4,20},{6,22},{8,24},{10,26},{12,28},{14,30},{16,0},... | collective-permute-start | bytes 221192 | tf_op jit(solution)/shard_map/ppermute | solution.py:35
  24.3 3.9 %collective-permute-done.5 = bf16[24,1536]{1,0:T(8,128)(2,1)S(1)} collective-permute-done((bf16[24,1536]{1,0:T(8,128)(2,1)S(1)}, bf16[24,1536]{1,0:T(8,128)(2,1)S(1)}, u32[]{:S(2)}, u32[]{:S(2)}) %collective-permute-start.5) | collective-permute-done | bytes 73760 | tf_op jit(solution)/shard_map/ppermute | solution.py:35
  28.1 2.1 %collective-permute-done.6 = bf16[24,1536]{1,0:T(8,128)(2,1)S(1)} collective-permute-done((bf16[24,1536]{1,0:T(8,128)(2,1)S(1)}, bf16[24,1536]{1,0:T(8,128)(2,1)S(1)}, u32[]{:S(2)}, u32[]{:S(2)}) %collective-permute-start.6) | collective-permute-done | bytes 73760 | tf_op jit(solution)/shard_map/ppermute | solution.py:35
  30.3 0.9 collective-permute-start.9
  31.2 1.5 %collective-permute-start.8 = (bf16[24,1536]{1,0:T(8,128)(2,1)S(1)}, bf16[24,1536]{1,0:T(8,128)(2,1)S(1)}, u32[]{:S(2)}, u32[]{:S(2)}) collective-permute-start(bf16[24,1536]{1,0:T(8,128)(2,1)S(1)} %pad_maximum_fusion.11), channel_id=1, source_target_pairs={{0,16},{2,18},{4,20},{6,22},{8,24},{10,26},{12,28},{14,30},{16,0},... | collective-permute-start | bytes 221192 | tf_op jit(solution)/shard_map/ppermute | solution.py:35
  32.7 2.1 %collective-permute-start.7 = (bf16[24,1536]{1,0:T(8,128)(2,1)S(1)}, bf16[24,1536]{1,0:T(8,128)(2,1)S(1)}, u32[]{:S(2)}, u32[]{:S(2)}) collective-permute-start(bf16[24,1536]{1,0:T(8,128)(2,1)S(1)} %pad_maximum_fusion.11), channel_id=1, source_target_pairs={{0,8},{2,10},{4,12},{6,14},{8,0},{10,2},{12,4},{14,6},{16,24},{18,... | collective-permute-start | bytes 221192 | tf_op jit(solution)/shard_map/ppermute | solution.py:35
  34.8 1.9 %collective-permute-done.9 = bf16[24,1536]{1,0:T(8,128)(2,1)S(1)} collective-permute-done((bf16[24,1536]{1,0:T(8,128)(2,1)S(1)}, bf16[24,1536]{1,0:T(8,128)(2,1)S(1)}, u32[]{:S(2)}, u32[]{:S(2)}) %collective-permute-start.9) | collective-permute-done | bytes 73760 | tf_op jit(solution)/shard_map/ppermute | solution.py:35
  36.7 1.3 %collective-permute-done.8 = bf16[24,1536]{1,0:T(8,128)(2,1)S(1)} collective-permute-done((bf16[24,1536]{1,0:T(8,128)(2,1)S(1)}, bf16[24,1536]{1,0:T(8,128)(2,1)S(1)}, u32[]{:S(2)}, u32[]{:S(2)}) %collective-permute-start.8) | collective-permute-done | bytes 73760 | tf_op jit(solution)/shard_map/ppermute | solution.py:35
  38.2 1.2 %collective-permute-start.12 = (bf16[4,24,768]{2,1,0:T(8,128)(2,1)S(1)}, bf16[4,24,768]{2,1,0:T(8,128)(2,1)S(1)}, u32[]{:S(2)}, u32[]{:S(2)}) collective-permute-start(bf16[4,24,768]{2,1,0:T(8,128)(2,1)S(1)} %get-tuple-element.89), channel_id=1, source_target_pairs={{0,2},{2,0},{4,6},{6,4},{8,10},{10,8},{12,14},{14,12},{16,18},{18,... | collective-permute-start | bytes 442376 | tf_op jit(solution)/shard_map/ppermute | solution.py:35
  39.7 1.5 %collective-permute-start.10 = (bf16[4,24,768]{2,1,0:T(8,128)(2,1)S(1)}, bf16[4,24,768]{2,1,0:T(8,128)(2,1)S(1)}, u32[]{:S(2)}, u32[]{:S(2)}) collective-permute-start(bf16[4,24,768]{2,1,0:T(8,128)(2,1)S(1)} %get-tuple-element.90), channel_id=1, source_target_pairs={{0,4},{2,6},{4,0},{6,2},{8,12},{10,14},{12,8},{14,10},{16,20},{18,... | collective-permute-start | bytes 442376 | tf_op jit(solution)/shard_map/ppermute | solution.py:35
  41.2 3.3 %collective-permute-done.12 = bf16[4,24,768]{2,1,0:T(8,128)(2,1)S(1)} collective-permute-done((bf16[4,24,768]{2,1,0:T(8,128)(2,1)S(1)}, bf16[4,24,768]{2,1,0:T(8,128)(2,1)S(1)}, u32[]{:S(2)}, u32[]{:S(2)}) %collective-permute-start.12) | collective-permute-done | bytes 147488 | tf_op jit(solution)/shard_map/ppermute | solution.py:35
  44.6 1.7 %collective-permute-start.13 = (bf16[4,2,24,768]{3,2,0,1:T(8,128)(2,1)S(1)}, bf16[4,2,24,768]{3,2,0,1:T(8,128)(2,1)S(1)}, u32[]{:S(2)}, u32[]{:S(2)}) collective-permute-start(bf16[4,2,24,768]{3,2,0,1:T(8,128)(2,1)S(1)} %reverse_select_fusion.2), channel_id=1, source_target_pairs={{0,4},{2,6},{4,0},{6,2},{8,12},{10,14},{12,8},{14,10},{16,20},{18,... | collective-permute-start | bytes 884744 | tf_op jit(solution)/shard_map/ppermute | solution.py:35
  47.1 4.3 %collective-permute-done.13 = bf16[4,2,24,768]{3,2,0,1:T(8,128)(2,1)S(1)} collective-permute-done((bf16[4,2,24,768]{3,2,0,1:T(8,128)(2,1)S(1)}, bf16[4,2,24,768]{3,2,0,1:T(8,128)(2,1)S(1)}, u32[]{:S(2)}, u32[]{:S(2)}) %collective-permute-start.13) | collective-permute-done | bytes 294944 | tf_op jit(solution)/shard_map/ppermute | solution.py:35
  51.6 1.7 %collective-permute-done.11 = bf16[4,2,24,768]{3,2,1,0:T(8,128)(2,1)S(1)} collective-permute-done((bf16[4,2,24,768]{3,2,1,0:T(8,128)(2,1)S(1)}, bf16[4,2,24,768]{3,2,1,0:T(8,128)(2,1)S(1)}, u32[]{:S(2)}, u32[]{:S(2)}) %collective-permute-start.11) | collective-permute-done | bytes 294944 | tf_op jit(solution)/shard_map/ppermute | solution.py:35
  54.9 1.0 copy-done.1
  55.9 1.1 %shard_map.95.own_ref = f32[768,768]{1,0:T(8,128)S(1)} custom-call(bf16[768,768]{1,0:T(8,128)(2,1)S(1)} %copy-done.1, bf16[768,768]{1,0:T(8,128)(2,1)S(1)} %pad_maximum_fusion.1.shaped_ref), custom_call_target="tpu_custom_call" | custom-call | flops 905969664 | bytes 4194304 | tf_op jit(solution)/shard_map/pallas_call | solution.py:197
  57.0 0.6 collective-permute-done.14.shaped_ref
  57.6 1.1 %shard_map.96.refs_0_ = bf16[768,768]{1,0:T(8,128)(2,1)S(1)} custom-call(bf16[768,768]{1,0:T(8,128)(2,1)S(1)} %copy-done, bf16[768,768]{1,0:T(8,128)(2,1)S(1)} %collective-permute-done.14.shaped_ref, f32[768,768]{1,0:T(8,128)S(1)} %shard_map.95.own_ref), custom_call_target="tpu_custom_call" | custom-call | flops 905969664 | bytes 4194304 | tf_op jit(solution)/shard_map/pallas_call | solution.py:197
  58.9 0.7 collective-permute-start.27
  59.6 2.5 %collective-permute-start.24 = (bf16[48,768]{1,0:T(8,128)(2,1)S(1)}, bf16[48,768]{1,0:T(8,128)(2,1)S(1)}, u32[]{:S(2)}, u32[]{:S(2)}) collective-permute-start(bf16[48,768]{1,0:T(8,128)(2,1)S(1)} %get-tuple-element.68), channel_id=1, source_target_pairs={{0,20},{2,22},{4,16},{6,18},{8,28},{10,30},{12,24},{14,26},{16,4},... | collective-permute-start | bytes 221192 | tf_op jit(solution)/shard_map/ppermute | solution.py:35
  62.1 1.2 %collective-permute-start.21 = (bf16[48,768]{1,0:T(8,128)(2,1)S(1)}, bf16[48,768]{1,0:T(8,128)(2,1)S(1)}, u32[]{:S(2)}, u32[]{:S(2)}) collective-permute-start(bf16[48,768]{1,0:T(8,128)(2,1)S(1)} %get-tuple-element.71), channel_id=1, source_target_pairs={{0,4},{2,6},{4,0},{6,2},{8,12},{10,14},{12,8},{14,10},{16,20},{18,... | collective-permute-start | bytes 221192 | tf_op jit(solution)/shard_map/ppermute | solution.py:35
  63.3 0.6 collective-permute-start.18
  63.9 1.6 %collective-permute-start.15 = (bf16[48,768]{1,0:T(8,128)(2,1)S(1)}, bf16[48,768]{1,0:T(8,128)(2,1)S(1)}, u32[]{:S(2)}, u32[]{:S(2)}) collective-permute-start(bf16[48,768]{1,0:T(8,128)(2,1)S(1)} %get-tuple-element.77), channel_id=1, source_target_pairs={{0,2},{2,0},{4,6},{6,4},{8,10},{10,8},{12,14},{14,12},{16,18},{18,... | collective-permute-start | bytes 221192 | tf_op jit(solution)/shard_map/ppermute | solution.py:35
  65.5 3.0 %shard_map.97 = bf16[384,1536]{1,0:T(8,128)(2,1)} custom-call(bf16[768,768]{1,0:T(8,128)(2,1)S(1)} %shard_map.96.refs_0_, bf16[768,768]{1,0:T(8,128)(2,1)S(1)} %copy-done.4, bf16[768,768]{1,0:T(8,128)(2,1)S(1)} %copy-done.3), custom_call_target="tpu_custom_call" | custom-call | flops 1811939328 | bytes 4194304 | tf_op jit(solution)/shard_map/pallas_call | solution.py:197
  68.5 2.0 %shard_map.98.refs_1_ = bf16[768,768]{1,0:T(8,128)(2,1)S(1)} custom-call(bf16[768,768]{1,0:T(8,128)(2,1)S(1)} %bitcast.99, bf16[768,768]{1,0:T(8,128)(2,1)S(1)} %copy-done.4, bf16[768,768]{1,0:T(8,128)(2,1)S(1)} %copy-done.3), custom_call_target="tpu_custom_call" | custom-call | flops 1811939328 | bytes 4194304 | tf_op jit(solution)/shard_map/pallas_call | solution.py:197
  70.5 1.2 %collective-permute-start.28 = (bf16[48,768]{1,0:T(8,128)(2,1)S(1)}, bf16[48,768]{1,0:T(8,128)(2,1)S(1)}, u32[]{:S(2)}, u32[]{:S(2)}) collective-permute-start(bf16[48,768]{1,0:T(8,128)(2,1)S(1)} %get-tuple-element.56), channel_id=1, source_target_pairs={{0,6},{2,4},{4,2},{6,0},{8,14},{10,12},{12,10},{14,8},{16,22},{18,... | collective-permute-start | bytes 221192 | tf_op jit(solution)/shard_map/ppermute | solution.py:35
  71.7 1.7 %collective-permute-start.25 = (bf16[48,768]{1,0:T(8,128)(2,1)S(1)}, bf16[48,768]{1,0:T(8,128)(2,1)S(1)}, u32[]{:S(2)}, u32[]{:S(2)}) collective-permute-start(bf16[48,768]{1,0:T(8,128)(2,1)S(1)} %get-tuple-element.48), channel_id=1, source_target_pairs={{0,10},{2,8},{4,14},{6,12},{8,2},{10,0},{12,6},{14,4},{16,26},{18,... | collective-permute-start | bytes 221192 | tf_op jit(solution)/shard_map/ppermute | solution.py:35
  73.5 2.5 %collective-permute-start.22 = (bf16[48,768]{1,0:T(8,128)(2,1)S(1)}, bf16[48,768]{1,0:T(8,128)(2,1)S(1)}, u32[]{:S(2)}, u32[]{:S(2)}) collective-permute-start(bf16[48,768]{1,0:T(8,128)(2,1)S(1)} %get-tuple-element.46), channel_id=1, source_target_pairs={{0,24},{2,26},{4,28},{6,30},{8,16},{10,18},{12,20},{14,22},{16,8},... | collective-permute-start | bytes 221192 | tf_op jit(solution)/shard_map/ppermute | solution.py:35
  76.1 2.6 %collective-permute-start.16 = (bf16[48,768]{1,0:T(8,128)(2,1)S(1)}, bf16[48,768]{1,0:T(8,128)(2,1)S(1)}, u32[]{:S(2)}, u32[]{:S(2)}) collective-permute-start(bf16[48,768]{1,0:T(8,128)(2,1)S(1)} %get-tuple-element.42), channel_id=1, source_target_pairs={{0,22},{2,20},{4,18},{6,16},{8,30},{10,28},{12,26},{14,24},{16,6},... | collective-permute-start | bytes 221192 | tf_op jit(solution)/shard_map/ppermute | solution.py:35
  78.7 3.3 %collective-permute-start.29 = (bf16[48,768]{1,0:T(8,128)(2,1)S(1)}, bf16[48,768]{1,0:T(8,128)(2,1)S(1)}, u32[]{:S(2)}, u32[]{:S(2)}) collective-permute-start(bf16[48,768]{1,0:T(8,128)(2,1)S(1)} %get-tuple-element.62), channel_id=1, source_target_pairs={{0,26},{2,24},{4,30},{6,28},{8,18},{10,16},{12,22},{14,20},{16,10}... | collective-permute-start | bytes 221192 | tf_op jit(solution)/shard_map/ppermute | solution.py:35
  82.1 2.3 %collective-permute-start.26 = (bf16[48,768]{1,0:T(8,128)(2,1)S(1)}, bf16[48,768]{1,0:T(8,128)(2,1)S(1)}, u32[]{:S(2)}, u32[]{:S(2)}) collective-permute-start(bf16[48,768]{1,0:T(8,128)(2,1)S(1)} %get-tuple-element.49), channel_id=1, source_target_pairs={{0,30},{2,28},{4,26},{6,24},{8,22},{10,20},{12,18},{14,16},{16,14}... | collective-permute-start | bytes 221192 | tf_op jit(solution)/shard_map/ppermute | solution.py:35
  84.4 2.3 %collective-permute-start.20 = (bf16[48,768]{1,0:T(8,128)(2,1)S(1)}, bf16[48,768]{1,0:T(8,128)(2,1)S(1)}, u32[]{:S(2)}, u32[]{:S(2)}) collective-permute-start(bf16[48,768]{1,0:T(8,128)(2,1)S(1)} %get-tuple-element.45), channel_id=1, source_target_pairs={{0,28},{2,30},{4,24},{6,26},{8,20},{10,22},{12,16},{14,18},{16,12}... | collective-permute-start | bytes 221192 | tf_op jit(solution)/shard_map/ppermute | solution.py:35
  86.8 3.0 %collective-permute-start.17 = (bf16[48,768]{1,0:T(8,128)(2,1)S(1)}, bf16[48,768]{1,0:T(8,128)(2,1)S(1)}, u32[]{:S(2)}, u32[]{:S(2)}) collective-permute-start(bf16[48,768]{1,0:T(8,128)(2,1)S(1)} %get-tuple-element.43), channel_id=1, source_target_pairs={{0,12},{2,14},{4,8},{6,10},{8,4},{10,6},{12,0},{14,2},{16,28},{18,... | collective-permute-start | bytes 221192 | tf_op jit(solution)/shard_map/ppermute | solution.py:35
  89.8 1.5 %shard_map.99.refs_2_ = f32[32,16]{1,0:T(8,128)S(1)} custom-call(bf16[576,768]{1,0:T(8,128)(2,1)S(1)} %constant_dynamic-update-slice_fusion.refs_0_, bf16[768,768]{1,0:T(8,128)(2,1)S(1)} %shard_map.98.refs_1_), custom_call_target="tpu_custom_call" | custom-call | flops 679477248 | bytes 4194304 | tf_op jit(solution)/shard_map/pallas_call | solution.py:197
  91.9 0.8 collective-permute-done.17
  92.7 1.7 %shard_map.100 = f32[32,16]{1,0:T(8,128)} custom-call(bf16[192,768]{1,0:T(8,128)(2,1)S(1)} %pad_maximum_fusion.10.refs_0_, bf16[768,768]{1,0:T(8,128)(2,1)S(1)} %shard_map.98.refs_1_, f32[32,16]{1,0:T(8,128)S(1)} %shard_map.99.refs_2_), custom_call_target="tpu_custom_call" | custom-call | flops 226492416 | bytes 4194304 | tf_op jit(solution)/shard_map/pallas_call | solution.py:197
  94.3 3.5 %all-to-all-start = ((f32[32,1,16]{2,1,0:T(1,128)}), f32[32,1,16]{2,1,0:T(1,128)S(1)}, u32[]{:S(2)}, u32[]{:S(2)}) async-start(f32[32,1,16]{2,1,0:T(1,128)} %bitcast.53), calls=%async_computation | async-start | bytes 32768 | tf_op jit(solution)/shard_map/all_to_all | solution.py:346
  97.8 1.1 %pad_maximum_fusion = bf16[384,1536]{1,0:T(8,128)(2,1)} fusion(bf16[384,384]{1,0:T(8,128)(2,1)S(1)} %copy-done.11, bf16[384,384]{1,0:T(8,128)(2,1)S(1)} %copy-done.9, bf16[384,384]{1,0:T(8,128)(2,1)S(1)} %copy-done.13, bf16[384,384]{1,0:T(8,128)(2,1)S(1)} %copy-done.7), kind=kLoop, calls=%fused_computation.8 | loop fusion | flops 4718592 | bytes 2359296 | tf_op jit(solution)/shard_map/concatenate | solution.py:280
  98.9 6.0 %all-to-all-done = f32[32,1,16]{2,1,0:T(1,128)S(1)} async-done(((f32[32,1,16]{2,1,0:T(1,128)}), f32[32,1,16]{2,1,0:T(1,128)S(1)}, u32[]{:S(2)}, u32[]{:S(2)}) %all-to-all-start) | async-done | bytes 2080 | tf_op jit(solution)/shard_map/all_to_all | solution.py:346
  (96 shorter events, 4.9 us)
Async XLA Ops:
  2.5 10.0 %collective-permute-start.2 = (bf16[4,2,24,768]{3,2,0,1:T(8,128)(2,1)S(1)}, bf16[4,2,24,768]{3,2,0,1:T(8,128)(2,1)S(1)}, u32[]{:S(2)}, u32[]{:S(2)}) collective-permute-start(bf16[4,2,24,768]{3,2,0,1:T(8,128)(2,1)S(1)} %copy.19), channel_id=1, source_target_pairs={{0,4},{2,6},{4,0},{6,2},{8,12},{10,14},{12,8},{14,10},{16,20},{18,... | collective-permute-start | bytes 884744 | tf_op jit(solution)/shard_map/ppermute | solution.py:35
  5.5 8.9 %collective-permute-start = (bf16[4,2,24,768]{3,2,0,1:T(8,128)(2,1)S(1)}, bf16[4,2,24,768]{3,2,0,1:T(8,128)(2,1)S(1)}, u32[]{:S(2)}, u32[]{:S(2)}) collective-permute-start(bf16[4,2,24,768]{3,2,0,1:T(8,128)(2,1)S(1)} %copy.17), channel_id=1, source_target_pairs={{0,2},{2,0},{4,6},{6,4},{8,10},{10,8},{12,14},{14,12},{16,18},{18,... | collective-permute-start | bytes 884744 | tf_op jit(solution)/shard_map/ppermute | solution.py:35
  12.6 5.2 %collective-permute-start.3 = (bf16[4,24,768]{2,1,0:T(8,128)(2,1)S(1)}, bf16[4,24,768]{2,1,0:T(8,128)(2,1)S(1)}, u32[]{:S(2)}, u32[]{:S(2)}) collective-permute-start(bf16[4,24,768]{2,1,0:T(8,128)(2,1)S(1)} %fusion.5), channel_id=1, source_target_pairs={{0,2},{2,0},{4,6},{6,4},{8,10},{10,8},{12,14},{14,12},{16,18},{18,... | collective-permute-start | bytes 442376 | tf_op jit(solution)/shard_map/ppermute | solution.py:35
  14.5 5.2 %collective-permute-start.1 = (bf16[4,24,768]{2,1,0:T(8,128)(2,1)S(1)}, bf16[4,24,768]{2,1,0:T(8,128)(2,1)S(1)}, u32[]{:S(2)}, u32[]{:S(2)}) collective-permute-start(bf16[4,24,768]{2,1,0:T(8,128)(2,1)S(1)} %fusion.4), channel_id=1, source_target_pairs={{0,4},{2,6},{4,0},{6,2},{8,12},{10,14},{12,8},{14,10},{16,20},{18,... | collective-permute-start | bytes 442376 | tf_op jit(solution)/shard_map/ppermute | solution.py:35
  19.8 4.5 %collective-permute-start.4 = (bf16[24,1536]{1,0:T(8,128)(2,1)S(1)}, bf16[24,1536]{1,0:T(8,128)(2,1)S(1)}, u32[]{:S(2)}, u32[]{:S(2)}) collective-permute-start(bf16[24,1536]{1,0:T(8,128)(2,1)S(1)} %get-tuple-element.84), channel_id=1, source_target_pairs={{0,8},{2,10},{4,12},{6,14},{8,0},{10,2},{12,4},{14,6},{16,24},{18,... | collective-permute-start | bytes 221192 | tf_op jit(solution)/shard_map/ppermute | solution.py:35
  21.4 6.7 %collective-permute-start.5 = (bf16[24,1536]{1,0:T(8,128)(2,1)S(1)}, bf16[24,1536]{1,0:T(8,128)(2,1)S(1)}, u32[]{:S(2)}, u32[]{:S(2)}) collective-permute-start(bf16[24,1536]{1,0:T(8,128)(2,1)S(1)} %get-tuple-element.85), channel_id=1, source_target_pairs={{0,16},{2,18},{4,20},{6,22},{8,24},{10,26},{12,28},{14,30},{16,0},... | collective-permute-start | bytes 221192 | tf_op jit(solution)/shard_map/ppermute | solution.py:35
  24.0 6.3 %collective-permute-start.6 = (bf16[24,1536]{1,0:T(8,128)(2,1)S(1)}, bf16[24,1536]{1,0:T(8,128)(2,1)S(1)}, u32[]{:S(2)}, u32[]{:S(2)}) collective-permute-start(bf16[24,1536]{1,0:T(8,128)(2,1)S(1)} %get-tuple-element.86), channel_id=1, source_target_pairs={{0,24},{2,26},{4,28},{6,30},{8,16},{10,18},{12,20},{14,22},{16,8},... | collective-permute-start | bytes 221192 | tf_op jit(solution)/shard_map/ppermute | solution.py:35
  30.3 6.4 %collective-permute-start.9 = (bf16[24,1536]{1,0:T(8,128)(2,1)S(1)}, bf16[24,1536]{1,0:T(8,128)(2,1)S(1)}, u32[]{:S(2)}, u32[]{:S(2)}) collective-permute-start(bf16[24,1536]{1,0:T(8,128)(2,1)S(1)} %pad_maximum_fusion.11), channel_id=1, source_target_pairs={{0,24},{2,26},{4,28},{6,30},{8,16},{10,18},{12,20},{14,22},{16,8},... | collective-permute-start | bytes 221192 | tf_op jit(solution)/shard_map/ppermute | solution.py:35
  31.2 6.8 %collective-permute-start.8 = (bf16[24,1536]{1,0:T(8,128)(2,1)S(1)}, bf16[24,1536]{1,0:T(8,128)(2,1)S(1)}, u32[]{:S(2)}, u32[]{:S(2)}) collective-permute-start(bf16[24,1536]{1,0:T(8,128)(2,1)S(1)} %pad_maximum_fusion.11), channel_id=1, source_target_pairs={{0,16},{2,18},{4,20},{6,22},{8,24},{10,26},{12,28},{14,30},{16,0},... | collective-permute-start | bytes 221192 | tf_op jit(solution)/shard_map/ppermute | solution.py:35
  32.7 5.4 %collective-permute-start.7 = (bf16[24,1536]{1,0:T(8,128)(2,1)S(1)}, bf16[24,1536]{1,0:T(8,128)(2,1)S(1)}, u32[]{:S(2)}, u32[]{:S(2)}) collective-permute-start(bf16[24,1536]{1,0:T(8,128)(2,1)S(1)} %pad_maximum_fusion.11), channel_id=1, source_target_pairs={{0,8},{2,10},{4,12},{6,14},{8,0},{10,2},{12,4},{14,6},{16,24},{18,... | collective-permute-start | bytes 221192 | tf_op jit(solution)/shard_map/ppermute | solution.py:35
  38.1 1.4 %copy-start.5 = (bf16[1,384,1536]{2,1,0:T(8,128)(2,1)S(1)}, bf16[1,384,1536]{2,1,0:T(8,128)(2,1)}, u32[]{:S(2)}) copy-start(bf16[1,384,1536]{2,1,0:T(8,128)(2,1)} %param.7) | copy-start | bytes 3538948
  38.2 6.3 %collective-permute-start.12 = (bf16[4,24,768]{2,1,0:T(8,128)(2,1)S(1)}, bf16[4,24,768]{2,1,0:T(8,128)(2,1)S(1)}, u32[]{:S(2)}, u32[]{:S(2)}) collective-permute-start(bf16[4,24,768]{2,1,0:T(8,128)(2,1)S(1)} %get-tuple-element.89), channel_id=1, source_target_pairs={{0,2},{2,0},{4,6},{6,4},{8,10},{10,8},{12,14},{14,12},{16,18},{18,... | collective-permute-start | bytes 442376 | tf_op jit(solution)/shard_map/ppermute | solution.py:35
  39.7 6.6 %collective-permute-start.10 = (bf16[4,24,768]{2,1,0:T(8,128)(2,1)S(1)}, bf16[4,24,768]{2,1,0:T(8,128)(2,1)S(1)}, u32[]{:S(2)}, u32[]{:S(2)}) collective-permute-start(bf16[4,24,768]{2,1,0:T(8,128)(2,1)S(1)} %get-tuple-element.90), channel_id=1, source_target_pairs={{0,4},{2,6},{4,0},{6,2},{8,12},{10,14},{12,8},{14,10},{16,20},{18,... | collective-permute-start | bytes 442376 | tf_op jit(solution)/shard_map/ppermute | solution.py:35
  44.6 6.8 %collective-permute-start.13 = (bf16[4,2,24,768]{3,2,0,1:T(8,128)(2,1)S(1)}, bf16[4,2,24,768]{3,2,0,1:T(8,128)(2,1)S(1)}, u32[]{:S(2)}, u32[]{:S(2)}) collective-permute-start(bf16[4,2,24,768]{3,2,0,1:T(8,128)(2,1)S(1)} %reverse_select_fusion.2), channel_id=1, source_target_pairs={{0,4},{2,6},{4,0},{6,2},{8,12},{10,14},{12,8},{14,10},{16,20},{18,... | collective-permute-start | bytes 884744 | tf_op jit(solution)/shard_map/ppermute | solution.py:35
  46.5 6.8 %collective-permute-start.11 = (bf16[4,2,24,768]{3,2,1,0:T(8,128)(2,1)S(1)}, bf16[4,2,24,768]{3,2,1,0:T(8,128)(2,1)S(1)}, u32[]{:S(2)}, u32[]{:S(2)}) collective-permute-start(bf16[4,2,24,768]{3,2,1,0:T(8,128)(2,1)S(1)} %reverse_select_fusion.3), channel_id=1, source_target_pairs={{0,2},{2,0},{4,6},{6,4},{8,10},{10,8},{12,14},{14,12},{16,18},{18,... | collective-permute-start | bytes 884744 | tf_op jit(solution)/shard_map/ppermute | solution.py:35
  53.6 0.7 copy-start.6
  53.6 0.8 copy-start.8
  53.6 0.9 copy-start.10
  53.6 1.0 copy-start.12
  54.6 1.3 %copy-start.1 = (bf16[768,768]{1,0:T(8,128)(2,1)S(1)}, bf16[768,768]{1,0:T(8,128)(2,1)}, u32[]{:S(2)}) copy-start(bf16[768,768]{1,0:T(8,128)(2,1)} %constant.164.clone.table_ref) | copy-start | bytes 3538948
  54.7 2.9 %collective-permute-start.14 = (bf16[768,768]{1,0:T(8,128)(2,1)S(1)}, bf16[768,768]{1,0:T(8,128)(2,1)S(1)}, u32[]{:S(2)}, u32[]{:S(2)}) collective-permute-start(bf16[768,768]{1,0:T(8,128)(2,1)S(1)} %pad_maximum_fusion.1.shaped_ref), channel_id=1, source_target_pairs={{0,1},{1,0},{2,3},{3,2},{4,5},{5,4},{6,7},{7,6},{8,9},{9,8},{10,11... | collective-permute-start | bytes 3538952 | tf_op jit(solution)/shard_map/ppermute | solution.py:288
  55.9 1.7 %copy-start = (bf16[768,768]{1,0:T(8,128)(2,1)S(1)}, bf16[768,768]{1,0:T(8,128)(2,1)}, u32[]{:S(2)}) copy-start(bf16[768,768]{1,0:T(8,128)(2,1)} %constant.165.clone.table_ref) | copy-start | bytes 3538948
  57.6 7.8 %copy-start.4 = (bf16[768,768]{1,0:T(8,128)(2,1)S(1)}, bf16[768,768]{1,0:T(8,128)(2,1)}, u32[]{:S(2)}) copy-start(bf16[768,768]{1,0:T(8,128)(2,1)} %constant.162.clone.refs_1_.re_ref) | copy-start | bytes 3538948
  58.7 6.8 %copy-start.3 = (bf16[768,768]{1,0:T(8,128)(2,1)S(1)}, bf16[768,768]{1,0:T(8,128)(2,1)}, u32[]{:S(2)}) copy-start(bf16[768,768]{1,0:T(8,128)(2,1)} %constant.163.clone.refs_2_.im_ref) | copy-start | bytes 3538948
  58.9 11.6 %collective-permute-start.27 = (bf16[48,768]{1,0:T(8,128)(2,1)S(1)}, bf16[48,768]{1,0:T(8,128)(2,1)S(1)}, u32[]{:S(2)}, u32[]{:S(2)}) collective-permute-start(bf16[48,768]{1,0:T(8,128)(2,1)S(1)} %get-tuple-element.66), channel_id=1, source_target_pairs={{0,16},{2,18},{4,20},{6,22},{8,24},{10,26},{12,28},{14,30},{16,0},... | collective-permute-start | bytes 221192 | tf_op jit(solution)/shard_map/ppermute | solution.py:35
  59.6 12.1 %collective-permute-start.24 = (bf16[48,768]{1,0:T(8,128)(2,1)S(1)}, bf16[48,768]{1,0:T(8,128)(2,1)S(1)}, u32[]{:S(2)}, u32[]{:S(2)}) collective-permute-start(bf16[48,768]{1,0:T(8,128)(2,1)S(1)} %get-tuple-element.68), channel_id=1, source_target_pairs={{0,20},{2,22},{4,16},{6,18},{8,28},{10,30},{12,24},{14,26},{16,4},... | collective-permute-start | bytes 221192 | tf_op jit(solution)/shard_map/ppermute | solution.py:35
  62.1 11.4 %collective-permute-start.21 = (bf16[48,768]{1,0:T(8,128)(2,1)S(1)}, bf16[48,768]{1,0:T(8,128)(2,1)S(1)}, u32[]{:S(2)}, u32[]{:S(2)}) collective-permute-start(bf16[48,768]{1,0:T(8,128)(2,1)S(1)} %get-tuple-element.71), channel_id=1, source_target_pairs={{0,4},{2,6},{4,0},{6,2},{8,12},{10,14},{12,8},{14,10},{16,20},{18,... | collective-permute-start | bytes 221192 | tf_op jit(solution)/shard_map/ppermute | solution.py:35
  63.3 12.7 %collective-permute-start.18 = (bf16[48,768]{1,0:T(8,128)(2,1)S(1)}, bf16[48,768]{1,0:T(8,128)(2,1)S(1)}, u32[]{:S(2)}, u32[]{:S(2)}) collective-permute-start(bf16[48,768]{1,0:T(8,128)(2,1)S(1)} %get-tuple-element.74), channel_id=1, source_target_pairs={{0,18},{2,16},{4,22},{6,20},{8,26},{10,24},{12,30},{14,28},{16,2},... | collective-permute-start | bytes 221192 | tf_op jit(solution)/shard_map/ppermute | solution.py:35
  63.9 4.6 %copy-start.2 = (bf16[2,16,24,768]{3,2,1,0:T(8,128)(2,1)S(1)}, bf16[2,16,24,768]{3,2,1,0:T(8,128)(2,1)}, u32[]{:S(2)}) copy-start(bf16[2,16,24,768]{3,2,1,0:T(8,128)(2,1)} %param.9) | copy-start | bytes 3538948
  63.9 12.2 %collective-permute-start.15 = (bf16[48,768]{1,0:T(8,128)(2,1)S(1)}, bf16[48,768]{1,0:T(8,128)(2,1)S(1)}, u32[]{:S(2)}, u32[]{:S(2)}) collective-permute-start(bf16[48,768]{1,0:T(8,128)(2,1)S(1)} %get-tuple-element.77), channel_id=1, source_target_pairs={{0,2},{2,0},{4,6},{6,4},{8,10},{10,8},{12,14},{14,12},{16,18},{18,... | collective-permute-start | bytes 221192 | tf_op jit(solution)/shard_map/ppermute | solution.py:35
  70.5 8.2 %collective-permute-start.28 = (bf16[48,768]{1,0:T(8,128)(2,1)S(1)}, bf16[48,768]{1,0:T(8,128)(2,1)S(1)}, u32[]{:S(2)}, u32[]{:S(2)}) collective-permute-start(bf16[48,768]{1,0:T(8,128)(2,1)S(1)} %get-tuple-element.56), channel_id=1, source_target_pairs={{0,6},{2,4},{4,2},{6,0},{8,14},{10,12},{12,10},{14,8},{16,22},{18,... | collective-permute-start | bytes 221192 | tf_op jit(solution)/shard_map/ppermute | solution.py:35
  71.7 10.4 %collective-permute-start.25 = (bf16[48,768]{1,0:T(8,128)(2,1)S(1)}, bf16[48,768]{1,0:T(8,128)(2,1)S(1)}, u32[]{:S(2)}, u32[]{:S(2)}) collective-permute-start(bf16[48,768]{1,0:T(8,128)(2,1)S(1)} %get-tuple-element.48), channel_id=1, source_target_pairs={{0,10},{2,8},{4,14},{6,12},{8,2},{10,0},{12,6},{14,4},{16,26},{18,... | collective-permute-start | bytes 221192 | tf_op jit(solution)/shard_map/ppermute | solution.py:35
  73.5 10.9 %collective-permute-start.22 = (bf16[48,768]{1,0:T(8,128)(2,1)S(1)}, bf16[48,768]{1,0:T(8,128)(2,1)S(1)}, u32[]{:S(2)}, u32[]{:S(2)}) collective-permute-start(bf16[48,768]{1,0:T(8,128)(2,1)S(1)} %get-tuple-element.46), channel_id=1, source_target_pairs={{0,24},{2,26},{4,28},{6,30},{8,16},{10,18},{12,20},{14,22},{16,8},... | collective-permute-start | bytes 221192 | tf_op jit(solution)/shard_map/ppermute | solution.py:35
  76.0 8.5 %collective-permute-start.19 = (bf16[48,768]{1,0:T(8,128)(2,1)S(1)}, bf16[48,768]{1,0:T(8,128)(2,1)S(1)}, u32[]{:S(2)}, u32[]{:S(2)}) collective-permute-start(bf16[48,768]{1,0:T(8,128)(2,1)S(1)} %get-tuple-element.44), channel_id=1, source_target_pairs={{0,8},{2,10},{4,12},{6,14},{8,0},{10,2},{12,4},{14,6},{16,24},{18,... | collective-permute-start | bytes 221192 | tf_op jit(solution)/shard_map/ppermute | solution.py:35
  76.1 10.7 %collective-permute-start.16 = (bf16[48,768]{1,0:T(8,128)(2,1)S(1)}, bf16[48,768]{1,0:T(8,128)(2,1)S(1)}, u32[]{:S(2)}, u32[]{:S(2)}) collective-permute-start(bf16[48,768]{1,0:T(8,128)(2,1)S(1)} %get-tuple-element.42), channel_id=1, source_target_pairs={{0,22},{2,20},{4,18},{6,16},{8,30},{10,28},{12,26},{14,24},{16,6},... | collective-permute-start | bytes 221192 | tf_op jit(solution)/shard_map/ppermute | solution.py:35
  78.7 11.1 %collective-permute-start.29 = (bf16[48,768]{1,0:T(8,128)(2,1)S(1)}, bf16[48,768]{1,0:T(8,128)(2,1)S(1)}, u32[]{:S(2)}, u32[]{:S(2)}) collective-permute-start(bf16[48,768]{1,0:T(8,128)(2,1)S(1)} %get-tuple-element.62), channel_id=1, source_target_pairs={{0,26},{2,24},{4,30},{6,28},{8,18},{10,16},{12,22},{14,20},{16,10}... | collective-permute-start | bytes 221192 | tf_op jit(solution)/shard_map/ppermute | solution.py:35
  82.1 9.3 %collective-permute-start.26 = (bf16[48,768]{1,0:T(8,128)(2,1)S(1)}, bf16[48,768]{1,0:T(8,128)(2,1)S(1)}, u32[]{:S(2)}, u32[]{:S(2)}) collective-permute-start(bf16[48,768]{1,0:T(8,128)(2,1)S(1)} %get-tuple-element.49), channel_id=1, source_target_pairs={{0,30},{2,28},{4,26},{6,24},{8,22},{10,20},{12,18},{14,16},{16,14}... | collective-permute-start | bytes 221192 | tf_op jit(solution)/shard_map/ppermute | solution.py:35
  84.4 7.0 %collective-permute-start.23 = (bf16[48,768]{1,0:T(8,128)(2,1)S(1)}, bf16[48,768]{1,0:T(8,128)(2,1)S(1)}, u32[]{:S(2)}, u32[]{:S(2)}) collective-permute-start(bf16[48,768]{1,0:T(8,128)(2,1)S(1)} %get-tuple-element.47), channel_id=1, source_target_pairs={{0,14},{2,12},{4,10},{6,8},{8,6},{10,4},{12,2},{14,0},{16,30},{18,... | collective-permute-start | bytes 221192 | tf_op jit(solution)/shard_map/ppermute | solution.py:35
  84.4 7.4 %collective-permute-start.20 = (bf16[48,768]{1,0:T(8,128)(2,1)S(1)}, bf16[48,768]{1,0:T(8,128)(2,1)S(1)}, u32[]{:S(2)}, u32[]{:S(2)}) collective-permute-start(bf16[48,768]{1,0:T(8,128)(2,1)S(1)} %get-tuple-element.45), channel_id=1, source_target_pairs={{0,28},{2,30},{4,24},{6,26},{8,20},{10,22},{12,16},{14,18},{16,12}... | collective-permute-start | bytes 221192 | tf_op jit(solution)/shard_map/ppermute | solution.py:35
  86.8 5.9 %collective-permute-start.17 = (bf16[48,768]{1,0:T(8,128)(2,1)S(1)}, bf16[48,768]{1,0:T(8,128)(2,1)S(1)}, u32[]{:S(2)}, u32[]{:S(2)}) collective-permute-start(bf16[48,768]{1,0:T(8,128)(2,1)S(1)} %get-tuple-element.43), channel_id=1, source_target_pairs={{0,12},{2,14},{4,8},{6,10},{8,4},{10,6},{12,0},{14,2},{16,28},{18,... | collective-permute-start | bytes 221192 | tf_op jit(solution)/shard_map/ppermute | solution.py:35
  91.3 6.5 %copy-start.7 = (bf16[384,384]{1,0:T(8,128)(2,1)S(1)}, bf16[384,384]{1,0:T(8,128)(2,1)}, u32[]{:S(2)}) copy-start(bf16[384,384]{1,0:T(8,128)(2,1)} %copy-done.6) | copy-start | bytes 884740
  91.3 6.5 %copy-start.9 = (bf16[384,384]{1,0:T(8,128)(2,1)S(1)}, bf16[384,384]{1,0:T(8,128)(2,1)}, u32[]{:S(2)}) copy-start(bf16[384,384]{1,0:T(8,128)(2,1)} %copy-done.8) | copy-start | bytes 884740
  91.3 6.5 %copy-start.11 = (bf16[384,384]{1,0:T(8,128)(2,1)S(1)}, bf16[384,384]{1,0:T(8,128)(2,1)}, u32[]{:S(2)}) copy-start(bf16[384,384]{1,0:T(8,128)(2,1)} %copy-done.10) | copy-start | bytes 884740
  91.3 6.5 %copy-start.13 = (bf16[384,384]{1,0:T(8,128)(2,1)S(1)}, bf16[384,384]{1,0:T(8,128)(2,1)}, u32[]{:S(2)}) copy-start(bf16[384,384]{1,0:T(8,128)(2,1)} %copy-done.12) | copy-start | bytes 884740
  94.3 10.6 %all-to-all-start = ((f32[32,1,16]{2,1,0:T(1,128)}), f32[32,1,16]{2,1,0:T(1,128)S(1)}, u32[]{:S(2)}, u32[]{:S(2)}) async-start(f32[32,1,16]{2,1,0:T(1,128)} %bitcast.53), calls=%async_computation | async-start | bytes 32768 | tf_op jit(solution)/shard_map/all_to_all | solution.py:346

commit v10 on v8

--- a/solution.py
+++ b/solution.py
@@ -146,7 +146,7 @@
     )
 
 
-def coupling_kernel(block_rows, by_xor, fields_ref, targets_ref, out_ref):
+def coupling_kernel(block_rows, by_xor, fields_ref, targets_ref, out_ref, held):
     modes = out_ref.shape[1]
     product = lax.dot_general(
         fields_ref[...], targets_ref[...], (((1,), (1,)), ((), ())), preferred_element_type=f32
@@ -165,18 +165,22 @@
         product = jnp.sum(product.reshape(left // block_rows, block_rows, right), 1)
     else:
         product = exactly(groups(left), product, ((1,), (0,)))
-    product = exactly(product, groups(right), ((1,), (1,)))
-    by_re, by_im = product[:, :modes], product[:, modes:]
-    mode = lax.broadcasted_iota(jnp.int32, (modes, 2 * modes), 0)
+    product = product.reshape(modes, 2, right)
+    real, imag = product[:, 0], product[:, 1]
+    right = right // 2
+    both = jnp.concatenate(
+        [real[:, :right] + imag[:, right:], imag[:, :right] - real[:, right:]], 0
+    )
+    held[...] = exactly(both, groups(right), ((1,), (1,)))
     if by_xor:
-        mode = mode ^ lax.axis_index("modes")
-        mode = mode % (modes // 2) * 2 + mode // (modes // 2)
-    from_row = lax.broadcasted_iota(jnp.int32, (modes, 2 * modes), 1)
-    real = jnp.where(from_row == 2 * mode, 1.0, 0.0).astype(f32)
-    imag = jnp.where(from_row == 2 * mode + 1, 1.0, 0.0).astype(f32)
-    inner = ((1,), (0,))
-    out_ref[:modes] = exactly(real, by_re, inner) + exactly(imag, by_im, inner)
-    out_ref[modes:] = exactly(imag, by_re, inner) - exactly(real, by_im, inner)
+        me, there = lax.axis_index("modes"), modes // 2
+        for mode in range(modes):
+            e = mode ^ me
+            at = e % there * 2 + e // there
+            out_ref[pl.ds(mode, 1)] = held[pl.ds(at, 1)]
+            out_ref[pl.ds(modes + mode, 1)] = held[pl.ds(modes + at, 1)]
+    else:
+        out_ref[...] = held[...]
 
 
 def kernel_call(kernel, shape, dtype, flops, operands, grant=12, **more):
@@ -206,13 +210,6 @@
     sizes = [size for _, size in reversed(digits)]
     half = grid_size // 2
     matmul = 2 * local_rows * double_width * double_width
-
-    c_re, c_im = propagator(grid_size)
-    full_re, full_im = jnp.asarray(c_re, bf16), jnp.asarray(c_im, bf16)
-    column_shape = (2 * local_rows, grid_size)
-    seen = kernel_call(
-        targets_kernel, column_shape, bf16, matmul, (targets.reshape(column_shape), full_re, full_im)
-    )
 
     me = lax.axis_index("modes")
     owns = [me // stride % size for stride, size in digits]
@@ -227,7 +224,7 @@
             [bf16, f32, bf16, f32],
             8 * local_rows * double_width,
             (forward[0], backward[0]),
-            grant=12,
+            grant=52,
             in_specs=[pl.BlockSpec(memory_space=pltpu.HBM)] * 2,
             scratch_shapes=[pltpu.VMEM((local_rows, double_width), bf16)] * 2
             + [pltpu.SemaphoreType.DMA((2 * local_rows // (4 * block_rows),))],
@@ -250,8 +247,6 @@
             else:
                 send, keep = split_digit(partial, owns[d], size, axes[d])
             got = [exchange(v, (e + 1) * stride, count) for e, v in enumerate(send)]
-            if at == 0 and part == 0:
-                got, seen = lax.optimization_barrier((got, seen))
             partial = reduce_digit(keep, got)
             axes = [a - (a > axes[d]) for a in axes]
         kept.append(partial)
@@ -289,6 +284,8 @@
     ).astype(bf16)
     other = lax.ppermute(shaped, "rows", [(0, 1), (1, 0)])
 
+    c_re, c_im = propagator(grid_size)
+    full_re, full_im = jnp.asarray(c_re, bf16), jnp.asarray(c_im, bf16)
     owners = count if block_rows % 8 == 0 else 1
     order = np.arange(local_rows).reshape(owners, -1)
 
@@ -297,10 +294,11 @@
         rows = np.stack([np.concatenate([real, -imag], 1)[order], np.concatenate([imag, real], 1)[order]], 1)
         return jnp.asarray(rows.reshape(2 * local_rows, -1), bf16)
 
+    column_shape = (2 * local_rows, grid_size)
     columns = kernel_call(
         own_kernel, column_shape, f32, matmul // 2, (table(slice(0, local_rows)), shaped)
     )
-    columns, other, phase_plane = lax.optimization_barrier((columns, other, phase_plane))
+    columns, other = lax.optimization_barrier((columns, other))
     columns = kernel_call(
         other_kernel, column_shape, bf16, matmul // 2, (table(slice(local_rows, None)), other, columns)
     )
@@ -315,14 +313,21 @@
                 block, pixels[at - LANES] = lax.optimization_barrier((block, pixels[at - LANES]))
             pixels.append(exchange(block, e, count))
     else:
-        pixels = (lax.all_to_all(blocks, "modes", 0, 0, tiled=True),)
-
+        pixels = [lax.all_to_all(blocks, "modes", 0, 0, tiled=True)]
+
+    if len(pixels) > 1:
+        targets, pixels[1] = lax.optimization_barrier((targets, pixels[1]))
+    seen = kernel_call(
+        targets_kernel, column_shape, bf16, matmul, (targets.reshape(column_shape), full_re, full_im)
+    )
+    rows = jnp.concatenate(pixels, 0).reshape(column_shape)
     term = kernel_call(
         lambda *refs: coupling_kernel(block_rows, len(pixels) > 1, *refs),
         (2 * mode_total, mode_total),
         f32,
         matmul,
-        (jnp.concatenate(pixels, 0).reshape(column_shape), seen),
+        (rows, seen),
+        scratch_shapes=[pltpu.VMEM((2 * mode_total, mode_total), f32)],
     )
     columns, term = lax.optimization_barrier((columns, term))
     output_fields = kernel_call(

time: 112 us -> 109 us (0.973)
  local copies, waits for them, and re-layouts: 8.33 us -> 2.86 us
  waiting for transfers between devices: 37 us -> 39.7 us
  other arithmetic: 5.3 us -> 3.37 us
    unnamed x55 -> x45, local copies, waits for them, and re-layouts: 6.42 us -> 2.38 us
    ppermute x29, waiting for transfers between devices: 32.8 us -> 35.6 us  [exchange(): lax.ppermute(values, 'modes', [(i, i ^ offset) for i in range(count)])]
    add x5, other arithmetic: 2.12 us -> 0.19 us  [reduce_digit(): keep = keep + g.astype(f32)]
    reshape x2, local copies, waits for them, and re-layouts: 1.48 us -> 0.04 us  [local(): send = [halves[2 * part].reshape(*left, block_rows, grid_size)]]
    ppermute x29, starting transfers between devices: 45.1 us -> 46.2 us  [exchange(): lax.ppermute(values, 'modes', [(i, i ^ offset) for i in range(count)])]
  transfers between devices with their start and end apart: 31 -> 31, of which waited for: 13 -> 13; matrix products, arithmetic and copies ran while one was open for 4% -> 2% of each run, Pallas kernels for 5% -> 6%
where the time goes in v10:
time: 109 us; the launch traced here: 108 us
  starting transfers between devices  50.2 us (46%)
  waiting for transfers between devices  39.7 us (36%)
  Pallas kernels  11 us (10%)
  other arithmetic  3.37 us (3%)
  local copies, waits for them, and re-layouts  2.86 us (3%)
  between operations  1.22 us (1%)
    ppermute x29, starting transfers between devices, exchange(): lax.ppermute(values, 'modes', [(i, i ^ offset) for i in range(count)])  46.2 us
    ppermute x29, waiting for transfers between devices, exchange(): lax.ppermute(values, 'modes', [(i, i ^ offset) for i in range(count)])  35.6 us
    pallas_call x6, Pallas kernels, kernel_call(): pl.pallas_call(kernel, out_shape=out_shape, compiler_params=pltpu.Compile...  11 us
    all_to_all x1, waiting for transfers between devices, local(): pieces = lax.all_to_all(term, ('modes', 'rows'), 0, 0, tiled=True)  4.13 us
    all_to_all x1, starting transfers between devices, local(): pieces = lax.all_to_all(term, ('modes', 'rows'), 0, 0, tiled=True)  3.84 us
    unnamed x45, local copies, waits for them, and re-layouts  2.38 us
  transfers between devices with their start and end apart: 31, of which 13 were waited for; matrix products, arithmetic and copies ran while one was open for 2% of the time, Pallas kernels for 6%

profile of v10, /device:TPU:0, one launch (start us, length us, event | category | flops | bytes accessed | tf_op | source)
XLA Modules:
  0.0 108.3 jit_solution(13329195800670638675)
XLA Ops:
  0.6 1.8 %shard_map.94 = (bf16[192,768]{1,0:T(8,128)(2,1)S(1)}, f32[192,768]{1,0:T(8,128)S(1)}, bf16[192,768]{1,0:T(8,128)(2,1)S(1)}, f32[192,768]{1,0:T(8,128)S(1)}) custom-call(bf16[384,1536]{1,0:T(8,128)(2,1)} %bitcast.100, bf16[384,1536]{1,0:T(8,128)(2,1)} %bitcast.103), custom_call_target="tpu_custom_call" | custom-call | flops 4718592 | bytes 4194304 | tf_op jit(solution)/shard_map/pallas_call | solution.py:194
  2.5 3.0 %collective-permute-start.2 = (bf16[4,2,24,768]{3,2,0,1:T(8,128)(2,1)S(1)}, bf16[4,2,24,768]{3,2,0,1:T(8,128)(2,1)S(1)}, u32[]{:S(2)}, u32[]{:S(2)}) collective-permute-start(bf16[4,2,24,768]{3,2,0,1:T(8,128)(2,1)S(1)} %copy.19), channel_id=1, source_target_pairs={{0,4},{2,6},{4,0},{6,2},{8,12},{10,14},{12,8},{14,10},{16,20},{18,... | collective-permute-start | bytes 884744 | tf_op jit(solution)/shard_map/ppermute | solution.py:34
  5.5 1.6 %collective-permute-start = (bf16[4,2,24,768]{3,2,0,1:T(8,128)(2,1)S(1)}, bf16[4,2,24,768]{3,2,0,1:T(8,128)(2,1)S(1)}, u32[]{:S(2)}, u32[]{:S(2)}) collective-permute-start(bf16[4,2,24,768]{3,2,0,1:T(8,128)(2,1)S(1)} %copy.17), channel_id=1, source_target_pairs={{0,2},{2,0},{4,6},{6,4},{8,10},{10,8},{12,14},{14,12},{16,18},{18,... | collective-permute-start | bytes 884744 | tf_op jit(solution)/shard_map/ppermute | solution.py:34
  7.1 5.4 %collective-permute-done.2 = bf16[4,2,24,768]{3,2,0,1:T(8,128)(2,1)S(1)} collective-permute-done((bf16[4,2,24,768]{3,2,0,1:T(8,128)(2,1)S(1)}, bf16[4,2,24,768]{3,2,0,1:T(8,128)(2,1)S(1)}, u32[]{:S(2)}, u32[]{:S(2)}) %collective-permute-start.2) | collective-permute-done | bytes 294944 | tf_op jit(solution)/shard_map/ppermute | solution.py:34
  12.6 1.8 %collective-permute-start.3 = (bf16[4,24,768]{2,1,0:T(8,128)(2,1)S(1)}, bf16[4,24,768]{2,1,0:T(8,128)(2,1)S(1)}, u32[]{:S(2)}, u32[]{:S(2)}) collective-permute-start(bf16[4,24,768]{2,1,0:T(8,128)(2,1)S(1)} %fusion.5), channel_id=1, source_target_pairs={{0,2},{2,0},{4,6},{6,4},{8,10},{10,8},{12,14},{14,12},{16,18},{18,... | collective-permute-start | bytes 442376 | tf_op jit(solution)/shard_map/ppermute | solution.py:34
  14.5 1.6 %collective-permute-start.1 = (bf16[4,24,768]{2,1,0:T(8,128)(2,1)S(1)}, bf16[4,24,768]{2,1,0:T(8,128)(2,1)S(1)}, u32[]{:S(2)}, u32[]{:S(2)}) collective-permute-start(bf16[4,24,768]{2,1,0:T(8,128)(2,1)S(1)} %fusion.4), channel_id=1, source_target_pairs={{0,4},{2,6},{4,0},{6,2},{8,12},{10,14},{12,8},{14,10},{16,20},{18,... | collective-permute-start | bytes 442376 | tf_op jit(solution)/shard_map/ppermute | solution.py:34
  16.1 1.8 %collective-permute-done.3 = bf16[4,24,768]{2,1,0:T(8,128)(2,1)S(1)} collective-permute-done((bf16[4,24,768]{2,1,0:T(8,128)(2,1)S(1)}, bf16[4,24,768]{2,1,0:T(8,128)(2,1)S(1)}, u32[]{:S(2)}, u32[]{:S(2)}) %collective-permute-start.3) | collective-permute-done | bytes 147488 | tf_op jit(solution)/shard_map/ppermute | solution.py:34
  17.8 1.8 %collective-permute-done.1 = bf16[4,24,768]{2,1,0:T(8,128)(2,1)S(1)} collective-permute-done((bf16[4,24,768]{2,1,0:T(8,128)(2,1)S(1)}, bf16[4,24,768]{2,1,0:T(8,128)(2,1)S(1)}, u32[]{:S(2)}, u32[]{:S(2)}) %collective-permute-start.1) | collective-permute-done | bytes 147488 | tf_op jit(solution)/shard_map/ppermute | solution.py:34
  19.8 1.6 %collective-permute-start.4 = (bf16[24,1536]{1,0:T(8,128)(2,1)S(1)}, bf16[24,1536]{1,0:T(8,128)(2,1)S(1)}, u32[]{:S(2)}, u32[]{:S(2)}) collective-permute-start(bf16[24,1536]{1,0:T(8,128)(2,1)S(1)} %get-tuple-element.84), channel_id=1, source_target_pairs={{0,8},{2,10},{4,12},{6,14},{8,0},{10,2},{12,4},{14,6},{16,24},{18,... | collective-permute-start | bytes 221192 | tf_op jit(solution)/shard_map/ppermute | solution.py:34
  21.4 2.6 %collective-permute-start.5 = (bf16[24,1536]{1,0:T(8,128)(2,1)S(1)}, bf16[24,1536]{1,0:T(8,128)(2,1)S(1)}, u32[]{:S(2)}, u32[]{:S(2)}) collective-permute-start(bf16[24,1536]{1,0:T(8,128)(2,1)S(1)} %get-tuple-element.85), channel_id=1, source_target_pairs={{0,16},{2,18},{4,20},{6,22},{8,24},{10,26},{12,28},{14,30},{16,0},... | collective-permute-start | bytes 221192 | tf_op jit(solution)/shard_map/ppermute | solution.py:34
  24.3 3.9 %collective-permute-done.5 = bf16[24,1536]{1,0:T(8,128)(2,1)S(1)} collective-permute-done((bf16[24,1536]{1,0:T(8,128)(2,1)S(1)}, bf16[24,1536]{1,0:T(8,128)(2,1)S(1)}, u32[]{:S(2)}, u32[]{:S(2)}) %collective-permute-start.5) | collective-permute-done | bytes 73760 | tf_op jit(solution)/shard_map/ppermute | solution.py:34
  28.1 2.1 %collective-permute-done.6 = bf16[24,1536]{1,0:T(8,128)(2,1)S(1)} collective-permute-done((bf16[24,1536]{1,0:T(8,128)(2,1)S(1)}, bf16[24,1536]{1,0:T(8,128)(2,1)S(1)}, u32[]{:S(2)}, u32[]{:S(2)}) %collective-permute-start.6) | collective-permute-done | bytes 73760 | tf_op jit(solution)/shard_map/ppermute | solution.py:34
  30.3 0.9 collective-permute-start.9
  31.2 1.5 %collective-permute-start.8 = (bf16[24,1536]{1,0:T(8,128)(2,1)S(1)}, bf16[24,1536]{1,0:T(8,128)(2,1)S(1)}, u32[]{:S(2)}, u32[]{:S(2)}) collective-permute-start(bf16[24,1536]{1,0:T(8,128)(2,1)S(1)} %pad_maximum_fusion.10), channel_id=1, source_target_pairs={{0,16},{2,18},{4,20},{6,22},{8,24},{10,26},{12,28},{14,30},{16,0},... | collective-permute-start | bytes 221192 | tf_op jit(solution)/shard_map/ppermute | solution.py:34
  32.7 2.1 %collective-permute-start.7 = (bf16[24,1536]{1,0:T(8,128)(2,1)S(1)}, bf16[24,1536]{1,0:T(8,128)(2,1)S(1)}, u32[]{:S(2)}, u32[]{:S(2)}) collective-permute-start(bf16[24,1536]{1,0:T(8,128)(2,1)S(1)} %pad_maximum_fusion.10), channel_id=1, source_target_pairs={{0,8},{2,10},{4,12},{6,14},{8,0},{10,2},{12,4},{14,6},{16,24},{18,... | collective-permute-start | bytes 221192 | tf_op jit(solution)/shard_map/ppermute | solution.py:34
  34.8 1.9 %collective-permute-done.9 = bf16[24,1536]{1,0:T(8,128)(2,1)S(1)} collective-permute-done((bf16[24,1536]{1,0:T(8,128)(2,1)S(1)}, bf16[24,1536]{1,0:T(8,128)(2,1)S(1)}, u32[]{:S(2)}, u32[]{:S(2)}) %collective-permute-start.9) | collective-permute-done | bytes 73760 | tf_op jit(solution)/shard_map/ppermute | solution.py:34
  36.7 1.3 %collective-permute-done.8 = bf16[24,1536]{1,0:T(8,128)(2,1)S(1)} collective-permute-done((bf16[24,1536]{1,0:T(8,128)(2,1)S(1)}, bf16[24,1536]{1,0:T(8,128)(2,1)S(1)}, u32[]{:S(2)}, u32[]{:S(2)}) %collective-permute-start.8) | collective-permute-done | bytes 73760 | tf_op jit(solution)/shard_map/ppermute | solution.py:34
  38.2 1.2 %collective-permute-start.12 = (bf16[4,24,768]{2,1,0:T(8,128)(2,1)S(1)}, bf16[4,24,768]{2,1,0:T(8,128)(2,1)S(1)}, u32[]{:S(2)}, u32[]{:S(2)}) collective-permute-start(bf16[4,24,768]{2,1,0:T(8,128)(2,1)S(1)} %get-tuple-element.89), channel_id=1, source_target_pairs={{0,2},{2,0},{4,6},{6,4},{8,10},{10,8},{12,14},{14,12},{16,18},{18,... | collective-permute-start | bytes 442376 | tf_op jit(solution)/shard_map/ppermute | solution.py:34
  39.7 1.5 %collective-permute-start.10 = (bf16[4,24,768]{2,1,0:T(8,128)(2,1)S(1)}, bf16[4,24,768]{2,1,0:T(8,128)(2,1)S(1)}, u32[]{:S(2)}, u32[]{:S(2)}) collective-permute-start(bf16[4,24,768]{2,1,0:T(8,128)(2,1)S(1)} %get-tuple-element.90), channel_id=1, source_target_pairs={{0,4},{2,6},{4,0},{6,2},{8,12},{10,14},{12,8},{14,10},{16,20},{18,... | collective-permute-start | bytes 442376 | tf_op jit(solution)/shard_map/ppermute | solution.py:34
  41.2 3.3 %collective-permute-done.12 = bf16[4,24,768]{2,1,0:T(8,128)(2,1)S(1)} collective-permute-done((bf16[4,24,768]{2,1,0:T(8,128)(2,1)S(1)}, bf16[4,24,768]{2,1,0:T(8,128)(2,1)S(1)}, u32[]{:S(2)}, u32[]{:S(2)}) %collective-permute-start.12) | collective-permute-done | bytes 147488 | tf_op jit(solution)/shard_map/ppermute | solution.py:34
  44.6 1.7 %collective-permute-start.13 = (bf16[4,2,24,768]{3,2,0,1:T(8,128)(2,1)S(1)}, bf16[4,2,24,768]{3,2,0,1:T(8,128)(2,1)S(1)}, u32[]{:S(2)}, u32[]{:S(2)}) collective-permute-start(bf16[4,2,24,768]{3,2,0,1:T(8,128)(2,1)S(1)} %reverse_select_fusion.2), channel_id=1, source_target_pairs={{0,4},{2,6},{4,0},{6,2},{8,12},{10,14},{12,8},{14,10},{16,20},{18,... | collective-permute-start | bytes 884744 | tf_op jit(solution)/shard_map/ppermute | solution.py:34
  47.1 4.3 %collective-permute-done.13 = bf16[4,2,24,768]{3,2,0,1:T(8,128)(2,1)S(1)} collective-permute-done((bf16[4,2,24,768]{3,2,0,1:T(8,128)(2,1)S(1)}, bf16[4,2,24,768]{3,2,0,1:T(8,128)(2,1)S(1)}, u32[]{:S(2)}, u32[]{:S(2)}) %collective-permute-start.13) | collective-permute-done | bytes 294944 | tf_op jit(solution)/shard_map/ppermute | solution.py:34
  51.6 1.7 %collective-permute-done.11 = bf16[4,2,24,768]{3,2,1,0:T(8,128)(2,1)S(1)} collective-permute-done((bf16[4,2,24,768]{3,2,1,0:T(8,128)(2,1)S(1)}, bf16[4,2,24,768]{3,2,1,0:T(8,128)(2,1)S(1)}, u32[]{:S(2)}, u32[]{:S(2)}) %collective-permute-start.11) | collective-permute-done | bytes 294944 | tf_op jit(solution)/shard_map/ppermute | solution.py:34
  54.9 1.0 copy-done.1
  55.9 1.1 shard_map.95.own_ref
  57.1 1.1 %pad_maximum_fusion = bf16[384,1536]{1,0:T(8,128)(2,1)} fusion(bf16[384,384]{1,0:T(8,128)(2,1)S(1)} %copy-done.12, bf16[384,384]{1,0:T(8,128)(2,1)S(1)} %copy-done.10, bf16[384,384]{1,0:T(8,128)(2,1)S(1)} %copy-done.14, bf16[384,384]{1,0:T(8,128)(2,1)S(1)} %copy-done.8), kind=kLoop, calls=%fused_computation.8 | loop fusion | flops 4718592 | bytes 2359296 | tf_op jit(solution)/shard_map/concatenate | solution.py:277
  58.2 0.6 copy-done
  58.8 1.1 %shard_map.96.refs_0_ = bf16[768,768]{1,0:T(8,128)(2,1)S(1)} custom-call(bf16[768,768]{1,0:T(8,128)(2,1)S(1)} %copy-done, bf16[768,768]{1,0:T(8,128)(2,1)S(1)} %collective-permute-done.14.shaped_ref, f32[768,768]{1,0:T(8,128)S(1)} %shard_map.95.own_ref), custom_call_target="tpu_custom_call" | custom-call | flops 905969664 | bytes 4194304 | tf_op jit(solution)/shard_map/pallas_call | solution.py:194
  60.1 1.0 collective-permute-start.19
  61.1 1.2 %collective-permute-start.18 = (bf16[48,768]{1,0:T(8,128)(2,1)S(1)}, bf16[48,768]{1,0:T(8,128)(2,1)S(1)}, u32[]{:S(2)}, u32[]{:S(2)}) collective-permute-start(bf16[48,768]{1,0:T(8,128)(2,1)S(1)} %get-tuple-element.72), channel_id=1, source_target_pairs={{0,4},{2,6},{4,0},{6,2},{8,12},{10,14},{12,8},{14,10},{16,20},{18,... | collective-permute-start | bytes 221192 | tf_op jit(solution)/shard_map/ppermute | solution.py:34
  62.3 2.1 %collective-permute-start.17 = (bf16[48,768]{1,0:T(8,128)(2,1)S(1)}, bf16[48,768]{1,0:T(8,128)(2,1)S(1)}, u32[]{:S(2)}, u32[]{:S(2)}) collective-permute-start(bf16[48,768]{1,0:T(8,128)(2,1)S(1)} %get-tuple-element.74), channel_id=1, source_target_pairs={{0,18},{2,16},{4,22},{6,20},{8,26},{10,24},{12,30},{14,28},{16,2},... | collective-permute-start | bytes 221192 | tf_op jit(solution)/shard_map/ppermute | solution.py:34
  64.4 1.6 %collective-permute-start.16 = (bf16[48,768]{1,0:T(8,128)(2,1)S(1)}, bf16[48,768]{1,0:T(8,128)(2,1)S(1)}, u32[]{:S(2)}, u32[]{:S(2)}) collective-permute-start(bf16[48,768]{1,0:T(8,128)(2,1)S(1)} %get-tuple-element.76), channel_id=1, source_target_pairs={{0,2},{2,0},{4,6},{6,4},{8,10},{10,8},{12,14},{14,12},{16,18},{18,... | collective-permute-start | bytes 221192 | tf_op jit(solution)/shard_map/ppermute | solution.py:34
  66.0 0.7 collective-permute-start.15
  66.7 3.6 %collective-permute-done.19 = bf16[48,768]{1,0:T(8,128)(2,1)S(1)} collective-permute-done((bf16[48,768]{1,0:T(8,128)(2,1)S(1)}, bf16[48,768]{1,0:T(8,128)(2,1)S(1)}, u32[]{:S(2)}, u32[]{:S(2)}) %collective-permute-start.19) | collective-permute-done | bytes 73760 | tf_op jit(solution)/shard_map/ppermute | solution.py:34
  70.3 1.2 %collective-permute-start.23 = (bf16[48,768]{1,0:T(8,128)(2,1)S(1)}, bf16[48,768]{1,0:T(8,128)(2,1)S(1)}, u32[]{:S(2)}, u32[]{:S(2)}) collective-permute-start(bf16[48,768]{1,0:T(8,128)(2,1)S(1)} %get-tuple-element.51), channel_id=1, source_target_pairs={{0,24},{2,26},{4,28},{6,30},{8,16},{10,18},{12,20},{14,22},{16,8},... | collective-permute-start | bytes 221192 | tf_op jit(solution)/shard_map/ppermute | solution.py:34
  71.6 4.6 %collective-permute-start.21 = (bf16[48,768]{1,0:T(8,128)(2,1)S(1)}, bf16[48,768]{1,0:T(8,128)(2,1)S(1)}, u32[]{:S(2)}, u32[]{:S(2)}) collective-permute-start(bf16[48,768]{1,0:T(8,128)(2,1)S(1)} %get-tuple-element.47), channel_id=1, source_target_pairs={{0,22},{2,20},{4,18},{6,16},{8,30},{10,28},{12,26},{14,24},{16,6},... | collective-permute-start | bytes 221192 | tf_op jit(solution)/shard_map/ppermute | solution.py:34
  76.2 1.6 %collective-permute-start.20 = (bf16[48,768]{1,0:T(8,128)(2,1)S(1)}, bf16[48,768]{1,0:T(8,128)(2,1)S(1)}, u32[]{:S(2)}, u32[]{:S(2)}) collective-permute-start(bf16[48,768]{1,0:T(8,128)(2,1)S(1)} %get-tuple-element.45), channel_id=1, source_target_pairs={{0,6},{2,4},{4,2},{6,0},{8,14},{10,12},{12,10},{14,8},{16,22},{18,... | collective-permute-start | bytes 221192 | tf_op jit(solution)/shard_map/ppermute | solution.py:34
  77.8 2.0 %shard_map.97.refs_1_ = bf16[768,768]{1,0:T(8,128)(2,1)S(1)} custom-call(bf16[768,768]{1,0:T(8,128)(2,1)S(1)} %bitcast.99, bf16[768,768]{1,0:T(8,128)(2,1)S(1)} %copy-done.4, bf16[768,768]{1,0:T(8,128)(2,1)S(1)} %copy-done.3), custom_call_target="tpu_custom_call" | custom-call | flops 1811939328 | bytes 4194304 | tf_op jit(solution)/shard_map/pallas_call | solution.py:194
  79.9 3.5 %collective-permute-start.29 = (bf16[48,768]{1,0:T(8,128)(2,1)S(1)}, bf16[48,768]{1,0:T(8,128)(2,1)S(1)}, u32[]{:S(2)}, u32[]{:S(2)}) collective-permute-start(bf16[48,768]{1,0:T(8,128)(2,1)S(1)} %get-tuple-element.59), channel_id=1, source_target_pairs={{0,30},{2,28},{4,26},{6,24},{8,22},{10,20},{12,18},{14,16},{16,14}... | collective-permute-start | bytes 221192 | tf_op jit(solution)/shard_map/ppermute | solution.py:34
  83.4 1.5 %collective-permute-start.27 = (bf16[48,768]{1,0:T(8,128)(2,1)S(1)}, bf16[48,768]{1,0:T(8,128)(2,1)S(1)}, u32[]{:S(2)}, u32[]{:S(2)}) collective-permute-start(bf16[48,768]{1,0:T(8,128)(2,1)S(1)} %get-tuple-element.57), channel_id=1, source_target_pairs={{0,28},{2,30},{4,24},{6,26},{8,20},{10,22},{12,16},{14,18},{16,12}... | collective-permute-start | bytes 221192 | tf_op jit(solution)/shard_map/ppermute | solution.py:34
  84.9 2.7 %collective-permute-start.26 = (bf16[48,768]{1,0:T(8,128)(2,1)S(1)}, bf16[48,768]{1,0:T(8,128)(2,1)S(1)}, u32[]{:S(2)}, u32[]{:S(2)}) collective-permute-start(bf16[48,768]{1,0:T(8,128)(2,1)S(1)} %get-tuple-element.56), channel_id=1, source_target_pairs={{0,12},{2,14},{4,8},{6,10},{8,4},{10,6},{12,0},{14,2},{16,28},{18,... | collective-permute-start | bytes 221192 | tf_op jit(solution)/shard_map/ppermute | solution.py:34
  87.6 2.7 %collective-permute-start.25 = (bf16[48,768]{1,0:T(8,128)(2,1)S(1)}, bf16[48,768]{1,0:T(8,128)(2,1)S(1)}, u32[]{:S(2)}, u32[]{:S(2)}) collective-permute-start(bf16[48,768]{1,0:T(8,128)(2,1)S(1)} %get-tuple-element.55), channel_id=1, source_target_pairs={{0,26},{2,24},{4,30},{6,28},{8,18},{10,16},{12,22},{14,20},{16,10}... | collective-permute-start | bytes 221192 | tf_op jit(solution)/shard_map/ppermute | solution.py:34
  90.4 4.3 %collective-permute-done.25 = bf16[48,768]{1,0:T(8,128)(2,1)S(1)} collective-permute-done((bf16[48,768]{1,0:T(8,128)(2,1)S(1)}, bf16[48,768]{1,0:T(8,128)(2,1)S(1)}, u32[]{:S(2)}, u32[]{:S(2)}) %collective-permute-start.25) | collective-permute-done | bytes 73760 | tf_op jit(solution)/shard_map/ppermute | solution.py:34
  94.7 2.0 %shard_map.98 = f32[32,16]{1,0:T(8,128)} custom-call(bf16[768,768]{1,0:T(8,128)(2,1)S(1)} %constant_dynamic-update-slice_fusion.refs_0_, bf16[768,768]{1,0:T(8,128)(2,1)S(1)} %shard_map.97.refs_1_), custom_call_target="tpu_custom_call" | custom-call | flops 1811939328 | bytes 4194304 | tf_op jit(solution)/shard_map/pallas_call | solution.py:194
  96.8 3.8 %all-to-all-start = ((f32[32,1,16]{2,1,0:T(1,128)}), f32[32,1,16]{2,1,0:T(1,128)S(1)}, u32[]{:S(2)}, u32[]{:S(2)}) async-start(f32[32,1,16]{2,1,0:T(1,128)} %bitcast.53), calls=%async_computation | async-start | bytes 32768 | tf_op jit(solution)/shard_map/all_to_all | solution.py:340
  100.6 3.0 %shard_map.99 = bf16[384,1536]{1,0:T(8,128)(2,1)} custom-call(bf16[768,768]{1,0:T(8,128)(2,1)S(1)} %shard_map.96.refs_0_, bf16[768,768]{1,0:T(8,128)(2,1)S(1)} %copy-done.5, bf16[768,768]{1,0:T(8,128)(2,1)S(1)} %copy-done.3), custom_call_target="tpu_custom_call" | custom-call | flops 1811939328 | bytes 4194304 | tf_op jit(solution)/shard_map/pallas_call | solution.py:194
  103.6 4.1 %all-to-all-done = f32[32,1,16]{2,1,0:T(1,128)S(1)} async-done(((f32[32,1,16]{2,1,0:T(1,128)}), f32[32,1,16]{2,1,0:T(1,128)S(1)}, u32[]{:S(2)}, u32[]{:S(2)}) %all-to-all-start) | async-done | bytes 2080 | tf_op jit(solution)/shard_map/all_to_all | solution.py:340
  107.8 0.6 reduce_sum.9
  (100 shorter events, 3.9 us)
Async XLA Ops:
  2.5 10.0 %collective-permute-start.2 = (bf16[4,2,24,768]{3,2,0,1:T(8,128)(2,1)S(1)}, bf16[4,2,24,768]{3,2,0,1:T(8,128)(2,1)S(1)}, u32[]{:S(2)}, u32[]{:S(2)}) collective-permute-start(bf16[4,2,24,768]{3,2,0,1:T(8,128)(2,1)S(1)} %copy.19), channel_id=1, source_target_pairs={{0,4},{2,6},{4,0},{6,2},{8,12},{10,14},{12,8},{14,10},{16,20},{18,... | collective-permute-start | bytes 884744 | tf_op jit(solution)/shard_map/ppermute | solution.py:34
  5.5 8.9 %collective-permute-start = (bf16[4,2,24,768]{3,2,0,1:T(8,128)(2,1)S(1)}, bf16[4,2,24,768]{3,2,0,1:T(8,128)(2,1)S(1)}, u32[]{:S(2)}, u32[]{:S(2)}) collective-permute-start(bf16[4,2,24,768]{3,2,0,1:T(8,128)(2,1)S(1)} %copy.17), channel_id=1, source_target_pairs={{0,2},{2,0},{4,6},{6,4},{8,10},{10,8},{12,14},{14,12},{16,18},{18,... | collective-permute-start | bytes 884744 | tf_op jit(solution)/shard_map/ppermute | solution.py:34
  12.6 5.2 %collective-permute-start.3 = (bf16[4,24,768]{2,1,0:T(8,128)(2,1)S(1)}, bf16[4,24,768]{2,1,0:T(8,128)(2,1)S(1)}, u32[]{:S(2)}, u32[]{:S(2)}) collective-permute-start(bf16[4,24,768]{2,1,0:T(8,128)(2,1)S(1)} %fusion.5), channel_id=1, source_target_pairs={{0,2},{2,0},{4,6},{6,4},{8,10},{10,8},{12,14},{14,12},{16,18},{18,... | collective-permute-start | bytes 442376 | tf_op jit(solution)/shard_map/ppermute | solution.py:34
  14.5 5.2 %collective-permute-start.1 = (bf16[4,24,768]{2,1,0:T(8,128)(2,1)S(1)}, bf16[4,24,768]{2,1,0:T(8,128)(2,1)S(1)}, u32[]{:S(2)}, u32[]{:S(2)}) collective-permute-start(bf16[4,24,768]{2,1,0:T(8,128)(2,1)S(1)} %fusion.4), channel_id=1, source_target_pairs={{0,4},{2,6},{4,0},{6,2},{8,12},{10,14},{12,8},{14,10},{16,20},{18,... | collective-permute-start | bytes 442376 | tf_op jit(solution)/shard_map/ppermute | solution.py:34
  19.8 4.5 %collective-permute-start.4 = (bf16[24,1536]{1,0:T(8,128)(2,1)S(1)}, bf16[24,1536]{1,0:T(8,128)(2,1)S(1)}, u32[]{:S(2)}, u32[]{:S(2)}) collective-permute-start(bf16[24,1536]{1,0:T(8,128)(2,1)S(1)} %get-tuple-element.84), channel_id=1, source_target_pairs={{0,8},{2,10},{4,12},{6,14},{8,0},{10,2},{12,4},{14,6},{16,24},{18,... | collective-permute-start | bytes 221192 | tf_op jit(solution)/shard_map/ppermute | solution.py:34
  21.4 6.7 %collective-permute-start.5 = (bf16[24,1536]{1,0:T(8,128)(2,1)S(1)}, bf16[24,1536]{1,0:T(8,128)(2,1)S(1)}, u32[]{:S(2)}, u32[]{:S(2)}) collective-permute-start(bf16[24,1536]{1,0:T(8,128)(2,1)S(1)} %get-tuple-element.85), channel_id=1, source_target_pairs={{0,16},{2,18},{4,20},{6,22},{8,24},{10,26},{12,28},{14,30},{16,0},... | collective-permute-start | bytes 221192 | tf_op jit(solution)/shard_map/ppermute | solution.py:34
  24.0 6.3 %collective-permute-start.6 = (bf16[24,1536]{1,0:T(8,128)(2,1)S(1)}, bf16[24,1536]{1,0:T(8,128)(2,1)S(1)}, u32[]{:S(2)}, u32[]{:S(2)}) collective-permute-start(bf16[24,1536]{1,0:T(8,128)(2,1)S(1)} %get-tuple-element.86), channel_id=1, source_target_pairs={{0,24},{2,26},{4,28},{6,30},{8,16},{10,18},{12,20},{14,22},{16,8},... | collective-permute-start | bytes 221192 | tf_op jit(solution)/shard_map/ppermute | solution.py:34
  30.3 6.4 %collective-permute-start.9 = (bf16[24,1536]{1,0:T(8,128)(2,1)S(1)}, bf16[24,1536]{1,0:T(8,128)(2,1)S(1)}, u32[]{:S(2)}, u32[]{:S(2)}) collective-permute-start(bf16[24,1536]{1,0:T(8,128)(2,1)S(1)} %pad_maximum_fusion.10), channel_id=1, source_target_pairs={{0,24},{2,26},{4,28},{6,30},{8,16},{10,18},{12,20},{14,22},{16,8},... | collective-permute-start | bytes 221192 | tf_op jit(solution)/shard_map/ppermute | solution.py:34
  31.2 6.8 %collective-permute-start.8 = (bf16[24,1536]{1,0:T(8,128)(2,1)S(1)}, bf16[24,1536]{1,0:T(8,128)(2,1)S(1)}, u32[]{:S(2)}, u32[]{:S(2)}) collective-permute-start(bf16[24,1536]{1,0:T(8,128)(2,1)S(1)} %pad_maximum_fusion.10), channel_id=1, source_target_pairs={{0,16},{2,18},{4,20},{6,22},{8,24},{10,26},{12,28},{14,30},{16,0},... | collective-permute-start | bytes 221192 | tf_op jit(solution)/shard_map/ppermute | solution.py:34
  32.7 5.4 %collective-permute-start.7 = (bf16[24,1536]{1,0:T(8,128)(2,1)S(1)}, bf16[24,1536]{1,0:T(8,128)(2,1)S(1)}, u32[]{:S(2)}, u32[]{:S(2)}) collective-permute-start(bf16[24,1536]{1,0:T(8,128)(2,1)S(1)} %pad_maximum_fusion.10), channel_id=1, source_target_pairs={{0,8},{2,10},{4,12},{6,14},{8,0},{10,2},{12,4},{14,6},{16,24},{18,... | collective-permute-start | bytes 221192 | tf_op jit(solution)/shard_map/ppermute | solution.py:34
  38.1 1.4 %copy-start.6 = (bf16[1,384,1536]{2,1,0:T(8,128)(2,1)S(1)}, bf16[1,384,1536]{2,1,0:T(8,128)(2,1)}, u32[]{:S(2)}) copy-start(bf16[1,384,1536]{2,1,0:T(8,128)(2,1)} %param.7) | copy-start | bytes 3538948
  38.2 6.3 %collective-permute-start.12 = (bf16[4,24,768]{2,1,0:T(8,128)(2,1)S(1)}, bf16[4,24,768]{2,1,0:T(8,128)(2,1)S(1)}, u32[]{:S(2)}, u32[]{:S(2)}) collective-permute-start(bf16[4,24,768]{2,1,0:T(8,128)(2,1)S(1)} %get-tuple-element.89), channel_id=1, source_target_pairs={{0,2},{2,0},{4,6},{6,4},{8,10},{10,8},{12,14},{14,12},{16,18},{18,... | collective-permute-start | bytes 442376 | tf_op jit(solution)/shard_map/ppermute | solution.py:34
  39.7 6.6 %collective-permute-start.10 = (bf16[4,24,768]{2,1,0:T(8,128)(2,1)S(1)}, bf16[4,24,768]{2,1,0:T(8,128)(2,1)S(1)}, u32[]{:S(2)}, u32[]{:S(2)}) collective-permute-start(bf16[4,24,768]{2,1,0:T(8,128)(2,1)S(1)} %get-tuple-element.90), channel_id=1, source_target_pairs={{0,4},{2,6},{4,0},{6,2},{8,12},{10,14},{12,8},{14,10},{16,20},{18,... | collective-permute-start | bytes 442376 | tf_op jit(solution)/shard_map/ppermute | solution.py:34
  44.6 6.8 %collective-permute-start.13 = (bf16[4,2,24,768]{3,2,0,1:T(8,128)(2,1)S(1)}, bf16[4,2,24,768]{3,2,0,1:T(8,128)(2,1)S(1)}, u32[]{:S(2)}, u32[]{:S(2)}) collective-permute-start(bf16[4,2,24,768]{3,2,0,1:T(8,128)(2,1)S(1)} %reverse_select_fusion.2), channel_id=1, source_target_pairs={{0,4},{2,6},{4,0},{6,2},{8,12},{10,14},{12,8},{14,10},{16,20},{18,... | collective-permute-start | bytes 884744 | tf_op jit(solution)/shard_map/ppermute | solution.py:34
  46.5 6.8 %collective-permute-start.11 = (bf16[4,2,24,768]{3,2,1,0:T(8,128)(2,1)S(1)}, bf16[4,2,24,768]{3,2,1,0:T(8,128)(2,1)S(1)}, u32[]{:S(2)}, u32[]{:S(2)}) collective-permute-start(bf16[4,2,24,768]{3,2,1,0:T(8,128)(2,1)S(1)} %reverse_select_fusion.3), channel_id=1, source_target_pairs={{0,2},{2,0},{4,6},{6,4},{8,10},{10,8},{12,14},{14,12},{16,18},{18,... | collective-permute-start | bytes 884744 | tf_op jit(solution)/shard_map/ppermute | solution.py:34
  53.6 0.7 copy-start.7
  53.6 0.8 copy-start.9
  53.6 0.9 copy-start.11
  53.6 1.0 copy-start.13
  54.6 1.3 %copy-start.1 = (bf16[768,768]{1,0:T(8,128)(2,1)S(1)}, bf16[768,768]{1,0:T(8,128)(2,1)}, u32[]{:S(2)}) copy-start(bf16[768,768]{1,0:T(8,128)(2,1)} %constant.164.clone.table_ref) | copy-start | bytes 3538948
  54.7 3.5 %collective-permute-start.14 = (bf16[768,768]{1,0:T(8,128)(2,1)S(1)}, bf16[768,768]{1,0:T(8,128)(2,1)S(1)}, u32[]{:S(2)}, u32[]{:S(2)}) collective-permute-start(bf16[768,768]{1,0:T(8,128)(2,1)S(1)} %pad_maximum_fusion.1.shaped_ref), channel_id=1, source_target_pairs={{0,1},{1,0},{2,3},{3,2},{4,5},{5,4},{6,7},{7,6},{8,9},{9,8},{10,11... | collective-permute-start | bytes 3538952 | tf_op jit(solution)/shard_map/ppermute | solution.py:285
  55.9 1.1 %copy-start.8 = (bf16[384,384]{1,0:T(8,128)(2,1)S(1)}, bf16[384,384]{1,0:T(8,128)(2,1)}, u32[]{:S(2)}) copy-start(bf16[384,384]{1,0:T(8,128)(2,1)} %copy-done.7) | copy-start | bytes 884740
  55.9 1.1 %copy-start.10 = (bf16[384,384]{1,0:T(8,128)(2,1)S(1)}, bf16[384,384]{1,0:T(8,128)(2,1)}, u32[]{:S(2)}) copy-start(bf16[384,384]{1,0:T(8,128)(2,1)} %copy-done.9) | copy-start | bytes 884740
  55.9 1.1 %copy-start.12 = (bf16[384,384]{1,0:T(8,128)(2,1)S(1)}, bf16[384,384]{1,0:T(8,128)(2,1)}, u32[]{:S(2)}) copy-start(bf16[384,384]{1,0:T(8,128)(2,1)} %copy-done.11) | copy-start | bytes 884740
  55.9 1.2 %copy-start.14 = (bf16[384,384]{1,0:T(8,128)(2,1)S(1)}, bf16[384,384]{1,0:T(8,128)(2,1)}, u32[]{:S(2)}) copy-start(bf16[384,384]{1,0:T(8,128)(2,1)} %copy-done.13) | copy-start | bytes 884740
  57.1 1.7 %copy-start = (bf16[768,768]{1,0:T(8,128)(2,1)S(1)}, bf16[768,768]{1,0:T(8,128)(2,1)}, u32[]{:S(2)}) copy-start(bf16[768,768]{1,0:T(8,128)(2,1)} %constant.165.clone.table_ref) | copy-start | bytes 3538948
  58.8 19.0 %copy-start.4 = (bf16[768,768]{1,0:T(8,128)(2,1)S(1)}, bf16[768,768]{1,0:T(8,128)(2,1)}, u32[]{:S(2)}) copy-start(bf16[768,768]{1,0:T(8,128)(2,1)} %constant.162.clone.re_ref.refs_1_) | copy-start | bytes 3538948
  59.9 17.9 %copy-start.2 = (bf16[2,16,24,768]{3,2,1,0:T(8,128)(2,1)S(1)}, bf16[2,16,24,768]{3,2,1,0:T(8,128)(2,1)}, u32[]{:S(2)}) copy-start(bf16[2,16,24,768]{3,2,1,0:T(8,128)(2,1)} %param.9) | copy-start | bytes 3538948
  59.9 17.9 %copy-start.3 = (bf16[768,768]{1,0:T(8,128)(2,1)S(1)}, bf16[768,768]{1,0:T(8,128)(2,1)}, u32[]{:S(2)}) copy-start(bf16[768,768]{1,0:T(8,128)(2,1)} %constant.163.clone.im_ref.refs_2_) | copy-start | bytes 3538948
  60.1 10.3 %collective-permute-start.19 = (bf16[48,768]{1,0:T(8,128)(2,1)S(1)}, bf16[48,768]{1,0:T(8,128)(2,1)S(1)}, u32[]{:S(2)}, u32[]{:S(2)}) collective-permute-start(bf16[48,768]{1,0:T(8,128)(2,1)S(1)} %get-tuple-element.70), channel_id=1, source_target_pairs={{0,20},{2,22},{4,16},{6,18},{8,28},{10,30},{12,24},{14,26},{16,4},... | collective-permute-start | bytes 221192 | tf_op jit(solution)/shard_map/ppermute | solution.py:34
  61.1 9.3 %collective-permute-start.18 = (bf16[48,768]{1,0:T(8,128)(2,1)S(1)}, bf16[48,768]{1,0:T(8,128)(2,1)S(1)}, u32[]{:S(2)}, u32[]{:S(2)}) collective-permute-start(bf16[48,768]{1,0:T(8,128)(2,1)S(1)} %get-tuple-element.72), channel_id=1, source_target_pairs={{0,4},{2,6},{4,0},{6,2},{8,12},{10,14},{12,8},{14,10},{16,20},{18,... | collective-permute-start | bytes 221192 | tf_op jit(solution)/shard_map/ppermute | solution.py:34
  62.3 9.3 %collective-permute-start.17 = (bf16[48,768]{1,0:T(8,128)(2,1)S(1)}, bf16[48,768]{1,0:T(8,128)(2,1)S(1)}, u32[]{:S(2)}, u32[]{:S(2)}) collective-permute-start(bf16[48,768]{1,0:T(8,128)(2,1)S(1)} %get-tuple-element.74), channel_id=1, source_target_pairs={{0,18},{2,16},{4,22},{6,20},{8,26},{10,24},{12,30},{14,28},{16,2},... | collective-permute-start | bytes 221192 | tf_op jit(solution)/shard_map/ppermute | solution.py:34
  64.4 7.2 %collective-permute-start.16 = (bf16[48,768]{1,0:T(8,128)(2,1)S(1)}, bf16[48,768]{1,0:T(8,128)(2,1)S(1)}, u32[]{:S(2)}, u32[]{:S(2)}) collective-permute-start(bf16[48,768]{1,0:T(8,128)(2,1)S(1)} %get-tuple-element.76), channel_id=1, source_target_pairs={{0,2},{2,0},{4,6},{6,4},{8,10},{10,8},{12,14},{14,12},{16,18},{18,... | collective-permute-start | bytes 221192 | tf_op jit(solution)/shard_map/ppermute | solution.py:34
  66.0 10.2 %collective-permute-start.15 = (bf16[48,768]{1,0:T(8,128)(2,1)S(1)}, bf16[48,768]{1,0:T(8,128)(2,1)S(1)}, u32[]{:S(2)}, u32[]{:S(2)}) collective-permute-start(bf16[48,768]{1,0:T(8,128)(2,1)S(1)} %get-tuple-element.78), channel_id=1, source_target_pairs={{0,16},{2,18},{4,20},{6,22},{8,24},{10,26},{12,28},{14,30},{16,0},... | collective-permute-start | bytes 221192 | tf_op jit(solution)/shard_map/ppermute | solution.py:34
  70.3 9.5 %collective-permute-start.24 = (bf16[48,768]{1,0:T(8,128)(2,1)S(1)}, bf16[48,768]{1,0:T(8,128)(2,1)S(1)}, u32[]{:S(2)}, u32[]{:S(2)}) collective-permute-start(bf16[48,768]{1,0:T(8,128)(2,1)S(1)} %get-tuple-element.53), channel_id=1, source_target_pairs={{0,10},{2,8},{4,14},{6,12},{8,2},{10,0},{12,6},{14,4},{16,26},{18,... | collective-permute-start | bytes 221192 | tf_op jit(solution)/shard_map/ppermute | solution.py:34
  70.3 13.1 %collective-permute-start.23 = (bf16[48,768]{1,0:T(8,128)(2,1)S(1)}, bf16[48,768]{1,0:T(8,128)(2,1)S(1)}, u32[]{:S(2)}, u32[]{:S(2)}) collective-permute-start(bf16[48,768]{1,0:T(8,128)(2,1)S(1)} %get-tuple-element.51), channel_id=1, source_target_pairs={{0,24},{2,26},{4,28},{6,30},{8,16},{10,18},{12,20},{14,22},{16,8},... | collective-permute-start | bytes 221192 | tf_op jit(solution)/shard_map/ppermute | solution.py:34
  71.6 11.8 %collective-permute-start.22 = (bf16[48,768]{1,0:T(8,128)(2,1)S(1)}, bf16[48,768]{1,0:T(8,128)(2,1)S(1)}, u32[]{:S(2)}, u32[]{:S(2)}) collective-permute-start(bf16[48,768]{1,0:T(8,128)(2,1)S(1)} %get-tuple-element.49), channel_id=1, source_target_pairs={{0,8},{2,10},{4,12},{6,14},{8,0},{10,2},{12,4},{14,6},{16,24},{18,... | collective-permute-start | bytes 221192 | tf_op jit(solution)/shard_map/ppermute | solution.py:34
  71.6 13.3 %collective-permute-start.21 = (bf16[48,768]{1,0:T(8,128)(2,1)S(1)}, bf16[48,768]{1,0:T(8,128)(2,1)S(1)}, u32[]{:S(2)}, u32[]{:S(2)}) collective-permute-start(bf16[48,768]{1,0:T(8,128)(2,1)S(1)} %get-tuple-element.47), channel_id=1, source_target_pairs={{0,22},{2,20},{4,18},{6,16},{8,30},{10,28},{12,26},{14,24},{16,6},... | collective-permute-start | bytes 221192 | tf_op jit(solution)/shard_map/ppermute | solution.py:34
  76.2 11.4 %collective-permute-start.20 = (bf16[48,768]{1,0:T(8,128)(2,1)S(1)}, bf16[48,768]{1,0:T(8,128)(2,1)S(1)}, u32[]{:S(2)}, u32[]{:S(2)}) collective-permute-start(bf16[48,768]{1,0:T(8,128)(2,1)S(1)} %get-tuple-element.45), channel_id=1, source_target_pairs={{0,6},{2,4},{4,2},{6,0},{8,14},{10,12},{12,10},{14,8},{16,22},{18,... | collective-permute-start | bytes 221192 | tf_op jit(solution)/shard_map/ppermute | solution.py:34
  79.9 14.9 %collective-permute-start.29 = (bf16[48,768]{1,0:T(8,128)(2,1)S(1)}, bf16[48,768]{1,0:T(8,128)(2,1)S(1)}, u32[]{:S(2)}, u32[]{:S(2)}) collective-permute-start(bf16[48,768]{1,0:T(8,128)(2,1)S(1)} %get-tuple-element.59), channel_id=1, source_target_pairs={{0,30},{2,28},{4,26},{6,24},{8,22},{10,20},{12,18},{14,16},{16,14}... | collective-permute-start | bytes 221192 | tf_op jit(solution)/shard_map/ppermute | solution.py:34
  83.4 11.3 %collective-permute-start.28 = (bf16[48,768]{1,0:T(8,128)(2,1)S(1)}, bf16[48,768]{1,0:T(8,128)(2,1)S(1)}, u32[]{:S(2)}, u32[]{:S(2)}) collective-permute-start(bf16[48,768]{1,0:T(8,128)(2,1)S(1)} %get-tuple-element.58), channel_id=1, source_target_pairs={{0,14},{2,12},{4,10},{6,8},{8,6},{10,4},{12,2},{14,0},{16,30},{18,... | collective-permute-start | bytes 221192 | tf_op jit(solution)/shard_map/ppermute | solution.py:34
  83.4 11.3 %collective-permute-start.27 = (bf16[48,768]{1,0:T(8,128)(2,1)S(1)}, bf16[48,768]{1,0:T(8,128)(2,1)S(1)}, u32[]{:S(2)}, u32[]{:S(2)}) collective-permute-start(bf16[48,768]{1,0:T(8,128)(2,1)S(1)} %get-tuple-element.57), channel_id=1, source_target_pairs={{0,28},{2,30},{4,24},{6,26},{8,20},{10,22},{12,16},{14,18},{16,12}... | collective-permute-start | bytes 221192 | tf_op jit(solution)/shard_map/ppermute | solution.py:34
  84.9 9.7 %collective-permute-start.26 = (bf16[48,768]{1,0:T(8,128)(2,1)S(1)}, bf16[48,768]{1,0:T(8,128)(2,1)S(1)}, u32[]{:S(2)}, u32[]{:S(2)}) collective-permute-start(bf16[48,768]{1,0:T(8,128)(2,1)S(1)} %get-tuple-element.56), channel_id=1, source_target_pairs={{0,12},{2,14},{4,8},{6,10},{8,4},{10,6},{12,0},{14,2},{16,28},{18,... | collective-permute-start | bytes 221192 | tf_op jit(solution)/shard_map/ppermute | solution.py:34
  87.6 7.1 %collective-permute-start.25 = (bf16[48,768]{1,0:T(8,128)(2,1)S(1)}, bf16[48,768]{1,0:T(8,128)(2,1)S(1)}, u32[]{:S(2)}, u32[]{:S(2)}) collective-permute-start(bf16[48,768]{1,0:T(8,128)(2,1)S(1)} %get-tuple-element.55), channel_id=1, source_target_pairs={{0,26},{2,24},{4,30},{6,28},{8,18},{10,16},{12,22},{14,20},{16,10}... | collective-permute-start | bytes 221192 | tf_op jit(solution)/shard_map/ppermute | solution.py:34
  94.7 5.9 %copy-start.5 = (bf16[768,768]{1,0:T(8,128)(2,1)S(1)}, bf16[768,768]{1,0:T(8,128)(2,1)}, u32[]{:S(2)}) copy-start(bf16[768,768]{1,0:T(8,128)(2,1)} %constant.162.clone.re_ref.refs_1_) | copy-start | bytes 3538948
  96.8 11.0 %all-to-all-start = ((f32[32,1,16]{2,1,0:T(1,128)}), f32[32,1,16]{2,1,0:T(1,128)S(1)}, u32[]{:S(2)}, u32[]{:S(2)}) async-start(f32[32,1,16]{2,1,0:T(1,128)} %bitcast.53), calls=%async_computation | async-start | bytes 32768 | tf_op jit(solution)/shard_map/all_to_all | solution.py:340

commit v11 on v10

--- a/solution.py
+++ b/solution.py
@@ -28,6 +28,16 @@
         stride *= 2
     digits.append((stride, count // stride))
     return digits
+
+
+def turns(count):
+    far, near = list(range(count // 2, count)), list(range(1, count // 2))
+    taken = [0]
+    while far or near:
+        some = far[:3] + near[: LANES - len(far[:3])]
+        far, near = far[3:], near[LANES - len(far[:3]) :]
+        taken += some[::-1]
+    return taken
 
 
 def exchange(values, offset, count):
@@ -173,12 +183,10 @@
     )
     held[...] = exactly(both, groups(right), ((1,), (1,)))
     if by_xor:
-        me, there = lax.axis_index("modes"), modes // 2
-        for mode in range(modes):
-            e = mode ^ me
-            at = e % there * 2 + e // there
-            out_ref[pl.ds(mode, 1)] = held[pl.ds(at, 1)]
-            out_ref[pl.ds(modes + mode, 1)] = held[pl.ds(modes + at, 1)]
+        me = lax.axis_index("modes")
+        for at, e in enumerate(turns(modes)):
+            out_ref[pl.ds(me ^ e, 1)] = held[pl.ds(at, 1)]
+            out_ref[pl.ds(modes + (me ^ e), 1)] = held[pl.ds(modes + at, 1)]
     else:
         out_ref[...] = held[...]
 
@@ -305,9 +313,8 @@
     blocks = columns.reshape(owners, 2, -1, block_rows, grid_size).transpose(0, 2, 1, 3, 4)
     blocks = blocks.reshape(count, 2 * block_rows, grid_size)
     if count <= 16:
-        turns = [at // 2 + count // 2 * (at % 2) for at in range(count)]
         pixels = [pick(blocks, me, 0)]
-        for at, e in enumerate(turns[1:], 1):
+        for at, e in enumerate(turns(count)[1:], 1):
             block = pick(blocks, me ^ e, 0)
             if at > LANES:
                 block, pixels[at - LANES] = lax.optimization_barrier((block, pixels[at - LANES]))
@@ -315,11 +322,18 @@
     else:
         pixels = [lax.all_to_all(blocks, "modes", 0, 0, tiled=True)]
 
-    if len(pixels) > 1:
-        targets, pixels[1] = lax.optimization_barrier((targets, pixels[1]))
+    output_fields = kernel_call(
+        lambda *refs: fields_kernel(block_rows, *refs),
+        (local_rows, double_width),
+        bf16,
+        matmul,
+        (columns, full_re, full_im),
+    )
+    targets, output_fields = lax.optimization_barrier((targets, output_fields))
     seen = kernel_call(
         targets_kernel, column_shape, bf16, matmul, (targets.reshape(column_shape), full_re, full_im)
     )
+    seen, output_fields = lax.optimization_barrier((seen, output_fields))
     rows = jnp.concatenate(pixels, 0).reshape(column_shape)
     term = kernel_call(
         lambda *refs: coupling_kernel(block_rows, len(pixels) > 1, *refs),
@@ -328,14 +342,6 @@
         matmul,
         (rows, seen),
         scratch_shapes=[pltpu.VMEM((2 * mode_total, mode_total), f32)],
-    )
-    columns, term = lax.optimization_barrier((columns, term))
-    output_fields = kernel_call(
-        lambda *refs: fields_kernel(block_rows, *refs),
-        (local_rows, double_width),
-        bf16,
-        matmul,
-        (columns, full_re, full_im),
     )
     pieces = lax.all_to_all(term, ("modes", "rows"), 0, 0, tiled=True)
     coupling = jnp.sum(pieces, 0, keepdims=True)

time: 109 us -> 110 us (level)
  waiting for transfers between devices: 39.7 us -> 41.7 us
    all_to_all x1, waiting for transfers between devices: 4.13 us -> 5.99 us  [local(): pieces = lax.all_to_all(term, ('modes', 'rows'), 0, 0, tiled=True)]
    unnamed x45 -> x43, local copies, waits for them, and re-layouts: 2.38 us -> 1.71 us
  transfers between devices with their start and end apart: 31 -> 31, of which waited for: 13 -> 14; matrix products, arithmetic and copies ran while one was open for 2% -> 2% of each run, Pallas kernels for 6% -> 6%
where the time goes in v11:
time: 110 us
  starting transfers between devices  50.7 us (46%)
  waiting for transfers between devices  41.7 us (38%)
  Pallas kernels  11 us (10%)
  other arithmetic  3.38 us (3%)
  local copies, waits for them, and re-layouts  2.18 us (2%)
  between operations  1.23 us (1%)
    ppermute x29, starting transfers between devices, exchange(): lax.ppermute(values, 'modes', [(i, i ^ offset) for i in range(count)])  46 us
    ppermute x29, waiting for transfers between devices, exchange(): lax.ppermute(values, 'modes', [(i, i ^ offset) for i in range(count)])  35.1 us
    pallas_call x6, Pallas kernels, kernel_call(): pl.pallas_call(kernel, out_shape=out_shape, compiler_params=pltpu.Compile...  11 us
    all_to_all x1, waiting for transfers between devices, local(): pieces = lax.all_to_all(term, ('modes', 'rows'), 0, 0, tiled=True)  5.99 us
    all_to_all x1, starting transfers between devices, local(): pieces = lax.all_to_all(term, ('modes', 'rows'), 0, 0, tiled=True)  4.6 us
  transfers between devices with their start and end apart: 31, of which 14 were waited for; matrix products, arithmetic and copies ran while one was open for 2% of the time, Pallas kernels for 6%

profile of v11, /device:TPU:0, one launch (start us, length us, event | category | flops | bytes accessed | tf_op | source)
XLA Modules:
  0.0 110.2 jit_solution(4922239756273114779)
XLA Ops:
  0.6 1.8 %shard_map.94 = (bf16[192,768]{1,0:T(8,128)(2,1)S(1)}, f32[192,768]{1,0:T(8,128)S(1)}, bf16[192,768]{1,0:T(8,128)(2,1)S(1)}, f32[192,768]{1,0:T(8,128)S(1)}) custom-call(bf16[384,1536]{1,0:T(8,128)(2,1)} %bitcast.100, bf16[384,1536]{1,0:T(8,128)(2,1)} %bitcast.103), custom_call_target="tpu_custom_call" | custom-call | flops 4718592 | bytes 4194304 | tf_op jit(solution)/shard_map/pallas_call | solution.py:202
  2.5 3.0 %collective-permute-start.2 = (bf16[4,2,24,768]{3,2,0,1:T(8,128)(2,1)S(1)}, bf16[4,2,24,768]{3,2,0,1:T(8,128)(2,1)S(1)}, u32[]{:S(2)}, u32[]{:S(2)}) collective-permute-start(bf16[4,2,24,768]{3,2,0,1:T(8,128)(2,1)S(1)} %copy.19), channel_id=1, source_target_pairs={{0,4},{2,6},{4,0},{6,2},{8,12},{10,14},{12,8},{14,10},{16,20},{18,... | collective-permute-start | bytes 884744 | tf_op jit(solution)/shard_map/ppermute | solution.py:44
  5.5 1.6 %collective-permute-start = (bf16[4,2,24,768]{3,2,0,1:T(8,128)(2,1)S(1)}, bf16[4,2,24,768]{3,2,0,1:T(8,128)(2,1)S(1)}, u32[]{:S(2)}, u32[]{:S(2)}) collective-permute-start(bf16[4,2,24,768]{3,2,0,1:T(8,128)(2,1)S(1)} %copy.17), channel_id=1, source_target_pairs={{0,2},{2,0},{4,6},{6,4},{8,10},{10,8},{12,14},{14,12},{16,18},{18,... | collective-permute-start | bytes 884744 | tf_op jit(solution)/shard_map/ppermute | solution.py:44
  7.1 5.4 %collective-permute-done.2 = bf16[4,2,24,768]{3,2,0,1:T(8,128)(2,1)S(1)} collective-permute-done((bf16[4,2,24,768]{3,2,0,1:T(8,128)(2,1)S(1)}, bf16[4,2,24,768]{3,2,0,1:T(8,128)(2,1)S(1)}, u32[]{:S(2)}, u32[]{:S(2)}) %collective-permute-start.2) | collective-permute-done | bytes 294944 | tf_op jit(solution)/shard_map/ppermute | solution.py:44
  12.6 1.8 %collective-permute-start.3 = (bf16[4,24,768]{2,1,0:T(8,128)(2,1)S(1)}, bf16[4,24,768]{2,1,0:T(8,128)(2,1)S(1)}, u32[]{:S(2)}, u32[]{:S(2)}) collective-permute-start(bf16[4,24,768]{2,1,0:T(8,128)(2,1)S(1)} %fusion.5), channel_id=1, source_target_pairs={{0,2},{2,0},{4,6},{6,4},{8,10},{10,8},{12,14},{14,12},{16,18},{18,... | collective-permute-start | bytes 442376 | tf_op jit(solution)/shard_map/ppermute | solution.py:44
  14.5 1.6 %collective-permute-start.1 = (bf16[4,24,768]{2,1,0:T(8,128)(2,1)S(1)}, bf16[4,24,768]{2,1,0:T(8,128)(2,1)S(1)}, u32[]{:S(2)}, u32[]{:S(2)}) collective-permute-start(bf16[4,24,768]{2,1,0:T(8,128)(2,1)S(1)} %fusion.4), channel_id=1, source_target_pairs={{0,4},{2,6},{4,0},{6,2},{8,12},{10,14},{12,8},{14,10},{16,20},{18,... | collective-permute-start | bytes 442376 | tf_op jit(solution)/shard_map/ppermute | solution.py:44
  16.1 1.8 %collective-permute-done.3 = bf16[4,24,768]{2,1,0:T(8,128)(2,1)S(1)} collective-permute-done((bf16[4,24,768]{2,1,0:T(8,128)(2,1)S(1)}, bf16[4,24,768]{2,1,0:T(8,128)(2,1)S(1)}, u32[]{:S(2)}, u32[]{:S(2)}) %collective-permute-start.3) | collective-permute-done | bytes 147488 | tf_op jit(solution)/shard_map/ppermute | solution.py:44
  17.8 1.8 %collective-permute-done.1 = bf16[4,24,768]{2,1,0:T(8,128)(2,1)S(1)} collective-permute-done((bf16[4,24,768]{2,1,0:T(8,128)(2,1)S(1)}, bf16[4,24,768]{2,1,0:T(8,128)(2,1)S(1)}, u32[]{:S(2)}, u32[]{:S(2)}) %collective-permute-start.1) | collective-permute-done | bytes 147488 | tf_op jit(solution)/shard_map/ppermute | solution.py:44
  19.8 1.6 %collective-permute-start.4 = (bf16[24,1536]{1,0:T(8,128)(2,1)S(1)}, bf16[24,1536]{1,0:T(8,128)(2,1)S(1)}, u32[]{:S(2)}, u32[]{:S(2)}) collective-permute-start(bf16[24,1536]{1,0:T(8,128)(2,1)S(1)} %get-tuple-element.84), channel_id=1, source_target_pairs={{0,8},{2,10},{4,12},{6,14},{8,0},{10,2},{12,4},{14,6},{16,24},{18,... | collective-permute-start | bytes 221192 | tf_op jit(solution)/shard_map/ppermute | solution.py:44
  21.4 2.6 %collective-permute-start.5 = (bf16[24,1536]{1,0:T(8,128)(2,1)S(1)}, bf16[24,1536]{1,0:T(8,128)(2,1)S(1)}, u32[]{:S(2)}, u32[]{:S(2)}) collective-permute-start(bf16[24,1536]{1,0:T(8,128)(2,1)S(1)} %get-tuple-element.85), channel_id=1, source_target_pairs={{0,16},{2,18},{4,20},{6,22},{8,24},{10,26},{12,28},{14,30},{16,0},... | collective-permute-start | bytes 221192 | tf_op jit(solution)/shard_map/ppermute | solution.py:44
  24.3 3.9 %collective-permute-done.5 = bf16[24,1536]{1,0:T(8,128)(2,1)S(1)} collective-permute-done((bf16[24,1536]{1,0:T(8,128)(2,1)S(1)}, bf16[24,1536]{1,0:T(8,128)(2,1)S(1)}, u32[]{:S(2)}, u32[]{:S(2)}) %collective-permute-start.5) | collective-permute-done | bytes 73760 | tf_op jit(solution)/shard_map/ppermute | solution.py:44
  28.1 2.1 %collective-permute-done.6 = bf16[24,1536]{1,0:T(8,128)(2,1)S(1)} collective-permute-done((bf16[24,1536]{1,0:T(8,128)(2,1)S(1)}, bf16[24,1536]{1,0:T(8,128)(2,1)S(1)}, u32[]{:S(2)}, u32[]{:S(2)}) %collective-permute-start.6) | collective-permute-done | bytes 73760 | tf_op jit(solution)/shard_map/ppermute | solution.py:44
  30.3 0.9 collective-permute-start.9
  31.2 1.5 %collective-permute-start.8 = (bf16[24,1536]{1,0:T(8,128)(2,1)S(1)}, bf16[24,1536]{1,0:T(8,128)(2,1)S(1)}, u32[]{:S(2)}, u32[]{:S(2)}) collective-permute-start(bf16[24,1536]{1,0:T(8,128)(2,1)S(1)} %pad_maximum_fusion.10), channel_id=1, source_target_pairs={{0,16},{2,18},{4,20},{6,22},{8,24},{10,26},{12,28},{14,30},{16,0},... | collective-permute-start | bytes 221192 | tf_op jit(solution)/shard_map/ppermute | solution.py:44
  32.7 2.1 %collective-permute-start.7 = (bf16[24,1536]{1,0:T(8,128)(2,1)S(1)}, bf16[24,1536]{1,0:T(8,128)(2,1)S(1)}, u32[]{:S(2)}, u32[]{:S(2)}) collective-permute-start(bf16[24,1536]{1,0:T(8,128)(2,1)S(1)} %pad_maximum_fusion.10), channel_id=1, source_target_pairs={{0,8},{2,10},{4,12},{6,14},{8,0},{10,2},{12,4},{14,6},{16,24},{18,... | collective-permute-start | bytes 221192 | tf_op jit(solution)/shard_map/ppermute | solution.py:44
  34.8 1.9 %collective-permute-done.9 = bf16[24,1536]{1,0:T(8,128)(2,1)S(1)} collective-permute-done((bf16[24,1536]{1,0:T(8,128)(2,1)S(1)}, bf16[24,1536]{1,0:T(8,128)(2,1)S(1)}, u32[]{:S(2)}, u32[]{:S(2)}) %collective-permute-start.9) | collective-permute-done | bytes 73760 | tf_op jit(solution)/shard_map/ppermute | solution.py:44
  36.7 1.3 %collective-permute-done.8 = bf16[24,1536]{1,0:T(8,128)(2,1)S(1)} collective-permute-done((bf16[24,1536]{1,0:T(8,128)(2,1)S(1)}, bf16[24,1536]{1,0:T(8,128)(2,1)S(1)}, u32[]{:S(2)}, u32[]{:S(2)}) %collective-permute-start.8) | collective-permute-done | bytes 73760 | tf_op jit(solution)/shard_map/ppermute | solution.py:44
  38.2 1.2 %collective-permute-start.12 = (bf16[4,24,768]{2,1,0:T(8,128)(2,1)S(1)}, bf16[4,24,768]{2,1,0:T(8,128)(2,1)S(1)}, u32[]{:S(2)}, u32[]{:S(2)}) collective-permute-start(bf16[4,24,768]{2,1,0:T(8,128)(2,1)S(1)} %get-tuple-element.89), channel_id=1, source_target_pairs={{0,2},{2,0},{4,6},{6,4},{8,10},{10,8},{12,14},{14,12},{16,18},{18,... | collective-permute-start | bytes 442376 | tf_op jit(solution)/shard_map/ppermute | solution.py:44
  39.7 1.5 %collective-permute-start.10 = (bf16[4,24,768]{2,1,0:T(8,128)(2,1)S(1)}, bf16[4,24,768]{2,1,0:T(8,128)(2,1)S(1)}, u32[]{:S(2)}, u32[]{:S(2)}) collective-permute-start(bf16[4,24,768]{2,1,0:T(8,128)(2,1)S(1)} %get-tuple-element.90), channel_id=1, source_target_pairs={{0,4},{2,6},{4,0},{6,2},{8,12},{10,14},{12,8},{14,10},{16,20},{18,... | collective-permute-start | bytes 442376 | tf_op jit(solution)/shard_map/ppermute | solution.py:44
  41.2 3.3 %collective-permute-done.12 = bf16[4,24,768]{2,1,0:T(8,128)(2,1)S(1)} collective-permute-done((bf16[4,24,768]{2,1,0:T(8,128)(2,1)S(1)}, bf16[4,24,768]{2,1,0:T(8,128)(2,1)S(1)}, u32[]{:S(2)}, u32[]{:S(2)}) %collective-permute-start.12) | collective-permute-done | bytes 147488 | tf_op jit(solution)/shard_map/ppermute | solution.py:44
  44.6 1.7 %collective-permute-start.13 = (bf16[4,2,24,768]{3,2,0,1:T(8,128)(2,1)S(1)}, bf16[4,2,24,768]{3,2,0,1:T(8,128)(2,1)S(1)}, u32[]{:S(2)}, u32[]{:S(2)}) collective-permute-start(bf16[4,2,24,768]{3,2,0,1:T(8,128)(2,1)S(1)} %reverse_select_fusion.2), channel_id=1, source_target_pairs={{0,4},{2,6},{4,0},{6,2},{8,12},{10,14},{12,8},{14,10},{16,20},{18,... | collective-permute-start | bytes 884744 | tf_op jit(solution)/shard_map/ppermute | solution.py:44
  47.1 4.3 %collective-permute-done.13 = bf16[4,2,24,768]{3,2,0,1:T(8,128)(2,1)S(1)} collective-permute-done((bf16[4,2,24,768]{3,2,0,1:T(8,128)(2,1)S(1)}, bf16[4,2,24,768]{3,2,0,1:T(8,128)(2,1)S(1)}, u32[]{:S(2)}, u32[]{:S(2)}) %collective-permute-start.13) | collective-permute-done | bytes 294944 | tf_op jit(solution)/shard_map/ppermute | solution.py:44
  51.6 1.7 %collective-permute-done.11 = bf16[4,2,24,768]{3,2,1,0:T(8,128)(2,1)S(1)} collective-permute-done((bf16[4,2,24,768]{3,2,1,0:T(8,128)(2,1)S(1)}, bf16[4,2,24,768]{3,2,1,0:T(8,128)(2,1)S(1)}, u32[]{:S(2)}, u32[]{:S(2)}) %collective-permute-start.11) | collective-permute-done | bytes 294944 | tf_op jit(solution)/shard_map/ppermute | solution.py:44
  54.9 1.0 copy-done.1
  55.9 1.1 shard_map.95.own_ref
  57.6 1.1 shard_map.96.refs_0_
  58.9 0.7 collective-permute-start.19
  59.6 2.1 %collective-permute-start.18 = (bf16[48,768]{1,0:T(8,128)(2,1)S(1)}, bf16[48,768]{1,0:T(8,128)(2,1)S(1)}, u32[]{:S(2)}, u32[]{:S(2)}) collective-permute-start(bf16[48,768]{1,0:T(8,128)(2,1)S(1)} %get-tuple-element.72), channel_id=1, source_target_pairs={{0,18},{2,16},{4,22},{6,20},{8,26},{10,24},{12,30},{14,28},{16,2},... | collective-permute-start | bytes 221192 | tf_op jit(solution)/shard_map/ppermute | solution.py:44
  61.7 1.4 %collective-permute-start.17 = (bf16[48,768]{1,0:T(8,128)(2,1)S(1)}, bf16[48,768]{1,0:T(8,128)(2,1)S(1)}, u32[]{:S(2)}, u32[]{:S(2)}) collective-permute-start(bf16[48,768]{1,0:T(8,128)(2,1)S(1)} %get-tuple-element.74), channel_id=1, source_target_pairs={{0,20},{2,22},{4,16},{6,18},{8,28},{10,30},{12,24},{14,26},{16,4},... | collective-permute-start | bytes 221192 | tf_op jit(solution)/shard_map/ppermute | solution.py:44
  63.1 1.1 %collective-permute-start.16 = (bf16[48,768]{1,0:T(8,128)(2,1)S(1)}, bf16[48,768]{1,0:T(8,128)(2,1)S(1)}, u32[]{:S(2)}, u32[]{:S(2)}) collective-permute-start(bf16[48,768]{1,0:T(8,128)(2,1)S(1)} %get-tuple-element.76), channel_id=1, source_target_pairs={{0,2},{2,0},{4,6},{6,4},{8,10},{10,8},{12,14},{14,12},{16,18},{18,... | collective-permute-start | bytes 221192 | tf_op jit(solution)/shard_map/ppermute | solution.py:44
  64.2 1.2 %collective-permute-start.15 = (bf16[48,768]{1,0:T(8,128)(2,1)S(1)}, bf16[48,768]{1,0:T(8,128)(2,1)S(1)}, u32[]{:S(2)}, u32[]{:S(2)}) collective-permute-start(bf16[48,768]{1,0:T(8,128)(2,1)S(1)} %get-tuple-element.78), channel_id=1, source_target_pairs={{0,4},{2,6},{4,0},{6,2},{8,12},{10,14},{12,8},{14,10},{16,20},{18,... | collective-permute-start | bytes 221192 | tf_op jit(solution)/shard_map/ppermute | solution.py:44
  65.5 3.0 %shard_map.97 = bf16[384,1536]{1,0:T(8,128)(2,1)} custom-call(bf16[768,768]{1,0:T(8,128)(2,1)S(1)} %shard_map.96.refs_0_, bf16[768,768]{1,0:T(8,128)(2,1)S(1)} %copy-done.4, bf16[768,768]{1,0:T(8,128)(2,1)S(1)} %copy-done.3), custom_call_target="tpu_custom_call" | custom-call | flops 1811939328 | bytes 4194304 | tf_op jit(solution)/shard_map/pallas_call | solution.py:202
  68.5 2.0 %shard_map.98.refs_1_ = bf16[768,768]{1,0:T(8,128)(2,1)S(1)} custom-call(bf16[768,768]{1,0:T(8,128)(2,1)S(1)} %bitcast.99, bf16[768,768]{1,0:T(8,128)(2,1)S(1)} %copy-done.4, bf16[768,768]{1,0:T(8,128)(2,1)S(1)} %copy-done.3), custom_call_target="tpu_custom_call" | custom-call | flops 1811939328 | bytes 4194304 | tf_op jit(solution)/shard_map/pallas_call | solution.py:202
  70.5 2.9 %collective-permute-start.24 = (bf16[48,768]{1,0:T(8,128)(2,1)S(1)}, bf16[48,768]{1,0:T(8,128)(2,1)S(1)}, u32[]{:S(2)}, u32[]{:S(2)}) collective-permute-start(bf16[48,768]{1,0:T(8,128)(2,1)S(1)} %get-tuple-element.55), channel_id=1, source_target_pairs={{0,22},{2,20},{4,18},{6,16},{8,30},{10,28},{12,26},{14,24},{16,6},... | collective-permute-start | bytes 221192 | tf_op jit(solution)/shard_map/ppermute | solution.py:44
  73.4 1.7 %collective-permute-start.23 = (bf16[48,768]{1,0:T(8,128)(2,1)S(1)}, bf16[48,768]{1,0:T(8,128)(2,1)S(1)}, u32[]{:S(2)}, u32[]{:S(2)}) collective-permute-start(bf16[48,768]{1,0:T(8,128)(2,1)S(1)} %get-tuple-element.53), channel_id=1, source_target_pairs={{0,24},{2,26},{4,28},{6,30},{8,16},{10,18},{12,20},{14,22},{16,8},... | collective-permute-start | bytes 221192 | tf_op jit(solution)/shard_map/ppermute | solution.py:44
  75.2 2.6 %collective-permute-start.22 = (bf16[48,768]{1,0:T(8,128)(2,1)S(1)}, bf16[48,768]{1,0:T(8,128)(2,1)S(1)}, u32[]{:S(2)}, u32[]{:S(2)}) collective-permute-start(bf16[48,768]{1,0:T(8,128)(2,1)S(1)} %get-tuple-element.51), channel_id=1, source_target_pairs={{0,26},{2,24},{4,30},{6,28},{8,18},{10,16},{12,22},{14,20},{16,10}... | collective-permute-start | bytes 221192 | tf_op jit(solution)/shard_map/ppermute | solution.py:44
  77.8 1.1 %collective-permute-start.21 = (bf16[48,768]{1,0:T(8,128)(2,1)S(1)}, bf16[48,768]{1,0:T(8,128)(2,1)S(1)}, u32[]{:S(2)}, u32[]{:S(2)}) collective-permute-start(bf16[48,768]{1,0:T(8,128)(2,1)S(1)} %get-tuple-element.49), channel_id=1, source_target_pairs={{0,6},{2,4},{4,2},{6,0},{8,14},{10,12},{12,10},{14,8},{16,22},{18,... | collective-permute-start | bytes 221192 | tf_op jit(solution)/shard_map/ppermute | solution.py:44
  79.0 3.4 %collective-permute-done.24 = bf16[48,768]{1,0:T(8,128)(2,1)S(1)} collective-permute-done((bf16[48,768]{1,0:T(8,128)(2,1)S(1)}, bf16[48,768]{1,0:T(8,128)(2,1)S(1)}, u32[]{:S(2)}, u32[]{:S(2)}) %collective-permute-start.24) | collective-permute-done | bytes 73760 | tf_op jit(solution)/shard_map/ppermute | solution.py:44
  82.4 1.4 %collective-permute-start.29 = (bf16[48,768]{1,0:T(8,128)(2,1)S(1)}, bf16[48,768]{1,0:T(8,128)(2,1)S(1)}, u32[]{:S(2)}, u32[]{:S(2)}) collective-permute-start(bf16[48,768]{1,0:T(8,128)(2,1)S(1)} %get-tuple-element.61), channel_id=1, source_target_pairs={{0,28},{2,30},{4,24},{6,26},{8,20},{10,22},{12,16},{14,18},{16,12}... | collective-permute-start | bytes 221192 | tf_op jit(solution)/shard_map/ppermute | solution.py:44
  83.8 0.9 collective-permute-start.28
  84.8 2.0 %collective-permute-start.27 = (bf16[48,768]{1,0:T(8,128)(2,1)S(1)}, bf16[48,768]{1,0:T(8,128)(2,1)S(1)}, u32[]{:S(2)}, u32[]{:S(2)}) collective-permute-start(bf16[48,768]{1,0:T(8,128)(2,1)S(1)} %get-tuple-element.59), channel_id=1, source_target_pairs={{0,10},{2,8},{4,14},{6,12},{8,2},{10,0},{12,6},{14,4},{16,26},{18,... | collective-permute-start | bytes 221192 | tf_op jit(solution)/shard_map/ppermute | solution.py:44
  86.8 2.8 %collective-permute-start.26 = (bf16[48,768]{1,0:T(8,128)(2,1)S(1)}, bf16[48,768]{1,0:T(8,128)(2,1)S(1)}, u32[]{:S(2)}, u32[]{:S(2)}) collective-permute-start(bf16[48,768]{1,0:T(8,128)(2,1)S(1)} %get-tuple-element.58), channel_id=1, source_target_pairs={{0,12},{2,14},{4,8},{6,10},{8,4},{10,6},{12,0},{14,2},{16,28},{18,... | collective-permute-start | bytes 221192 | tf_op jit(solution)/shard_map/ppermute | solution.py:44
  89.5 2.1 %collective-permute-start.25 = (bf16[48,768]{1,0:T(8,128)(2,1)S(1)}, bf16[48,768]{1,0:T(8,128)(2,1)S(1)}, u32[]{:S(2)}, u32[]{:S(2)}) collective-permute-start(bf16[48,768]{1,0:T(8,128)(2,1)S(1)} %get-tuple-element.57), channel_id=1, source_target_pairs={{0,14},{2,12},{4,10},{6,8},{8,6},{10,4},{12,2},{14,0},{16,30},{18,... | collective-permute-start | bytes 221192 | tf_op jit(solution)/shard_map/ppermute | solution.py:44
  91.7 4.0 %collective-permute-done.25 = bf16[48,768]{1,0:T(8,128)(2,1)S(1)} collective-permute-done((bf16[48,768]{1,0:T(8,128)(2,1)S(1)}, bf16[48,768]{1,0:T(8,128)(2,1)S(1)}, u32[]{:S(2)}, u32[]{:S(2)}) %collective-permute-start.25) | collective-permute-done | bytes 73760 | tf_op jit(solution)/shard_map/ppermute | solution.py:44
  95.8 2.0 %shard_map.99 = f32[32,16]{1,0:T(8,128)} custom-call(bf16[768,768]{1,0:T(8,128)(2,1)S(1)} %constant_dynamic-update-slice_fusion.refs_0_, bf16[768,768]{1,0:T(8,128)(2,1)S(1)} %shard_map.98.refs_1_), custom_call_target="tpu_custom_call" | custom-call | flops 1811939328 | bytes 4194304 | tf_op jit(solution)/shard_map/pallas_call | solution.py:202
  97.8 4.6 %all-to-all-start = ((f32[32,1,16]{2,1,0:T(1,128)}), f32[32,1,16]{2,1,0:T(1,128)S(1)}, u32[]{:S(2)}, u32[]{:S(2)}) async-start(f32[32,1,16]{2,1,0:T(1,128)} %bitcast.53), calls=%async_computation | async-start | bytes 32768 | tf_op jit(solution)/shard_map/all_to_all | solution.py:346
  102.5 1.1 %pad_maximum_fusion = bf16[384,1536]{1,0:T(8,128)(2,1)} fusion(bf16[384,384]{1,0:T(8,128)(2,1)S(1)} %copy-done.11, bf16[384,384]{1,0:T(8,128)(2,1)S(1)} %copy-done.9, bf16[384,384]{1,0:T(8,128)(2,1)S(1)} %copy-done.13, bf16[384,384]{1,0:T(8,128)(2,1)S(1)} %copy-done.7), kind=kLoop, calls=%fused_computation.8 | loop fusion | flops 4718592 | bytes 2359296 | tf_op jit(solution)/shard_map/concatenate | solution.py:285
  103.6 6.0 %all-to-all-done = f32[32,1,16]{2,1,0:T(1,128)S(1)} async-done(((f32[32,1,16]{2,1,0:T(1,128)}), f32[32,1,16]{2,1,0:T(1,128)S(1)}, u32[]{:S(2)}, u32[]{:S(2)}) %all-to-all-start) | async-done | bytes 2080 | tf_op jit(solution)/shard_map/all_to_all | solution.py:346
  (98 shorter events, 5.0 us)
Async XLA Ops:
  2.5 10.0 %collective-permute-start.2 = (bf16[4,2,24,768]{3,2,0,1:T(8,128)(2,1)S(1)}, bf16[4,2,24,768]{3,2,0,1:T(8,128)(2,1)S(1)}, u32[]{:S(2)}, u32[]{:S(2)}) collective-permute-start(bf16[4,2,24,768]{3,2,0,1:T(8,128)(2,1)S(1)} %copy.19), channel_id=1, source_target_pairs={{0,4},{2,6},{4,0},{6,2},{8,12},{10,14},{12,8},{14,10},{16,20},{18,... | collective-permute-start | bytes 884744 | tf_op jit(solution)/shard_map/ppermute | solution.py:44
  5.5 8.9 %collective-permute-start = (bf16[4,2,24,768]{3,2,0,1:T(8,128)(2,1)S(1)}, bf16[4,2,24,768]{3,2,0,1:T(8,128)(2,1)S(1)}, u32[]{:S(2)}, u32[]{:S(2)}) collective-permute-start(bf16[4,2,24,768]{3,2,0,1:T(8,128)(2,1)S(1)} %copy.17), channel_id=1, source_target_pairs={{0,2},{2,0},{4,6},{6,4},{8,10},{10,8},{12,14},{14,12},{16,18},{18,... | collective-permute-start | bytes 884744 | tf_op jit(solution)/shard_map/ppermute | solution.py:44
  12.6 5.2 %collective-permute-start.3 = (bf16[4,24,768]{2,1,0:T(8,128)(2,1)S(1)}, bf16[4,24,768]{2,1,0:T(8,128)(2,1)S(1)}, u32[]{:S(2)}, u32[]{:S(2)}) collective-permute-start(bf16[4,24,768]{2,1,0:T(8,128)(2,1)S(1)} %fusion.5), channel_id=1, source_target_pairs={{0,2},{2,0},{4,6},{6,4},{8,10},{10,8},{12,14},{14,12},{16,18},{18,... | collective-permute-start | bytes 442376 | tf_op jit(solution)/shard_map/ppermute | solution.py:44
  14.5 5.2 %collective-permute-start.1 = (bf16[4,24,768]{2,1,0:T(8,128)(2,1)S(1)}, bf16[4,24,768]{2,1,0:T(8,128)(2,1)S(1)}, u32[]{:S(2)}, u32[]{:S(2)}) collective-permute-start(bf16[4,24,768]{2,1,0:T(8,128)(2,1)S(1)} %fusion.4), channel_id=1, source_target_pairs={{0,4},{2,6},{4,0},{6,2},{8,12},{10,14},{12,8},{14,10},{16,20},{18,... | collective-permute-start | bytes 442376 | tf_op jit(solution)/shard_map/ppermute | solution.py:44
  19.8 4.5 %collective-permute-start.4 = (bf16[24,1536]{1,0:T(8,128)(2,1)S(1)}, bf16[24,1536]{1,0:T(8,128)(2,1)S(1)}, u32[]{:S(2)}, u32[]{:S(2)}) collective-permute-start(bf16[24,1536]{1,0:T(8,128)(2,1)S(1)} %get-tuple-element.84), channel_id=1, source_target_pairs={{0,8},{2,10},{4,12},{6,14},{8,0},{10,2},{12,4},{14,6},{16,24},{18,... | collective-permute-start | bytes 221192 | tf_op jit(solution)/shard_map/ppermute | solution.py:44
  21.4 6.7 %collective-permute-start.5 = (bf16[24,1536]{1,0:T(8,128)(2,1)S(1)}, bf16[24,1536]{1,0:T(8,128)(2,1)S(1)}, u32[]{:S(2)}, u32[]{:S(2)}) collective-permute-start(bf16[24,1536]{1,0:T(8,128)(2,1)S(1)} %get-tuple-element.85), channel_id=1, source_target_pairs={{0,16},{2,18},{4,20},{6,22},{8,24},{10,26},{12,28},{14,30},{16,0},... | collective-permute-start | bytes 221192 | tf_op jit(solution)/shard_map/ppermute | solution.py:44
  24.0 6.3 %collective-permute-start.6 = (bf16[24,1536]{1,0:T(8,128)(2,1)S(1)}, bf16[24,1536]{1,0:T(8,128)(2,1)S(1)}, u32[]{:S(2)}, u32[]{:S(2)}) collective-permute-start(bf16[24,1536]{1,0:T(8,128)(2,1)S(1)} %get-tuple-element.86), channel_id=1, source_target_pairs={{0,24},{2,26},{4,28},{6,30},{8,16},{10,18},{12,20},{14,22},{16,8},... | collective-permute-start | bytes 221192 | tf_op jit(solution)/shard_map/ppermute | solution.py:44
  30.3 6.4 %collective-permute-start.9 = (bf16[24,1536]{1,0:T(8,128)(2,1)S(1)}, bf16[24,1536]{1,0:T(8,128)(2,1)S(1)}, u32[]{:S(2)}, u32[]{:S(2)}) collective-permute-start(bf16[24,1536]{1,0:T(8,128)(2,1)S(1)} %pad_maximum_fusion.10), channel_id=1, source_target_pairs={{0,24},{2,26},{4,28},{6,30},{8,16},{10,18},{12,20},{14,22},{16,8},... | collective-permute-start | bytes 221192 | tf_op jit(solution)/shard_map/ppermute | solution.py:44
  31.2 6.8 %collective-permute-start.8 = (bf16[24,1536]{1,0:T(8,128)(2,1)S(1)}, bf16[24,1536]{1,0:T(8,128)(2,1)S(1)}, u32[]{:S(2)}, u32[]{:S(2)}) collective-permute-start(bf16[24,1536]{1,0:T(8,128)(2,1)S(1)} %pad_maximum_fusion.10), channel_id=1, source_target_pairs={{0,16},{2,18},{4,20},{6,22},{8,24},{10,26},{12,28},{14,30},{16,0},... | collective-permute-start | bytes 221192 | tf_op jit(solution)/shard_map/ppermute | solution.py:44
  32.7 5.4 %collective-permute-start.7 = (bf16[24,1536]{1,0:T(8,128)(2,1)S(1)}, bf16[24,1536]{1,0:T(8,128)(2,1)S(1)}, u32[]{:S(2)}, u32[]{:S(2)}) collective-permute-start(bf16[24,1536]{1,0:T(8,128)(2,1)S(1)} %pad_maximum_fusion.10), channel_id=1, source_target_pairs={{0,8},{2,10},{4,12},{6,14},{8,0},{10,2},{12,4},{14,6},{16,24},{18,... | collective-permute-start | bytes 221192 | tf_op jit(solution)/shard_map/ppermute | solution.py:44
  38.1 1.4 %copy-start.5 = (bf16[1,384,1536]{2,1,0:T(8,128)(2,1)S(1)}, bf16[1,384,1536]{2,1,0:T(8,128)(2,1)}, u32[]{:S(2)}) copy-start(bf16[1,384,1536]{2,1,0:T(8,128)(2,1)} %param.7) | copy-start | bytes 3538948
  38.2 6.3 %collective-permute-start.12 = (bf16[4,24,768]{2,1,0:T(8,128)(2,1)S(1)}, bf16[4,24,768]{2,1,0:T(8,128)(2,1)S(1)}, u32[]{:S(2)}, u32[]{:S(2)}) collective-permute-start(bf16[4,24,768]{2,1,0:T(8,128)(2,1)S(1)} %get-tuple-element.89), channel_id=1, source_target_pairs={{0,2},{2,0},{4,6},{6,4},{8,10},{10,8},{12,14},{14,12},{16,18},{18,... | collective-permute-start | bytes 442376 | tf_op jit(solution)/shard_map/ppermute | solution.py:44
  39.7 6.6 %collective-permute-start.10 = (bf16[4,24,768]{2,1,0:T(8,128)(2,1)S(1)}, bf16[4,24,768]{2,1,0:T(8,128)(2,1)S(1)}, u32[]{:S(2)}, u32[]{:S(2)}) collective-permute-start(bf16[4,24,768]{2,1,0:T(8,128)(2,1)S(1)} %get-tuple-element.90), channel_id=1, source_target_pairs={{0,4},{2,6},{4,0},{6,2},{8,12},{10,14},{12,8},{14,10},{16,20},{18,... | collective-permute-start | bytes 442376 | tf_op jit(solution)/shard_map/ppermute | solution.py:44
  44.6 6.8 %collective-permute-start.13 = (bf16[4,2,24,768]{3,2,0,1:T(8,128)(2,1)S(1)}, bf16[4,2,24,768]{3,2,0,1:T(8,128)(2,1)S(1)}, u32[]{:S(2)}, u32[]{:S(2)}) collective-permute-start(bf16[4,2,24,768]{3,2,0,1:T(8,128)(2,1)S(1)} %reverse_select_fusion.2), channel_id=1, source_target_pairs={{0,4},{2,6},{4,0},{6,2},{8,12},{10,14},{12,8},{14,10},{16,20},{18,... | collective-permute-start | bytes 884744 | tf_op jit(solution)/shard_map/ppermute | solution.py:44
  46.5 6.8 %collective-permute-start.11 = (bf16[4,2,24,768]{3,2,1,0:T(8,128)(2,1)S(1)}, bf16[4,2,24,768]{3,2,1,0:T(8,128)(2,1)S(1)}, u32[]{:S(2)}, u32[]{:S(2)}) collective-permute-start(bf16[4,2,24,768]{3,2,1,0:T(8,128)(2,1)S(1)} %reverse_select_fusion.3), channel_id=1, source_target_pairs={{0,2},{2,0},{4,6},{6,4},{8,10},{10,8},{12,14},{14,12},{16,18},{18,... | collective-permute-start | bytes 884744 | tf_op jit(solution)/shard_map/ppermute | solution.py:44
  53.6 0.7 copy-start.6
  53.6 0.8 copy-start.8
  53.6 0.9 copy-start.10
  53.6 1.0 copy-start.12
  54.6 1.3 %copy-start.1 = (bf16[768,768]{1,0:T(8,128)(2,1)S(1)}, bf16[768,768]{1,0:T(8,128)(2,1)}, u32[]{:S(2)}) copy-start(bf16[768,768]{1,0:T(8,128)(2,1)} %constant.164.clone.table_ref) | copy-start | bytes 3538948
  54.7 2.9 %collective-permute-start.14 = (bf16[768,768]{1,0:T(8,128)(2,1)S(1)}, bf16[768,768]{1,0:T(8,128)(2,1)S(1)}, u32[]{:S(2)}, u32[]{:S(2)}) collective-permute-start(bf16[768,768]{1,0:T(8,128)(2,1)S(1)} %pad_maximum_fusion.1.shaped_ref), channel_id=1, source_target_pairs={{0,1},{1,0},{2,3},{3,2},{4,5},{5,4},{6,7},{7,6},{8,9},{9,8},{10,11... | collective-permute-start | bytes 3538952 | tf_op jit(solution)/shard_map/ppermute | solution.py:293
  55.9 1.7 %copy-start = (bf16[768,768]{1,0:T(8,128)(2,1)S(1)}, bf16[768,768]{1,0:T(8,128)(2,1)}, u32[]{:S(2)}) copy-start(bf16[768,768]{1,0:T(8,128)(2,1)} %constant.165.clone.table_ref) | copy-start | bytes 3538948
  57.6 7.8 %copy-start.4 = (bf16[768,768]{1,0:T(8,128)(2,1)S(1)}, bf16[768,768]{1,0:T(8,128)(2,1)}, u32[]{:S(2)}) copy-start(bf16[768,768]{1,0:T(8,128)(2,1)} %constant.162.clone.refs_1_.re_ref) | copy-start | bytes 3538948
  58.7 6.8 %copy-start.3 = (bf16[768,768]{1,0:T(8,128)(2,1)S(1)}, bf16[768,768]{1,0:T(8,128)(2,1)}, u32[]{:S(2)}) copy-start(bf16[768,768]{1,0:T(8,128)(2,1)} %constant.163.clone.refs_2_.im_ref) | copy-start | bytes 3538948
  58.9 11.6 %collective-permute-start.19 = (bf16[48,768]{1,0:T(8,128)(2,1)S(1)}, bf16[48,768]{1,0:T(8,128)(2,1)S(1)}, u32[]{:S(2)}, u32[]{:S(2)}) collective-permute-start(bf16[48,768]{1,0:T(8,128)(2,1)S(1)} %get-tuple-element.70), channel_id=1, source_target_pairs={{0,16},{2,18},{4,20},{6,22},{8,24},{10,26},{12,28},{14,30},{16,0},... | collective-permute-start | bytes 221192 | tf_op jit(solution)/shard_map/ppermute | solution.py:44
  59.6 13.8 %collective-permute-start.18 = (bf16[48,768]{1,0:T(8,128)(2,1)S(1)}, bf16[48,768]{1,0:T(8,128)(2,1)S(1)}, u32[]{:S(2)}, u32[]{:S(2)}) collective-permute-start(bf16[48,768]{1,0:T(8,128)(2,1)S(1)} %get-tuple-element.72), channel_id=1, source_target_pairs={{0,18},{2,16},{4,22},{6,20},{8,26},{10,24},{12,30},{14,28},{16,2},... | collective-permute-start | bytes 221192 | tf_op jit(solution)/shard_map/ppermute | solution.py:44
  61.7 13.4 %collective-permute-start.17 = (bf16[48,768]{1,0:T(8,128)(2,1)S(1)}, bf16[48,768]{1,0:T(8,128)(2,1)S(1)}, u32[]{:S(2)}, u32[]{:S(2)}) collective-permute-start(bf16[48,768]{1,0:T(8,128)(2,1)S(1)} %get-tuple-element.74), channel_id=1, source_target_pairs={{0,20},{2,22},{4,16},{6,18},{8,28},{10,30},{12,24},{14,26},{16,4},... | collective-permute-start | bytes 221192 | tf_op jit(solution)/shard_map/ppermute | solution.py:44
  63.1 14.6 %collective-permute-start.16 = (bf16[48,768]{1,0:T(8,128)(2,1)S(1)}, bf16[48,768]{1,0:T(8,128)(2,1)S(1)}, u32[]{:S(2)}, u32[]{:S(2)}) collective-permute-start(bf16[48,768]{1,0:T(8,128)(2,1)S(1)} %get-tuple-element.76), channel_id=1, source_target_pairs={{0,2},{2,0},{4,6},{6,4},{8,10},{10,8},{12,14},{14,12},{16,18},{18,... | collective-permute-start | bytes 221192 | tf_op jit(solution)/shard_map/ppermute | solution.py:44
  64.2 4.2 %copy-start.2 = (bf16[2,16,24,768]{3,2,1,0:T(8,128)(2,1)S(1)}, bf16[2,16,24,768]{3,2,1,0:T(8,128)(2,1)}, u32[]{:S(2)}) copy-start(bf16[2,16,24,768]{3,2,1,0:T(8,128)(2,1)} %param.9) | copy-start | bytes 3538948
  64.2 14.7 %collective-permute-start.15 = (bf16[48,768]{1,0:T(8,128)(2,1)S(1)}, bf16[48,768]{1,0:T(8,128)(2,1)S(1)}, u32[]{:S(2)}, u32[]{:S(2)}) collective-permute-start(bf16[48,768]{1,0:T(8,128)(2,1)S(1)} %get-tuple-element.78), channel_id=1, source_target_pairs={{0,4},{2,6},{4,0},{6,2},{8,12},{10,14},{12,8},{14,10},{16,20},{18,... | collective-permute-start | bytes 221192 | tf_op jit(solution)/shard_map/ppermute | solution.py:44
  70.5 11.9 %collective-permute-start.24 = (bf16[48,768]{1,0:T(8,128)(2,1)S(1)}, bf16[48,768]{1,0:T(8,128)(2,1)S(1)}, u32[]{:S(2)}, u32[]{:S(2)}) collective-permute-start(bf16[48,768]{1,0:T(8,128)(2,1)S(1)} %get-tuple-element.55), channel_id=1, source_target_pairs={{0,22},{2,20},{4,18},{6,16},{8,30},{10,28},{12,26},{14,24},{16,6},... | collective-permute-start | bytes 221192 | tf_op jit(solution)/shard_map/ppermute | solution.py:44
  73.4 10.4 %collective-permute-start.23 = (bf16[48,768]{1,0:T(8,128)(2,1)S(1)}, bf16[48,768]{1,0:T(8,128)(2,1)S(1)}, u32[]{:S(2)}, u32[]{:S(2)}) collective-permute-start(bf16[48,768]{1,0:T(8,128)(2,1)S(1)} %get-tuple-element.53), channel_id=1, source_target_pairs={{0,24},{2,26},{4,28},{6,30},{8,16},{10,18},{12,20},{14,22},{16,8},... | collective-permute-start | bytes 221192 | tf_op jit(solution)/shard_map/ppermute | solution.py:44
  75.2 9.6 %collective-permute-start.22 = (bf16[48,768]{1,0:T(8,128)(2,1)S(1)}, bf16[48,768]{1,0:T(8,128)(2,1)S(1)}, u32[]{:S(2)}, u32[]{:S(2)}) collective-permute-start(bf16[48,768]{1,0:T(8,128)(2,1)S(1)} %get-tuple-element.51), channel_id=1, source_target_pairs={{0,26},{2,24},{4,30},{6,28},{8,18},{10,16},{12,22},{14,20},{16,10}... | collective-permute-start | bytes 221192 | tf_op jit(solution)/shard_map/ppermute | solution.py:44
  77.8 9.0 %collective-permute-start.21 = (bf16[48,768]{1,0:T(8,128)(2,1)S(1)}, bf16[48,768]{1,0:T(8,128)(2,1)S(1)}, u32[]{:S(2)}, u32[]{:S(2)}) collective-permute-start(bf16[48,768]{1,0:T(8,128)(2,1)S(1)} %get-tuple-element.49), channel_id=1, source_target_pairs={{0,6},{2,4},{4,2},{6,0},{8,14},{10,12},{12,10},{14,8},{16,22},{18,... | collective-permute-start | bytes 221192 | tf_op jit(solution)/shard_map/ppermute | solution.py:44
  78.9 10.6 %collective-permute-start.20 = (bf16[48,768]{1,0:T(8,128)(2,1)S(1)}, bf16[48,768]{1,0:T(8,128)(2,1)S(1)}, u32[]{:S(2)}, u32[]{:S(2)}) collective-permute-start(bf16[48,768]{1,0:T(8,128)(2,1)S(1)} %get-tuple-element.47), channel_id=1, source_target_pairs={{0,8},{2,10},{4,12},{6,14},{8,0},{10,2},{12,4},{14,6},{16,24},{18,... | collective-permute-start | bytes 221192 | tf_op jit(solution)/shard_map/ppermute | solution.py:44
  82.4 13.4 %collective-permute-start.29 = (bf16[48,768]{1,0:T(8,128)(2,1)S(1)}, bf16[48,768]{1,0:T(8,128)(2,1)S(1)}, u32[]{:S(2)}, u32[]{:S(2)}) collective-permute-start(bf16[48,768]{1,0:T(8,128)(2,1)S(1)} %get-tuple-element.61), channel_id=1, source_target_pairs={{0,28},{2,30},{4,24},{6,26},{8,20},{10,22},{12,16},{14,18},{16,12}... | collective-permute-start | bytes 221192 | tf_op jit(solution)/shard_map/ppermute | solution.py:44
  83.8 11.9 %collective-permute-start.28 = (bf16[48,768]{1,0:T(8,128)(2,1)S(1)}, bf16[48,768]{1,0:T(8,128)(2,1)S(1)}, u32[]{:S(2)}, u32[]{:S(2)}) collective-permute-start(bf16[48,768]{1,0:T(8,128)(2,1)S(1)} %get-tuple-element.60), channel_id=1, source_target_pairs={{0,30},{2,28},{4,26},{6,24},{8,22},{10,20},{12,18},{14,16},{16,14}... | collective-permute-start | bytes 221192 | tf_op jit(solution)/shard_map/ppermute | solution.py:44
  84.8 10.9 %collective-permute-start.27 = (bf16[48,768]{1,0:T(8,128)(2,1)S(1)}, bf16[48,768]{1,0:T(8,128)(2,1)S(1)}, u32[]{:S(2)}, u32[]{:S(2)}) collective-permute-start(bf16[48,768]{1,0:T(8,128)(2,1)S(1)} %get-tuple-element.59), channel_id=1, source_target_pairs={{0,10},{2,8},{4,14},{6,12},{8,2},{10,0},{12,6},{14,4},{16,26},{18,... | collective-permute-start | bytes 221192 | tf_op jit(solution)/shard_map/ppermute | solution.py:44
  86.8 8.9 %collective-permute-start.26 = (bf16[48,768]{1,0:T(8,128)(2,1)S(1)}, bf16[48,768]{1,0:T(8,128)(2,1)S(1)}, u32[]{:S(2)}, u32[]{:S(2)}) collective-permute-start(bf16[48,768]{1,0:T(8,128)(2,1)S(1)} %get-tuple-element.58), channel_id=1, source_target_pairs={{0,12},{2,14},{4,8},{6,10},{8,4},{10,6},{12,0},{14,2},{16,28},{18,... | collective-permute-start | bytes 221192 | tf_op jit(solution)/shard_map/ppermute | solution.py:44
  89.5 6.2 %collective-permute-start.25 = (bf16[48,768]{1,0:T(8,128)(2,1)S(1)}, bf16[48,768]{1,0:T(8,128)(2,1)S(1)}, u32[]{:S(2)}, u32[]{:S(2)}) collective-permute-start(bf16[48,768]{1,0:T(8,128)(2,1)S(1)} %get-tuple-element.57), channel_id=1, source_target_pairs={{0,14},{2,12},{4,10},{6,8},{8,6},{10,4},{12,2},{14,0},{16,30},{18,... | collective-permute-start | bytes 221192 | tf_op jit(solution)/shard_map/ppermute | solution.py:44
  95.8 6.7 %copy-start.7 = (bf16[384,384]{1,0:T(8,128)(2,1)S(1)}, bf16[384,384]{1,0:T(8,128)(2,1)}, u32[]{:S(2)}) copy-start(bf16[384,384]{1,0:T(8,128)(2,1)} %copy-done.6) | copy-start | bytes 884740
  95.8 6.7 %copy-start.9 = (bf16[384,384]{1,0:T(8,128)(2,1)S(1)}, bf16[384,384]{1,0:T(8,128)(2,1)}, u32[]{:S(2)}) copy-start(bf16[384,384]{1,0:T(8,128)(2,1)} %copy-done.8) | copy-start | bytes 884740
  95.8 6.7 %copy-start.11 = (bf16[384,384]{1,0:T(8,128)(2,1)S(1)}, bf16[384,384]{1,0:T(8,128)(2,1)}, u32[]{:S(2)}) copy-start(bf16[384,384]{1,0:T(8,128)(2,1)} %copy-done.10) | copy-start | bytes 884740
  95.8 6.6 %copy-start.13 = (bf16[384,384]{1,0:T(8,128)(2,1)S(1)}, bf16[384,384]{1,0:T(8,128)(2,1)}, u32[]{:S(2)}) copy-start(bf16[384,384]{1,0:T(8,128)(2,1)} %copy-done.12) | copy-start | bytes 884740
  97.8 11.8 %all-to-all-start = ((f32[32,1,16]{2,1,0:T(1,128)}), f32[32,1,16]{2,1,0:T(1,128)S(1)}, u32[]{:S(2)}, u32[]{:S(2)}) async-start(f32[32,1,16]{2,1,0:T(1,128)} %bitcast.53), calls=%async_computation | async-start | bytes 32768 | tf_op jit(solution)/shard_map/all_to_all | solution.py:346

commit v12 on v9

--- a/solution.py
+++ b/solution.py
@@ -66,41 +66,39 @@
     return back_re * fore_re + back_im * fore_im, back_re * fore_im - back_im * fore_re
 
 
-def products_kernel(rows, fore_hbm, back_hbm, send_a, keep_a, send_b, keep_b, fore_ref, back_ref, sems):
-    me = lax.axis_index("modes")
-    low, high = me % 2 == 1, me // 2 % 2 == 1
-    grid_size = fore_ref.shape[1] // 2
+def products_kernel(rows, part, fore_hbm, back_hbm, send, keep, fore_ref, back_ref, sems):
+    upper = lax.axis_index("modes") // (part + 1) % 2 == 1
+    grid_size = fore_ref.shape[1]
     half = grid_size // 2
     pair = 2 * rows
     groups = fore_ref.shape[0] // (4 * rows)
     copies = []
     for group in range(groups):
         at = pl.ds(group * 4 * rows, 4 * rows)
-        for k, (hbm, ref) in enumerate(((fore_hbm, fore_ref), (back_hbm, back_ref))):
-            copies.append(pltpu.make_async_copy(hbm.at[at], ref.at[at], sems.at[2 * group + k]))
+        for k in range(2):
+            come, into = pl.ds(k * grid_size + part * half, half), pl.ds(k * half, half)
+            for hbm, ref in ((fore_hbm, fore_ref), (back_hbm, back_ref)):
+                sem = sems.at[len(copies)]
+                copies.append(pltpu.make_async_copy(hbm.at[at, come], ref.at[at, into], sem))
     for copy in copies:
         copy.start()
     for group in range(groups):
-        copies[2 * group].wait()
-        copies[2 * group + 1].wait()
+        for copy in copies[4 * group : 4 * group + 4]:
+            copy.wait()
         at = pl.ds(group * 4 * rows, 4 * rows)
         out = pl.ds(group * pair, pair)
-        for part in range(2):
-            cols = [pl.ds(part * half, half), pl.ds(grid_size + part * half, half)]
-            fore_re, fore_im = [fore_ref[at, c].astype(f32) for c in cols]
-            back_re, back_im = [back_ref[at, c].astype(f32) for c in cols]
-            values = (back_re * fore_re + back_im * fore_im, back_re * fore_im - back_im * fore_re)
-            for k, v in enumerate(values):
-                into = pl.ds(k * half, half)
-                if part == 0:
-                    first = jnp.concatenate([v[:rows], v[pair : pair + rows]], 0)
-                    second = jnp.concatenate([v[rows:pair], v[pair + rows :]], 0)
-                    send_a[out, into] = jnp.where(low, first, second).astype(bf16)
-                    keep_a[out, into] = jnp.where(low, second, first)
-                else:
-                    first, second = v[:pair], v[pair:]
-                    send_b[out, into] = jnp.where(high, first, second).astype(bf16)
-                    keep_b[out, into] = jnp.where(high, second, first)
+        fore_re, fore_im = fore_ref[at, :half].astype(f32), fore_ref[at, half:].astype(f32)
+        back_re, back_im = back_ref[at, :half].astype(f32), back_ref[at, half:].astype(f32)
+        values = (back_re * fore_re + back_im * fore_im, back_re * fore_im - back_im * fore_re)
+        for k, v in enumerate(values):
+            into = pl.ds(k * half, half)
+            if part == 0:
+                first = jnp.concatenate([v[:rows], v[pair : pair + rows]], 0)
+                second = jnp.concatenate([v[rows:pair], v[pair + rows :]], 0)
+            else:
+                first, second = v[:pair], v[pair:]
+            send[out, into] = jnp.where(upper, first, second).astype(bf16)
+            keep[out, into] = jnp.where(upper, second, first)
 
 
 def times(one, two):
@@ -148,7 +146,7 @@
 
 
 def coupling_kernel(block_rows, by_xor, first, fields_ref, targets_ref, *rest):
-    out_ref = rest[-1]
+    out_ref, held = rest[-2:]
     modes = out_ref.shape[1]
     product = lax.dot_general(
         fields_ref[...], targets_ref[...], (((1,), (1,)), ((), ())), preferred_element_type=f32
@@ -167,23 +165,23 @@
         product = jnp.sum(product.reshape(left // block_rows, block_rows, right), 1)
     else:
         product = exactly(groups(left), product, ((1,), (0,)))
-    product = exactly(product, groups(right), ((1,), (1,)))
-    by_re, by_im = product[:, :modes], product[:, modes:]
-    sources = left // block_rows
-    mode = lax.broadcasted_iota(jnp.int32, (modes, sources), 0)
+    sources = left // block_rows // 2
+    product = product.reshape(sources, 2, right)
+    real, imag = product[:, 0], product[:, 1]
+    right = right // 2
+    both = jnp.concatenate(
+        [real[:, :right] + imag[:, right:], imag[:, :right] - real[:, right:]], 0
+    )
+    held[...] = exactly(both, groups(right), ((1,), (1,)))
+    out_ref[...] = rest[0][...] if len(rest) > 2 else jnp.zeros_like(out_ref)
+    me, there = lax.axis_index("modes"), modes // 2
     if by_xor:
-        mode = mode ^ lax.axis_index("modes")
-        mode = mode % (modes // 2) * 2 + mode // (modes // 2)
-    from_row = lax.broadcasted_iota(jnp.int32, (modes, sources), 1) + 2 * first
-    real = jnp.where(from_row == 2 * mode, 1.0, 0.0).astype(f32)
-    imag = jnp.where(from_row == 2 * mode + 1, 1.0, 0.0).astype(f32)
-    inner = ((1,), (0,))
-    total_re = exactly(real, by_re, inner) + exactly(imag, by_im, inner)
-    total_im = exactly(imag, by_re, inner) - exactly(real, by_im, inner)
-    if len(rest) > 1:
-        total_re, total_im = total_re + rest[0][:modes], total_im + rest[0][modes:]
-    out_ref[:modes] = total_re
-    out_ref[modes:] = total_im
+        for at in range(sources):
+            mode = me ^ ((first + at) // 2 + (first + at) % 2 * there)
+            out_ref[pl.ds(mode, 1)] = held[pl.ds(at, 1)]
+            out_ref[pl.ds(modes + mode, 1)] = held[pl.ds(sources + at, 1)]
+    else:
+        out_ref[...] = held[...]
 
 
 def kernel_call(kernel, shape, dtype, flops, operands, grant=12, **more):
@@ -221,17 +219,19 @@
     orders = [first, [1, 0] + first[2:]]
     kernel_first = block_rows % 8 == 0 and local_rows % (4 * block_rows) == 0
     if kernel_first:
-        halves = kernel_call(
-            lambda *refs: products_kernel(block_rows, *refs),
-            [(local_rows // 2, grid_size)] * 4,
-            [bf16, f32, bf16, f32],
-            8 * local_rows * double_width,
-            (forward[0], backward[0]),
-            grant=52,
-            in_specs=[pl.BlockSpec(memory_space=pltpu.HBM)] * 2,
-            scratch_shapes=[pltpu.VMEM((local_rows, double_width), bf16)] * 2
-            + [pltpu.SemaphoreType.DMA((2 * local_rows // (4 * block_rows),))],
-        )
+        halves = []
+        for part in range(2):
+            halves += kernel_call(
+                lambda *refs: products_kernel(block_rows, part, *refs),
+                [(local_rows // 2, grid_size)] * 2,
+                [bf16, f32],
+                4 * local_rows * double_width,
+                (forward[0], backward[0]),
+                grant=52,
+                in_specs=[pl.BlockSpec(memory_space=pltpu.HBM)] * 2,
+                scratch_shapes=[pltpu.VMEM((local_rows, grid_size), bf16)] * 2
+                + [pltpu.SemaphoreType.DMA((local_rows // block_rows,))],
+            )
     else:
         product = product_of(forward[0], backward[0])
     kept = []
@@ -341,6 +341,7 @@
                 f32,
                 2 * rows.shape[0] * 2 * local_rows * grid_size,
                 (rows, seen) if term is None else (rows, seen, term),
+                scratch_shapes=[pltpu.VMEM((rows.shape[0] // block_rows, mode_total), f32)],
             )
             at += len(group)
     pieces = lax.all_to_all(term, ("modes", "rows"), 0, 0, tiled=True)

time: 106 us -> 109 us (1.028)
  waiting for transfers between devices: 35.5 us -> 40.7 us
  starting transfers between devices: 51.1 us -> 47.9 us
    ppermute x29, waiting for transfers between devices: 28.9 us -> 34 us  [exchange(): lax.ppermute(values, 'modes', [(i, i ^ offset) for i in range(count)])]
    ppermute x29, starting transfers between devices: 47.5 us -> 44.5 us  [exchange(): lax.ppermute(values, 'modes', [(i, i ^ offset) for i in range(count)])]
    pallas_call x7 -> x8, Pallas kernels: 12.1 us -> 12.8 us  [kernel_call(): pl.pallas_call(kernel, out_shape=out_shape, compiler_params=pltpu.Compile...]
  transfers between devices with their start and end apart: 31 -> 31, of which waited for: 14 -> 16; matrix products, arithmetic and copies ran while one was open for 2% -> 2% of each run, Pallas kernels for 7% -> 8%
where the time goes in v12:
time: 109 us; the launch traced here: 108 us
  starting transfers between devices  47.9 us (44%)
  waiting for transfers between devices  40.7 us (37%)
  Pallas kernels  12.8 us (12%)
  other arithmetic  3.4 us (3%)
  local copies, waits for them, and re-layouts  2.17 us (2%)
  between operations  1.23 us (1%)
    ppermute x29, starting transfers between devices, exchange(): lax.ppermute(values, 'modes', [(i, i ^ offset) for i in range(count)])  44.5 us
    ppermute x29, waiting for transfers between devices, exchange(): lax.ppermute(values, 'modes', [(i, i ^ offset) for i in range(count)])  34 us
    pallas_call x8, Pallas kernels, kernel_call(): pl.pallas_call(kernel, out_shape=out_shape, compiler_params=pltpu.Compile...  12.8 us
    all_to_all x1, waiting for transfers between devices, local(): pieces = lax.all_to_all(term, ('modes', 'rows'), 0, 0, tiled=True)  6 us
    all_to_all x1, starting transfers between devices, local(): pieces = lax.all_to_all(term, ('modes', 'rows'), 0, 0, tiled=True)  3.33 us
  transfers between devices with their start and end apart: 31, of which 16 were waited for; matrix products, arithmetic and copies ran while one was open for 2% of the time, Pallas kernels for 8%

profile of v12, /device:TPU:0, one launch (start us, length us, event | category | flops | bytes accessed | tf_op | source)
XLA Modules:
  0.0 108.2 jit_solution(14018252047052671670)
XLA Ops:
  0.6 1.6 %shard_map.95 = (bf16[192,768]{1,0:T(8,128)(2,1)S(1)}, f32[192,768]{1,0:T(8,128)S(1)}) custom-call(bf16[384,1536]{1,0:T(8,128)(2,1)} %bitcast.100, bf16[384,1536]{1,0:T(8,128)(2,1)} %bitcast.102), custom_call_target="tpu_custom_call" | custom-call | flops 2359296 | bytes 4194304 | tf_op jit(solution)/shard_map/pallas_call | solution.py:195
  2.2 3.0 %collective-permute-start.2 = (bf16[4,2,24,768]{3,2,0,1:T(8,128)(2,1)S(1)}, bf16[4,2,24,768]{3,2,0,1:T(8,128)(2,1)S(1)}, u32[]{:S(2)}, u32[]{:S(2)}) collective-permute-start(bf16[4,2,24,768]{3,2,0,1:T(8,128)(2,1)S(1)} %copy.19), channel_id=1, source_target_pairs={{0,4},{2,6},{4,0},{6,2},{8,12},{10,14},{12,8},{14,10},{16,20},{18,... | collective-permute-start | bytes 884744 | tf_op jit(solution)/shard_map/ppermute | solution.py:35
  5.3 1.6 %shard_map.94 = (bf16[192,768]{1,0:T(8,128)(2,1)S(1)}, f32[192,768]{1,0:T(8,128)S(1)}) custom-call(bf16[384,1536]{1,0:T(8,128)(2,1)} %bitcast.101, bf16[384,1536]{1,0:T(8,128)(2,1)} %bitcast.103), custom_call_target="tpu_custom_call" | custom-call | flops 2359296 | bytes 4194304 | tf_op jit(solution)/shard_map/pallas_call | solution.py:195
  6.9 1.6 %collective-permute-start = (bf16[4,2,24,768]{3,2,0,1:T(8,128)(2,1)S(1)}, bf16[4,2,24,768]{3,2,0,1:T(8,128)(2,1)S(1)}, u32[]{:S(2)}, u32[]{:S(2)}) collective-permute-start(bf16[4,2,24,768]{3,2,0,1:T(8,128)(2,1)S(1)} %copy.17), channel_id=1, source_target_pairs={{0,2},{2,0},{4,6},{6,4},{8,10},{10,8},{12,14},{14,12},{16,18},{18,... | collective-permute-start | bytes 884744 | tf_op jit(solution)/shard_map/ppermute | solution.py:35
  8.4 3.9 %collective-permute-done.2 = bf16[4,2,24,768]{3,2,0,1:T(8,128)(2,1)S(1)} collective-permute-done((bf16[4,2,24,768]{3,2,0,1:T(8,128)(2,1)S(1)}, bf16[4,2,24,768]{3,2,0,1:T(8,128)(2,1)S(1)}, u32[]{:S(2)}, u32[]{:S(2)}) %collective-permute-start.2) | collective-permute-done | bytes 294944 | tf_op jit(solution)/shard_map/ppermute | solution.py:35
  12.4 1.8 %collective-permute-start.3 = (bf16[4,24,768]{2,1,0:T(8,128)(2,1)S(1)}, bf16[4,24,768]{2,1,0:T(8,128)(2,1)S(1)}, u32[]{:S(2)}, u32[]{:S(2)}) collective-permute-start(bf16[4,24,768]{2,1,0:T(8,128)(2,1)S(1)} %fusion.5), channel_id=1, source_target_pairs={{0,2},{2,0},{4,6},{6,4},{8,10},{10,8},{12,14},{14,12},{16,18},{18,... | collective-permute-start | bytes 442376 | tf_op jit(solution)/shard_map/ppermute | solution.py:35
  14.1 2.3 %collective-permute-done = bf16[4,2,24,768]{3,2,0,1:T(8,128)(2,1)S(1)} collective-permute-done((bf16[4,2,24,768]{3,2,0,1:T(8,128)(2,1)S(1)}, bf16[4,2,24,768]{3,2,0,1:T(8,128)(2,1)S(1)}, u32[]{:S(2)}, u32[]{:S(2)}) %collective-permute-start) | collective-permute-done | bytes 294944 | tf_op jit(solution)/shard_map/ppermute | solution.py:35
  16.6 2.0 %collective-permute-done.3 = bf16[4,24,768]{2,1,0:T(8,128)(2,1)S(1)} collective-permute-done((bf16[4,24,768]{2,1,0:T(8,128)(2,1)S(1)}, bf16[4,24,768]{2,1,0:T(8,128)(2,1)S(1)}, u32[]{:S(2)}, u32[]{:S(2)}) %collective-permute-start.3) | collective-permute-done | bytes 147488 | tf_op jit(solution)/shard_map/ppermute | solution.py:35
  18.6 3.1 %collective-permute-done.1 = bf16[4,24,768]{2,1,0:T(8,128)(2,1)S(1)} collective-permute-done((bf16[4,24,768]{2,1,0:T(8,128)(2,1)S(1)}, bf16[4,24,768]{2,1,0:T(8,128)(2,1)S(1)}, u32[]{:S(2)}, u32[]{:S(2)}) %collective-permute-start.1) | collective-permute-done | bytes 147488 | tf_op jit(solution)/shard_map/ppermute | solution.py:35
  21.8 1.7 %collective-permute-start.4 = (bf16[24,1536]{1,0:T(8,128)(2,1)S(1)}, bf16[24,1536]{1,0:T(8,128)(2,1)S(1)}, u32[]{:S(2)}, u32[]{:S(2)}) collective-permute-start(bf16[24,1536]{1,0:T(8,128)(2,1)S(1)} %get-tuple-element.84), channel_id=1, source_target_pairs={{0,8},{2,10},{4,12},{6,14},{8,0},{10,2},{12,4},{14,6},{16,24},{18,... | collective-permute-start | bytes 221192 | tf_op jit(solution)/shard_map/ppermute | solution.py:35
  23.5 2.6 %collective-permute-start.5 = (bf16[24,1536]{1,0:T(8,128)(2,1)S(1)}, bf16[24,1536]{1,0:T(8,128)(2,1)S(1)}, u32[]{:S(2)}, u32[]{:S(2)}) collective-permute-start(bf16[24,1536]{1,0:T(8,128)(2,1)S(1)} %get-tuple-element.85), channel_id=1, source_target_pairs={{0,16},{2,18},{4,20},{6,22},{8,24},{10,26},{12,28},{14,30},{16,0},... | collective-permute-start | bytes 221192 | tf_op jit(solution)/shard_map/ppermute | solution.py:35
  26.3 3.6 %collective-permute-done.5 = bf16[24,1536]{1,0:T(8,128)(2,1)S(1)} collective-permute-done((bf16[24,1536]{1,0:T(8,128)(2,1)S(1)}, bf16[24,1536]{1,0:T(8,128)(2,1)S(1)}, u32[]{:S(2)}, u32[]{:S(2)}) %collective-permute-start.5) | collective-permute-done | bytes 73760 | tf_op jit(solution)/shard_map/ppermute | solution.py:35
  29.8 3.1 %collective-permute-done.6 = bf16[24,1536]{1,0:T(8,128)(2,1)S(1)} collective-permute-done((bf16[24,1536]{1,0:T(8,128)(2,1)S(1)}, bf16[24,1536]{1,0:T(8,128)(2,1)S(1)}, u32[]{:S(2)}, u32[]{:S(2)}) %collective-permute-start.6) | collective-permute-done | bytes 73760 | tf_op jit(solution)/shard_map/ppermute | solution.py:35
  33.4 1.5 %collective-permute-start.8 = (bf16[24,1536]{1,0:T(8,128)(2,1)S(1)}, bf16[24,1536]{1,0:T(8,128)(2,1)S(1)}, u32[]{:S(2)}, u32[]{:S(2)}) collective-permute-start(bf16[24,1536]{1,0:T(8,128)(2,1)S(1)} %pad_maximum_fusion.11), channel_id=1, source_target_pairs={{0,16},{2,18},{4,20},{6,22},{8,24},{10,26},{12,28},{14,30},{16,0},... | collective-permute-start | bytes 221192 | tf_op jit(solution)/shard_map/ppermute | solution.py:35
  35.0 2.5 %collective-permute-start.7 = (bf16[24,1536]{1,0:T(8,128)(2,1)S(1)}, bf16[24,1536]{1,0:T(8,128)(2,1)S(1)}, u32[]{:S(2)}, u32[]{:S(2)}) collective-permute-start(bf16[24,1536]{1,0:T(8,128)(2,1)S(1)} %pad_maximum_fusion.11), channel_id=1, source_target_pairs={{0,8},{2,10},{4,12},{6,14},{8,0},{10,2},{12,4},{14,6},{16,24},{18,... | collective-permute-start | bytes 221192 | tf_op jit(solution)/shard_map/ppermute | solution.py:35
  37.5 1.9 %collective-permute-done.9 = bf16[24,1536]{1,0:T(8,128)(2,1)S(1)} collective-permute-done((bf16[24,1536]{1,0:T(8,128)(2,1)S(1)}, bf16[24,1536]{1,0:T(8,128)(2,1)S(1)}, u32[]{:S(2)}, u32[]{:S(2)}) %collective-permute-start.9) | collective-permute-done | bytes 73760 | tf_op jit(solution)/shard_map/ppermute | solution.py:35
  39.4 0.8 collective-permute-done.8
  40.4 1.6 %collective-permute-start.12 = (bf16[4,24,768]{2,1,0:T(8,128)(2,1)S(1)}, bf16[4,24,768]{2,1,0:T(8,128)(2,1)S(1)}, u32[]{:S(2)}, u32[]{:S(2)}) collective-permute-start(bf16[4,24,768]{2,1,0:T(8,128)(2,1)S(1)} %get-tuple-element.89), channel_id=1, source_target_pairs={{0,2},{2,0},{4,6},{6,4},{8,10},{10,8},{12,14},{14,12},{16,18},{18,... | collective-permute-start | bytes 442376 | tf_op jit(solution)/shard_map/ppermute | solution.py:35
  42.4 4.8 %collective-permute-done.12 = bf16[4,24,768]{2,1,0:T(8,128)(2,1)S(1)} collective-permute-done((bf16[4,24,768]{2,1,0:T(8,128)(2,1)S(1)}, bf16[4,24,768]{2,1,0:T(8,128)(2,1)S(1)}, u32[]{:S(2)}, u32[]{:S(2)}) %collective-permute-start.12) | collective-permute-done | bytes 147488 | tf_op jit(solution)/shard_map/ppermute | solution.py:35
  47.6 1.5 %collective-permute-start.11 = (bf16[4,2,24,768]{3,2,1,0:T(8,128)(2,1)S(1)}, bf16[4,2,24,768]{3,2,1,0:T(8,128)(2,1)S(1)}, u32[]{:S(2)}, u32[]{:S(2)}) collective-permute-start(bf16[4,2,24,768]{3,2,1,0:T(8,128)(2,1)S(1)} %reverse_select_fusion.3), channel_id=1, source_target_pairs={{0,2},{2,0},{4,6},{6,4},{8,10},{10,8},{12,14},{14,12},{16,18},{18,... | collective-permute-start | bytes 884744 | tf_op jit(solution)/shard_map/ppermute | solution.py:35
  49.1 4.9 %collective-permute-done.13 = bf16[4,2,24,768]{3,2,0,1:T(8,128)(2,1)S(1)} collective-permute-done((bf16[4,2,24,768]{3,2,0,1:T(8,128)(2,1)S(1)}, bf16[4,2,24,768]{3,2,0,1:T(8,128)(2,1)S(1)}, u32[]{:S(2)}, u32[]{:S(2)}) %collective-permute-start.13) | collective-permute-done | bytes 294944 | tf_op jit(solution)/shard_map/ppermute | solution.py:35
  54.8 0.4 fusion.1
  56.0 1.0 copy-done.1
  57.0 1.1 shard_map.96.own_ref
  58.1 0.6 collective-permute-done.14.shaped_ref
  58.7 1.1 %shard_map.97.refs_0_ = bf16[768,768]{1,0:T(8,128)(2,1)S(1)} custom-call(bf16[768,768]{1,0:T(8,128)(2,1)S(1)} %copy-done, bf16[768,768]{1,0:T(8,128)(2,1)S(1)} %collective-permute-done.14.shaped_ref, f32[768,768]{1,0:T(8,128)S(1)} %shard_map.96.own_ref), custom_call_target="tpu_custom_call" | custom-call | flops 905969664 | bytes 4194304 | tf_op jit(solution)/shard_map/pallas_call | solution.py:195
  60.0 1.3 %collective-permute-start.27 = (bf16[48,768]{1,0:T(8,128)(2,1)S(1)}, bf16[48,768]{1,0:T(8,128)(2,1)S(1)}, u32[]{:S(2)}, u32[]{:S(2)}) collective-permute-start(bf16[48,768]{1,0:T(8,128)(2,1)S(1)} %get-tuple-element.66), channel_id=1, source_target_pairs={{0,16},{2,18},{4,20},{6,22},{8,24},{10,26},{12,28},{14,30},{16,0},... | collective-permute-start | bytes 221192 | tf_op jit(solution)/shard_map/ppermute | solution.py:35
  61.3 3.0 %collective-permute-start.24 = (bf16[48,768]{1,0:T(8,128)(2,1)S(1)}, bf16[48,768]{1,0:T(8,128)(2,1)S(1)}, u32[]{:S(2)}, u32[]{:S(2)}) collective-permute-start(bf16[48,768]{1,0:T(8,128)(2,1)S(1)} %get-tuple-element.68), channel_id=1, source_target_pairs={{0,20},{2,22},{4,16},{6,18},{8,28},{10,30},{12,24},{14,26},{16,4},... | collective-permute-start | bytes 221192 | tf_op jit(solution)/shard_map/ppermute | solution.py:35
  64.4 2.1 %collective-permute-start.18 = (bf16[48,768]{1,0:T(8,128)(2,1)S(1)}, bf16[48,768]{1,0:T(8,128)(2,1)S(1)}, u32[]{:S(2)}, u32[]{:S(2)}) collective-permute-start(bf16[48,768]{1,0:T(8,128)(2,1)S(1)} %get-tuple-element.74), channel_id=1, source_target_pairs={{0,18},{2,16},{4,22},{6,20},{8,26},{10,24},{12,30},{14,28},{16,2},... | collective-permute-start | bytes 221192 | tf_op jit(solution)/shard_map/ppermute | solution.py:35
  66.6 0.6 collective-permute-start.15
  67.1 3.0 %shard_map.98 = bf16[384,1536]{1,0:T(8,128)(2,1)} custom-call(bf16[768,768]{1,0:T(8,128)(2,1)S(1)} %shard_map.97.refs_0_, bf16[768,768]{1,0:T(8,128)(2,1)S(1)} %copy-done.4, bf16[768,768]{1,0:T(8,128)(2,1)S(1)} %copy-done.3), custom_call_target="tpu_custom_call" | custom-call | flops 1811939328 | bytes 4194304 | tf_op jit(solution)/shard_map/pallas_call | solution.py:195
  70.2 2.0 %shard_map.99.refs_1_ = bf16[768,768]{1,0:T(8,128)(2,1)S(1)} custom-call(bf16[768,768]{1,0:T(8,128)(2,1)S(1)} %bitcast.99, bf16[768,768]{1,0:T(8,128)(2,1)S(1)} %copy-done.4, bf16[768,768]{1,0:T(8,128)(2,1)S(1)} %copy-done.3), custom_call_target="tpu_custom_call" | custom-call | flops 1811939328 | bytes 4194304 | tf_op jit(solution)/shard_map/pallas_call | solution.py:195
  72.2 3.0 %collective-permute-start.28 = (bf16[48,768]{1,0:T(8,128)(2,1)S(1)}, bf16[48,768]{1,0:T(8,128)(2,1)S(1)}, u32[]{:S(2)}, u32[]{:S(2)}) collective-permute-start(bf16[48,768]{1,0:T(8,128)(2,1)S(1)} %get-tuple-element.56), channel_id=1, source_target_pairs={{0,6},{2,4},{4,2},{6,0},{8,14},{10,12},{12,10},{14,8},{16,22},{18,... | collective-permute-start | bytes 221192 | tf_op jit(solution)/shard_map/ppermute | solution.py:35
  75.1 2.0 %collective-permute-start.25 = (bf16[48,768]{1,0:T(8,128)(2,1)S(1)}, bf16[48,768]{1,0:T(8,128)(2,1)S(1)}, u32[]{:S(2)}, u32[]{:S(2)}) collective-permute-start(bf16[48,768]{1,0:T(8,128)(2,1)S(1)} %get-tuple-element.48), channel_id=1, source_target_pairs={{0,10},{2,8},{4,14},{6,12},{8,2},{10,0},{12,6},{14,4},{16,26},{18,... | collective-permute-start | bytes 221192 | tf_op jit(solution)/shard_map/ppermute | solution.py:35
  77.1 1.1 collective-permute-start.22
  78.2 3.7 %collective-permute-start.16 = (bf16[48,768]{1,0:T(8,128)(2,1)S(1)}, bf16[48,768]{1,0:T(8,128)(2,1)S(1)}, u32[]{:S(2)}, u32[]{:S(2)}) collective-permute-start(bf16[48,768]{1,0:T(8,128)(2,1)S(1)} %get-tuple-element.42), channel_id=1, source_target_pairs={{0,22},{2,20},{4,18},{6,16},{8,30},{10,28},{12,26},{14,24},{16,6},... | collective-permute-start | bytes 221192 | tf_op jit(solution)/shard_map/ppermute | solution.py:35
  82.0 1.2 %collective-permute-start.29 = (bf16[48,768]{1,0:T(8,128)(2,1)S(1)}, bf16[48,768]{1,0:T(8,128)(2,1)S(1)}, u32[]{:S(2)}, u32[]{:S(2)}) collective-permute-start(bf16[48,768]{1,0:T(8,128)(2,1)S(1)} %get-tuple-element.62), channel_id=1, source_target_pairs={{0,26},{2,24},{4,30},{6,28},{8,18},{10,16},{12,22},{14,20},{16,10}... | collective-permute-start | bytes 221192 | tf_op jit(solution)/shard_map/ppermute | solution.py:35
  83.2 5.0 %collective-permute-start.26 = (bf16[48,768]{1,0:T(8,128)(2,1)S(1)}, bf16[48,768]{1,0:T(8,128)(2,1)S(1)}, u32[]{:S(2)}, u32[]{:S(2)}) collective-permute-start(bf16[48,768]{1,0:T(8,128)(2,1)S(1)} %get-tuple-element.49), channel_id=1, source_target_pairs={{0,30},{2,28},{4,26},{6,24},{8,22},{10,20},{12,18},{14,16},{16,14}... | collective-permute-start | bytes 221192 | tf_op jit(solution)/shard_map/ppermute | solution.py:35
  88.2 0.6 collective-permute-start.20
  88.8 2.4 %collective-permute-start.17 = (bf16[48,768]{1,0:T(8,128)(2,1)S(1)}, bf16[48,768]{1,0:T(8,128)(2,1)S(1)}, u32[]{:S(2)}, u32[]{:S(2)}) collective-permute-start(bf16[48,768]{1,0:T(8,128)(2,1)S(1)} %get-tuple-element.43), channel_id=1, source_target_pairs={{0,12},{2,14},{4,8},{6,10},{8,4},{10,6},{12,0},{14,2},{16,28},{18,... | collective-permute-start | bytes 221192 | tf_op jit(solution)/shard_map/ppermute | solution.py:35
  91.3 1.2 %shard_map.100.refs_2_ = f32[32,16]{1,0:T(8,128)S(1)} custom-call(bf16[576,768]{1,0:T(8,128)(2,1)S(1)} %constant_dynamic-update-slice_fusion.refs_0_, bf16[768,768]{1,0:T(8,128)(2,1)S(1)} %shard_map.99.refs_1_), custom_call_target="tpu_custom_call" | custom-call | flops 679477248 | bytes 4194304 | tf_op jit(solution)/shard_map/pallas_call | solution.py:195
  92.5 2.5 %collective-permute-done.23 = bf16[48,768]{1,0:T(8,128)(2,1)S(1)} collective-permute-done((bf16[48,768]{1,0:T(8,128)(2,1)S(1)}, bf16[48,768]{1,0:T(8,128)(2,1)S(1)}, u32[]{:S(2)}, u32[]{:S(2)}) %collective-permute-start.23) | collective-permute-done | bytes 73760 | tf_op jit(solution)/shard_map/ppermute | solution.py:35
  95.0 0.8 collective-permute-done.20
  95.8 1.4 %shard_map.101 = f32[32,16]{1,0:T(8,128)} custom-call(bf16[192,768]{1,0:T(8,128)(2,1)S(1)} %pad_maximum_fusion.10.refs_0_, bf16[768,768]{1,0:T(8,128)(2,1)S(1)} %shard_map.99.refs_1_, f32[32,16]{1,0:T(8,128)S(1)} %shard_map.100.refs_2_), custom_call_target="tpu_custom_call" | custom-call | flops 226492416 | bytes 4194304 | tf_op jit(solution)/shard_map/pallas_call | solution.py:195
  97.2 3.3 %all-to-all-start = ((f32[32,1,16]{2,1,0:T(1,128)}), f32[32,1,16]{2,1,0:T(1,128)S(1)}, u32[]{:S(2)}, u32[]{:S(2)}) async-start(f32[32,1,16]{2,1,0:T(1,128)} %bitcast.53), calls=%async_computation | async-start | bytes 32768 | tf_op jit(solution)/shard_map/all_to_all | solution.py:347
  100.6 1.1 %pad_maximum_fusion = bf16[384,1536]{1,0:T(8,128)(2,1)} fusion(bf16[384,384]{1,0:T(8,128)(2,1)S(1)} %copy-done.11, bf16[384,384]{1,0:T(8,128)(2,1)S(1)} %copy-done.9, bf16[384,384]{1,0:T(8,128)(2,1)S(1)} %copy-done.13, bf16[384,384]{1,0:T(8,128)(2,1)S(1)} %copy-done.7), kind=kLoop, calls=%fused_computation.8 | loop fusion | flops 4718592 | bytes 2359296 | tf_op jit(solution)/shard_map/concatenate | solution.py:280
  101.7 6.0 %all-to-all-done = f32[32,1,16]{2,1,0:T(1,128)S(1)} async-done(((f32[32,1,16]{2,1,0:T(1,128)}), f32[32,1,16]{2,1,0:T(1,128)S(1)}, u32[]{:S(2)}, u32[]{:S(2)}) %all-to-all-start) | async-done | bytes 2080 | tf_op jit(solution)/shard_map/all_to_all | solution.py:347
  107.7 0.6 reduce_sum.9
  (97 shorter events, 3.6 us)
Async XLA Ops:
  2.2 10.0 %collective-permute-start.2 = (bf16[4,2,24,768]{3,2,0,1:T(8,128)(2,1)S(1)}, bf16[4,2,24,768]{3,2,0,1:T(8,128)(2,1)S(1)}, u32[]{:S(2)}, u32[]{:S(2)}) collective-permute-start(bf16[4,2,24,768]{3,2,0,1:T(8,128)(2,1)S(1)} %copy.19), channel_id=1, source_target_pairs={{0,4},{2,6},{4,0},{6,2},{8,12},{10,14},{12,8},{14,10},{16,20},{18,... | collective-permute-start | bytes 884744 | tf_op jit(solution)/shard_map/ppermute | solution.py:35
  6.9 9.6 %collective-permute-start = (bf16[4,2,24,768]{3,2,0,1:T(8,128)(2,1)S(1)}, bf16[4,2,24,768]{3,2,0,1:T(8,128)(2,1)S(1)}, u32[]{:S(2)}, u32[]{:S(2)}) collective-permute-start(bf16[4,2,24,768]{3,2,0,1:T(8,128)(2,1)S(1)} %copy.17), channel_id=1, source_target_pairs={{0,2},{2,0},{4,6},{6,4},{8,10},{10,8},{12,14},{14,12},{16,18},{18,... | collective-permute-start | bytes 884744 | tf_op jit(solution)/shard_map/ppermute | solution.py:35
  12.4 6.2 %collective-permute-start.3 = (bf16[4,24,768]{2,1,0:T(8,128)(2,1)S(1)}, bf16[4,24,768]{2,1,0:T(8,128)(2,1)S(1)}, u32[]{:S(2)}, u32[]{:S(2)}) collective-permute-start(bf16[4,24,768]{2,1,0:T(8,128)(2,1)S(1)} %fusion.5), channel_id=1, source_target_pairs={{0,2},{2,0},{4,6},{6,4},{8,10},{10,8},{12,14},{14,12},{16,18},{18,... | collective-permute-start | bytes 442376 | tf_op jit(solution)/shard_map/ppermute | solution.py:35
  16.5 5.2 %collective-permute-start.1 = (bf16[4,24,768]{2,1,0:T(8,128)(2,1)S(1)}, bf16[4,24,768]{2,1,0:T(8,128)(2,1)S(1)}, u32[]{:S(2)}, u32[]{:S(2)}) collective-permute-start(bf16[4,24,768]{2,1,0:T(8,128)(2,1)S(1)} %fusion.4), channel_id=1, source_target_pairs={{0,4},{2,6},{4,0},{6,2},{8,12},{10,14},{12,8},{14,10},{16,20},{18,... | collective-permute-start | bytes 442376 | tf_op jit(solution)/shard_map/ppermute | solution.py:35
  21.8 4.5 %collective-permute-start.4 = (bf16[24,1536]{1,0:T(8,128)(2,1)S(1)}, bf16[24,1536]{1,0:T(8,128)(2,1)S(1)}, u32[]{:S(2)}, u32[]{:S(2)}) collective-permute-start(bf16[24,1536]{1,0:T(8,128)(2,1)S(1)} %get-tuple-element.84), channel_id=1, source_target_pairs={{0,8},{2,10},{4,12},{6,14},{8,0},{10,2},{12,4},{14,6},{16,24},{18,... | collective-permute-start | bytes 221192 | tf_op jit(solution)/shard_map/ppermute | solution.py:35
  23.5 6.3 %collective-permute-start.5 = (bf16[24,1536]{1,0:T(8,128)(2,1)S(1)}, bf16[24,1536]{1,0:T(8,128)(2,1)S(1)}, u32[]{:S(2)}, u32[]{:S(2)}) collective-permute-start(bf16[24,1536]{1,0:T(8,128)(2,1)S(1)} %get-tuple-element.85), channel_id=1, source_target_pairs={{0,16},{2,18},{4,20},{6,22},{8,24},{10,26},{12,28},{14,30},{16,0},... | collective-permute-start | bytes 221192 | tf_op jit(solution)/shard_map/ppermute | solution.py:35
  26.1 6.8 %collective-permute-start.6 = (bf16[24,1536]{1,0:T(8,128)(2,1)S(1)}, bf16[24,1536]{1,0:T(8,128)(2,1)S(1)}, u32[]{:S(2)}, u32[]{:S(2)}) collective-permute-start(bf16[24,1536]{1,0:T(8,128)(2,1)S(1)} %get-tuple-element.86), channel_id=1, source_target_pairs={{0,24},{2,26},{4,28},{6,30},{8,16},{10,18},{12,20},{14,22},{16,8},... | collective-permute-start | bytes 221192 | tf_op jit(solution)/shard_map/ppermute | solution.py:35
  33.0 6.4 %collective-permute-start.9 = (bf16[24,1536]{1,0:T(8,128)(2,1)S(1)}, bf16[24,1536]{1,0:T(8,128)(2,1)S(1)}, u32[]{:S(2)}, u32[]{:S(2)}) collective-permute-start(bf16[24,1536]{1,0:T(8,128)(2,1)S(1)} %pad_maximum_fusion.11), channel_id=1, source_target_pairs={{0,24},{2,26},{4,28},{6,30},{8,16},{10,18},{12,20},{14,22},{16,8},... | collective-permute-start | bytes 221192 | tf_op jit(solution)/shard_map/ppermute | solution.py:35
  33.4 6.8 %collective-permute-start.8 = (bf16[24,1536]{1,0:T(8,128)(2,1)S(1)}, bf16[24,1536]{1,0:T(8,128)(2,1)S(1)}, u32[]{:S(2)}, u32[]{:S(2)}) collective-permute-start(bf16[24,1536]{1,0:T(8,128)(2,1)S(1)} %pad_maximum_fusion.11), channel_id=1, source_target_pairs={{0,16},{2,18},{4,20},{6,22},{8,24},{10,26},{12,28},{14,30},{16,0},... | collective-permute-start | bytes 221192 | tf_op jit(solution)/shard_map/ppermute | solution.py:35
  35.0 5.3 %collective-permute-start.7 = (bf16[24,1536]{1,0:T(8,128)(2,1)S(1)}, bf16[24,1536]{1,0:T(8,128)(2,1)S(1)}, u32[]{:S(2)}, u32[]{:S(2)}) collective-permute-start(bf16[24,1536]{1,0:T(8,128)(2,1)S(1)} %pad_maximum_fusion.11), channel_id=1, source_target_pairs={{0,8},{2,10},{4,12},{6,14},{8,0},{10,2},{12,4},{14,6},{16,24},{18,... | collective-permute-start | bytes 221192 | tf_op jit(solution)/shard_map/ppermute | solution.py:35
  40.3 1.7 %copy-start.5 = (bf16[1,384,1536]{2,1,0:T(8,128)(2,1)S(1)}, bf16[1,384,1536]{2,1,0:T(8,128)(2,1)}, u32[]{:S(2)}) copy-start(bf16[1,384,1536]{2,1,0:T(8,128)(2,1)} %param.7) | copy-start | bytes 3538948
  40.4 6.8 %collective-permute-start.12 = (bf16[4,24,768]{2,1,0:T(8,128)(2,1)S(1)}, bf16[4,24,768]{2,1,0:T(8,128)(2,1)S(1)}, u32[]{:S(2)}, u32[]{:S(2)}) collective-permute-start(bf16[4,24,768]{2,1,0:T(8,128)(2,1)S(1)} %get-tuple-element.89), channel_id=1, source_target_pairs={{0,2},{2,0},{4,6},{6,4},{8,10},{10,8},{12,14},{14,12},{16,18},{18,... | collective-permute-start | bytes 442376 | tf_op jit(solution)/shard_map/ppermute | solution.py:35
  42.3 5.2 %collective-permute-start.10 = (bf16[4,24,768]{2,1,0:T(8,128)(2,1)S(1)}, bf16[4,24,768]{2,1,0:T(8,128)(2,1)S(1)}, u32[]{:S(2)}, u32[]{:S(2)}) collective-permute-start(bf16[4,24,768]{2,1,0:T(8,128)(2,1)S(1)} %get-tuple-element.90), channel_id=1, source_target_pairs={{0,4},{2,6},{4,0},{6,2},{8,12},{10,14},{12,8},{14,10},{16,20},{18,... | collective-permute-start | bytes 442376 | tf_op jit(solution)/shard_map/ppermute | solution.py:35
  47.3 6.8 %collective-permute-start.13 = (bf16[4,2,24,768]{3,2,0,1:T(8,128)(2,1)S(1)}, bf16[4,2,24,768]{3,2,0,1:T(8,128)(2,1)S(1)}, u32[]{:S(2)}, u32[]{:S(2)}) collective-permute-start(bf16[4,2,24,768]{3,2,0,1:T(8,128)(2,1)S(1)} %reverse_select_fusion.2), channel_id=1, source_target_pairs={{0,4},{2,6},{4,0},{6,2},{8,12},{10,14},{12,8},{14,10},{16,20},{18,... | collective-permute-start | bytes 884744 | tf_op jit(solution)/shard_map/ppermute | solution.py:35
  47.6 6.8 %collective-permute-start.11 = (bf16[4,2,24,768]{3,2,1,0:T(8,128)(2,1)S(1)}, bf16[4,2,24,768]{3,2,1,0:T(8,128)(2,1)S(1)}, u32[]{:S(2)}, u32[]{:S(2)}) collective-permute-start(bf16[4,2,24,768]{3,2,1,0:T(8,128)(2,1)S(1)} %reverse_select_fusion.3), channel_id=1, source_target_pairs={{0,2},{2,0},{4,6},{6,4},{8,10},{10,8},{12,14},{14,12},{16,18},{18,... | collective-permute-start | bytes 884744 | tf_op jit(solution)/shard_map/ppermute | solution.py:35
  54.7 0.7 copy-start.6
  54.7 0.8 copy-start.8
  54.7 0.9 copy-start.10
  54.7 1.0 copy-start.12
  55.7 1.3 %copy-start.1 = (bf16[768,768]{1,0:T(8,128)(2,1)S(1)}, bf16[768,768]{1,0:T(8,128)(2,1)}, u32[]{:S(2)}) copy-start(bf16[768,768]{1,0:T(8,128)(2,1)} %constant.164.clone.table_ref) | copy-start | bytes 3538948
  55.8 2.9 %collective-permute-start.14 = (bf16[768,768]{1,0:T(8,128)(2,1)S(1)}, bf16[768,768]{1,0:T(8,128)(2,1)S(1)}, u32[]{:S(2)}, u32[]{:S(2)}) collective-permute-start(bf16[768,768]{1,0:T(8,128)(2,1)S(1)} %pad_maximum_fusion.1.shaped_ref), channel_id=1, source_target_pairs={{0,1},{1,0},{2,3},{3,2},{4,5},{5,4},{6,7},{7,6},{8,9},{9,8},{10,11... | collective-permute-start | bytes 3538952 | tf_op jit(solution)/shard_map/ppermute | solution.py:288
  57.0 1.7 %copy-start = (bf16[768,768]{1,0:T(8,128)(2,1)S(1)}, bf16[768,768]{1,0:T(8,128)(2,1)}, u32[]{:S(2)}) copy-start(bf16[768,768]{1,0:T(8,128)(2,1)} %constant.165.clone.table_ref) | copy-start | bytes 3538948
  58.7 8.4 %copy-start.4 = (bf16[768,768]{1,0:T(8,128)(2,1)S(1)}, bf16[768,768]{1,0:T(8,128)(2,1)}, u32[]{:S(2)}) copy-start(bf16[768,768]{1,0:T(8,128)(2,1)} %constant.162.clone.refs_1_.re_ref) | copy-start | bytes 3538948
  59.8 7.3 %copy-start.3 = (bf16[768,768]{1,0:T(8,128)(2,1)S(1)}, bf16[768,768]{1,0:T(8,128)(2,1)}, u32[]{:S(2)}) copy-start(bf16[768,768]{1,0:T(8,128)(2,1)} %constant.163.clone.refs_2_.im_ref) | copy-start | bytes 3538948
  60.0 12.2 %collective-permute-start.27 = (bf16[48,768]{1,0:T(8,128)(2,1)S(1)}, bf16[48,768]{1,0:T(8,128)(2,1)S(1)}, u32[]{:S(2)}, u32[]{:S(2)}) collective-permute-start(bf16[48,768]{1,0:T(8,128)(2,1)S(1)} %get-tuple-element.66), channel_id=1, source_target_pairs={{0,16},{2,18},{4,20},{6,22},{8,24},{10,26},{12,28},{14,30},{16,0},... | collective-permute-start | bytes 221192 | tf_op jit(solution)/shard_map/ppermute | solution.py:35
  61.3 13.9 %collective-permute-start.24 = (bf16[48,768]{1,0:T(8,128)(2,1)S(1)}, bf16[48,768]{1,0:T(8,128)(2,1)S(1)}, u32[]{:S(2)}, u32[]{:S(2)}) collective-permute-start(bf16[48,768]{1,0:T(8,128)(2,1)S(1)} %get-tuple-element.68), channel_id=1, source_target_pairs={{0,20},{2,22},{4,16},{6,18},{8,28},{10,30},{12,24},{14,26},{16,4},... | collective-permute-start | bytes 221192 | tf_op jit(solution)/shard_map/ppermute | solution.py:35
  64.3 12.8 %collective-permute-start.21 = (bf16[48,768]{1,0:T(8,128)(2,1)S(1)}, bf16[48,768]{1,0:T(8,128)(2,1)S(1)}, u32[]{:S(2)}, u32[]{:S(2)}) collective-permute-start(bf16[48,768]{1,0:T(8,128)(2,1)S(1)} %get-tuple-element.71), channel_id=1, source_target_pairs={{0,4},{2,6},{4,0},{6,2},{8,12},{10,14},{12,8},{14,10},{16,20},{18,... | collective-permute-start | bytes 221192 | tf_op jit(solution)/shard_map/ppermute | solution.py:35
  64.4 13.8 %collective-permute-start.18 = (bf16[48,768]{1,0:T(8,128)(2,1)S(1)}, bf16[48,768]{1,0:T(8,128)(2,1)S(1)}, u32[]{:S(2)}, u32[]{:S(2)}) collective-permute-start(bf16[48,768]{1,0:T(8,128)(2,1)S(1)} %get-tuple-element.74), channel_id=1, source_target_pairs={{0,18},{2,16},{4,22},{6,20},{8,26},{10,24},{12,30},{14,28},{16,2},... | collective-permute-start | bytes 221192 | tf_op jit(solution)/shard_map/ppermute | solution.py:35
  66.6 3.6 %copy-start.2 = (bf16[2,16,24,768]{3,2,1,0:T(8,128)(2,1)S(1)}, bf16[2,16,24,768]{3,2,1,0:T(8,128)(2,1)}, u32[]{:S(2)}) copy-start(bf16[2,16,24,768]{3,2,1,0:T(8,128)(2,1)} %param.9) | copy-start | bytes 3538948
  66.6 11.6 %collective-permute-start.15 = (bf16[48,768]{1,0:T(8,128)(2,1)S(1)}, bf16[48,768]{1,0:T(8,128)(2,1)S(1)}, u32[]{:S(2)}, u32[]{:S(2)}) collective-permute-start(bf16[48,768]{1,0:T(8,128)(2,1)S(1)} %get-tuple-element.77), channel_id=1, source_target_pairs={{0,2},{2,0},{4,6},{6,4},{8,10},{10,8},{12,14},{14,12},{16,18},{18,... | collective-permute-start | bytes 221192 | tf_op jit(solution)/shard_map/ppermute | solution.py:35
  72.2 9.8 %collective-permute-start.28 = (bf16[48,768]{1,0:T(8,128)(2,1)S(1)}, bf16[48,768]{1,0:T(8,128)(2,1)S(1)}, u32[]{:S(2)}, u32[]{:S(2)}) collective-permute-start(bf16[48,768]{1,0:T(8,128)(2,1)S(1)} %get-tuple-element.56), channel_id=1, source_target_pairs={{0,6},{2,4},{4,2},{6,0},{8,14},{10,12},{12,10},{14,8},{16,22},{18,... | collective-permute-start | bytes 221192 | tf_op jit(solution)/shard_map/ppermute | solution.py:35
  75.1 8.0 %collective-permute-start.25 = (bf16[48,768]{1,0:T(8,128)(2,1)S(1)}, bf16[48,768]{1,0:T(8,128)(2,1)S(1)}, u32[]{:S(2)}, u32[]{:S(2)}) collective-permute-start(bf16[48,768]{1,0:T(8,128)(2,1)S(1)} %get-tuple-element.48), channel_id=1, source_target_pairs={{0,10},{2,8},{4,14},{6,12},{8,2},{10,0},{12,6},{14,4},{16,26},{18,... | collective-permute-start | bytes 221192 | tf_op jit(solution)/shard_map/ppermute | solution.py:35
  77.1 11.1 %collective-permute-start.22 = (bf16[48,768]{1,0:T(8,128)(2,1)S(1)}, bf16[48,768]{1,0:T(8,128)(2,1)S(1)}, u32[]{:S(2)}, u32[]{:S(2)}) collective-permute-start(bf16[48,768]{1,0:T(8,128)(2,1)S(1)} %get-tuple-element.46), channel_id=1, source_target_pairs={{0,24},{2,26},{4,28},{6,30},{8,16},{10,18},{12,20},{14,22},{16,8},... | collective-permute-start | bytes 221192 | tf_op jit(solution)/shard_map/ppermute | solution.py:35
  78.2 10.0 %collective-permute-start.19 = (bf16[48,768]{1,0:T(8,128)(2,1)S(1)}, bf16[48,768]{1,0:T(8,128)(2,1)S(1)}, u32[]{:S(2)}, u32[]{:S(2)}) collective-permute-start(bf16[48,768]{1,0:T(8,128)(2,1)S(1)} %get-tuple-element.44), channel_id=1, source_target_pairs={{0,8},{2,10},{4,12},{6,14},{8,0},{10,2},{12,4},{14,6},{16,24},{18,... | collective-permute-start | bytes 221192 | tf_op jit(solution)/shard_map/ppermute | solution.py:35
  78.2 10.6 %collective-permute-start.16 = (bf16[48,768]{1,0:T(8,128)(2,1)S(1)}, bf16[48,768]{1,0:T(8,128)(2,1)S(1)}, u32[]{:S(2)}, u32[]{:S(2)}) collective-permute-start(bf16[48,768]{1,0:T(8,128)(2,1)S(1)} %get-tuple-element.42), channel_id=1, source_target_pairs={{0,22},{2,20},{4,18},{6,16},{8,30},{10,28},{12,26},{14,24},{16,6},... | collective-permute-start | bytes 221192 | tf_op jit(solution)/shard_map/ppermute | solution.py:35
  82.0 9.2 %collective-permute-start.29 = (bf16[48,768]{1,0:T(8,128)(2,1)S(1)}, bf16[48,768]{1,0:T(8,128)(2,1)S(1)}, u32[]{:S(2)}, u32[]{:S(2)}) collective-permute-start(bf16[48,768]{1,0:T(8,128)(2,1)S(1)} %get-tuple-element.62), channel_id=1, source_target_pairs={{0,26},{2,24},{4,30},{6,28},{8,18},{10,16},{12,22},{14,20},{16,10}... | collective-permute-start | bytes 221192 | tf_op jit(solution)/shard_map/ppermute | solution.py:35
  83.2 9.3 %collective-permute-start.26 = (bf16[48,768]{1,0:T(8,128)(2,1)S(1)}, bf16[48,768]{1,0:T(8,128)(2,1)S(1)}, u32[]{:S(2)}, u32[]{:S(2)}) collective-permute-start(bf16[48,768]{1,0:T(8,128)(2,1)S(1)} %get-tuple-element.49), channel_id=1, source_target_pairs={{0,30},{2,28},{4,26},{6,24},{8,22},{10,20},{12,18},{14,16},{16,14}... | collective-permute-start | bytes 221192 | tf_op jit(solution)/shard_map/ppermute | solution.py:35
  88.2 6.8 %collective-permute-start.23 = (bf16[48,768]{1,0:T(8,128)(2,1)S(1)}, bf16[48,768]{1,0:T(8,128)(2,1)S(1)}, u32[]{:S(2)}, u32[]{:S(2)}) collective-permute-start(bf16[48,768]{1,0:T(8,128)(2,1)S(1)} %get-tuple-element.47), channel_id=1, source_target_pairs={{0,14},{2,12},{4,10},{6,8},{8,6},{10,4},{12,2},{14,0},{16,30},{18,... | collective-permute-start | bytes 221192 | tf_op jit(solution)/shard_map/ppermute | solution.py:35
  88.2 7.6 %collective-permute-start.20 = (bf16[48,768]{1,0:T(8,128)(2,1)S(1)}, bf16[48,768]{1,0:T(8,128)(2,1)S(1)}, u32[]{:S(2)}, u32[]{:S(2)}) collective-permute-start(bf16[48,768]{1,0:T(8,128)(2,1)S(1)} %get-tuple-element.45), channel_id=1, source_target_pairs={{0,28},{2,30},{4,24},{6,26},{8,20},{10,22},{12,16},{14,18},{16,12}... | collective-permute-start | bytes 221192 | tf_op jit(solution)/shard_map/ppermute | solution.py:35
  88.8 7.0 %collective-permute-start.17 = (bf16[48,768]{1,0:T(8,128)(2,1)S(1)}, bf16[48,768]{1,0:T(8,128)(2,1)S(1)}, u32[]{:S(2)}, u32[]{:S(2)}) collective-permute-start(bf16[48,768]{1,0:T(8,128)(2,1)S(1)} %get-tuple-element.43), channel_id=1, source_target_pairs={{0,12},{2,14},{4,8},{6,10},{8,4},{10,6},{12,0},{14,2},{16,28},{18,... | collective-permute-start | bytes 221192 | tf_op jit(solution)/shard_map/ppermute | solution.py:35
  92.5 8.1 %copy-start.7 = (bf16[384,384]{1,0:T(8,128)(2,1)S(1)}, bf16[384,384]{1,0:T(8,128)(2,1)}, u32[]{:S(2)}) copy-start(bf16[384,384]{1,0:T(8,128)(2,1)} %copy-done.6) | copy-start | bytes 884740
  92.5 8.1 %copy-start.9 = (bf16[384,384]{1,0:T(8,128)(2,1)S(1)}, bf16[384,384]{1,0:T(8,128)(2,1)}, u32[]{:S(2)}) copy-start(bf16[384,384]{1,0:T(8,128)(2,1)} %copy-done.8) | copy-start | bytes 884740
  92.5 8.1 %copy-start.11 = (bf16[384,384]{1,0:T(8,128)(2,1)S(1)}, bf16[384,384]{1,0:T(8,128)(2,1)}, u32[]{:S(2)}) copy-start(bf16[384,384]{1,0:T(8,128)(2,1)} %copy-done.10) | copy-start | bytes 884740
  92.5 8.1 %copy-start.13 = (bf16[384,384]{1,0:T(8,128)(2,1)S(1)}, bf16[384,384]{1,0:T(8,128)(2,1)}, u32[]{:S(2)}) copy-start(bf16[384,384]{1,0:T(8,128)(2,1)} %copy-done.12) | copy-start | bytes 884740
  97.2 10.5 %all-to-all-start = ((f32[32,1,16]{2,1,0:T(1,128)}), f32[32,1,16]{2,1,0:T(1,128)S(1)}, u32[]{:S(2)}, u32[]{:S(2)}) async-start(f32[32,1,16]{2,1,0:T(1,128)} %bitcast.53), calls=%async_computation | async-start | bytes 32768 | tf_op jit(solution)/shard_map/all_to_all | solution.py:347

commit v13 on v9

--- a/solution.py
+++ b/solution.py
@@ -148,7 +148,7 @@
 
 
 def coupling_kernel(block_rows, by_xor, first, fields_ref, targets_ref, *rest):
-    out_ref = rest[-1]
+    out_ref, held = rest[-2:]
     modes = out_ref.shape[1]
     product = lax.dot_general(
         fields_ref[...], targets_ref[...], (((1,), (1,)), ((), ())), preferred_element_type=f32
@@ -167,23 +167,23 @@
         product = jnp.sum(product.reshape(left // block_rows, block_rows, right), 1)
     else:
         product = exactly(groups(left), product, ((1,), (0,)))
-    product = exactly(product, groups(right), ((1,), (1,)))
-    by_re, by_im = product[:, :modes], product[:, modes:]
-    sources = left // block_rows
-    mode = lax.broadcasted_iota(jnp.int32, (modes, sources), 0)
+    sources = left // block_rows // 2
+    product = product.reshape(sources, 2, right)
+    real, imag = product[:, 0], product[:, 1]
+    right = right // 2
+    both = jnp.concatenate(
+        [real[:, :right] + imag[:, right:], imag[:, :right] - real[:, right:]], 0
+    )
+    held[...] = exactly(both, groups(right), ((1,), (1,)))
+    out_ref[...] = rest[0][...] if len(rest) > 2 else jnp.zeros_like(out_ref)
+    me, there = lax.axis_index("modes"), modes // 2
     if by_xor:
-        mode = mode ^ lax.axis_index("modes")
-        mode = mode % (modes // 2) * 2 + mode // (modes // 2)
-    from_row = lax.broadcasted_iota(jnp.int32, (modes, sources), 1) + 2 * first
-    real = jnp.where(from_row == 2 * mode, 1.0, 0.0).astype(f32)
-    imag = jnp.where(from_row == 2 * mode + 1, 1.0, 0.0).astype(f32)
-    inner = ((1,), (0,))
-    total_re = exactly(real, by_re, inner) + exactly(imag, by_im, inner)
-    total_im = exactly(imag, by_re, inner) - exactly(real, by_im, inner)
-    if len(rest) > 1:
-        total_re, total_im = total_re + rest[0][:modes], total_im + rest[0][modes:]
-    out_ref[:modes] = total_re
-    out_ref[modes:] = total_im
+        for at in range(sources):
+            mode = me ^ ((first + at) // 2 + (first + at) % 2 * there)
+            out_ref[pl.ds(mode, 1)] = held[pl.ds(at, 1)]
+            out_ref[pl.ds(modes + mode, 1)] = held[pl.ds(sources + at, 1)]
+    else:
+        out_ref[...] = held[...]
 
 
 def kernel_call(kernel, shape, dtype, flops, operands, grant=12, **more):
@@ -270,16 +270,18 @@
     for part, order in enumerate(orders):
         piece = block[..., part * grid_size : (part + 1) * grid_size]
         done = [last]
-        for d in reversed(order):
+        for at, d in enumerate(reversed(order)):
             axis = sum(1 for other in done if other > d)
             piece = gather_digit(piece, owns[d], *digits[d], axis, count)
+            if part == 0 and at == 0:
+                piece, forward = lax.optimization_barrier((piece, forward))
             done.append(d)
         planes.append(piece.reshape(local_rows, grid_size))
+    fore = forward[0].astype(f32)
     plane_re = jnp.concatenate([p[:, :half] for p in planes], -1)
     plane_im = jnp.concatenate([p[:, half:] for p in planes], -1)
     phase_plane = jnp.concatenate([plane_re, plane_im], -1)
 
-    fore = forward[0].astype(f32)
     fore_re, fore_im = fore[:, :grid_size], fore[:, grid_size:]
     plane_re, plane_im = plane_re.astype(f32), plane_im.astype(f32)
     shaped = jnp.concatenate(
@@ -341,6 +343,7 @@
                 f32,
                 2 * rows.shape[0] * 2 * local_rows * grid_size,
                 (rows, seen) if term is None else (rows, seen, term),
+                scratch_shapes=[pltpu.VMEM((rows.shape[0] // block_rows, mode_total), f32)],
             )
             at += len(group)
     pieces = lax.all_to_all(term, ("modes", "rows"), 0, 0, tiled=True)

time: 106 us -> 106 us (level)
  waiting for transfers between devices: 35.5 us -> 38 us
  starting transfers between devices: 51.1 us -> 49.6 us
    ppermute x29, waiting for transfers between devices: 28.9 us -> 31.4 us  [exchange(): lax.ppermute(values, 'modes', [(i, i ^ offset) for i in range(count)])]
    ppermute x29, starting transfers between devices: 47.5 us -> 46.4 us  [exchange(): lax.ppermute(values, 'modes', [(i, i ^ offset) for i in range(count)])]
  transfers between devices with their start and end apart: 31 -> 31, of which waited for: 14 -> 16; matrix products, arithmetic and copies ran while one was open for 2% -> 2% of each run, Pallas kernels for 7% -> 7%
where the time goes in v13:
time: 106 us
  starting transfers between devices  49.6 us (47%)
  waiting for transfers between devices  38 us (36%)
  Pallas kernels  11.5 us (11%)
  other arithmetic  3.34 us (3%)
  local copies, waits for them, and re-layouts  2.15 us (2%)
  between operations  1.18 us (1%)
    ppermute x29, starting transfers between devices, exchange(): lax.ppermute(values, 'modes', [(i, i ^ offset) for i in range(count)])  46.4 us
    ppermute x29, waiting for transfers between devices, exchange(): lax.ppermute(values, 'modes', [(i, i ^ offset) for i in range(count)])  31.4 us
    pallas_call x7, Pallas kernels, kernel_call(): pl.pallas_call(kernel, out_shape=out_shape, compiler_params=pltpu.Compile...  11.5 us
    all_to_all x1, waiting for transfers between devices, local(): pieces = lax.all_to_all(term, ('modes', 'rows'), 0, 0, tiled=True)  5.99 us
    all_to_all x1, starting transfers between devices, local(): pieces = lax.all_to_all(term, ('modes', 'rows'), 0, 0, tiled=True)  3.13 us
  transfers between devices with their start and end apart: 31, of which 16 were waited for; matrix products, arithmetic and copies ran while one was open for 2% of the time, Pallas kernels for 7%

profile of v13, /device:TPU:0, one launch (start us, length us, event | category | flops | bytes accessed | tf_op | source)
XLA Modules:
  0.0 105.8 jit_solution(14919524137987189867)
XLA Ops:
  0.6 1.8 %shard_map.94 = (bf16[192,768]{1,0:T(8,128)(2,1)S(1)}, f32[192,768]{1,0:T(8,128)S(1)}, bf16[192,768]{1,0:T(8,128)(2,1)S(1)}, f32[192,768]{1,0:T(8,128)S(1)}) custom-call(bf16[384,1536]{1,0:T(8,128)(2,1)} %bitcast.101, bf16[384,1536]{1,0:T(8,128)(2,1)} %bitcast.104), custom_call_target="tpu_custom_call" | custom-call | flops 4718592 | bytes 4194304 | tf_op jit(solution)/shard_map/pallas_call | solution.py:197
  2.5 3.0 %collective-permute-start.2 = (bf16[4,2,24,768]{3,2,0,1:T(8,128)(2,1)S(1)}, bf16[4,2,24,768]{3,2,0,1:T(8,128)(2,1)S(1)}, u32[]{:S(2)}, u32[]{:S(2)}) collective-permute-start(bf16[4,2,24,768]{3,2,0,1:T(8,128)(2,1)S(1)} %copy.19), channel_id=1, source_target_pairs={{0,4},{2,6},{4,0},{6,2},{8,12},{10,14},{12,8},{14,10},{16,20},{18,... | collective-permute-start | bytes 884744 | tf_op jit(solution)/shard_map/ppermute | solution.py:35
  5.5 1.6 %collective-permute-start = (bf16[4,2,24,768]{3,2,0,1:T(8,128)(2,1)S(1)}, bf16[4,2,24,768]{3,2,0,1:T(8,128)(2,1)S(1)}, u32[]{:S(2)}, u32[]{:S(2)}) collective-permute-start(bf16[4,2,24,768]{3,2,0,1:T(8,128)(2,1)S(1)} %copy.17), channel_id=1, source_target_pairs={{0,2},{2,0},{4,6},{6,4},{8,10},{10,8},{12,14},{14,12},{16,18},{18,... | collective-permute-start | bytes 884744 | tf_op jit(solution)/shard_map/ppermute | solution.py:35
  7.1 5.4 %collective-permute-done.2 = bf16[4,2,24,768]{3,2,0,1:T(8,128)(2,1)S(1)} collective-permute-done((bf16[4,2,24,768]{3,2,0,1:T(8,128)(2,1)S(1)}, bf16[4,2,24,768]{3,2,0,1:T(8,128)(2,1)S(1)}, u32[]{:S(2)}, u32[]{:S(2)}) %collective-permute-start.2) | collective-permute-done | bytes 294944 | tf_op jit(solution)/shard_map/ppermute | solution.py:35
  12.6 1.8 %collective-permute-start.3 = (bf16[4,24,768]{2,1,0:T(8,128)(2,1)S(1)}, bf16[4,24,768]{2,1,0:T(8,128)(2,1)S(1)}, u32[]{:S(2)}, u32[]{:S(2)}) collective-permute-start(bf16[4,24,768]{2,1,0:T(8,128)(2,1)S(1)} %fusion.5), channel_id=1, source_target_pairs={{0,2},{2,0},{4,6},{6,4},{8,10},{10,8},{12,14},{14,12},{16,18},{18,... | collective-permute-start | bytes 442376 | tf_op jit(solution)/shard_map/ppermute | solution.py:35
  14.5 1.6 %collective-permute-start.1 = (bf16[4,24,768]{2,1,0:T(8,128)(2,1)S(1)}, bf16[4,24,768]{2,1,0:T(8,128)(2,1)S(1)}, u32[]{:S(2)}, u32[]{:S(2)}) collective-permute-start(bf16[4,24,768]{2,1,0:T(8,128)(2,1)S(1)} %fusion.4), channel_id=1, source_target_pairs={{0,4},{2,6},{4,0},{6,2},{8,12},{10,14},{12,8},{14,10},{16,20},{18,... | collective-permute-start | bytes 442376 | tf_op jit(solution)/shard_map/ppermute | solution.py:35
  16.1 1.8 %collective-permute-done.3 = bf16[4,24,768]{2,1,0:T(8,128)(2,1)S(1)} collective-permute-done((bf16[4,24,768]{2,1,0:T(8,128)(2,1)S(1)}, bf16[4,24,768]{2,1,0:T(8,128)(2,1)S(1)}, u32[]{:S(2)}, u32[]{:S(2)}) %collective-permute-start.3) | collective-permute-done | bytes 147488 | tf_op jit(solution)/shard_map/ppermute | solution.py:35
  17.8 1.8 %collective-permute-done.1 = bf16[4,24,768]{2,1,0:T(8,128)(2,1)S(1)} collective-permute-done((bf16[4,24,768]{2,1,0:T(8,128)(2,1)S(1)}, bf16[4,24,768]{2,1,0:T(8,128)(2,1)S(1)}, u32[]{:S(2)}, u32[]{:S(2)}) %collective-permute-start.1) | collective-permute-done | bytes 147488 | tf_op jit(solution)/shard_map/ppermute | solution.py:35
  19.8 1.6 %collective-permute-start.4 = (bf16[24,1536]{1,0:T(8,128)(2,1)S(1)}, bf16[24,1536]{1,0:T(8,128)(2,1)S(1)}, u32[]{:S(2)}, u32[]{:S(2)}) collective-permute-start(bf16[24,1536]{1,0:T(8,128)(2,1)S(1)} %get-tuple-element.88), channel_id=1, source_target_pairs={{0,8},{2,10},{4,12},{6,14},{8,0},{10,2},{12,4},{14,6},{16,24},{18,... | collective-permute-start | bytes 221192 | tf_op jit(solution)/shard_map/ppermute | solution.py:35
  21.4 2.6 %collective-permute-start.5 = (bf16[24,1536]{1,0:T(8,128)(2,1)S(1)}, bf16[24,1536]{1,0:T(8,128)(2,1)S(1)}, u32[]{:S(2)}, u32[]{:S(2)}) collective-permute-start(bf16[24,1536]{1,0:T(8,128)(2,1)S(1)} %get-tuple-element.89), channel_id=1, source_target_pairs={{0,16},{2,18},{4,20},{6,22},{8,24},{10,26},{12,28},{14,30},{16,0},... | collective-permute-start | bytes 221192 | tf_op jit(solution)/shard_map/ppermute | solution.py:35
  24.3 3.9 %collective-permute-done.5 = bf16[24,1536]{1,0:T(8,128)(2,1)S(1)} collective-permute-done((bf16[24,1536]{1,0:T(8,128)(2,1)S(1)}, bf16[24,1536]{1,0:T(8,128)(2,1)S(1)}, u32[]{:S(2)}, u32[]{:S(2)}) %collective-permute-start.5) | collective-permute-done | bytes 73760 | tf_op jit(solution)/shard_map/ppermute | solution.py:35
  28.1 2.1 %collective-permute-done.6 = bf16[24,1536]{1,0:T(8,128)(2,1)S(1)} collective-permute-done((bf16[24,1536]{1,0:T(8,128)(2,1)S(1)}, bf16[24,1536]{1,0:T(8,128)(2,1)S(1)}, u32[]{:S(2)}, u32[]{:S(2)}) %collective-permute-start.6) | collective-permute-done | bytes 73760 | tf_op jit(solution)/shard_map/ppermute | solution.py:35
  30.3 0.9 collective-permute-start.9
  31.2 1.5 %collective-permute-start.8 = (bf16[24,1536]{1,0:T(8,128)(2,1)S(1)}, bf16[24,1536]{1,0:T(8,128)(2,1)S(1)}, u32[]{:S(2)}, u32[]{:S(2)}) collective-permute-start(bf16[24,1536]{1,0:T(8,128)(2,1)S(1)} %pad_maximum_fusion.11), channel_id=1, source_target_pairs={{0,16},{2,18},{4,20},{6,22},{8,24},{10,26},{12,28},{14,30},{16,0},... | collective-permute-start | bytes 221192 | tf_op jit(solution)/shard_map/ppermute | solution.py:35
  32.7 2.1 %collective-permute-start.7 = (bf16[24,1536]{1,0:T(8,128)(2,1)S(1)}, bf16[24,1536]{1,0:T(8,128)(2,1)S(1)}, u32[]{:S(2)}, u32[]{:S(2)}) collective-permute-start(bf16[24,1536]{1,0:T(8,128)(2,1)S(1)} %pad_maximum_fusion.11), channel_id=1, source_target_pairs={{0,8},{2,10},{4,12},{6,14},{8,0},{10,2},{12,4},{14,6},{16,24},{18,... | collective-permute-start | bytes 221192 | tf_op jit(solution)/shard_map/ppermute | solution.py:35
  34.8 1.9 %collective-permute-done.9 = bf16[24,1536]{1,0:T(8,128)(2,1)S(1)} collective-permute-done((bf16[24,1536]{1,0:T(8,128)(2,1)S(1)}, bf16[24,1536]{1,0:T(8,128)(2,1)S(1)}, u32[]{:S(2)}, u32[]{:S(2)}) %collective-permute-start.9) | collective-permute-done | bytes 73760 | tf_op jit(solution)/shard_map/ppermute | solution.py:35
  36.7 1.3 %collective-permute-done.8 = bf16[24,1536]{1,0:T(8,128)(2,1)S(1)} collective-permute-done((bf16[24,1536]{1,0:T(8,128)(2,1)S(1)}, bf16[24,1536]{1,0:T(8,128)(2,1)S(1)}, u32[]{:S(2)}, u32[]{:S(2)}) %collective-permute-start.8) | collective-permute-done | bytes 73760 | tf_op jit(solution)/shard_map/ppermute | solution.py:35
  38.2 1.6 %collective-permute-start.10 = (bf16[4,24,768]{2,1,0:T(8,128)(2,1)S(1)}, bf16[4,24,768]{2,1,0:T(8,128)(2,1)S(1)}, u32[]{:S(2)}, u32[]{:S(2)}) collective-permute-start(bf16[4,24,768]{2,1,0:T(8,128)(2,1)S(1)} %get-tuple-element.94), channel_id=1, source_target_pairs={{0,4},{2,6},{4,0},{6,2},{8,12},{10,14},{12,8},{14,10},{16,20},{18,... | collective-permute-start | bytes 442376 | tf_op jit(solution)/shard_map/ppermute | solution.py:35
  40.3 4.6 %collective-permute-done.10 = bf16[4,24,768]{2,1,0:T(8,128)(2,1)S(1)} collective-permute-done((bf16[4,24,768]{2,1,0:T(8,128)(2,1)S(1)}, bf16[4,24,768]{2,1,0:T(8,128)(2,1)S(1)}, u32[]{:S(2)}, u32[]{:S(2)}) %collective-permute-start.10) | collective-permute-done | bytes 147488 | tf_op jit(solution)/shard_map/ppermute | solution.py:35
  45.0 1.5 %collective-permute-done.12 = bf16[4,24,768]{2,1,0:T(8,128)(2,1)S(1)} collective-permute-done((bf16[4,24,768]{2,1,0:T(8,128)(2,1)S(1)}, bf16[4,24,768]{2,1,0:T(8,128)(2,1)S(1)}, u32[]{:S(2)}, u32[]{:S(2)}) %collective-permute-start.12) | collective-permute-done | bytes 147488 | tf_op jit(solution)/shard_map/ppermute | solution.py:35
  46.6 0.6 collective-permute-start.13
  47.2 1.2 %collective-permute-start.11 = (bf16[4,2,24,768]{3,2,1,0:T(8,128)(2,1)S(1)}, bf16[4,2,24,768]{3,2,1,0:T(8,128)(2,1)S(1)}, u32[]{:S(2)}, u32[]{:S(2)}) collective-permute-start(bf16[4,2,24,768]{3,2,1,0:T(8,128)(2,1)S(1)} %reverse_select_fusion.3), channel_id=1, source_target_pairs={{0,2},{2,0},{4,6},{6,4},{8,10},{10,8},{12,14},{14,12},{16,18},{18,... | collective-permute-start | bytes 884744 | tf_op jit(solution)/shard_map/ppermute | solution.py:35
  48.7 4.7 %collective-permute-done.13 = bf16[4,2,24,768]{3,2,0,1:T(8,128)(2,1)S(1)} collective-permute-done((bf16[4,2,24,768]{3,2,0,1:T(8,128)(2,1)S(1)}, bf16[4,2,24,768]{3,2,0,1:T(8,128)(2,1)S(1)}, u32[]{:S(2)}, u32[]{:S(2)}) %collective-permute-start.13) | collective-permute-done | bytes 294944 | tf_op jit(solution)/shard_map/ppermute | solution.py:35
  55.4 1.0 copy-done.1
  56.5 1.1 %shard_map.95.own_ref = f32[768,768]{1,0:T(8,128)S(1)} custom-call(bf16[768,768]{1,0:T(8,128)(2,1)S(1)} %copy-done.1, bf16[768,768]{1,0:T(8,128)(2,1)S(1)} %pad_maximum_fusion.1.shaped_ref), custom_call_target="tpu_custom_call" | custom-call | flops 905969664 | bytes 4194304 | tf_op jit(solution)/shard_map/pallas_call | solution.py:197
  57.5 0.6 collective-permute-done.14.shaped_ref
  58.2 1.1 %shard_map.96.refs_0_ = bf16[768,768]{1,0:T(8,128)(2,1)S(1)} custom-call(bf16[768,768]{1,0:T(8,128)(2,1)S(1)} %copy-done, bf16[768,768]{1,0:T(8,128)(2,1)S(1)} %collective-permute-done.14.shaped_ref, f32[768,768]{1,0:T(8,128)S(1)} %shard_map.95.own_ref), custom_call_target="tpu_custom_call" | custom-call | flops 905969664 | bytes 4194304 | tf_op jit(solution)/shard_map/pallas_call | solution.py:197
  59.4 0.8 collective-permute-start.27
  60.2 3.2 %collective-permute-start.24 = (bf16[48,768]{1,0:T(8,128)(2,1)S(1)}, bf16[48,768]{1,0:T(8,128)(2,1)S(1)}, u32[]{:S(2)}, u32[]{:S(2)}) collective-permute-start(bf16[48,768]{1,0:T(8,128)(2,1)S(1)} %get-tuple-element.72), channel_id=1, source_target_pairs={{0,20},{2,22},{4,16},{6,18},{8,28},{10,30},{12,24},{14,26},{16,4},... | collective-permute-start | bytes 221192 | tf_op jit(solution)/shard_map/ppermute | solution.py:35
  63.9 1.3 %collective-permute-start.18 = (bf16[48,768]{1,0:T(8,128)(2,1)S(1)}, bf16[48,768]{1,0:T(8,128)(2,1)S(1)}, u32[]{:S(2)}, u32[]{:S(2)}) collective-permute-start(bf16[48,768]{1,0:T(8,128)(2,1)S(1)} %get-tuple-element.78), channel_id=1, source_target_pairs={{0,18},{2,16},{4,22},{6,20},{8,26},{10,24},{12,30},{14,28},{16,2},... | collective-permute-start | bytes 221192 | tf_op jit(solution)/shard_map/ppermute | solution.py:35
  65.2 0.9 collective-permute-start.15
  66.1 3.0 %shard_map.97 = bf16[384,1536]{1,0:T(8,128)(2,1)} custom-call(bf16[768,768]{1,0:T(8,128)(2,1)S(1)} %shard_map.96.refs_0_, bf16[768,768]{1,0:T(8,128)(2,1)S(1)} %copy-done.4, bf16[768,768]{1,0:T(8,128)(2,1)S(1)} %copy-done.3), custom_call_target="tpu_custom_call" | custom-call | flops 1811939328 | bytes 4194304 | tf_op jit(solution)/shard_map/pallas_call | solution.py:197
  69.1 2.0 %shard_map.98.refs_1_ = bf16[768,768]{1,0:T(8,128)(2,1)S(1)} custom-call(bf16[768,768]{1,0:T(8,128)(2,1)S(1)} %bitcast.100, bf16[768,768]{1,0:T(8,128)(2,1)S(1)} %copy-done.4, bf16[768,768]{1,0:T(8,128)(2,1)S(1)} %copy-done.3), custom_call_target="tpu_custom_call" | custom-call | flops 1811939328 | bytes 4194304 | tf_op jit(solution)/shard_map/pallas_call | solution.py:197
  71.1 1.5 %collective-permute-start.28 = (bf16[48,768]{1,0:T(8,128)(2,1)S(1)}, bf16[48,768]{1,0:T(8,128)(2,1)S(1)}, u32[]{:S(2)}, u32[]{:S(2)}) collective-permute-start(bf16[48,768]{1,0:T(8,128)(2,1)S(1)} %get-tuple-element.60), channel_id=1, source_target_pairs={{0,6},{2,4},{4,2},{6,0},{8,14},{10,12},{12,10},{14,8},{16,22},{18,... | collective-permute-start | bytes 221192 | tf_op jit(solution)/shard_map/ppermute | solution.py:35
  72.6 2.4 %collective-permute-start.25 = (bf16[48,768]{1,0:T(8,128)(2,1)S(1)}, bf16[48,768]{1,0:T(8,128)(2,1)S(1)}, u32[]{:S(2)}, u32[]{:S(2)}) collective-permute-start(bf16[48,768]{1,0:T(8,128)(2,1)S(1)} %get-tuple-element.52), channel_id=1, source_target_pairs={{0,10},{2,8},{4,14},{6,12},{8,2},{10,0},{12,6},{14,4},{16,26},{18,... | collective-permute-start | bytes 221192 | tf_op jit(solution)/shard_map/ppermute | solution.py:35
  75.0 2.2 %collective-permute-start.22 = (bf16[48,768]{1,0:T(8,128)(2,1)S(1)}, bf16[48,768]{1,0:T(8,128)(2,1)S(1)}, u32[]{:S(2)}, u32[]{:S(2)}) collective-permute-start(bf16[48,768]{1,0:T(8,128)(2,1)S(1)} %get-tuple-element.50), channel_id=1, source_target_pairs={{0,24},{2,26},{4,28},{6,30},{8,16},{10,18},{12,20},{14,22},{16,8},... | collective-permute-start | bytes 221192 | tf_op jit(solution)/shard_map/ppermute | solution.py:35
  77.5 2.4 %collective-permute-start.16 = (bf16[48,768]{1,0:T(8,128)(2,1)S(1)}, bf16[48,768]{1,0:T(8,128)(2,1)S(1)}, u32[]{:S(2)}, u32[]{:S(2)}) collective-permute-start(bf16[48,768]{1,0:T(8,128)(2,1)S(1)} %get-tuple-element.46), channel_id=1, source_target_pairs={{0,22},{2,20},{4,18},{6,16},{8,30},{10,28},{12,26},{14,24},{16,6},... | collective-permute-start | bytes 221192 | tf_op jit(solution)/shard_map/ppermute | solution.py:35
  80.0 2.6 %collective-permute-start.29 = (bf16[48,768]{1,0:T(8,128)(2,1)S(1)}, bf16[48,768]{1,0:T(8,128)(2,1)S(1)}, u32[]{:S(2)}, u32[]{:S(2)}) collective-permute-start(bf16[48,768]{1,0:T(8,128)(2,1)S(1)} %get-tuple-element.66), channel_id=1, source_target_pairs={{0,26},{2,24},{4,30},{6,28},{8,18},{10,16},{12,22},{14,20},{16,10}... | collective-permute-start | bytes 221192 | tf_op jit(solution)/shard_map/ppermute | solution.py:35
  82.6 2.4 %collective-permute-start.26 = (bf16[48,768]{1,0:T(8,128)(2,1)S(1)}, bf16[48,768]{1,0:T(8,128)(2,1)S(1)}, u32[]{:S(2)}, u32[]{:S(2)}) collective-permute-start(bf16[48,768]{1,0:T(8,128)(2,1)S(1)} %get-tuple-element.53), channel_id=1, source_target_pairs={{0,30},{2,28},{4,26},{6,24},{8,22},{10,20},{12,18},{14,16},{16,14}... | collective-permute-start | bytes 221192 | tf_op jit(solution)/shard_map/ppermute | solution.py:35
  85.0 3.0 %collective-permute-start.20 = (bf16[48,768]{1,0:T(8,128)(2,1)S(1)}, bf16[48,768]{1,0:T(8,128)(2,1)S(1)}, u32[]{:S(2)}, u32[]{:S(2)}) collective-permute-start(bf16[48,768]{1,0:T(8,128)(2,1)S(1)} %get-tuple-element.49), channel_id=1, source_target_pairs={{0,28},{2,30},{4,24},{6,26},{8,20},{10,22},{12,16},{14,18},{16,12}... | collective-permute-start | bytes 221192 | tf_op jit(solution)/shard_map/ppermute | solution.py:35
  88.1 2.2 %collective-permute-start.17 = (bf16[48,768]{1,0:T(8,128)(2,1)S(1)}, bf16[48,768]{1,0:T(8,128)(2,1)S(1)}, u32[]{:S(2)}, u32[]{:S(2)}) collective-permute-start(bf16[48,768]{1,0:T(8,128)(2,1)S(1)} %get-tuple-element.47), channel_id=1, source_target_pairs={{0,12},{2,14},{4,8},{6,10},{8,4},{10,6},{12,0},{14,2},{16,28},{18,... | collective-permute-start | bytes 221192 | tf_op jit(solution)/shard_map/ppermute | solution.py:35
  90.4 1.2 %shard_map.99.refs_2_ = f32[32,16]{1,0:T(8,128)S(1)} custom-call(bf16[576,768]{1,0:T(8,128)(2,1)S(1)} %constant_dynamic-update-slice_fusion.refs_0_, bf16[768,768]{1,0:T(8,128)(2,1)S(1)} %shard_map.98.refs_1_), custom_call_target="tpu_custom_call" | custom-call | flops 679477248 | bytes 4194304 | tf_op jit(solution)/shard_map/pallas_call | solution.py:197
  91.7 1.1 %collective-permute-done.20 = bf16[48,768]{1,0:T(8,128)(2,1)S(1)} collective-permute-done((bf16[48,768]{1,0:T(8,128)(2,1)S(1)}, bf16[48,768]{1,0:T(8,128)(2,1)S(1)}, u32[]{:S(2)}, u32[]{:S(2)}) %collective-permute-start.20) | collective-permute-done | bytes 73760 | tf_op jit(solution)/shard_map/ppermute | solution.py:35
  92.8 0.8 collective-permute-done.17
  93.6 1.4 %shard_map.100 = f32[32,16]{1,0:T(8,128)} custom-call(bf16[192,768]{1,0:T(8,128)(2,1)S(1)} %pad_maximum_fusion.10.refs_0_, bf16[768,768]{1,0:T(8,128)(2,1)S(1)} %shard_map.98.refs_1_, f32[32,16]{1,0:T(8,128)S(1)} %shard_map.99.refs_2_), custom_call_target="tpu_custom_call" | custom-call | flops 226492416 | bytes 4194304 | tf_op jit(solution)/shard_map/pallas_call | solution.py:197
  95.0 3.1 %all-to-all-start = ((f32[32,1,16]{2,1,0:T(1,128)}), f32[32,1,16]{2,1,0:T(1,128)S(1)}, u32[]{:S(2)}, u32[]{:S(2)}) async-start(f32[32,1,16]{2,1,0:T(1,128)} %bitcast.55), calls=%async_computation | async-start | bytes 32768 | tf_op jit(solution)/shard_map/all_to_all | solution.py:349
  98.1 1.1 %pad_maximum_fusion = bf16[384,1536]{1,0:T(8,128)(2,1)} fusion(bf16[384,384]{1,0:T(8,128)(2,1)S(1)} %copy-done.11, bf16[384,384]{1,0:T(8,128)(2,1)S(1)} %copy-done.9, bf16[384,384]{1,0:T(8,128)(2,1)S(1)} %copy-done.13, bf16[384,384]{1,0:T(8,128)(2,1)S(1)} %copy-done.7), kind=kLoop, calls=%fused_computation.8 | loop fusion | flops 4718592 | bytes 2359296 | tf_op jit(solution)/shard_map/concatenate | solution.py:283
  99.2 6.0 %all-to-all-done = f32[32,1,16]{2,1,0:T(1,128)S(1)} async-done(((f32[32,1,16]{2,1,0:T(1,128)}), f32[32,1,16]{2,1,0:T(1,128)S(1)}, u32[]{:S(2)}, u32[]{:S(2)}) %all-to-all-start) | async-done | bytes 2080 | tf_op jit(solution)/shard_map/all_to_all | solution.py:349
  (95 shorter events, 5.4 us)
Async XLA Ops:
  2.5 10.0 %collective-permute-start.2 = (bf16[4,2,24,768]{3,2,0,1:T(8,128)(2,1)S(1)}, bf16[4,2,24,768]{3,2,0,1:T(8,128)(2,1)S(1)}, u32[]{:S(2)}, u32[]{:S(2)}) collective-permute-start(bf16[4,2,24,768]{3,2,0,1:T(8,128)(2,1)S(1)} %copy.19), channel_id=1, source_target_pairs={{0,4},{2,6},{4,0},{6,2},{8,12},{10,14},{12,8},{14,10},{16,20},{18,... | collective-permute-start | bytes 884744 | tf_op jit(solution)/shard_map/ppermute | solution.py:35
  5.5 8.9 %collective-permute-start = (bf16[4,2,24,768]{3,2,0,1:T(8,128)(2,1)S(1)}, bf16[4,2,24,768]{3,2,0,1:T(8,128)(2,1)S(1)}, u32[]{:S(2)}, u32[]{:S(2)}) collective-permute-start(bf16[4,2,24,768]{3,2,0,1:T(8,128)(2,1)S(1)} %copy.17), channel_id=1, source_target_pairs={{0,2},{2,0},{4,6},{6,4},{8,10},{10,8},{12,14},{14,12},{16,18},{18,... | collective-permute-start | bytes 884744 | tf_op jit(solution)/shard_map/ppermute | solution.py:35
  12.6 5.2 %collective-permute-start.3 = (bf16[4,24,768]{2,1,0:T(8,128)(2,1)S(1)}, bf16[4,24,768]{2,1,0:T(8,128)(2,1)S(1)}, u32[]{:S(2)}, u32[]{:S(2)}) collective-permute-start(bf16[4,24,768]{2,1,0:T(8,128)(2,1)S(1)} %fusion.5), channel_id=1, source_target_pairs={{0,2},{2,0},{4,6},{6,4},{8,10},{10,8},{12,14},{14,12},{16,18},{18,... | collective-permute-start | bytes 442376 | tf_op jit(solution)/shard_map/ppermute | solution.py:35
  14.5 5.2 %collective-permute-start.1 = (bf16[4,24,768]{2,1,0:T(8,128)(2,1)S(1)}, bf16[4,24,768]{2,1,0:T(8,128)(2,1)S(1)}, u32[]{:S(2)}, u32[]{:S(2)}) collective-permute-start(bf16[4,24,768]{2,1,0:T(8,128)(2,1)S(1)} %fusion.4), channel_id=1, source_target_pairs={{0,4},{2,6},{4,0},{6,2},{8,12},{10,14},{12,8},{14,10},{16,20},{18,... | collective-permute-start | bytes 442376 | tf_op jit(solution)/shard_map/ppermute | solution.py:35
  19.8 4.5 %collective-permute-start.4 = (bf16[24,1536]{1,0:T(8,128)(2,1)S(1)}, bf16[24,1536]{1,0:T(8,128)(2,1)S(1)}, u32[]{:S(2)}, u32[]{:S(2)}) collective-permute-start(bf16[24,1536]{1,0:T(8,128)(2,1)S(1)} %get-tuple-element.88), channel_id=1, source_target_pairs={{0,8},{2,10},{4,12},{6,14},{8,0},{10,2},{12,4},{14,6},{16,24},{18,... | collective-permute-start | bytes 221192 | tf_op jit(solution)/shard_map/ppermute | solution.py:35
  21.4 6.7 %collective-permute-start.5 = (bf16[24,1536]{1,0:T(8,128)(2,1)S(1)}, bf16[24,1536]{1,0:T(8,128)(2,1)S(1)}, u32[]{:S(2)}, u32[]{:S(2)}) collective-permute-start(bf16[24,1536]{1,0:T(8,128)(2,1)S(1)} %get-tuple-element.89), channel_id=1, source_target_pairs={{0,16},{2,18},{4,20},{6,22},{8,24},{10,26},{12,28},{14,30},{16,0},... | collective-permute-start | bytes 221192 | tf_op jit(solution)/shard_map/ppermute | solution.py:35
  24.0 6.3 %collective-permute-start.6 = (bf16[24,1536]{1,0:T(8,128)(2,1)S(1)}, bf16[24,1536]{1,0:T(8,128)(2,1)S(1)}, u32[]{:S(2)}, u32[]{:S(2)}) collective-permute-start(bf16[24,1536]{1,0:T(8,128)(2,1)S(1)} %get-tuple-element.90), channel_id=1, source_target_pairs={{0,24},{2,26},{4,28},{6,30},{8,16},{10,18},{12,20},{14,22},{16,8},... | collective-permute-start | bytes 221192 | tf_op jit(solution)/shard_map/ppermute | solution.py:35
  30.3 6.4 %collective-permute-start.9 = (bf16[24,1536]{1,0:T(8,128)(2,1)S(1)}, bf16[24,1536]{1,0:T(8,128)(2,1)S(1)}, u32[]{:S(2)}, u32[]{:S(2)}) collective-permute-start(bf16[24,1536]{1,0:T(8,128)(2,1)S(1)} %pad_maximum_fusion.11), channel_id=1, source_target_pairs={{0,24},{2,26},{4,28},{6,30},{8,16},{10,18},{12,20},{14,22},{16,8},... | collective-permute-start | bytes 221192 | tf_op jit(solution)/shard_map/ppermute | solution.py:35
  31.2 6.8 %collective-permute-start.8 = (bf16[24,1536]{1,0:T(8,128)(2,1)S(1)}, bf16[24,1536]{1,0:T(8,128)(2,1)S(1)}, u32[]{:S(2)}, u32[]{:S(2)}) collective-permute-start(bf16[24,1536]{1,0:T(8,128)(2,1)S(1)} %pad_maximum_fusion.11), channel_id=1, source_target_pairs={{0,16},{2,18},{4,20},{6,22},{8,24},{10,26},{12,28},{14,30},{16,0},... | collective-permute-start | bytes 221192 | tf_op jit(solution)/shard_map/ppermute | solution.py:35
  32.7 5.4 %collective-permute-start.7 = (bf16[24,1536]{1,0:T(8,128)(2,1)S(1)}, bf16[24,1536]{1,0:T(8,128)(2,1)S(1)}, u32[]{:S(2)}, u32[]{:S(2)}) collective-permute-start(bf16[24,1536]{1,0:T(8,128)(2,1)S(1)} %pad_maximum_fusion.11), channel_id=1, source_target_pairs={{0,8},{2,10},{4,12},{6,14},{8,0},{10,2},{12,4},{14,6},{16,24},{18,... | collective-permute-start | bytes 221192 | tf_op jit(solution)/shard_map/ppermute | solution.py:35
  38.2 6.7 %collective-permute-start.10 = (bf16[4,24,768]{2,1,0:T(8,128)(2,1)S(1)}, bf16[4,24,768]{2,1,0:T(8,128)(2,1)S(1)}, u32[]{:S(2)}, u32[]{:S(2)}) collective-permute-start(bf16[4,24,768]{2,1,0:T(8,128)(2,1)S(1)} %get-tuple-element.94), channel_id=1, source_target_pairs={{0,4},{2,6},{4,0},{6,2},{8,12},{10,14},{12,8},{14,10},{16,20},{18,... | collective-permute-start | bytes 442376 | tf_op jit(solution)/shard_map/ppermute | solution.py:35
  39.8 6.7 %collective-permute-start.12 = (bf16[4,24,768]{2,1,0:T(8,128)(2,1)S(1)}, bf16[4,24,768]{2,1,0:T(8,128)(2,1)S(1)}, u32[]{:S(2)}, u32[]{:S(2)}) collective-permute-start(bf16[4,24,768]{2,1,0:T(8,128)(2,1)S(1)} %get-tuple-element.93), channel_id=1, source_target_pairs={{0,2},{2,0},{4,6},{6,4},{8,10},{10,8},{12,14},{14,12},{16,18},{18,... | collective-permute-start | bytes 442376 | tf_op jit(solution)/shard_map/ppermute | solution.py:35
  44.9 3.4 %copy-start.5 = (bf16[1,384,1536]{2,1,0:T(8,128)(2,1)S(1)}, bf16[1,384,1536]{2,1,0:T(8,128)(2,1)}, u32[]{:S(2)}) copy-start(bf16[1,384,1536]{2,1,0:T(8,128)(2,1)} %param.7) | copy-start | bytes 3538948
  46.6 6.8 %collective-permute-start.13 = (bf16[4,2,24,768]{3,2,0,1:T(8,128)(2,1)S(1)}, bf16[4,2,24,768]{3,2,0,1:T(8,128)(2,1)S(1)}, u32[]{:S(2)}, u32[]{:S(2)}) collective-permute-start(bf16[4,2,24,768]{3,2,0,1:T(8,128)(2,1)S(1)} %reverse_select_fusion.2), channel_id=1, source_target_pairs={{0,4},{2,6},{4,0},{6,2},{8,12},{10,14},{12,8},{14,10},{16,20},{18,... | collective-permute-start | bytes 884744 | tf_op jit(solution)/shard_map/ppermute | solution.py:35
  47.2 6.7 %collective-permute-start.11 = (bf16[4,2,24,768]{3,2,1,0:T(8,128)(2,1)S(1)}, bf16[4,2,24,768]{3,2,1,0:T(8,128)(2,1)S(1)}, u32[]{:S(2)}, u32[]{:S(2)}) collective-permute-start(bf16[4,2,24,768]{3,2,1,0:T(8,128)(2,1)S(1)} %reverse_select_fusion.3), channel_id=1, source_target_pairs={{0,2},{2,0},{4,6},{6,4},{8,10},{10,8},{12,14},{14,12},{16,18},{18,... | collective-permute-start | bytes 884744 | tf_op jit(solution)/shard_map/ppermute | solution.py:35
  54.2 0.7 copy-start.6
  54.2 0.8 copy-start.8
  54.2 0.9 copy-start.10
  54.2 1.0 copy-start.12
  55.2 1.3 %copy-start.1 = (bf16[768,768]{1,0:T(8,128)(2,1)S(1)}, bf16[768,768]{1,0:T(8,128)(2,1)}, u32[]{:S(2)}) copy-start(bf16[768,768]{1,0:T(8,128)(2,1)} %constant.164.clone.table_ref) | copy-start | bytes 3538948
  55.3 2.9 %collective-permute-start.14 = (bf16[768,768]{1,0:T(8,128)(2,1)S(1)}, bf16[768,768]{1,0:T(8,128)(2,1)S(1)}, u32[]{:S(2)}, u32[]{:S(2)}) collective-permute-start(bf16[768,768]{1,0:T(8,128)(2,1)S(1)} %pad_maximum_fusion.1.shaped_ref), channel_id=1, source_target_pairs={{0,1},{1,0},{2,3},{3,2},{4,5},{5,4},{6,7},{7,6},{8,9},{9,8},{10,11... | collective-permute-start | bytes 3538952 | tf_op jit(solution)/shard_map/ppermute | solution.py:290
  56.5 1.7 %copy-start = (bf16[768,768]{1,0:T(8,128)(2,1)S(1)}, bf16[768,768]{1,0:T(8,128)(2,1)}, u32[]{:S(2)}) copy-start(bf16[768,768]{1,0:T(8,128)(2,1)} %constant.165.clone.table_ref) | copy-start | bytes 3538948
  58.2 7.9 %copy-start.4 = (bf16[768,768]{1,0:T(8,128)(2,1)S(1)}, bf16[768,768]{1,0:T(8,128)(2,1)}, u32[]{:S(2)}) copy-start(bf16[768,768]{1,0:T(8,128)(2,1)} %constant.162.clone.refs_1_.re_ref) | copy-start | bytes 3538948
  59.3 6.8 %copy-start.3 = (bf16[768,768]{1,0:T(8,128)(2,1)S(1)}, bf16[768,768]{1,0:T(8,128)(2,1)}, u32[]{:S(2)}) copy-start(bf16[768,768]{1,0:T(8,128)(2,1)} %constant.163.clone.refs_2_.im_ref) | copy-start | bytes 3538948
  59.4 11.7 %collective-permute-start.27 = (bf16[48,768]{1,0:T(8,128)(2,1)S(1)}, bf16[48,768]{1,0:T(8,128)(2,1)S(1)}, u32[]{:S(2)}, u32[]{:S(2)}) collective-permute-start(bf16[48,768]{1,0:T(8,128)(2,1)S(1)} %get-tuple-element.70), channel_id=1, source_target_pairs={{0,16},{2,18},{4,20},{6,22},{8,24},{10,26},{12,28},{14,30},{16,0},... | collective-permute-start | bytes 221192 | tf_op jit(solution)/shard_map/ppermute | solution.py:35
  60.2 12.4 %collective-permute-start.24 = (bf16[48,768]{1,0:T(8,128)(2,1)S(1)}, bf16[48,768]{1,0:T(8,128)(2,1)S(1)}, u32[]{:S(2)}, u32[]{:S(2)}) collective-permute-start(bf16[48,768]{1,0:T(8,128)(2,1)S(1)} %get-tuple-element.72), channel_id=1, source_target_pairs={{0,20},{2,22},{4,16},{6,18},{8,28},{10,30},{12,24},{14,26},{16,4},... | collective-permute-start | bytes 221192 | tf_op jit(solution)/shard_map/ppermute | solution.py:35
  63.4 11.7 %collective-permute-start.21 = (bf16[48,768]{1,0:T(8,128)(2,1)S(1)}, bf16[48,768]{1,0:T(8,128)(2,1)S(1)}, u32[]{:S(2)}, u32[]{:S(2)}) collective-permute-start(bf16[48,768]{1,0:T(8,128)(2,1)S(1)} %get-tuple-element.75), channel_id=1, source_target_pairs={{0,4},{2,6},{4,0},{6,2},{8,12},{10,14},{12,8},{14,10},{16,20},{18,... | collective-permute-start | bytes 221192 | tf_op jit(solution)/shard_map/ppermute | solution.py:35
  63.9 13.4 %collective-permute-start.18 = (bf16[48,768]{1,0:T(8,128)(2,1)S(1)}, bf16[48,768]{1,0:T(8,128)(2,1)S(1)}, u32[]{:S(2)}, u32[]{:S(2)}) collective-permute-start(bf16[48,768]{1,0:T(8,128)(2,1)S(1)} %get-tuple-element.78), channel_id=1, source_target_pairs={{0,18},{2,16},{4,22},{6,20},{8,26},{10,24},{12,30},{14,28},{16,2},... | collective-permute-start | bytes 221192 | tf_op jit(solution)/shard_map/ppermute | solution.py:35
  65.2 3.9 %copy-start.2 = (bf16[2,16,24,768]{3,2,1,0:T(8,128)(2,1)S(1)}, bf16[2,16,24,768]{3,2,1,0:T(8,128)(2,1)}, u32[]{:S(2)}) copy-start(bf16[2,16,24,768]{3,2,1,0:T(8,128)(2,1)} %param.9) | copy-start | bytes 3538948
  65.2 12.3 %collective-permute-start.15 = (bf16[48,768]{1,0:T(8,128)(2,1)S(1)}, bf16[48,768]{1,0:T(8,128)(2,1)S(1)}, u32[]{:S(2)}, u32[]{:S(2)}) collective-permute-start(bf16[48,768]{1,0:T(8,128)(2,1)S(1)} %get-tuple-element.81), channel_id=1, source_target_pairs={{0,2},{2,0},{4,6},{6,4},{8,10},{10,8},{12,14},{14,12},{16,18},{18,... | collective-permute-start | bytes 221192 | tf_op jit(solution)/shard_map/ppermute | solution.py:35
  71.1 8.9 %collective-permute-start.28 = (bf16[48,768]{1,0:T(8,128)(2,1)S(1)}, bf16[48,768]{1,0:T(8,128)(2,1)S(1)}, u32[]{:S(2)}, u32[]{:S(2)}) collective-permute-start(bf16[48,768]{1,0:T(8,128)(2,1)S(1)} %get-tuple-element.60), channel_id=1, source_target_pairs={{0,6},{2,4},{4,2},{6,0},{8,14},{10,12},{12,10},{14,8},{16,22},{18,... | collective-permute-start | bytes 221192 | tf_op jit(solution)/shard_map/ppermute | solution.py:35
  72.6 10.0 %collective-permute-start.25 = (bf16[48,768]{1,0:T(8,128)(2,1)S(1)}, bf16[48,768]{1,0:T(8,128)(2,1)S(1)}, u32[]{:S(2)}, u32[]{:S(2)}) collective-permute-start(bf16[48,768]{1,0:T(8,128)(2,1)S(1)} %get-tuple-element.52), channel_id=1, source_target_pairs={{0,10},{2,8},{4,14},{6,12},{8,2},{10,0},{12,6},{14,4},{16,26},{18,... | collective-permute-start | bytes 221192 | tf_op jit(solution)/shard_map/ppermute | solution.py:35
  75.0 10.0 %collective-permute-start.22 = (bf16[48,768]{1,0:T(8,128)(2,1)S(1)}, bf16[48,768]{1,0:T(8,128)(2,1)S(1)}, u32[]{:S(2)}, u32[]{:S(2)}) collective-permute-start(bf16[48,768]{1,0:T(8,128)(2,1)S(1)} %get-tuple-element.50), channel_id=1, source_target_pairs={{0,24},{2,26},{4,28},{6,30},{8,16},{10,18},{12,20},{14,22},{16,8},... | collective-permute-start | bytes 221192 | tf_op jit(solution)/shard_map/ppermute | solution.py:35
  77.3 7.7 %collective-permute-start.19 = (bf16[48,768]{1,0:T(8,128)(2,1)S(1)}, bf16[48,768]{1,0:T(8,128)(2,1)S(1)}, u32[]{:S(2)}, u32[]{:S(2)}) collective-permute-start(bf16[48,768]{1,0:T(8,128)(2,1)S(1)} %get-tuple-element.48), channel_id=1, source_target_pairs={{0,8},{2,10},{4,12},{6,14},{8,0},{10,2},{12,4},{14,6},{16,24},{18,... | collective-permute-start | bytes 221192 | tf_op jit(solution)/shard_map/ppermute | solution.py:35
  77.5 10.5 %collective-permute-start.16 = (bf16[48,768]{1,0:T(8,128)(2,1)S(1)}, bf16[48,768]{1,0:T(8,128)(2,1)S(1)}, u32[]{:S(2)}, u32[]{:S(2)}) collective-permute-start(bf16[48,768]{1,0:T(8,128)(2,1)S(1)} %get-tuple-element.46), channel_id=1, source_target_pairs={{0,22},{2,20},{4,18},{6,16},{8,30},{10,28},{12,26},{14,24},{16,6},... | collective-permute-start | bytes 221192 | tf_op jit(solution)/shard_map/ppermute | solution.py:35
  80.0 10.4 %collective-permute-start.29 = (bf16[48,768]{1,0:T(8,128)(2,1)S(1)}, bf16[48,768]{1,0:T(8,128)(2,1)S(1)}, u32[]{:S(2)}, u32[]{:S(2)}) collective-permute-start(bf16[48,768]{1,0:T(8,128)(2,1)S(1)} %get-tuple-element.66), channel_id=1, source_target_pairs={{0,26},{2,24},{4,30},{6,28},{8,18},{10,16},{12,22},{14,20},{16,10}... | collective-permute-start | bytes 221192 | tf_op jit(solution)/shard_map/ppermute | solution.py:35
  82.6 9.0 %collective-permute-start.26 = (bf16[48,768]{1,0:T(8,128)(2,1)S(1)}, bf16[48,768]{1,0:T(8,128)(2,1)S(1)}, u32[]{:S(2)}, u32[]{:S(2)}) collective-permute-start(bf16[48,768]{1,0:T(8,128)(2,1)S(1)} %get-tuple-element.53), channel_id=1, source_target_pairs={{0,30},{2,28},{4,26},{6,24},{8,22},{10,20},{12,18},{14,16},{16,14}... | collective-permute-start | bytes 221192 | tf_op jit(solution)/shard_map/ppermute | solution.py:35
  85.0 6.7 %collective-permute-start.23 = (bf16[48,768]{1,0:T(8,128)(2,1)S(1)}, bf16[48,768]{1,0:T(8,128)(2,1)S(1)}, u32[]{:S(2)}, u32[]{:S(2)}) collective-permute-start(bf16[48,768]{1,0:T(8,128)(2,1)S(1)} %get-tuple-element.51), channel_id=1, source_target_pairs={{0,14},{2,12},{4,10},{6,8},{8,6},{10,4},{12,2},{14,0},{16,30},{18,... | collective-permute-start | bytes 221192 | tf_op jit(solution)/shard_map/ppermute | solution.py:35
  85.0 7.8 %collective-permute-start.20 = (bf16[48,768]{1,0:T(8,128)(2,1)S(1)}, bf16[48,768]{1,0:T(8,128)(2,1)S(1)}, u32[]{:S(2)}, u32[]{:S(2)}) collective-permute-start(bf16[48,768]{1,0:T(8,128)(2,1)S(1)} %get-tuple-element.49), channel_id=1, source_target_pairs={{0,28},{2,30},{4,24},{6,26},{8,20},{10,22},{12,16},{14,18},{16,12}... | collective-permute-start | bytes 221192 | tf_op jit(solution)/shard_map/ppermute | solution.py:35
  88.1 5.5 %collective-permute-start.17 = (bf16[48,768]{1,0:T(8,128)(2,1)S(1)}, bf16[48,768]{1,0:T(8,128)(2,1)S(1)}, u32[]{:S(2)}, u32[]{:S(2)}) collective-permute-start(bf16[48,768]{1,0:T(8,128)(2,1)S(1)} %get-tuple-element.47), channel_id=1, source_target_pairs={{0,12},{2,14},{4,8},{6,10},{8,4},{10,6},{12,0},{14,2},{16,28},{18,... | collective-permute-start | bytes 221192 | tf_op jit(solution)/shard_map/ppermute | solution.py:35
  91.6 6.5 %copy-start.7 = (bf16[384,384]{1,0:T(8,128)(2,1)S(1)}, bf16[384,384]{1,0:T(8,128)(2,1)}, u32[]{:S(2)}) copy-start(bf16[384,384]{1,0:T(8,128)(2,1)} %copy-done.6) | copy-start | bytes 884740
  91.6 6.5 %copy-start.9 = (bf16[384,384]{1,0:T(8,128)(2,1)S(1)}, bf16[384,384]{1,0:T(8,128)(2,1)}, u32[]{:S(2)}) copy-start(bf16[384,384]{1,0:T(8,128)(2,1)} %copy-done.8) | copy-start | bytes 884740
  91.6 6.5 %copy-start.11 = (bf16[384,384]{1,0:T(8,128)(2,1)S(1)}, bf16[384,384]{1,0:T(8,128)(2,1)}, u32[]{:S(2)}) copy-start(bf16[384,384]{1,0:T(8,128)(2,1)} %copy-done.10) | copy-start | bytes 884740
  91.6 6.5 %copy-start.13 = (bf16[384,384]{1,0:T(8,128)(2,1)S(1)}, bf16[384,384]{1,0:T(8,128)(2,1)}, u32[]{:S(2)}) copy-start(bf16[384,384]{1,0:T(8,128)(2,1)} %copy-done.12) | copy-start | bytes 884740
  95.0 10.3 %all-to-all-start = ((f32[32,1,16]{2,1,0:T(1,128)}), f32[32,1,16]{2,1,0:T(1,128)S(1)}, u32[]{:S(2)}, u32[]{:S(2)}) async-start(f32[32,1,16]{2,1,0:T(1,128)} %bitcast.55), calls=%async_computation | async-start | bytes 32768 | tf_op jit(solution)/shard_map/all_to_all | solution.py:349

commit v14 on v5

--- a/solution.py
+++ b/solution.py
@@ -164,15 +164,13 @@
         product = jnp.sum(product.reshape(left // block_rows, block_rows, right), 1)
     else:
         product = exactly(groups(left), product, ((1,), (0,)))
-    product = exactly(product, groups(right), ((1,), (1,)))
-    by_re, by_im = product[:, :modes], product[:, modes:]
-    mode = lax.broadcasted_iota(jnp.int32, (modes, 2 * modes), 0)
-    from_row = lax.broadcasted_iota(jnp.int32, (modes, 2 * modes), 1)
-    real = jnp.where(from_row == 2 * mode, 1.0, 0.0).astype(f32)
-    imag = jnp.where(from_row == 2 * mode + 1, 1.0, 0.0).astype(f32)
-    inner = ((1,), (0,))
-    out_ref[:modes] = exactly(real, by_re, inner) + exactly(imag, by_im, inner)
-    out_ref[modes:] = exactly(imag, by_re, inner) - exactly(real, by_im, inner)
+    product = product.reshape(modes, 2, right)
+    real, imag = product[:, 0], product[:, 1]
+    right = right // 2
+    both = jnp.concatenate(
+        [real[:, :right] + imag[:, right:], imag[:, :right] - real[:, right:]], 0
+    )
+    out_ref[...] = exactly(both, groups(right), ((1,), (1,)))
 
 
 def kernel_call(kernel, shape, dtype, flops, operands, grant=12, **more):
@@ -216,6 +214,7 @@
             [bf16, f32, bf16, f32],
             8 * local_rows * double_width,
             (forward[0], backward[0]),
+            grant=52,
             in_specs=[pl.BlockSpec(memory_space=pltpu.HBM)] * 2,
             scratch_shapes=[pltpu.VMEM((local_rows, double_width), bf16)] * 2
             + [pltpu.SemaphoreType.DMA((2 * local_rows // (4 * block_rows),))],
@@ -295,11 +294,8 @@
     )
     blocks = columns.reshape(owners, 2, -1, block_rows, grid_size).transpose(0, 2, 1, 3, 4)
     blocks = blocks.reshape(count, 2 * block_rows, grid_size)
-    pixels = lax.all_to_all(blocks, "modes", 0, 0, tiled=True).reshape(column_shape)
-
-    seen = kernel_call(
-        targets_kernel, column_shape, bf16, matmul, (targets.reshape(column_shape), full_re, full_im)
-    )
+    pixels = lax.all_to_all(blocks, "modes", 0, 0, tiled=True)
+
     output_fields = kernel_call(
         lambda *refs: fields_kernel(block_rows, *refs),
         (local_rows, double_width),
@@ -307,14 +303,21 @@
         matmul,
         (columns, full_re, full_im),
     )
-    pixels, output_fields, seen = lax.optimization_barrier((pixels, output_fields, seen))
-
+    target_re, target_im = targets.reshape(2, local_rows, grid_size)
+    seen = jnp.concatenate(
+        [
+            times(target_re, full_re) + times(target_im, full_im),
+            times(target_im, full_re) - times(target_re, full_im),
+        ],
+        0,
+    ).astype(bf16)
+    pixels, output_fields = lax.optimization_barrier((pixels, output_fields))
     term = kernel_call(
         lambda *refs: coupling_kernel(block_rows, *refs),
         (2 * mode_total, mode_total),
         f32,
         matmul,
-        (pixels, seen),
+        (pixels.reshape(column_shape), seen),
     )
     pieces = lax.all_to_all(term, ("modes", "rows"), 0, 0, tiled=True)
     coupling = jnp.sum(pieces, 0, keepdims=True)

time: 112 us -> 105 us (0.938)
  local copies, waits for them, and re-layouts: 8.13 us -> 3.34 us
  waiting for transfers between devices: 53.8 us -> 51.1 us
  matrix products: 0 us -> 2.51 us
  Pallas kernels: 13 us -> 11.3 us
    unnamed x38 -> x12, local copies, waits for them, and re-layouts: 7.8 us -> 2.92 us
    ppermute x14, waiting for transfers between devices: 28.7 us -> 26.1 us  [exchange(): lax.ppermute(values, 'modes', [(i, i ^ offset) for i in range(count)])]
    dot_general x0 -> x4, matrix products: none -> 2.51 us  [times(): return jnp.dot(one, two, preferred_element_type=f32)]
    pallas_call x6 -> x5, Pallas kernels: 13 us -> 11.3 us  [kernel_call(): pl.pallas_call(kernel, out_shape=out_shape, compiler_params=pltpu.Compile...]
  transfers between devices with their start and end apart: 17 -> 17, of which waited for: 13 -> 13; matrix products, arithmetic and copies ran while one was open for 2% -> 4% of each run, Pallas kernels for 7% -> 5%
where the time goes in v14:
time: 105 us
  waiting for transfers between devices  51.1 us (49%)
  starting transfers between devices  32.4 us (31%)
  Pallas kernels  11.3 us (11%)
  other arithmetic  3.42 us (3%)
  local copies, waits for them, and re-layouts  3.34 us (3%)
  matrix products  2.51 us (2%)
    ppermute x14, waiting for transfers between devices, exchange(): lax.ppermute(values, 'modes', [(i, i ^ offset) for i in range(count)])  26.1 us
    ppermute x14, starting transfers between devices, exchange(): lax.ppermute(values, 'modes', [(i, i ^ offset) for i in range(count)])  22.1 us
    all_to_all x1, waiting for transfers between devices, local(): pixels = lax.all_to_all(blocks, 'modes', 0, 0, tiled=True)  18.3 us
    pallas_call x5, Pallas kernels, kernel_call(): pl.pallas_call(kernel, out_shape=out_shape, compiler_params=pltpu.Compile...  11.3 us
    all_to_all x1, waiting for transfers between devices, local(): pieces = lax.all_to_all(term, ('modes', 'rows'), 0, 0, tiled=True)  6.03 us
    all_to_all x1, starting transfers between devices, local(): pieces = lax.all_to_all(term, ('modes', 'rows'), 0, 0, tiled=True)  5.74 us
    all_to_all x1, starting transfers between devices, local(): pixels = lax.all_to_all(blocks, 'modes', 0, 0, tiled=True)  4.47 us
    unnamed x12, local copies, waits for them, and re-layouts  2.92 us
  transfers between devices with their start and end apart: 17, of which 13 were waited for; matrix products, arithmetic and copies ran while one was open for 4% of the time, Pallas kernels for 5%

profile of v14, /device:TPU:0, one launch (start us, length us, event | category | flops | bytes accessed | tf_op | source)
XLA Modules:
  0.0 104.9 jit_solution(15246735132706835035)
XLA Ops:
  0.6 1.8 %shard_map.94 = (bf16[192,768]{1,0:T(8,128)(2,1)S(1)}, f32[192,768]{1,0:T(8,128)S(1)}, bf16[192,768]{1,0:T(8,128)(2,1)S(1)}, f32[192,768]{1,0:T(8,128)S(1)}) custom-call(bf16[384,1536]{1,0:T(8,128)(2,1)} %bitcast.84, bf16[384,1536]{1,0:T(8,128)(2,1)} %bitcast.87), custom_call_target="tpu_custom_call" | custom-call | flops 4718592 | bytes 4194304 | tf_op jit(solution)/shard_map/pallas_call | solution.py:184
  2.5 3.0 %collective-permute-start = (bf16[4,2,24,768]{3,2,0,1:T(8,128)(2,1)S(1)}, bf16[4,2,24,768]{3,2,0,1:T(8,128)(2,1)S(1)}, u32[]{:S(2)}, u32[]{:S(2)}) collective-permute-start(bf16[4,2,24,768]{3,2,0,1:T(8,128)(2,1)S(1)} %copy.17), channel_id=1, source_target_pairs={{0,2},{2,0},{4,6},{6,4},{8,10},{10,8},{12,14},{14,12},{16,18},{18,... | collective-permute-start | bytes 884744 | tf_op jit(solution)/shard_map/ppermute | solution.py:33
  5.5 1.6 %collective-permute-start.2 = (bf16[4,2,24,768]{3,2,0,1:T(8,128)(2,1)S(1)}, bf16[4,2,24,768]{3,2,0,1:T(8,128)(2,1)S(1)}, u32[]{:S(2)}, u32[]{:S(2)}) collective-permute-start(bf16[4,2,24,768]{3,2,0,1:T(8,128)(2,1)S(1)} %copy.19), channel_id=1, source_target_pairs={{0,4},{2,6},{4,0},{6,2},{8,12},{10,14},{12,8},{14,10},{16,20},{18,... | collective-permute-start | bytes 884744 | tf_op jit(solution)/shard_map/ppermute | solution.py:33
  7.1 5.4 %collective-permute-done = bf16[4,2,24,768]{3,2,0,1:T(8,128)(2,1)S(1)} collective-permute-done((bf16[4,2,24,768]{3,2,0,1:T(8,128)(2,1)S(1)}, bf16[4,2,24,768]{3,2,0,1:T(8,128)(2,1)S(1)}, u32[]{:S(2)}, u32[]{:S(2)}) %collective-permute-start) | collective-permute-done | bytes 294944 | tf_op jit(solution)/shard_map/ppermute | solution.py:33
  12.6 1.8 %collective-permute-start.1 = (bf16[4,24,768]{2,1,0:T(8,128)(2,1)S(1)}, bf16[4,24,768]{2,1,0:T(8,128)(2,1)S(1)}, u32[]{:S(2)}, u32[]{:S(2)}) collective-permute-start(bf16[4,24,768]{2,1,0:T(8,128)(2,1)S(1)} %fusion.8), channel_id=1, source_target_pairs={{0,4},{2,6},{4,0},{6,2},{8,12},{10,14},{12,8},{14,10},{16,20},{18,... | collective-permute-start | bytes 442376 | tf_op jit(solution)/shard_map/ppermute | solution.py:33
  14.5 1.6 %collective-permute-start.3 = (bf16[4,24,768]{2,1,0:T(8,128)(2,1)S(1)}, bf16[4,24,768]{2,1,0:T(8,128)(2,1)S(1)}, u32[]{:S(2)}, u32[]{:S(2)}) collective-permute-start(bf16[4,24,768]{2,1,0:T(8,128)(2,1)S(1)} %fusion.9), channel_id=1, source_target_pairs={{0,2},{2,0},{4,6},{6,4},{8,10},{10,8},{12,14},{14,12},{16,18},{18,... | collective-permute-start | bytes 442376 | tf_op jit(solution)/shard_map/ppermute | solution.py:33
  16.1 1.7 %collective-permute-done.1 = bf16[4,24,768]{2,1,0:T(8,128)(2,1)S(1)} collective-permute-done((bf16[4,24,768]{2,1,0:T(8,128)(2,1)S(1)}, bf16[4,24,768]{2,1,0:T(8,128)(2,1)S(1)}, u32[]{:S(2)}, u32[]{:S(2)}) %collective-permute-start.1) | collective-permute-done | bytes 147488 | tf_op jit(solution)/shard_map/ppermute | solution.py:33
  17.8 1.9 %collective-permute-done.3 = bf16[4,24,768]{2,1,0:T(8,128)(2,1)S(1)} collective-permute-done((bf16[4,24,768]{2,1,0:T(8,128)(2,1)S(1)}, bf16[4,24,768]{2,1,0:T(8,128)(2,1)S(1)}, u32[]{:S(2)}, u32[]{:S(2)}) %collective-permute-start.3) | collective-permute-done | bytes 147488 | tf_op jit(solution)/shard_map/ppermute | solution.py:33
  19.8 3.7 %collective-permute-start.6 = (bf16[24,1536]{1,0:T(8,128)(2,1)S(1)}, bf16[24,1536]{1,0:T(8,128)(2,1)S(1)}, u32[]{:S(2)}, u32[]{:S(2)}) collective-permute-start(bf16[24,1536]{1,0:T(8,128)(2,1)S(1)} %get-tuple-element.29), channel_id=1, source_target_pairs={{0,24},{2,26},{4,28},{6,30},{8,16},{10,18},{12,20},{14,22},{16,8},... | collective-permute-start | bytes 221192 | tf_op jit(solution)/shard_map/ppermute | solution.py:33
  23.5 0.8 collective-permute-start.4
  24.2 2.2 %collective-permute-done.6 = bf16[24,1536]{1,0:T(8,128)(2,1)S(1)} collective-permute-done((bf16[24,1536]{1,0:T(8,128)(2,1)S(1)}, bf16[24,1536]{1,0:T(8,128)(2,1)S(1)}, u32[]{:S(2)}, u32[]{:S(2)}) %collective-permute-start.6) | collective-permute-done | bytes 73760 | tf_op jit(solution)/shard_map/ppermute | solution.py:33
  26.4 2.5 %collective-permute-done.5 = bf16[24,1536]{1,0:T(8,128)(2,1)S(1)} collective-permute-done((bf16[24,1536]{1,0:T(8,128)(2,1)S(1)}, bf16[24,1536]{1,0:T(8,128)(2,1)S(1)}, u32[]{:S(2)}, u32[]{:S(2)}) %collective-permute-start.5) | collective-permute-done | bytes 73760 | tf_op jit(solution)/shard_map/ppermute | solution.py:33
  29.0 1.7 %collective-permute-start.9 = (bf16[24,1536]{1,0:T(8,128)(2,1)S(1)}, bf16[24,1536]{1,0:T(8,128)(2,1)S(1)}, u32[]{:S(2)}, u32[]{:S(2)}) collective-permute-start(bf16[24,1536]{1,0:T(8,128)(2,1)S(1)} %pad_maximum_fusion.11), channel_id=1, source_target_pairs={{0,24},{2,26},{4,28},{6,30},{8,16},{10,18},{12,20},{14,22},{16,8},... | collective-permute-start | bytes 221192 | tf_op jit(solution)/shard_map/ppermute | solution.py:33
  30.7 0.4 collective-permute-start.8
  31.1 2.4 %collective-permute-start.7 = (bf16[24,1536]{1,0:T(8,128)(2,1)S(1)}, bf16[24,1536]{1,0:T(8,128)(2,1)S(1)}, u32[]{:S(2)}, u32[]{:S(2)}) collective-permute-start(bf16[24,1536]{1,0:T(8,128)(2,1)S(1)} %pad_maximum_fusion.11), channel_id=1, source_target_pairs={{0,8},{2,10},{4,12},{6,14},{8,0},{10,2},{12,4},{14,6},{16,24},{18,... | collective-permute-start | bytes 221192 | tf_op jit(solution)/shard_map/ppermute | solution.py:33
  33.5 1.8 %collective-permute-done.9 = bf16[24,1536]{1,0:T(8,128)(2,1)S(1)} collective-permute-done((bf16[24,1536]{1,0:T(8,128)(2,1)S(1)}, bf16[24,1536]{1,0:T(8,128)(2,1)S(1)}, u32[]{:S(2)}, u32[]{:S(2)}) %collective-permute-start.9) | collective-permute-done | bytes 73760 | tf_op jit(solution)/shard_map/ppermute | solution.py:33
  35.3 1.6 %collective-permute-done.8 = bf16[24,1536]{1,0:T(8,128)(2,1)S(1)} collective-permute-done((bf16[24,1536]{1,0:T(8,128)(2,1)S(1)}, bf16[24,1536]{1,0:T(8,128)(2,1)S(1)}, u32[]{:S(2)}, u32[]{:S(2)}) %collective-permute-start.8) | collective-permute-done | bytes 73760 | tf_op jit(solution)/shard_map/ppermute | solution.py:33
  37.0 1.3 %collective-permute-start.10 = (bf16[4,24,768]{2,1,0:T(8,128)(2,1)S(1)}, bf16[4,24,768]{2,1,0:T(8,128)(2,1)S(1)}, u32[]{:S(2)}, u32[]{:S(2)}) collective-permute-start(bf16[4,24,768]{2,1,0:T(8,128)(2,1)S(1)} %get-tuple-element.33), channel_id=1, source_target_pairs={{0,4},{2,6},{4,0},{6,2},{8,12},{10,14},{12,8},{14,10},{16,20},{18,... | collective-permute-start | bytes 442376 | tf_op jit(solution)/shard_map/ppermute | solution.py:33
  38.2 0.3 bitcast_convert_fusion
  38.5 1.4 %collective-permute-start.12 = (bf16[4,24,768]{2,1,0:T(8,128)(2,1)S(1)}, bf16[4,24,768]{2,1,0:T(8,128)(2,1)S(1)}, u32[]{:S(2)}, u32[]{:S(2)}) collective-permute-start(bf16[4,24,768]{2,1,0:T(8,128)(2,1)S(1)} %get-tuple-element.32), channel_id=1, source_target_pairs={{0,2},{2,0},{4,6},{6,4},{8,10},{10,8},{12,14},{14,12},{16,18},{18,... | collective-permute-start | bytes 442376 | tf_op jit(solution)/shard_map/ppermute | solution.py:33
  40.0 3.4 %collective-permute-done.10 = bf16[4,24,768]{2,1,0:T(8,128)(2,1)S(1)} collective-permute-done((bf16[4,24,768]{2,1,0:T(8,128)(2,1)S(1)}, bf16[4,24,768]{2,1,0:T(8,128)(2,1)S(1)}, u32[]{:S(2)}, u32[]{:S(2)}) %collective-permute-start.10) | collective-permute-done | bytes 147488 | tf_op jit(solution)/shard_map/ppermute | solution.py:33
  43.4 1.6 %collective-permute-start.11 = (bf16[4,2,24,768]{3,2,1,0:T(8,128)(2,1)S(1)}, bf16[4,2,24,768]{3,2,1,0:T(8,128)(2,1)S(1)}, u32[]{:S(2)}, u32[]{:S(2)}) collective-permute-start(bf16[4,2,24,768]{3,2,1,0:T(8,128)(2,1)S(1)} %reverse_select_fusion.3), channel_id=1, source_target_pairs={{0,2},{2,0},{4,6},{6,4},{8,10},{10,8},{12,14},{14,12},{16,18},{18,... | collective-permute-start | bytes 884744 | tf_op jit(solution)/shard_map/ppermute | solution.py:33
  45.3 0.9 collective-permute-start.13
  46.2 4.0 %collective-permute-done.11 = bf16[4,2,24,768]{3,2,1,0:T(8,128)(2,1)S(1)} collective-permute-done((bf16[4,2,24,768]{3,2,1,0:T(8,128)(2,1)S(1)}, bf16[4,2,24,768]{3,2,1,0:T(8,128)(2,1)S(1)}, u32[]{:S(2)}, u32[]{:S(2)}) %collective-permute-start.11) | collective-permute-done | bytes 294944 | tf_op jit(solution)/shard_map/ppermute | solution.py:33
  50.3 0.1 reverse_select_fusion.1
  50.4 1.6 %collective-permute-done.13 = bf16[4,2,24,768]{3,2,0,1:T(8,128)(2,1)S(1)} collective-permute-done((bf16[4,2,24,768]{3,2,0,1:T(8,128)(2,1)S(1)}, bf16[4,2,24,768]{3,2,0,1:T(8,128)(2,1)S(1)}, u32[]{:S(2)}, u32[]{:S(2)}) %collective-permute-start.13) | collective-permute-done | bytes 294944 | tf_op jit(solution)/shard_map/ppermute | solution.py:33
  52.1 0.1 reverse_select_fusion
  52.3 0.1 fusion.25
  52.4 0.4 fusion.5
  52.8 0.1 pad_maximum_fusion.1.shaped_ref
  53.0 1.1 %copy-done.3 = bf16[768,768]{1,0:T(8,128)(2,1)S(1)} copy-done((bf16[768,768]{1,0:T(8,128)(2,1)S(1)}, bf16[768,768]{1,0:T(8,128)(2,1)}, u32[]{:S(2)}) %copy-start.3) | copy-done | bytes 1179672
  54.1 1.1 %shard_map.95.own_ref = f32[768,768]{1,0:T(8,128)S(1)} custom-call(bf16[768,768]{1,0:T(8,128)(2,1)S(1)} %copy-done.3, bf16[768,768]{1,0:T(8,128)(2,1)S(1)} %pad_maximum_fusion.1.shaped_ref), custom_call_target="tpu_custom_call" | custom-call | flops 905969664 | bytes 4194304 | tf_op jit(solution)/shard_map/pallas_call | solution.py:184
  55.2 0.7 collective-permute-done.14.shaped_ref
  55.8 2.1 %shard_map.96.refs_0_ = bf16[768,768]{1,0:T(8,128)(2,1)} custom-call(bf16[768,768]{1,0:T(8,128)(2,1)S(1)} %copy-done.2, bf16[768,768]{1,0:T(8,128)(2,1)S(1)} %collective-permute-done.14.shaped_ref, f32[768,768]{1,0:T(8,128)S(1)} %shard_map.95.own_ref), custom_call_target="tpu_custom_call" | custom-call | flops 905969664 | bytes 4194304 | tf_op jit(solution)/shard_map/pallas_call | solution.py:184
  57.9 4.5 %all-to-all-start = ((bf16[16,48,768]{2,1,0:T(8,128)(2,1)}), bf16[16,48,768]{2,1,0:T(8,128)(2,1)S(1)}, u32[]{:S(2)}, u32[]{:S(2)}) async-start(bf16[16,48,768]{2,1,0:T(8,128)(2,1)} %bitcast.33), calls=%async_computation | async-start | bytes 2359296 | tf_op jit(solution)/shard_map/all_to_all | solution.py:297
  62.5 1.2 %copy-done.1 = bf16[768,768]{1,0:T(8,128)(2,1)S(1)} copy-done((bf16[768,768]{1,0:T(8,128)(2,1)S(1)}, bf16[768,768]{1,0:T(8,128)(2,1)}, u32[]{:S(2)}) %copy-start.1) | copy-done | bytes 1179672
  63.7 0.6 fusion.28
  64.3 0.6 fusion.27
  65.0 0.6 copy-done
  65.6 0.6 fusion.2
  66.2 0.6 fusion.3
  67.0 4.3 %shard_map.97 = bf16[384,1536]{1,0:T(8,128)(2,1)} custom-call(bf16[768,768]{1,0:T(8,128)(2,1)} %shard_map.96.refs_0_, bf16[768,768]{1,0:T(8,128)(2,1)S(1)} %copy-done.1, bf16[768,768]{1,0:T(8,128)(2,1)S(1)} %copy-done), custom_call_target="tpu_custom_call" | custom-call | flops 1811939328 | bytes 4194304 | tf_op jit(solution)/shard_map/pallas_call | solution.py:184
  71.2 18.3 %all-to-all-done = bf16[16,48,768]{2,1,0:T(8,128)(2,1)S(1)} async-done(((bf16[16,48,768]{2,1,0:T(8,128)(2,1)}), bf16[16,48,768]{2,1,0:T(8,128)(2,1)S(1)}, u32[]{:S(2)}, u32[]{:S(2)}) %all-to-all-start) | async-done | bytes 1179680 | tf_op jit(solution)/shard_map/all_to_all | solution.py:297
  89.5 2.0 %shard_map.98 = f32[32,16]{1,0:T(8,128)} custom-call(bf16[768,768]{1,0:T(8,128)(2,1)S(1)} %bitcast.75, bf16[768,768]{1,0:T(8,128)(2,1)S(1)} %pad_maximum_fusion.2.refs_1_), custom_call_target="tpu_custom_call" | custom-call | flops 1811939328 | bytes 4194304 | tf_op jit(solution)/shard_map/pallas_call | solution.py:184
  91.5 5.7 %all-to-all-start.1 = ((f32[32,1,16]{2,1,0:T(1,128)}), f32[32,1,16]{2,1,0:T(1,128)S(1)}, u32[]{:S(2)}, u32[]{:S(2)}) async-start(f32[32,1,16]{2,1,0:T(1,128)} %bitcast.41), calls=%async_computation.1 | async-start | bytes 32768 | tf_op jit(solution)/shard_map/all_to_all | solution.py:322
  97.2 1.1 %pad_maximum_fusion = bf16[384,1536]{1,0:T(8,128)(2,1)} fusion(bf16[384,384]{1,0:T(8,128)(2,1)S(1)} %get-tuple-element.42, bf16[384,384]{1,0:T(8,128)(2,1)S(1)} %get-tuple-element.24, bf16[384,384]{1,0:T(8,128)(2,1)S(1)} %get-tuple-element.43, bf16[384,384]{1,0:T(8,128)(2,1)S(1)} %get-tuple-element.23), kind=kLoop, calls=%fused_computation.14 | loop fusion | flops 4718592 | bytes 2359296 | tf_op jit(solution)/shard_map/concatenate | solution.py:267
  98.4 6.0 %all-to-all-done.1 = f32[32,1,16]{2,1,0:T(1,128)S(1)} async-done(((f32[32,1,16]{2,1,0:T(1,128)}), f32[32,1,16]{2,1,0:T(1,128)S(1)}, u32[]{:S(2)}, u32[]{:S(2)}) %all-to-all-start.1) | async-done | bytes 2080 | tf_op jit(solution)/shard_map/all_to_all | solution.py:322
  104.4 0.6 reduce_sum.9
  (42 shorter events, 1.2 us)
Async XLA Ops:
  2.5 10.0 %collective-permute-start = (bf16[4,2,24,768]{3,2,0,1:T(8,128)(2,1)S(1)}, bf16[4,2,24,768]{3,2,0,1:T(8,128)(2,1)S(1)}, u32[]{:S(2)}, u32[]{:S(2)}) collective-permute-start(bf16[4,2,24,768]{3,2,0,1:T(8,128)(2,1)S(1)} %copy.17), channel_id=1, source_target_pairs={{0,2},{2,0},{4,6},{6,4},{8,10},{10,8},{12,14},{14,12},{16,18},{18,... | collective-permute-start | bytes 884744 | tf_op jit(solution)/shard_map/ppermute | solution.py:33
  5.5 8.9 %collective-permute-start.2 = (bf16[4,2,24,768]{3,2,0,1:T(8,128)(2,1)S(1)}, bf16[4,2,24,768]{3,2,0,1:T(8,128)(2,1)S(1)}, u32[]{:S(2)}, u32[]{:S(2)}) collective-permute-start(bf16[4,2,24,768]{3,2,0,1:T(8,128)(2,1)S(1)} %copy.19), channel_id=1, source_target_pairs={{0,4},{2,6},{4,0},{6,2},{8,12},{10,14},{12,8},{14,10},{16,20},{18,... | collective-permute-start | bytes 884744 | tf_op jit(solution)/shard_map/ppermute | solution.py:33
  12.6 5.2 %collective-permute-start.1 = (bf16[4,24,768]{2,1,0:T(8,128)(2,1)S(1)}, bf16[4,24,768]{2,1,0:T(8,128)(2,1)S(1)}, u32[]{:S(2)}, u32[]{:S(2)}) collective-permute-start(bf16[4,24,768]{2,1,0:T(8,128)(2,1)S(1)} %fusion.8), channel_id=1, source_target_pairs={{0,4},{2,6},{4,0},{6,2},{8,12},{10,14},{12,8},{14,10},{16,20},{18,... | collective-permute-start | bytes 442376 | tf_op jit(solution)/shard_map/ppermute | solution.py:33
  14.5 5.2 %collective-permute-start.3 = (bf16[4,24,768]{2,1,0:T(8,128)(2,1)S(1)}, bf16[4,24,768]{2,1,0:T(8,128)(2,1)S(1)}, u32[]{:S(2)}, u32[]{:S(2)}) collective-permute-start(bf16[4,24,768]{2,1,0:T(8,128)(2,1)S(1)} %fusion.9), channel_id=1, source_target_pairs={{0,2},{2,0},{4,6},{6,4},{8,10},{10,8},{12,14},{14,12},{16,18},{18,... | collective-permute-start | bytes 442376 | tf_op jit(solution)/shard_map/ppermute | solution.py:33
  19.8 6.6 %collective-permute-start.6 = (bf16[24,1536]{1,0:T(8,128)(2,1)S(1)}, bf16[24,1536]{1,0:T(8,128)(2,1)S(1)}, u32[]{:S(2)}, u32[]{:S(2)}) collective-permute-start(bf16[24,1536]{1,0:T(8,128)(2,1)S(1)} %get-tuple-element.29), channel_id=1, source_target_pairs={{0,24},{2,26},{4,28},{6,30},{8,16},{10,18},{12,20},{14,22},{16,8},... | collective-permute-start | bytes 221192 | tf_op jit(solution)/shard_map/ppermute | solution.py:33
  23.5 5.5 %collective-permute-start.5 = (bf16[24,1536]{1,0:T(8,128)(2,1)S(1)}, bf16[24,1536]{1,0:T(8,128)(2,1)S(1)}, u32[]{:S(2)}, u32[]{:S(2)}) collective-permute-start(bf16[24,1536]{1,0:T(8,128)(2,1)S(1)} %get-tuple-element.28), channel_id=1, source_target_pairs={{0,16},{2,18},{4,20},{6,22},{8,24},{10,26},{12,28},{14,30},{16,0},... | collective-permute-start | bytes 221192 | tf_op jit(solution)/shard_map/ppermute | solution.py:33
  23.5 5.5 %collective-permute-start.4 = (bf16[24,1536]{1,0:T(8,128)(2,1)S(1)}, bf16[24,1536]{1,0:T(8,128)(2,1)S(1)}, u32[]{:S(2)}, u32[]{:S(2)}) collective-permute-start(bf16[24,1536]{1,0:T(8,128)(2,1)S(1)} %get-tuple-element.27), channel_id=1, source_target_pairs={{0,8},{2,10},{4,12},{6,14},{8,0},{10,2},{12,4},{14,6},{16,24},{18,... | collective-permute-start | bytes 221192 | tf_op jit(solution)/shard_map/ppermute | solution.py:33
  29.0 6.2 %collective-permute-start.9 = (bf16[24,1536]{1,0:T(8,128)(2,1)S(1)}, bf16[24,1536]{1,0:T(8,128)(2,1)S(1)}, u32[]{:S(2)}, u32[]{:S(2)}) collective-permute-start(bf16[24,1536]{1,0:T(8,128)(2,1)S(1)} %pad_maximum_fusion.11), channel_id=1, source_target_pairs={{0,24},{2,26},{4,28},{6,30},{8,16},{10,18},{12,20},{14,22},{16,8},... | collective-permute-start | bytes 221192 | tf_op jit(solution)/shard_map/ppermute | solution.py:33
  30.7 6.1 %collective-permute-start.8 = (bf16[24,1536]{1,0:T(8,128)(2,1)S(1)}, bf16[24,1536]{1,0:T(8,128)(2,1)S(1)}, u32[]{:S(2)}, u32[]{:S(2)}) collective-permute-start(bf16[24,1536]{1,0:T(8,128)(2,1)S(1)} %pad_maximum_fusion.11), channel_id=1, source_target_pairs={{0,16},{2,18},{4,20},{6,22},{8,24},{10,26},{12,28},{14,30},{16,0},... | collective-permute-start | bytes 221192 | tf_op jit(solution)/shard_map/ppermute | solution.py:33
  31.1 5.8 %collective-permute-start.7 = (bf16[24,1536]{1,0:T(8,128)(2,1)S(1)}, bf16[24,1536]{1,0:T(8,128)(2,1)S(1)}, u32[]{:S(2)}, u32[]{:S(2)}) collective-permute-start(bf16[24,1536]{1,0:T(8,128)(2,1)S(1)} %pad_maximum_fusion.11), channel_id=1, source_target_pairs={{0,8},{2,10},{4,12},{6,14},{8,0},{10,2},{12,4},{14,6},{16,24},{18,... | collective-permute-start | bytes 221192 | tf_op jit(solution)/shard_map/ppermute | solution.py:33
  36.8 1.4 %copy-start.4 = (bf16[1,384,1536]{2,1,0:T(8,128)(2,1)S(1)}, bf16[1,384,1536]{2,1,0:T(8,128)(2,1)}, u32[]{:S(2)}) copy-start(bf16[1,384,1536]{2,1,0:T(8,128)(2,1)} %param.7) | copy-start | bytes 3538948
  37.0 6.4 %collective-permute-start.10 = (bf16[4,24,768]{2,1,0:T(8,128)(2,1)S(1)}, bf16[4,24,768]{2,1,0:T(8,128)(2,1)S(1)}, u32[]{:S(2)}, u32[]{:S(2)}) collective-permute-start(bf16[4,24,768]{2,1,0:T(8,128)(2,1)S(1)} %get-tuple-element.33), channel_id=1, source_target_pairs={{0,4},{2,6},{4,0},{6,2},{8,12},{10,14},{12,8},{14,10},{16,20},{18,... | collective-permute-start | bytes 442376 | tf_op jit(solution)/shard_map/ppermute | solution.py:33
  38.5 6.6 %collective-permute-start.12 = (bf16[4,24,768]{2,1,0:T(8,128)(2,1)S(1)}, bf16[4,24,768]{2,1,0:T(8,128)(2,1)S(1)}, u32[]{:S(2)}, u32[]{:S(2)}) collective-permute-start(bf16[4,24,768]{2,1,0:T(8,128)(2,1)S(1)} %get-tuple-element.32), channel_id=1, source_target_pairs={{0,2},{2,0},{4,6},{6,4},{8,10},{10,8},{12,14},{14,12},{16,18},{18,... | collective-permute-start | bytes 442376 | tf_op jit(solution)/shard_map/ppermute | solution.py:33
  43.4 6.8 %collective-permute-start.11 = (bf16[4,2,24,768]{3,2,1,0:T(8,128)(2,1)S(1)}, bf16[4,2,24,768]{3,2,1,0:T(8,128)(2,1)S(1)}, u32[]{:S(2)}, u32[]{:S(2)}) collective-permute-start(bf16[4,2,24,768]{3,2,1,0:T(8,128)(2,1)S(1)} %reverse_select_fusion.3), channel_id=1, source_target_pairs={{0,2},{2,0},{4,6},{6,4},{8,10},{10,8},{12,14},{14,12},{16,18},{18,... | collective-permute-start | bytes 884744 | tf_op jit(solution)/shard_map/ppermute | solution.py:33
  45.3 6.8 %collective-permute-start.13 = (bf16[4,2,24,768]{3,2,0,1:T(8,128)(2,1)S(1)}, bf16[4,2,24,768]{3,2,0,1:T(8,128)(2,1)S(1)}, u32[]{:S(2)}, u32[]{:S(2)}) collective-permute-start(bf16[4,2,24,768]{3,2,0,1:T(8,128)(2,1)S(1)} %reverse_select_fusion.2), channel_id=1, source_target_pairs={{0,4},{2,6},{4,0},{6,2},{8,12},{10,14},{12,8},{14,10},{16,20},{18,... | collective-permute-start | bytes 884744 | tf_op jit(solution)/shard_map/ppermute | solution.py:33
  52.8 1.3 %copy-start.3 = (bf16[768,768]{1,0:T(8,128)(2,1)S(1)}, bf16[768,768]{1,0:T(8,128)(2,1)}, u32[]{:S(2)}) copy-start(bf16[768,768]{1,0:T(8,128)(2,1)} %constant.107.clone.table_ref) | copy-start | bytes 3538948
  52.9 2.9 %copy-start.2 = (bf16[768,768]{1,0:T(8,128)(2,1)S(1)}, bf16[768,768]{1,0:T(8,128)(2,1)}, u32[]{:S(2)}) copy-start(bf16[768,768]{1,0:T(8,128)(2,1)} %constant.108.clone.table_ref) | copy-start | bytes 3538948
  52.9 2.9 %collective-permute-start.14 = (bf16[768,768]{1,0:T(8,128)(2,1)S(1)}, bf16[768,768]{1,0:T(8,128)(2,1)S(1)}, u32[]{:S(2)}, u32[]{:S(2)}) collective-permute-start(bf16[768,768]{1,0:T(8,128)(2,1)S(1)} %pad_maximum_fusion.1.shaped_ref), channel_id=1, source_target_pairs={{0,1},{1,0},{2,3},{3,2},{4,5},{5,4},{6,7},{7,6},{8,9},{9,8},{10,11... | collective-permute-start | bytes 3538952 | tf_op jit(solution)/shard_map/ppermute | solution.py:275
  57.9 4.5 %copy-start.5 = (bf16[2,16,24,768]{3,2,1,0:T(8,128)(2,1)S(1)}, bf16[2,16,24,768]{3,2,1,0:T(8,128)(2,1)}, u32[]{:S(2)}) copy-start(bf16[2,16,24,768]{3,2,1,0:T(8,128)(2,1)} %param.9) | copy-start | bytes 3538948
  57.9 31.6 %all-to-all-start = ((bf16[16,48,768]{2,1,0:T(8,128)(2,1)}), bf16[16,48,768]{2,1,0:T(8,128)(2,1)S(1)}, u32[]{:S(2)}, u32[]{:S(2)}) async-start(bf16[16,48,768]{2,1,0:T(8,128)(2,1)} %bitcast.33), calls=%async_computation | async-start | bytes 2359296 | tf_op jit(solution)/shard_map/all_to_all | solution.py:297
  62.4 1.3 %copy-start.1 = (bf16[768,768]{1,0:T(8,128)(2,1)S(1)}, bf16[768,768]{1,0:T(8,128)(2,1)}, u32[]{:S(2)}) copy-start(bf16[768,768]{1,0:T(8,128)(2,1)} %constant.105.clone.refs_1_) | copy-start | bytes 3538948
  64.3 1.3 %copy-start = (bf16[768,768]{1,0:T(8,128)(2,1)S(1)}, bf16[768,768]{1,0:T(8,128)(2,1)}, u32[]{:S(2)}) copy-start(bf16[768,768]{1,0:T(8,128)(2,1)} %constant.106.clone.refs_2_) | copy-start | bytes 3538948
  91.5 12.9 %all-to-all-start.1 = ((f32[32,1,16]{2,1,0:T(1,128)}), f32[32,1,16]{2,1,0:T(1,128)S(1)}, u32[]{:S(2)}, u32[]{:S(2)}) async-start(f32[32,1,16]{2,1,0:T(1,128)} %bitcast.41), calls=%async_computation.1 | async-start | bytes 32768 | tf_op jit(solution)/shard_map/all_to_all | solution.py:322

commit v15 on v14

--- a/solution.py
+++ b/solution.py
@@ -109,8 +109,18 @@
     out_ref[...] = times(table_ref[...], shaped_ref[...])
 
 
-def other_kernel(table_ref, shaped_ref, own_ref, out_ref):
-    out_ref[...] = (own_ref[...] + times(table_ref[...], shaped_ref[...])).astype(bf16)
+def other_kernel(table_ref, shaped_ref, own_ref, out_hbm, held, sems):
+    half, piece = held.shape[0] // 2, held.shape[0] // 8
+    copies = []
+    for start in (0, half):
+        at = pl.ds(start, half)
+        held[at] = (own_ref[at] + times(table_ref[at], shaped_ref[...])).astype(bf16)
+        for first in range(start, start + half, piece):
+            rows = pl.ds(first, piece)
+            copies.append(pltpu.make_async_copy(held.at[rows], out_hbm.at[rows], sems.at[len(copies)]))
+            copies[-1].start()
+    for copy in copies:
+        copy.wait()
 
 
 def fields_kernel(block_rows, columns_ref, re_ref, im_ref, out_ref):
@@ -151,9 +161,7 @@
         fields_ref[...], targets_ref[...], (((1,), (1,)), ((), ())), preferred_element_type=f32
     )
     left, right = product.shape
-    row = lax.broadcasted_iota(jnp.int32, (left, right), 0) % block_rows
-    col = lax.broadcasted_iota(jnp.int32, (left, right), 1) % block_rows
-    product = jnp.where(row == col, product, 0.0)
+    col = lax.broadcasted_iota(jnp.int32, (1, right), 1) % block_rows
 
     def groups(size):
         member = lax.broadcasted_iota(jnp.int32, (size // block_rows, size), 1) // block_rows
@@ -161,9 +169,12 @@
         return jnp.where(member == group, 1.0, 0.0).astype(f32)
 
     if block_rows % 8 == 0:
-        product = jnp.sum(product.reshape(left // block_rows, block_rows, right), 1)
+        product = product.reshape(left // block_rows, block_rows, right)
+        same = lax.broadcasted_iota(jnp.int32, (block_rows, right), 0) == col
+        product = jnp.sum(jnp.where(same[None], product, 0.0), 1)
     else:
-        product = exactly(groups(left), product, ((1,), (0,)))
+        same = lax.broadcasted_iota(jnp.int32, (left, 1), 0) % block_rows == col
+        product = exactly(groups(left), jnp.where(same, product, 0.0), ((1,), (0,)))
     product = product.reshape(modes, 2, right)
     real, imag = product[:, 0], product[:, 1]
     right = right // 2
@@ -290,7 +301,9 @@
     )
     columns, other = lax.optimization_barrier((columns, other))
     columns = kernel_call(
-        other_kernel, column_shape, bf16, matmul // 2, (table(slice(local_rows, None)), other, columns)
+        other_kernel, column_shape, bf16, matmul // 2, (table(slice(local_rows, None)), other, columns),
+        out_specs=pl.BlockSpec(memory_space=pltpu.HBM),
+        scratch_shapes=[pltpu.VMEM(column_shape, bf16), pltpu.SemaphoreType.DMA((8,))],
     )
     blocks = columns.reshape(owners, 2, -1, block_rows, grid_size).transpose(0, 2, 1, 3, 4)
     blocks = blocks.reshape(count, 2 * block_rows, grid_size)

time: 105 us -> 105 us (level)
  no operation moved by 1% of the time
where the time goes in v15:
time: 105 us
  waiting for transfers between devices  51.1 us (49%)
  starting transfers between devices  32.4 us (31%)
  Pallas kernels  11.1 us (11%)
  other arithmetic  3.42 us (3%)
  local copies, waits for them, and re-layouts  3.34 us (3%)
  matrix products  2.51 us (2%)
    ppermute x14, waiting for transfers between devices, exchange(): lax.ppermute(values, 'modes', [(i, i ^ offset) for i in range(count)])  26.1 us
    ppermute x14, starting transfers between devices, exchange(): lax.ppermute(values, 'modes', [(i, i ^ offset) for i in range(count)])  22.1 us
    all_to_all x1, waiting for transfers between devices, local(): pixels = lax.all_to_all(blocks, 'modes', 0, 0, tiled=True)  18.3 us
    pallas_call x5, Pallas kernels, kernel_call(): pl.pallas_call(kernel, out_shape=out_shape, compiler_params=pltpu.Compile...  11.1 us
    all_to_all x1, waiting for transfers between devices, local(): pieces = lax.all_to_all(term, ('modes', 'rows'), 0, 0, tiled=True)  6.03 us
    all_to_all x1, starting transfers between devices, local(): pieces = lax.all_to_all(term, ('modes', 'rows'), 0, 0, tiled=True)  5.74 us
    all_to_all x1, starting transfers between devices, local(): pixels = lax.all_to_all(blocks, 'modes', 0, 0, tiled=True)  4.48 us
    unnamed x12, local copies, waits for them, and re-layouts  2.92 us
  transfers between devices with their start and end apart: 17, of which 13 were waited for; matrix products, arithmetic and copies ran while one was open for 4% of the time, Pallas kernels for 5%

profile of v15, /device:TPU:0, one launch (start us, length us, event | category | flops | bytes accessed | tf_op | source)
XLA Modules:
  0.0 104.8 jit_solution(3013903329710109202)
XLA Ops:
  0.6 1.8 %shard_map.94 = (bf16[192,768]{1,0:T(8,128)(2,1)S(1)}, f32[192,768]{1,0:T(8,128)S(1)}, bf16[192,768]{1,0:T(8,128)(2,1)S(1)}, f32[192,768]{1,0:T(8,128)S(1)}) custom-call(bf16[384,1536]{1,0:T(8,128)(2,1)} %bitcast.84, bf16[384,1536]{1,0:T(8,128)(2,1)} %bitcast.87), custom_call_target="tpu_custom_call" | custom-call | flops 4718592 | bytes 4194304 | tf_op jit(solution)/shard_map/pallas_call | solution.py:195
  2.5 3.0 %collective-permute-start = (bf16[4,2,24,768]{3,2,0,1:T(8,128)(2,1)S(1)}, bf16[4,2,24,768]{3,2,0,1:T(8,128)(2,1)S(1)}, u32[]{:S(2)}, u32[]{:S(2)}) collective-permute-start(bf16[4,2,24,768]{3,2,0,1:T(8,128)(2,1)S(1)} %copy.17), channel_id=1, source_target_pairs={{0,2},{2,0},{4,6},{6,4},{8,10},{10,8},{12,14},{14,12},{16,18},{18,... | collective-permute-start | bytes 884744 | tf_op jit(solution)/shard_map/ppermute | solution.py:33
  5.5 1.6 %collective-permute-start.2 = (bf16[4,2,24,768]{3,2,0,1:T(8,128)(2,1)S(1)}, bf16[4,2,24,768]{3,2,0,1:T(8,128)(2,1)S(1)}, u32[]{:S(2)}, u32[]{:S(2)}) collective-permute-start(bf16[4,2,24,768]{3,2,0,1:T(8,128)(2,1)S(1)} %copy.19), channel_id=1, source_target_pairs={{0,4},{2,6},{4,0},{6,2},{8,12},{10,14},{12,8},{14,10},{16,20},{18,... | collective-permute-start | bytes 884744 | tf_op jit(solution)/shard_map/ppermute | solution.py:33
  7.1 5.4 %collective-permute-done = bf16[4,2,24,768]{3,2,0,1:T(8,128)(2,1)S(1)} collective-permute-done((bf16[4,2,24,768]{3,2,0,1:T(8,128)(2,1)S(1)}, bf16[4,2,24,768]{3,2,0,1:T(8,128)(2,1)S(1)}, u32[]{:S(2)}, u32[]{:S(2)}) %collective-permute-start) | collective-permute-done | bytes 294944 | tf_op jit(solution)/shard_map/ppermute | solution.py:33
  12.6 1.8 %collective-permute-start.1 = (bf16[4,24,768]{2,1,0:T(8,128)(2,1)S(1)}, bf16[4,24,768]{2,1,0:T(8,128)(2,1)S(1)}, u32[]{:S(2)}, u32[]{:S(2)}) collective-permute-start(bf16[4,24,768]{2,1,0:T(8,128)(2,1)S(1)} %fusion.8), channel_id=1, source_target_pairs={{0,4},{2,6},{4,0},{6,2},{8,12},{10,14},{12,8},{14,10},{16,20},{18,... | collective-permute-start | bytes 442376 | tf_op jit(solution)/shard_map/ppermute | solution.py:33
  14.5 1.6 %collective-permute-start.3 = (bf16[4,24,768]{2,1,0:T(8,128)(2,1)S(1)}, bf16[4,24,768]{2,1,0:T(8,128)(2,1)S(1)}, u32[]{:S(2)}, u32[]{:S(2)}) collective-permute-start(bf16[4,24,768]{2,1,0:T(8,128)(2,1)S(1)} %fusion.9), channel_id=1, source_target_pairs={{0,2},{2,0},{4,6},{6,4},{8,10},{10,8},{12,14},{14,12},{16,18},{18,... | collective-permute-start | bytes 442376 | tf_op jit(solution)/shard_map/ppermute | solution.py:33
  16.1 1.7 %collective-permute-done.1 = bf16[4,24,768]{2,1,0:T(8,128)(2,1)S(1)} collective-permute-done((bf16[4,24,768]{2,1,0:T(8,128)(2,1)S(1)}, bf16[4,24,768]{2,1,0:T(8,128)(2,1)S(1)}, u32[]{:S(2)}, u32[]{:S(2)}) %collective-permute-start.1) | collective-permute-done | bytes 147488 | tf_op jit(solution)/shard_map/ppermute | solution.py:33
  17.8 1.9 %collective-permute-done.3 = bf16[4,24,768]{2,1,0:T(8,128)(2,1)S(1)} collective-permute-done((bf16[4,24,768]{2,1,0:T(8,128)(2,1)S(1)}, bf16[4,24,768]{2,1,0:T(8,128)(2,1)S(1)}, u32[]{:S(2)}, u32[]{:S(2)}) %collective-permute-start.3) | collective-permute-done | bytes 147488 | tf_op jit(solution)/shard_map/ppermute | solution.py:33
  19.8 3.7 %collective-permute-start.6 = (bf16[24,1536]{1,0:T(8,128)(2,1)S(1)}, bf16[24,1536]{1,0:T(8,128)(2,1)S(1)}, u32[]{:S(2)}, u32[]{:S(2)}) collective-permute-start(bf16[24,1536]{1,0:T(8,128)(2,1)S(1)} %get-tuple-element.29), channel_id=1, source_target_pairs={{0,24},{2,26},{4,28},{6,30},{8,16},{10,18},{12,20},{14,22},{16,8},... | collective-permute-start | bytes 221192 | tf_op jit(solution)/shard_map/ppermute | solution.py:33
  23.5 0.8 collective-permute-start.4
  24.2 2.2 %collective-permute-done.6 = bf16[24,1536]{1,0:T(8,128)(2,1)S(1)} collective-permute-done((bf16[24,1536]{1,0:T(8,128)(2,1)S(1)}, bf16[24,1536]{1,0:T(8,128)(2,1)S(1)}, u32[]{:S(2)}, u32[]{:S(2)}) %collective-permute-start.6) | collective-permute-done | bytes 73760 | tf_op jit(solution)/shard_map/ppermute | solution.py:33
  26.4 2.5 %collective-permute-done.5 = bf16[24,1536]{1,0:T(8,128)(2,1)S(1)} collective-permute-done((bf16[24,1536]{1,0:T(8,128)(2,1)S(1)}, bf16[24,1536]{1,0:T(8,128)(2,1)S(1)}, u32[]{:S(2)}, u32[]{:S(2)}) %collective-permute-start.5) | collective-permute-done | bytes 73760 | tf_op jit(solution)/shard_map/ppermute | solution.py:33
  29.0 1.7 %collective-permute-start.9 = (bf16[24,1536]{1,0:T(8,128)(2,1)S(1)}, bf16[24,1536]{1,0:T(8,128)(2,1)S(1)}, u32[]{:S(2)}, u32[]{:S(2)}) collective-permute-start(bf16[24,1536]{1,0:T(8,128)(2,1)S(1)} %pad_maximum_fusion.11), channel_id=1, source_target_pairs={{0,24},{2,26},{4,28},{6,30},{8,16},{10,18},{12,20},{14,22},{16,8},... | collective-permute-start | bytes 221192 | tf_op jit(solution)/shard_map/ppermute | solution.py:33
  30.7 0.4 collective-permute-start.8
  31.1 2.4 %collective-permute-start.7 = (bf16[24,1536]{1,0:T(8,128)(2,1)S(1)}, bf16[24,1536]{1,0:T(8,128)(2,1)S(1)}, u32[]{:S(2)}, u32[]{:S(2)}) collective-permute-start(bf16[24,1536]{1,0:T(8,128)(2,1)S(1)} %pad_maximum_fusion.11), channel_id=1, source_target_pairs={{0,8},{2,10},{4,12},{6,14},{8,0},{10,2},{12,4},{14,6},{16,24},{18,... | collective-permute-start | bytes 221192 | tf_op jit(solution)/shard_map/ppermute | solution.py:33
  33.5 1.8 %collective-permute-done.9 = bf16[24,1536]{1,0:T(8,128)(2,1)S(1)} collective-permute-done((bf16[24,1536]{1,0:T(8,128)(2,1)S(1)}, bf16[24,1536]{1,0:T(8,128)(2,1)S(1)}, u32[]{:S(2)}, u32[]{:S(2)}) %collective-permute-start.9) | collective-permute-done | bytes 73760 | tf_op jit(solution)/shard_map/ppermute | solution.py:33
  35.3 1.6 %collective-permute-done.8 = bf16[24,1536]{1,0:T(8,128)(2,1)S(1)} collective-permute-done((bf16[24,1536]{1,0:T(8,128)(2,1)S(1)}, bf16[24,1536]{1,0:T(8,128)(2,1)S(1)}, u32[]{:S(2)}, u32[]{:S(2)}) %collective-permute-start.8) | collective-permute-done | bytes 73760 | tf_op jit(solution)/shard_map/ppermute | solution.py:33
  37.0 1.3 %collective-permute-start.10 = (bf16[4,24,768]{2,1,0:T(8,128)(2,1)S(1)}, bf16[4,24,768]{2,1,0:T(8,128)(2,1)S(1)}, u32[]{:S(2)}, u32[]{:S(2)}) collective-permute-start(bf16[4,24,768]{2,1,0:T(8,128)(2,1)S(1)} %get-tuple-element.33), channel_id=1, source_target_pairs={{0,4},{2,6},{4,0},{6,2},{8,12},{10,14},{12,8},{14,10},{16,20},{18,... | collective-permute-start | bytes 442376 | tf_op jit(solution)/shard_map/ppermute | solution.py:33
  38.2 0.3 bitcast_convert_fusion
  38.5 1.4 %collective-permute-start.12 = (bf16[4,24,768]{2,1,0:T(8,128)(2,1)S(1)}, bf16[4,24,768]{2,1,0:T(8,128)(2,1)S(1)}, u32[]{:S(2)}, u32[]{:S(2)}) collective-permute-start(bf16[4,24,768]{2,1,0:T(8,128)(2,1)S(1)} %get-tuple-element.32), channel_id=1, source_target_pairs={{0,2},{2,0},{4,6},{6,4},{8,10},{10,8},{12,14},{14,12},{16,18},{18,... | collective-permute-start | bytes 442376 | tf_op jit(solution)/shard_map/ppermute | solution.py:33
  40.0 3.4 %collective-permute-done.10 = bf16[4,24,768]{2,1,0:T(8,128)(2,1)S(1)} collective-permute-done((bf16[4,24,768]{2,1,0:T(8,128)(2,1)S(1)}, bf16[4,24,768]{2,1,0:T(8,128)(2,1)S(1)}, u32[]{:S(2)}, u32[]{:S(2)}) %collective-permute-start.10) | collective-permute-done | bytes 147488 | tf_op jit(solution)/shard_map/ppermute | solution.py:33
  43.4 1.6 %collective-permute-start.11 = (bf16[4,2,24,768]{3,2,1,0:T(8,128)(2,1)S(1)}, bf16[4,2,24,768]{3,2,1,0:T(8,128)(2,1)S(1)}, u32[]{:S(2)}, u32[]{:S(2)}) collective-permute-start(bf16[4,2,24,768]{3,2,1,0:T(8,128)(2,1)S(1)} %reverse_select_fusion.3), channel_id=1, source_target_pairs={{0,2},{2,0},{4,6},{6,4},{8,10},{10,8},{12,14},{14,12},{16,18},{18,... | collective-permute-start | bytes 884744 | tf_op jit(solution)/shard_map/ppermute | solution.py:33
  45.3 0.9 collective-permute-start.13
  46.2 4.0 %collective-permute-done.11 = bf16[4,2,24,768]{3,2,1,0:T(8,128)(2,1)S(1)} collective-permute-done((bf16[4,2,24,768]{3,2,1,0:T(8,128)(2,1)S(1)}, bf16[4,2,24,768]{3,2,1,0:T(8,128)(2,1)S(1)}, u32[]{:S(2)}, u32[]{:S(2)}) %collective-permute-start.11) | collective-permute-done | bytes 294944 | tf_op jit(solution)/shard_map/ppermute | solution.py:33
  50.3 0.1 reverse_select_fusion.1
  50.4 1.6 %collective-permute-done.13 = bf16[4,2,24,768]{3,2,0,1:T(8,128)(2,1)S(1)} collective-permute-done((bf16[4,2,24,768]{3,2,0,1:T(8,128)(2,1)S(1)}, bf16[4,2,24,768]{3,2,0,1:T(8,128)(2,1)S(1)}, u32[]{:S(2)}, u32[]{:S(2)}) %collective-permute-start.13) | collective-permute-done | bytes 294944 | tf_op jit(solution)/shard_map/ppermute | solution.py:33
  52.1 0.1 reverse_select_fusion
  52.3 0.1 fusion.25
  52.4 0.4 fusion.5
  53.0 1.1 %copy-done.3 = bf16[768,768]{1,0:T(8,128)(2,1)S(1)} copy-done((bf16[768,768]{1,0:T(8,128)(2,1)S(1)}, bf16[768,768]{1,0:T(8,128)(2,1)}, u32[]{:S(2)}) %copy-start.3) | copy-done | bytes 1179672
  54.1 1.1 %shard_map.95.own_ref = f32[768,768]{1,0:T(8,128)S(1)} custom-call(bf16[768,768]{1,0:T(8,128)(2,1)S(1)} %copy-done.3, bf16[768,768]{1,0:T(8,128)(2,1)S(1)} %pad_maximum_fusion.1.shaped_ref), custom_call_target="tpu_custom_call" | custom-call | flops 905969664 | bytes 4194304 | tf_op jit(solution)/shard_map/pallas_call | solution.py:195
  55.2 0.7 collective-permute-done.14.shaped_ref
  55.8 2.0 %shard_map.96.refs_0_ = bf16[768,768]{1,0:T(8,128)(2,1)} custom-call(bf16[768,768]{1,0:T(8,128)(2,1)S(1)} %copy-done.2, bf16[768,768]{1,0:T(8,128)(2,1)S(1)} %collective-permute-done.14.shaped_ref, f32[768,768]{1,0:T(8,128)S(1)} %shard_map.95.own_ref), custom_call_target="tpu_custom_call" | custom-call | flops 905969664 | bytes 4194304 | tf_op jit(solution)/shard_map/pallas_call | solution.py:195
  57.8 4.5 %all-to-all-start = ((bf16[16,48,768]{2,1,0:T(8,128)(2,1)}), bf16[16,48,768]{2,1,0:T(8,128)(2,1)S(1)}, u32[]{:S(2)}, u32[]{:S(2)}) async-start(bf16[16,48,768]{2,1,0:T(8,128)(2,1)} %bitcast.33), calls=%async_computation | async-start | bytes 2359296 | tf_op jit(solution)/shard_map/all_to_all | solution.py:310
  62.4 1.2 %copy-done.1 = bf16[768,768]{1,0:T(8,128)(2,1)S(1)} copy-done((bf16[768,768]{1,0:T(8,128)(2,1)S(1)}, bf16[768,768]{1,0:T(8,128)(2,1)}, u32[]{:S(2)}) %copy-start.1) | copy-done | bytes 1179672
  63.6 0.6 fusion.28
  64.2 0.6 fusion.27
  64.9 0.6 copy-done
  65.5 0.6 fusion.2
  66.1 0.6 fusion.3
  66.8 0.1 pad_maximum_fusion.2.refs_1_
  66.9 4.3 %shard_map.97 = bf16[384,1536]{1,0:T(8,128)(2,1)} custom-call(bf16[768,768]{1,0:T(8,128)(2,1)} %shard_map.96.refs_0_, bf16[768,768]{1,0:T(8,128)(2,1)S(1)} %copy-done.1, bf16[768,768]{1,0:T(8,128)(2,1)S(1)} %copy-done), custom_call_target="tpu_custom_call" | custom-call | flops 1811939328 | bytes 4194304 | tf_op jit(solution)/shard_map/pallas_call | solution.py:195
  71.2 18.3 %all-to-all-done = bf16[16,48,768]{2,1,0:T(8,128)(2,1)S(1)} async-done(((bf16[16,48,768]{2,1,0:T(8,128)(2,1)}), bf16[16,48,768]{2,1,0:T(8,128)(2,1)S(1)}, u32[]{:S(2)}, u32[]{:S(2)}) %all-to-all-start) | async-done | bytes 1179680 | tf_op jit(solution)/shard_map/all_to_all | solution.py:310
  89.4 2.0 %shard_map.98 = f32[32,16]{1,0:T(8,128)} custom-call(bf16[768,768]{1,0:T(8,128)(2,1)S(1)} %bitcast.75, bf16[768,768]{1,0:T(8,128)(2,1)S(1)} %pad_maximum_fusion.2.refs_1_), custom_call_target="tpu_custom_call" | custom-call | flops 1811939328 | bytes 4194304 | tf_op jit(solution)/shard_map/pallas_call | solution.py:195
  91.4 5.7 %all-to-all-start.1 = ((f32[32,1,16]{2,1,0:T(1,128)}), f32[32,1,16]{2,1,0:T(1,128)S(1)}, u32[]{:S(2)}, u32[]{:S(2)}) async-start(f32[32,1,16]{2,1,0:T(1,128)} %bitcast.41), calls=%async_computation.1 | async-start | bytes 32768 | tf_op jit(solution)/shard_map/all_to_all | solution.py:335
  97.1 1.1 %pad_maximum_fusion = bf16[384,1536]{1,0:T(8,128)(2,1)} fusion(bf16[384,384]{1,0:T(8,128)(2,1)S(1)} %get-tuple-element.42, bf16[384,384]{1,0:T(8,128)(2,1)S(1)} %get-tuple-element.24, bf16[384,384]{1,0:T(8,128)(2,1)S(1)} %get-tuple-element.43, bf16[384,384]{1,0:T(8,128)(2,1)S(1)} %get-tuple-element.23), kind=kLoop, calls=%fused_computation.14 | loop fusion | flops 4718592 | bytes 2359296 | tf_op jit(solution)/shard_map/concatenate | solution.py:278
  98.2 6.0 %all-to-all-done.1 = f32[32,1,16]{2,1,0:T(1,128)S(1)} async-done(((f32[32,1,16]{2,1,0:T(1,128)}), f32[32,1,16]{2,1,0:T(1,128)S(1)}, u32[]{:S(2)}, u32[]{:S(2)}) %all-to-all-start.1) | async-done | bytes 2080 | tf_op jit(solution)/shard_map/all_to_all | solution.py:335
  104.3 0.6 reduce_sum.9
  (42 shorter events, 1.2 us)
Async XLA Ops:
  2.5 10.0 %collective-permute-start = (bf16[4,2,24,768]{3,2,0,1:T(8,128)(2,1)S(1)}, bf16[4,2,24,768]{3,2,0,1:T(8,128)(2,1)S(1)}, u32[]{:S(2)}, u32[]{:S(2)}) collective-permute-start(bf16[4,2,24,768]{3,2,0,1:T(8,128)(2,1)S(1)} %copy.17), channel_id=1, source_target_pairs={{0,2},{2,0},{4,6},{6,4},{8,10},{10,8},{12,14},{14,12},{16,18},{18,... | collective-permute-start | bytes 884744 | tf_op jit(solution)/shard_map/ppermute | solution.py:33
  5.5 8.9 %collective-permute-start.2 = (bf16[4,2,24,768]{3,2,0,1:T(8,128)(2,1)S(1)}, bf16[4,2,24,768]{3,2,0,1:T(8,128)(2,1)S(1)}, u32[]{:S(2)}, u32[]{:S(2)}) collective-permute-start(bf16[4,2,24,768]{3,2,0,1:T(8,128)(2,1)S(1)} %copy.19), channel_id=1, source_target_pairs={{0,4},{2,6},{4,0},{6,2},{8,12},{10,14},{12,8},{14,10},{16,20},{18,... | collective-permute-start | bytes 884744 | tf_op jit(solution)/shard_map/ppermute | solution.py:33
  12.6 5.2 %collective-permute-start.1 = (bf16[4,24,768]{2,1,0:T(8,128)(2,1)S(1)}, bf16[4,24,768]{2,1,0:T(8,128)(2,1)S(1)}, u32[]{:S(2)}, u32[]{:S(2)}) collective-permute-start(bf16[4,24,768]{2,1,0:T(8,128)(2,1)S(1)} %fusion.8), channel_id=1, source_target_pairs={{0,4},{2,6},{4,0},{6,2},{8,12},{10,14},{12,8},{14,10},{16,20},{18,... | collective-permute-start | bytes 442376 | tf_op jit(solution)/shard_map/ppermute | solution.py:33
  14.5 5.2 %collective-permute-start.3 = (bf16[4,24,768]{2,1,0:T(8,128)(2,1)S(1)}, bf16[4,24,768]{2,1,0:T(8,128)(2,1)S(1)}, u32[]{:S(2)}, u32[]{:S(2)}) collective-permute-start(bf16[4,24,768]{2,1,0:T(8,128)(2,1)S(1)} %fusion.9), channel_id=1, source_target_pairs={{0,2},{2,0},{4,6},{6,4},{8,10},{10,8},{12,14},{14,12},{16,18},{18,... | collective-permute-start | bytes 442376 | tf_op jit(solution)/shard_map/ppermute | solution.py:33
  19.8 6.6 %collective-permute-start.6 = (bf16[24,1536]{1,0:T(8,128)(2,1)S(1)}, bf16[24,1536]{1,0:T(8,128)(2,1)S(1)}, u32[]{:S(2)}, u32[]{:S(2)}) collective-permute-start(bf16[24,1536]{1,0:T(8,128)(2,1)S(1)} %get-tuple-element.29), channel_id=1, source_target_pairs={{0,24},{2,26},{4,28},{6,30},{8,16},{10,18},{12,20},{14,22},{16,8},... | collective-permute-start | bytes 221192 | tf_op jit(solution)/shard_map/ppermute | solution.py:33
  23.5 5.5 %collective-permute-start.5 = (bf16[24,1536]{1,0:T(8,128)(2,1)S(1)}, bf16[24,1536]{1,0:T(8,128)(2,1)S(1)}, u32[]{:S(2)}, u32[]{:S(2)}) collective-permute-start(bf16[24,1536]{1,0:T(8,128)(2,1)S(1)} %get-tuple-element.28), channel_id=1, source_target_pairs={{0,16},{2,18},{4,20},{6,22},{8,24},{10,26},{12,28},{14,30},{16,0},... | collective-permute-start | bytes 221192 | tf_op jit(solution)/shard_map/ppermute | solution.py:33
  23.5 5.5 %collective-permute-start.4 = (bf16[24,1536]{1,0:T(8,128)(2,1)S(1)}, bf16[24,1536]{1,0:T(8,128)(2,1)S(1)}, u32[]{:S(2)}, u32[]{:S(2)}) collective-permute-start(bf16[24,1536]{1,0:T(8,128)(2,1)S(1)} %get-tuple-element.27), channel_id=1, source_target_pairs={{0,8},{2,10},{4,12},{6,14},{8,0},{10,2},{12,4},{14,6},{16,24},{18,... | collective-permute-start | bytes 221192 | tf_op jit(solution)/shard_map/ppermute | solution.py:33
  29.0 6.2 %collective-permute-start.9 = (bf16[24,1536]{1,0:T(8,128)(2,1)S(1)}, bf16[24,1536]{1,0:T(8,128)(2,1)S(1)}, u32[]{:S(2)}, u32[]{:S(2)}) collective-permute-start(bf16[24,1536]{1,0:T(8,128)(2,1)S(1)} %pad_maximum_fusion.11), channel_id=1, source_target_pairs={{0,24},{2,26},{4,28},{6,30},{8,16},{10,18},{12,20},{14,22},{16,8},... | collective-permute-start | bytes 221192 | tf_op jit(solution)/shard_map/ppermute | solution.py:33
  30.7 6.1 %collective-permute-start.8 = (bf16[24,1536]{1,0:T(8,128)(2,1)S(1)}, bf16[24,1536]{1,0:T(8,128)(2,1)S(1)}, u32[]{:S(2)}, u32[]{:S(2)}) collective-permute-start(bf16[24,1536]{1,0:T(8,128)(2,1)S(1)} %pad_maximum_fusion.11), channel_id=1, source_target_pairs={{0,16},{2,18},{4,20},{6,22},{8,24},{10,26},{12,28},{14,30},{16,0},... | collective-permute-start | bytes 221192 | tf_op jit(solution)/shard_map/ppermute | solution.py:33
  31.1 5.8 %collective-permute-start.7 = (bf16[24,1536]{1,0:T(8,128)(2,1)S(1)}, bf16[24,1536]{1,0:T(8,128)(2,1)S(1)}, u32[]{:S(2)}, u32[]{:S(2)}) collective-permute-start(bf16[24,1536]{1,0:T(8,128)(2,1)S(1)} %pad_maximum_fusion.11), channel_id=1, source_target_pairs={{0,8},{2,10},{4,12},{6,14},{8,0},{10,2},{12,4},{14,6},{16,24},{18,... | collective-permute-start | bytes 221192 | tf_op jit(solution)/shard_map/ppermute | solution.py:33
  36.8 1.4 %copy-start.4 = (bf16[1,384,1536]{2,1,0:T(8,128)(2,1)S(1)}, bf16[1,384,1536]{2,1,0:T(8,128)(2,1)}, u32[]{:S(2)}) copy-start(bf16[1,384,1536]{2,1,0:T(8,128)(2,1)} %param.7) | copy-start | bytes 3538948
  37.0 6.4 %collective-permute-start.10 = (bf16[4,24,768]{2,1,0:T(8,128)(2,1)S(1)}, bf16[4,24,768]{2,1,0:T(8,128)(2,1)S(1)}, u32[]{:S(2)}, u32[]{:S(2)}) collective-permute-start(bf16[4,24,768]{2,1,0:T(8,128)(2,1)S(1)} %get-tuple-element.33), channel_id=1, source_target_pairs={{0,4},{2,6},{4,0},{6,2},{8,12},{10,14},{12,8},{14,10},{16,20},{18,... | collective-permute-start | bytes 442376 | tf_op jit(solution)/shard_map/ppermute | solution.py:33
  38.5 6.6 %collective-permute-start.12 = (bf16[4,24,768]{2,1,0:T(8,128)(2,1)S(1)}, bf16[4,24,768]{2,1,0:T(8,128)(2,1)S(1)}, u32[]{:S(2)}, u32[]{:S(2)}) collective-permute-start(bf16[4,24,768]{2,1,0:T(8,128)(2,1)S(1)} %get-tuple-element.32), channel_id=1, source_target_pairs={{0,2},{2,0},{4,6},{6,4},{8,10},{10,8},{12,14},{14,12},{16,18},{18,... | collective-permute-start | bytes 442376 | tf_op jit(solution)/shard_map/ppermute | solution.py:33
  43.4 6.8 %collective-permute-start.11 = (bf16[4,2,24,768]{3,2,1,0:T(8,128)(2,1)S(1)}, bf16[4,2,24,768]{3,2,1,0:T(8,128)(2,1)S(1)}, u32[]{:S(2)}, u32[]{:S(2)}) collective-permute-start(bf16[4,2,24,768]{3,2,1,0:T(8,128)(2,1)S(1)} %reverse_select_fusion.3), channel_id=1, source_target_pairs={{0,2},{2,0},{4,6},{6,4},{8,10},{10,8},{12,14},{14,12},{16,18},{18,... | collective-permute-start | bytes 884744 | tf_op jit(solution)/shard_map/ppermute | solution.py:33
  45.3 6.8 %collective-permute-start.13 = (bf16[4,2,24,768]{3,2,0,1:T(8,128)(2,1)S(1)}, bf16[4,2,24,768]{3,2,0,1:T(8,128)(2,1)S(1)}, u32[]{:S(2)}, u32[]{:S(2)}) collective-permute-start(bf16[4,2,24,768]{3,2,0,1:T(8,128)(2,1)S(1)} %reverse_select_fusion.2), channel_id=1, source_target_pairs={{0,4},{2,6},{4,0},{6,2},{8,12},{10,14},{12,8},{14,10},{16,20},{18,... | collective-permute-start | bytes 884744 | tf_op jit(solution)/shard_map/ppermute | solution.py:33
  52.8 1.3 %copy-start.3 = (bf16[768,768]{1,0:T(8,128)(2,1)S(1)}, bf16[768,768]{1,0:T(8,128)(2,1)}, u32[]{:S(2)}) copy-start(bf16[768,768]{1,0:T(8,128)(2,1)} %constant.107.clone.table_ref) | copy-start | bytes 3538948
  52.9 2.9 %copy-start.2 = (bf16[768,768]{1,0:T(8,128)(2,1)S(1)}, bf16[768,768]{1,0:T(8,128)(2,1)}, u32[]{:S(2)}) copy-start(bf16[768,768]{1,0:T(8,128)(2,1)} %constant.108.clone.table_ref) | copy-start | bytes 3538948
  52.9 2.9 %collective-permute-start.14 = (bf16[768,768]{1,0:T(8,128)(2,1)S(1)}, bf16[768,768]{1,0:T(8,128)(2,1)S(1)}, u32[]{:S(2)}, u32[]{:S(2)}) collective-permute-start(bf16[768,768]{1,0:T(8,128)(2,1)S(1)} %pad_maximum_fusion.1.shaped_ref), channel_id=1, source_target_pairs={{0,1},{1,0},{2,3},{3,2},{4,5},{5,4},{6,7},{7,6},{8,9},{9,8},{10,11... | collective-permute-start | bytes 3538952 | tf_op jit(solution)/shard_map/ppermute | solution.py:286
  57.8 4.5 %copy-start.5 = (bf16[2,16,24,768]{3,2,1,0:T(8,128)(2,1)S(1)}, bf16[2,16,24,768]{3,2,1,0:T(8,128)(2,1)}, u32[]{:S(2)}) copy-start(bf16[2,16,24,768]{3,2,1,0:T(8,128)(2,1)} %param.9) | copy-start | bytes 3538948
  57.8 31.6 %all-to-all-start = ((bf16[16,48,768]{2,1,0:T(8,128)(2,1)}), bf16[16,48,768]{2,1,0:T(8,128)(2,1)S(1)}, u32[]{:S(2)}, u32[]{:S(2)}) async-start(bf16[16,48,768]{2,1,0:T(8,128)(2,1)} %bitcast.33), calls=%async_computation | async-start | bytes 2359296 | tf_op jit(solution)/shard_map/all_to_all | solution.py:310
  62.3 1.3 %copy-start.1 = (bf16[768,768]{1,0:T(8,128)(2,1)S(1)}, bf16[768,768]{1,0:T(8,128)(2,1)}, u32[]{:S(2)}) copy-start(bf16[768,768]{1,0:T(8,128)(2,1)} %constant.105.clone.refs_1_) | copy-start | bytes 3538948
  64.2 1.3 %copy-start = (bf16[768,768]{1,0:T(8,128)(2,1)S(1)}, bf16[768,768]{1,0:T(8,128)(2,1)}, u32[]{:S(2)}) copy-start(bf16[768,768]{1,0:T(8,128)(2,1)} %constant.106.clone.refs_2_) | copy-start | bytes 3538948
  91.4 12.9 %all-to-all-start.1 = ((f32[32,1,16]{2,1,0:T(1,128)}), f32[32,1,16]{2,1,0:T(1,128)S(1)}, u32[]{:S(2)}, u32[]{:S(2)}) async-start(f32[32,1,16]{2,1,0:T(1,128)} %bitcast.41), calls=%async_computation.1 | async-start | bytes 32768 | tf_op jit(solution)/shard_map/all_to_all | solution.py:335

commit v16 on v15

--- a/solution.py
+++ b/solution.py
@@ -156,7 +156,7 @@
 
 
 def coupling_kernel(block_rows, fields_ref, targets_ref, out_ref):
-    modes = out_ref.shape[1]
+    modes = out_ref.shape[2]
     product = lax.dot_general(
         fields_ref[...], targets_ref[...], (((1,), (1,)), ((), ())), preferred_element_type=f32
     )
@@ -181,7 +181,8 @@
     both = jnp.concatenate(
         [real[:, :right] + imag[:, right:], imag[:, :right] - real[:, right:]], 0
     )
-    out_ref[...] = exactly(both, groups(right), ((1,), (1,)))
+    total = exactly(both, groups(right), ((1,), (1,))).reshape(modes, 2, modes)
+    out_ref[0], out_ref[1] = total[:, 0], total[:, 1]
 
 
 def kernel_call(kernel, shape, dtype, flops, operands, grant=12, **more):
@@ -327,12 +328,14 @@
     pixels, output_fields = lax.optimization_barrier((pixels, output_fields))
     term = kernel_call(
         lambda *refs: coupling_kernel(block_rows, *refs),
-        (2 * mode_total, mode_total),
+        (2, mode_total, mode_total),
         f32,
         matmul,
         (pixels.reshape(column_shape), seen),
     )
-    pieces = lax.all_to_all(term, ("modes", "rows"), 0, 0, tiled=True)
+    core = lax.axis_index("rows")
+    came = lax.ppermute(pick(term, 1 - core, 0), "rows", [(0, 1), (1, 0)])
+    pieces = lax.all_to_all(pick(term, core, 0) + came, "modes", 0, 0, tiled=True)
     coupling = jnp.sum(pieces, 0, keepdims=True)
     return (phase_plane, output_fields[None], coupling)
 

time: 105 us -> 108 us (1.029)
  waiting for transfers between devices: 51.1 us -> 52.4 us
  starting transfers between devices: 32.4 us -> 33.5 us
    ppermute x0 -> x1, waiting for transfers between devices: none -> 1.16 us  [local(): came = lax.ppermute(pick(term, 1 - core, 0), 'rows', [(0, 1), (1, 0)])]
  transfers between devices with their start and end apart: 17 -> 18, of which waited for: 13 -> 14; matrix products, arithmetic and copies ran while one was open for 4% -> 4% of each run, Pallas kernels for 5% -> 5%
where the time goes in v16:
time: 108 us; the launch traced here: 107 us
  waiting for transfers between devices  52.4 us (49%)
  starting transfers between devices  33.5 us (31%)
  Pallas kernels  10.5 us (10%)
  other arithmetic  4 us (4%)
  local copies, waits for them, and re-layouts  3.35 us (3%)
  matrix products  2.51 us (2%)
    ppermute x14, waiting for transfers between devices, exchange(): lax.ppermute(values, 'modes', [(i, i ^ offset) for i in range(count)])  26.1 us
    ppermute x14, starting transfers between devices, exchange(): lax.ppermute(values, 'modes', [(i, i ^ offset) for i in range(count)])  22.1 us
    all_to_all x1, waiting for transfers between devices, local(): pixels = lax.all_to_all(blocks, 'modes', 0, 0, tiled=True)  18.3 us
    pallas_call x5, Pallas kernels, kernel_call(): pl.pallas_call(kernel, out_shape=out_shape, compiler_params=pltpu.Compile...  10.5 us
    all_to_all x1, starting transfers between devices, local(): lax.all_to_all(pick(term, core, 0) + came, 'modes', 0, 0, tiled=True)  6.76 us
    all_to_all x1, waiting for transfers between devices, local(): lax.all_to_all(pick(term, core, 0) + came, 'modes', 0, 0, tiled=True)  6.15 us
    all_to_all x1, starting transfers between devices, local(): pixels = lax.all_to_all(blocks, 'modes', 0, 0, tiled=True)  4.48 us
    unnamed x12, local copies, waits for them, and re-layouts  2.93 us
  transfers between devices with their start and end apart: 18, of which 14 were waited for; matrix products, arithmetic and copies ran while one was open for 4% of the time, Pallas kernels for 5%

profile of v16, /device:TPU:0, one launch (start us, length us, event | category | flops | bytes accessed | tf_op | source)
XLA Modules:
  0.0 107.2 jit_solution(8753825988462254262)
XLA Ops:
  0.6 1.8 %shard_map.94 = (bf16[192,768]{1,0:T(8,128)(2,1)S(1)}, f32[192,768]{1,0:T(8,128)S(1)}, bf16[192,768]{1,0:T(8,128)(2,1)S(1)}, f32[192,768]{1,0:T(8,128)S(1)}) custom-call(bf16[384,1536]{1,0:T(8,128)(2,1)} %bitcast.86, bf16[384,1536]{1,0:T(8,128)(2,1)} %bitcast.89), custom_call_target="tpu_custom_call" | custom-call | flops 4718592 | bytes 4194304 | tf_op jit(solution)/shard_map/pallas_call | solution.py:196
  2.5 3.0 %collective-permute-start = (bf16[4,2,24,768]{3,2,0,1:T(8,128)(2,1)S(1)}, bf16[4,2,24,768]{3,2,0,1:T(8,128)(2,1)S(1)}, u32[]{:S(2)}, u32[]{:S(2)}) collective-permute-start(bf16[4,2,24,768]{3,2,0,1:T(8,128)(2,1)S(1)} %copy.17), channel_id=1, source_target_pairs={{0,2},{2,0},{4,6},{6,4},{8,10},{10,8},{12,14},{14,12},{16,18},{18,... | collective-permute-start | bytes 884744 | tf_op jit(solution)/shard_map/ppermute | solution.py:33
  5.5 1.6 %collective-permute-start.2 = (bf16[4,2,24,768]{3,2,0,1:T(8,128)(2,1)S(1)}, bf16[4,2,24,768]{3,2,0,1:T(8,128)(2,1)S(1)}, u32[]{:S(2)}, u32[]{:S(2)}) collective-permute-start(bf16[4,2,24,768]{3,2,0,1:T(8,128)(2,1)S(1)} %copy.19), channel_id=1, source_target_pairs={{0,4},{2,6},{4,0},{6,2},{8,12},{10,14},{12,8},{14,10},{16,20},{18,... | collective-permute-start | bytes 884744 | tf_op jit(solution)/shard_map/ppermute | solution.py:33
  7.1 5.4 %collective-permute-done = bf16[4,2,24,768]{3,2,0,1:T(8,128)(2,1)S(1)} collective-permute-done((bf16[4,2,24,768]{3,2,0,1:T(8,128)(2,1)S(1)}, bf16[4,2,24,768]{3,2,0,1:T(8,128)(2,1)S(1)}, u32[]{:S(2)}, u32[]{:S(2)}) %collective-permute-start) | collective-permute-done | bytes 294944 | tf_op jit(solution)/shard_map/ppermute | solution.py:33
  12.6 1.8 %collective-permute-start.1 = (bf16[4,24,768]{2,1,0:T(8,128)(2,1)S(1)}, bf16[4,24,768]{2,1,0:T(8,128)(2,1)S(1)}, u32[]{:S(2)}, u32[]{:S(2)}) collective-permute-start(bf16[4,24,768]{2,1,0:T(8,128)(2,1)S(1)} %fusion.8), channel_id=1, source_target_pairs={{0,4},{2,6},{4,0},{6,2},{8,12},{10,14},{12,8},{14,10},{16,20},{18,... | collective-permute-start | bytes 442376 | tf_op jit(solution)/shard_map/ppermute | solution.py:33
  14.5 1.6 %collective-permute-start.3 = (bf16[4,24,768]{2,1,0:T(8,128)(2,1)S(1)}, bf16[4,24,768]{2,1,0:T(8,128)(2,1)S(1)}, u32[]{:S(2)}, u32[]{:S(2)}) collective-permute-start(bf16[4,24,768]{2,1,0:T(8,128)(2,1)S(1)} %fusion.9), channel_id=1, source_target_pairs={{0,2},{2,0},{4,6},{6,4},{8,10},{10,8},{12,14},{14,12},{16,18},{18,... | collective-permute-start | bytes 442376 | tf_op jit(solution)/shard_map/ppermute | solution.py:33
  16.1 1.7 %collective-permute-done.1 = bf16[4,24,768]{2,1,0:T(8,128)(2,1)S(1)} collective-permute-done((bf16[4,24,768]{2,1,0:T(8,128)(2,1)S(1)}, bf16[4,24,768]{2,1,0:T(8,128)(2,1)S(1)}, u32[]{:S(2)}, u32[]{:S(2)}) %collective-permute-start.1) | collective-permute-done | bytes 147488 | tf_op jit(solution)/shard_map/ppermute | solution.py:33
  17.8 1.9 %collective-permute-done.3 = bf16[4,24,768]{2,1,0:T(8,128)(2,1)S(1)} collective-permute-done((bf16[4,24,768]{2,1,0:T(8,128)(2,1)S(1)}, bf16[4,24,768]{2,1,0:T(8,128)(2,1)S(1)}, u32[]{:S(2)}, u32[]{:S(2)}) %collective-permute-start.3) | collective-permute-done | bytes 147488 | tf_op jit(solution)/shard_map/ppermute | solution.py:33
  19.8 3.7 %collective-permute-start.6 = (bf16[24,1536]{1,0:T(8,128)(2,1)S(1)}, bf16[24,1536]{1,0:T(8,128)(2,1)S(1)}, u32[]{:S(2)}, u32[]{:S(2)}) collective-permute-start(bf16[24,1536]{1,0:T(8,128)(2,1)S(1)} %get-tuple-element.29), channel_id=1, source_target_pairs={{0,24},{2,26},{4,28},{6,30},{8,16},{10,18},{12,20},{14,22},{16,8},... | collective-permute-start | bytes 221192 | tf_op jit(solution)/shard_map/ppermute | solution.py:33
  23.5 0.8 collective-permute-start.4
  24.2 2.2 %collective-permute-done.6 = bf16[24,1536]{1,0:T(8,128)(2,1)S(1)} collective-permute-done((bf16[24,1536]{1,0:T(8,128)(2,1)S(1)}, bf16[24,1536]{1,0:T(8,128)(2,1)S(1)}, u32[]{:S(2)}, u32[]{:S(2)}) %collective-permute-start.6) | collective-permute-done | bytes 73760 | tf_op jit(solution)/shard_map/ppermute | solution.py:33
  26.4 2.5 %collective-permute-done.5 = bf16[24,1536]{1,0:T(8,128)(2,1)S(1)} collective-permute-done((bf16[24,1536]{1,0:T(8,128)(2,1)S(1)}, bf16[24,1536]{1,0:T(8,128)(2,1)S(1)}, u32[]{:S(2)}, u32[]{:S(2)}) %collective-permute-start.5) | collective-permute-done | bytes 73760 | tf_op jit(solution)/shard_map/ppermute | solution.py:33
  29.0 1.7 %collective-permute-start.9 = (bf16[24,1536]{1,0:T(8,128)(2,1)S(1)}, bf16[24,1536]{1,0:T(8,128)(2,1)S(1)}, u32[]{:S(2)}, u32[]{:S(2)}) collective-permute-start(bf16[24,1536]{1,0:T(8,128)(2,1)S(1)} %pad_maximum_fusion.11), channel_id=1, source_target_pairs={{0,24},{2,26},{4,28},{6,30},{8,16},{10,18},{12,20},{14,22},{16,8},... | collective-permute-start | bytes 221192 | tf_op jit(solution)/shard_map/ppermute | solution.py:33
  30.7 0.4 collective-permute-start.8
  31.1 2.4 %collective-permute-start.7 = (bf16[24,1536]{1,0:T(8,128)(2,1)S(1)}, bf16[24,1536]{1,0:T(8,128)(2,1)S(1)}, u32[]{:S(2)}, u32[]{:S(2)}) collective-permute-start(bf16[24,1536]{1,0:T(8,128)(2,1)S(1)} %pad_maximum_fusion.11), channel_id=1, source_target_pairs={{0,8},{2,10},{4,12},{6,14},{8,0},{10,2},{12,4},{14,6},{16,24},{18,... | collective-permute-start | bytes 221192 | tf_op jit(solution)/shard_map/ppermute | solution.py:33
  33.5 1.8 %collective-permute-done.9 = bf16[24,1536]{1,0:T(8,128)(2,1)S(1)} collective-permute-done((bf16[24,1536]{1,0:T(8,128)(2,1)S(1)}, bf16[24,1536]{1,0:T(8,128)(2,1)S(1)}, u32[]{:S(2)}, u32[]{:S(2)}) %collective-permute-start.9) | collective-permute-done | bytes 73760 | tf_op jit(solution)/shard_map/ppermute | solution.py:33
  35.3 1.6 %collective-permute-done.8 = bf16[24,1536]{1,0:T(8,128)(2,1)S(1)} collective-permute-done((bf16[24,1536]{1,0:T(8,128)(2,1)S(1)}, bf16[24,1536]{1,0:T(8,128)(2,1)S(1)}, u32[]{:S(2)}, u32[]{:S(2)}) %collective-permute-start.8) | collective-permute-done | bytes 73760 | tf_op jit(solution)/shard_map/ppermute | solution.py:33
  37.0 1.3 %collective-permute-start.10 = (bf16[4,24,768]{2,1,0:T(8,128)(2,1)S(1)}, bf16[4,24,768]{2,1,0:T(8,128)(2,1)S(1)}, u32[]{:S(2)}, u32[]{:S(2)}) collective-permute-start(bf16[4,24,768]{2,1,0:T(8,128)(2,1)S(1)} %get-tuple-element.33), channel_id=1, source_target_pairs={{0,4},{2,6},{4,0},{6,2},{8,12},{10,14},{12,8},{14,10},{16,20},{18,... | collective-permute-start | bytes 442376 | tf_op jit(solution)/shard_map/ppermute | solution.py:33
  38.2 0.3 bitcast_convert_fusion
  38.5 1.4 %collective-permute-start.12 = (bf16[4,24,768]{2,1,0:T(8,128)(2,1)S(1)}, bf16[4,24,768]{2,1,0:T(8,128)(2,1)S(1)}, u32[]{:S(2)}, u32[]{:S(2)}) collective-permute-start(bf16[4,24,768]{2,1,0:T(8,128)(2,1)S(1)} %get-tuple-element.32), channel_id=1, source_target_pairs={{0,2},{2,0},{4,6},{6,4},{8,10},{10,8},{12,14},{14,12},{16,18},{18,... | collective-permute-start | bytes 442376 | tf_op jit(solution)/shard_map/ppermute | solution.py:33
  40.0 3.4 %collective-permute-done.10 = bf16[4,24,768]{2,1,0:T(8,128)(2,1)S(1)} collective-permute-done((bf16[4,24,768]{2,1,0:T(8,128)(2,1)S(1)}, bf16[4,24,768]{2,1,0:T(8,128)(2,1)S(1)}, u32[]{:S(2)}, u32[]{:S(2)}) %collective-permute-start.10) | collective-permute-done | bytes 147488 | tf_op jit(solution)/shard_map/ppermute | solution.py:33
  43.4 1.6 %collective-permute-start.11 = (bf16[4,2,24,768]{3,2,1,0:T(8,128)(2,1)S(1)}, bf16[4,2,24,768]{3,2,1,0:T(8,128)(2,1)S(1)}, u32[]{:S(2)}, u32[]{:S(2)}) collective-permute-start(bf16[4,2,24,768]{3,2,1,0:T(8,128)(2,1)S(1)} %reverse_select_fusion.3), channel_id=1, source_target_pairs={{0,2},{2,0},{4,6},{6,4},{8,10},{10,8},{12,14},{14,12},{16,18},{18,... | collective-permute-start | bytes 884744 | tf_op jit(solution)/shard_map/ppermute | solution.py:33
  45.3 0.9 collective-permute-start.13
  46.2 4.0 %collective-permute-done.11 = bf16[4,2,24,768]{3,2,1,0:T(8,128)(2,1)S(1)} collective-permute-done((bf16[4,2,24,768]{3,2,1,0:T(8,128)(2,1)S(1)}, bf16[4,2,24,768]{3,2,1,0:T(8,128)(2,1)S(1)}, u32[]{:S(2)}, u32[]{:S(2)}) %collective-permute-start.11) | collective-permute-done | bytes 294944 | tf_op jit(solution)/shard_map/ppermute | solution.py:33
  50.4 1.6 %collective-permute-done.13 = bf16[4,2,24,768]{3,2,0,1:T(8,128)(2,1)S(1)} collective-permute-done((bf16[4,2,24,768]{3,2,0,1:T(8,128)(2,1)S(1)}, bf16[4,2,24,768]{3,2,0,1:T(8,128)(2,1)S(1)}, u32[]{:S(2)}, u32[]{:S(2)}) %collective-permute-start.13) | collective-permute-done | bytes 294944 | tf_op jit(solution)/shard_map/ppermute | solution.py:33
  52.1 0.1 reverse_select_fusion
  52.3 0.1 fusion.25
  52.4 0.4 fusion.5
  53.0 1.1 %copy-done.3 = bf16[768,768]{1,0:T(8,128)(2,1)S(1)} copy-done((bf16[768,768]{1,0:T(8,128)(2,1)S(1)}, bf16[768,768]{1,0:T(8,128)(2,1)}, u32[]{:S(2)}) %copy-start.3) | copy-done | bytes 1179672
  54.1 1.1 %shard_map.95.own_ref = f32[768,768]{1,0:T(8,128)S(1)} custom-call(bf16[768,768]{1,0:T(8,128)(2,1)S(1)} %copy-done.3, bf16[768,768]{1,0:T(8,128)(2,1)S(1)} %pad_maximum_fusion.1.shaped_ref), custom_call_target="tpu_custom_call" | custom-call | flops 905969664 | bytes 4194304 | tf_op jit(solution)/shard_map/pallas_call | solution.py:196
  55.2 0.7 collective-permute-done.14.shaped_ref
  55.8 2.0 %shard_map.96.refs_0_ = bf16[768,768]{1,0:T(8,128)(2,1)} custom-call(bf16[768,768]{1,0:T(8,128)(2,1)S(1)} %copy-done.2, bf16[768,768]{1,0:T(8,128)(2,1)S(1)} %collective-permute-done.14.shaped_ref, f32[768,768]{1,0:T(8,128)S(1)} %shard_map.95.own_ref), custom_call_target="tpu_custom_call" | custom-call | flops 905969664 | bytes 4194304 | tf_op jit(solution)/shard_map/pallas_call | solution.py:196
  57.8 4.5 %all-to-all-start = ((bf16[16,48,768]{2,1,0:T(8,128)(2,1)}), bf16[16,48,768]{2,1,0:T(8,128)(2,1)S(1)}, u32[]{:S(2)}, u32[]{:S(2)}) async-start(bf16[16,48,768]{2,1,0:T(8,128)(2,1)} %bitcast.33), calls=%async_computation | async-start | bytes 2359296 | tf_op jit(solution)/shard_map/all_to_all | solution.py:311
  62.4 1.2 %copy-done.1 = bf16[768,768]{1,0:T(8,128)(2,1)S(1)} copy-done((bf16[768,768]{1,0:T(8,128)(2,1)S(1)}, bf16[768,768]{1,0:T(8,128)(2,1)}, u32[]{:S(2)}) %copy-start.1) | copy-done | bytes 1179672
  63.6 0.6 fusion.28
  64.2 0.6 fusion.27
  64.9 0.6 copy-done
  65.5 0.6 fusion.2
  66.2 0.6 fusion.3
  66.9 4.3 %shard_map.97 = bf16[384,1536]{1,0:T(8,128)(2,1)} custom-call(bf16[768,768]{1,0:T(8,128)(2,1)} %shard_map.96.refs_0_, bf16[768,768]{1,0:T(8,128)(2,1)S(1)} %copy-done.1, bf16[768,768]{1,0:T(8,128)(2,1)S(1)} %copy-done), custom_call_target="tpu_custom_call" | custom-call | flops 1811939328 | bytes 4194304 | tf_op jit(solution)/shard_map/pallas_call | solution.py:196
  71.2 18.3 %all-to-all-done = bf16[16,48,768]{2,1,0:T(8,128)(2,1)S(1)} async-done(((bf16[16,48,768]{2,1,0:T(8,128)(2,1)}), bf16[16,48,768]{2,1,0:T(8,128)(2,1)S(1)}, u32[]{:S(2)}, u32[]{:S(2)}) %all-to-all-start) | async-done | bytes 1179680 | tf_op jit(solution)/shard_map/all_to_all | solution.py:311
  89.4 1.4 %shard_map.98 = f32[2,16,16]{2,1,0:T(8,128)S(1)} custom-call(bf16[768,768]{1,0:T(8,128)(2,1)S(1)} %bitcast.77, bf16[768,768]{1,0:T(8,128)(2,1)S(1)} %pad_maximum_fusion.2.refs_1_), custom_call_target="tpu_custom_call" | custom-call | flops 1811939328 | bytes 4194304 | tf_op jit(solution)/shard_map/pallas_call | solution.py:196
  90.9 1.2 %collective-permute-done.15 = f32[16,16]{1,0:T(8,128)S(1)} collective-permute-done((f32[16,16]{1,0:T(8,128)S(1)}, f32[16,16]{1,0:T(8,128)S(1)}, u32[]{:S(2)}, u32[]{:S(2)}) %collective-permute-start.15) | collective-permute-done | bytes 1056 | tf_op jit(solution)/shard_map/ppermute | solution.py:337
  92.0 0.6 bitcast_add_fusion.2
  92.6 6.8 %all-to-all-start.1 = ((f32[16,1,16]{2,1,0:T(1,128)}), f32[16,1,16]{2,1,0:T(1,128)S(1)}, u32[]{:S(2)}, u32[]{:S(2)}) async-start(f32[16,1,16]{2,1,0:T(1,128)} %bitcast.42), calls=%async_computation.1 | async-start | bytes 16384 | tf_op jit(solution)/shard_map/all_to_all | solution.py:338
  99.4 1.1 %pad_maximum_fusion = bf16[384,1536]{1,0:T(8,128)(2,1)} fusion(bf16[384,384]{1,0:T(8,128)(2,1)S(1)} %get-tuple-element.42, bf16[384,384]{1,0:T(8,128)(2,1)S(1)} %get-tuple-element.24, bf16[384,384]{1,0:T(8,128)(2,1)S(1)} %get-tuple-element.43, bf16[384,384]{1,0:T(8,128)(2,1)S(1)} %get-tuple-element.23), kind=kLoop, calls=%fused_computation.14 | loop fusion | flops 4718592 | bytes 2359296 | tf_op jit(solution)/shard_map/concatenate | solution.py:279
  100.5 6.2 %all-to-all-done.1 = f32[16,1,16]{2,1,0:T(1,128)S(1)} async-done(((f32[16,1,16]{2,1,0:T(1,128)}), f32[16,1,16]{2,1,0:T(1,128)S(1)}, u32[]{:S(2)}, u32[]{:S(2)}) %all-to-all-start.1) | async-done | bytes 1056 | tf_op jit(solution)/shard_map/all_to_all | solution.py:338
  106.7 0.5 reduce_sum.9
  (46 shorter events, 1.5 us)
Async XLA Ops:
  2.5 10.0 %collective-permute-start = (bf16[4,2,24,768]{3,2,0,1:T(8,128)(2,1)S(1)}, bf16[4,2,24,768]{3,2,0,1:T(8,128)(2,1)S(1)}, u32[]{:S(2)}, u32[]{:S(2)}) collective-permute-start(bf16[4,2,24,768]{3,2,0,1:T(8,128)(2,1)S(1)} %copy.17), channel_id=1, source_target_pairs={{0,2},{2,0},{4,6},{6,4},{8,10},{10,8},{12,14},{14,12},{16,18},{18,... | collective-permute-start | bytes 884744 | tf_op jit(solution)/shard_map/ppermute | solution.py:33
  5.5 8.9 %collective-permute-start.2 = (bf16[4,2,24,768]{3,2,0,1:T(8,128)(2,1)S(1)}, bf16[4,2,24,768]{3,2,0,1:T(8,128)(2,1)S(1)}, u32[]{:S(2)}, u32[]{:S(2)}) collective-permute-start(bf16[4,2,24,768]{3,2,0,1:T(8,128)(2,1)S(1)} %copy.19), channel_id=1, source_target_pairs={{0,4},{2,6},{4,0},{6,2},{8,12},{10,14},{12,8},{14,10},{16,20},{18,... | collective-permute-start | bytes 884744 | tf_op jit(solution)/shard_map/ppermute | solution.py:33
  12.6 5.2 %collective-permute-start.1 = (bf16[4,24,768]{2,1,0:T(8,128)(2,1)S(1)}, bf16[4,24,768]{2,1,0:T(8,128)(2,1)S(1)}, u32[]{:S(2)}, u32[]{:S(2)}) collective-permute-start(bf16[4,24,768]{2,1,0:T(8,128)(2,1)S(1)} %fusion.8), channel_id=1, source_target_pairs={{0,4},{2,6},{4,0},{6,2},{8,12},{10,14},{12,8},{14,10},{16,20},{18,... | collective-permute-start | bytes 442376 | tf_op jit(solution)/shard_map/ppermute | solution.py:33
  14.5 5.2 %collective-permute-start.3 = (bf16[4,24,768]{2,1,0:T(8,128)(2,1)S(1)}, bf16[4,24,768]{2,1,0:T(8,128)(2,1)S(1)}, u32[]{:S(2)}, u32[]{:S(2)}) collective-permute-start(bf16[4,24,768]{2,1,0:T(8,128)(2,1)S(1)} %fusion.9), channel_id=1, source_target_pairs={{0,2},{2,0},{4,6},{6,4},{8,10},{10,8},{12,14},{14,12},{16,18},{18,... | collective-permute-start | bytes 442376 | tf_op jit(solution)/shard_map/ppermute | solution.py:33
  19.8 6.6 %collective-permute-start.6 = (bf16[24,1536]{1,0:T(8,128)(2,1)S(1)}, bf16[24,1536]{1,0:T(8,128)(2,1)S(1)}, u32[]{:S(2)}, u32[]{:S(2)}) collective-permute-start(bf16[24,1536]{1,0:T(8,128)(2,1)S(1)} %get-tuple-element.29), channel_id=1, source_target_pairs={{0,24},{2,26},{4,28},{6,30},{8,16},{10,18},{12,20},{14,22},{16,8},... | collective-permute-start | bytes 221192 | tf_op jit(solution)/shard_map/ppermute | solution.py:33
  23.5 5.5 %collective-permute-start.5 = (bf16[24,1536]{1,0:T(8,128)(2,1)S(1)}, bf16[24,1536]{1,0:T(8,128)(2,1)S(1)}, u32[]{:S(2)}, u32[]{:S(2)}) collective-permute-start(bf16[24,1536]{1,0:T(8,128)(2,1)S(1)} %get-tuple-element.28), channel_id=1, source_target_pairs={{0,16},{2,18},{4,20},{6,22},{8,24},{10,26},{12,28},{14,30},{16,0},... | collective-permute-start | bytes 221192 | tf_op jit(solution)/shard_map/ppermute | solution.py:33
  23.5 5.5 %collective-permute-start.4 = (bf16[24,1536]{1,0:T(8,128)(2,1)S(1)}, bf16[24,1536]{1,0:T(8,128)(2,1)S(1)}, u32[]{:S(2)}, u32[]{:S(2)}) collective-permute-start(bf16[24,1536]{1,0:T(8,128)(2,1)S(1)} %get-tuple-element.27), channel_id=1, source_target_pairs={{0,8},{2,10},{4,12},{6,14},{8,0},{10,2},{12,4},{14,6},{16,24},{18,... | collective-permute-start | bytes 221192 | tf_op jit(solution)/shard_map/ppermute | solution.py:33
  29.0 6.2 %collective-permute-start.9 = (bf16[24,1536]{1,0:T(8,128)(2,1)S(1)}, bf16[24,1536]{1,0:T(8,128)(2,1)S(1)}, u32[]{:S(2)}, u32[]{:S(2)}) collective-permute-start(bf16[24,1536]{1,0:T(8,128)(2,1)S(1)} %pad_maximum_fusion.11), channel_id=1, source_target_pairs={{0,24},{2,26},{4,28},{6,30},{8,16},{10,18},{12,20},{14,22},{16,8},... | collective-permute-start | bytes 221192 | tf_op jit(solution)/shard_map/ppermute | solution.py:33
  30.7 6.1 %collective-permute-start.8 = (bf16[24,1536]{1,0:T(8,128)(2,1)S(1)}, bf16[24,1536]{1,0:T(8,128)(2,1)S(1)}, u32[]{:S(2)}, u32[]{:S(2)}) collective-permute-start(bf16[24,1536]{1,0:T(8,128)(2,1)S(1)} %pad_maximum_fusion.11), channel_id=1, source_target_pairs={{0,16},{2,18},{4,20},{6,22},{8,24},{10,26},{12,28},{14,30},{16,0},... | collective-permute-start | bytes 221192 | tf_op jit(solution)/shard_map/ppermute | solution.py:33
  31.1 5.8 %collective-permute-start.7 = (bf16[24,1536]{1,0:T(8,128)(2,1)S(1)}, bf16[24,1536]{1,0:T(8,128)(2,1)S(1)}, u32[]{:S(2)}, u32[]{:S(2)}) collective-permute-start(bf16[24,1536]{1,0:T(8,128)(2,1)S(1)} %pad_maximum_fusion.11), channel_id=1, source_target_pairs={{0,8},{2,10},{4,12},{6,14},{8,0},{10,2},{12,4},{14,6},{16,24},{18,... | collective-permute-start | bytes 221192 | tf_op jit(solution)/shard_map/ppermute | solution.py:33
  36.8 1.4 %copy-start.4 = (bf16[1,384,1536]{2,1,0:T(8,128)(2,1)S(1)}, bf16[1,384,1536]{2,1,0:T(8,128)(2,1)}, u32[]{:S(2)}) copy-start(bf16[1,384,1536]{2,1,0:T(8,128)(2,1)} %param.7) | copy-start | bytes 3538948
  37.0 6.4 %collective-permute-start.10 = (bf16[4,24,768]{2,1,0:T(8,128)(2,1)S(1)}, bf16[4,24,768]{2,1,0:T(8,128)(2,1)S(1)}, u32[]{:S(2)}, u32[]{:S(2)}) collective-permute-start(bf16[4,24,768]{2,1,0:T(8,128)(2,1)S(1)} %get-tuple-element.33), channel_id=1, source_target_pairs={{0,4},{2,6},{4,0},{6,2},{8,12},{10,14},{12,8},{14,10},{16,20},{18,... | collective-permute-start | bytes 442376 | tf_op jit(solution)/shard_map/ppermute | solution.py:33
  38.5 6.6 %collective-permute-start.12 = (bf16[4,24,768]{2,1,0:T(8,128)(2,1)S(1)}, bf16[4,24,768]{2,1,0:T(8,128)(2,1)S(1)}, u32[]{:S(2)}, u32[]{:S(2)}) collective-permute-start(bf16[4,24,768]{2,1,0:T(8,128)(2,1)S(1)} %get-tuple-element.32), channel_id=1, source_target_pairs={{0,2},{2,0},{4,6},{6,4},{8,10},{10,8},{12,14},{14,12},{16,18},{18,... | collective-permute-start | bytes 442376 | tf_op jit(solution)/shard_map/ppermute | solution.py:33
  43.4 6.8 %collective-permute-start.11 = (bf16[4,2,24,768]{3,2,1,0:T(8,128)(2,1)S(1)}, bf16[4,2,24,768]{3,2,1,0:T(8,128)(2,1)S(1)}, u32[]{:S(2)}, u32[]{:S(2)}) collective-permute-start(bf16[4,2,24,768]{3,2,1,0:T(8,128)(2,1)S(1)} %reverse_select_fusion.3), channel_id=1, source_target_pairs={{0,2},{2,0},{4,6},{6,4},{8,10},{10,8},{12,14},{14,12},{16,18},{18,... | collective-permute-start | bytes 884744 | tf_op jit(solution)/shard_map/ppermute | solution.py:33
  45.3 6.8 %collective-permute-start.13 = (bf16[4,2,24,768]{3,2,0,1:T(8,128)(2,1)S(1)}, bf16[4,2,24,768]{3,2,0,1:T(8,128)(2,1)S(1)}, u32[]{:S(2)}, u32[]{:S(2)}) collective-permute-start(bf16[4,2,24,768]{3,2,0,1:T(8,128)(2,1)S(1)} %reverse_select_fusion.2), channel_id=1, source_target_pairs={{0,4},{2,6},{4,0},{6,2},{8,12},{10,14},{12,8},{14,10},{16,20},{18,... | collective-permute-start | bytes 884744 | tf_op jit(solution)/shard_map/ppermute | solution.py:33
  52.8 1.3 %copy-start.3 = (bf16[768,768]{1,0:T(8,128)(2,1)S(1)}, bf16[768,768]{1,0:T(8,128)(2,1)}, u32[]{:S(2)}) copy-start(bf16[768,768]{1,0:T(8,128)(2,1)} %constant.116.clone.table_ref) | copy-start | bytes 3538948
  52.9 2.9 %copy-start.2 = (bf16[768,768]{1,0:T(8,128)(2,1)S(1)}, bf16[768,768]{1,0:T(8,128)(2,1)}, u32[]{:S(2)}) copy-start(bf16[768,768]{1,0:T(8,128)(2,1)} %constant.117.clone.table_ref) | copy-start | bytes 3538948
  52.9 2.9 %collective-permute-start.14 = (bf16[768,768]{1,0:T(8,128)(2,1)S(1)}, bf16[768,768]{1,0:T(8,128)(2,1)S(1)}, u32[]{:S(2)}, u32[]{:S(2)}) collective-permute-start(bf16[768,768]{1,0:T(8,128)(2,1)S(1)} %pad_maximum_fusion.1.shaped_ref), channel_id=1, source_target_pairs={{0,1},{1,0},{2,3},{3,2},{4,5},{5,4},{6,7},{7,6},{8,9},{9,8},{10,11... | collective-permute-start | bytes 3538952 | tf_op jit(solution)/shard_map/ppermute | solution.py:287
  57.8 4.5 %copy-start.5 = (bf16[2,16,24,768]{3,2,1,0:T(8,128)(2,1)S(1)}, bf16[2,16,24,768]{3,2,1,0:T(8,128)(2,1)}, u32[]{:S(2)}) copy-start(bf16[2,16,24,768]{3,2,1,0:T(8,128)(2,1)} %param.9) | copy-start | bytes 3538948
  57.8 31.6 %all-to-all-start = ((bf16[16,48,768]{2,1,0:T(8,128)(2,1)}), bf16[16,48,768]{2,1,0:T(8,128)(2,1)S(1)}, u32[]{:S(2)}, u32[]{:S(2)}) async-start(bf16[16,48,768]{2,1,0:T(8,128)(2,1)} %bitcast.33), calls=%async_computation | async-start | bytes 2359296 | tf_op jit(solution)/shard_map/all_to_all | solution.py:311
  62.3 1.3 %copy-start.1 = (bf16[768,768]{1,0:T(8,128)(2,1)S(1)}, bf16[768,768]{1,0:T(8,128)(2,1)}, u32[]{:S(2)}) copy-start(bf16[768,768]{1,0:T(8,128)(2,1)} %constant.114.clone.refs_1_) | copy-start | bytes 3538948
  64.2 1.3 %copy-start = (bf16[768,768]{1,0:T(8,128)(2,1)S(1)}, bf16[768,768]{1,0:T(8,128)(2,1)}, u32[]{:S(2)}) copy-start(bf16[768,768]{1,0:T(8,128)(2,1)} %constant.115.clone.refs_2_) | copy-start | bytes 3538948
  90.8 1.2 %collective-permute-start.15 = (f32[16,16]{1,0:T(8,128)S(1)}, f32[16,16]{1,0:T(8,128)S(1)}, u32[]{:S(2)}, u32[]{:S(2)}) collective-permute-start(f32[16,16]{1,0:T(8,128)S(1)} %dynamic-slice_bitcast_fusion), channel_id=1, source_target_pairs={{0,1},{1,0},{2,3},{3,2},{4,5},{5,4},{6,7},{7,6},{8,9},{9,8},{10,11... | collective-permute-start | bytes 3080 | tf_op jit(solution)/shard_map/ppermute | solution.py:337
  92.6 14.0 %all-to-all-start.1 = ((f32[16,1,16]{2,1,0:T(1,128)}), f32[16,1,16]{2,1,0:T(1,128)S(1)}, u32[]{:S(2)}, u32[]{:S(2)}) async-start(f32[16,1,16]{2,1,0:T(1,128)} %bitcast.42), calls=%async_computation.1 | async-start | bytes 16384 | tf_op jit(solution)/shard_map/all_to_all | solution.py:338

commit v17 on v16

--- a/solution.py
+++ b/solution.py
@@ -325,7 +325,7 @@
         ],
         0,
     ).astype(bf16)
-    pixels, output_fields = lax.optimization_barrier((pixels, output_fields))
+    pixels, output_fields, phase_plane = lax.optimization_barrier((pixels, output_fields, phase_plane))
     term = kernel_call(
         lambda *refs: coupling_kernel(block_rows, *refs),
         (2, mode_total, mode_total),
@@ -334,9 +334,14 @@
         (pixels.reshape(column_shape), seen),
     )
     core = lax.axis_index("rows")
-    came = lax.ppermute(pick(term, 1 - core, 0), "rows", [(0, 1), (1, 0)])
-    pieces = lax.all_to_all(pick(term, core, 0) + came, "modes", 0, 0, tiled=True)
-    coupling = jnp.sum(pieces, 0, keepdims=True)
+    total = pick(term, core, 0) + lax.ppermute(pick(term, 1 - core, 0), "rows", [(0, 1), (1, 0)])
+    stride = count
+    while stride > 1:
+        stride //= 2
+        own = me // stride % 2
+        total = total.reshape(2, -1, mode_total)
+        total = pick(total, own, 0) + exchange(pick(total, 1 - own, 0), stride, count)
+    coupling = total.reshape(1, mode_total)
     return (phase_plane, output_fields[None], coupling)
 
 

time: 108 us -> 110 us (1.019)
  starting transfers between devices: 33.5 us -> 35.3 us
    ppermute x14 -> x18, starting transfers between devices: 22.1 us -> 30.7 us  [exchange(): lax.ppermute(values, 'modes', [(i, i ^ offset) for i in range(count)])]
    ppermute x14 -> x18, waiting for transfers between devices: 26.1 us -> 34.3 us  [exchange(): lax.ppermute(values, 'modes', [(i, i ^ offset) for i in range(count)])]
    all_to_all x1 -> x0, starting transfers between devices: 6.76 us -> none  [local(): lax.all_to_all(pick(term, core, 0) + came, 'modes', 0, 0, tiled=True)]
    all_to_all x1 -> x0, waiting for transfers between devices: 6.15 us -> none  [local(): lax.all_to_all(pick(term, core, 0) + came, 'modes', 0, 0, tiled=True)]
    all_to_all x1, waiting for transfers between devices: 18.3 us -> 17.1 us  [local(): pixels = lax.all_to_all(blocks, 'modes', 0, 0, tiled=True)]
  transfers between devices with their start and end apart: 18 -> 21, of which waited for: 14 -> 17; matrix products, arithmetic and copies ran while one was open for 4% -> 4% of each run, Pallas kernels for 5% -> 5%
where the time goes in v17:
time: 110 us; the launch traced here: 109 us
  waiting for transfers between devices  53.2 us (48%)
  starting transfers between devices  35.3 us (32%)
  Pallas kernels  10.6 us (10%)
  other arithmetic  3.39 us (3%)
  local copies, waits for them, and re-layouts  3.38 us (3%)
  matrix products  2.51 us (2%)
    ppermute x18, waiting for transfers between devices, exchange(): lax.ppermute(values, 'modes', [(i, i ^ offset) for i in range(count)])  34.3 us
    ppermute x18, starting transfers between devices, exchange(): lax.ppermute(values, 'modes', [(i, i ^ offset) for i in range(count)])  30.7 us
    all_to_all x1, waiting for transfers between devices, local(): pixels = lax.all_to_all(blocks, 'modes', 0, 0, tiled=True)  17.1 us
    pallas_call x5, Pallas kernels, kernel_call(): pl.pallas_call(kernel, out_shape=out_shape, compiler_params=pltpu.Compile...  10.6 us
    all_to_all x1, starting transfers between devices, local(): pixels = lax.all_to_all(blocks, 'modes', 0, 0, tiled=True)  4.48 us
    unnamed x12, local copies, waits for them, and re-layouts  2.93 us
    dot_general x4, matrix products, times(): return jnp.dot(one, two, preferred_element_type=f32)  2.51 us
  transfers between devices with their start and end apart: 21, of which 17 were waited for; matrix products, arithmetic and copies ran while one was open for 4% of the time, Pallas kernels for 5%

profile of v17, /device:TPU:0, one launch (start us, length us, event | category | flops | bytes accessed | tf_op | source)
XLA Modules:
  0.0 109.4 jit_solution(2550230631710393919)
XLA Ops:
  0.6 1.8 %shard_map.94 = (bf16[192,768]{1,0:T(8,128)(2,1)S(1)}, f32[192,768]{1,0:T(8,128)S(1)}, bf16[192,768]{1,0:T(8,128)(2,1)S(1)}, f32[192,768]{1,0:T(8,128)S(1)}) custom-call(bf16[384,1536]{1,0:T(8,128)(2,1)} %bitcast.108, bf16[384,1536]{1,0:T(8,128)(2,1)} %bitcast.111), custom_call_target="tpu_custom_call" | custom-call | flops 4718592 | bytes 4194304 | tf_op jit(solution)/shard_map/pallas_call | solution.py:196
  2.5 3.0 %collective-permute-start = (bf16[4,2,24,768]{3,2,0,1:T(8,128)(2,1)S(1)}, bf16[4,2,24,768]{3,2,0,1:T(8,128)(2,1)S(1)}, u32[]{:S(2)}, u32[]{:S(2)}) collective-permute-start(bf16[4,2,24,768]{3,2,0,1:T(8,128)(2,1)S(1)} %copy.10), channel_id=1, source_target_pairs={{0,2},{2,0},{4,6},{6,4},{8,10},{10,8},{12,14},{14,12},{16,18},{18,... | collective-permute-start | bytes 884744 | tf_op jit(solution)/shard_map/ppermute | solution.py:33
  5.5 1.6 %collective-permute-start.2 = (bf16[4,2,24,768]{3,2,0,1:T(8,128)(2,1)S(1)}, bf16[4,2,24,768]{3,2,0,1:T(8,128)(2,1)S(1)}, u32[]{:S(2)}, u32[]{:S(2)}) collective-permute-start(bf16[4,2,24,768]{3,2,0,1:T(8,128)(2,1)S(1)} %copy.12), channel_id=1, source_target_pairs={{0,4},{2,6},{4,0},{6,2},{8,12},{10,14},{12,8},{14,10},{16,20},{18,... | collective-permute-start | bytes 884744 | tf_op jit(solution)/shard_map/ppermute | solution.py:33
  7.1 5.4 %collective-permute-done = bf16[4,2,24,768]{3,2,0,1:T(8,128)(2,1)S(1)} collective-permute-done((bf16[4,2,24,768]{3,2,0,1:T(8,128)(2,1)S(1)}, bf16[4,2,24,768]{3,2,0,1:T(8,128)(2,1)S(1)}, u32[]{:S(2)}, u32[]{:S(2)}) %collective-permute-start) | collective-permute-done | bytes 294944 | tf_op jit(solution)/shard_map/ppermute | solution.py:33
  12.6 1.8 %collective-permute-start.1 = (bf16[4,24,768]{2,1,0:T(8,128)(2,1)S(1)}, bf16[4,24,768]{2,1,0:T(8,128)(2,1)S(1)}, u32[]{:S(2)}, u32[]{:S(2)}) collective-permute-start(bf16[4,24,768]{2,1,0:T(8,128)(2,1)S(1)} %fusion.8), channel_id=1, source_target_pairs={{0,4},{2,6},{4,0},{6,2},{8,12},{10,14},{12,8},{14,10},{16,20},{18,... | collective-permute-start | bytes 442376 | tf_op jit(solution)/shard_map/ppermute | solution.py:33
  14.5 1.6 %collective-permute-start.3 = (bf16[4,24,768]{2,1,0:T(8,128)(2,1)S(1)}, bf16[4,24,768]{2,1,0:T(8,128)(2,1)S(1)}, u32[]{:S(2)}, u32[]{:S(2)}) collective-permute-start(bf16[4,24,768]{2,1,0:T(8,128)(2,1)S(1)} %fusion.9), channel_id=1, source_target_pairs={{0,2},{2,0},{4,6},{6,4},{8,10},{10,8},{12,14},{14,12},{16,18},{18,... | collective-permute-start | bytes 442376 | tf_op jit(solution)/shard_map/ppermute | solution.py:33
  16.1 1.7 %collective-permute-done.1 = bf16[4,24,768]{2,1,0:T(8,128)(2,1)S(1)} collective-permute-done((bf16[4,24,768]{2,1,0:T(8,128)(2,1)S(1)}, bf16[4,24,768]{2,1,0:T(8,128)(2,1)S(1)}, u32[]{:S(2)}, u32[]{:S(2)}) %collective-permute-start.1) | collective-permute-done | bytes 147488 | tf_op jit(solution)/shard_map/ppermute | solution.py:33
  17.8 1.9 %collective-permute-done.3 = bf16[4,24,768]{2,1,0:T(8,128)(2,1)S(1)} collective-permute-done((bf16[4,24,768]{2,1,0:T(8,128)(2,1)S(1)}, bf16[4,24,768]{2,1,0:T(8,128)(2,1)S(1)}, u32[]{:S(2)}, u32[]{:S(2)}) %collective-permute-start.3) | collective-permute-done | bytes 147488 | tf_op jit(solution)/shard_map/ppermute | solution.py:33
  19.8 3.7 %collective-permute-start.6 = (bf16[24,1536]{1,0:T(8,128)(2,1)S(1)}, bf16[24,1536]{1,0:T(8,128)(2,1)S(1)}, u32[]{:S(2)}, u32[]{:S(2)}) collective-permute-start(bf16[24,1536]{1,0:T(8,128)(2,1)S(1)} %get-tuple-element.31), channel_id=1, source_target_pairs={{0,24},{2,26},{4,28},{6,30},{8,16},{10,18},{12,20},{14,22},{16,8},... | collective-permute-start | bytes 221192 | tf_op jit(solution)/shard_map/ppermute | solution.py:33
  23.5 0.8 collective-permute-start.4
  24.2 2.2 %collective-permute-done.6 = bf16[24,1536]{1,0:T(8,128)(2,1)S(1)} collective-permute-done((bf16[24,1536]{1,0:T(8,128)(2,1)S(1)}, bf16[24,1536]{1,0:T(8,128)(2,1)S(1)}, u32[]{:S(2)}, u32[]{:S(2)}) %collective-permute-start.6) | collective-permute-done | bytes 73760 | tf_op jit(solution)/shard_map/ppermute | solution.py:33
  26.4 2.5 %collective-permute-done.5 = bf16[24,1536]{1,0:T(8,128)(2,1)S(1)} collective-permute-done((bf16[24,1536]{1,0:T(8,128)(2,1)S(1)}, bf16[24,1536]{1,0:T(8,128)(2,1)S(1)}, u32[]{:S(2)}, u32[]{:S(2)}) %collective-permute-start.5) | collective-permute-done | bytes 73760 | tf_op jit(solution)/shard_map/ppermute | solution.py:33
  29.0 1.7 %collective-permute-start.9 = (bf16[24,1536]{1,0:T(8,128)(2,1)S(1)}, bf16[24,1536]{1,0:T(8,128)(2,1)S(1)}, u32[]{:S(2)}, u32[]{:S(2)}) collective-permute-start(bf16[24,1536]{1,0:T(8,128)(2,1)S(1)} %pad_maximum_fusion.11), channel_id=1, source_target_pairs={{0,24},{2,26},{4,28},{6,30},{8,16},{10,18},{12,20},{14,22},{16,8},... | collective-permute-start | bytes 221192 | tf_op jit(solution)/shard_map/ppermute | solution.py:33
  31.1 2.4 %collective-permute-start.7 = (bf16[24,1536]{1,0:T(8,128)(2,1)S(1)}, bf16[24,1536]{1,0:T(8,128)(2,1)S(1)}, u32[]{:S(2)}, u32[]{:S(2)}) collective-permute-start(bf16[24,1536]{1,0:T(8,128)(2,1)S(1)} %pad_maximum_fusion.11), channel_id=1, source_target_pairs={{0,8},{2,10},{4,12},{6,14},{8,0},{10,2},{12,4},{14,6},{16,24},{18,... | collective-permute-start | bytes 221192 | tf_op jit(solution)/shard_map/ppermute | solution.py:33
  33.5 1.8 %collective-permute-done.9 = bf16[24,1536]{1,0:T(8,128)(2,1)S(1)} collective-permute-done((bf16[24,1536]{1,0:T(8,128)(2,1)S(1)}, bf16[24,1536]{1,0:T(8,128)(2,1)S(1)}, u32[]{:S(2)}, u32[]{:S(2)}) %collective-permute-start.9) | collective-permute-done | bytes 73760 | tf_op jit(solution)/shard_map/ppermute | solution.py:33
  35.3 1.6 %collective-permute-done.8 = bf16[24,1536]{1,0:T(8,128)(2,1)S(1)} collective-permute-done((bf16[24,1536]{1,0:T(8,128)(2,1)S(1)}, bf16[24,1536]{1,0:T(8,128)(2,1)S(1)}, u32[]{:S(2)}, u32[]{:S(2)}) %collective-permute-start.8) | collective-permute-done | bytes 73760 | tf_op jit(solution)/shard_map/ppermute | solution.py:33
  37.0 1.3 %collective-permute-start.10 = (bf16[4,24,768]{2,1,0:T(8,128)(2,1)S(1)}, bf16[4,24,768]{2,1,0:T(8,128)(2,1)S(1)}, u32[]{:S(2)}, u32[]{:S(2)}) collective-permute-start(bf16[4,24,768]{2,1,0:T(8,128)(2,1)S(1)} %get-tuple-element.35), channel_id=1, source_target_pairs={{0,4},{2,6},{4,0},{6,2},{8,12},{10,14},{12,8},{14,10},{16,20},{18,... | collective-permute-start | bytes 442376 | tf_op jit(solution)/shard_map/ppermute | solution.py:33
  38.5 1.4 %collective-permute-start.12 = (bf16[4,24,768]{2,1,0:T(8,128)(2,1)S(1)}, bf16[4,24,768]{2,1,0:T(8,128)(2,1)S(1)}, u32[]{:S(2)}, u32[]{:S(2)}) collective-permute-start(bf16[4,24,768]{2,1,0:T(8,128)(2,1)S(1)} %get-tuple-element.34), channel_id=1, source_target_pairs={{0,2},{2,0},{4,6},{6,4},{8,10},{10,8},{12,14},{14,12},{16,18},{18,... | collective-permute-start | bytes 442376 | tf_op jit(solution)/shard_map/ppermute | solution.py:33
  40.0 3.4 %collective-permute-done.10 = bf16[4,24,768]{2,1,0:T(8,128)(2,1)S(1)} collective-permute-done((bf16[4,24,768]{2,1,0:T(8,128)(2,1)S(1)}, bf16[4,24,768]{2,1,0:T(8,128)(2,1)S(1)}, u32[]{:S(2)}, u32[]{:S(2)}) %collective-permute-start.10) | collective-permute-done | bytes 147488 | tf_op jit(solution)/shard_map/ppermute | solution.py:33
  43.4 1.6 %collective-permute-start.11 = (bf16[4,2,24,768]{3,2,1,0:T(8,128)(2,1)S(1)}, bf16[4,2,24,768]{3,2,1,0:T(8,128)(2,1)S(1)}, u32[]{:S(2)}, u32[]{:S(2)}) collective-permute-start(bf16[4,2,24,768]{3,2,1,0:T(8,128)(2,1)S(1)} %reverse_select_fusion.3), channel_id=1, source_target_pairs={{0,2},{2,0},{4,6},{6,4},{8,10},{10,8},{12,14},{14,12},{16,18},{18,... | collective-permute-start | bytes 884744 | tf_op jit(solution)/shard_map/ppermute | solution.py:33
  45.3 0.9 collective-permute-start.13
  46.2 4.0 %collective-permute-done.11 = bf16[4,2,24,768]{3,2,1,0:T(8,128)(2,1)S(1)} collective-permute-done((bf16[4,2,24,768]{3,2,1,0:T(8,128)(2,1)S(1)}, bf16[4,2,24,768]{3,2,1,0:T(8,128)(2,1)S(1)}, u32[]{:S(2)}, u32[]{:S(2)}) %collective-permute-start.11) | collective-permute-done | bytes 294944 | tf_op jit(solution)/shard_map/ppermute | solution.py:33
  50.4 1.6 %collective-permute-done.13 = bf16[4,2,24,768]{3,2,0,1:T(8,128)(2,1)S(1)} collective-permute-done((bf16[4,2,24,768]{3,2,0,1:T(8,128)(2,1)S(1)}, bf16[4,2,24,768]{3,2,0,1:T(8,128)(2,1)S(1)}, u32[]{:S(2)}, u32[]{:S(2)}) %collective-permute-start.13) | collective-permute-done | bytes 294944 | tf_op jit(solution)/shard_map/ppermute | solution.py:33
  53.0 1.1 copy-done.3
  54.1 1.1 shard_map.95.own_ref
  55.2 0.7 collective-permute-done.14.shaped_ref
  55.8 2.0 %shard_map.96.refs_0_ = bf16[768,768]{1,0:T(8,128)(2,1)} custom-call(bf16[768,768]{1,0:T(8,128)(2,1)S(1)} %copy-done.2, bf16[768,768]{1,0:T(8,128)(2,1)S(1)} %collective-permute-done.14.shaped_ref, f32[768,768]{1,0:T(8,128)S(1)} %shard_map.95.own_ref), custom_call_target="tpu_custom_call" | custom-call | flops 905969664 | bytes 4194304 | tf_op jit(solution)/shard_map/pallas_call | solution.py:196
  57.9 4.5 %all-to-all-start = ((bf16[16,48,768]{2,1,0:T(8,128)(2,1)}), bf16[16,48,768]{2,1,0:T(8,128)(2,1)S(1)}, u32[]{:S(2)}, u32[]{:S(2)}) async-start(bf16[16,48,768]{2,1,0:T(8,128)(2,1)} %bitcast.33), calls=%async_computation | async-start | bytes 2359296 | tf_op jit(solution)/shard_map/all_to_all | solution.py:311
  62.5 1.2 %copy-done.1 = bf16[768,768]{1,0:T(8,128)(2,1)S(1)} copy-done((bf16[768,768]{1,0:T(8,128)(2,1)S(1)}, bf16[768,768]{1,0:T(8,128)(2,1)}, u32[]{:S(2)}) %copy-start.1) | copy-done | bytes 1179672
  63.7 0.6 fusion.39
  64.3 0.6 fusion.38
  64.9 0.6 copy-done
  65.6 0.6 fusion.2
  66.2 0.6 fusion.3
  66.9 1.1 %pad_maximum_fusion.1 = bf16[384,1536]{1,0:T(8,128)(2,1)} fusion(bf16[384,384]{1,0:T(8,128)(2,1)S(1)} %get-tuple-element.44, bf16[384,384]{1,0:T(8,128)(2,1)S(1)} %get-tuple-element.26, bf16[384,384]{1,0:T(8,128)(2,1)S(1)} %get-tuple-element.45, bf16[384,384]{1,0:T(8,128)(2,1)S(1)} %get-tuple-element.25), kind=kLoop, calls=%fused_computation.15 | loop fusion | flops 4718592 | bytes 2359296 | tf_op jit(solution)/shard_map/concatenate | solution.py:279
  68.1 4.3 %shard_map.97 = bf16[384,1536]{1,0:T(8,128)(2,1)} custom-call(bf16[768,768]{1,0:T(8,128)(2,1)} %shard_map.96.refs_0_, bf16[768,768]{1,0:T(8,128)(2,1)S(1)} %copy-done.1, bf16[768,768]{1,0:T(8,128)(2,1)S(1)} %copy-done), custom_call_target="tpu_custom_call" | custom-call | flops 1811939328 | bytes 4194304 | tf_op jit(solution)/shard_map/pallas_call | solution.py:196
  72.3 17.1 %all-to-all-done = bf16[16,48,768]{2,1,0:T(8,128)(2,1)S(1)} async-done(((bf16[16,48,768]{2,1,0:T(8,128)(2,1)}), bf16[16,48,768]{2,1,0:T(8,128)(2,1)S(1)}, u32[]{:S(2)}, u32[]{:S(2)}) %all-to-all-start) | async-done | bytes 1179680 | tf_op jit(solution)/shard_map/all_to_all | solution.py:311
  89.5 1.4 %shard_map.98 = f32[2,16,16]{2,1,0:T(8,128)S(1)} custom-call(bf16[768,768]{1,0:T(8,128)(2,1)S(1)} %bitcast.99, bf16[768,768]{1,0:T(8,128)(2,1)S(1)} %pad_maximum_fusion.2.refs_1_), custom_call_target="tpu_custom_call" | custom-call | flops 1811939328 | bytes 4194304 | tf_op jit(solution)/shard_map/pallas_call | solution.py:196
  91.0 1.1 %collective-permute-done.15 = f32[16,16]{1,0:T(8,128)S(1)} collective-permute-done((f32[16,16]{1,0:T(8,128)S(1)}, f32[16,16]{1,0:T(8,128)S(1)}, u32[]{:S(2)}, u32[]{:S(2)}) %collective-permute-start.15) | collective-permute-done | bytes 1056 | tf_op jit(solution)/shard_map/ppermute | solution.py:337
  92.1 3.4 %collective-permute-start.16 = (f32[8,16]{1,0:T(8,128)S(1)}, f32[8,16]{1,0:T(8,128)S(1)}, u32[]{:S(2)}, u32[]{:S(2)}) collective-permute-start(f32[8,16]{1,0:T(8,128)S(1)} %fusion.27), channel_id=1, source_target_pairs={{0,16},{2,18},{4,20},{6,22},{8,24},{10,26},{12,28},{14,30},{16,0},... | collective-permute-start | bytes 1544 | tf_op jit(solution)/shard_map/ppermute | solution.py:33
  95.5 1.6 %collective-permute-done.16 = f32[8,16]{1,0:T(8,128)S(1)} collective-permute-done((f32[8,16]{1,0:T(8,128)S(1)}, f32[8,16]{1,0:T(8,128)S(1)}, u32[]{:S(2)}, u32[]{:S(2)}) %collective-permute-start.16) | collective-permute-done | bytes 544 | tf_op jit(solution)/shard_map/ppermute | solution.py:33
  97.1 3.1 %collective-permute-start.17 = (f32[4,16]{1,0:T(4,128)S(1)}, f32[4,16]{1,0:T(4,128)S(1)}, u32[]{:S(2)}, u32[]{:S(2)}) collective-permute-start(f32[4,16]{1,0:T(4,128)S(1)} %fusion.30), channel_id=1, source_target_pairs={{0,8},{2,10},{4,12},{6,14},{8,0},{10,2},{12,4},{14,6},{16,24},{18,... | collective-permute-start | bytes 776 | tf_op jit(solution)/shard_map/ppermute | solution.py:33
  100.1 1.6 %collective-permute-done.17 = f32[4,16]{1,0:T(4,128)S(1)} collective-permute-done((f32[4,16]{1,0:T(4,128)S(1)}, f32[4,16]{1,0:T(4,128)S(1)}, u32[]{:S(2)}, u32[]{:S(2)}) %collective-permute-start.17) | collective-permute-done | bytes 288 | tf_op jit(solution)/shard_map/ppermute | solution.py:33
  101.7 1.4 %collective-permute-start.18 = (f32[2,16]{1,0:T(2,128)S(1)}, f32[2,16]{1,0:T(2,128)S(1)}, u32[]{:S(2)}, u32[]{:S(2)}) collective-permute-start(f32[2,16]{1,0:T(2,128)S(1)} %fusion.33), channel_id=1, source_target_pairs={{0,4},{2,6},{4,0},{6,2},{8,12},{10,14},{12,8},{14,10},{16,20},{18,... | collective-permute-start | bytes 392 | tf_op jit(solution)/shard_map/ppermute | solution.py:33
  103.0 2.2 %collective-permute-done.18 = f32[2,16]{1,0:T(2,128)S(1)} collective-permute-done((f32[2,16]{1,0:T(2,128)S(1)}, f32[2,16]{1,0:T(2,128)S(1)}, u32[]{:S(2)}, u32[]{:S(2)}) %collective-permute-start.18) | collective-permute-done | bytes 160 | tf_op jit(solution)/shard_map/ppermute | solution.py:33
  105.3 0.8 collective-permute-start.19
  106.1 2.8 %collective-permute-done.19 = f32[1,16]{1,0:T(1,128)S(1)} collective-permute-done((f32[1,16]{1,0:T(1,128)S(1)}, f32[1,16]{1,0:T(1,128)S(1)}, u32[]{:S(2)}, u32[]{:S(2)}) %collective-permute-start.19) | collective-permute-done | bytes 96 | tf_op jit(solution)/shard_map/ppermute | solution.py:33
  108.9 0.5 fusion.34
  (59 shorter events, 2.8 us)
Async XLA Ops:
  2.5 10.0 %collective-permute-start = (bf16[4,2,24,768]{3,2,0,1:T(8,128)(2,1)S(1)}, bf16[4,2,24,768]{3,2,0,1:T(8,128)(2,1)S(1)}, u32[]{:S(2)}, u32[]{:S(2)}) collective-permute-start(bf16[4,2,24,768]{3,2,0,1:T(8,128)(2,1)S(1)} %copy.10), channel_id=1, source_target_pairs={{0,2},{2,0},{4,6},{6,4},{8,10},{10,8},{12,14},{14,12},{16,18},{18,... | collective-permute-start | bytes 884744 | tf_op jit(solution)/shard_map/ppermute | solution.py:33
  5.5 8.9 %collective-permute-start.2 = (bf16[4,2,24,768]{3,2,0,1:T(8,128)(2,1)S(1)}, bf16[4,2,24,768]{3,2,0,1:T(8,128)(2,1)S(1)}, u32[]{:S(2)}, u32[]{:S(2)}) collective-permute-start(bf16[4,2,24,768]{3,2,0,1:T(8,128)(2,1)S(1)} %copy.12), channel_id=1, source_target_pairs={{0,4},{2,6},{4,0},{6,2},{8,12},{10,14},{12,8},{14,10},{16,20},{18,... | collective-permute-start | bytes 884744 | tf_op jit(solution)/shard_map/ppermute | solution.py:33
  12.6 5.2 %collective-permute-start.1 = (bf16[4,24,768]{2,1,0:T(8,128)(2,1)S(1)}, bf16[4,24,768]{2,1,0:T(8,128)(2,1)S(1)}, u32[]{:S(2)}, u32[]{:S(2)}) collective-permute-start(bf16[4,24,768]{2,1,0:T(8,128)(2,1)S(1)} %fusion.8), channel_id=1, source_target_pairs={{0,4},{2,6},{4,0},{6,2},{8,12},{10,14},{12,8},{14,10},{16,20},{18,... | collective-permute-start | bytes 442376 | tf_op jit(solution)/shard_map/ppermute | solution.py:33
  14.5 5.2 %collective-permute-start.3 = (bf16[4,24,768]{2,1,0:T(8,128)(2,1)S(1)}, bf16[4,24,768]{2,1,0:T(8,128)(2,1)S(1)}, u32[]{:S(2)}, u32[]{:S(2)}) collective-permute-start(bf16[4,24,768]{2,1,0:T(8,128)(2,1)S(1)} %fusion.9), channel_id=1, source_target_pairs={{0,2},{2,0},{4,6},{6,4},{8,10},{10,8},{12,14},{14,12},{16,18},{18,... | collective-permute-start | bytes 442376 | tf_op jit(solution)/shard_map/ppermute | solution.py:33
  19.8 6.6 %collective-permute-start.6 = (bf16[24,1536]{1,0:T(8,128)(2,1)S(1)}, bf16[24,1536]{1,0:T(8,128)(2,1)S(1)}, u32[]{:S(2)}, u32[]{:S(2)}) collective-permute-start(bf16[24,1536]{1,0:T(8,128)(2,1)S(1)} %get-tuple-element.31), channel_id=1, source_target_pairs={{0,24},{2,26},{4,28},{6,30},{8,16},{10,18},{12,20},{14,22},{16,8},... | collective-permute-start | bytes 221192 | tf_op jit(solution)/shard_map/ppermute | solution.py:33
  23.5 5.5 %collective-permute-start.5 = (bf16[24,1536]{1,0:T(8,128)(2,1)S(1)}, bf16[24,1536]{1,0:T(8,128)(2,1)S(1)}, u32[]{:S(2)}, u32[]{:S(2)}) collective-permute-start(bf16[24,1536]{1,0:T(8,128)(2,1)S(1)} %get-tuple-element.30), channel_id=1, source_target_pairs={{0,16},{2,18},{4,20},{6,22},{8,24},{10,26},{12,28},{14,30},{16,0},... | collective-permute-start | bytes 221192 | tf_op jit(solution)/shard_map/ppermute | solution.py:33
  23.5 5.5 %collective-permute-start.4 = (bf16[24,1536]{1,0:T(8,128)(2,1)S(1)}, bf16[24,1536]{1,0:T(8,128)(2,1)S(1)}, u32[]{:S(2)}, u32[]{:S(2)}) collective-permute-start(bf16[24,1536]{1,0:T(8,128)(2,1)S(1)} %get-tuple-element.29), channel_id=1, source_target_pairs={{0,8},{2,10},{4,12},{6,14},{8,0},{10,2},{12,4},{14,6},{16,24},{18,... | collective-permute-start | bytes 221192 | tf_op jit(solution)/shard_map/ppermute | solution.py:33
  29.0 6.2 %collective-permute-start.9 = (bf16[24,1536]{1,0:T(8,128)(2,1)S(1)}, bf16[24,1536]{1,0:T(8,128)(2,1)S(1)}, u32[]{:S(2)}, u32[]{:S(2)}) collective-permute-start(bf16[24,1536]{1,0:T(8,128)(2,1)S(1)} %pad_maximum_fusion.11), channel_id=1, source_target_pairs={{0,24},{2,26},{4,28},{6,30},{8,16},{10,18},{12,20},{14,22},{16,8},... | collective-permute-start | bytes 221192 | tf_op jit(solution)/shard_map/ppermute | solution.py:33
  30.7 6.1 %collective-permute-start.8 = (bf16[24,1536]{1,0:T(8,128)(2,1)S(1)}, bf16[24,1536]{1,0:T(8,128)(2,1)S(1)}, u32[]{:S(2)}, u32[]{:S(2)}) collective-permute-start(bf16[24,1536]{1,0:T(8,128)(2,1)S(1)} %pad_maximum_fusion.11), channel_id=1, source_target_pairs={{0,16},{2,18},{4,20},{6,22},{8,24},{10,26},{12,28},{14,30},{16,0},... | collective-permute-start | bytes 221192 | tf_op jit(solution)/shard_map/ppermute | solution.py:33
  31.1 5.8 %collective-permute-start.7 = (bf16[24,1536]{1,0:T(8,128)(2,1)S(1)}, bf16[24,1536]{1,0:T(8,128)(2,1)S(1)}, u32[]{:S(2)}, u32[]{:S(2)}) collective-permute-start(bf16[24,1536]{1,0:T(8,128)(2,1)S(1)} %pad_maximum_fusion.11), channel_id=1, source_target_pairs={{0,8},{2,10},{4,12},{6,14},{8,0},{10,2},{12,4},{14,6},{16,24},{18,... | collective-permute-start | bytes 221192 | tf_op jit(solution)/shard_map/ppermute | solution.py:33
  36.8 1.4 %copy-start.4 = (bf16[1,384,1536]{2,1,0:T(8,128)(2,1)S(1)}, bf16[1,384,1536]{2,1,0:T(8,128)(2,1)}, u32[]{:S(2)}) copy-start(bf16[1,384,1536]{2,1,0:T(8,128)(2,1)} %param.7) | copy-start | bytes 3538948
  37.0 6.4 %collective-permute-start.10 = (bf16[4,24,768]{2,1,0:T(8,128)(2,1)S(1)}, bf16[4,24,768]{2,1,0:T(8,128)(2,1)S(1)}, u32[]{:S(2)}, u32[]{:S(2)}) collective-permute-start(bf16[4,24,768]{2,1,0:T(8,128)(2,1)S(1)} %get-tuple-element.35), channel_id=1, source_target_pairs={{0,4},{2,6},{4,0},{6,2},{8,12},{10,14},{12,8},{14,10},{16,20},{18,... | collective-permute-start | bytes 442376 | tf_op jit(solution)/shard_map/ppermute | solution.py:33
  38.5 6.6 %collective-permute-start.12 = (bf16[4,24,768]{2,1,0:T(8,128)(2,1)S(1)}, bf16[4,24,768]{2,1,0:T(8,128)(2,1)S(1)}, u32[]{:S(2)}, u32[]{:S(2)}) collective-permute-start(bf16[4,24,768]{2,1,0:T(8,128)(2,1)S(1)} %get-tuple-element.34), channel_id=1, source_target_pairs={{0,2},{2,0},{4,6},{6,4},{8,10},{10,8},{12,14},{14,12},{16,18},{18,... | collective-permute-start | bytes 442376 | tf_op jit(solution)/shard_map/ppermute | solution.py:33
  43.4 6.8 %collective-permute-start.11 = (bf16[4,2,24,768]{3,2,1,0:T(8,128)(2,1)S(1)}, bf16[4,2,24,768]{3,2,1,0:T(8,128)(2,1)S(1)}, u32[]{:S(2)}, u32[]{:S(2)}) collective-permute-start(bf16[4,2,24,768]{3,2,1,0:T(8,128)(2,1)S(1)} %reverse_select_fusion.3), channel_id=1, source_target_pairs={{0,2},{2,0},{4,6},{6,4},{8,10},{10,8},{12,14},{14,12},{16,18},{18,... | collective-permute-start | bytes 884744 | tf_op jit(solution)/shard_map/ppermute | solution.py:33
  45.3 6.8 %collective-permute-start.13 = (bf16[4,2,24,768]{3,2,0,1:T(8,128)(2,1)S(1)}, bf16[4,2,24,768]{3,2,0,1:T(8,128)(2,1)S(1)}, u32[]{:S(2)}, u32[]{:S(2)}) collective-permute-start(bf16[4,2,24,768]{3,2,0,1:T(8,128)(2,1)S(1)} %reverse_select_fusion.2), channel_id=1, source_target_pairs={{0,4},{2,6},{4,0},{6,2},{8,12},{10,14},{12,8},{14,10},{16,20},{18,... | collective-permute-start | bytes 884744 | tf_op jit(solution)/shard_map/ppermute | solution.py:33
  52.8 1.3 %copy-start.3 = (bf16[768,768]{1,0:T(8,128)(2,1)S(1)}, bf16[768,768]{1,0:T(8,128)(2,1)}, u32[]{:S(2)}) copy-start(bf16[768,768]{1,0:T(8,128)(2,1)} %constant.170.clone.table_ref) | copy-start | bytes 3538948
  52.9 2.9 %copy-start.2 = (bf16[768,768]{1,0:T(8,128)(2,1)S(1)}, bf16[768,768]{1,0:T(8,128)(2,1)}, u32[]{:S(2)}) copy-start(bf16[768,768]{1,0:T(8,128)(2,1)} %constant.171.clone.table_ref) | copy-start | bytes 3538948
  52.9 2.9 %collective-permute-start.14 = (bf16[768,768]{1,0:T(8,128)(2,1)S(1)}, bf16[768,768]{1,0:T(8,128)(2,1)S(1)}, u32[]{:S(2)}, u32[]{:S(2)}) collective-permute-start(bf16[768,768]{1,0:T(8,128)(2,1)S(1)} %pad_maximum_fusion.shaped_ref), channel_id=1, source_target_pairs={{0,1},{1,0},{2,3},{3,2},{4,5},{5,4},{6,7},{7,6},{8,9},{9,8},{10,11... | collective-permute-start | bytes 3538952 | tf_op jit(solution)/shard_map/ppermute | solution.py:287
  57.9 4.5 %copy-start.5 = (bf16[2,16,24,768]{3,2,1,0:T(8,128)(2,1)S(1)}, bf16[2,16,24,768]{3,2,1,0:T(8,128)(2,1)}, u32[]{:S(2)}) copy-start(bf16[2,16,24,768]{3,2,1,0:T(8,128)(2,1)} %param.9) | copy-start | bytes 3538948
  57.9 31.6 %all-to-all-start = ((bf16[16,48,768]{2,1,0:T(8,128)(2,1)}), bf16[16,48,768]{2,1,0:T(8,128)(2,1)S(1)}, u32[]{:S(2)}, u32[]{:S(2)}) async-start(bf16[16,48,768]{2,1,0:T(8,128)(2,1)} %bitcast.33), calls=%async_computation | async-start | bytes 2359296 | tf_op jit(solution)/shard_map/all_to_all | solution.py:311
  62.4 1.3 %copy-start.1 = (bf16[768,768]{1,0:T(8,128)(2,1)S(1)}, bf16[768,768]{1,0:T(8,128)(2,1)}, u32[]{:S(2)}) copy-start(bf16[768,768]{1,0:T(8,128)(2,1)} %constant.168.clone.refs_1_) | copy-start | bytes 3538948
  64.3 1.3 %copy-start = (bf16[768,768]{1,0:T(8,128)(2,1)S(1)}, bf16[768,768]{1,0:T(8,128)(2,1)}, u32[]{:S(2)}) copy-start(bf16[768,768]{1,0:T(8,128)(2,1)} %constant.169.clone.refs_2_) | copy-start | bytes 3538948
  90.9 1.2 %collective-permute-start.15 = (f32[16,16]{1,0:T(8,128)S(1)}, f32[16,16]{1,0:T(8,128)S(1)}, u32[]{:S(2)}, u32[]{:S(2)}) collective-permute-start(f32[16,16]{1,0:T(8,128)S(1)} %dynamic-slice_bitcast_fusion), channel_id=1, source_target_pairs={{0,1},{1,0},{2,3},{3,2},{4,5},{5,4},{6,7},{7,6},{8,9},{9,8},{10,11... | collective-permute-start | bytes 3080 | tf_op jit(solution)/shard_map/ppermute | solution.py:337
  92.1 4.9 %collective-permute-start.16 = (f32[8,16]{1,0:T(8,128)S(1)}, f32[8,16]{1,0:T(8,128)S(1)}, u32[]{:S(2)}, u32[]{:S(2)}) collective-permute-start(f32[8,16]{1,0:T(8,128)S(1)} %fusion.27), channel_id=1, source_target_pairs={{0,16},{2,18},{4,20},{6,22},{8,24},{10,26},{12,28},{14,30},{16,0},... | collective-permute-start | bytes 1544 | tf_op jit(solution)/shard_map/ppermute | solution.py:33
  97.1 4.6 %collective-permute-start.17 = (f32[4,16]{1,0:T(4,128)S(1)}, f32[4,16]{1,0:T(4,128)S(1)}, u32[]{:S(2)}, u32[]{:S(2)}) collective-permute-start(f32[4,16]{1,0:T(4,128)S(1)} %fusion.30), channel_id=1, source_target_pairs={{0,8},{2,10},{4,12},{6,14},{8,0},{10,2},{12,4},{14,6},{16,24},{18,... | collective-permute-start | bytes 776 | tf_op jit(solution)/shard_map/ppermute | solution.py:33
  101.7 3.6 %collective-permute-start.18 = (f32[2,16]{1,0:T(2,128)S(1)}, f32[2,16]{1,0:T(2,128)S(1)}, u32[]{:S(2)}, u32[]{:S(2)}) collective-permute-start(f32[2,16]{1,0:T(2,128)S(1)} %fusion.33), channel_id=1, source_target_pairs={{0,4},{2,6},{4,0},{6,2},{8,12},{10,14},{12,8},{14,10},{16,20},{18,... | collective-permute-start | bytes 392 | tf_op jit(solution)/shard_map/ppermute | solution.py:33
  105.3 3.6 %collective-permute-start.19 = (f32[1,16]{1,0:T(1,128)S(1)}, f32[1,16]{1,0:T(1,128)S(1)}, u32[]{:S(2)}, u32[]{:S(2)}) collective-permute-start(f32[1,16]{1,0:T(1,128)S(1)} %constant_dynamic-slice_fusion), channel_id=1, source_target_pairs={{0,2},{2,0},{4,6},{6,4},{8,10},{10,8},{12,14},{14,12},{16,18},{18,... | collective-permute-start | bytes 200 | tf_op jit(solution)/shard_map/ppermute | solution.py:33

commit v18 on v14

--- a/solution.py
+++ b/solution.py
@@ -105,12 +105,16 @@
     return jnp.dot(one, two, preferred_element_type=f32)
 
 
-def own_kernel(table_ref, shaped_ref, out_ref):
-    out_ref[...] = times(table_ref[...], shaped_ref[...])
-
-
-def other_kernel(table_ref, shaped_ref, own_ref, out_ref):
-    out_ref[...] = (own_ref[...] + times(table_ref[...], shaped_ref[...])).astype(bf16)
+def own_kernel(table_ref, first_ref, second_ref, out_ref):
+    half = first_ref.shape[1]
+    out_ref[:, :half] = times(table_ref[...], first_ref[...])
+    out_ref[:, half:] = times(table_ref[...], second_ref[...])
+
+
+def other_kernel(table_ref, first_ref, second_ref, own_ref, out_ref):
+    half = first_ref.shape[1]
+    out_ref[:, :half] = (own_ref[:, :half] + times(table_ref[...], first_ref[...])).astype(bf16)
+    out_ref[:, half:] = (own_ref[:, half:] + times(table_ref[...], second_ref[...])).astype(bf16)
 
 
 def fields_kernel(block_rows, columns_ref, re_ref, im_ref, out_ref):
@@ -268,11 +272,14 @@
 
     fore = forward[0].astype(f32)
     fore_re, fore_im = fore[:, :grid_size], fore[:, grid_size:]
-    plane_re, plane_im = plane_re.astype(f32), plane_im.astype(f32)
-    shaped = jnp.concatenate(
-        [fore_re * plane_re - fore_im * plane_im, fore_re * plane_im + fore_im * plane_re], 0
-    ).astype(bf16)
-    other = lax.ppermute(shaped, "rows", [(0, 1), (1, 0)])
+    shaped = []
+    for part, plane in enumerate(planes):
+        cols = slice(part * half, (part + 1) * half)
+        real, imag = plane[:, :half].astype(f32), plane[:, half:].astype(f32)
+        from_re, from_im = fore_re[:, cols], fore_im[:, cols]
+        rows = [from_re * real - from_im * imag, from_re * imag + from_im * real]
+        shaped.append(jnp.concatenate(rows, 0).astype(bf16))
+    other = [lax.ppermute(s, "rows", [(0, 1), (1, 0)]) for s in shaped]
 
     c_re, c_im = propagator(grid_size)
     full_re, full_im = jnp.asarray(c_re, bf16), jnp.asarray(c_im, bf16)
@@ -286,11 +293,11 @@
 
     column_shape = (2 * local_rows, grid_size)
     columns = kernel_call(
-        own_kernel, column_shape, f32, matmul // 2, (table(slice(0, local_rows)), shaped)
-    )
-    columns, other = lax.optimization_barrier((columns, other))
+        own_kernel, column_shape, f32, matmul // 2, (table(slice(0, local_rows)), *shaped)
+    )
+    columns, *other = lax.optimization_barrier((columns, *other))
     columns = kernel_call(
-        other_kernel, column_shape, bf16, matmul // 2, (table(slice(local_rows, None)), other, columns)
+        other_kernel, column_shape, bf16, matmul // 2, (table(slice(local_rows, None)), *other, columns)
     )
     blocks = columns.reshape(owners, 2, -1, block_rows, grid_size).transpose(0, 2, 1, 3, 4)
     blocks = blocks.reshape(count, 2 * block_rows, grid_size)

time: 105 us -> 105 us (level)
  waiting for transfers between devices: 51.1 us -> 49.2 us
    unnamed x12 -> x18, local copies, waits for them, and re-layouts: 2.92 us -> 1.35 us
    all_to_all x1, waiting for transfers between devices: 18.3 us -> 16.8 us  [local(): pixels = lax.all_to_all(blocks, 'modes', 0, 0, tiled=True)]
    another operation x1, local copies, waits for them, and re-layouts: 0.08 us -> 1.42 us  [local(): target_re, target_im = targets.reshape(2, local_rows, grid_size)]
  transfers between devices with their start and end apart: 17 -> 18, of which waited for: 13 -> 13; matrix products, arithmetic and copies ran while one was open for 4% -> 7% of each run, Pallas kernels for 5% -> 5%
where the time goes in v18:
time: 105 us
  waiting for transfers between devices  49.2 us (47%)
  starting transfers between devices  32.8 us (31%)
  Pallas kernels  11.9 us (11%)
  local copies, waits for them, and re-layouts  4.05 us (4%)
  other arithmetic  3.45 us (3%)
  matrix products  2.51 us (2%)
    ppermute x14, waiting for transfers between devices, exchange(): lax.ppermute(values, 'modes', [(i, i ^ offset) for i in range(count)])  26.1 us
    ppermute x14, starting transfers between devices, exchange(): lax.ppermute(values, 'modes', [(i, i ^ offset) for i in range(count)])  22.1 us
    all_to_all x1, waiting for transfers between devices, local(): pixels = lax.all_to_all(blocks, 'modes', 0, 0, tiled=True)  16.8 us
    pallas_call x5, Pallas kernels, kernel_call(): pl.pallas_call(kernel, out_shape=out_shape, compiler_params=pltpu.Compile...  11.9 us
    all_to_all x1, waiting for transfers between devices, local(): pieces = lax.all_to_all(term, ('modes', 'rows'), 0, 0, tiled=True)  6 us
    all_to_all x1, starting transfers between devices, local(): pieces = lax.all_to_all(term, ('modes', 'rows'), 0, 0, tiled=True)  5.74 us
    all_to_all x1, starting transfers between devices, local(): pixels = lax.all_to_all(blocks, 'modes', 0, 0, tiled=True)  4.35 us
    dot_general x4, matrix products, times(): return jnp.dot(one, two, preferred_element_type=f32)  2.51 us
  transfers between devices with their start and end apart: 18, of which 13 were waited for; matrix products, arithmetic and copies ran while one was open for 7% of the time, Pallas kernels for 5%

profile of v18, /device:TPU:0, one launch (start us, length us, event | category | flops | bytes accessed | tf_op | source)
XLA Modules:
  0.0 104.9 jit_solution(2208765263137347445)
XLA Ops:
  0.6 1.8 %shard_map.94 = (bf16[192,768]{1,0:T(8,128)(2,1)S(1)}, f32[192,768]{1,0:T(8,128)S(1)}, bf16[192,768]{1,0:T(8,128)(2,1)S(1)}, f32[192,768]{1,0:T(8,128)S(1)}) custom-call(bf16[384,1536]{1,0:T(8,128)(2,1)} %bitcast.88, bf16[384,1536]{1,0:T(8,128)(2,1)} %bitcast.89), custom_call_target="tpu_custom_call" | custom-call | flops 4718592 | bytes 4194304 | tf_op jit(solution)/shard_map/pallas_call | solution.py:188
  2.5 3.0 %collective-permute-start = (bf16[4,2,24,768]{3,2,0,1:T(8,128)(2,1)S(1)}, bf16[4,2,24,768]{3,2,0,1:T(8,128)(2,1)S(1)}, u32[]{:S(2)}, u32[]{:S(2)}) collective-permute-start(bf16[4,2,24,768]{3,2,0,1:T(8,128)(2,1)S(1)} %copy.17), channel_id=1, source_target_pairs={{0,2},{2,0},{4,6},{6,4},{8,10},{10,8},{12,14},{14,12},{16,18},{18,... | collective-permute-start | bytes 884744 | tf_op jit(solution)/shard_map/ppermute | solution.py:33
  5.5 1.6 %collective-permute-start.2 = (bf16[4,2,24,768]{3,2,0,1:T(8,128)(2,1)S(1)}, bf16[4,2,24,768]{3,2,0,1:T(8,128)(2,1)S(1)}, u32[]{:S(2)}, u32[]{:S(2)}) collective-permute-start(bf16[4,2,24,768]{3,2,0,1:T(8,128)(2,1)S(1)} %copy.19), channel_id=1, source_target_pairs={{0,4},{2,6},{4,0},{6,2},{8,12},{10,14},{12,8},{14,10},{16,20},{18,... | collective-permute-start | bytes 884744 | tf_op jit(solution)/shard_map/ppermute | solution.py:33
  7.1 5.4 %collective-permute-done = bf16[4,2,24,768]{3,2,0,1:T(8,128)(2,1)S(1)} collective-permute-done((bf16[4,2,24,768]{3,2,0,1:T(8,128)(2,1)S(1)}, bf16[4,2,24,768]{3,2,0,1:T(8,128)(2,1)S(1)}, u32[]{:S(2)}, u32[]{:S(2)}) %collective-permute-start) | collective-permute-done | bytes 294944 | tf_op jit(solution)/shard_map/ppermute | solution.py:33
  12.6 1.8 %collective-permute-start.1 = (bf16[4,24,768]{2,1,0:T(8,128)(2,1)S(1)}, bf16[4,24,768]{2,1,0:T(8,128)(2,1)S(1)}, u32[]{:S(2)}, u32[]{:S(2)}) collective-permute-start(bf16[4,24,768]{2,1,0:T(8,128)(2,1)S(1)} %fusion.12), channel_id=1, source_target_pairs={{0,4},{2,6},{4,0},{6,2},{8,12},{10,14},{12,8},{14,10},{16,20},{18,... | collective-permute-start | bytes 442376 | tf_op jit(solution)/shard_map/ppermute | solution.py:33
  14.5 1.6 %collective-permute-start.3 = (bf16[4,24,768]{2,1,0:T(8,128)(2,1)S(1)}, bf16[4,24,768]{2,1,0:T(8,128)(2,1)S(1)}, u32[]{:S(2)}, u32[]{:S(2)}) collective-permute-start(bf16[4,24,768]{2,1,0:T(8,128)(2,1)S(1)} %fusion.13), channel_id=1, source_target_pairs={{0,2},{2,0},{4,6},{6,4},{8,10},{10,8},{12,14},{14,12},{16,18},{18,... | collective-permute-start | bytes 442376 | tf_op jit(solution)/shard_map/ppermute | solution.py:33
  16.1 1.7 %collective-permute-done.1 = bf16[4,24,768]{2,1,0:T(8,128)(2,1)S(1)} collective-permute-done((bf16[4,24,768]{2,1,0:T(8,128)(2,1)S(1)}, bf16[4,24,768]{2,1,0:T(8,128)(2,1)S(1)}, u32[]{:S(2)}, u32[]{:S(2)}) %collective-permute-start.1) | collective-permute-done | bytes 147488 | tf_op jit(solution)/shard_map/ppermute | solution.py:33
  17.8 1.9 %collective-permute-done.3 = bf16[4,24,768]{2,1,0:T(8,128)(2,1)S(1)} collective-permute-done((bf16[4,24,768]{2,1,0:T(8,128)(2,1)S(1)}, bf16[4,24,768]{2,1,0:T(8,128)(2,1)S(1)}, u32[]{:S(2)}, u32[]{:S(2)}) %collective-permute-start.3) | collective-permute-done | bytes 147488 | tf_op jit(solution)/shard_map/ppermute | solution.py:33
  19.8 3.7 %collective-permute-start.6 = (bf16[24,1536]{1,0:T(8,128)(2,1)S(1)}, bf16[24,1536]{1,0:T(8,128)(2,1)S(1)}, u32[]{:S(2)}, u32[]{:S(2)}) collective-permute-start(bf16[24,1536]{1,0:T(8,128)(2,1)S(1)} %get-tuple-element.35), channel_id=1, source_target_pairs={{0,24},{2,26},{4,28},{6,30},{8,16},{10,18},{12,20},{14,22},{16,8},... | collective-permute-start | bytes 221192 | tf_op jit(solution)/shard_map/ppermute | solution.py:33
  23.5 0.8 collective-permute-start.4
  24.2 2.2 %collective-permute-done.6 = bf16[24,1536]{1,0:T(8,128)(2,1)S(1)} collective-permute-done((bf16[24,1536]{1,0:T(8,128)(2,1)S(1)}, bf16[24,1536]{1,0:T(8,128)(2,1)S(1)}, u32[]{:S(2)}, u32[]{:S(2)}) %collective-permute-start.6) | collective-permute-done | bytes 73760 | tf_op jit(solution)/shard_map/ppermute | solution.py:33
  26.4 2.5 %collective-permute-done.5 = bf16[24,1536]{1,0:T(8,128)(2,1)S(1)} collective-permute-done((bf16[24,1536]{1,0:T(8,128)(2,1)S(1)}, bf16[24,1536]{1,0:T(8,128)(2,1)S(1)}, u32[]{:S(2)}, u32[]{:S(2)}) %collective-permute-start.5) | collective-permute-done | bytes 73760 | tf_op jit(solution)/shard_map/ppermute | solution.py:33
  29.0 1.7 %collective-permute-start.9 = (bf16[24,1536]{1,0:T(8,128)(2,1)S(1)}, bf16[24,1536]{1,0:T(8,128)(2,1)S(1)}, u32[]{:S(2)}, u32[]{:S(2)}) collective-permute-start(bf16[24,1536]{1,0:T(8,128)(2,1)S(1)} %pad_maximum_fusion.10), channel_id=1, source_target_pairs={{0,24},{2,26},{4,28},{6,30},{8,16},{10,18},{12,20},{14,22},{16,8},... | collective-permute-start | bytes 221192 | tf_op jit(solution)/shard_map/ppermute | solution.py:33
  30.7 0.4 collective-permute-start.8
  31.1 2.4 %collective-permute-start.7 = (bf16[24,1536]{1,0:T(8,128)(2,1)S(1)}, bf16[24,1536]{1,0:T(8,128)(2,1)S(1)}, u32[]{:S(2)}, u32[]{:S(2)}) collective-permute-start(bf16[24,1536]{1,0:T(8,128)(2,1)S(1)} %pad_maximum_fusion.10), channel_id=1, source_target_pairs={{0,8},{2,10},{4,12},{6,14},{8,0},{10,2},{12,4},{14,6},{16,24},{18,... | collective-permute-start | bytes 221192 | tf_op jit(solution)/shard_map/ppermute | solution.py:33
  33.5 1.8 %collective-permute-done.9 = bf16[24,1536]{1,0:T(8,128)(2,1)S(1)} collective-permute-done((bf16[24,1536]{1,0:T(8,128)(2,1)S(1)}, bf16[24,1536]{1,0:T(8,128)(2,1)S(1)}, u32[]{:S(2)}, u32[]{:S(2)}) %collective-permute-start.9) | collective-permute-done | bytes 73760 | tf_op jit(solution)/shard_map/ppermute | solution.py:33
  35.3 1.6 %collective-permute-done.8 = bf16[24,1536]{1,0:T(8,128)(2,1)S(1)} collective-permute-done((bf16[24,1536]{1,0:T(8,128)(2,1)S(1)}, bf16[24,1536]{1,0:T(8,128)(2,1)S(1)}, u32[]{:S(2)}, u32[]{:S(2)}) %collective-permute-start.8) | collective-permute-done | bytes 73760 | tf_op jit(solution)/shard_map/ppermute | solution.py:33
  37.0 1.3 %collective-permute-start.10 = (bf16[4,24,768]{2,1,0:T(8,128)(2,1)S(1)}, bf16[4,24,768]{2,1,0:T(8,128)(2,1)S(1)}, u32[]{:S(2)}, u32[]{:S(2)}) collective-permute-start(bf16[4,24,768]{2,1,0:T(8,128)(2,1)S(1)} %get-tuple-element.39), channel_id=1, source_target_pairs={{0,4},{2,6},{4,0},{6,2},{8,12},{10,14},{12,8},{14,10},{16,20},{18,... | collective-permute-start | bytes 442376 | tf_op jit(solution)/shard_map/ppermute | solution.py:33
  38.2 0.3 bitcast_convert_fusion
  38.5 1.4 %collective-permute-start.12 = (bf16[4,24,768]{2,1,0:T(8,128)(2,1)S(1)}, bf16[4,24,768]{2,1,0:T(8,128)(2,1)S(1)}, u32[]{:S(2)}, u32[]{:S(2)}) collective-permute-start(bf16[4,24,768]{2,1,0:T(8,128)(2,1)S(1)} %get-tuple-element.38), channel_id=1, source_target_pairs={{0,2},{2,0},{4,6},{6,4},{8,10},{10,8},{12,14},{14,12},{16,18},{18,... | collective-permute-start | bytes 442376 | tf_op jit(solution)/shard_map/ppermute | solution.py:33
  40.0 3.4 %collective-permute-done.10 = bf16[4,24,768]{2,1,0:T(8,128)(2,1)S(1)} collective-permute-done((bf16[4,24,768]{2,1,0:T(8,128)(2,1)S(1)}, bf16[4,24,768]{2,1,0:T(8,128)(2,1)S(1)}, u32[]{:S(2)}, u32[]{:S(2)}) %collective-permute-start.10) | collective-permute-done | bytes 147488 | tf_op jit(solution)/shard_map/ppermute | solution.py:33
  43.4 1.6 %collective-permute-start.11 = (bf16[4,2,24,768]{3,2,0,1:T(8,128)(2,1)S(1)}, bf16[4,2,24,768]{3,2,0,1:T(8,128)(2,1)S(1)}, u32[]{:S(2)}, u32[]{:S(2)}) collective-permute-start(bf16[4,2,24,768]{3,2,0,1:T(8,128)(2,1)S(1)} %reverse_select_fusion.3), channel_id=1, source_target_pairs={{0,2},{2,0},{4,6},{6,4},{8,10},{10,8},{12,14},{14,12},{16,18},{18,... | collective-permute-start | bytes 884744 | tf_op jit(solution)/shard_map/ppermute | solution.py:33
  45.3 0.9 collective-permute-start.13
  46.2 4.0 %collective-permute-done.11 = bf16[4,2,24,768]{3,2,0,1:T(8,128)(2,1)S(1)} collective-permute-done((bf16[4,2,24,768]{3,2,0,1:T(8,128)(2,1)S(1)}, bf16[4,2,24,768]{3,2,0,1:T(8,128)(2,1)S(1)}, u32[]{:S(2)}, u32[]{:S(2)}) %collective-permute-start.11) | collective-permute-done | bytes 294944 | tf_op jit(solution)/shard_map/ppermute | solution.py:33
  50.3 0.1 reverse_select_fusion.1
  50.5 1.6 %collective-permute-done.13 = bf16[4,2,24,768]{3,2,1,0:T(8,128)(2,1)S(1)} collective-permute-done((bf16[4,2,24,768]{3,2,1,0:T(8,128)(2,1)S(1)}, bf16[4,2,24,768]{3,2,1,0:T(8,128)(2,1)S(1)}, u32[]{:S(2)}, u32[]{:S(2)}) %collective-permute-start.13) | collective-permute-done | bytes 294944 | tf_op jit(solution)/shard_map/ppermute | solution.py:33
  52.2 0.4 fusion.9
  52.9 0.6 collective-permute-start.15
  53.4 0.5 copy-done.3
  53.9 1.4 %shard_map.95.own_ref = f32[768,768]{1,0:T(8,128)S(1)} custom-call(bf16[768,768]{1,0:T(8,128)(2,1)S(1)} %copy-done.3, bf16[768,384]{1,0:T(8,128)(2,1)S(1)} %pad_maximum_fusion.4.first_ref, bf16[768,384]{1,0:T(8,128)(2,1)S(1)} %pad_maximum_fusion.5.second_ref), custom_call_target="tpu_custom_call" | custom-call | flops 905969664 | bytes 4194304 | tf_op jit(solution)/shard_map/pallas_call | solution.py:188
  55.3 0.3 collective-permute-done.15.second_ref
  55.6 2.4 %shard_map.96.refs_0_ = bf16[768,768]{1,0:T(8,128)(2,1)} custom-call(bf16[768,768]{1,0:T(8,128)(2,1)S(1)} %copy-done.2, bf16[768,384]{1,0:T(8,128)(2,1)S(1)} %collective-permute-done.14.first_ref, bf16[768,384]{1,0:T(8,128)(2,1)S(1)} %collective-permute-done.15.second_ref, f32[768,768]{1,0:T(8,128)S(1)} %shard_map.95.own_ref), custom_call_target="tpu_custom_call" | custom-call | flops 905969664 | bytes 4194304 | tf_op jit(solution)/shard_map/pallas_call | solution.py:188
  58.0 4.3 %all-to-all-start = ((bf16[16,48,768]{2,1,0:T(8,128)(2,1)}), bf16[16,48,768]{2,1,0:T(8,128)(2,1)S(1)}, u32[]{:S(2)}, u32[]{:S(2)}) async-start(bf16[16,48,768]{2,1,0:T(8,128)(2,1)} %bitcast.33), calls=%async_computation | async-start | bytes 2359296 | tf_op jit(solution)/shard_map/all_to_all | solution.py:304
  62.4 1.4 %fusion.28 = (bf16[1,16,24,768]{3,2,1,0:T(8,128)(2,1)S(1)}, bf16[1,16,24,768]{3,2,1,0:T(8,128)(2,1)S(1)}) fusion(bf16[2,16,24,768]{3,2,1,0:T(8,128)(2,1)} %param.9), kind=kLoop, calls=%fused_computation.80 | loop fusion | bytes 2359296 | tf_op jit(solution)/shard_map/unstack | solution.py:313
  63.8 0.2 copy-done.1
  64.0 0.6 fusion.32
  64.6 0.6 fusion.31
  65.3 0.6 copy-done
  65.9 0.6 fusion.2
  66.5 0.6 fusion.3
  67.3 1.1 %fusion.29 = (bf16[384,384]{1,0:T(8,128)(2,1)}, bf16[384,384]{1,0:T(8,128)(2,1)}, bf16[384,384]{1,0:T(8,128)(2,1)}, bf16[384,384]{1,0:T(8,128)(2,1)}) fusion(bf16[384,768]{1,0:T(8,128)(2,1)S(1)} %bitcast.81, bf16[384,768]{1,0:T(8,128)(2,1)S(1)} %bitcast.83), kind=kLoop, calls=%fused_computation.81 | loop fusion | bytes 2359296 | tf_op jit(solution)/shard_map/slice | solution.py:269
  68.3 4.3 %shard_map.97 = bf16[384,1536]{1,0:T(8,128)(2,1)} custom-call(bf16[768,768]{1,0:T(8,128)(2,1)} %shard_map.96.refs_0_, bf16[768,768]{1,0:T(8,128)(2,1)S(1)} %copy-done.1, bf16[768,768]{1,0:T(8,128)(2,1)S(1)} %copy-done), custom_call_target="tpu_custom_call" | custom-call | flops 1811939328 | bytes 4194304 | tf_op jit(solution)/shard_map/pallas_call | solution.py:188
  72.6 16.8 %all-to-all-done = bf16[16,48,768]{2,1,0:T(8,128)(2,1)S(1)} async-done(((bf16[16,48,768]{2,1,0:T(8,128)(2,1)}), bf16[16,48,768]{2,1,0:T(8,128)(2,1)S(1)}, u32[]{:S(2)}, u32[]{:S(2)}) %all-to-all-start) | async-done | bytes 1179680 | tf_op jit(solution)/shard_map/all_to_all | solution.py:304
  89.5 2.0 %shard_map.98 = f32[32,16]{1,0:T(8,128)} custom-call(bf16[768,768]{1,0:T(8,128)(2,1)S(1)} %bitcast.75, bf16[768,768]{1,0:T(8,128)(2,1)S(1)} %pad_maximum_fusion.1.refs_1_), custom_call_target="tpu_custom_call" | custom-call | flops 1811939328 | bytes 4194304 | tf_op jit(solution)/shard_map/pallas_call | solution.py:188
  91.5 5.7 %all-to-all-start.1 = ((f32[32,1,16]{2,1,0:T(1,128)}), f32[32,1,16]{2,1,0:T(1,128)S(1)}, u32[]{:S(2)}, u32[]{:S(2)}) async-start(f32[32,1,16]{2,1,0:T(1,128)} %bitcast.41), calls=%async_computation.1 | async-start | bytes 32768 | tf_op jit(solution)/shard_map/all_to_all | solution.py:329
  97.3 1.1 %pad_maximum_fusion = bf16[384,1536]{1,0:T(8,128)(2,1)} fusion(bf16[384,384]{1,0:T(8,128)(2,1)S(1)} %copy-done.7, bf16[384,384]{1,0:T(8,128)(2,1)S(1)} %copy-done.6, bf16[384,384]{1,0:T(8,128)(2,1)S(1)} %copy-done.8, bf16[384,384]{1,0:T(8,128)(2,1)S(1)} %copy-done.5), kind=kLoop, calls=%fused_computation.6 | loop fusion | flops 4718592 | bytes 2359296 | tf_op jit(solution)/shard_map/concatenate | solution.py:271
  98.4 6.0 %all-to-all-done.1 = f32[32,1,16]{2,1,0:T(1,128)S(1)} async-done(((f32[32,1,16]{2,1,0:T(1,128)}), f32[32,1,16]{2,1,0:T(1,128)S(1)}, u32[]{:S(2)}, u32[]{:S(2)}) %all-to-all-start.1) | async-done | bytes 2080 | tf_op jit(solution)/shard_map/all_to_all | solution.py:329
  104.4 0.6 reduce_sum.9
  (51 shorter events, 1.4 us)
Async XLA Ops:
  2.5 10.0 %collective-permute-start = (bf16[4,2,24,768]{3,2,0,1:T(8,128)(2,1)S(1)}, bf16[4,2,24,768]{3,2,0,1:T(8,128)(2,1)S(1)}, u32[]{:S(2)}, u32[]{:S(2)}) collective-permute-start(bf16[4,2,24,768]{3,2,0,1:T(8,128)(2,1)S(1)} %copy.17), channel_id=1, source_target_pairs={{0,2},{2,0},{4,6},{6,4},{8,10},{10,8},{12,14},{14,12},{16,18},{18,... | collective-permute-start | bytes 884744 | tf_op jit(solution)/shard_map/ppermute | solution.py:33
  5.5 8.9 %collective-permute-start.2 = (bf16[4,2,24,768]{3,2,0,1:T(8,128)(2,1)S(1)}, bf16[4,2,24,768]{3,2,0,1:T(8,128)(2,1)S(1)}, u32[]{:S(2)}, u32[]{:S(2)}) collective-permute-start(bf16[4,2,24,768]{3,2,0,1:T(8,128)(2,1)S(1)} %copy.19), channel_id=1, source_target_pairs={{0,4},{2,6},{4,0},{6,2},{8,12},{10,14},{12,8},{14,10},{16,20},{18,... | collective-permute-start | bytes 884744 | tf_op jit(solution)/shard_map/ppermute | solution.py:33
  12.6 5.2 %collective-permute-start.1 = (bf16[4,24,768]{2,1,0:T(8,128)(2,1)S(1)}, bf16[4,24,768]{2,1,0:T(8,128)(2,1)S(1)}, u32[]{:S(2)}, u32[]{:S(2)}) collective-permute-start(bf16[4,24,768]{2,1,0:T(8,128)(2,1)S(1)} %fusion.12), channel_id=1, source_target_pairs={{0,4},{2,6},{4,0},{6,2},{8,12},{10,14},{12,8},{14,10},{16,20},{18,... | collective-permute-start | bytes 442376 | tf_op jit(solution)/shard_map/ppermute | solution.py:33
  14.5 5.2 %collective-permute-start.3 = (bf16[4,24,768]{2,1,0:T(8,128)(2,1)S(1)}, bf16[4,24,768]{2,1,0:T(8,128)(2,1)S(1)}, u32[]{:S(2)}, u32[]{:S(2)}) collective-permute-start(bf16[4,24,768]{2,1,0:T(8,128)(2,1)S(1)} %fusion.13), channel_id=1, source_target_pairs={{0,2},{2,0},{4,6},{6,4},{8,10},{10,8},{12,14},{14,12},{16,18},{18,... | collective-permute-start | bytes 442376 | tf_op jit(solution)/shard_map/ppermute | solution.py:33
  19.8 6.6 %collective-permute-start.6 = (bf16[24,1536]{1,0:T(8,128)(2,1)S(1)}, bf16[24,1536]{1,0:T(8,128)(2,1)S(1)}, u32[]{:S(2)}, u32[]{:S(2)}) collective-permute-start(bf16[24,1536]{1,0:T(8,128)(2,1)S(1)} %get-tuple-element.35), channel_id=1, source_target_pairs={{0,24},{2,26},{4,28},{6,30},{8,16},{10,18},{12,20},{14,22},{16,8},... | collective-permute-start | bytes 221192 | tf_op jit(solution)/shard_map/ppermute | solution.py:33
  23.5 5.5 %collective-permute-start.5 = (bf16[24,1536]{1,0:T(8,128)(2,1)S(1)}, bf16[24,1536]{1,0:T(8,128)(2,1)S(1)}, u32[]{:S(2)}, u32[]{:S(2)}) collective-permute-start(bf16[24,1536]{1,0:T(8,128)(2,1)S(1)} %get-tuple-element.34), channel_id=1, source_target_pairs={{0,16},{2,18},{4,20},{6,22},{8,24},{10,26},{12,28},{14,30},{16,0},... | collective-permute-start | bytes 221192 | tf_op jit(solution)/shard_map/ppermute | solution.py:33
  23.5 5.5 %collective-permute-start.4 = (bf16[24,1536]{1,0:T(8,128)(2,1)S(1)}, bf16[24,1536]{1,0:T(8,128)(2,1)S(1)}, u32[]{:S(2)}, u32[]{:S(2)}) collective-permute-start(bf16[24,1536]{1,0:T(8,128)(2,1)S(1)} %get-tuple-element.33), channel_id=1, source_target_pairs={{0,8},{2,10},{4,12},{6,14},{8,0},{10,2},{12,4},{14,6},{16,24},{18,... | collective-permute-start | bytes 221192 | tf_op jit(solution)/shard_map/ppermute | solution.py:33
  29.0 6.2 %collective-permute-start.9 = (bf16[24,1536]{1,0:T(8,128)(2,1)S(1)}, bf16[24,1536]{1,0:T(8,128)(2,1)S(1)}, u32[]{:S(2)}, u32[]{:S(2)}) collective-permute-start(bf16[24,1536]{1,0:T(8,128)(2,1)S(1)} %pad_maximum_fusion.10), channel_id=1, source_target_pairs={{0,24},{2,26},{4,28},{6,30},{8,16},{10,18},{12,20},{14,22},{16,8},... | collective-permute-start | bytes 221192 | tf_op jit(solution)/shard_map/ppermute | solution.py:33
  30.7 6.1 %collective-permute-start.8 = (bf16[24,1536]{1,0:T(8,128)(2,1)S(1)}, bf16[24,1536]{1,0:T(8,128)(2,1)S(1)}, u32[]{:S(2)}, u32[]{:S(2)}) collective-permute-start(bf16[24,1536]{1,0:T(8,128)(2,1)S(1)} %pad_maximum_fusion.10), channel_id=1, source_target_pairs={{0,16},{2,18},{4,20},{6,22},{8,24},{10,26},{12,28},{14,30},{16,0},... | collective-permute-start | bytes 221192 | tf_op jit(solution)/shard_map/ppermute | solution.py:33
  31.1 5.8 %collective-permute-start.7 = (bf16[24,1536]{1,0:T(8,128)(2,1)S(1)}, bf16[24,1536]{1,0:T(8,128)(2,1)S(1)}, u32[]{:S(2)}, u32[]{:S(2)}) collective-permute-start(bf16[24,1536]{1,0:T(8,128)(2,1)S(1)} %pad_maximum_fusion.10), channel_id=1, source_target_pairs={{0,8},{2,10},{4,12},{6,14},{8,0},{10,2},{12,4},{14,6},{16,24},{18,... | collective-permute-start | bytes 221192 | tf_op jit(solution)/shard_map/ppermute | solution.py:33
  36.8 1.4 %copy-start.4 = (bf16[1,384,1536]{2,1,0:T(8,128)(2,1)S(1)}, bf16[1,384,1536]{2,1,0:T(8,128)(2,1)}, u32[]{:S(2)}) copy-start(bf16[1,384,1536]{2,1,0:T(8,128)(2,1)} %param.7) | copy-start | bytes 3538948
  37.0 6.4 %collective-permute-start.10 = (bf16[4,24,768]{2,1,0:T(8,128)(2,1)S(1)}, bf16[4,24,768]{2,1,0:T(8,128)(2,1)S(1)}, u32[]{:S(2)}, u32[]{:S(2)}) collective-permute-start(bf16[4,24,768]{2,1,0:T(8,128)(2,1)S(1)} %get-tuple-element.39), channel_id=1, source_target_pairs={{0,4},{2,6},{4,0},{6,2},{8,12},{10,14},{12,8},{14,10},{16,20},{18,... | collective-permute-start | bytes 442376 | tf_op jit(solution)/shard_map/ppermute | solution.py:33
  38.5 6.6 %collective-permute-start.12 = (bf16[4,24,768]{2,1,0:T(8,128)(2,1)S(1)}, bf16[4,24,768]{2,1,0:T(8,128)(2,1)S(1)}, u32[]{:S(2)}, u32[]{:S(2)}) collective-permute-start(bf16[4,24,768]{2,1,0:T(8,128)(2,1)S(1)} %get-tuple-element.38), channel_id=1, source_target_pairs={{0,2},{2,0},{4,6},{6,4},{8,10},{10,8},{12,14},{14,12},{16,18},{18,... | collective-permute-start | bytes 442376 | tf_op jit(solution)/shard_map/ppermute | solution.py:33
  43.4 6.8 %collective-permute-start.11 = (bf16[4,2,24,768]{3,2,0,1:T(8,128)(2,1)S(1)}, bf16[4,2,24,768]{3,2,0,1:T(8,128)(2,1)S(1)}, u32[]{:S(2)}, u32[]{:S(2)}) collective-permute-start(bf16[4,2,24,768]{3,2,0,1:T(8,128)(2,1)S(1)} %reverse_select_fusion.3), channel_id=1, source_target_pairs={{0,2},{2,0},{4,6},{6,4},{8,10},{10,8},{12,14},{14,12},{16,18},{18,... | collective-permute-start | bytes 884744 | tf_op jit(solution)/shard_map/ppermute | solution.py:33
  45.3 6.8 %collective-permute-start.13 = (bf16[4,2,24,768]{3,2,1,0:T(8,128)(2,1)S(1)}, bf16[4,2,24,768]{3,2,1,0:T(8,128)(2,1)S(1)}, u32[]{:S(2)}, u32[]{:S(2)}) collective-permute-start(bf16[4,2,24,768]{3,2,1,0:T(8,128)(2,1)S(1)} %reverse_select_fusion.2), channel_id=1, source_target_pairs={{0,4},{2,6},{4,0},{6,2},{8,12},{10,14},{12,8},{14,10},{16,20},{18,... | collective-permute-start | bytes 884744 | tf_op jit(solution)/shard_map/ppermute | solution.py:33
  52.6 1.3 %copy-start.3 = (bf16[768,768]{1,0:T(8,128)(2,1)S(1)}, bf16[768,768]{1,0:T(8,128)(2,1)}, u32[]{:S(2)}) copy-start(bf16[768,768]{1,0:T(8,128)(2,1)} %constant.107.clone.table_ref) | copy-start | bytes 3538948
  52.7 2.6 %collective-permute-start.14 = (bf16[768,384]{1,0:T(8,128)(2,1)S(1)}, bf16[768,384]{1,0:T(8,128)(2,1)S(1)}, u32[]{:S(2)}, u32[]{:S(2)}) collective-permute-start(bf16[768,384]{1,0:T(8,128)(2,1)S(1)} %pad_maximum_fusion.4.first_ref), channel_id=1, source_target_pairs={{0,1},{1,0},{2,3},{3,2},{4,5},{5,4},{6,7},{7,6},{8,9},{9,8},{10,11... | collective-permute-start | bytes 1769480 | tf_op jit(solution)/shard_map/ppermute | solution.py:282
  52.8 2.8 %copy-start.2 = (bf16[768,768]{1,0:T(8,128)(2,1)S(1)}, bf16[768,768]{1,0:T(8,128)(2,1)}, u32[]{:S(2)}) copy-start(bf16[768,768]{1,0:T(8,128)(2,1)} %constant.108.clone.table_ref) | copy-start | bytes 3538948
  52.9 2.8 %collective-permute-start.15 = (bf16[768,384]{1,0:T(8,128)(2,1)S(1)}, bf16[768,384]{1,0:T(8,128)(2,1)S(1)}, u32[]{:S(2)}, u32[]{:S(2)}) collective-permute-start(bf16[768,384]{1,0:T(8,128)(2,1)S(1)} %pad_maximum_fusion.5.second_ref), channel_id=1, source_target_pairs={{0,1},{1,0},{2,3},{3,2},{4,5},{5,4},{6,7},{7,6},{8,9},{9,8},{10,11... | collective-permute-start | bytes 1769480 | tf_op jit(solution)/shard_map/ppermute | solution.py:282
  58.0 31.5 %all-to-all-start = ((bf16[16,48,768]{2,1,0:T(8,128)(2,1)}), bf16[16,48,768]{2,1,0:T(8,128)(2,1)S(1)}, u32[]{:S(2)}, u32[]{:S(2)}) async-start(bf16[16,48,768]{2,1,0:T(8,128)(2,1)} %bitcast.33), calls=%async_computation | async-start | bytes 2359296 | tf_op jit(solution)/shard_map/all_to_all | solution.py:304
  62.4 1.6 %copy-start.1 = (bf16[768,768]{1,0:T(8,128)(2,1)S(1)}, bf16[768,768]{1,0:T(8,128)(2,1)}, u32[]{:S(2)}) copy-start(bf16[768,768]{1,0:T(8,128)(2,1)} %constant.105.clone.refs_1_) | copy-start | bytes 3538948
  64.6 1.3 %copy-start = (bf16[768,768]{1,0:T(8,128)(2,1)S(1)}, bf16[768,768]{1,0:T(8,128)(2,1)}, u32[]{:S(2)}) copy-start(bf16[768,768]{1,0:T(8,128)(2,1)} %constant.106.clone.refs_2_) | copy-start | bytes 3538948
  89.5 7.7 %copy-start.5 = (bf16[384,384]{1,0:T(8,128)(2,1)S(1)}, bf16[384,384]{1,0:T(8,128)(2,1)}, u32[]{:S(2)}) copy-start(bf16[384,384]{1,0:T(8,128)(2,1)} %get-tuple-element.29) | copy-start | bytes 884740
  89.5 7.8 %copy-start.6 = (bf16[384,384]{1,0:T(8,128)(2,1)S(1)}, bf16[384,384]{1,0:T(8,128)(2,1)}, u32[]{:S(2)}) copy-start(bf16[384,384]{1,0:T(8,128)(2,1)} %get-tuple-element.30) | copy-start | bytes 884740
  89.5 7.8 %copy-start.7 = (bf16[384,384]{1,0:T(8,128)(2,1)S(1)}, bf16[384,384]{1,0:T(8,128)(2,1)}, u32[]{:S(2)}) copy-start(bf16[384,384]{1,0:T(8,128)(2,1)} %get-tuple-element.48) | copy-start | bytes 884740
  89.5 7.8 %copy-start.8 = (bf16[384,384]{1,0:T(8,128)(2,1)S(1)}, bf16[384,384]{1,0:T(8,128)(2,1)}, u32[]{:S(2)}) copy-start(bf16[384,384]{1,0:T(8,128)(2,1)} %get-tuple-element.49) | copy-start | bytes 884740
  91.5 12.9 %all-to-all-start.1 = ((f32[32,1,16]{2,1,0:T(1,128)}), f32[32,1,16]{2,1,0:T(1,128)S(1)}, u32[]{:S(2)}, u32[]{:S(2)}) async-start(f32[32,1,16]{2,1,0:T(1,128)} %bitcast.41), calls=%async_computation.1 | async-start | bytes 32768 | tf_op jit(solution)/shard_map/all_to_all | solution.py:329

commit v19 on v18

--- a/solution.py
+++ b/solution.py
@@ -318,7 +318,7 @@
         ],
         0,
     ).astype(bf16)
-    pixels, output_fields = lax.optimization_barrier((pixels, output_fields))
+    pixels, output_fields, phase_plane = lax.optimization_barrier((pixels, output_fields, phase_plane))
     term = kernel_call(
         lambda *refs: coupling_kernel(block_rows, *refs),
         (2 * mode_total, mode_total),

time: 105 us -> 105 us (level)
  blocking collectives: 0 us -> 12.7 us
  waiting for transfers between devices: 49.2 us -> 43 us
  starting transfers between devices: 32.8 us -> 27.5 us
    all_to_all x0 -> x1, blocking collectives: none -> 12.7 us  [local(): pieces = lax.all_to_all(term, ('modes', 'rows'), 0, 0, tiled=True)]
    all_to_all x1 -> x0, waiting for transfers between devices: 6 us -> none  [local(): pieces = lax.all_to_all(term, ('modes', 'rows'), 0, 0, tiled=True)]
    all_to_all x1 -> x0, starting transfers between devices: 5.74 us -> none  [local(): pieces = lax.all_to_all(term, ('modes', 'rows'), 0, 0, tiled=True)]
  transfers between devices with their start and end apart: 18 -> 17, of which waited for: 13 -> 12; matrix products, arithmetic and copies ran while one was open for 7% -> 6% of each run, Pallas kernels for 5% -> 5%
where the time goes in v19:
time: 105 us
  waiting for transfers between devices  43 us (41%)
  starting transfers between devices  27.5 us (26%)
  blocking collectives  12.7 us (12%)
  Pallas kernels  11.3 us (11%)
  other arithmetic  3.45 us (3%)
  local copies, waits for them, and re-layouts  3.09 us (3%)
  matrix products  2.52 us (2%)
    ppermute x14, waiting for transfers between devices, exchange(): lax.ppermute(values, 'modes', [(i, i ^ offset) for i in range(count)])  26 us
    ppermute x14, starting transfers between devices, exchange(): lax.ppermute(values, 'modes', [(i, i ^ offset) for i in range(count)])  21.9 us
    all_to_all x1, waiting for transfers between devices, local(): pixels = lax.all_to_all(blocks, 'modes', 0, 0, tiled=True)  16.7 us
    all_to_all x1, blocking collectives, local(): pieces = lax.all_to_all(term, ('modes', 'rows'), 0, 0, tiled=True)  12.7 us
    pallas_call x5, Pallas kernels, kernel_call(): pl.pallas_call(kernel, out_shape=out_shape, compiler_params=pltpu.Compile...  11.3 us
    all_to_all x1, starting transfers between devices, local(): pixels = lax.all_to_all(blocks, 'modes', 0, 0, tiled=True)  5 us
    dot_general x4, matrix products, times(): return jnp.dot(one, two, preferred_element_type=f32)  2.52 us
  transfers between devices with their start and end apart: 17, of which 12 were waited for; matrix products, arithmetic and copies ran while one was open for 6% of the time, Pallas kernels for 5%

profile of v19, /device:TPU:0, one launch (start us, length us, event | category | flops | bytes accessed | tf_op | source)
XLA Modules:
  0.0 104.6 jit_solution(8579308636775950731)
XLA Ops:
  0.6 1.8 %shard_map.94 = (bf16[192,768]{1,0:T(8,128)(2,1)S(1)}, f32[192,768]{1,0:T(8,128)S(1)}, bf16[192,768]{1,0:T(8,128)(2,1)S(1)}, f32[192,768]{1,0:T(8,128)S(1)}) custom-call(bf16[384,1536]{1,0:T(8,128)(2,1)} %bitcast.89, bf16[384,1536]{1,0:T(8,128)(2,1)} %bitcast.90), custom_call_target="tpu_custom_call" | custom-call | flops 4718592 | bytes 4194304 | tf_op jit(solution)/shard_map/pallas_call | solution.py:188
  2.5 3.0 %collective-permute-start = (bf16[4,2,24,768]{3,2,0,1:T(8,128)(2,1)S(1)}, bf16[4,2,24,768]{3,2,0,1:T(8,128)(2,1)S(1)}, u32[]{:S(2)}, u32[]{:S(2)}) collective-permute-start(bf16[4,2,24,768]{3,2,0,1:T(8,128)(2,1)S(1)} %copy.17), channel_id=1, source_target_pairs={{0,2},{2,0},{4,6},{6,4},{8,10},{10,8},{12,14},{14,12},{16,18},{18,... | collective-permute-start | bytes 884744 | tf_op jit(solution)/shard_map/ppermute | solution.py:33
  5.5 1.6 %collective-permute-start.2 = (bf16[4,2,24,768]{3,2,0,1:T(8,128)(2,1)S(1)}, bf16[4,2,24,768]{3,2,0,1:T(8,128)(2,1)S(1)}, u32[]{:S(2)}, u32[]{:S(2)}) collective-permute-start(bf16[4,2,24,768]{3,2,0,1:T(8,128)(2,1)S(1)} %copy.19), channel_id=1, source_target_pairs={{0,4},{2,6},{4,0},{6,2},{8,12},{10,14},{12,8},{14,10},{16,20},{18,... | collective-permute-start | bytes 884744 | tf_op jit(solution)/shard_map/ppermute | solution.py:33
  7.1 5.4 %collective-permute-done = bf16[4,2,24,768]{3,2,0,1:T(8,128)(2,1)S(1)} collective-permute-done((bf16[4,2,24,768]{3,2,0,1:T(8,128)(2,1)S(1)}, bf16[4,2,24,768]{3,2,0,1:T(8,128)(2,1)S(1)}, u32[]{:S(2)}, u32[]{:S(2)}) %collective-permute-start) | collective-permute-done | bytes 294944 | tf_op jit(solution)/shard_map/ppermute | solution.py:33
  12.6 1.8 %collective-permute-start.1 = (bf16[4,24,768]{2,1,0:T(8,128)(2,1)S(1)}, bf16[4,24,768]{2,1,0:T(8,128)(2,1)S(1)}, u32[]{:S(2)}, u32[]{:S(2)}) collective-permute-start(bf16[4,24,768]{2,1,0:T(8,128)(2,1)S(1)} %fusion.12), channel_id=1, source_target_pairs={{0,4},{2,6},{4,0},{6,2},{8,12},{10,14},{12,8},{14,10},{16,20},{18,... | collective-permute-start | bytes 442376 | tf_op jit(solution)/shard_map/ppermute | solution.py:33
  14.5 1.6 %collective-permute-start.3 = (bf16[4,24,768]{2,1,0:T(8,128)(2,1)S(1)}, bf16[4,24,768]{2,1,0:T(8,128)(2,1)S(1)}, u32[]{:S(2)}, u32[]{:S(2)}) collective-permute-start(bf16[4,24,768]{2,1,0:T(8,128)(2,1)S(1)} %fusion.13), channel_id=1, source_target_pairs={{0,2},{2,0},{4,6},{6,4},{8,10},{10,8},{12,14},{14,12},{16,18},{18,... | collective-permute-start | bytes 442376 | tf_op jit(solution)/shard_map/ppermute | solution.py:33
  16.1 1.7 %collective-permute-done.1 = bf16[4,24,768]{2,1,0:T(8,128)(2,1)S(1)} collective-permute-done((bf16[4,24,768]{2,1,0:T(8,128)(2,1)S(1)}, bf16[4,24,768]{2,1,0:T(8,128)(2,1)S(1)}, u32[]{:S(2)}, u32[]{:S(2)}) %collective-permute-start.1) | collective-permute-done | bytes 147488 | tf_op jit(solution)/shard_map/ppermute | solution.py:33
  17.8 1.9 %collective-permute-done.3 = bf16[4,24,768]{2,1,0:T(8,128)(2,1)S(1)} collective-permute-done((bf16[4,24,768]{2,1,0:T(8,128)(2,1)S(1)}, bf16[4,24,768]{2,1,0:T(8,128)(2,1)S(1)}, u32[]{:S(2)}, u32[]{:S(2)}) %collective-permute-start.3) | collective-permute-done | bytes 147488 | tf_op jit(solution)/shard_map/ppermute | solution.py:33
  19.8 3.7 %collective-permute-start.6 = (bf16[24,1536]{1,0:T(8,128)(2,1)S(1)}, bf16[24,1536]{1,0:T(8,128)(2,1)S(1)}, u32[]{:S(2)}, u32[]{:S(2)}) collective-permute-start(bf16[24,1536]{1,0:T(8,128)(2,1)S(1)} %get-tuple-element.37), channel_id=1, source_target_pairs={{0,24},{2,26},{4,28},{6,30},{8,16},{10,18},{12,20},{14,22},{16,8},... | collective-permute-start | bytes 221192 | tf_op jit(solution)/shard_map/ppermute | solution.py:33
  23.5 0.8 collective-permute-start.4
  24.2 2.2 %collective-permute-done.6 = bf16[24,1536]{1,0:T(8,128)(2,1)S(1)} collective-permute-done((bf16[24,1536]{1,0:T(8,128)(2,1)S(1)}, bf16[24,1536]{1,0:T(8,128)(2,1)S(1)}, u32[]{:S(2)}, u32[]{:S(2)}) %collective-permute-start.6) | collective-permute-done | bytes 73760 | tf_op jit(solution)/shard_map/ppermute | solution.py:33
  26.4 2.5 %collective-permute-done.5 = bf16[24,1536]{1,0:T(8,128)(2,1)S(1)} collective-permute-done((bf16[24,1536]{1,0:T(8,128)(2,1)S(1)}, bf16[24,1536]{1,0:T(8,128)(2,1)S(1)}, u32[]{:S(2)}, u32[]{:S(2)}) %collective-permute-start.5) | collective-permute-done | bytes 73760 | tf_op jit(solution)/shard_map/ppermute | solution.py:33
  29.0 1.7 %collective-permute-start.9 = (bf16[24,1536]{1,0:T(8,128)(2,1)S(1)}, bf16[24,1536]{1,0:T(8,128)(2,1)S(1)}, u32[]{:S(2)}, u32[]{:S(2)}) collective-permute-start(bf16[24,1536]{1,0:T(8,128)(2,1)S(1)} %pad_maximum_fusion.10), channel_id=1, source_target_pairs={{0,24},{2,26},{4,28},{6,30},{8,16},{10,18},{12,20},{14,22},{16,8},... | collective-permute-start | bytes 221192 | tf_op jit(solution)/shard_map/ppermute | solution.py:33
  30.7 0.4 collective-permute-start.8
  31.1 2.4 %collective-permute-start.7 = (bf16[24,1536]{1,0:T(8,128)(2,1)S(1)}, bf16[24,1536]{1,0:T(8,128)(2,1)S(1)}, u32[]{:S(2)}, u32[]{:S(2)}) collective-permute-start(bf16[24,1536]{1,0:T(8,128)(2,1)S(1)} %pad_maximum_fusion.10), channel_id=1, source_target_pairs={{0,8},{2,10},{4,12},{6,14},{8,0},{10,2},{12,4},{14,6},{16,24},{18,... | collective-permute-start | bytes 221192 | tf_op jit(solution)/shard_map/ppermute | solution.py:33
  33.5 1.8 %collective-permute-done.9 = bf16[24,1536]{1,0:T(8,128)(2,1)S(1)} collective-permute-done((bf16[24,1536]{1,0:T(8,128)(2,1)S(1)}, bf16[24,1536]{1,0:T(8,128)(2,1)S(1)}, u32[]{:S(2)}, u32[]{:S(2)}) %collective-permute-start.9) | collective-permute-done | bytes 73760 | tf_op jit(solution)/shard_map/ppermute | solution.py:33
  35.3 1.6 %collective-permute-done.8 = bf16[24,1536]{1,0:T(8,128)(2,1)S(1)} collective-permute-done((bf16[24,1536]{1,0:T(8,128)(2,1)S(1)}, bf16[24,1536]{1,0:T(8,128)(2,1)S(1)}, u32[]{:S(2)}, u32[]{:S(2)}) %collective-permute-start.8) | collective-permute-done | bytes 73760 | tf_op jit(solution)/shard_map/ppermute | solution.py:33
  37.0 1.6 %collective-permute-start.12 = (bf16[4,24,768]{2,1,0:T(8,128)(2,1)S(1)}, bf16[4,24,768]{2,1,0:T(8,128)(2,1)S(1)}, u32[]{:S(2)}, u32[]{:S(2)}) collective-permute-start(bf16[4,24,768]{2,1,0:T(8,128)(2,1)S(1)} %get-tuple-element.40), channel_id=1, source_target_pairs={{0,2},{2,0},{4,6},{6,4},{8,10},{10,8},{12,14},{14,12},{16,18},{18,... | collective-permute-start | bytes 442376 | tf_op jit(solution)/shard_map/ppermute | solution.py:33
  38.6 0.3 bitcast_convert_fusion
  38.8 0.8 collective-permute-start.10
  39.7 3.6 %collective-permute-done.12 = bf16[4,24,768]{2,1,0:T(8,128)(2,1)S(1)} collective-permute-done((bf16[4,24,768]{2,1,0:T(8,128)(2,1)S(1)}, bf16[4,24,768]{2,1,0:T(8,128)(2,1)S(1)}, u32[]{:S(2)}, u32[]{:S(2)}) %collective-permute-start.12) | collective-permute-done | bytes 147488 | tf_op jit(solution)/shard_map/ppermute | solution.py:33
  43.4 1.4 %collective-permute-start.13 = (bf16[4,2,24,768]{3,2,1,0:T(8,128)(2,1)S(1)}, bf16[4,2,24,768]{3,2,1,0:T(8,128)(2,1)S(1)}, u32[]{:S(2)}, u32[]{:S(2)}) collective-permute-start(bf16[4,2,24,768]{3,2,1,0:T(8,128)(2,1)S(1)} %reverse_select_fusion.2), channel_id=1, source_target_pairs={{0,4},{2,6},{4,0},{6,2},{8,12},{10,14},{12,8},{14,10},{16,20},{18,... | collective-permute-start | bytes 884744 | tf_op jit(solution)/shard_map/ppermute | solution.py:33
  44.9 1.2 %collective-permute-start.11 = (bf16[4,2,24,768]{3,2,0,1:T(8,128)(2,1)S(1)}, bf16[4,2,24,768]{3,2,0,1:T(8,128)(2,1)S(1)}, u32[]{:S(2)}, u32[]{:S(2)}) collective-permute-start(bf16[4,2,24,768]{3,2,0,1:T(8,128)(2,1)S(1)} %reverse_select_fusion.3), channel_id=1, source_target_pairs={{0,2},{2,0},{4,6},{6,4},{8,10},{10,8},{12,14},{14,12},{16,18},{18,... | collective-permute-start | bytes 884744 | tf_op jit(solution)/shard_map/ppermute | solution.py:33
  46.2 4.0 %collective-permute-done.13 = bf16[4,2,24,768]{3,2,1,0:T(8,128)(2,1)S(1)} collective-permute-done((bf16[4,2,24,768]{3,2,1,0:T(8,128)(2,1)S(1)}, bf16[4,2,24,768]{3,2,1,0:T(8,128)(2,1)S(1)}, u32[]{:S(2)}, u32[]{:S(2)}) %collective-permute-start.13) | collective-permute-done | bytes 294944 | tf_op jit(solution)/shard_map/ppermute | solution.py:33
  50.2 0.1 reverse_select_fusion
  50.3 1.4 %collective-permute-done.11 = bf16[4,2,24,768]{3,2,0,1:T(8,128)(2,1)S(1)} collective-permute-done((bf16[4,2,24,768]{3,2,0,1:T(8,128)(2,1)S(1)}, bf16[4,2,24,768]{3,2,0,1:T(8,128)(2,1)S(1)}, u32[]{:S(2)}, u32[]{:S(2)}) %collective-permute-start.11) | collective-permute-done | bytes 294944 | tf_op jit(solution)/shard_map/ppermute | solution.py:33
  51.8 0.1 reverse_select_fusion.1
  51.9 0.4 fusion.9
  52.6 0.6 collective-permute-start.15
  53.1 0.5 copy-done.3
  53.6 1.4 %shard_map.95.own_ref = f32[768,768]{1,0:T(8,128)S(1)} custom-call(bf16[768,768]{1,0:T(8,128)(2,1)S(1)} %copy-done.3, bf16[768,384]{1,0:T(8,128)(2,1)S(1)} %pad_maximum_fusion.3.first_ref, bf16[768,384]{1,0:T(8,128)(2,1)S(1)} %pad_maximum_fusion.5.second_ref), custom_call_target="tpu_custom_call" | custom-call | flops 905969664 | bytes 4194304 | tf_op jit(solution)/shard_map/pallas_call | solution.py:188
  55.0 0.3 collective-permute-done.15.second_ref
  55.3 2.4 %shard_map.96.refs_0_ = bf16[768,768]{1,0:T(8,128)(2,1)} custom-call(bf16[768,768]{1,0:T(8,128)(2,1)S(1)} %copy-done.2, bf16[768,384]{1,0:T(8,128)(2,1)S(1)} %collective-permute-done.14.first_ref, bf16[768,384]{1,0:T(8,128)(2,1)S(1)} %collective-permute-done.15.second_ref, f32[768,768]{1,0:T(8,128)S(1)} %shard_map.95.own_ref), custom_call_target="tpu_custom_call" | custom-call | flops 905969664 | bytes 4194304 | tf_op jit(solution)/shard_map/pallas_call | solution.py:188
  57.8 5.0 %all-to-all-start = ((bf16[16,48,768]{2,1,0:T(8,128)(2,1)}), bf16[16,48,768]{2,1,0:T(8,128)(2,1)S(1)}, u32[]{:S(2)}, u32[]{:S(2)}) async-start(bf16[16,48,768]{2,1,0:T(8,128)(2,1)} %bitcast.33), calls=%async_computation | async-start | bytes 2359296 | tf_op jit(solution)/shard_map/all_to_all | solution.py:304
  62.8 1.4 %fusion.28 = (bf16[1,16,24,768]{3,2,1,0:T(8,128)(2,1)S(1)}, bf16[1,16,24,768]{3,2,1,0:T(8,128)(2,1)S(1)}) fusion(bf16[2,16,24,768]{3,2,1,0:T(8,128)(2,1)} %param.9), kind=kLoop, calls=%fused_computation.80 | loop fusion | bytes 2359296 | tf_op jit(solution)/shard_map/unstack | solution.py:313
  64.2 0.2 copy-done.1
  64.4 0.6 fusion.32
  65.1 0.6 fusion.31
  65.7 0.6 copy-done
  66.3 0.6 fusion.2
  67.0 0.6 fusion.3
  67.7 0.1 fusion.29
  67.8 1.1 %pad_maximum_fusion = bf16[384,1536]{1,0:T(8,128)(2,1)} fusion(bf16[384,384]{1,0:T(8,128)(2,1)S(1)} %get-tuple-element.50, bf16[384,384]{1,0:T(8,128)(2,1)S(1)} %get-tuple-element.32, bf16[384,384]{1,0:T(8,128)(2,1)S(1)} %get-tuple-element.51, bf16[384,384]{1,0:T(8,128)(2,1)S(1)} %get-tuple-element.31), kind=kLoop, calls=%fused_computation.6 | loop fusion | flops 4718592 | bytes 2359296 | tf_op jit(solution)/shard_map/concatenate | solution.py:271
  68.9 4.3 %shard_map.97 = bf16[384,1536]{1,0:T(8,128)(2,1)} custom-call(bf16[768,768]{1,0:T(8,128)(2,1)} %shard_map.96.refs_0_, bf16[768,768]{1,0:T(8,128)(2,1)S(1)} %copy-done.1, bf16[768,768]{1,0:T(8,128)(2,1)S(1)} %copy-done), custom_call_target="tpu_custom_call" | custom-call | flops 1811939328 | bytes 4194304 | tf_op jit(solution)/shard_map/pallas_call | solution.py:188
  73.2 16.7 %all-to-all-done = bf16[16,48,768]{2,1,0:T(8,128)(2,1)S(1)} async-done(((bf16[16,48,768]{2,1,0:T(8,128)(2,1)}), bf16[16,48,768]{2,1,0:T(8,128)(2,1)S(1)}, u32[]{:S(2)}, u32[]{:S(2)}) %all-to-all-start) | async-done | bytes 1179680 | tf_op jit(solution)/shard_map/all_to_all | solution.py:304
  89.9 1.4 %shard_map.98 = f32[32,16]{1,0:T(8,128)S(1)} custom-call(bf16[768,768]{1,0:T(8,128)(2,1)S(1)} %bitcast.75, bf16[768,768]{1,0:T(8,128)(2,1)S(1)} %pad_maximum_fusion.1.refs_1_), custom_call_target="tpu_custom_call" | custom-call | flops 1811939328 | bytes 4194304 | tf_op jit(solution)/shard_map/pallas_call | solution.py:188
  91.3 12.7 %all_to_all.14 = f32[32,1,16]{2,1,0:T(1,128)S(1)} all-to-all(f32[32,1,16]{2,1,0:T(1,128)S(1)} %bitcast.80), channel_id=1, replica_groups=mesh['modes'=16,'rows'=2] {'modes','rows'}, dimensions={0} | all-to-all | bytes 4096 | tf_op jit(solution)/shard_map/all_to_all | solution.py:329
  104.0 0.6 reduce_sum.9
  (42 shorter events, 1.2 us)
Async XLA Ops:
  2.5 10.0 %collective-permute-start = (bf16[4,2,24,768]{3,2,0,1:T(8,128)(2,1)S(1)}, bf16[4,2,24,768]{3,2,0,1:T(8,128)(2,1)S(1)}, u32[]{:S(2)}, u32[]{:S(2)}) collective-permute-start(bf16[4,2,24,768]{3,2,0,1:T(8,128)(2,1)S(1)} %copy.17), channel_id=1, source_target_pairs={{0,2},{2,0},{4,6},{6,4},{8,10},{10,8},{12,14},{14,12},{16,18},{18,... | collective-permute-start | bytes 884744 | tf_op jit(solution)/shard_map/ppermute | solution.py:33
  5.5 8.9 %collective-permute-start.2 = (bf16[4,2,24,768]{3,2,0,1:T(8,128)(2,1)S(1)}, bf16[4,2,24,768]{3,2,0,1:T(8,128)(2,1)S(1)}, u32[]{:S(2)}, u32[]{:S(2)}) collective-permute-start(bf16[4,2,24,768]{3,2,0,1:T(8,128)(2,1)S(1)} %copy.19), channel_id=1, source_target_pairs={{0,4},{2,6},{4,0},{6,2},{8,12},{10,14},{12,8},{14,10},{16,20},{18,... | collective-permute-start | bytes 884744 | tf_op jit(solution)/shard_map/ppermute | solution.py:33
  12.6 5.2 %collective-permute-start.1 = (bf16[4,24,768]{2,1,0:T(8,128)(2,1)S(1)}, bf16[4,24,768]{2,1,0:T(8,128)(2,1)S(1)}, u32[]{:S(2)}, u32[]{:S(2)}) collective-permute-start(bf16[4,24,768]{2,1,0:T(8,128)(2,1)S(1)} %fusion.12), channel_id=1, source_target_pairs={{0,4},{2,6},{4,0},{6,2},{8,12},{10,14},{12,8},{14,10},{16,20},{18,... | collective-permute-start | bytes 442376 | tf_op jit(solution)/shard_map/ppermute | solution.py:33
  14.5 5.2 %collective-permute-start.3 = (bf16[4,24,768]{2,1,0:T(8,128)(2,1)S(1)}, bf16[4,24,768]{2,1,0:T(8,128)(2,1)S(1)}, u32[]{:S(2)}, u32[]{:S(2)}) collective-permute-start(bf16[4,24,768]{2,1,0:T(8,128)(2,1)S(1)} %fusion.13), channel_id=1, source_target_pairs={{0,2},{2,0},{4,6},{6,4},{8,10},{10,8},{12,14},{14,12},{16,18},{18,... | collective-permute-start | bytes 442376 | tf_op jit(solution)/shard_map/ppermute | solution.py:33
  19.8 6.6 %collective-permute-start.6 = (bf16[24,1536]{1,0:T(8,128)(2,1)S(1)}, bf16[24,1536]{1,0:T(8,128)(2,1)S(1)}, u32[]{:S(2)}, u32[]{:S(2)}) collective-permute-start(bf16[24,1536]{1,0:T(8,128)(2,1)S(1)} %get-tuple-element.37), channel_id=1, source_target_pairs={{0,24},{2,26},{4,28},{6,30},{8,16},{10,18},{12,20},{14,22},{16,8},... | collective-permute-start | bytes 221192 | tf_op jit(solution)/shard_map/ppermute | solution.py:33
  23.5 5.5 %collective-permute-start.5 = (bf16[24,1536]{1,0:T(8,128)(2,1)S(1)}, bf16[24,1536]{1,0:T(8,128)(2,1)S(1)}, u32[]{:S(2)}, u32[]{:S(2)}) collective-permute-start(bf16[24,1536]{1,0:T(8,128)(2,1)S(1)} %get-tuple-element.36), channel_id=1, source_target_pairs={{0,16},{2,18},{4,20},{6,22},{8,24},{10,26},{12,28},{14,30},{16,0},... | collective-permute-start | bytes 221192 | tf_op jit(solution)/shard_map/ppermute | solution.py:33
  23.5 5.5 %collective-permute-start.4 = (bf16[24,1536]{1,0:T(8,128)(2,1)S(1)}, bf16[24,1536]{1,0:T(8,128)(2,1)S(1)}, u32[]{:S(2)}, u32[]{:S(2)}) collective-permute-start(bf16[24,1536]{1,0:T(8,128)(2,1)S(1)} %get-tuple-element.35), channel_id=1, source_target_pairs={{0,8},{2,10},{4,12},{6,14},{8,0},{10,2},{12,4},{14,6},{16,24},{18,... | collective-permute-start | bytes 221192 | tf_op jit(solution)/shard_map/ppermute | solution.py:33
  29.0 6.2 %collective-permute-start.9 = (bf16[24,1536]{1,0:T(8,128)(2,1)S(1)}, bf16[24,1536]{1,0:T(8,128)(2,1)S(1)}, u32[]{:S(2)}, u32[]{:S(2)}) collective-permute-start(bf16[24,1536]{1,0:T(8,128)(2,1)S(1)} %pad_maximum_fusion.10), channel_id=1, source_target_pairs={{0,24},{2,26},{4,28},{6,30},{8,16},{10,18},{12,20},{14,22},{16,8},... | collective-permute-start | bytes 221192 | tf_op jit(solution)/shard_map/ppermute | solution.py:33
  30.7 6.1 %collective-permute-start.8 = (bf16[24,1536]{1,0:T(8,128)(2,1)S(1)}, bf16[24,1536]{1,0:T(8,128)(2,1)S(1)}, u32[]{:S(2)}, u32[]{:S(2)}) collective-permute-start(bf16[24,1536]{1,0:T(8,128)(2,1)S(1)} %pad_maximum_fusion.10), channel_id=1, source_target_pairs={{0,16},{2,18},{4,20},{6,22},{8,24},{10,26},{12,28},{14,30},{16,0},... | collective-permute-start | bytes 221192 | tf_op jit(solution)/shard_map/ppermute | solution.py:33
  31.1 5.8 %collective-permute-start.7 = (bf16[24,1536]{1,0:T(8,128)(2,1)S(1)}, bf16[24,1536]{1,0:T(8,128)(2,1)S(1)}, u32[]{:S(2)}, u32[]{:S(2)}) collective-permute-start(bf16[24,1536]{1,0:T(8,128)(2,1)S(1)} %pad_maximum_fusion.10), channel_id=1, source_target_pairs={{0,8},{2,10},{4,12},{6,14},{8,0},{10,2},{12,4},{14,6},{16,24},{18,... | collective-permute-start | bytes 221192 | tf_op jit(solution)/shard_map/ppermute | solution.py:33
  36.8 1.7 %copy-start.4 = (bf16[1,384,1536]{2,1,0:T(8,128)(2,1)S(1)}, bf16[1,384,1536]{2,1,0:T(8,128)(2,1)}, u32[]{:S(2)}) copy-start(bf16[1,384,1536]{2,1,0:T(8,128)(2,1)} %param.7) | copy-start | bytes 3538948
  37.0 6.3 %collective-permute-start.12 = (bf16[4,24,768]{2,1,0:T(8,128)(2,1)S(1)}, bf16[4,24,768]{2,1,0:T(8,128)(2,1)S(1)}, u32[]{:S(2)}, u32[]{:S(2)}) collective-permute-start(bf16[4,24,768]{2,1,0:T(8,128)(2,1)S(1)} %get-tuple-element.40), channel_id=1, source_target_pairs={{0,2},{2,0},{4,6},{6,4},{8,10},{10,8},{12,14},{14,12},{16,18},{18,... | collective-permute-start | bytes 442376 | tf_op jit(solution)/shard_map/ppermute | solution.py:33
  38.8 6.0 %collective-permute-start.10 = (bf16[4,24,768]{2,1,0:T(8,128)(2,1)S(1)}, bf16[4,24,768]{2,1,0:T(8,128)(2,1)S(1)}, u32[]{:S(2)}, u32[]{:S(2)}) collective-permute-start(bf16[4,24,768]{2,1,0:T(8,128)(2,1)S(1)} %get-tuple-element.41), channel_id=1, source_target_pairs={{0,4},{2,6},{4,0},{6,2},{8,12},{10,14},{12,8},{14,10},{16,20},{18,... | collective-permute-start | bytes 442376 | tf_op jit(solution)/shard_map/ppermute | solution.py:33
  43.4 6.8 %collective-permute-start.13 = (bf16[4,2,24,768]{3,2,1,0:T(8,128)(2,1)S(1)}, bf16[4,2,24,768]{3,2,1,0:T(8,128)(2,1)S(1)}, u32[]{:S(2)}, u32[]{:S(2)}) collective-permute-start(bf16[4,2,24,768]{3,2,1,0:T(8,128)(2,1)S(1)} %reverse_select_fusion.2), channel_id=1, source_target_pairs={{0,4},{2,6},{4,0},{6,2},{8,12},{10,14},{12,8},{14,10},{16,20},{18,... | collective-permute-start | bytes 884744 | tf_op jit(solution)/shard_map/ppermute | solution.py:33
  44.9 6.8 %collective-permute-start.11 = (bf16[4,2,24,768]{3,2,0,1:T(8,128)(2,1)S(1)}, bf16[4,2,24,768]{3,2,0,1:T(8,128)(2,1)S(1)}, u32[]{:S(2)}, u32[]{:S(2)}) collective-permute-start(bf16[4,2,24,768]{3,2,0,1:T(8,128)(2,1)S(1)} %reverse_select_fusion.3), channel_id=1, source_target_pairs={{0,2},{2,0},{4,6},{6,4},{8,10},{10,8},{12,14},{14,12},{16,18},{18,... | collective-permute-start | bytes 884744 | tf_op jit(solution)/shard_map/ppermute | solution.py:33
  52.3 1.3 %copy-start.3 = (bf16[768,768]{1,0:T(8,128)(2,1)S(1)}, bf16[768,768]{1,0:T(8,128)(2,1)}, u32[]{:S(2)}) copy-start(bf16[768,768]{1,0:T(8,128)(2,1)} %constant.107.clone.table_ref) | copy-start | bytes 3538948
  52.4 2.6 %collective-permute-start.14 = (bf16[768,384]{1,0:T(8,128)(2,1)S(1)}, bf16[768,384]{1,0:T(8,128)(2,1)S(1)}, u32[]{:S(2)}, u32[]{:S(2)}) collective-permute-start(bf16[768,384]{1,0:T(8,128)(2,1)S(1)} %pad_maximum_fusion.3.first_ref), channel_id=1, source_target_pairs={{0,1},{1,0},{2,3},{3,2},{4,5},{5,4},{6,7},{7,6},{8,9},{9,8},{10,11... | collective-permute-start | bytes 1769480 | tf_op jit(solution)/shard_map/ppermute | solution.py:282
  52.6 2.8 %copy-start.2 = (bf16[768,768]{1,0:T(8,128)(2,1)S(1)}, bf16[768,768]{1,0:T(8,128)(2,1)}, u32[]{:S(2)}) copy-start(bf16[768,768]{1,0:T(8,128)(2,1)} %constant.108.clone.table_ref) | copy-start | bytes 3538948
  52.6 2.8 %collective-permute-start.15 = (bf16[768,384]{1,0:T(8,128)(2,1)S(1)}, bf16[768,384]{1,0:T(8,128)(2,1)S(1)}, u32[]{:S(2)}, u32[]{:S(2)}) collective-permute-start(bf16[768,384]{1,0:T(8,128)(2,1)S(1)} %pad_maximum_fusion.5.second_ref), channel_id=1, source_target_pairs={{0,1},{1,0},{2,3},{3,2},{4,5},{5,4},{6,7},{7,6},{8,9},{9,8},{10,11... | collective-permute-start | bytes 1769480 | tf_op jit(solution)/shard_map/ppermute | solution.py:282
  57.8 32.1 %all-to-all-start = ((bf16[16,48,768]{2,1,0:T(8,128)(2,1)}), bf16[16,48,768]{2,1,0:T(8,128)(2,1)S(1)}, u32[]{:S(2)}, u32[]{:S(2)}) async-start(bf16[16,48,768]{2,1,0:T(8,128)(2,1)} %bitcast.33), calls=%async_computation | async-start | bytes 2359296 | tf_op jit(solution)/shard_map/all_to_all | solution.py:304
  62.8 1.6 %copy-start.1 = (bf16[768,768]{1,0:T(8,128)(2,1)S(1)}, bf16[768,768]{1,0:T(8,128)(2,1)}, u32[]{:S(2)}) copy-start(bf16[768,768]{1,0:T(8,128)(2,1)} %constant.105.clone.refs_1_) | copy-start | bytes 3538948
  65.1 1.3 %copy-start = (bf16[768,768]{1,0:T(8,128)(2,1)S(1)}, bf16[768,768]{1,0:T(8,128)(2,1)}, u32[]{:S(2)}) copy-start(bf16[768,768]{1,0:T(8,128)(2,1)} %constant.106.clone.refs_2_) | copy-start | bytes 3538948
